TPU v7x, 32 devices: a whole 2x2x4 slice. The times are simulated.
32 devices in a mesh: groups: 2 (over y), store: 16 (over z, x, core).
Axes of the slice: x: 2, y: 2, z: 4, core: 2. Of those that a mesh axis runs over, the one named last changes fastest.
Arguments:
- store: bfloat16 [4096, 16, 1024], P(('groups', 'store')), parts along dimension 0, may hold values from -6 to 6
- page_table: int32 [32, 128], P(('groups', 'store')), parts along dimension 0, may hold values from 0 to 2047, as said below
- sel_pos: int32 [32, 160], P(('groups', 'store')), parts along dimension 0, may hold values from 0 to 2047, as said below
- fresh_kv: bfloat16 [32, 160, 1024], P(('groups', 'store')), parts along dimension 0, may hold values from -6 to 6
- queries: bfloat16 [32, 160, 6144], P(('groups', 'store')), parts along dimension 0, may hold values from -256 to 256
Outputs:
- attended: bfloat16 [32, 160, 6144], P(('groups', 'store')), parts along dimension 0
- store_out: bfloat16 [4096, 16, 1024], P(('groups', 'store')), parts along dimension 0
There are 2 independent parts, one for each index of `groups`. A program takes and returns all parts, laid end to end along the dimension named above; each array names one. Nothing has to cross between parts.
Inputs may be any that keep to these rules, and one draw needn't show every extreme that they name: `page_table`: every page slot appears exactly once in the whole table. Slot s lies on device s // 128 of store. One request has at most 8 pages on any one device, and exactly 8 on some. `sel_pos`: each row rises strictly. At most 2 positions of one row fall in one page of 16 tokens, and exactly 2 in some page of every row.
All inputs are finite; a program needn't handle non-finite values.
Results may differ from a plain program's by a relative error of at most 0.0039.
Values may be sent and summed in bfloat16 or wider, within the bound.
No kernel may reach another device: no remote copies, remote signals or barrier semaphores. Data moves between devices by JAX's collectives and lax.ppermute only.
A program may use at most 192 MiB of HBM per device.

v0:
```python
import functools

import jax
import jax.numpy as jnp
from jax import lax
from jax.experimental import pallas as pl
from jax.experimental.pallas import tpu as pltpu
from jax.sharding import PartitionSpec as P

HEAD_WIDTH = 128
KEY_VALUE_HEADS = 4
QUERY_GROUP = 12
SELP = 2
LANES = 128
OFFSET_LANE = 64
QUERY_BLOCK = 32
TILE_PAGES = 16
HIDDEN = -1e30


def nt_dot(a, b):
    return lax.dot_general(a, b, (((1,), (1,)), ((), ())), preferred_element_type=jnp.float32)


def plan_kernel(hold, holders, row_slots, page_len, table_ref, sel_ref, fresh_ref, out_ref, wide):
    pages = table_ref.shape[1]
    picked = sel_ref.shape[1]
    wide_lanes = wide.shape[1]
    chunks = fresh_ref.shape[1] // LANES
    f32 = jnp.float32
    slot_row = jnp.broadcast_to(table_ref[...], (pages, pages))
    owner_row = slot_row // hold
    local_row = (slot_row - owner_row * hold).astype(f32)
    owner_row = owner_row.astype(f32)
    owner_col = owner_row.T
    sub = lax.broadcasted_iota(jnp.int32, (pages, pages), 0)
    lane = lax.broadcasted_iota(jnp.int32, (pages, pages), 1)
    earlier = jnp.where((owner_row == owner_col) & (lane < sub), 1.0, 0.0)
    rank_col = jnp.sum(earlier, axis=1, keepdims=True)
    owner_col = owner_col[:, 0:1]

    holder = lax.broadcasted_iota(jnp.int32, (holders, pages), 0).astype(f32)
    owned = jnp.where(holder == owner_row[0:1, :], local_row[0:1, :], 0.0)
    at_rank = jnp.where(lane.astype(f32) == rank_col, 1.0, 0.0)
    numbers = jnp.dot(
        owned.astype(jnp.bfloat16), at_rank.astype(jnp.bfloat16), preferred_element_type=f32
    )

    wide[...] = jnp.full(wide.shape, -1, jnp.int32)
    wide[0:1, 0:picked] = sel_ref[...]
    position = wide[...]
    page = lax.shift_right_arithmetic(position, page_len.bit_length() - 1)
    offset = (position & (page_len - 1)).astype(f32)
    lane8 = lax.broadcasted_iota(jnp.int32, wide.shape, 1)
    second = jnp.where((page == pltpu.roll(page, 1, axis=1)) & (lane8 > 0), 1.0, 0.0)
    page, offset, second = page[0:1], offset[0:1], second[0:1]
    valid = lane8[0:1] < picked
    sub_wide = lax.broadcasted_iota(jnp.int32, (pages, wide_lanes), 0)
    in_page = jnp.where(sub_wide == page, 1.0, 0.0)
    owner = jnp.sum(in_page * owner_col, axis=0, keepdims=True)
    place = SELP * jnp.sum(in_page * rank_col, axis=0, keepdims=True) + second
    spot = jnp.where(valid, owner * row_slots + place, -1.0)

    holder_wide = lax.broadcasted_iota(jnp.int32, (holders, wide_lanes), 0).astype(f32)
    marked = jnp.where((holder_wide == owner) & valid, offset + 1.0, 0.0)
    place_lane = lax.broadcasted_iota(jnp.int32, (LANES, wide_lanes), 0).astype(f32)
    at_place = jnp.where(place_lane == place + OFFSET_LANE, 1.0, 0.0)
    offsets = nt_dot(marked.astype(jnp.bfloat16), at_place.astype(jnp.bfloat16))
    index_rows = numbers + offsets

    spot_row = spot[:, 0:picked]
    spots = holders * row_slots
    step = min(spots, 256)
    for start in range(0, spots, step):
        spot_id = lax.broadcasted_iota(jnp.int32, (step, picked), 0).astype(f32) + float(start)
        choose = jnp.where(spot_id == spot_row, 1.0, 0.0).astype(jnp.bfloat16)
        rows = jnp.dot(choose, fresh_ref[...], preferred_element_type=f32).astype(jnp.bfloat16)
        for h in range(step // row_slots):
            for c in range(chunks):
                out_ref[start // row_slots + h, c * row_slots : (c + 1) * row_slots, :] = rows[
                    h * row_slots : (h + 1) * row_slots, c * LANES : (c + 1) * LANES
                ]
    for h in range(holders):
        out_ref[h, chunks * row_slots :, :] = jnp.broadcast_to(
            index_rows[h : h + 1, :], (16, LANES)
        ).astype(jnp.bfloat16)


def apply_kernel(splits, row_slots, entries_ref, store_ref, store_out, *rest):
    sends = rest[: len(splits)]
    blended, index_vmem, index_smem, load_sem, index_sem, store_sem, send_sem = rest[len(splits) :]
    holders, capacity = blended.shape[0], blended.shape[1]
    page_len, width = store_ref.shape[1], store_ref.shape[2]
    chunks = width // LANES

    def index_row(r, carry):
        block = entries_ref[r, chunks * row_slots :, :].astype(jnp.float32).astype(jnp.int32)
        index_vmem[pl.ds(r, 1), :] = block[0:1, :]
        return carry

    lax.fori_loop(0, holders, index_row, 0)
    index_copy = pltpu.make_async_copy(index_vmem, index_smem, index_sem)
    index_copy.start()
    index_copy.wait()

    row_id = lax.broadcasted_iota(jnp.int32, (page_len, LANES), 0)

    def one_request(r, carry):
        for k in range(capacity):
            number = index_smem[r, k]
            first = index_smem[r, OFFSET_LANE + SELP * k] - 1
            second = index_smem[r, OFFSET_LANE + SELP * k + 1] - 1
            is_first = row_id == first
            is_second = row_id == second
            for c in range(chunks):
                rows = entries_ref[r, c * row_slots : (c + 1) * row_slots, :].astype(jnp.float32)
                old = store_ref[number, :, c * LANES : (c + 1) * LANES].astype(jnp.float32)
                new = jnp.where(is_first, rows[SELP * k : SELP * k + 1, :], old)
                new = jnp.where(is_second, rows[SELP * k + 1 : SELP * k + 2, :], new)
                blended[r, k, :, c * LANES : (c + 1) * LANES] = new.astype(jnp.bfloat16)
        for (low, high), send in zip(splits, sends):
            pltpu.make_async_copy(blended.at[r, pl.ds(low, high - low)], send.at[r], send_sem).start()
        for k in range(capacity):
            number = index_smem[r, k]
            pltpu.make_async_copy(blended.at[r, k], store_out.at[number], store_sem).start()
        return carry

    lax.fori_loop(0, holders, one_request, 0)
    for (low, high), send in zip(splits, sends):
        pltpu.make_async_copy(send, send, send_sem).wait()
    pltpu.make_async_copy(store_out, store_out, store_sem).wait()


def attend_kernel(first, last, source_ref, tiles_ref, sel_ref, position_ref, query_ref, *rest):
    rest = list(rest)
    state_in = [] if first else [rest.pop(0) for _ in range(3)]
    context = rest.pop(0)
    outs = [rest.pop(0) for _ in range(1 if last else 3)]
    kv, mixed, peak, total, sem = rest
    pages, page_len = context.shape[0], context.shape[1]
    block = query_ref.shape[0]
    tile = TILE_PAGES * page_len
    rows = QUERY_GROUP * block
    scale = 1.4426950408889634 / HEAD_WIDTH**0.5
    f32 = jnp.float32
    step = pl.program_id(0)

    @pl.when(step == 0)
    def _():
        def fetch(i, carry):
            pltpu.make_async_copy(context.at[source_ref[i]], kv.at[i], sem).start()
            return carry

        lax.fori_loop(0, pages, fetch, 0)
        pltpu.make_async_copy(context, kv, sem).wait()

    lane = lax.broadcasted_iota(jnp.int32, (block, LANES), 1)
    for g in range(KEY_VALUE_HEADS):
        for i in range(QUERY_GROUP):
            head = g * QUERY_GROUP + i
            part = slice(i * block, (i + 1) * block)
            if first:
                mixed[g, part, :] = jnp.zeros((block, LANES), f32)
                peak[g, part, :] = jnp.full((block, LANES), HIDDEN, f32)
                total[g, part, :] = jnp.zeros((block, LANES), f32)
            else:
                mixed[g, part, :] = state_in[0][:, head * LANES : (head + 1) * LANES]
                peak[g, part, :] = jnp.broadcast_to(
                    state_in[1][:, head : head + 1], (block, LANES)
                )
                total[g, part, :] = jnp.where(lane == 0, state_in[2][:, head : head + 1], 0.0)

    sel = sel_ref[...]

    def one_tile(t, carry):
        start = pl.multiple_of(t * tile, tile)
        where_page = pl.ds(pl.multiple_of(t * TILE_PAGES, TILE_PAGES), TILE_PAGES)
        position = position_ref[:, pl.ds(start, tile)]
        bias = jnp.where(position <= sel, 0.0, HIDDEN).astype(f32)
        bias = jnp.concatenate([bias] * QUERY_GROUP, axis=0)
        for g in range(KEY_VALUE_HEADS):
            q = jnp.concatenate(
                [
                    query_ref[:, (g * QUERY_GROUP + i) * LANES : (g * QUERY_GROUP + i + 1) * LANES]
                    for i in range(QUERY_GROUP)
                ],
                axis=0,
            )
            key = kv[where_page, :, g * LANES : (g + 1) * LANES].reshape(tile, LANES)
            at = (KEY_VALUE_HEADS + g) * LANES
            value = kv[where_page, :, at : at + LANES].reshape(tile, LANES)
            scores = nt_dot(q, key) + bias
            old = peak[g, :, 0:1]
            new = jnp.maximum(old, jnp.max(scores, axis=1, keepdims=True))
            raised = jnp.exp2((scores - new) * scale)
            shrink = jnp.exp2((old - new) * scale)
            partial = raised[:, 0:LANES]
            for c in range(1, tile // LANES):
                partial = partial + raised[:, c * LANES : (c + 1) * LANES]
            total[g] = total[g] * shrink + partial
            mixed[g] = mixed[g] * shrink + jnp.dot(
                raised.astype(jnp.bfloat16), value, preferred_element_type=f32
            )
            peak[g] = jnp.broadcast_to(new, (rows, LANES))
        return carry

    lax.fori_loop(0, tiles_ref[step], one_tile, 0)

    for g in range(KEY_VALUE_HEADS):
        whole = jnp.sum(total[g], axis=1, keepdims=True)
        if last:
            done = (mixed[g] / whole).astype(jnp.bfloat16)
        for i in range(QUERY_GROUP):
            head = g * QUERY_GROUP + i
            part = slice(i * block, (i + 1) * block)
            if last:
                outs[0][:, head * LANES : (head + 1) * LANES] = done[part, :]
            else:
                outs[0][:, head * LANES : (head + 1) * LANES] = mixed[g, part, :]
                outs[1][:, head : head + 1] = peak[g, part, 0:1]
                outs[2][:, head : head + 1] = whole[part, :]


def attend(first, last, source, tiles, sel_column, position, queries, state, context):
    picked, features = queries.shape
    pages, page_len, width = context.shape
    steps = picked // QUERY_BLOCK
    rows = QUERY_GROUP * QUERY_BLOCK
    wide = pl.BlockSpec((QUERY_BLOCK, features), lambda b, *_: (b, 0))
    narrow = pl.BlockSpec((QUERY_BLOCK, LANES), lambda b, *_: (b, 0))
    state_specs = [wide, narrow, narrow]
    state_shapes = [
        jax.ShapeDtypeStruct((picked, features), jnp.float32),
        jax.ShapeDtypeStruct((picked, LANES), jnp.float32),
        jax.ShapeDtypeStruct((picked, LANES), jnp.float32),
    ]
    share = 0.6
    return pl.pallas_call(
        functools.partial(attend_kernel, first, last),
        grid_spec=pltpu.PrefetchScalarGridSpec(
            num_scalar_prefetch=2,
            grid=(steps,),
            in_specs=[
                pl.BlockSpec((QUERY_BLOCK, 1), lambda b, *_: (b, 0)),
                pl.BlockSpec((1, pages * page_len), lambda b, *_: (0, 0)),
                wide,
                *([] if first else state_specs),
                pl.BlockSpec(memory_space=pl.ANY),
            ],
            out_specs=[wide] if last else state_specs,
            scratch_shapes=[
                pltpu.VMEM((pages, page_len, width), jnp.bfloat16),
                pltpu.VMEM((KEY_VALUE_HEADS, rows, LANES), jnp.float32),
                pltpu.VMEM((KEY_VALUE_HEADS, rows, LANES), jnp.float32),
                pltpu.VMEM((KEY_VALUE_HEADS, rows, LANES), jnp.float32),
                pltpu.SemaphoreType.DMA,
            ],
        ),
        out_shape=[jax.ShapeDtypeStruct((picked, features), jnp.bfloat16)] if last else state_shapes,
        compiler_params=pltpu.CompilerParams(
            dimension_semantics=("arbitrary",), vmem_limit_bytes=40 * 1024 * 1024
        ),
        cost_estimate=pl.CostEstimate(
            flops=int(share * 8 * picked * features * pages * page_len),
            bytes_accessed=2 * pages * page_len * width + 6 * picked * features,
            transcendentals=int(share * picked * features // LANES * pages * page_len),
        ),
    )(source, tiles, sel_column, position, queries, *state, context)


def page_order(slots, positions, hold, splits, page_len):
    pages = slots.shape[0]
    number = jnp.arange(pages)
    before = number[None, :] < number[:, None]
    owners = slots // hold
    ranks = jnp.sum(((owners[None, :] == owners[:, None]) & before).astype(jnp.int32), axis=1)
    last_page = positions.reshape(-1, QUERY_BLOCK)[:, -1] // page_len
    orders = []
    for low, high in splits:
        member = (ranks >= low) & (ranks < high)
        count = pages * (high - low) // splits[-1][1]
        place = jnp.sum((member[None, :] & before).astype(jnp.int32), axis=1)
        hit = (member[None, :] & (place[None, :] == jnp.arange(count)[:, None])).astype(jnp.int32)
        source = jnp.sum(hit * (owners * (high - low) + ranks - low)[None, :], axis=1)
        page = jnp.sum(hit * number[None, :], axis=1)
        position = (page[:, None] * page_len + jnp.arange(page_len)[None, :]).reshape(1, -1)
        seen = jnp.sum((page[None, :] <= last_page[:, None]).astype(jnp.int32), axis=1)
        orders.append((source, (seen + TILE_PAGES - 1) // TILE_PAGES, position))
    return orders


def per_device(store, page_table, sel_pos, fresh_kv, queries):
    holders = lax.axis_size("store")
    hold, page_len, width = store.shape
    pages = page_table.shape[1]
    picked = sel_pos.shape[1]
    capacity = max(1, pages // holders)
    row_slots = -(-SELP * capacity // 16) * 16
    chunks = width // LANES
    packed_rows = chunks * row_slots + 16
    late = capacity // 4
    splits = ((0, capacity - late), (capacity - late, capacity)) if late else ((0, capacity),)

    packed = pl.pallas_call(
        functools.partial(plan_kernel, hold, holders, row_slots, page_len),
        out_shape=jax.ShapeDtypeStruct((holders, packed_rows, LANES), jnp.bfloat16),
        scratch_shapes=[pltpu.VMEM((8, -(-picked // LANES) * LANES), jnp.int32)],
        compiler_params=pltpu.CompilerParams(vmem_limit_bytes=32 * 1024 * 1024),
    )(page_table, sel_pos, fresh_kv[0])
    entries = lax.all_to_all(packed, "store", split_axis=0, concat_axis=0, tiled=True)

    any_space = pl.BlockSpec(memory_space=pl.ANY)
    vmem = pl.BlockSpec(memory_space=pltpu.VMEM)
    store_out, *parts = pl.pallas_call(
        functools.partial(apply_kernel, splits, row_slots),
        out_shape=[
            jax.ShapeDtypeStruct(store.shape, store.dtype),
            *[
                jax.ShapeDtypeStruct((holders, high - low, page_len, width), store.dtype)
                for low, high in splits
            ],
        ],
        in_specs=[vmem, vmem],
        out_specs=[any_space] * (1 + len(splits)),
        scratch_shapes=[
            pltpu.VMEM((holders, capacity, page_len, width), store.dtype),
            pltpu.VMEM((holders, LANES), jnp.int32),
            pltpu.SMEM((holders, LANES), jnp.int32),
            pltpu.SemaphoreType.DMA,
            pltpu.SemaphoreType.DMA,
            pltpu.SemaphoreType.DMA,
            pltpu.SemaphoreType.DMA,
        ],
        compiler_params=pltpu.CompilerParams(vmem_limit_bytes=32 * 1024 * 1024),
    )(entries, store)

    orders = page_order(page_table[0], sel_pos[0], hold, splits, page_len)
    sel_column = sel_pos.reshape(picked, 1)
    arrived = [
        lax.all_to_all(part, "store", split_axis=0, concat_axis=0, tiled=True).reshape(
            -1, page_len, width
        )
        for part in parts
    ]
    state = ()
    for at, (context, (source, tiles, position)) in enumerate(zip(arrived, orders)):
        state = attend(
            at == 0,
            at == len(splits) - 1,
            source,
            tiles,
            sel_column,
            position,
            queries[0],
            state,
            context,
        )
    return (state[0][None], store_out)


def solution(mesh):
    return jax.shard_map(
        per_device,
        mesh=mesh,
        in_specs=(
            P(("groups", "store"), None, None),
            P(("groups", "store"), None),
            P(("groups", "store"), None),
            P(("groups", "store"), None, None),
            P(("groups", "store"), None, None),
        ),
        out_specs=(P(("groups", "store"), None, None), P(("groups", "store"), None, None)),
        check_vma=False,
    )
```

profile of v0, /device:TPU:9, one launch (start us, length us, event | category | flops | bytes accessed | tf_op | source)
XLA Modules:
  0.0 205.7 jit_solution(9918213546552898170)
XLA Ops:
  0.6 1.0 copy-done.9
  1.6 0.7 copy-done.10
  2.3 0.7 copy-done.12
  2.9 0.7 shard_map.68
  3.6 22.3 %all_to_all.15.entries_ref = bf16[16,144,128]{2,1,0:T(8,128)(2,1)S(1)} all-to-all(bf16[16,144,128]{2,1,0:T(8,128)(2,1)S(1)} %shard_map.68), channel_id=1, replica_groups=mesh['groups'=2,'store'=16] {'store'}, dimensions={0} | all-to-all | bytes 1179648 | tf_op jit(solution)/shard_map/all_to_all | solution.py:310
  25.9 2.2 %copy-done = bf16[128,16,1024]{2,1,0:T(8,128)(2,1)S(1)} copy-done((bf16[128,16,1024]{2,1,0:T(8,128)(2,1)S(1)}, bf16[128,16,1024]{2,1,0:T(8,128)(2,1)}, u32[]{:S(2)}) %copy-start) | copy-done | bytes 4194328
  28.1 8.7 %shard_map.69 = (bf16[128,16,1024]{2,1,0:T(8,128)(2,1)}, bf16[16,6,16,1024]{3,2,1,0:T(8,128)(2,1)S(1)}, bf16[16,2,16,1024]{3,2,1,0:T(8,128)(2,1)S(1)}) custom-call(bf16[16,144,128]{2,1,0:T(8,128)(2,1)S(1)} %all_to_all.15.entries_ref, bf16[128,16,1024]{2,1,0:T(8,128)(2,1)S(1)} %copy-done), custom_call_target="tpu_custom_call" | custom-call | tf_op jit(solution)/shard_map/pallas_call | solution.py:314
  36.8 1.7 copy-done.5
  38.5 1.0 copy-done.8
  39.4 5.1 %all-to-all-start.1 = ((bf16[16,6,16,1024]{3,2,1,0:T(8,128)(2,1)}), bf16[16,6,16,1024]{3,2,1,0:T(8,128)(2,1)S(1)}, u32[]{:S(2)}, u32[]{:S(2)}) async-start(bf16[16,6,16,1024]{3,2,1,0:T(8,128)(2,1)} %copy-done.5), calls=%async_computation.1 | async-start | bytes 6291456 | tf_op jit(solution)/shard_map/all_to_all | solution.py:340
  44.5 0.5 broadcast.195
  45.0 0.6 reduce.3
  45.9 0.2 convert_reduce_fusion.2
  46.7 65.7 %all-to-all-done.1 = bf16[16,6,16,1024]{3,2,1,0:T(8,128)(2,1)S(1)} async-done(((bf16[16,6,16,1024]{3,2,1,0:T(8,128)(2,1)}), bf16[16,6,16,1024]{3,2,1,0:T(8,128)(2,1)S(1)}, u32[]{:S(2)}, u32[]{:S(2)}) %all-to-all-start.1) | async-done | bytes 3145760 | tf_op jit(solution)/shard_map/all_to_all | solution.py:340
  112.4 1.7 copy-done.3
  114.0 7.0 %all-to-all-start.2 = ((bf16[16,2,16,1024]{3,2,1,0:T(8,128)(2,1)}), bf16[16,2,16,1024]{3,2,1,0:T(8,128)(2,1)S(1)}, u32[]{:S(2)}, u32[]{:S(2)}) async-start(bf16[16,2,16,1024]{3,2,1,0:T(8,128)(2,1)} %copy-done.8), calls=%async_computation.2 | async-start | bytes 2097152 | tf_op jit(solution)/shard_map/all_to_all | solution.py:340
  121.2 0.2 convert_reduce_fusion.3
  121.4 0.2 convert_reduce_fusion.4
  121.6 1.9 copy-done.4
  123.5 1.5 copy-done.6
  125.0 60.5 %shard_map.70 = (f32[160,6144]{1,0:T(8,128)S(1)}, f32[160,128]{1,0:T(8,128)S(1)}, f32[160,128]{1,0:T(8,128)S(1)}) custom-call(s32[96]{0:T(128)S(1)} %get-tuple-element.15.source_ref, s32[5]{0:T(128)S(1)} %and_select_fusion.tiles_ref, s32[160,1]{1,0:T(8,128)S(1)} %copy.13.sel_ref, s32[1,1536]{1,0:T(1,128)S(1)} %add.85.position_ref, ...), custom_call_target="tpu_custom_call" | custom-call | flops 7247757312 | bytes 9043968 | tf_op jit(solution)/shard_map/pallas_call | solution.py:238
  185.6 1.9 copy-done.1
  187.4 2.1 %copy-done.2 = f32[160,6144]{1,0:T(8,128)S(1)} copy-done((f32[160,6144]{1,0:T(8,128)S(1)}, f32[160,6144]{1,0:T(8,128)}, u32[]{:S(2)}) %copy-start.2) | copy-done | bytes 3932184
  189.6 16.2 %shard_map.71 = bf16[160,6144]{1,0:T(8,128)(2,1)} custom-call(s32[32]{0:T(128)S(1)} %get-tuple-element.17.source_ref, s32[5]{0:T(128)S(1)} %and_select_fusion.1.tiles_ref, s32[160,1]{1,0:T(8,128)S(1)} %copy.13.sel_ref, s32[1,512]{1,0:T(1,128)S(1)} %add.80.position_ref, bf16[160,6144]{1,0:T(8,128)(2,1)S(1)} %bitcast.34, f32[160,6144]{1,0:T(8,128)S(1)} %copy-done.2, ...), custom_call_target="tpu_custom_call" | custom-call | flops 2415919104 | bytes 6946816 | tf_op jit(solution)/shard_map/pallas_call | solution.py:238
  (38 shorter events, 1.1 us)
Async XLA Ops:
  0.6 1.0 copy-start.9
  1.6 0.7 copy-start.10
  2.3 0.7 copy-start.12
  25.9 2.2 %copy-start = (bf16[128,16,1024]{2,1,0:T(8,128)(2,1)S(1)}, bf16[128,16,1024]{2,1,0:T(8,128)(2,1)}, u32[]{:S(2)}) copy-start(bf16[128,16,1024]{2,1,0:T(8,128)(2,1)} %store_ref.1) | copy-start | bytes 12582916
  36.8 1.7 copy-start.5
  38.5 1.0 copy-start.8
  39.4 5.6 %copy-start.11 = (s32[1,160]{1,0:T(1,128)S(1)}, s32[1,160]{1,0:T(1,128)}, u32[]{:S(2)}) copy-start(s32[1,160]{1,0:T(1,128)} %sel_ref.1) | copy-start | bytes 1924
  39.4 6.4 %copy-start.13 = (s32[1,128]{1,0:T(1,128)S(1)}, s32[1,128]{1,0:T(1,128)}, u32[]{:S(2)}) copy-start(s32[1,128]{1,0:T(1,128)} %table_ref.1) | copy-start | bytes 1540
  39.4 72.9 %all-to-all-start.1 = ((bf16[16,6,16,1024]{3,2,1,0:T(8,128)(2,1)}), bf16[16,6,16,1024]{3,2,1,0:T(8,128)(2,1)S(1)}, u32[]{:S(2)}, u32[]{:S(2)}) async-start(bf16[16,6,16,1024]{3,2,1,0:T(8,128)(2,1)} %copy-done.5), calls=%async_computation.1 | async-start | bytes 6291456 | tf_op jit(solution)/shard_map/all_to_all | solution.py:340
  112.4 1.7 copy-start.3
  114.0 73.4 %all-to-all-start.2 = ((bf16[16,2,16,1024]{3,2,1,0:T(8,128)(2,1)}), bf16[16,2,16,1024]{3,2,1,0:T(8,128)(2,1)S(1)}, u32[]{:S(2)}, u32[]{:S(2)}) async-start(bf16[16,2,16,1024]{3,2,1,0:T(8,128)(2,1)} %copy-done.8), calls=%async_computation.2 | async-start | bytes 2097152 | tf_op jit(solution)/shard_map/all_to_all | solution.py:340
  121.6 1.9 copy-start.4
  123.5 1.5 copy-start.6
  125.0 62.4 %copy-start.7 = (bf16[1,160,6144]{2,1,0:T(8,128)(2,1)S(1)}, bf16[1,160,6144]{2,1,0:T(8,128)(2,1)}, u32[]{:S(2)}) copy-start(bf16[1,160,6144]{2,1,0:T(8,128)(2,1)} %param.9) | copy-start | bytes 5898244
  185.6 1.9 copy-start.1
  187.4 2.1 %copy-start.2 = (f32[160,6144]{1,0:T(8,128)S(1)}, f32[160,6144]{1,0:T(8,128)}, u32[]{:S(2)}) copy-start(f32[160,6144]{1,0:T(8,128)} %copy-done.1) | copy-start | bytes 11796484
where the time goes:
time: 207 us; the launch traced here: 206 us
  Pallas kernels  86 us (42%)
  waiting for transfers between devices  65.7 us (32%)
  blocking collectives  22.3 us (11%)
  local copies, waits for them, and re-layouts  17.2 us (8%)
  starting transfers between devices  12 us (6%)
    pallas_call x2, Pallas kernels, attend(): pl.pallas_call(functools.partial(attend_kernel, first, last), grid_spec=p...  76.7 us
    all_to_all x2, waiting for transfers between devices, per_device(): lax.all_to_all(part, 'store', split_axis=0, concat_axis=0, tiled=True)  65.7 us
    all_to_all x1, blocking collectives, per_device(): lax.all_to_all(packed, 'store', split_axis=0, concat_axis=0, tiled=True)  22.3 us
    unnamed x30, local copies, waits for them, and re-layouts  16.8 us
    all_to_all x2, starting transfers between devices, per_device(): lax.all_to_all(part, 'store', split_axis=0, concat_axis=0, tiled=True)  12 us
    pallas_call x1, Pallas kernels, per_device(): pl.pallas_call(functools.partial(apply_kernel, splits, row_slots), out_sh...  8.65 us
  transfers between devices with their start and end apart: 2, of which 1 were waited for; matrix products, arithmetic and copies ran while one was open for 1% of the time, Pallas kernels for 29%

commit v1 on v0

v1 whole, which is shorter than its diff:
```python
import functools

import jax
import jax.numpy as jnp
from jax import lax
from jax.experimental import pallas as pl
from jax.experimental.pallas import tpu as pltpu
from jax.sharding import PartitionSpec as P

HEAD_WIDTH = 128
KEY_VALUE_HEADS = 4
QUERY_GROUP = 12
SELP = 2
LANES = 128
VMEM_LIMIT = 60 * 1024 * 1024
QUERY_BLOCK = 32
TILE_PAGES = 16
HIDDEN = -1e30


def nt_dot(a, b):
    return lax.dot_general(a, b, (((1,), (1,)), ((), ())), preferred_element_type=jnp.float32)


def plan_kernel(hold, holders, row_slots, page_len, table_ref, sel_ref, fresh_ref, out_ref, wide):
    pages = table_ref.shape[1]
    picked = sel_ref.shape[1]
    wide_lanes = wide.shape[1]
    chunks = fresh_ref.shape[1] // LANES
    f32 = jnp.float32
    slot_row = jnp.broadcast_to(table_ref[...], (pages, pages))
    owner_row = slot_row // hold
    local_row = (slot_row - owner_row * hold).astype(f32)
    owner_row = owner_row.astype(f32)
    owner_col = owner_row.T
    sub = lax.broadcasted_iota(jnp.int32, (pages, pages), 0)
    lane = lax.broadcasted_iota(jnp.int32, (pages, pages), 1)
    earlier = jnp.where((owner_row == owner_col) & (lane < sub), 1.0, 0.0)
    rank_col = jnp.sum(earlier, axis=1, keepdims=True)
    owner_col = owner_col[:, 0:1]

    holder = lax.broadcasted_iota(jnp.int32, (holders, pages), 0).astype(f32)
    owned = jnp.where(holder == owner_row[0:1, :], local_row[0:1, :], 0.0)
    at_rank = jnp.where(lane.astype(f32) == rank_col, 1.0, 0.0)
    numbers = jnp.dot(
        owned.astype(jnp.bfloat16), at_rank.astype(jnp.bfloat16), preferred_element_type=f32
    )

    wide[...] = jnp.full(wide.shape, -1, jnp.int32)
    wide[0:1, 0:picked] = sel_ref[...]
    position = wide[...]
    page = lax.shift_right_arithmetic(position, page_len.bit_length() - 1)
    offset = (position & (page_len - 1)).astype(f32)
    lane8 = lax.broadcasted_iota(jnp.int32, wide.shape, 1)
    second = jnp.where((page == pltpu.roll(page, 1, axis=1)) & (lane8 > 0), 1.0, 0.0)
    page, offset, second = page[0:1], offset[0:1], second[0:1]
    valid = lane8[0:1] < picked
    sub_wide = lax.broadcasted_iota(jnp.int32, (pages, wide_lanes), 0)
    in_page = jnp.where(sub_wide == page, 1.0, 0.0)
    owner = jnp.sum(in_page * owner_col, axis=0, keepdims=True)
    rank = jnp.sum(in_page * rank_col, axis=0, keepdims=True)
    place = SELP * rank + second
    spot = jnp.where(valid, owner * row_slots + place, -1.0)

    holder_wide = lax.broadcasted_iota(jnp.int32, (holders, wide_lanes), 0).astype(f32)
    marked = jnp.where((holder_wide == owner) & valid, rank * page_len + offset + 1.0, 0.0)
    place_lane = lax.broadcasted_iota(jnp.int32, (LANES, wide_lanes), 0).astype(f32)
    at_place = jnp.where(place_lane == place, 1.0, 0.0)
    targets = nt_dot(marked.astype(jnp.bfloat16), at_place.astype(jnp.bfloat16))

    spot_row = spot[:, 0:picked]
    spots = holders * row_slots
    step = min(spots, 256)
    for start in range(0, spots, step):
        spot_id = lax.broadcasted_iota(jnp.int32, (step, picked), 0).astype(f32) + float(start)
        choose = jnp.where(spot_id == spot_row, 1.0, 0.0).astype(jnp.bfloat16)
        rows = jnp.dot(choose, fresh_ref[...], preferred_element_type=f32).astype(jnp.bfloat16)
        for h in range(step // row_slots):
            for c in range(chunks):
                out_ref[start // row_slots + h, c * row_slots : (c + 1) * row_slots, :] = rows[
                    h * row_slots : (h + 1) * row_slots, c * LANES : (c + 1) * LANES
                ]
    sub16 = lax.broadcasted_iota(jnp.int32, (16, LANES), 0)
    for h in range(holders):
        block = jnp.where(sub16 == 0, numbers[h : h + 1, :], 0.0)
        block = jnp.where(sub16 == 1, targets[h : h + 1, :], block)
        out_ref[h, chunks * row_slots :, :] = block.astype(jnp.bfloat16)


def blend_kernel(splits, row_slots, entries_hbm, store_hbm, *rest):
    sends, numbers_out = rest[: len(splits)], rest[len(splits)]
    store, blended, entries, numbers, load_sem, index_sem, entries_sem, send_sem = rest[len(splits) + 1 :]
    holders, capacity, page_len, width = blended.shape
    chunks = width // LANES
    rows_here = capacity * page_len
    f32 = jnp.float32
    load = pltpu.make_async_copy(store_hbm, store, load_sem)
    arrive = pltpu.make_async_copy(entries_hbm, entries, entries_sem)
    arrive.start()
    load.start()
    arrive.wait()

    def index_row(r, carry):
        block = entries[r, chunks * row_slots :, :].astype(f32).astype(jnp.int32)
        numbers_out[pl.ds(r, 1), :] = block[0:1, :]
        return carry

    lax.fori_loop(0, holders, index_row, 0)
    index_copy = pltpu.make_async_copy(numbers_out, numbers, index_sem)
    index_copy.start()
    index_copy.wait()
    load.wait()

    row_id = lax.broadcasted_iota(jnp.int32, (rows_here, row_slots), 0).astype(f32)

    def one_request(r, carry):
        targets = entries[r, chunks * row_slots :, :].astype(f32)[1:2, 0:row_slots] - 1.0
        hit = jnp.where(row_id == targets, 1.0, 0.0)
        keep = 1.0 - jnp.sum(hit, axis=1, keepdims=True)
        keep = jnp.broadcast_to(keep, (rows_here, LANES)).astype(jnp.bfloat16)
        hit = hit.astype(jnp.bfloat16)
        for c in range(chunks):
            lanes = slice(c * LANES, (c + 1) * LANES)
            rows = entries[r, c * row_slots : (c + 1) * row_slots, :]
            fresh = jnp.dot(hit, rows, preferred_element_type=f32).astype(jnp.bfloat16)
            for k in range(capacity):
                part = slice(k * page_len, (k + 1) * page_len)
                blended[r, k, :, lanes] = store[numbers[r, k], :, lanes] * keep[part] + fresh[part]
        for (low, high), send in zip(splits, sends):
            pltpu.make_async_copy(blended.at[r, pl.ds(low, high - low)], send.at[r], send_sem).start()
        return carry

    lax.fori_loop(0, holders, one_request, 0)
    for send in sends:
        pltpu.make_async_copy(send, send, send_sem).wait()


def write_back_kernel(splits, numbers, *rest):
    sends, store_out, sem = rest[: len(splits)], rest[len(splits)], rest[len(splits) + 1]
    holders = numbers.shape[0]

    def one_request(r, carry):
        for (low, high), send in zip(splits, sends):
            for k in range(low, high):
                pltpu.make_async_copy(send.at[r, k - low], store_out.at[numbers[r, k]], sem).start()
        return carry

    lax.fori_loop(0, holders, one_request, 0)
    pltpu.make_async_copy(store_out, store_out, sem).wait()


def attend_kernel(first, last, source, page_number, tiles, sel_ref, query_ref, *rest):
    rest = list(rest)
    state_in = [] if first else [rest.pop(0) for _ in range(2)]
    context = rest.pop(0)
    outs = [rest.pop(0) for _ in range(1 if last else 2)]
    kv, values, query, mixed, stats, sem = rest
    pages, page_len = context.shape[0], context.shape[1]
    block = query_ref.shape[0]
    tile = TILE_PAGES * page_len
    lanes = QUERY_GROUP * block
    scale = 1.4426950408889634 / HEAD_WIDTH**0.5
    f32 = jnp.float32
    step = pl.program_id(0)
    eye = jnp.where(
        lax.broadcasted_iota(jnp.int32, (LANES, LANES), 0)
        == lax.broadcasted_iota(jnp.int32, (LANES, LANES), 1),
        1.0,
        0.0,
    ).astype(jnp.bfloat16)

    @pl.when(step == 0)
    def _():
        def fetch(i, carry):
            pltpu.make_async_copy(context.at[source[i]], kv.at[i], sem).start()
            return carry

        lax.fori_loop(0, pages, fetch, 0)
        pltpu.make_async_copy(context, kv, sem).wait()

        def turn(t, carry):
            here = pl.ds(t * TILE_PAGES, TILE_PAGES)
            for g in range(KEY_VALUE_HEADS):
                at = (KEY_VALUE_HEADS + g) * LANES
                value = kv[here, :, at : at + LANES].reshape(tile, LANES)
                values[t, g] = nt_dot(eye, value).astype(jnp.bfloat16)
            return carry

        lax.fori_loop(0, pages // TILE_PAGES, turn, 0)

    for g in range(KEY_VALUE_HEADS):
        for i in range(QUERY_GROUP):
            head = g * QUERY_GROUP + i
            query[g, i * block : (i + 1) * block, :] = query_ref[:, head * LANES : (head + 1) * LANES]
    if first:
        mixed[...] = jnp.zeros(mixed.shape, f32)
        stats[0:KEY_VALUE_HEADS, :] = jnp.full((KEY_VALUE_HEADS, lanes), HIDDEN, f32)
        stats[KEY_VALUE_HEADS:, :] = jnp.zeros((KEY_VALUE_HEADS, lanes), f32)
    else:
        mixed[...] = state_in[0][0]
        stats[...] = state_in[1][0]

    sel = sel_ref[0]
    in_page = lax.broadcasted_iota(jnp.int32, (page_len, LANES), 0)

    def one_tile(t, carry):
        here = pl.ds(t * TILE_PAGES, TILE_PAGES)
        bias = jnp.concatenate(
            [
                jnp.where(in_page + page_number[t * TILE_PAGES + k] * page_len <= sel, 0.0, HIDDEN)
                for k in range(TILE_PAGES)
            ],
            axis=0,
        ).astype(f32)
        scores = []
        for g in range(KEY_VALUE_HEADS):
            key = kv[here, :, g * LANES : (g + 1) * LANES].reshape(tile, LANES)
            scores.append(nt_dot(key, query[g]))
        for g in range(KEY_VALUE_HEADS):
            raised, shrinks = [], []
            for n in range(lanes // LANES):
                part = slice(n * LANES, (n + 1) * LANES)
                s = scores[g][:, part] + bias
                old = stats[g : g + 1, part]
                new = jnp.maximum(old, jnp.max(s, axis=0, keepdims=True))
                p = jnp.exp2((s - new) * scale)
                shrink = jnp.exp2((old - new) * scale)
                at = KEY_VALUE_HEADS + g
                stats[at : at + 1, part] = stats[at : at + 1, part] * shrink + jnp.sum(
                    p, axis=0, keepdims=True
                )
                stats[g : g + 1, part] = new
                raised.append(p.astype(jnp.bfloat16))
                shrinks.append(shrink)
            raised = jnp.concatenate(raised, axis=1)
            shrink = jnp.concatenate(shrinks, axis=1)
            mixed[g] = mixed[g] * shrink + jnp.dot(
                values[t, g], raised, preferred_element_type=f32
            )
        return carry

    lax.fori_loop(0, tiles[step], one_tile, 0)

    if last:
        for g in range(KEY_VALUE_HEADS):
            at = KEY_VALUE_HEADS + g
            done = (mixed[g] * (1.0 / stats[at : at + 1, :])).astype(jnp.bfloat16)
            for n in range(lanes // LANES):
                turned = nt_dot(eye, done[:, n * LANES : (n + 1) * LANES]).astype(jnp.bfloat16)
                for i in range(LANES // block):
                    head = g * QUERY_GROUP + n * (LANES // block) + i
                    outs[0][:, head * LANES : (head + 1) * LANES] = turned[
                        i * block : (i + 1) * block, :
                    ]
    else:
        outs[0][0] = mixed[...]
        outs[1][0] = stats[...]


def attend(first, last, order, sel_lanes, queries, state, context):
    picked, features = queries.shape
    pages, page_len, width = context.shape
    steps = picked // QUERY_BLOCK
    lanes = QUERY_GROUP * QUERY_BLOCK
    wide = pl.BlockSpec((QUERY_BLOCK, features), lambda b, *_: (b, 0))
    state_specs = [
        pl.BlockSpec((1, KEY_VALUE_HEADS, LANES, lanes), lambda b, *_: (b, 0, 0, 0)),
        pl.BlockSpec((1, 2 * KEY_VALUE_HEADS, lanes), lambda b, *_: (b, 0, 0)),
    ]
    state_shapes = [
        jax.ShapeDtypeStruct((steps, KEY_VALUE_HEADS, LANES, lanes), jnp.float32),
        jax.ShapeDtypeStruct((steps, 2 * KEY_VALUE_HEADS, lanes), jnp.float32),
    ]
    share = 0.6
    return pl.pallas_call(
        functools.partial(attend_kernel, first, last),
        grid_spec=pltpu.PrefetchScalarGridSpec(
            num_scalar_prefetch=3,
            grid=(steps,),
            in_specs=[
                pl.BlockSpec((1, 1, LANES), lambda b, *_: (b, 0, 0)),
                wide,
                *([] if first else state_specs),
                pl.BlockSpec(memory_space=pltpu.HBM),
            ],
            out_specs=[wide] if last else state_specs,
            scratch_shapes=[
                pltpu.VMEM((pages, page_len, width), jnp.bfloat16),
                pltpu.VMEM(
                    (pages // TILE_PAGES, KEY_VALUE_HEADS, LANES, TILE_PAGES * page_len), jnp.bfloat16
                ),
                pltpu.VMEM((KEY_VALUE_HEADS, lanes, LANES), jnp.bfloat16),
                pltpu.VMEM((KEY_VALUE_HEADS, LANES, lanes), jnp.float32),
                pltpu.VMEM((2 * KEY_VALUE_HEADS, lanes), jnp.float32),
                pltpu.SemaphoreType.DMA,
            ],
        ),
        out_shape=[jax.ShapeDtypeStruct((picked, features), jnp.bfloat16)] if last else state_shapes,
        compiler_params=pltpu.CompilerParams(
            dimension_semantics=("arbitrary",), vmem_limit_bytes=VMEM_LIMIT
        ),
        cost_estimate=pl.CostEstimate(
            flops=int(share * 8 * picked * features * pages * page_len),
            bytes_accessed=2 * pages * page_len * width + 6 * picked * features,
            transcendentals=int(share * picked * features // LANES * pages * page_len),
        ),
    )(*order, sel_lanes, queries, *state, context)


def page_order(slots, positions, hold, splits, page_len):
    pages = slots.shape[0]
    number = jnp.arange(pages)
    before = number[None, :] < number[:, None]
    owners = slots // hold
    ranks = jnp.sum(((owners[None, :] == owners[:, None]) & before).astype(jnp.int32), axis=1)
    last_page = positions.reshape(-1, QUERY_BLOCK)[:, -1] // page_len
    orders = []
    for low, high in splits:
        member = (ranks >= low) & (ranks < high)
        count = pages * (high - low) // splits[-1][1]
        place = jnp.sum((member[None, :] & before).astype(jnp.int32), axis=1)
        hit = (member[None, :] & (place[None, :] == jnp.arange(count)[:, None])).astype(jnp.int32)
        source = jnp.sum(hit * (owners * (high - low) + ranks - low)[None, :], axis=1)
        page = jnp.sum(hit * number[None, :], axis=1)
        seen = jnp.sum((page[None, :] <= last_page[:, None]).astype(jnp.int32), axis=1)
        orders.append((source, page, (seen + TILE_PAGES - 1) // TILE_PAGES))
    return orders


def per_device(store, page_table, sel_pos, fresh_kv, queries):
    holders = lax.axis_size("store")
    hold, page_len, width = store.shape
    pages = page_table.shape[1]
    picked = sel_pos.shape[1]
    capacity = max(1, pages // holders)
    row_slots = -(-SELP * capacity // 16) * 16
    chunks = width // LANES
    packed_rows = chunks * row_slots + 16
    late = capacity // 4
    splits = ((0, capacity - late), (capacity - late, capacity)) if late else ((0, capacity),)
    hbm = pl.BlockSpec(memory_space=pltpu.HBM)
    vmem = pl.BlockSpec(memory_space=pltpu.VMEM)
    params = pltpu.CompilerParams(vmem_limit_bytes=VMEM_LIMIT)

    packed = pl.pallas_call(
        functools.partial(plan_kernel, hold, holders, row_slots, page_len),
        out_shape=jax.ShapeDtypeStruct((holders, packed_rows, LANES), jnp.bfloat16),
        scratch_shapes=[pltpu.VMEM((8, -(-picked // LANES) * LANES), jnp.int32)],
        compiler_params=params,
    )(page_table, sel_pos, fresh_kv[0])
    entries = lax.all_to_all(packed, "store", split_axis=0, concat_axis=0, tiled=True)

    *parts, numbers = pl.pallas_call(
        functools.partial(blend_kernel, splits, row_slots),
        out_shape=[
            *[
                jax.ShapeDtypeStruct((holders, high - low, page_len, width), store.dtype)
                for low, high in splits
            ],
            jax.ShapeDtypeStruct((holders, LANES), jnp.int32),
        ],
        in_specs=[hbm, hbm],
        out_specs=[hbm] * len(splits) + [vmem],
        scratch_shapes=[
            pltpu.VMEM(store.shape, store.dtype),
            pltpu.VMEM((holders, capacity, page_len, width), store.dtype),
            pltpu.VMEM((holders, packed_rows, LANES), store.dtype),
            pltpu.SMEM((holders, LANES), jnp.int32),
            pltpu.SemaphoreType.DMA,
            pltpu.SemaphoreType.DMA,
            pltpu.SemaphoreType.DMA,
            pltpu.SemaphoreType.DMA,
        ],
        compiler_params=params,
    )(entries, store)

    store_out = pl.pallas_call(
        functools.partial(write_back_kernel, splits),
        grid_spec=pltpu.PrefetchScalarGridSpec(
            num_scalar_prefetch=1,
            grid=(1,),
            in_specs=[hbm] * len(splits),
            out_specs=hbm,
            scratch_shapes=[pltpu.SemaphoreType.DMA],
        ),
        out_shape=jax.ShapeDtypeStruct(store.shape, store.dtype),
        compiler_params=params,
        cost_estimate=pl.CostEstimate(flops=0, bytes_accessed=4 * store.size, transcendentals=0),
    )(numbers, *parts)

    orders = page_order(page_table[0], sel_pos[0], hold, splits, page_len)
    sel_lanes = jnp.tile(sel_pos.reshape(-1, 1, QUERY_BLOCK), (1, 1, LANES // QUERY_BLOCK))
    arrived = [
        lax.all_to_all(part, "store", split_axis=0, concat_axis=0, tiled=True).reshape(
            -1, page_len, width
        )
        for part in parts
    ]
    state = ()
    for at, (context, order) in enumerate(zip(arrived, orders)):
        state = attend(
            at == 0, at == len(splits) - 1, order, sel_lanes, queries[0], state, context
        )
    return (state[0][None], store_out)


def solution(mesh):
    return jax.shard_map(
        per_device,
        mesh=mesh,
        in_specs=(
            P(("groups", "store"), None, None),
            P(("groups", "store"), None),
            P(("groups", "store"), None),
            P(("groups", "store"), None, None),
            P(("groups", "store"), None, None),
        ),
        out_specs=(P(("groups", "store"), None, None), P(("groups", "store"), None, None)),
        check_vma=False,
    )
```

time: 207 us -> 287 us (1.39)
  Pallas kernels: 86 us -> 175 us
  local copies, waits for them, and re-layouts: 17.2 us -> 4.12 us
    pallas_call x1 -> x2, Pallas kernels: 8.65 us -> 136 us  [the longest x1 129 us: per_device(): pl.pallas_call(functools.partial(write_back_kernel, splits), grid_spec=pl...]
    pallas_call x2, Pallas kernels: 76.7 us -> 36.8 us  [attend(): pl.pallas_call(functools.partial(attend_kernel, first, last), grid_spec=p...]
    unnamed x30 -> x14, local copies, waits for them, and re-layouts: 16.8 us -> 3.28 us
  transfers between devices with their start and end apart: 2 -> 2, of which waited for: 1 -> 1; matrix products, arithmetic and copies ran while one was open for 1% -> 2% of each run, Pallas kernels for 29% -> 54%
where the time goes in v1:
time: 287 us; the launch traced here: 286 us
  Pallas kernels  175 us (61%)
  waiting for transfers between devices  67.6 us (24%)
  blocking collectives  22.7 us (8%)
  starting transfers between devices  11.9 us (4%)
  local copies, waits for them, and re-layouts  4.12 us (1%)
  other arithmetic  3.81 us (1%)
    pallas_call x1, Pallas kernels, per_device(): pl.pallas_call(functools.partial(write_back_kernel, splits), grid_spec=pl...  129 us
    all_to_all x2, waiting for transfers between devices, per_device(): lax.all_to_all(part, 'store', split_axis=0, concat_axis=0, tiled=True)  67.6 us
    pallas_call x2, Pallas kernels, attend(): pl.pallas_call(functools.partial(attend_kernel, first, last), grid_spec=p...  36.8 us
    all_to_all x1, blocking collectives, per_device(): lax.all_to_all(packed, 'store', split_axis=0, concat_axis=0, tiled=True)  22.7 us
    all_to_all x2, starting transfers between devices, per_device(): lax.all_to_all(part, 'store', split_axis=0, concat_axis=0, tiled=True)  11.9 us
    pallas_call x1, Pallas kernels, per_device(): pl.pallas_call(functools.partial(blend_kernel, splits, row_slots), out_sh...  6.96 us
  transfers between devices with their start and end apart: 2, of which 1 were waited for; matrix products, arithmetic and copies ran while one was open for 2% of the time, Pallas kernels for 54%

profile of v1, /device:TPU:9, one launch (start us, length us, event | category | flops | bytes accessed | tf_op | source)
XLA Modules:
  0.0 285.9 jit_solution(16767203155849522041)
XLA Ops:
  0.6 2.3 shard_map.68
  3.0 22.7 %all_to_all.15.entries_hbm = bf16[16,144,128]{2,1,0:T(8,128)(2,1)} all-to-all(bf16[16,144,128]{2,1,0:T(8,128)(2,1)} %shard_map.68), channel_id=1, replica_groups=mesh['groups'=2,'store'=16] {'store'}, dimensions={0} | all-to-all | bytes 1179648 | tf_op jit(solution)/shard_map/all_to_all | solution.py:351
  25.6 7.0 %shard_map.69 = (bf16[16,6,16,1024]{3,2,1,0:T(8,128)(2,1)}, bf16[16,2,16,1024]{3,2,1,0:T(8,128)(2,1)}, s32[16,128]{1,0:T(8,128)}) custom-call(bf16[16,144,128]{2,1,0:T(8,128)(2,1)} %all_to_all.15.entries_hbm, bf16[128,16,1024]{2,1,0:T(8,128)(2,1)} %store_hbm.1), custom_call_target="tpu_custom_call" | custom-call | tf_op jit(solution)/shard_map/pallas_call | solution.py:353
  32.6 5.0 %all-to-all-start.1 = ((bf16[16,6,16,1024]{3,2,1,0:T(8,128)(2,1)}), bf16[16,6,16,1024]{3,2,1,0:T(8,128)(2,1)S(1)}, u32[]{:S(2)}, u32[]{:S(2)}) async-start(bf16[16,6,16,1024]{3,2,1,0:T(8,128)(2,1)} %get-tuple-element.7.rest_0_), calls=%async_computation.1 | async-start | bytes 6291456 | tf_op jit(solution)/shard_map/all_to_all | solution.py:394
  37.6 0.2 convert_reduce_fusion.2
  37.8 67.6 %all-to-all-done.1 = bf16[16,6,16,1024]{3,2,1,0:T(8,128)(2,1)S(1)} async-done(((bf16[16,6,16,1024]{3,2,1,0:T(8,128)(2,1)}), bf16[16,6,16,1024]{3,2,1,0:T(8,128)(2,1)S(1)}, u32[]{:S(2)}, u32[]{:S(2)}) %all-to-all-start.1) | async-done | bytes 3145760 | tf_op jit(solution)/shard_map/all_to_all | solution.py:394
  105.4 1.7 copy-done.1
  107.1 7.0 %all-to-all-start.2 = ((bf16[16,2,16,1024]{3,2,1,0:T(8,128)(2,1)}), bf16[16,2,16,1024]{3,2,1,0:T(8,128)(2,1)S(1)}, u32[]{:S(2)}, u32[]{:S(2)}) async-start(bf16[16,2,16,1024]{3,2,1,0:T(8,128)(2,1)} %get-tuple-element.10.rest_1_), calls=%async_computation.2 | async-start | bytes 2097152 | tf_op jit(solution)/shard_map/all_to_all | solution.py:394
  114.1 0.5 broadcast.180
  114.6 0.7 reduce.3
  115.2 0.1 reshape_squeeze.3
  115.4 0.1 copy.9
  115.5 0.7 tile.9.sel_ref
  116.2 0.1 convert_reduce_fusion
  116.3 0.7 select_reduce_fusion.2
  117.0 0.2 convert_reduce_fusion.4
  117.2 0.6 select_reduce_fusion
  117.8 0.2 convert_reduce_fusion.3
  118.0 0.6 and_select_fusion.1.tiles
  118.6 0.6 and_select_fusion.tiles
  119.1 129.0 %shard_map.72 = bf16[128,16,1024]{2,1,0:T(8,128)(2,1)} custom-call(s32[16,128]{1,0:T(8,128)} %get-tuple-element.11.numbers, bf16[16,6,16,1024]{3,2,1,0:T(8,128)(2,1)} %get-tuple-element.7.rest_0_, bf16[16,2,16,1024]{3,2,1,0:T(8,128)(2,1)} %get-tuple-element.10.rest_1_), custom_call_target="tpu_custom_call" | custom-call | bytes 8388608 | tf_op jit(solution)/shard_map/pallas_call | solution.py:377
  248.1 25.6 %shard_map.70 = (f32[5,4,128,384]{3,2,1,0:T(8,128)}, f32[5,8,384]{2,1,0:T(8,128)}) custom-call(s32[96]{0:T(128)} %get-tuple-element.13.source, s32[96]{0:T(128)} %copy-done.5, s32[5]{0:T(128)} %and_select_fusion.tiles, s32[5,1,128]{2,1,0:T(1,128)} %tile.9.sel_ref, bf16[160,6144]{1,0:T(8,128)(2,1)} %bitcast.32, bf16[96,16,1024]{2,1,0:T(8,128)(2,1)} %bitcast.31), custom_call_target="tpu_custom_call" | custom-call | flops 7247757312 | bytes 9043968 | tf_op jit(solution)/shard_map/pallas_call | solution.py:275
  273.7 1.0 copy-done
  274.7 11.2 %shard_map.71 = bf16[160,6144]{1,0:T(8,128)(2,1)} custom-call(s32[32]{0:T(128)} %get-tuple-element.15.source, s32[32]{0:T(128)} %copy-done.3, s32[5]{0:T(128)} %and_select_fusion.1.tiles, s32[5,1,128]{2,1,0:T(1,128)} %tile.9.sel_ref, bf16[160,6144]{1,0:T(8,128)(2,1)} %bitcast.33, f32[5,4,128,384]{3,2,1,0:T(8,128)} %get-tuple-element.8.rest_0_, ...), custom_call_target="tpu_custom_call" | custom-call | flops 2415919104 | bytes 6946816 | tf_op jit(solution)/shard_map/pallas_call | solution.py:275
  (18 shorter events, 0.2 us)
Async XLA Ops:
  32.6 5.0 %copy-start.4 = (s32[1,128]{1,0:T(1,128)S(1)}, s32[1,128]{1,0:T(1,128)}, u32[]{:S(2)}) copy-start(s32[1,128]{1,0:T(1,128)} %table_ref.1) | copy-start | bytes 1540
  32.6 82.0 %copy-start.2 = (s32[1,160]{1,0:T(1,128)S(1)}, s32[1,160]{1,0:T(1,128)}, u32[]{:S(2)}) copy-start(s32[1,160]{1,0:T(1,128)} %sel_ref.1) | copy-start | bytes 1924
  32.6 72.8 %all-to-all-start.1 = ((bf16[16,6,16,1024]{3,2,1,0:T(8,128)(2,1)}), bf16[16,6,16,1024]{3,2,1,0:T(8,128)(2,1)S(1)}, u32[]{:S(2)}, u32[]{:S(2)}) async-start(bf16[16,6,16,1024]{3,2,1,0:T(8,128)(2,1)} %get-tuple-element.7.rest_0_), calls=%async_computation.1 | async-start | bytes 6291456 | tf_op jit(solution)/shard_map/all_to_all | solution.py:394
  105.4 1.7 copy-start.1
  107.1 166.6 %all-to-all-start.2 = ((bf16[16,2,16,1024]{3,2,1,0:T(8,128)(2,1)}), bf16[16,2,16,1024]{3,2,1,0:T(8,128)(2,1)S(1)}, u32[]{:S(2)}, u32[]{:S(2)}) async-start(bf16[16,2,16,1024]{3,2,1,0:T(8,128)(2,1)} %get-tuple-element.10.rest_1_), calls=%async_computation.2 | async-start | bytes 2097152 | tf_op jit(solution)/shard_map/all_to_all | solution.py:394
  117.0 131.1 %copy-start.3 = (s32[32]{0:T(128)}, s32[32]{0:T(128)S(1)}, u32[]{:S(2)}) copy-start(s32[32]{0:T(128)S(1)} %get-tuple-element.14.page_number) | copy-start | bytes 388
  117.8 130.3 %copy-start.5 = (s32[96]{0:T(128)}, s32[96]{0:T(128)S(1)}, u32[]{:S(2)}) copy-start(s32[96]{0:T(128)S(1)} %get-tuple-element.12.page_number) | copy-start | bytes 1156
  273.7 1.0 copy-start

commit v2 on v1

--- a/solution.py
+++ b/solution.py
@@ -15,6 +15,7 @@
 VMEM_LIMIT = 60 * 1024 * 1024
 QUERY_BLOCK = 32
 TILE_PAGES = 16
+LATE_TILE_PAGES = 8
 HIDDEN = -1e30
 
 
@@ -136,20 +137,26 @@
 
 
 def write_back_kernel(splits, numbers, *rest):
-    sends, store_out, sem = rest[: len(splits)], rest[len(splits)], rest[len(splits) + 1]
+    sends, store_out = rest[: len(splits)], rest[len(splits)]
+    held, load_sem, sem = rest[len(splits) + 1 : -2], rest[-2], rest[-1]
     holders = numbers.shape[0]
+    loads = [pltpu.make_async_copy(send, part, load_sem) for send, part in zip(sends, held)]
+    for load in loads:
+        load.start()
+    for load in loads:
+        load.wait()
 
     def one_request(r, carry):
-        for (low, high), send in zip(splits, sends):
+        for (low, high), part in zip(splits, held):
             for k in range(low, high):
-                pltpu.make_async_copy(send.at[r, k - low], store_out.at[numbers[r, k]], sem).start()
+                pltpu.make_async_copy(part.at[r, k - low], store_out.at[numbers[r, k]], sem).start()
         return carry
 
     lax.fori_loop(0, holders, one_request, 0)
     pltpu.make_async_copy(store_out, store_out, sem).wait()
 
 
-def attend_kernel(first, last, source, page_number, tiles, sel_ref, query_ref, *rest):
+def attend_kernel(first, last, tile_pages, source, page_number, tiles, sel_ref, query_ref, *rest):
     rest = list(rest)
     state_in = [] if first else [rest.pop(0) for _ in range(2)]
     context = rest.pop(0)
@@ -157,7 +164,7 @@
     kv, values, query, mixed, stats, sem = rest
     pages, page_len = context.shape[0], context.shape[1]
     block = query_ref.shape[0]
-    tile = TILE_PAGES * page_len
+    tile = tile_pages * page_len
     lanes = QUERY_GROUP * block
     scale = 1.4426950408889634 / HEAD_WIDTH**0.5
     f32 = jnp.float32
@@ -179,14 +186,14 @@
         pltpu.make_async_copy(context, kv, sem).wait()
 
         def turn(t, carry):
-            here = pl.ds(t * TILE_PAGES, TILE_PAGES)
+            here = pl.ds(t * tile_pages, tile_pages)
             for g in range(KEY_VALUE_HEADS):
                 at = (KEY_VALUE_HEADS + g) * LANES
                 value = kv[here, :, at : at + LANES].reshape(tile, LANES)
                 values[t, g] = nt_dot(eye, value).astype(jnp.bfloat16)
             return carry
 
-        lax.fori_loop(0, pages // TILE_PAGES, turn, 0)
+        lax.fori_loop(0, pages // tile_pages, turn, 0)
 
     for g in range(KEY_VALUE_HEADS):
         for i in range(QUERY_GROUP):
@@ -204,11 +211,11 @@
     in_page = lax.broadcasted_iota(jnp.int32, (page_len, LANES), 0)
 
     def one_tile(t, carry):
-        here = pl.ds(t * TILE_PAGES, TILE_PAGES)
+        here = pl.ds(t * tile_pages, tile_pages)
         bias = jnp.concatenate(
             [
-                jnp.where(in_page + page_number[t * TILE_PAGES + k] * page_len <= sel, 0.0, HIDDEN)
-                for k in range(TILE_PAGES)
+                jnp.where(in_page + page_number[t * tile_pages + k] * page_len <= sel, 0.0, HIDDEN)
+                for k in range(tile_pages)
             ],
             axis=0,
         ).astype(f32)
@@ -257,7 +264,7 @@
         outs[1][0] = stats[...]
 
 
-def attend(first, last, order, sel_lanes, queries, state, context):
+def attend(first, last, tile_pages, order, sel_lanes, queries, state, context):
     picked, features = queries.shape
     pages, page_len, width = context.shape
     steps = picked // QUERY_BLOCK
@@ -273,7 +280,7 @@
     ]
     share = 0.6
     return pl.pallas_call(
-        functools.partial(attend_kernel, first, last),
+        functools.partial(attend_kernel, first, last, tile_pages),
         grid_spec=pltpu.PrefetchScalarGridSpec(
             num_scalar_prefetch=3,
             grid=(steps,),
@@ -287,7 +294,7 @@
             scratch_shapes=[
                 pltpu.VMEM((pages, page_len, width), jnp.bfloat16),
                 pltpu.VMEM(
-                    (pages // TILE_PAGES, KEY_VALUE_HEADS, LANES, TILE_PAGES * page_len), jnp.bfloat16
+                    (pages // tile_pages, KEY_VALUE_HEADS, LANES, tile_pages * page_len), jnp.bfloat16
                 ),
                 pltpu.VMEM((KEY_VALUE_HEADS, lanes, LANES), jnp.bfloat16),
                 pltpu.VMEM((KEY_VALUE_HEADS, LANES, lanes), jnp.float32),
@@ -315,15 +322,15 @@
     ranks = jnp.sum(((owners[None, :] == owners[:, None]) & before).astype(jnp.int32), axis=1)
     last_page = positions.reshape(-1, QUERY_BLOCK)[:, -1] // page_len
     orders = []
-    for low, high in splits:
+    for (low, high), tile_pages in splits:
         member = (ranks >= low) & (ranks < high)
-        count = pages * (high - low) // splits[-1][1]
+        count = pages * (high - low) // splits[-1][0][1]
         place = jnp.sum((member[None, :] & before).astype(jnp.int32), axis=1)
         hit = (member[None, :] & (place[None, :] == jnp.arange(count)[:, None])).astype(jnp.int32)
         source = jnp.sum(hit * (owners * (high - low) + ranks - low)[None, :], axis=1)
         page = jnp.sum(hit * number[None, :], axis=1)
         seen = jnp.sum((page[None, :] <= last_page[:, None]).astype(jnp.int32), axis=1)
-        orders.append((source, page, (seen + TILE_PAGES - 1) // TILE_PAGES))
+        orders.append((source, page, (seen + tile_pages - 1) // tile_pages))
     return orders
 
 
@@ -381,15 +388,24 @@
             grid=(1,),
             in_specs=[hbm] * len(splits),
             out_specs=hbm,
-            scratch_shapes=[pltpu.SemaphoreType.DMA],
+            scratch_shapes=[
+                *[pltpu.VMEM(part.shape, part.dtype) for part in parts],
+                pltpu.SemaphoreType.DMA,
+                pltpu.SemaphoreType.DMA,
+            ],
         ),
         out_shape=jax.ShapeDtypeStruct(store.shape, store.dtype),
         compiler_params=params,
         cost_estimate=pl.CostEstimate(flops=0, bytes_accessed=4 * store.size, transcendentals=0),
     )(numbers, *parts)
 
-    orders = page_order(page_table[0], sel_pos[0], hold, splits, page_len)
+    tiles = [LATE_TILE_PAGES if low else TILE_PAGES for low, _ in splits]
+    orders = page_order(page_table[0], sel_pos[0], hold, list(zip(splits, tiles)), page_len)
     sel_lanes = jnp.tile(sel_pos.reshape(-1, 1, QUERY_BLOCK), (1, 1, LANES // QUERY_BLOCK))
+    if len(parts) > 1:
+        parts[1:], store_out, orders, sel_lanes = lax.optimization_barrier(
+            (parts[1:], store_out, orders, sel_lanes)
+        )
     arrived = [
         lax.all_to_all(part, "store", split_axis=0, concat_axis=0, tiled=True).reshape(
             -1, page_len, width
@@ -399,7 +415,7 @@
     state = ()
     for at, (context, order) in enumerate(zip(arrived, orders)):
         state = attend(
-            at == 0, at == len(splits) - 1, order, sel_lanes, queries[0], state, context
+            at == 0, at == len(splits) - 1, tiles[at], order, sel_lanes, queries[0], state, context
         )
     return (state[0][None], store_out)
 

time: 287 us -> 154 us (0.54)
  Pallas kernels: 175 us -> 52.1 us
  waiting for transfers between devices: 67.6 us -> 57.6 us
    pallas_call x1, Pallas kernels: 129 us -> 4.92 us  [per_device(): pl.pallas_call(functools.partial(write_back_kernel, splits), grid_spec=pl...]
    all_to_all x2, waiting for transfers between devices: 67.6 us -> 57.6 us  [per_device(): lax.all_to_all(part, 'store', split_axis=0, concat_axis=0, tiled=True)]
  transfers between devices with their start and end apart: 2 -> 2, of which waited for: 1 -> 1; matrix products, arithmetic and copies ran while one was open for 2% -> 3% of each run, Pallas kernels for 54% -> 20%
where the time goes in v2:
time: 154 us; the launch traced here: 153 us
  waiting for transfers between devices  57.6 us (37%)
  Pallas kernels  52.1 us (34%)
  blocking collectives  22.7 us (15%)
  starting transfers between devices  11.9 us (8%)
  local copies, waits for them, and re-layouts  4.12 us (3%)
  other arithmetic  3.81 us (2%)
    all_to_all x2, waiting for transfers between devices, per_device(): lax.all_to_all(part, 'store', split_axis=0, concat_axis=0, tiled=True)  57.6 us
    pallas_call x2, Pallas kernels, attend(): pl.pallas_call(functools.partial(attend_kernel, first, last, tile_pages),...  37.9 us
    all_to_all x1, blocking collectives, per_device(): lax.all_to_all(packed, 'store', split_axis=0, concat_axis=0, tiled=True)  22.7 us
    all_to_all x2, starting transfers between devices, per_device(): lax.all_to_all(part, 'store', split_axis=0, concat_axis=0, tiled=True)  11.9 us
    pallas_call x1, Pallas kernels, per_device(): pl.pallas_call(functools.partial(blend_kernel, splits, row_slots), out_sh...  6.96 us
    pallas_call x1, Pallas kernels, per_device(): pl.pallas_call(functools.partial(write_back_kernel, splits), grid_spec=pl...  4.92 us
    unnamed x14, local copies, waits for them, and re-layouts  3.28 us
  transfers between devices with their start and end apart: 2, of which 1 were waited for; matrix products, arithmetic and copies ran while one was open for 3% of the time, Pallas kernels for 20%

profile of v2, /device:TPU:9, one launch (start us, length us, event | category | flops | bytes accessed | tf_op | source)
XLA Modules:
  0.0 152.9 jit_solution(1377785194736531611)
XLA Ops:
  0.6 2.3 %shard_map.68 = bf16[16,144,128]{2,1,0:T(8,128)(2,1)} custom-call(s32[1,128]{1,0:T(1,128)} %table_ref.1, s32[1,160]{1,0:T(1,128)} %sel_ref.1, bf16[160,1024]{1,0:T(8,128)(2,1)} %bitcast.35), custom_call_target="tpu_custom_call" | custom-call | tf_op jit(solution)/shard_map/pallas_call | solution.py:352
  3.0 22.7 %all_to_all.15.entries_hbm = bf16[16,144,128]{2,1,0:T(8,128)(2,1)} all-to-all(bf16[16,144,128]{2,1,0:T(8,128)(2,1)} %shard_map.68), channel_id=1, replica_groups=mesh['groups'=2,'store'=16] {'store'}, dimensions={0} | all-to-all | bytes 1179648 | tf_op jit(solution)/shard_map/all_to_all | solution.py:358
  25.6 7.0 %shard_map.69 = (bf16[16,6,16,1024]{3,2,1,0:T(8,128)(2,1)}, bf16[16,2,16,1024]{3,2,1,0:T(8,128)(2,1)}, s32[16,128]{1,0:T(8,128)}) custom-call(bf16[16,144,128]{2,1,0:T(8,128)(2,1)} %all_to_all.15.entries_hbm, bf16[128,16,1024]{2,1,0:T(8,128)(2,1)} %store_hbm.1), custom_call_target="tpu_custom_call" | custom-call | tf_op jit(solution)/shard_map/pallas_call | solution.py:360
  32.6 5.0 %all-to-all-start.1 = ((bf16[16,6,16,1024]{3,2,1,0:T(8,128)(2,1)}), bf16[16,6,16,1024]{3,2,1,0:T(8,128)(2,1)S(1)}, u32[]{:S(2)}, u32[]{:S(2)}) async-start(bf16[16,6,16,1024]{3,2,1,0:T(8,128)(2,1)} %get-tuple-element.18.rest_0_), calls=%async_computation.1 | async-start | bytes 6291456 | tf_op jit(solution)/shard_map/all_to_all | solution.py:410
  37.6 0.5 broadcast.181
  38.1 0.7 reduce.3
  38.7 0.1 reshape_squeeze.3
  38.9 0.1 copy.9
  39.0 0.7 tile.9.sel_ref
  39.7 0.2 convert_reduce_fusion.2
  39.9 0.1 convert_reduce_fusion
  40.0 0.7 select_reduce_fusion.2
  40.8 0.2 convert_reduce_fusion.3
  40.9 0.6 select_reduce_fusion
  41.5 0.2 convert_reduce_fusion.4
  41.7 0.6 and_select_fusion.1.tiles
  42.3 0.6 and_select_fusion.tiles
  42.9 4.9 %shard_map.70 = bf16[128,16,1024]{2,1,0:T(8,128)(2,1)} custom-call(s32[16,128]{1,0:T(8,128)} %get-tuple-element.17.numbers, bf16[16,6,16,1024]{3,2,1,0:T(8,128)(2,1)} %get-tuple-element.18.rest_0_, bf16[16,2,16,1024]{3,2,1,0:T(8,128)(2,1)} %get-tuple-element.28.rest_1_), custom_call_target="tpu_custom_call" | custom-call | bytes 8388608 | tf_op jit(solution)/shard_map/pallas_call | solution.py:384
  47.8 57.6 %all-to-all-done.1 = bf16[16,6,16,1024]{3,2,1,0:T(8,128)(2,1)S(1)} async-done(((bf16[16,6,16,1024]{3,2,1,0:T(8,128)(2,1)}), bf16[16,6,16,1024]{3,2,1,0:T(8,128)(2,1)S(1)}, u32[]{:S(2)}, u32[]{:S(2)}) %all-to-all-start.1) | async-done | bytes 3145760 | tf_op jit(solution)/shard_map/all_to_all | solution.py:410
  105.4 1.7 %copy-done.1 = bf16[16,6,16,1024]{3,2,1,0:T(8,128)(2,1)} copy-done((bf16[16,6,16,1024]{3,2,1,0:T(8,128)(2,1)}, bf16[16,6,16,1024]{3,2,1,0:T(8,128)(2,1)S(1)}, u32[]{:S(2)}) %copy-start.1) | copy-done | bytes 3145752
  107.1 7.0 %all-to-all-start.2 = ((bf16[16,2,16,1024]{3,2,1,0:T(8,128)(2,1)}), bf16[16,2,16,1024]{3,2,1,0:T(8,128)(2,1)S(1)}, u32[]{:S(2)}, u32[]{:S(2)}) async-start(bf16[16,2,16,1024]{3,2,1,0:T(8,128)(2,1)} %get-tuple-element.28.rest_1_), calls=%async_computation.2 | async-start | bytes 2097152 | tf_op jit(solution)/shard_map/all_to_all | solution.py:410
  114.0 25.6 %shard_map.71 = (f32[5,4,128,384]{3,2,1,0:T(8,128)}, f32[5,8,384]{2,1,0:T(8,128)}) custom-call(s32[96]{0:T(128)} %get-tuple-element.23.source, s32[96]{0:T(128)} %copy-done.5, s32[5]{0:T(128)} %and_select_fusion.1.tiles, s32[5,1,128]{2,1,0:T(1,128)} %tile.9.sel_ref, bf16[160,6144]{1,0:T(8,128)(2,1)} %bitcast.32, bf16[96,16,1024]{2,1,0:T(8,128)(2,1)} %bitcast.31), custom_call_target="tpu_custom_call" | custom-call | flops 7247757312 | bytes 9043968 | tf_op jit(solution)/shard_map/pallas_call | solution.py:282
  139.6 1.0 copy-done
  140.6 12.3 %shard_map.72 = bf16[160,6144]{1,0:T(8,128)(2,1)} custom-call(s32[32]{0:T(128)} %get-tuple-element.19.source, s32[32]{0:T(128)} %copy-done.3, s32[5]{0:T(128)} %and_select_fusion.tiles, s32[5,1,128]{2,1,0:T(1,128)} %tile.9.sel_ref, bf16[160,6144]{1,0:T(8,128)(2,1)} %bitcast.33, f32[5,4,128,384]{3,2,1,0:T(8,128)} %get-tuple-element.26.rest_0_, ...), custom_call_target="tpu_custom_call" | custom-call | flops 2415919104 | bytes 6946816 | tf_op jit(solution)/shard_map/pallas_call | solution.py:282
  (18 shorter events, 0.2 us)
Async XLA Ops:
  32.6 5.5 %copy-start.2 = (s32[1,160]{1,0:T(1,128)S(1)}, s32[1,160]{1,0:T(1,128)}, u32[]{:S(2)}) copy-start(s32[1,160]{1,0:T(1,128)} %sel_ref.1) | copy-start | bytes 1924
  32.6 7.1 %copy-start.4 = (s32[1,128]{1,0:T(1,128)S(1)}, s32[1,128]{1,0:T(1,128)}, u32[]{:S(2)}) copy-start(s32[1,128]{1,0:T(1,128)} %table_ref.1) | copy-start | bytes 1540
  32.6 72.8 %all-to-all-start.1 = ((bf16[16,6,16,1024]{3,2,1,0:T(8,128)(2,1)}), bf16[16,6,16,1024]{3,2,1,0:T(8,128)(2,1)S(1)}, u32[]{:S(2)}, u32[]{:S(2)}) async-start(bf16[16,6,16,1024]{3,2,1,0:T(8,128)(2,1)} %get-tuple-element.18.rest_0_), calls=%async_computation.1 | async-start | bytes 6291456 | tf_op jit(solution)/shard_map/all_to_all | solution.py:410
  40.7 7.1 %copy-start.3 = (s32[32]{0:T(128)}, s32[32]{0:T(128)S(1)}, u32[]{:S(2)}) copy-start(s32[32]{0:T(128)S(1)} %get-tuple-element.20.page_number) | copy-start | bytes 388
  41.5 6.3 %copy-start.5 = (s32[96]{0:T(128)}, s32[96]{0:T(128)S(1)}, u32[]{:S(2)}) copy-start(s32[96]{0:T(128)S(1)} %get-tuple-element.24.page_number) | copy-start | bytes 1156
  105.4 1.7 %copy-start.1 = (bf16[16,6,16,1024]{3,2,1,0:T(8,128)(2,1)}, bf16[16,6,16,1024]{3,2,1,0:T(8,128)(2,1)S(1)}, u32[]{:S(2)}) copy-start(bf16[16,6,16,1024]{3,2,1,0:T(8,128)(2,1)S(1)} %all-to-all-done.1) | copy-start | bytes 9437188
  107.1 32.5 %all-to-all-start.2 = ((bf16[16,2,16,1024]{3,2,1,0:T(8,128)(2,1)}), bf16[16,2,16,1024]{3,2,1,0:T(8,128)(2,1)S(1)}, u32[]{:S(2)}, u32[]{:S(2)}) async-start(bf16[16,2,16,1024]{3,2,1,0:T(8,128)(2,1)} %get-tuple-element.28.rest_1_), calls=%async_computation.2 | async-start | bytes 2097152 | tf_op jit(solution)/shard_map/all_to_all | solution.py:410
  139.6 1.0 copy-start

commit v3 on v2

--- a/solution.py
+++ b/solution.py
@@ -88,10 +88,11 @@
         out_ref[h, chunks * row_slots :, :] = block.astype(jnp.bfloat16)
 
 
-def blend_kernel(splits, row_slots, entries_hbm, store_hbm, *rest):
-    sends, numbers_out = rest[: len(splits)], rest[len(splits)]
-    store, blended, entries, numbers, load_sem, index_sem, entries_sem, send_sem = rest[len(splits) + 1 :]
-    holders, capacity, page_len, width = blended.shape
+def blend_kernel(row_slots, own, entries_hbm, store_hbm, *rest):
+    holders = entries_hbm.shape[0]
+    sends, numbers_out = rest[:holders], rest[holders]
+    store, blended, entries, numbers, load_sem, index_sem, entries_sem, send_sem = rest[holders + 1 :]
+    _, capacity, page_len, width = blended.shape
     chunks = width // LANES
     rows_here = capacity * page_len
     f32 = jnp.float32
@@ -113,8 +114,8 @@
     load.wait()
 
     row_id = lax.broadcasted_iota(jnp.int32, (rows_here, row_slots), 0).astype(f32)
-
-    def one_request(r, carry):
+    for d in range(holders):
+        r = own[0] ^ d
         targets = entries[r, chunks * row_slots :, :].astype(f32)[1:2, 0:row_slots] - 1.0
         hit = jnp.where(row_id == targets, 1.0, 0.0)
         keep = 1.0 - jnp.sum(hit, axis=1, keepdims=True)
@@ -126,43 +127,38 @@
             fresh = jnp.dot(hit, rows, preferred_element_type=f32).astype(jnp.bfloat16)
             for k in range(capacity):
                 part = slice(k * page_len, (k + 1) * page_len)
-                blended[r, k, :, lanes] = store[numbers[r, k], :, lanes] * keep[part] + fresh[part]
-        for (low, high), send in zip(splits, sends):
-            pltpu.make_async_copy(blended.at[r, pl.ds(low, high - low)], send.at[r], send_sem).start()
-        return carry
-
-    lax.fori_loop(0, holders, one_request, 0)
-    for send in sends:
-        pltpu.make_async_copy(send, send, send_sem).wait()
-
-
-def write_back_kernel(splits, numbers, *rest):
-    sends, store_out = rest[: len(splits)], rest[len(splits)]
-    held, load_sem, sem = rest[len(splits) + 1 : -2], rest[-2], rest[-1]
+                blended[d, k, :, lanes] = store[numbers[r, k], :, lanes] * keep[part] + fresh[part]
+        pltpu.make_async_copy(blended.at[d], sends[d], send_sem).start()
+    pltpu.make_async_copy(blended, blended, send_sem).wait()
+
+
+def write_back_kernel(own, numbers, *rest):
     holders = numbers.shape[0]
-    loads = [pltpu.make_async_copy(send, part, load_sem) for send, part in zip(sends, held)]
-    for load in loads:
-        load.start()
-    for load in loads:
-        load.wait()
-
-    def one_request(r, carry):
-        for (low, high), part in zip(splits, held):
-            for k in range(low, high):
-                pltpu.make_async_copy(part.at[r, k - low], store_out.at[numbers[r, k]], sem).start()
+    sends, store_out = rest[:holders], rest[holders]
+    held, load_sem, sem = rest[holders + 1 :]
+    capacity = held.shape[1]
+    for d in range(holders):
+        pltpu.make_async_copy(sends[d], held.at[d], load_sem).start()
+    pltpu.make_async_copy(held, held, load_sem).wait()
+
+    def one_request(d, carry):
+        r = own[0] ^ d
+        for k in range(capacity):
+            pltpu.make_async_copy(held.at[d, k], store_out.at[numbers[r, k]], sem).start()
         return carry
 
     lax.fori_loop(0, holders, one_request, 0)
     pltpu.make_async_copy(store_out, store_out, sem).wait()
 
 
-def attend_kernel(first, last, tile_pages, source, page_number, tiles, sel_ref, query_ref, *rest):
+def attend_kernel(first, last, tile_pages, sources, place, page_number, tiles, sel_ref, query_ref, *rest):
     rest = list(rest)
     state_in = [] if first else [rest.pop(0) for _ in range(2)]
-    context = rest.pop(0)
+    contexts = [rest.pop(0) for _ in range(sources)]
     outs = [rest.pop(0) for _ in range(1 if last else 2)]
     kv, values, query, mixed, stats, sem = rest
-    pages, page_len = context.shape[0], context.shape[1]
+    pages, page_len = kv.shape[0], kv.shape[1]
+    capacity = pages // sources
     block = query_ref.shape[0]
     tile = tile_pages * page_len
     lanes = QUERY_GROUP * block
@@ -178,12 +174,10 @@
 
     @pl.when(step == 0)
     def _():
-        def fetch(i, carry):
-            pltpu.make_async_copy(context.at[source[i]], kv.at[i], sem).start()
-            return carry
-
-        lax.fori_loop(0, pages, fetch, 0)
-        pltpu.make_async_copy(context, kv, sem).wait()
+        for i, context in enumerate(contexts):
+            for k in range(capacity):
+                pltpu.make_async_copy(context.at[k], kv.at[place[i * capacity + k]], sem).start()
+        pltpu.make_async_copy(kv, kv, sem).wait()
 
         def turn(t, carry):
             here = pl.ds(t * tile_pages, tile_pages)
@@ -264,9 +258,10 @@
         outs[1][0] = stats[...]
 
 
-def attend(first, last, tile_pages, order, sel_lanes, queries, state, context):
+def attend(first, last, tile_pages, order, sel_lanes, queries, state, contexts):
     picked, features = queries.shape
-    pages, page_len, width = context.shape
+    capacity, page_len, width = contexts[0].shape
+    pages = capacity * len(contexts)
     steps = picked // QUERY_BLOCK
     lanes = QUERY_GROUP * QUERY_BLOCK
     wide = pl.BlockSpec((QUERY_BLOCK, features), lambda b, *_: (b, 0))
@@ -280,7 +275,7 @@
     ]
     share = 0.6
     return pl.pallas_call(
-        functools.partial(attend_kernel, first, last, tile_pages),
+        functools.partial(attend_kernel, first, last, tile_pages, len(contexts)),
         grid_spec=pltpu.PrefetchScalarGridSpec(
             num_scalar_prefetch=3,
             grid=(steps,),
@@ -288,7 +283,7 @@
                 pl.BlockSpec((1, 1, LANES), lambda b, *_: (b, 0, 0)),
                 wide,
                 *([] if first else state_specs),
-                pl.BlockSpec(memory_space=pltpu.HBM),
+                *[pl.BlockSpec(memory_space=pltpu.HBM)] * len(contexts),
             ],
             out_specs=[wide] if last else state_specs,
             scratch_shapes=[
@@ -311,26 +306,32 @@
             bytes_accessed=2 * pages * page_len * width + 6 * picked * features,
             transcendentals=int(share * picked * features // LANES * pages * page_len),
         ),
-    )(*order, sel_lanes, queries, *state, context)
-
-
-def page_order(slots, positions, hold, splits, page_len):
+    )(*order, sel_lanes, queries, *state, *contexts)
+
+
+def page_order(slots, positions, own, hold, capacity, groups, page_len):
     pages = slots.shape[0]
     number = jnp.arange(pages)
     before = number[None, :] < number[:, None]
     owners = slots // hold
     ranks = jnp.sum(((owners[None, :] == owners[:, None]) & before).astype(jnp.int32), axis=1)
+    distance = owners ^ own
     last_page = positions.reshape(-1, QUERY_BLOCK)[:, -1] // page_len
     orders = []
-    for (low, high), tile_pages in splits:
-        member = (ranks >= low) & (ranks < high)
-        count = pages * (high - low) // splits[-1][0][1]
+    for group, tile_pages in groups:
+        count = len(group) * capacity
+        arrival = jnp.full((pages,), -1, jnp.int32)
+        for i, d in enumerate(group):
+            arrival = jnp.where(distance == d, i * capacity + ranks, arrival)
+        member = arrival >= 0
         place = jnp.sum((member[None, :] & before).astype(jnp.int32), axis=1)
-        hit = (member[None, :] & (place[None, :] == jnp.arange(count)[:, None])).astype(jnp.int32)
-        source = jnp.sum(hit * (owners * (high - low) + ranks - low)[None, :], axis=1)
-        page = jnp.sum(hit * number[None, :], axis=1)
+        index = jnp.arange(count)[:, None]
+        places = jnp.sum(jnp.where(arrival[None, :] == index, place[None, :], 0), axis=1)
+        page = jnp.sum(
+            jnp.where(member[None, :] & (place[None, :] == index), number[None, :], 0), axis=1
+        )
         seen = jnp.sum((page[None, :] <= last_page[:, None]).astype(jnp.int32), axis=1)
-        orders.append((source, page, (seen + tile_pages - 1) // tile_pages))
+        orders.append((places, page, (seen + tile_pages - 1) // tile_pages))
     return orders
 
 
@@ -343,11 +344,15 @@
     row_slots = -(-SELP * capacity // 16) * 16
     chunks = width // LANES
     packed_rows = chunks * row_slots + 16
-    late = capacity // 4
-    splits = ((0, capacity - late), (capacity - late, capacity)) if late else ((0, capacity),)
     hbm = pl.BlockSpec(memory_space=pltpu.HBM)
     vmem = pl.BlockSpec(memory_space=pltpu.VMEM)
     params = pltpu.CompilerParams(vmem_limit_bytes=VMEM_LIMIT)
+    own = lax.axis_index("store")
+    own_word = own.reshape(1).astype(jnp.int32)
+    if holders == 16:
+        groups = [((0, 8, 12, 4, 9, 13, 5, 1, 6, 2, 7, 3), TILE_PAGES), ((10, 14, 11, 15), LATE_TILE_PAGES)]
+    else:
+        groups = [(tuple(range(holders)), TILE_PAGES)]
 
     packed = pl.pallas_call(
         functools.partial(plan_kernel, hold, holders, row_slots, page_len),
@@ -358,38 +363,39 @@
     entries = lax.all_to_all(packed, "store", split_axis=0, concat_axis=0, tiled=True)
 
     *parts, numbers = pl.pallas_call(
-        functools.partial(blend_kernel, splits, row_slots),
-        out_shape=[
-            *[
-                jax.ShapeDtypeStruct((holders, high - low, page_len, width), store.dtype)
-                for low, high in splits
-            ],
-            jax.ShapeDtypeStruct((holders, LANES), jnp.int32),
-        ],
-        in_specs=[hbm, hbm],
-        out_specs=[hbm] * len(splits) + [vmem],
-        scratch_shapes=[
-            pltpu.VMEM(store.shape, store.dtype),
-            pltpu.VMEM((holders, capacity, page_len, width), store.dtype),
-            pltpu.VMEM((holders, packed_rows, LANES), store.dtype),
-            pltpu.SMEM((holders, LANES), jnp.int32),
-            pltpu.SemaphoreType.DMA,
-            pltpu.SemaphoreType.DMA,
-            pltpu.SemaphoreType.DMA,
-            pltpu.SemaphoreType.DMA,
-        ],
-        compiler_params=params,
-    )(entries, store)
-
-    store_out = pl.pallas_call(
-        functools.partial(write_back_kernel, splits),
+        functools.partial(blend_kernel, row_slots),
         grid_spec=pltpu.PrefetchScalarGridSpec(
             num_scalar_prefetch=1,
             grid=(1,),
-            in_specs=[hbm] * len(splits),
+            in_specs=[hbm, hbm],
+            out_specs=[hbm] * holders + [vmem],
+            scratch_shapes=[
+                pltpu.VMEM(store.shape, store.dtype),
+                pltpu.VMEM((holders, capacity, page_len, width), store.dtype),
+                pltpu.VMEM((holders, packed_rows, LANES), store.dtype),
+                pltpu.SMEM((holders, LANES), jnp.int32),
+                pltpu.SemaphoreType.DMA,
+                pltpu.SemaphoreType.DMA,
+                pltpu.SemaphoreType.DMA,
+                pltpu.SemaphoreType.DMA,
+            ],
+        ),
+        out_shape=[
+            *[jax.ShapeDtypeStruct((capacity, page_len, width), store.dtype)] * holders,
+            jax.ShapeDtypeStruct((holders, LANES), jnp.int32),
+        ],
+        compiler_params=params,
+    )(own_word, entries, store)
+
+    store_out = pl.pallas_call(
+        write_back_kernel,
+        grid_spec=pltpu.PrefetchScalarGridSpec(
+            num_scalar_prefetch=2,
+            grid=(1,),
+            in_specs=[hbm] * holders,
             out_specs=hbm,
             scratch_shapes=[
-                *[pltpu.VMEM(part.shape, part.dtype) for part in parts],
+                pltpu.VMEM((holders, capacity, page_len, width), store.dtype),
                 pltpu.SemaphoreType.DMA,
                 pltpu.SemaphoreType.DMA,
             ],
@@ -397,25 +403,21 @@
         out_shape=jax.ShapeDtypeStruct(store.shape, store.dtype),
         compiler_params=params,
         cost_estimate=pl.CostEstimate(flops=0, bytes_accessed=4 * store.size, transcendentals=0),
-    )(numbers, *parts)
-
-    tiles = [LATE_TILE_PAGES if low else TILE_PAGES for low, _ in splits]
-    orders = page_order(page_table[0], sel_pos[0], hold, list(zip(splits, tiles)), page_len)
+    )(own_word, numbers, *parts)
+
+    orders = page_order(page_table[0], sel_pos[0], own, hold, capacity, groups, page_len)
     sel_lanes = jnp.tile(sel_pos.reshape(-1, 1, QUERY_BLOCK), (1, 1, LANES // QUERY_BLOCK))
-    if len(parts) > 1:
-        parts[1:], store_out, orders, sel_lanes = lax.optimization_barrier(
-            (parts[1:], store_out, orders, sel_lanes)
-        )
-    arrived = [
-        lax.all_to_all(part, "store", split_axis=0, concat_axis=0, tiled=True).reshape(
-            -1, page_len, width
-        )
-        for part in parts
-    ]
+    arrived = {0: parts[0]}
+    for group, _ in groups:
+        for d in group:
+            if d:
+                pairs = [(h, h ^ d) for h in range(holders)]
+                arrived[d] = lax.ppermute(parts[d], "store", pairs)
     state = ()
-    for at, (context, order) in enumerate(zip(arrived, orders)):
+    for at, ((group, tile_pages), order) in enumerate(zip(groups, orders)):
+        contexts = [arrived[d] for d in group]
         state = attend(
-            at == 0, at == len(splits) - 1, tiles[at], order, sel_lanes, queries[0], state, context
+            at == 0, at == len(groups) - 1, tile_pages, order, sel_lanes, queries[0], state, contexts
         )
     return (state[0][None], store_out)
 

time: 154 us -> 153 us (level)
  blocking collectives: 22.7 us -> 0 us
  starting transfers between devices: 11.9 us -> 27.8 us
  waiting for transfers between devices: 57.6 us -> 63.4 us
  other arithmetic: 3.81 us -> 5.81 us
    ppermute x0 -> x15, waiting for transfers between devices: none -> 50.8 us  [per_device(): arrived[d] = lax.ppermute(parts[d], 'store', pairs)]
    all_to_all x2 -> x1, waiting for transfers between devices: 57.6 us -> 12.6 us  [per_device(): lax.all_to_all(packed, 'store', split_axis=0, concat_axis=0, tiled=True)]
    all_to_all x1 -> x0, blocking collectives: 22.7 us -> none  [per_device(): lax.all_to_all(packed, 'store', split_axis=0, concat_axis=0, tiled=True)]
    ppermute x0 -> x15, starting transfers between devices: none -> 21.2 us  [per_device(): arrived[d] = lax.ppermute(parts[d], 'store', pairs)]
    all_to_all x2 -> x1, starting transfers between devices: 11.9 us -> 6.59 us  [per_device(): lax.all_to_all(packed, 'store', split_axis=0, concat_axis=0, tiled=True)]
    unnamed x14 -> x40, local copies, waits for them, and re-layouts: 3.28 us -> 2.2 us
  transfers between devices with their start and end apart: 2 -> 16, of which waited for: 1 -> 9; matrix products, arithmetic and copies ran while one was open for 3% -> 5% of each run, Pallas kernels for 20% -> 18%
where the time goes in v3:
time: 153 us; the launch traced here: 152 us
  waiting for transfers between devices  63.4 us (41%)
  Pallas kernels  51.4 us (34%)
  starting transfers between devices  27.8 us (18%)
  other arithmetic  5.81 us (4%)
  local copies, waits for them, and re-layouts  3.03 us (2%)
    ppermute x15, waiting for transfers between devices, per_device(): arrived[d] = lax.ppermute(parts[d], 'store', pairs)  50.8 us
    pallas_call x2, Pallas kernels, attend(): pl.pallas_call(functools.partial(attend_kernel, first, last, tile_pages,...  38.6 us
    ppermute x15, starting transfers between devices, per_device(): arrived[d] = lax.ppermute(parts[d], 'store', pairs)  21.2 us
    all_to_all x1, waiting for transfers between devices, per_device(): lax.all_to_all(packed, 'store', split_axis=0, concat_axis=0, tiled=True)  12.6 us
    all_to_all x1, starting transfers between devices, per_device(): lax.all_to_all(packed, 'store', split_axis=0, concat_axis=0, tiled=True)  6.59 us
    pallas_call x1, Pallas kernels, per_device(): pl.pallas_call(functools.partial(blend_kernel, row_slots), grid_spec=pltp...  5.46 us
    pallas_call x1, Pallas kernels, per_device(): pl.pallas_call(write_back_kernel, grid_spec=pltpu.PrefetchScalarGridSpec(...  5.03 us
  transfers between devices with their start and end apart: 16, of which 9 were waited for; matrix products, arithmetic and copies ran while one was open for 5% of the time, Pallas kernels for 18%

profile of v3, /device:TPU:9, one launch (start us, length us, event | category | flops | bytes accessed | tf_op | source)
XLA Modules:
  0.0 152.3 jit_solution(7677870204701533790)
XLA Ops:
  0.6 2.3 %shard_map.68 = bf16[16,144,128]{2,1,0:T(8,128)(2,1)} custom-call(s32[1,128]{1,0:T(1,128)} %table_ref.1, s32[1,160]{1,0:T(1,128)} %sel_ref.1, bf16[160,1024]{1,0:T(8,128)(2,1)} %bitcast.69), custom_call_target="tpu_custom_call" | custom-call | tf_op jit(solution)/shard_map/pallas_call | solution.py:357
  3.0 6.6 %all-to-all-start = ((bf16[16,144,128]{2,1,0:T(8,128)(2,1)}), bf16[16,144,128]{2,1,0:T(8,128)(2,1)S(1)}, u32[]{:S(2)}, u32[]{:S(2)}) async-start(bf16[16,144,128]{2,1,0:T(8,128)(2,1)} %shard_map.68), calls=%async_computation | async-start | bytes 1179648 | tf_op jit(solution)/shard_map/all_to_all | solution.py:363
  12.5 12.6 %all-to-all-done.entries_hbm = bf16[16,144,128]{2,1,0:T(8,128)(2,1)S(1)} async-done(((bf16[16,144,128]{2,1,0:T(8,128)(2,1)}), bf16[16,144,128]{2,1,0:T(8,128)(2,1)S(1)}, u32[]{:S(2)}, u32[]{:S(2)}) %all-to-all-start) | async-done | bytes 589856 | tf_op jit(solution)/shard_map/all_to_all | solution.py:363
  25.9 5.5 %shard_map.69 = (bf16[8,16,1024]{2,1,0:T(8,128)(2,1)}, bf16[8,16,1024]{2,1,0:T(8,128)(2,1)}, bf16[8,16,1024]{2,1,0:T(8,128)(2,1)}, bf16[8,16,1024]{2,1,0:T(8,128...) custom-call(s32[1]{0:T(128)} %bitcast.9.own, ...), custom_call_target="tpu_custom_call" | custom-call | tf_op jit(solution)/shard_map/pallas_call | solution.py:365
  34.5 2.7 %collective-permute-start.2 = (bf16[8,16,1024]{2,1,0:T(8,128)(2,1)}, bf16[8,16,1024]{2,1,0:T(8,128)(2,1)S(1)}, u32[]{:S(2)}, u32[]{:S(2)}) collective-permute-start(bf16[8,16,1024]{2,1,0:T(8,128)(2,1)} %get-tuple-element.24.rest_4_), channel_id=1, source_target_pairs={{0,4},{1,5},{2,6},{3,7},{4,0},{5,1},{6,2},{7,3},{8,12},{9,13},{10,... | collective-permute-start | bytes 786440 | tf_op jit(solution)/shard_map/ppermute | solution.py:415
  37.2 1.4 collective-permute-start.3
  39.2 10.0 %collective-permute-done.rest_1_ = bf16[8,16,1024]{2,1,0:T(8,128)(2,1)S(1)} collective-permute-done((bf16[8,16,1024]{2,1,0:T(8,128)(2,1)}, bf16[8,16,1024]{2,1,0:T(8,128)(2,1)S(1)}, u32[]{:S(2)}, u32[]{:S(2)}) %collective-permute-start) | collective-permute-done | bytes 262176 | tf_op jit(solution)/shard_map/ppermute | solution.py:415
  49.2 3.9 %collective-permute-start.5 = (bf16[8,16,1024]{2,1,0:T(8,128)(2,1)}, bf16[8,16,1024]{2,1,0:T(8,128)(2,1)S(1)}, u32[]{:S(2)}, u32[]{:S(2)}) collective-permute-start(bf16[8,16,1024]{2,1,0:T(8,128)(2,1)} %get-tuple-element.27.rest_5_), channel_id=1, source_target_pairs={{0,5},{1,4},{2,7},{3,6},{4,1},{5,0},{6,3},{7,2},{8,13},{9,12},{10,... | collective-permute-start | bytes 786440 | tf_op jit(solution)/shard_map/ppermute | solution.py:415
  53.8 12.8 %collective-permute-done.1.rest_2_ = bf16[8,16,1024]{2,1,0:T(8,128)(2,1)S(1)} collective-permute-done((bf16[8,16,1024]{2,1,0:T(8,128)(2,1)}, bf16[8,16,1024]{2,1,0:T(8,128)(2,1)S(1)}, u32[]{:S(2)}, u32[]{:S(2)}) %collective-permute-start.1) | collective-permute-done | bytes 262176 | tf_op jit(solution)/shard_map/ppermute | solution.py:415
  66.6 2.3 %collective-permute-start.6 = (bf16[8,16,1024]{2,1,0:T(8,128)(2,1)}, bf16[8,16,1024]{2,1,0:T(8,128)(2,1)S(1)}, u32[]{:S(2)}, u32[]{:S(2)}) collective-permute-start(bf16[8,16,1024]{2,1,0:T(8,128)(2,1)} %get-tuple-element.28.rest_1_), channel_id=1, source_target_pairs={{0,1},{1,0},{2,3},{3,2},{4,5},{5,4},{6,7},{7,6},{8,9},{9,8},{10,11... | collective-permute-start | bytes 786440 | tf_op jit(solution)/shard_map/ppermute | solution.py:415
  68.9 2.9 %collective-permute-done.3.rest_4_ = bf16[8,16,1024]{2,1,0:T(8,128)(2,1)S(1)} collective-permute-done((bf16[8,16,1024]{2,1,0:T(8,128)(2,1)}, bf16[8,16,1024]{2,1,0:T(8,128)(2,1)S(1)}, u32[]{:S(2)}, u32[]{:S(2)}) %collective-permute-start.3) | collective-permute-done | bytes 262176 | tf_op jit(solution)/shard_map/ppermute | solution.py:415
  72.3 6.5 %collective-permute-done.4.rest_5_ = bf16[8,16,1024]{2,1,0:T(8,128)(2,1)S(1)} collective-permute-done((bf16[8,16,1024]{2,1,0:T(8,128)(2,1)}, bf16[8,16,1024]{2,1,0:T(8,128)(2,1)S(1)}, u32[]{:S(2)}, u32[]{:S(2)}) %collective-permute-start.4) | collective-permute-done | bytes 262176 | tf_op jit(solution)/shard_map/ppermute | solution.py:415
  78.9 1.1 collective-permute-start.10
  81.5 5.0 %shard_map.72 = bf16[128,16,1024]{2,1,0:T(8,128)(2,1)} custom-call(s32[1]{0:T(128)} %bitcast.9.own, s32[16,128]{1,0:T(8,128)} %get-tuple-element.39.numbers, bf16[8,16,1024]{2,1,0:T(8,128)(2,1)} %get-tuple-element.21.rest_0_, bf16[8,16,1024]{2,1,0:T(8,128)(2,1)} %get-tuple-element.28.rest_1_, bf16[8,16,1024]{2,1,0:T(8,128)(2,1)} %get-tuple-element.30.rest_2_, ...), custom_call_target="tpu_custom_call" | custom-call | bytes 8388608 | tf_op jit(solution)/shard_map/pallas_call | solution.py:390
  86.6 2.7 %collective-permute-start.11 = (bf16[8,16,1024]{2,1,0:T(8,128)(2,1)S(1)}, bf16[8,16,1024]{2,1,0:T(8,128)(2,1)S(1)}, u32[]{:S(2)}, u32[]{:S(2)}) collective-permute-start(bf16[8,16,1024]{2,1,0:T(8,128)(2,1)S(1)} %copy-done.4), channel_id=1, source_target_pairs={{0,10},{1,11},{2,8},{3,9},{4,14},{5,15},{6,12},{7,13},{8,2},{9,3},... | collective-permute-start | bytes 786440 | tf_op jit(solution)/shard_map/ppermute | solution.py:415
  89.3 1.3 collective-permute-start.12
  90.6 2.6 %collective-permute-start.13 = (bf16[8,16,1024]{2,1,0:T(8,128)(2,1)S(1)}, bf16[8,16,1024]{2,1,0:T(8,128)(2,1)S(1)}, u32[]{:S(2)}, u32[]{:S(2)}) collective-permute-start(bf16[8,16,1024]{2,1,0:T(8,128)(2,1)S(1)} %copy-done.2), channel_id=1, source_target_pairs={{0,11},{1,10},{2,9},{3,8},{4,15},{5,14},{6,13},{7,12},{8,3},{9,2},... | collective-permute-start | bytes 786440 | tf_op jit(solution)/shard_map/ppermute | solution.py:415
  93.2 1.1 collective-permute-start.14
  94.3 6.5 %collective-permute-done.10.rest_11_ = bf16[8,16,1024]{2,1,0:T(8,128)(2,1)} collective-permute-done((bf16[8,16,1024]{2,1,0:T(8,128)(2,1)}, bf16[8,16,1024]{2,1,0:T(8,128)(2,1)}, u32[]{:S(2)}, u32[]{:S(2)}) %collective-permute-start.10) | collective-permute-done | bytes 262176 | tf_op jit(solution)/shard_map/ppermute | solution.py:415
  100.8 23.1 %shard_map.70 = (f32[5,4,128,384]{3,2,1,0:T(8,128)}, f32[5,8,384]{2,1,0:T(8,128)}) custom-call(s32[96]{0:T(128)} %get-tuple-element.41.place, s32[96]{0:T(128)} %copy-done.11, s32[5]{0:T(128)} %and_select_fusion.tiles, s32[5,1,128]{2,1,0:T(1,128)} %tile.9.sel_ref, bf16[160,6144]{1,0:T(8,128)(2,1)} %bitcast.66, ...), custom_call_target="tpu_custom_call" | custom-call | flops 7247757312 | bytes 9043968 | tf_op jit(solution)/shard_map/pallas_call | solution.py:277
  123.9 0.9 collective-permute-done.12.rest_3_
  124.9 3.4 %collective-permute-done.13.rest_4_ = bf16[8,16,1024]{2,1,0:T(8,128)(2,1)S(1)} collective-permute-done((bf16[8,16,1024]{2,1,0:T(8,128)(2,1)S(1)}, bf16[8,16,1024]{2,1,0:T(8,128)(2,1)S(1)}, u32[]{:S(2)}, u32[]{:S(2)}) %collective-permute-start.13) | collective-permute-done | bytes 262176 | tf_op jit(solution)/shard_map/ppermute | solution.py:415
  128.3 7.8 %collective-permute-done.14.rest_5_ = bf16[8,16,1024]{2,1,0:T(8,128)(2,1)S(1)} collective-permute-done((bf16[8,16,1024]{2,1,0:T(8,128)(2,1)S(1)}, bf16[8,16,1024]{2,1,0:T(8,128)(2,1)S(1)}, u32[]{:S(2)}, u32[]{:S(2)}) %collective-permute-start.14) | collective-permute-done | bytes 262176 | tf_op jit(solution)/shard_map/ppermute | solution.py:415
  136.8 15.5 %shard_map.71 = bf16[160,6144]{1,0:T(8,128)(2,1)} custom-call(s32[32]{0:T(128)} %get-tuple-element.43.place, s32[32]{0:T(128)} %copy-done.10, s32[5]{0:T(128)} %and_select_fusion.1.tiles, s32[5,1,128]{2,1,0:T(1,128)} %tile.9.sel_ref, bf16[160,6144]{1,0:T(8,128)(2,1)} %bitcast.67, f32[5,4,128,384]{3,2,1,0:T(8,128)} %get-tuple-element.33.rest_0_, ...), custom_call_target="tpu_custom_call" | custom-call | flops 2415919104 | bytes 6946816 | tf_op jit(solution)/shard_map/pallas_call | solution.py:277
  (70 shorter events, 11.1 us)
Async XLA Ops:
  0.6 32.4 %copy-start.9 = (s32[1,160]{1,0:T(1,128)S(1)}, s32[1,160]{1,0:T(1,128)}, u32[]{:S(2)}) copy-start(s32[1,160]{1,0:T(1,128)} %sel_ref.1) | copy-start | bytes 1924
  3.0 22.1 %all-to-all-start = ((bf16[16,144,128]{2,1,0:T(8,128)(2,1)}), bf16[16,144,128]{2,1,0:T(8,128)(2,1)S(1)}, u32[]{:S(2)}, u32[]{:S(2)}) async-start(bf16[16,144,128]{2,1,0:T(8,128)(2,1)} %shard_map.68), calls=%async_computation | async-start | bytes 1179648 | tf_op jit(solution)/shard_map/all_to_all | solution.py:363
  12.5 74.0 %copy-start.11 = (s32[96]{0:T(128)}, s32[96]{0:T(128)S(1)}, u32[]{:S(2)}) copy-start(s32[96]{0:T(128)S(1)} %get-tuple-element.40.page_number) | copy-start | bytes 1156
  31.4 17.8 %collective-permute-start = (bf16[8,16,1024]{2,1,0:T(8,128)(2,1)}, bf16[8,16,1024]{2,1,0:T(8,128)(2,1)S(1)}, u32[]{:S(2)}, u32[]{:S(2)}) collective-permute-start(bf16[8,16,1024]{2,1,0:T(8,128)(2,1)} %get-tuple-element.22.rest_8_), channel_id=1, source_target_pairs={{0,8},{1,9},{2,10},{3,11},{4,12},{5,13},{6,14},{7,15},{8,0},{9,1},... | collective-permute-start | bytes 786440 | tf_op jit(solution)/shard_map/ppermute | solution.py:415
  32.5 54.0 %copy-start.10 = (s32[32]{0:T(128)}, s32[32]{0:T(128)S(1)}, u32[]{:S(2)}) copy-start(s32[32]{0:T(128)S(1)} %get-tuple-element.42.page_number) | copy-start | bytes 388
  33.9 32.6 %collective-permute-start.1 = (bf16[8,16,1024]{2,1,0:T(8,128)(2,1)}, bf16[8,16,1024]{2,1,0:T(8,128)(2,1)S(1)}, u32[]{:S(2)}, u32[]{:S(2)}) collective-permute-start(bf16[8,16,1024]{2,1,0:T(8,128)(2,1)} %get-tuple-element.23.rest_12_), channel_id=1, source_target_pairs={{0,12},{1,13},{2,14},{3,15},{4,8},{5,9},{6,10},{7,11},{8,4},{9,5},... | collective-permute-start | bytes 786440 | tf_op jit(solution)/shard_map/ppermute | solution.py:415
  34.5 34.3 %collective-permute-start.2 = (bf16[8,16,1024]{2,1,0:T(8,128)(2,1)}, bf16[8,16,1024]{2,1,0:T(8,128)(2,1)S(1)}, u32[]{:S(2)}, u32[]{:S(2)}) collective-permute-start(bf16[8,16,1024]{2,1,0:T(8,128)(2,1)} %get-tuple-element.24.rest_4_), channel_id=1, source_target_pairs={{0,4},{1,5},{2,6},{3,7},{4,0},{5,1},{6,2},{7,3},{8,12},{9,13},{10,... | collective-permute-start | bytes 786440 | tf_op jit(solution)/shard_map/ppermute | solution.py:415
  37.2 34.5 %collective-permute-start.3 = (bf16[8,16,1024]{2,1,0:T(8,128)(2,1)}, bf16[8,16,1024]{2,1,0:T(8,128)(2,1)S(1)}, u32[]{:S(2)}, u32[]{:S(2)}) collective-permute-start(bf16[8,16,1024]{2,1,0:T(8,128)(2,1)} %get-tuple-element.25.rest_9_), channel_id=1, source_target_pairs={{0,9},{1,8},{2,11},{3,10},{4,13},{5,12},{6,15},{7,14},{8,1},{9,0},... | collective-permute-start | bytes 786440 | tf_op jit(solution)/shard_map/ppermute | solution.py:415
  38.7 40.2 %collective-permute-start.4 = (bf16[8,16,1024]{2,1,0:T(8,128)(2,1)}, bf16[8,16,1024]{2,1,0:T(8,128)(2,1)S(1)}, u32[]{:S(2)}, u32[]{:S(2)}) collective-permute-start(bf16[8,16,1024]{2,1,0:T(8,128)(2,1)} %get-tuple-element.26.rest_13_), channel_id=1, source_target_pairs={{0,13},{1,12},{2,15},{3,14},{4,9},{5,8},{6,11},{7,10},{8,5},{9,4},... | collective-permute-start | bytes 786440 | tf_op jit(solution)/shard_map/ppermute | solution.py:415
  49.2 37.3 %copy-start.12 = (bf16[8,16,1024]{2,1,0:T(8,128)(2,1)}, bf16[8,16,1024]{2,1,0:T(8,128)(2,1)S(1)}, u32[]{:S(2)}) copy-start(bf16[8,16,1024]{2,1,0:T(8,128)(2,1)S(1)} %collective-permute-done.rest_1_) | copy-start | bytes 786436
  49.2 29.7 %collective-permute-start.5 = (bf16[8,16,1024]{2,1,0:T(8,128)(2,1)}, bf16[8,16,1024]{2,1,0:T(8,128)(2,1)S(1)}, u32[]{:S(2)}, u32[]{:S(2)}) collective-permute-start(bf16[8,16,1024]{2,1,0:T(8,128)(2,1)} %get-tuple-element.27.rest_5_), channel_id=1, source_target_pairs={{0,5},{1,4},{2,7},{3,6},{4,1},{5,0},{6,3},{7,2},{8,13},{9,12},{10,... | collective-permute-start | bytes 786440 | tf_op jit(solution)/shard_map/ppermute | solution.py:415
  66.6 20.0 %copy-start.13 = (bf16[8,16,1024]{2,1,0:T(8,128)(2,1)}, bf16[8,16,1024]{2,1,0:T(8,128)(2,1)S(1)}, u32[]{:S(2)}) copy-start(bf16[8,16,1024]{2,1,0:T(8,128)(2,1)S(1)} %collective-permute-done.1.rest_2_) | copy-start | bytes 786436
  66.6 20.0 %collective-permute-start.6 = (bf16[8,16,1024]{2,1,0:T(8,128)(2,1)}, bf16[8,16,1024]{2,1,0:T(8,128)(2,1)S(1)}, u32[]{:S(2)}, u32[]{:S(2)}) collective-permute-start(bf16[8,16,1024]{2,1,0:T(8,128)(2,1)} %get-tuple-element.28.rest_1_), channel_id=1, source_target_pairs={{0,1},{1,0},{2,3},{3,2},{4,5},{5,4},{6,7},{7,6},{8,9},{9,8},{10,11... | collective-permute-start | bytes 786440 | tf_op jit(solution)/shard_map/ppermute | solution.py:415
  68.8 17.7 %copy-start.14 = (bf16[8,16,1024]{2,1,0:T(8,128)(2,1)}, bf16[8,16,1024]{2,1,0:T(8,128)(2,1)S(1)}, u32[]{:S(2)}) copy-start(bf16[8,16,1024]{2,1,0:T(8,128)(2,1)S(1)} %collective-permute-done.2.rest_3_) | copy-start | bytes 786436
  68.9 20.4 %collective-permute-start.7 = (bf16[8,16,1024]{2,1,0:T(8,128)(2,1)}, bf16[8,16,1024]{2,1,0:T(8,128)(2,1)}, u32[]{:S(2)}, u32[]{:S(2)}) collective-permute-start(bf16[8,16,1024]{2,1,0:T(8,128)(2,1)} %get-tuple-element.29.rest_6_), channel_id=1, source_target_pairs={{0,6},{1,7},{2,4},{3,5},{4,2},{5,3},{6,0},{7,1},{8,14},{9,15},{10,... | collective-permute-start | bytes 786440 | tf_op jit(solution)/shard_map/ppermute | solution.py:415
  71.7 14.8 %copy-start.15 = (bf16[8,16,1024]{2,1,0:T(8,128)(2,1)}, bf16[8,16,1024]{2,1,0:T(8,128)(2,1)S(1)}, u32[]{:S(2)}) copy-start(bf16[8,16,1024]{2,1,0:T(8,128)(2,1)S(1)} %collective-permute-done.3.rest_4_) | copy-start | bytes 786436
  71.7 18.9 %collective-permute-start.8 = (bf16[8,16,1024]{2,1,0:T(8,128)(2,1)}, bf16[8,16,1024]{2,1,0:T(8,128)(2,1)}, u32[]{:S(2)}, u32[]{:S(2)}) collective-permute-start(bf16[8,16,1024]{2,1,0:T(8,128)(2,1)} %get-tuple-element.30.rest_2_), channel_id=1, source_target_pairs={{0,2},{1,3},{2,0},{3,1},{4,6},{5,7},{6,4},{7,5},{8,10},{9,11},{10,... | collective-permute-start | bytes 786440 | tf_op jit(solution)/shard_map/ppermute | solution.py:415
  78.9 14.3 %collective-permute-start.9 = (bf16[8,16,1024]{2,1,0:T(8,128)(2,1)}, bf16[8,16,1024]{2,1,0:T(8,128)(2,1)}, u32[]{:S(2)}, u32[]{:S(2)}) collective-permute-start(bf16[8,16,1024]{2,1,0:T(8,128)(2,1)} %get-tuple-element.31.rest_7_), channel_id=1, source_target_pairs={{0,7},{1,6},{2,5},{3,4},{4,3},{5,2},{6,1},{7,0},{8,15},{9,14},{10,... | collective-permute-start | bytes 786440 | tf_op jit(solution)/shard_map/ppermute | solution.py:415
  78.9 21.9 %collective-permute-start.10 = (bf16[8,16,1024]{2,1,0:T(8,128)(2,1)}, bf16[8,16,1024]{2,1,0:T(8,128)(2,1)}, u32[]{:S(2)}, u32[]{:S(2)}) collective-permute-start(bf16[8,16,1024]{2,1,0:T(8,128)(2,1)} %get-tuple-element.32.rest_3_), channel_id=1, source_target_pairs={{0,3},{1,2},{2,1},{3,0},{4,7},{5,6},{6,5},{7,4},{8,11},{9,10},{10,... | collective-permute-start | bytes 786440 | tf_op jit(solution)/shard_map/ppermute | solution.py:415
  86.6 14.2 %copy-start.18 = (bf16[8,16,1024]{2,1,0:T(8,128)(2,1)}, bf16[8,16,1024]{2,1,0:T(8,128)(2,1)S(1)}, u32[]{:S(2)}) copy-start(bf16[8,16,1024]{2,1,0:T(8,128)(2,1)S(1)} %collective-permute-done.6.rest_7_) | copy-start | bytes 786436
  86.6 37.3 %collective-permute-start.11 = (bf16[8,16,1024]{2,1,0:T(8,128)(2,1)S(1)}, bf16[8,16,1024]{2,1,0:T(8,128)(2,1)S(1)}, u32[]{:S(2)}, u32[]{:S(2)}) collective-permute-start(bf16[8,16,1024]{2,1,0:T(8,128)(2,1)S(1)} %copy-done.4), channel_id=1, source_target_pairs={{0,10},{1,11},{2,8},{3,9},{4,14},{5,15},{6,12},{7,13},{8,2},{9,3},... | collective-permute-start | bytes 786440 | tf_op jit(solution)/shard_map/ppermute | solution.py:415
  89.3 35.6 %collective-permute-start.12 = (bf16[8,16,1024]{2,1,0:T(8,128)(2,1)S(1)}, bf16[8,16,1024]{2,1,0:T(8,128)(2,1)S(1)}, u32[]{:S(2)}, u32[]{:S(2)}) collective-permute-start(bf16[8,16,1024]{2,1,0:T(8,128)(2,1)S(1)} %copy-done.3), channel_id=1, source_target_pairs={{0,14},{1,15},{2,12},{3,13},{4,10},{5,11},{6,8},{7,9},{8,6},{9,7},... | collective-permute-start | bytes 786440 | tf_op jit(solution)/shard_map/ppermute | solution.py:415
  90.6 37.7 %collective-permute-start.13 = (bf16[8,16,1024]{2,1,0:T(8,128)(2,1)S(1)}, bf16[8,16,1024]{2,1,0:T(8,128)(2,1)S(1)}, u32[]{:S(2)}, u32[]{:S(2)}) collective-permute-start(bf16[8,16,1024]{2,1,0:T(8,128)(2,1)S(1)} %copy-done.2), channel_id=1, source_target_pairs={{0,11},{1,10},{2,9},{3,8},{4,15},{5,14},{6,13},{7,12},{8,3},{9,2},... | collective-permute-start | bytes 786440 | tf_op jit(solution)/shard_map/ppermute | solution.py:415
  93.2 42.9 %collective-permute-start.14 = (bf16[8,16,1024]{2,1,0:T(8,128)(2,1)S(1)}, bf16[8,16,1024]{2,1,0:T(8,128)(2,1)S(1)}, u32[]{:S(2)}, u32[]{:S(2)}) collective-permute-start(bf16[8,16,1024]{2,1,0:T(8,128)(2,1)S(1)} %copy-done.1), channel_id=1, source_target_pairs={{0,15},{1,14},{2,13},{3,12},{4,11},{5,10},{6,9},{7,8},{8,7},{9,6},... | collective-permute-start | bytes 786440 | tf_op jit(solution)/shard_map/ppermute | solution.py:415
  (11 other events, 82.0 us)

commit v4 on v3

v4 whole, which is shorter than its diff:
```python
import functools

import jax
import jax.numpy as jnp
from jax import lax
from jax.experimental import pallas as pl
from jax.experimental.pallas import tpu as pltpu
from jax.sharding import PartitionSpec as P

HEAD_WIDTH = 128
KEY_VALUE_HEADS = 4
QUERY_GROUP = 12
SELP = 2
LANES = 128
ROW_SLOTS = 16
VMEM_LIMIT = 60 * 1024 * 1024
QUERY_BLOCK = 32
TILE_PAGES = 16
LATE_TILE_PAGES = 8
HIDDEN = -1e30
FAR_PAGE = 1 << 20


def nt_dot(a, b):
    return lax.dot_general(a, b, (((1,), (1,)), ((), ())), preferred_element_type=jnp.float32)


def one_hot(condition):
    return jnp.where(condition, 1.0, 0.0)


def pair_places(hold, page_len, table_ref, sel_ref, wide):
    pages = table_ref.shape[1]
    picked = sel_ref.shape[1]
    f32 = jnp.float32
    slots = jnp.broadcast_to(table_ref[...], (pages, pages))
    owners = slots // hold
    local_row = (slots - owners * hold).astype(f32)[0:1]
    owner_row = owners.astype(f32)
    owner_col = owner_row.T
    sub = lax.broadcasted_iota(jnp.int32, (pages, pages), 0)
    lane = lax.broadcasted_iota(jnp.int32, (pages, pages), 1)
    earlier = one_hot((owner_row == owner_col) & (lane < sub))
    rank_col = jnp.sum(earlier, axis=1, keepdims=True)

    wide[...] = jnp.full(wide.shape, -1, jnp.int32)
    wide[0:1, 0:picked] = sel_ref[...]
    position = wide[...]
    page = lax.shift_right_arithmetic(position, page_len.bit_length() - 1)
    offset = (position & (page_len - 1)).astype(f32)[0:1]
    lane_wide = lax.broadcasted_iota(jnp.int32, wide.shape, 1)
    second = one_hot((page == pltpu.roll(page, 1, axis=1)) & (lane_wide > 0))[0:1]
    valid = lane_wide[0:1] < picked
    sub_wide = lax.broadcasted_iota(jnp.int32, (pages, wide.shape[1]), 0)
    in_page = one_hot(sub_wide == page[0:1])
    owner = jnp.sum(in_page * owner_col[:, 0:1], axis=0, keepdims=True)
    rank = jnp.sum(in_page * rank_col, axis=0, keepdims=True)
    return owner_row[0:1], local_row, rank_col, owner, rank, second, offset, valid


def index_kernel(hold, page_len, table_ref, sel_ref, out_ref, wide):
    holders = out_ref.shape[0]
    pages = table_ref.shape[1]
    f32 = jnp.float32
    bf16 = jnp.bfloat16
    owner_row, local_row, rank_col, owner, rank, second, offset, valid = pair_places(
        hold, page_len, table_ref, sel_ref, wide
    )
    holder = lax.broadcasted_iota(jnp.int32, (holders, pages), 0).astype(f32)
    owned = jnp.where(holder == owner_row, local_row, 0.0)
    lane = lax.broadcasted_iota(jnp.int32, (pages, LANES), 1).astype(f32)
    numbers = jnp.dot(
        owned.astype(bf16), one_hot(lane == rank_col).astype(bf16), preferred_element_type=f32
    )
    holder_wide = lax.broadcasted_iota(jnp.int32, (holders, wide.shape[1]), 0).astype(f32)
    marked = jnp.where((holder_wide == owner) & valid, rank * page_len + offset + 1.0, 0.0)
    place_lane = lax.broadcasted_iota(jnp.int32, (LANES, wide.shape[1]), 0).astype(f32)
    at_place = one_hot(place_lane == SELP * rank + second)
    targets = nt_dot(marked.astype(bf16), at_place.astype(bf16))
    for h in range(holders):
        out_ref[h, 0:1, :] = numbers[h : h + 1, :].astype(jnp.int32)
        out_ref[h, 1:2, :] = targets[h : h + 1, :].astype(jnp.int32)


def rows_kernel(hold, page_len, early, own, table_ref, sel_ref, fresh_ref, packed_out, *rest):
    outs, wide, packed, sem = rest[:-3], rest[-3], rest[-2], rest[-1]
    holders = packed.shape[0]
    picked = sel_ref.shape[1]
    f32 = jnp.float32
    _, _, _, owner, rank, second, _, valid = pair_places(hold, page_len, table_ref, sel_ref, wide)
    spot = jnp.where(valid, owner * ROW_SLOTS + SELP * rank + second, -1.0)[:, 0:picked]
    step = min(holders, 16)
    for start in range(0, holders, step):
        spot_id = lax.broadcasted_iota(jnp.int32, (step * ROW_SLOTS, picked), 0).astype(f32)
        choose = one_hot(spot_id + float(start * ROW_SLOTS) == spot).astype(jnp.bfloat16)
        rows = jnp.dot(choose, fresh_ref[...], preferred_element_type=f32).astype(jnp.bfloat16)
        packed[start : start + step] = rows.reshape(step, ROW_SLOTS, fresh_ref.shape[1])
    copies = [pltpu.make_async_copy(packed, packed_out, sem)]
    for d, out in zip(early, outs):
        copies.append(pltpu.make_async_copy(packed.at[pl.ds(own[0] ^ d, 1)], out, sem))
    for copy in copies:
        copy.start()
    for copy in copies:
        copy.wait()


def gather_kernel(capacity, own, index, store_hbm, rows_hbm, *rest):
    sends, (store, rows, load_sem, rows_sem, send_sem) = rest[:-5], rest[-5:]
    load = pltpu.make_async_copy(store_hbm, store, load_sem)
    load_rows = pltpu.make_async_copy(rows_hbm, rows, rows_sem)
    load.start()
    load_rows.start()
    load_rows.wait()
    load.wait()
    for d, send in enumerate(sends):
        r = own[0] ^ d
        for k in range(capacity):
            pltpu.make_async_copy(store.at[index[r, 0, k]], send.at[k], send_sem).start()
        if send.shape[0] > capacity:
            pltpu.make_async_copy(rows.at[r], send.at[capacity], send_sem).start()
    for send in sends:
        pltpu.make_async_copy(send, send, send_sem).wait()


def write_back_kernel(own, index, targets_ref, store_hbm, *rest):
    holders = index.shape[0]
    arrived, store_out = rest[:holders], rest[holders]
    store, rows, blended, load_sem, rows_sem, out_sem = rest[holders + 1 :]
    _, capacity, page_len, width = blended.shape
    rows_here = capacity * page_len
    f32 = jnp.float32
    load = pltpu.make_async_copy(store_hbm, store, load_sem)
    load.start()
    for d in range(holders):
        last = arrived[d].shape[0] - 1
        pltpu.make_async_copy(arrived[d].at[last], rows.at[d], rows_sem).start()
    pltpu.make_async_copy(rows, rows, rows_sem).wait()
    load.wait()
    row_id = lax.broadcasted_iota(jnp.int32, (rows_here, ROW_SLOTS), 0)

    def one_request(d, carry):
        r = own[0] ^ d
        hit = one_hot(row_id == targets_ref[r][1:2, 0:ROW_SLOTS] - 1)
        keep = 1.0 - jnp.sum(hit, axis=1, keepdims=True)
        keep = jnp.broadcast_to(keep, (rows_here, LANES)).astype(jnp.bfloat16)
        hit = hit.astype(jnp.bfloat16)
        for c in range(width // LANES):
            lanes = slice(c * LANES, (c + 1) * LANES)
            fresh = jnp.dot(hit, rows[d, :, lanes], preferred_element_type=f32).astype(jnp.bfloat16)
            for k in range(capacity):
                part = slice(k * page_len, (k + 1) * page_len)
                blended[d, k, :, lanes] = store[index[r, 0, k], :, lanes] * keep[part] + fresh[part]
        for k in range(capacity):
            pltpu.make_async_copy(blended.at[d, k], store_out.at[index[r, 0, k]], out_sem).start()
        return carry

    lax.fori_loop(0, holders, one_request, 0)
    pltpu.make_async_copy(store_out, store_out, out_sem).wait()


def attend_kernel(first, last, tile_pages, sources, capacity, place, page_number, tiles, *rest):
    sel_ref, positions_ref, fresh_ref, query_ref, *rest = rest
    state_in = [] if first else [rest.pop(0) for _ in range(2)]
    contexts = [rest.pop(0) for _ in range(sources)]
    outs = [rest.pop(0) for _ in range(1 if last else 2)]
    kv, values, query, mixed, stats, sem = rest
    pages, page_len, width = kv.shape
    used = sources * capacity
    block = query_ref.shape[0]
    tile = tile_pages * page_len
    lanes = QUERY_GROUP * block
    scale = 1.4426950408889634 / HEAD_WIDTH**0.5
    f32 = jnp.float32
    bf16 = jnp.bfloat16
    step = pl.program_id(0)
    eye = one_hot(
        lax.broadcasted_iota(jnp.int32, (LANES, LANES), 0)
        == lax.broadcasted_iota(jnp.int32, (LANES, LANES), 1)
    ).astype(bf16)

    @pl.when(step == 0)
    def _():
        for i, context in enumerate(contexts):
            for k in range(capacity):
                pltpu.make_async_copy(context.at[k], kv.at[place[i * capacity + k]], sem).start()
        if pages > used:
            kv[used:] = jnp.zeros((pages - used, page_len, width), bf16)
        pltpu.make_async_copy(kv.at[0:used], kv.at[0:used], sem).wait()
        positions = positions_ref[...]
        row = lax.broadcasted_iota(jnp.int32, (page_len, positions.shape[1]), 0)
        ones = jnp.ones((positions.shape[1], LANES), bf16)

        def blend_and_turn(t, carry):
            here = pl.ds(t * tile_pages, tile_pages)
            hit = jnp.concatenate(
                [
                    one_hot(row + page_number[t * tile_pages + k] * page_len == positions)
                    for k in range(tile_pages)
                ],
                axis=0,
            ).astype(bf16)
            keep = (1.0 - jnp.dot(hit, ones, preferred_element_type=f32)).astype(bf16)
            for c in range(width // LANES):
                part = slice(c * LANES, (c + 1) * LANES)
                fresh = jnp.dot(hit, fresh_ref[:, part], preferred_element_type=f32).astype(bf16)
                old = kv[here, :, part].reshape(tile, LANES)
                new = old * keep + fresh
                kv[here, :, part] = new.reshape(tile_pages, page_len, LANES)
                if c >= KEY_VALUE_HEADS:
                    values[t, c - KEY_VALUE_HEADS] = nt_dot(eye, new).astype(bf16)
            return carry

        lax.fori_loop(0, pages // tile_pages, blend_and_turn, 0)

    for g in range(KEY_VALUE_HEADS):
        for i in range(QUERY_GROUP):
            head = g * QUERY_GROUP + i
            query[g, i * block : (i + 1) * block, :] = query_ref[:, head * LANES : (head + 1) * LANES]
    if first:
        mixed[...] = jnp.zeros(mixed.shape, f32)
        stats[0:KEY_VALUE_HEADS, :] = jnp.full((KEY_VALUE_HEADS, lanes), HIDDEN, f32)
        stats[KEY_VALUE_HEADS:, :] = jnp.zeros((KEY_VALUE_HEADS, lanes), f32)
    else:
        mixed[...] = state_in[0][0]
        stats[...] = state_in[1][0]

    sel = sel_ref[0]
    in_page = lax.broadcasted_iota(jnp.int32, (page_len, LANES), 0)

    def one_tile(t, carry):
        here = pl.ds(t * tile_pages, tile_pages)
        bias = jnp.concatenate(
            [
                jnp.where(in_page + page_number[t * tile_pages + k] * page_len <= sel, 0.0, HIDDEN)
                for k in range(tile_pages)
            ],
            axis=0,
        ).astype(f32)

        def score(g):
            key = kv[here, :, g * LANES : (g + 1) * LANES].reshape(tile, LANES)
            return nt_dot(key, query[g])

        upcoming = score(0)
        for g in range(KEY_VALUE_HEADS):
            scores = upcoming
            if g + 1 < KEY_VALUE_HEADS:
                upcoming = score(g + 1)
            raised, shrinks = [], []
            at = KEY_VALUE_HEADS + g
            for n in range(lanes // LANES):
                part = slice(n * LANES, (n + 1) * LANES)
                s = scores[:, part] + bias
                old = stats[g : g + 1, part]
                new = jnp.maximum(old, jnp.max(s, axis=0, keepdims=True))
                p = jnp.exp2((s - new) * scale)
                shrink = jnp.exp2((old - new) * scale)
                stats[at : at + 1, part] = stats[at : at + 1, part] * shrink + jnp.sum(
                    p, axis=0, keepdims=True
                )
                stats[g : g + 1, part] = new
                raised.append(p.astype(bf16))
                shrinks.append(shrink)
            raised = jnp.concatenate(raised, axis=1)
            shrink = jnp.concatenate(shrinks, axis=1)
            mixed[g] = mixed[g] * shrink + jnp.dot(
                values[t, g], raised, preferred_element_type=f32
            )
        return carry

    lax.fori_loop(0, tiles[step], one_tile, 0)

    if last:
        done = []
        for g in range(KEY_VALUE_HEADS):
            at = KEY_VALUE_HEADS + g
            part = (mixed[g] * (1.0 / stats[at : at + 1, :])).astype(bf16)
            done += [part[:, n * LANES : (n + 1) * LANES] for n in range(lanes // LANES)]
        turned = nt_dot(eye, jnp.concatenate(done, axis=0)).astype(bf16)
        for n in range(len(done)):
            for i in range(LANES // block):
                head = n * (LANES // block) + i
                outs[0][:, head * LANES : (head + 1) * LANES] = turned[
                    i * block : (i + 1) * block, n * LANES : (n + 1) * LANES
                ]
    else:
        outs[0][0] = mixed[...]
        outs[1][0] = stats[...]


def attend(first, last, tile_pages, capacity, order, sel_lanes, positions, fresh, queries, state, contexts):
    picked, features = queries.shape
    _, page_len, width = contexts[0].shape
    pages = order[1].shape[0]
    steps = picked // QUERY_BLOCK
    lanes = QUERY_GROUP * QUERY_BLOCK
    wide = pl.BlockSpec((QUERY_BLOCK, features), lambda b, *_: (b, 0))
    state_specs = [
        pl.BlockSpec((1, KEY_VALUE_HEADS, LANES, lanes), lambda b, *_: (b, 0, 0, 0)),
        pl.BlockSpec((1, 2 * KEY_VALUE_HEADS, lanes), lambda b, *_: (b, 0, 0)),
    ]
    state_shapes = [
        jax.ShapeDtypeStruct((steps, KEY_VALUE_HEADS, LANES, lanes), jnp.float32),
        jax.ShapeDtypeStruct((steps, 2 * KEY_VALUE_HEADS, lanes), jnp.float32),
    ]
    share = 0.6
    return pl.pallas_call(
        functools.partial(attend_kernel, first, last, tile_pages, len(contexts), capacity),
        grid_spec=pltpu.PrefetchScalarGridSpec(
            num_scalar_prefetch=3,
            grid=(steps,),
            in_specs=[
                pl.BlockSpec((1, 1, LANES), lambda b, *_: (b, 0, 0)),
                pl.BlockSpec(positions.shape, lambda b, *_: (0, 0)),
                pl.BlockSpec(fresh.shape, lambda b, *_: (0, 0)),
                wide,
                *([] if first else state_specs),
                *[pl.BlockSpec(memory_space=pltpu.HBM)] * len(contexts),
            ],
            out_specs=[wide] if last else state_specs,
            scratch_shapes=[
                pltpu.VMEM((pages, page_len, width), jnp.bfloat16),
                pltpu.VMEM(
                    (pages // tile_pages, KEY_VALUE_HEADS, LANES, tile_pages * page_len), jnp.bfloat16
                ),
                pltpu.VMEM((KEY_VALUE_HEADS, lanes, LANES), jnp.bfloat16),
                pltpu.VMEM((KEY_VALUE_HEADS, LANES, lanes), jnp.float32),
                pltpu.VMEM((2 * KEY_VALUE_HEADS, lanes), jnp.float32),
                pltpu.SemaphoreType.DMA,
            ],
        ),
        out_shape=[jax.ShapeDtypeStruct((picked, features), jnp.bfloat16)] if last else state_shapes,
        compiler_params=pltpu.CompilerParams(
            dimension_semantics=("arbitrary",), vmem_limit_bytes=VMEM_LIMIT
        ),
        cost_estimate=pl.CostEstimate(
            flops=int(share * 8 * picked * features * pages * page_len),
            bytes_accessed=2 * pages * page_len * width + 6 * picked * features,
            transcendentals=int(share * picked * features // LANES * pages * page_len),
        ),
    )(*order, sel_lanes, positions, fresh, queries, *state, *contexts)


def page_order(slots, positions, own, hold, capacity, groups, page_len):
    pages = slots.shape[0]
    number = jnp.arange(pages)
    before = number[None, :] < number[:, None]
    owners = slots // hold
    ranks = jnp.sum(((owners[None, :] == owners[:, None]) & before).astype(jnp.int32), axis=1)
    distance = owners ^ own
    last_page = positions.reshape(-1, QUERY_BLOCK)[:, -1] // page_len
    orders = []
    for group, tile_pages in groups:
        count = len(group) * capacity
        arrival = jnp.full((pages,), -1, jnp.int32)
        for i, d in enumerate(group):
            arrival = jnp.where(distance == d, i * capacity + ranks, arrival)
        member = arrival >= 0
        place = jnp.sum((member[None, :] & before).astype(jnp.int32), axis=1)
        index = jnp.arange(count)[:, None]
        places = jnp.sum(jnp.where(arrival[None, :] == index, place[None, :], 0), axis=1)
        index = jnp.arange(-(-count // tile_pages) * tile_pages)[:, None]
        page = jnp.sum(
            jnp.where(member[None, :] & (place[None, :] == index), number[None, :], 0), axis=1
        )
        page = jnp.where(index[:, 0] < count, page, FAR_PAGE)
        seen = jnp.sum((page[None, :] <= last_page[:, None]).astype(jnp.int32), axis=1)
        orders.append((places, page, (seen + tile_pages - 1) // tile_pages))
    return orders


def per_device(store, page_table, sel_pos, fresh_kv, queries):
    holders = lax.axis_size("store")
    hold, page_len, width = store.shape
    pages = page_table.shape[1]
    picked = sel_pos.shape[1]
    capacity = max(1, pages // holders)
    hbm = pl.BlockSpec(memory_space=pltpu.HBM)
    vmem = pl.BlockSpec(memory_space=pltpu.VMEM)
    dma = pltpu.SemaphoreType.DMA
    params = pltpu.CompilerParams(vmem_limit_bytes=VMEM_LIMIT)
    own = lax.axis_index("store")
    own_word = own.reshape(1).astype(jnp.int32)
    fresh = fresh_kv[0]
    wide = pltpu.VMEM((8, -(-picked // LANES) * LANES), jnp.int32)
    if holders == 16:
        order = (8, 4, 12, 5, 9, 6, 13, 7, 10, 1, 14, 2, 11, 3, 15)
        late = (14, 11, 15)
        early_rows = late
    else:
        order = tuple(range(1, holders))
        late = ()
        early_rows = ()
    groups = [((0, *[d for d in order if d not in late]), TILE_PAGES)]
    if late:
        groups.append((late, LATE_TILE_PAGES))

    def swap(x, d):
        return lax.ppermute(x, "store", [(h, h ^ d) for h in range(holders)])

    index = pl.pallas_call(
        functools.partial(index_kernel, hold, page_len),
        out_shape=jax.ShapeDtypeStruct((holders, 2, LANES), jnp.int32),
        scratch_shapes=[wide],
        compiler_params=params,
    )(page_table, sel_pos)
    index, table, positions = lax.optimization_barrier((index, page_table, sel_pos))
    index_in = lax.all_to_all(index, "store", split_axis=0, concat_axis=0, tiled=True)

    packed, *early_parts = pl.pallas_call(
        functools.partial(rows_kernel, hold, page_len, early_rows),
        grid_spec=pltpu.PrefetchScalarGridSpec(
            num_scalar_prefetch=1,
            grid=(1,),
            in_specs=[vmem, vmem, vmem],
            out_specs=[hbm] * (1 + len(early_rows)),
            scratch_shapes=[wide, pltpu.VMEM((holders, ROW_SLOTS, width), store.dtype), dma],
        ),
        out_shape=[
            jax.ShapeDtypeStruct((holders, ROW_SLOTS, width), store.dtype),
            *[jax.ShapeDtypeStruct((1, ROW_SLOTS, width), store.dtype)] * len(early_rows),
        ],
        compiler_params=params,
    )(own_word, table, positions, fresh)
    rows_in = {d: swap(part, d) for d, part in zip(early_rows, early_parts)}

    parts = pl.pallas_call(
        functools.partial(gather_kernel, capacity),
        grid_spec=pltpu.PrefetchScalarGridSpec(
            num_scalar_prefetch=2,
            grid=(1,),
            in_specs=[hbm, hbm],
            out_specs=[hbm] * holders,
            scratch_shapes=[
                pltpu.VMEM(store.shape, store.dtype),
                pltpu.VMEM((holders, ROW_SLOTS, width), store.dtype),
                dma,
                dma,
                dma,
            ],
        ),
        out_shape=[
            jax.ShapeDtypeStruct((capacity + (d not in early_rows), page_len, width), store.dtype)
            for d in range(holders)
        ],
        compiler_params=params,
    )(own_word, index_in, store, packed)
    arrived = {0: parts[0]}
    for d in order:
        arrived[d] = swap(parts[d], d)

    store_out = pl.pallas_call(
        write_back_kernel,
        grid_spec=pltpu.PrefetchScalarGridSpec(
            num_scalar_prefetch=2,
            grid=(1,),
            in_specs=[vmem, hbm] + [hbm] * holders,
            out_specs=hbm,
            scratch_shapes=[
                pltpu.VMEM(store.shape, store.dtype),
                pltpu.VMEM((holders, ROW_SLOTS, width), store.dtype),
                pltpu.VMEM((holders, capacity, page_len, width), store.dtype),
                dma,
                dma,
                dma,
            ],
        ),
        out_shape=jax.ShapeDtypeStruct(store.shape, store.dtype),
        compiler_params=params,
        cost_estimate=pl.CostEstimate(flops=0, bytes_accessed=4 * store.size, transcendentals=0),
    )(own_word, index_in, index_in, store, *[rows_in.get(d, arrived[d]) for d in range(holders)])

    orders = page_order(table[0], positions[0], own, hold, capacity, groups, page_len)
    sel_lanes = jnp.tile(positions.reshape(-1, 1, QUERY_BLOCK), (1, 1, LANES // QUERY_BLOCK))
    store_out, sel_lanes = lax.optimization_barrier((store_out, sel_lanes))
    state = ()
    for at, ((group, tile_pages), order) in enumerate(zip(groups, orders)):
        state = attend(
            at == 0,
            at == len(groups) - 1,
            tile_pages,
            capacity,
            order,
            sel_lanes,
            sel_pos,
            fresh,
            queries[0],
            state,
            [arrived[d] for d in group],
        )
    return (state[0][None], store_out)


def solution(mesh):
    return jax.shard_map(
        per_device,
        mesh=mesh,
        in_specs=(
            P(("groups", "store"), None, None),
            P(("groups", "store"), None),
            P(("groups", "store"), None),
            P(("groups", "store"), None, None),
            P(("groups", "store"), None, None),
        ),
        out_specs=(P(("groups", "store"), None, None), P(("groups", "store"), None, None)),
        check_vma=False,
    )
```

time: 153 us -> 188 us (1.23)
  Pallas kernels: 51.4 us -> 67 us
  starting transfers between devices: 27.8 us -> 42.6 us
  waiting for transfers between devices: 63.4 us -> 66.4 us
    ppermute x15 -> x18, waiting for transfers between devices: 50.8 us -> 66.4 us  [swap(): return lax.ppermute(x, 'store', [(h, h ^ d) for h in range(holders)])]
    ppermute x15 -> x18, starting transfers between devices: 21.2 us -> 36 us  [swap(): return lax.ppermute(x, 'store', [(h, h ^ d) for h in range(holders)])]
    all_to_all x1, waiting for transfers between devices: 12.6 us -> 0.01 us  [per_device(): lax.all_to_all(index, 'store', split_axis=0, concat_axis=0, tiled=True)]
    pallas_call x2, Pallas kernels: 38.6 us -> 49.5 us  [attend(): pl.pallas_call(functools.partial(attend_kernel, first, last, tile_pages,...]
    pallas_call x1, Pallas kernels: 5.03 us -> 8.19 us  [per_device(): pl.pallas_call(write_back_kernel, grid_spec=pltpu.PrefetchScalarGridSpec(...]
    pallas_call x2 -> x3, Pallas kernels: 7.79 us -> 9.34 us  [the longest x1 5.32 us: per_device(): pl.pallas_call(functools.partial(gather_kernel, capacity), grid_spec=pltp...]
  transfers between devices with their start and end apart: 16 -> 19, of which waited for: 9 -> 8; matrix products, arithmetic and copies ran while one was open for 5% -> 4% of each run, Pallas kernels for 18% -> 26%
where the time goes in v4:
time: 188 us
  Pallas kernels  67 us (36%)
  waiting for transfers between devices  66.4 us (35%)
  starting transfers between devices  42.6 us (23%)
  other arithmetic  6.56 us (3%)
  local copies, waits for them, and re-layouts  4.67 us (2%)
    ppermute x18, waiting for transfers between devices, swap(): return lax.ppermute(x, 'store', [(h, h ^ d) for h in range(holders)])  66.4 us
    pallas_call x2, Pallas kernels, attend(): pl.pallas_call(functools.partial(attend_kernel, first, last, tile_pages,...  49.5 us
    ppermute x18, starting transfers between devices, swap(): return lax.ppermute(x, 'store', [(h, h ^ d) for h in range(holders)])  36 us
    pallas_call x1, Pallas kernels, per_device(): pl.pallas_call(write_back_kernel, grid_spec=pltpu.PrefetchScalarGridSpec(...  8.19 us
    all_to_all x1, starting transfers between devices, per_device(): lax.all_to_all(index, 'store', split_axis=0, concat_axis=0, tiled=True)  6.58 us
    pallas_call x1, Pallas kernels, per_device(): pl.pallas_call(functools.partial(gather_kernel, capacity), grid_spec=pltp...  5.32 us
  transfers between devices with their start and end apart: 19, of which 8 were waited for; matrix products, arithmetic and copies ran while one was open for 4% of the time, Pallas kernels for 26%

profile of v4, /device:TPU:9, one launch (start us, length us, event | category | flops | bytes accessed | tf_op | source)
XLA Modules:
  0.0 188.1 jit_solution(4206410872911450344)
XLA Ops:
  0.6 1.7 shard_map.68
  2.3 6.6 %all-to-all-start = ((s32[16,2,128]{2,1,0:T(2,128)}), s32[16,2,128]{2,1,0:T(2,128)S(1)}, u32[]{:S(2)}, u32[]{:S(2)}) async-start(s32[16,2,128]{2,1,0:T(2,128)} %shard_map.68), calls=%async_computation | async-start | bytes 32768 | tf_op jit(solution)/shard_map/all_to_all | solution.py:408
  8.9 2.4 %shard_map.69 = (bf16[16,16,1024]{2,1,0:T(8,128)(2,1)}, bf16[1,16,1024]{2,1,0:T(8,128)(2,1)}, bf16[1,16,1024]{2,1,0:T(8,128)(2,1)}, bf16[1,16,1024]{2,1,0:T(8,128)(2,1)}) custom-call(s32[1]{0:T(128)} %bitcast.6.own, s32[1,128]{1,0:T(1,128)} %table_ref.2, s32[1,160]{1,0:T(1,128)} %rest_1_.3, bf16[160,1024]{1,0:T(8,128)(2,1)} %bitcast.70), custom_call_target="tpu_custom_call" | custom-call | tf_op jit(solution)/shard_map/pallas_call | solution.py:410
  11.2 3.3 %collective-permute-start.10 = (bf16[1,16,1024]{2,1,0:T(8,128)(2,1)}, bf16[1,16,1024]{2,1,0:T(8,128)(2,1)S(1)}, u32[]{:S(2)}, u32[]{:S(2)}) collective-permute-start(bf16[1,16,1024]{2,1,0:T(8,128)(2,1)} %get-tuple-element.44), channel_id=1, source_target_pairs={{0,11},{1,10},{2,9},{3,8},{4,15},{5,14},{6,13},{7,12},{8,3},{9,2},... | collective-permute-start | bytes 98312 | tf_op jit(solution)/shard_map/ppermute | solution.py:399
  14.5 2.7 %collective-permute-start.14 = (bf16[1,16,1024]{2,1,0:T(8,128)(2,1)}, bf16[1,16,1024]{2,1,0:T(8,128)(2,1)S(1)}, u32[]{:S(2)}, u32[]{:S(2)}) collective-permute-start(bf16[1,16,1024]{2,1,0:T(8,128)(2,1)} %get-tuple-element.48), channel_id=1, source_target_pairs={{0,15},{1,14},{2,13},{3,12},{4,11},{5,10},{6,9},{7,8},{8,7},{9,6},... | collective-permute-start | bytes 98312 | tf_op jit(solution)/shard_map/ppermute | solution.py:399
  23.1 5.3 %shard_map.70 = (bf16[9,16,1024]{2,1,0:T(8,128)(2,1)}, bf16[9,16,1024]{2,1,0:T(8,128)(2,1)}, bf16[9,16,1024]{2,1,0:T(8,128)(2,1)}, bf16[9,16,1024]{2,1,0:T(8,128...) custom-call(s32[1]{0:T(128)} %bitcast.6.own, ...), custom_call_target="tpu_custom_call" | custom-call | tf_op jit(solution)/shard_map/pallas_call | solution.py:427
  29.7 1.8 collective-permute-start.2
  32.1 2.1 %collective-permute-start.3 = (bf16[9,16,1024]{2,1,0:T(8,128)(2,1)}, bf16[9,16,1024]{2,1,0:T(8,128)(2,1)S(1)}, u32[]{:S(2)}, u32[]{:S(2)}) collective-permute-start(bf16[9,16,1024]{2,1,0:T(8,128)(2,1)} %get-tuple-element.37), channel_id=1, source_target_pairs={{0,4},{1,5},{2,6},{3,7},{4,0},{5,1},{6,2},{7,3},{8,12},{9,13},{10,... | collective-permute-start | bytes 884744 | tf_op jit(solution)/shard_map/ppermute | solution.py:399
  36.9 4.1 %collective-permute-start.6 = (bf16[9,16,1024]{2,1,0:T(8,128)(2,1)}, bf16[9,16,1024]{2,1,0:T(8,128)(2,1)S(1)}, u32[]{:S(2)}, u32[]{:S(2)}) collective-permute-start(bf16[9,16,1024]{2,1,0:T(8,128)(2,1)} %get-tuple-element.40), channel_id=1, source_target_pairs={{0,7},{1,6},{2,5},{3,4},{4,3},{5,2},{6,1},{7,0},{8,15},{9,14},{10,... | collective-permute-start | bytes 884744 | tf_op jit(solution)/shard_map/ppermute | solution.py:399
  41.7 2.4 %collective-permute-done.2.rest_3_.rest_16_ = bf16[9,16,1024]{2,1,0:T(8,128)(2,1)S(1)} collective-permute-done((bf16[9,16,1024]{2,1,0:T(8,128)(2,1)}, bf16[9,16,1024]{2,1,0:T(8,128)(2,1)S(1)}, u32[]{:S(2)}, u32[]{:S(2)}) %collective-permute-start.2) | collective-permute-done | bytes 294944 | tf_op jit(solution)/shard_map/ppermute | solution.py:399
  44.1 2.1 %collective-permute-start.7 = (bf16[9,16,1024]{2,1,0:T(8,128)(2,1)}, bf16[9,16,1024]{2,1,0:T(8,128)(2,1)S(1)}, u32[]{:S(2)}, u32[]{:S(2)}) collective-permute-start(bf16[9,16,1024]{2,1,0:T(8,128)(2,1)} %get-tuple-element.41), channel_id=1, source_target_pairs={{0,8},{1,9},{2,10},{3,11},{4,12},{5,13},{6,14},{7,15},{8,0},{9,1},... | collective-permute-start | bytes 884744 | tf_op jit(solution)/shard_map/ppermute | solution.py:399
  46.2 2.0 %collective-permute-done.4.rest_5_.rest_8_ = bf16[9,16,1024]{2,1,0:T(8,128)(2,1)S(1)} collective-permute-done((bf16[9,16,1024]{2,1,0:T(8,128)(2,1)}, bf16[9,16,1024]{2,1,0:T(8,128)(2,1)S(1)}, u32[]{:S(2)}, u32[]{:S(2)}) %collective-permute-start.4) | collective-permute-done | bytes 294944 | tf_op jit(solution)/shard_map/ppermute | solution.py:399
  48.2 1.8 collective-permute-start.9
  50.0 15.8 %collective-permute-done.5.rest_6_.rest_10_ = bf16[9,16,1024]{2,1,0:T(8,128)(2,1)S(1)} collective-permute-done((bf16[9,16,1024]{2,1,0:T(8,128)(2,1)}, bf16[9,16,1024]{2,1,0:T(8,128)(2,1)S(1)}, u32[]{:S(2)}, u32[]{:S(2)}) %collective-permute-start.5) | collective-permute-done | bytes 294944 | tf_op jit(solution)/shard_map/ppermute | solution.py:399
  67.0 5.1 %collective-permute-done.6.rest_7_.rest_12_ = bf16[9,16,1024]{2,1,0:T(8,128)(2,1)S(1)} collective-permute-done((bf16[9,16,1024]{2,1,0:T(8,128)(2,1)}, bf16[9,16,1024]{2,1,0:T(8,128)(2,1)S(1)}, u32[]{:S(2)}, u32[]{:S(2)}) %collective-permute-start.6) | collective-permute-done | bytes 294944 | tf_op jit(solution)/shard_map/ppermute | solution.py:399
  72.1 1.7 collective-permute-start.12
  75.4 6.0 %collective-permute-start.16 = (bf16[8,16,1024]{2,1,0:T(8,128)(2,1)}, bf16[8,16,1024]{2,1,0:T(8,128)(2,1)S(1)}, u32[]{:S(2)}, u32[]{:S(2)}) collective-permute-start(bf16[8,16,1024]{2,1,0:T(8,128)(2,1)} %get-tuple-element.53), channel_id=1, source_target_pairs={{0,11},{1,10},{2,9},{3,8},{4,15},{5,14},{6,13},{7,12},{8,3},{9,2},... | collective-permute-start | bytes 786440 | tf_op jit(solution)/shard_map/ppermute | solution.py:399
  81.4 21.9 %collective-permute-done.9.rest_10_.rest_13_ = bf16[9,16,1024]{2,1,0:T(8,128)(2,1)S(1)} collective-permute-done((bf16[9,16,1024]{2,1,0:T(8,128)(2,1)}, bf16[9,16,1024]{2,1,0:T(8,128)(2,1)S(1)}, u32[]{:S(2)}, u32[]{:S(2)}) %collective-permute-start.9) | collective-permute-done | bytes 294944 | tf_op jit(solution)/shard_map/ppermute | solution.py:399
  103.2 7.0 %collective-permute-start.17 = (bf16[8,16,1024]{2,1,0:T(8,128)(2,1)}, bf16[8,16,1024]{2,1,0:T(8,128)(2,1)}, u32[]{:S(2)}, u32[]{:S(2)}) collective-permute-start(bf16[8,16,1024]{2,1,0:T(8,128)(2,1)} %get-tuple-element.54), channel_id=1, source_target_pairs={{0,15},{1,14},{2,13},{3,12},{4,11},{5,10},{6,9},{7,8},{8,7},{9,6},... | collective-permute-start | bytes 786440 | tf_op jit(solution)/shard_map/ppermute | solution.py:399
  110.2 12.3 %collective-permute-done.11.rest_12_.rest_7_ = bf16[9,16,1024]{2,1,0:T(8,128)(2,1)S(1)} collective-permute-done((bf16[9,16,1024]{2,1,0:T(8,128)(2,1)}, bf16[9,16,1024]{2,1,0:T(8,128)(2,1)S(1)}, u32[]{:S(2)}, u32[]{:S(2)}) %collective-permute-start.11) | collective-permute-done | bytes 294944 | tf_op jit(solution)/shard_map/ppermute | solution.py:399
  122.5 6.3 %collective-permute-done.12.rest_13_.rest_11_ = bf16[9,16,1024]{2,1,0:T(8,128)(2,1)S(1)} collective-permute-done((bf16[9,16,1024]{2,1,0:T(8,128)(2,1)}, bf16[9,16,1024]{2,1,0:T(8,128)(2,1)S(1)}, u32[]{:S(2)}, u32[]{:S(2)}) %collective-permute-start.12) | collective-permute-done | bytes 294944 | tf_op jit(solution)/shard_map/ppermute | solution.py:399
  129.6 8.2 %shard_map.71 = bf16[128,16,1024]{2,1,0:T(8,128)(2,1)} custom-call(s32[1]{0:T(128)} %bitcast.6.own, s32[16,2,128]{2,1,0:T(2,128)} %copy-done.12, s32[16,2,128]{2,1,0:T(2,128)} %copy-done.12, bf16[128,16,1024]{2,1,0:T(8,128)(2,1)} %store_hbm.3, bf16[9,16,1024]{2,1,0:T(8,128)(2,1)} %get-tuple-element.33.rest_0_.rest_4_, bf16[9,16,1024]{2,1,0:T(8,128)(2,1)} %copy-done, ...), custom_call_target="tpu_custom_call" | custom-call | bytes 8388608 | tf_op jit(solution)/shard_map/pallas_call | solution.py:452
  137.8 33.9 %shard_map.72 = (f32[5,4,128,384]{3,2,1,0:T(8,128)}, f32[5,8,384]{2,1,0:T(8,128)}) custom-call(s32[104]{0:T(128)} %select_reduce_fusion.1.place, s32[112]{0:T(128)} %copy-done.19, s32[5]{0:T(128)} %and_select_fusion.tiles, s32[5,1,128]{2,1,0:T(1,128)} %tile.9.rest_0_, s32[1,160]{1,0:T(1,128)} %rest_1_.3, bf16[160,1024]{1,0:T(8,128)(2,1)} %bitcast.71, ...), custom_call_target="tpu_custom_call" | custom-call | flops 8455716864 | bytes 9568256 | tf_op jit(solution)/shard_map/pallas_call | solution.py:307
  172.6 15.6 %shard_map.73 = bf16[160,6144]{1,0:T(8,128)(2,1)} custom-call(s32[24]{0:T(128)} %get-tuple-element.57.place, s32[24]{0:T(128)} %copy-done.18, s32[5]{0:T(128)} %and_select_fusion.1.tiles, s32[5,1,128]{2,1,0:T(1,128)} %tile.9.rest_0_, s32[1,160]{1,0:T(1,128)} %rest_1_.3, bf16[160,1024]{1,0:T(8,128)(2,1)} %bitcast.72, bf16[160,6144]{1,0:T(8,128)(2,1)} %bitcast.68, ...), custom_call_target="tpu_custom_call" | custom-call | flops 1811939328 | bytes 6684672 | tf_op jit(solution)/shard_map/pallas_call | solution.py:307
  (83 shorter events, 15.3 us)
Async XLA Ops:
  2.3 20.2 %all-to-all-start = ((s32[16,2,128]{2,1,0:T(2,128)}), s32[16,2,128]{2,1,0:T(2,128)S(1)}, u32[]{:S(2)}, u32[]{:S(2)}) async-start(s32[16,2,128]{2,1,0:T(2,128)} %shard_map.68), calls=%async_computation | async-start | bytes 32768 | tf_op jit(solution)/shard_map/all_to_all | solution.py:408
  11.2 18.4 %collective-permute-start.10 = (bf16[1,16,1024]{2,1,0:T(8,128)(2,1)}, bf16[1,16,1024]{2,1,0:T(8,128)(2,1)S(1)}, u32[]{:S(2)}, u32[]{:S(2)}) collective-permute-start(bf16[1,16,1024]{2,1,0:T(8,128)(2,1)} %get-tuple-element.44), channel_id=1, source_target_pairs={{0,11},{1,10},{2,9},{3,8},{4,15},{5,14},{6,13},{7,12},{8,3},{9,2},... | collective-permute-start | bytes 98312 | tf_op jit(solution)/shard_map/ppermute | solution.py:399
  14.5 16.9 %collective-permute-start.13 = (bf16[1,16,1024]{2,1,0:T(8,128)(2,1)}, bf16[1,16,1024]{2,1,0:T(8,128)(2,1)S(1)}, u32[]{:S(2)}, u32[]{:S(2)}) collective-permute-start(bf16[1,16,1024]{2,1,0:T(8,128)(2,1)} %get-tuple-element.47), channel_id=1, source_target_pairs={{0,14},{1,15},{2,12},{3,13},{4,10},{5,11},{6,8},{7,9},{8,6},{9,7},... | collective-permute-start | bytes 98312 | tf_op jit(solution)/shard_map/ppermute | solution.py:399
  14.5 19.6 %collective-permute-start.14 = (bf16[1,16,1024]{2,1,0:T(8,128)(2,1)}, bf16[1,16,1024]{2,1,0:T(8,128)(2,1)S(1)}, u32[]{:S(2)}, u32[]{:S(2)}) collective-permute-start(bf16[1,16,1024]{2,1,0:T(8,128)(2,1)} %get-tuple-element.48), channel_id=1, source_target_pairs={{0,15},{1,14},{2,13},{3,12},{4,11},{5,10},{6,9},{7,8},{8,7},{9,6},... | collective-permute-start | bytes 98312 | tf_op jit(solution)/shard_map/ppermute | solution.py:399
  19.7 118.1 %copy-start.19 = (s32[112]{0:T(128)}, s32[112]{0:T(128)S(1)}, u32[]{:S(2)}) copy-start(s32[112]{0:T(128)S(1)} %compare_select_fusion.page_number) | copy-start | bytes 1348
  20.5 117.3 %copy-start.18 = (s32[24]{0:T(128)}, s32[24]{0:T(128)S(1)}, u32[]{:S(2)}) copy-start(s32[24]{0:T(128)S(1)} %compare_select_fusion.14.page_number) | copy-start | bytes 292
  28.4 6.4 %collective-permute-start = (bf16[9,16,1024]{2,1,0:T(8,128)(2,1)}, bf16[9,16,1024]{2,1,0:T(8,128)(2,1)S(1)}, u32[]{:S(2)}, u32[]{:S(2)}) collective-permute-start(bf16[9,16,1024]{2,1,0:T(8,128)(2,1)} %get-tuple-element.34), channel_id=1, source_target_pairs={{0,1},{1,0},{2,3},{3,2},{4,5},{5,4},{6,7},{7,6},{8,9},{9,8},{10,11... | collective-permute-start | bytes 884744 | tf_op jit(solution)/shard_map/ppermute | solution.py:399
  28.5 8.4 %collective-permute-start.1 = (bf16[9,16,1024]{2,1,0:T(8,128)(2,1)}, bf16[9,16,1024]{2,1,0:T(8,128)(2,1)S(1)}, u32[]{:S(2)}, u32[]{:S(2)}) collective-permute-start(bf16[9,16,1024]{2,1,0:T(8,128)(2,1)} %get-tuple-element.35), channel_id=1, source_target_pairs={{0,2},{1,3},{2,0},{3,1},{4,6},{5,7},{6,4},{7,5},{8,10},{9,11},{10,... | collective-permute-start | bytes 884744 | tf_op jit(solution)/shard_map/ppermute | solution.py:399
  29.7 99.2 %copy-start.15 = (bf16[1,16,1024]{2,1,0:T(8,128)(2,1)}, bf16[1,16,1024]{2,1,0:T(8,128)(2,1)S(1)}, u32[]{:S(2)}) copy-start(bf16[1,16,1024]{2,1,0:T(8,128)(2,1)S(1)} %collective-permute-done.10.rest_11_) | copy-start | bytes 98308
  29.7 14.4 %collective-permute-start.2 = (bf16[9,16,1024]{2,1,0:T(8,128)(2,1)}, bf16[9,16,1024]{2,1,0:T(8,128)(2,1)S(1)}, u32[]{:S(2)}, u32[]{:S(2)}) collective-permute-start(bf16[9,16,1024]{2,1,0:T(8,128)(2,1)} %get-tuple-element.36), channel_id=1, source_target_pairs={{0,3},{1,2},{2,1},{3,0},{4,7},{5,6},{6,5},{7,4},{8,11},{9,10},{10,... | collective-permute-start | bytes 884744 | tf_op jit(solution)/shard_map/ppermute | solution.py:399
  32.1 14.1 %collective-permute-start.3 = (bf16[9,16,1024]{2,1,0:T(8,128)(2,1)}, bf16[9,16,1024]{2,1,0:T(8,128)(2,1)S(1)}, u32[]{:S(2)}, u32[]{:S(2)}) collective-permute-start(bf16[9,16,1024]{2,1,0:T(8,128)(2,1)} %get-tuple-element.37), channel_id=1, source_target_pairs={{0,4},{1,5},{2,6},{3,7},{4,0},{5,1},{6,2},{7,3},{8,12},{9,13},{10,... | collective-permute-start | bytes 884744 | tf_op jit(solution)/shard_map/ppermute | solution.py:399
  34.8 13.4 %collective-permute-start.4 = (bf16[9,16,1024]{2,1,0:T(8,128)(2,1)}, bf16[9,16,1024]{2,1,0:T(8,128)(2,1)S(1)}, u32[]{:S(2)}, u32[]{:S(2)}) collective-permute-start(bf16[9,16,1024]{2,1,0:T(8,128)(2,1)} %get-tuple-element.38), channel_id=1, source_target_pairs={{0,5},{1,4},{2,7},{3,6},{4,1},{5,0},{6,3},{7,2},{8,13},{9,12},{10,... | collective-permute-start | bytes 884744 | tf_op jit(solution)/shard_map/ppermute | solution.py:399
  34.8 94.1 %copy-start = (bf16[9,16,1024]{2,1,0:T(8,128)(2,1)}, bf16[9,16,1024]{2,1,0:T(8,128)(2,1)S(1)}, u32[]{:S(2)}) copy-start(bf16[9,16,1024]{2,1,0:T(8,128)(2,1)S(1)} %collective-permute-done.rest_1_.rest_14_) | copy-start | bytes 884740
  34.8 31.1 %collective-permute-start.5 = (bf16[9,16,1024]{2,1,0:T(8,128)(2,1)}, bf16[9,16,1024]{2,1,0:T(8,128)(2,1)S(1)}, u32[]{:S(2)}, u32[]{:S(2)}) collective-permute-start(bf16[9,16,1024]{2,1,0:T(8,128)(2,1)} %get-tuple-element.39), channel_id=1, source_target_pairs={{0,6},{1,7},{2,4},{3,5},{4,2},{5,3},{6,0},{7,1},{8,14},{9,15},{10,... | collective-permute-start | bytes 884744 | tf_op jit(solution)/shard_map/ppermute | solution.py:399
  36.9 92.0 %copy-start.1 = (bf16[9,16,1024]{2,1,0:T(8,128)(2,1)}, bf16[9,16,1024]{2,1,0:T(8,128)(2,1)S(1)}, u32[]{:S(2)}) copy-start(bf16[9,16,1024]{2,1,0:T(8,128)(2,1)S(1)} %collective-permute-done.1.rest_2_.rest_15_) | copy-start | bytes 884740
  36.9 35.2 %collective-permute-start.6 = (bf16[9,16,1024]{2,1,0:T(8,128)(2,1)}, bf16[9,16,1024]{2,1,0:T(8,128)(2,1)S(1)}, u32[]{:S(2)}, u32[]{:S(2)}) collective-permute-start(bf16[9,16,1024]{2,1,0:T(8,128)(2,1)} %get-tuple-element.40), channel_id=1, source_target_pairs={{0,7},{1,6},{2,5},{3,4},{4,3},{5,2},{6,1},{7,0},{8,15},{9,14},{10,... | collective-permute-start | bytes 884744 | tf_op jit(solution)/shard_map/ppermute | solution.py:399
  44.1 31.0 %collective-permute-start.7 = (bf16[9,16,1024]{2,1,0:T(8,128)(2,1)}, bf16[9,16,1024]{2,1,0:T(8,128)(2,1)S(1)}, u32[]{:S(2)}, u32[]{:S(2)}) collective-permute-start(bf16[9,16,1024]{2,1,0:T(8,128)(2,1)} %get-tuple-element.41), channel_id=1, source_target_pairs={{0,8},{1,9},{2,10},{3,11},{4,12},{5,13},{6,14},{7,15},{8,0},{9,1},... | collective-permute-start | bytes 884744 | tf_op jit(solution)/shard_map/ppermute | solution.py:399
  46.2 29.2 %collective-permute-start.8 = (bf16[9,16,1024]{2,1,0:T(8,128)(2,1)}, bf16[9,16,1024]{2,1,0:T(8,128)(2,1)S(1)}, u32[]{:S(2)}, u32[]{:S(2)}) collective-permute-start(bf16[9,16,1024]{2,1,0:T(8,128)(2,1)} %get-tuple-element.42), channel_id=1, source_target_pairs={{0,9},{1,8},{2,11},{3,10},{4,13},{5,12},{6,15},{7,14},{8,1},{9,0},... | collective-permute-start | bytes 884744 | tf_op jit(solution)/shard_map/ppermute | solution.py:399
  48.2 55.0 %collective-permute-start.9 = (bf16[9,16,1024]{2,1,0:T(8,128)(2,1)}, bf16[9,16,1024]{2,1,0:T(8,128)(2,1)S(1)}, u32[]{:S(2)}, u32[]{:S(2)}) collective-permute-start(bf16[9,16,1024]{2,1,0:T(8,128)(2,1)} %get-tuple-element.43), channel_id=1, source_target_pairs={{0,10},{1,11},{2,8},{3,9},{4,14},{5,15},{6,12},{7,13},{8,2},{9,3},... | collective-permute-start | bytes 884744 | tf_op jit(solution)/shard_map/ppermute | solution.py:399
  65.8 56.7 %collective-permute-start.11 = (bf16[9,16,1024]{2,1,0:T(8,128)(2,1)}, bf16[9,16,1024]{2,1,0:T(8,128)(2,1)S(1)}, u32[]{:S(2)}, u32[]{:S(2)}) collective-permute-start(bf16[9,16,1024]{2,1,0:T(8,128)(2,1)} %get-tuple-element.45), channel_id=1, source_target_pairs={{0,12},{1,13},{2,14},{3,15},{4,8},{5,9},{6,10},{7,11},{8,4},{9,5},... | collective-permute-start | bytes 884744 | tf_op jit(solution)/shard_map/ppermute | solution.py:399
  72.1 56.7 %collective-permute-start.12 = (bf16[9,16,1024]{2,1,0:T(8,128)(2,1)}, bf16[9,16,1024]{2,1,0:T(8,128)(2,1)S(1)}, u32[]{:S(2)}, u32[]{:S(2)}) collective-permute-start(bf16[9,16,1024]{2,1,0:T(8,128)(2,1)} %get-tuple-element.46), channel_id=1, source_target_pairs={{0,13},{1,12},{2,15},{3,14},{4,9},{5,8},{6,11},{7,10},{8,5},{9,4},... | collective-permute-start | bytes 884744 | tf_op jit(solution)/shard_map/ppermute | solution.py:399
  75.1 96.7 %collective-permute-start.15 = (bf16[8,16,1024]{2,1,0:T(8,128)(2,1)}, bf16[8,16,1024]{2,1,0:T(8,128)(2,1)S(1)}, u32[]{:S(2)}, u32[]{:S(2)}) collective-permute-start(bf16[8,16,1024]{2,1,0:T(8,128)(2,1)} %get-tuple-element.52), channel_id=1, source_target_pairs={{0,14},{1,15},{2,12},{3,13},{4,10},{5,11},{6,8},{7,9},{8,6},{9,7},... | collective-permute-start | bytes 786440 | tf_op jit(solution)/shard_map/ppermute | solution.py:399
  75.4 96.4 %collective-permute-start.16 = (bf16[8,16,1024]{2,1,0:T(8,128)(2,1)}, bf16[8,16,1024]{2,1,0:T(8,128)(2,1)S(1)}, u32[]{:S(2)}, u32[]{:S(2)}) collective-permute-start(bf16[8,16,1024]{2,1,0:T(8,128)(2,1)} %get-tuple-element.53), channel_id=1, source_target_pairs={{0,11},{1,10},{2,9},{3,8},{4,15},{5,14},{6,13},{7,12},{8,3},{9,2},... | collective-permute-start | bytes 786440 | tf_op jit(solution)/shard_map/ppermute | solution.py:399
  103.2 68.5 %collective-permute-start.17 = (bf16[8,16,1024]{2,1,0:T(8,128)(2,1)}, bf16[8,16,1024]{2,1,0:T(8,128)(2,1)}, u32[]{:S(2)}, u32[]{:S(2)}) collective-permute-start(bf16[8,16,1024]{2,1,0:T(8,128)(2,1)} %get-tuple-element.54), channel_id=1, source_target_pairs={{0,15},{1,14},{2,13},{3,12},{4,11},{5,10},{6,9},{7,8},{8,7},{9,6},... | collective-permute-start | bytes 786440 | tf_op jit(solution)/shard_map/ppermute | solution.py:399
  (15 other events, 511.6 us)

commit v5 on v4

v5 whole, which is shorter than its diff:
```python
import functools

import jax
import jax.numpy as jnp
from jax import lax
from jax.experimental import pallas as pl
from jax.experimental.pallas import tpu as pltpu
from jax.sharding import PartitionSpec as P

HEAD_WIDTH = 128
KEY_VALUE_HEADS = 4
QUERY_GROUP = 12
SELP = 2
LANES = 128
ROW_SLOTS = 16
VMEM_LIMIT = 60 * 1024 * 1024
QUERY_BLOCK = 32
TILE_PAGES = 16
HIDDEN = -1e30
FAR_POSITION = 1 << 24


def nt_dot(a, b):
    return lax.dot_general(a, b, (((1,), (1,)), ((), ())), preferred_element_type=jnp.float32)


def one_hot(condition):
    return jnp.where(condition, 1.0, 0.0)


def pair_places(hold, page_len, table_ref, sel_ref, wide):
    pages = table_ref.shape[1]
    picked = sel_ref.shape[1]
    f32 = jnp.float32
    slots = jnp.broadcast_to(table_ref[...], (pages, pages))
    owners = slots // hold
    local_row = (slots - owners * hold).astype(f32)[0:1]
    owner_row = owners.astype(f32)
    owner_col = owner_row.T
    sub = lax.broadcasted_iota(jnp.int32, (pages, pages), 0)
    lane = lax.broadcasted_iota(jnp.int32, (pages, pages), 1)
    earlier = one_hot((owner_row == owner_col) & (lane < sub))
    rank_col = jnp.sum(earlier, axis=1, keepdims=True)

    wide[...] = jnp.full(wide.shape, -1, jnp.int32)
    wide[0:1, 0:picked] = sel_ref[...]
    position = wide[...]
    page = lax.shift_right_arithmetic(position, page_len.bit_length() - 1)
    offset = (position & (page_len - 1)).astype(f32)[0:1]
    lane_wide = lax.broadcasted_iota(jnp.int32, wide.shape, 1)
    second = one_hot((page == pltpu.roll(page, 1, axis=1)) & (lane_wide > 0))[0:1]
    valid = lane_wide[0:1] < picked
    sub_wide = lax.broadcasted_iota(jnp.int32, (pages, wide.shape[1]), 0)
    in_page = one_hot(sub_wide == page[0:1])
    owner = jnp.sum(in_page * owner_col[:, 0:1], axis=0, keepdims=True)
    rank = jnp.sum(in_page * rank_col, axis=0, keepdims=True)
    return owner_row[0:1], local_row, rank_col, owner, rank, second, offset, valid


def index_kernel(hold, page_len, first, own, table_ref, sel_ref, out_ref, *rest):
    first_refs, wide = rest[:-1], rest[-1]
    holders = out_ref.shape[0]
    pages = table_ref.shape[1]
    f32 = jnp.float32
    bf16 = jnp.bfloat16
    owner_row, local_row, rank_col, owner, rank, second, offset, valid = pair_places(
        hold, page_len, table_ref, sel_ref, wide
    )
    holder = lax.broadcasted_iota(jnp.int32, (holders, pages), 0).astype(f32)
    owned = jnp.where(holder == owner_row, local_row, 0.0)
    lane = lax.broadcasted_iota(jnp.int32, (pages, LANES), 1).astype(f32)
    numbers = jnp.dot(
        owned.astype(bf16), one_hot(lane == rank_col).astype(bf16), preferred_element_type=f32
    )
    holder_wide = lax.broadcasted_iota(jnp.int32, (holders, wide.shape[1]), 0).astype(f32)
    marked = jnp.where((holder_wide == owner) & valid, rank * page_len + offset + 1.0, 0.0)
    place_lane = lax.broadcasted_iota(jnp.int32, (LANES, wide.shape[1]), 0).astype(f32)
    at_place = one_hot(place_lane == SELP * rank + second)
    targets = nt_dot(marked.astype(bf16), at_place.astype(bf16))
    for h in range(holders):
        out_ref[h, 0:1, :] = numbers[h : h + 1, :].astype(jnp.int32)
        out_ref[h, 1:2, :] = targets[h : h + 1, :].astype(jnp.int32)
    for d, ref in zip(first, first_refs):
        ref[0] = out_ref[own[0] ^ d]


def rows_kernel(hold, page_len, table_ref, sel_ref, fresh_ref, packed, wide):
    holders = packed.shape[0]
    picked = sel_ref.shape[1]
    f32 = jnp.float32
    _, _, _, owner, rank, second, _, valid = pair_places(hold, page_len, table_ref, sel_ref, wide)
    spot = jnp.where(valid, owner * ROW_SLOTS + SELP * rank + second, -1.0)[:, 0:picked]
    step = min(holders, 16)
    for start in range(0, holders, step):
        spot_id = lax.broadcasted_iota(jnp.int32, (step * ROW_SLOTS, picked), 0).astype(f32)
        choose = one_hot(spot_id + float(start * ROW_SLOTS) == spot).astype(jnp.bfloat16)
        rows = jnp.dot(choose, fresh_ref[...], preferred_element_type=f32).astype(jnp.bfloat16)
        packed[start : start + step] = rows.reshape(step, ROW_SLOTS, fresh_ref.shape[1])


def first_gather_kernel(count, *refs):
    lists, store_hbm, sends = refs[:count], refs[count], refs[count + 1 : 2 * count + 1]
    held, load_sem, send_sem = refs[2 * count + 1 :]
    capacity = held.shape[1]
    for i, numbers in enumerate(lists):
        for k in range(capacity):
            pltpu.make_async_copy(store_hbm.at[numbers[0, 0, k]], held.at[i, k], load_sem).start()
    pltpu.make_async_copy(held, held, load_sem).wait()
    for i, send in enumerate(sends):
        pltpu.make_async_copy(held.at[i], send, send_sem).start()
    pltpu.make_async_copy(held, held, send_sem).wait()


def gather_kernel(capacity, distances, own, index, store_hbm, *rest):
    sends, (store, load_sem, send_sem) = rest[:-3], rest[-3:]
    load = pltpu.make_async_copy(store_hbm, store, load_sem)
    load.start()
    load.wait()
    for i in range(len(distances) if distances else index.shape[0]):
        r = own[0] ^ distances[i] if distances else i
        send = sends[i] if distances else sends[0].at[i]
        for k in range(capacity):
            pltpu.make_async_copy(store.at[index[r, 0, k]], send.at[k], send_sem).start()
    for send in sends:
        pltpu.make_async_copy(send, send, send_sem).wait()


def write_back_kernel(index, targets_ref, store_hbm, rows_hbm, store_out, *scratch):
    store, rows, blended, load_sem, rows_sem, out_sem = scratch
    holders, capacity, page_len, width = blended.shape
    rows_here = capacity * page_len
    f32 = jnp.float32
    load = pltpu.make_async_copy(store_hbm, store, load_sem)
    load_rows = pltpu.make_async_copy(rows_hbm, rows, rows_sem)
    load.start()
    load_rows.start()
    load_rows.wait()
    load.wait()
    row_id = lax.broadcasted_iota(jnp.int32, (rows_here, ROW_SLOTS), 0)

    def one_request(r, carry):
        hit = one_hot(row_id == targets_ref[r][1:2, 0:ROW_SLOTS] - 1)
        keep = 1.0 - jnp.sum(hit, axis=1, keepdims=True)
        keep = jnp.broadcast_to(keep, (rows_here, LANES)).astype(jnp.bfloat16)
        hit = hit.astype(jnp.bfloat16)
        for c in range(width // LANES):
            lanes = slice(c * LANES, (c + 1) * LANES)
            fresh = jnp.dot(hit, rows[r, :, lanes], preferred_element_type=f32).astype(jnp.bfloat16)
            for k in range(capacity):
                part = slice(k * page_len, (k + 1) * page_len)
                blended[r, k, :, lanes] = store[index[r, 0, k], :, lanes] * keep[part] + fresh[part]
        for k in range(capacity):
            pltpu.make_async_copy(blended.at[r, k], store_out.at[index[r, 0, k]], out_sem).start()
        return carry

    lax.fori_loop(0, holders, one_request, 0)
    pltpu.make_async_copy(store_out, store_out, out_sem).wait()


def attend_kernel(first, last, sources, place, page_number, tiles, *rest):
    sel_ref, positions_ref, query_ref, *rest = rest
    if first:
        fresh_ref, fresh_positions, *rest = rest
    state_in = () if first else rest[:2]
    rest = rest if first else rest[2:]
    contexts, rest = rest[:sources], rest[sources:]
    outs, rest = (rest[:1], rest[1:]) if last else (rest[:2], rest[2:])
    kv, values, position, query, mixed, stats, sem = rest
    pages, page_len, width = kv.shape
    each = contexts[0].shape[0]
    ahead = TILE_PAGES if first else 0
    block = query_ref.shape[0]
    tile = TILE_PAGES * page_len
    lanes = QUERY_GROUP * block
    scale = 1.4426950408889634 / HEAD_WIDTH**0.5
    f32 = jnp.float32
    bf16 = jnp.bfloat16
    step = pl.program_id(0)
    eye = one_hot(
        lax.broadcasted_iota(jnp.int32, (LANES, LANES), 0)
        == lax.broadcasted_iota(jnp.int32, (LANES, LANES), 1)
    ).astype(bf16)

    @pl.when(step == 0)
    def _():
        for i, context in enumerate(contexts):
            for k in range(each):
                pltpu.make_async_copy(context.at[k], kv.at[ahead + place[i * each + k]], sem).start()
        if first:
            picked = fresh_ref.shape[0]
            count = picked // page_len
            kv[0:count] = fresh_ref[...].reshape(count, page_len, width)
            kv[count:ahead] = jnp.zeros((ahead - count, page_len, width), bf16)
            position[0:picked, :] = fresh_positions[...]
            position[picked:tile, :] = jnp.full((tile - picked, LANES), FAR_POSITION, jnp.int32)
        positions = positions_ref[...]
        row = lax.broadcasted_iota(jnp.int32, (page_len, positions.shape[1]), 0)
        ones = jnp.ones((positions.shape[1], LANES), bf16)
        row_lanes = lax.broadcasted_iota(jnp.int32, (page_len, LANES), 0)

        def place_rows(t, carry):
            starts = [page_number[t * TILE_PAGES + k] * page_len for k in range(TILE_PAGES)]
            hit = jnp.concatenate([one_hot(row + start == positions) for start in starts], axis=0)
            hidden = jnp.dot(hit.astype(bf16), ones, preferred_element_type=f32)
            plain = jnp.concatenate([row_lanes + start for start in starts], axis=0)
            here = pl.ds(pl.multiple_of(ahead * page_len + t * tile, tile), tile)
            position[here, :] = jnp.where(hidden > 0.0, FAR_POSITION, plain)
            return carry

        lax.fori_loop(0, (pages - ahead) // TILE_PAGES, place_rows, 0)
        used = kv.at[ahead:]
        pltpu.make_async_copy(used, used, sem).wait()

        def turn(t, carry):
            here = pl.ds(t * TILE_PAGES, TILE_PAGES)
            for g in range(KEY_VALUE_HEADS):
                at = (KEY_VALUE_HEADS + g) * LANES
                value = kv[here, :, at : at + LANES].reshape(tile, LANES)
                values[t, g] = nt_dot(eye, value).astype(bf16)
            return carry

        lax.fori_loop(0, pages // TILE_PAGES, turn, 0)

    for g in range(KEY_VALUE_HEADS):
        for i in range(QUERY_GROUP):
            head = g * QUERY_GROUP + i
            query[g, i * block : (i + 1) * block, :] = query_ref[:, head * LANES : (head + 1) * LANES]
    if first:
        mixed[...] = jnp.zeros(mixed.shape, f32)
        stats[0:KEY_VALUE_HEADS, :] = jnp.full((KEY_VALUE_HEADS, lanes), HIDDEN, f32)
        stats[KEY_VALUE_HEADS:, :] = jnp.zeros((KEY_VALUE_HEADS, lanes), f32)
    else:
        mixed[...] = state_in[0][0]
        stats[...] = state_in[1][0]

    sel = sel_ref[0]

    def one_tile(t, carry):
        here = pl.ds(t * TILE_PAGES, TILE_PAGES)
        bias = jnp.where(
            position[pl.ds(pl.multiple_of(t * tile, tile), tile), :] <= sel, 0.0, HIDDEN
        ).astype(f32)

        def score(g):
            key = kv[here, :, g * LANES : (g + 1) * LANES].reshape(tile, LANES)
            return nt_dot(key, query[g])

        upcoming = score(0)
        for g in range(KEY_VALUE_HEADS):
            scores = upcoming
            if g + 1 < KEY_VALUE_HEADS:
                upcoming = score(g + 1)
            raised, shrinks = [], []
            at = KEY_VALUE_HEADS + g
            for n in range(lanes // LANES):
                part = slice(n * LANES, (n + 1) * LANES)
                s = scores[:, part] + bias
                old = stats[g : g + 1, part]
                new = jnp.maximum(old, jnp.max(s, axis=0, keepdims=True))
                p = jnp.exp2((s - new) * scale)
                shrink = jnp.exp2((old - new) * scale)
                stats[at : at + 1, part] = stats[at : at + 1, part] * shrink + jnp.sum(
                    p, axis=0, keepdims=True
                )
                stats[g : g + 1, part] = new
                raised.append(p.astype(bf16))
                shrinks.append(shrink)
            raised = jnp.concatenate(raised, axis=1)
            shrink = jnp.concatenate(shrinks, axis=1)
            mixed[g] = mixed[g] * shrink + jnp.dot(
                values[t, g], raised, preferred_element_type=f32
            )
        return carry

    lax.fori_loop(0, tiles[step], one_tile, 0)

    if last:
        done = []
        for g in range(KEY_VALUE_HEADS):
            at = KEY_VALUE_HEADS + g
            part = (mixed[g] * (1.0 / stats[at : at + 1, :])).astype(bf16)
            done += [part[:, n * LANES : (n + 1) * LANES] for n in range(lanes // LANES)]
        turned = nt_dot(eye, jnp.concatenate(done, axis=0)).astype(bf16)
        for n in range(len(done)):
            for i in range(LANES // block):
                head = n * (LANES // block) + i
                outs[0][:, head * LANES : (head + 1) * LANES] = turned[
                    i * block : (i + 1) * block, n * LANES : (n + 1) * LANES
                ]
    else:
        outs[0][0] = mixed[...]
        outs[1][0] = stats[...]


def attend(first, last, order, sel_lanes, positions, queries, fresh, state, contexts):
    picked, features = queries.shape
    each, page_len, width = contexts[0].shape
    pages = each * len(contexts) + (TILE_PAGES if first else 0)
    steps = picked // QUERY_BLOCK
    lanes = QUERY_GROUP * QUERY_BLOCK
    wide = pl.BlockSpec((QUERY_BLOCK, features), lambda b, *_: (b, 0))
    state_specs = [
        pl.BlockSpec((1, KEY_VALUE_HEADS, LANES, lanes), lambda b, *_: (b, 0, 0, 0)),
        pl.BlockSpec((1, 2 * KEY_VALUE_HEADS, lanes), lambda b, *_: (b, 0, 0)),
    ]
    state_shapes = [
        jax.ShapeDtypeStruct((steps, KEY_VALUE_HEADS, LANES, lanes), jnp.float32),
        jax.ShapeDtypeStruct((steps, 2 * KEY_VALUE_HEADS, lanes), jnp.float32),
    ]
    share = 0.6
    return pl.pallas_call(
        functools.partial(attend_kernel, first, last, len(contexts)),
        grid_spec=pltpu.PrefetchScalarGridSpec(
            num_scalar_prefetch=3,
            grid=(steps,),
            in_specs=[
                pl.BlockSpec((1, 1, LANES), lambda b, *_: (b, 0, 0)),
                pl.BlockSpec(positions.shape, lambda b, *_: (0, 0)),
                wide,
                *[pl.BlockSpec(x.shape, lambda b, *_: (0, 0)) for x in fresh if first],
                *([] if first else state_specs),
                *[pl.BlockSpec(memory_space=pltpu.HBM)] * len(contexts),
            ],
            out_specs=[wide] if last else state_specs,
            scratch_shapes=[
                pltpu.VMEM((pages, page_len, width), jnp.bfloat16),
                pltpu.VMEM(
                    (pages // TILE_PAGES, KEY_VALUE_HEADS, LANES, TILE_PAGES * page_len), jnp.bfloat16
                ),
                pltpu.VMEM((pages * page_len, LANES), jnp.int32),
                pltpu.VMEM((KEY_VALUE_HEADS, lanes, LANES), jnp.bfloat16),
                pltpu.VMEM((KEY_VALUE_HEADS, LANES, lanes), jnp.float32),
                pltpu.VMEM((2 * KEY_VALUE_HEADS, lanes), jnp.float32),
                pltpu.SemaphoreType.DMA,
            ],
        ),
        out_shape=[jax.ShapeDtypeStruct((picked, features), jnp.bfloat16)] if last else state_shapes,
        compiler_params=pltpu.CompilerParams(
            dimension_semantics=("arbitrary",), vmem_limit_bytes=VMEM_LIMIT
        ),
        cost_estimate=pl.CostEstimate(
            flops=int(share * 8 * picked * features * pages * page_len),
            bytes_accessed=2 * pages * page_len * width + 6 * picked * features,
            transcendentals=int(share * picked * features // LANES * pages * page_len),
        ),
    )(*order, sel_lanes, positions, queries, *[x for x in fresh if first], *state, *contexts)


def page_order(slots, positions, own, hold, capacity, groups, page_len):
    pages = slots.shape[0]
    number = jnp.arange(pages)
    before = number[None, :] < number[:, None]
    owners = slots // hold
    ranks = jnp.sum(((owners[None, :] == owners[:, None]) & before).astype(jnp.int32), axis=1)
    distance = owners ^ own
    last_page = positions.reshape(-1, QUERY_BLOCK)[:, -1] // page_len
    orders = []
    for at, group in enumerate(groups):
        if group is None:
            arrival = owners * capacity + ranks
            count = pages
        else:
            arrival = jnp.full((pages,), -1, jnp.int32)
            for i, d in enumerate(group):
                arrival = jnp.where(distance == d, i * capacity + ranks, arrival)
            count = len(group) * capacity
        member = arrival >= 0
        place = jnp.sum((member[None, :] & before).astype(jnp.int32), axis=1)
        index = jnp.arange(count)[:, None]
        places = jnp.sum(jnp.where(arrival[None, :] == index, place[None, :], 0), axis=1)
        page = jnp.sum(
            jnp.where(member[None, :] & (place[None, :] == index), number[None, :], 0), axis=1
        )
        seen = jnp.sum((page[None, :] <= last_page[:, None]).astype(jnp.int32), axis=1)
        orders.append((places, page, (seen + TILE_PAGES - 1) // TILE_PAGES + (at == 0)))
    return orders


def per_device(store, page_table, sel_pos, fresh_kv, queries):
    holders = lax.axis_size("store")
    hold, page_len, width = store.shape
    pages = page_table.shape[1]
    picked = sel_pos.shape[1]
    capacity = max(1, pages // holders)
    hbm = pl.BlockSpec(memory_space=pltpu.HBM)
    vmem = pl.BlockSpec(memory_space=pltpu.VMEM)
    dma = pltpu.SemaphoreType.DMA
    params = pltpu.CompilerParams(vmem_limit_bytes=VMEM_LIMIT)
    own = lax.axis_index("store")
    own_word = own.reshape(1).astype(jnp.int32)
    fresh = fresh_kv[0]
    wide = pltpu.VMEM((8, -(-picked // LANES) * LANES), jnp.int32)
    if holders == 16:
        first = (8, 12)
        groups = [(0, 8, 12, 4, 5, 1), (9, 6, 13, 7, 10, 2, 14, 3), (11, 15)]
        others = [d for group in groups for d in group if d not in first]
    else:
        first = ()
        groups = [None]
        others = None

    def swap(x, d):
        return lax.ppermute(x, "store", [(h, h ^ d) for h in range(holders)])

    def exchange(x):
        return lax.all_to_all(x, "store", split_axis=0, concat_axis=0, tiled=True)

    index, *lists = pl.pallas_call(
        functools.partial(index_kernel, hold, page_len, first),
        grid_spec=pltpu.PrefetchScalarGridSpec(
            num_scalar_prefetch=1,
            grid=(1,),
            in_specs=[vmem, vmem],
            out_specs=[vmem] * (1 + len(first)),
            scratch_shapes=[wide],
        ),
        out_shape=[
            jax.ShapeDtypeStruct((holders, 2, LANES), jnp.int32),
            *[jax.ShapeDtypeStruct((1, 2, LANES), jnp.int32)] * len(first),
        ],
        compiler_params=params,
    )(own_word, page_table, sel_pos)
    arrived = {}
    if first:
        lists = [swap(x, d) for x, d in zip(lists, first)]
        parts = pl.pallas_call(
            functools.partial(first_gather_kernel, len(first)),
            grid_spec=pltpu.PrefetchScalarGridSpec(
                num_scalar_prefetch=len(first),
                grid=(1,),
                in_specs=[hbm],
                out_specs=[hbm] * len(first),
                scratch_shapes=[
                    pltpu.VMEM((len(first), capacity, page_len, width), store.dtype),
                    dma,
                    dma,
                ],
            ),
            out_shape=[jax.ShapeDtypeStruct((capacity, page_len, width), store.dtype)] * len(first),
            compiler_params=params,
        )(*lists, store)
        parts, index, table, positions = lax.optimization_barrier(
            (parts, index, page_table, sel_pos)
        )
        arrived = {d: swap(part, d) for d, part in zip(first, parts)}
    else:
        table, positions = page_table, sel_pos
    index_in = exchange(index)

    packed = pl.pallas_call(
        functools.partial(rows_kernel, hold, page_len),
        out_shape=jax.ShapeDtypeStruct((holders, ROW_SLOTS, width), store.dtype),
        scratch_shapes=[wide],
        compiler_params=params,
    )(table, positions, fresh)

    each = jax.ShapeDtypeStruct((capacity, page_len, width), store.dtype)
    whole = jax.ShapeDtypeStruct((holders, capacity, page_len, width), store.dtype)
    parts = pl.pallas_call(
        functools.partial(gather_kernel, capacity, others),
        grid_spec=pltpu.PrefetchScalarGridSpec(
            num_scalar_prefetch=2,
            grid=(1,),
            in_specs=[hbm],
            out_specs=[hbm] * (len(others) if others else 1),
            scratch_shapes=[pltpu.VMEM(store.shape, store.dtype), dma, dma],
        ),
        out_shape=[each] * len(others) if others else [whole],
        compiler_params=params,
    )(own_word, index_in, store)
    parts, packed, table, positions = lax.optimization_barrier((parts, packed, table, positions))
    if others:
        for d, part in zip(others, parts):
            arrived[d] = swap(part, d) if d else part
        contexts = [[arrived[d] for d in group] for group in groups]
    else:
        contexts = [[exchange(parts[0]).reshape(pages, page_len, width)]]
    rows_in = exchange(packed)

    store_out = pl.pallas_call(
        write_back_kernel,
        grid_spec=pltpu.PrefetchScalarGridSpec(
            num_scalar_prefetch=1,
            grid=(1,),
            in_specs=[vmem, hbm, hbm],
            out_specs=hbm,
            scratch_shapes=[
                pltpu.VMEM(store.shape, store.dtype),
                pltpu.VMEM((holders, ROW_SLOTS, width), store.dtype),
                pltpu.VMEM((holders, capacity, page_len, width), store.dtype),
                dma,
                dma,
                dma,
            ],
        ),
        out_shape=jax.ShapeDtypeStruct(store.shape, store.dtype),
        compiler_params=params,
        cost_estimate=pl.CostEstimate(flops=0, bytes_accessed=4 * store.size, transcendentals=0),
    )(index_in, index_in, store, rows_in)

    orders = page_order(table[0], positions[0], own, hold, capacity, groups, page_len)
    sel_lanes = jnp.tile(positions.reshape(-1, 1, QUERY_BLOCK), (1, 1, LANES // QUERY_BLOCK))
    sel_rows = jnp.broadcast_to(positions.reshape(picked, 1), (picked, LANES))
    store_out, sel_lanes = lax.optimization_barrier((store_out, sel_lanes))
    state = ()
    for at, (arrays, order) in enumerate(zip(contexts, orders)):
        state = attend(
            at == 0,
            at == len(groups) - 1,
            order,
            sel_lanes,
            positions,
            queries[0],
            (fresh, sel_rows),
            state,
            arrays,
        )
    return (state[0][None], store_out)


def solution(mesh):
    return jax.shard_map(
        per_device,
        mesh=mesh,
        in_specs=(
            P(("groups", "store"), None, None),
            P(("groups", "store"), None),
            P(("groups", "store"), None),
            P(("groups", "store"), None, None),
            P(("groups", "store"), None, None),
        ),
        out_specs=(P(("groups", "store"), None, None), P(("groups", "store"), None, None)),
        check_vma=False,
    )
```

time: 188 us -> 139 us (0.74)
  waiting for transfers between devices: 66.4 us -> 19.5 us
  starting transfers between devices: 42.6 us -> 37.7 us
  Pallas kernels: 67 us -> 69.3 us
    ppermute x18 -> x17, waiting for transfers between devices: 66.4 us -> 18.9 us  [swap(): return lax.ppermute(x, 'store', [(h, h ^ d) for h in range(holders)])]
    ppermute x18 -> x17, starting transfers between devices: 36 us -> 23.8 us  [swap(): return lax.ppermute(x, 'store', [(h, h ^ d) for h in range(holders)])]
    all_to_all x1 -> x2, starting transfers between devices: 6.58 us -> 13.8 us  [exchange(): return lax.all_to_all(x, 'store', split_axis=0, concat_axis=0, tiled=True)]
    pallas_call x5 -> x7, Pallas kernels: 58.8 us -> 61.3 us  [the longest x3 49.9 us: attend(): pl.pallas_call(functools.partial(attend_kernel, first, last, len(contexts...]
  transfers between devices with their start and end apart: 19 -> 19, of which waited for: 8 -> 8; matrix products, arithmetic and copies ran while one was open for 4% -> 5% of each run, Pallas kernels for 26% -> 40%
where the time goes in v5:
time: 139 us; the launch traced here: 138 us
  Pallas kernels  69.3 us (50%)
  starting transfers between devices  37.7 us (27%)
  waiting for transfers between devices  19.5 us (14%)
  other arithmetic  5.27 us (4%)
  local copies, waits for them, and re-layouts  4.97 us (4%)
    pallas_call x3, Pallas kernels, attend(): pl.pallas_call(functools.partial(attend_kernel, first, last, len(contexts...  49.9 us
    ppermute x17, starting transfers between devices, swap(): return lax.ppermute(x, 'store', [(h, h ^ d) for h in range(holders)])  23.8 us
    ppermute x17, waiting for transfers between devices, swap(): return lax.ppermute(x, 'store', [(h, h ^ d) for h in range(holders)])  18.9 us
    all_to_all x2, starting transfers between devices, exchange(): return lax.all_to_all(x, 'store', split_axis=0, concat_axis=0, tiled=True)  13.8 us
    pallas_call x1, Pallas kernels, per_device(): pl.pallas_call(write_back_kernel, grid_spec=pltpu.PrefetchScalarGridSpec(...  8.02 us
    pallas_call x1, Pallas kernels, per_device(): pl.pallas_call(functools.partial(gather_kernel, capacity, others), grid_s...  4.89 us
    unnamed x49, local copies, waits for them, and re-layouts  2.83 us
  transfers between devices with their start and end apart: 19, of which 8 were waited for; matrix products, arithmetic and copies ran while one was open for 5% of the time, Pallas kernels for 40%

profile of v5, /device:TPU:9, one launch (start us, length us, event | category | flops | bytes accessed | tf_op | source)
XLA Modules:
  0.0 137.6 jit_solution(15802960025368052357)
XLA Ops:
  0.6 1.7 %shard_map.68 = (s32[16,2,128]{2,1,0:T(2,128)}, s32[1,2,128]{2,1,0:T(2,128)}, s32[1,2,128]{2,1,0:T(2,128)}) custom-call(s32[1]{0:T(128)} %bitcast.own, s32[1,128]{1,0:T(1,128)} %table_ref.2, s32[1,160]{1,0:T(1,128)} %rest_1_.2), custom_call_target="tpu_custom_call" | custom-call | tf_op jit(solution)/shard_map/pallas_call | solution.py:408
  2.3 2.3 %collective-permute-start = (s32[1,2,128]{2,1,0:T(2,128)}, s32[1,2,128]{2,1,0:T(2,128)S(1)}, u32[]{:S(2)}, u32[]{:S(2)}) collective-permute-start(s32[1,2,128]{2,1,0:T(2,128)} %get-tuple-element.49), channel_id=1, source_target_pairs={{0,8},{1,9},{2,10},{3,11},{4,12},{5,13},{6,14},{7,15},{8,0},{9,1},... | collective-permute-start | bytes 3080 | tf_op jit(solution)/shard_map/ppermute | solution.py:403
  4.6 1.2 collective-permute-done.refs_0_
  5.8 1.4 %collective-permute-done.1.refs_1_ = s32[1,2,128]{2,1,0:T(2,128)S(1)} collective-permute-done((s32[1,2,128]{2,1,0:T(2,128)}, s32[1,2,128]{2,1,0:T(2,128)S(1)}, u32[]{:S(2)}, u32[]{:S(2)}) %collective-permute-start.1) | collective-permute-done | bytes 1056 | tf_op jit(solution)/shard_map/ppermute | solution.py:403
  7.8 2.5 %shard_map.69 = (bf16[8,16,1024]{2,1,0:T(8,128)(2,1)}, bf16[8,16,1024]{2,1,0:T(8,128)(2,1)}) custom-call(s32[1,2,128]{2,1,0:T(2,128)} %copy-done.7, s32[1,2,128]{2,1,0:T(2,128)} %copy-done.8, bf16[128,16,1024]{2,1,0:T(8,128)(2,1)} %store_hbm.3), custom_call_target="tpu_custom_call" | custom-call | tf_op jit(solution)/shard_map/pallas_call | solution.py:426
  10.3 7.6 %all-to-all-start = ((s32[16,2,128]{2,1,0:T(2,128)}), s32[16,2,128]{2,1,0:T(2,128)S(1)}, u32[]{:S(2)}, u32[]{:S(2)}) async-start(s32[16,2,128]{2,1,0:T(2,128)} %get-tuple-element.54), calls=%async_computation | async-start | bytes 32768 | tf_op jit(solution)/shard_map/all_to_all | solution.py:406
  17.9 2.1 %collective-permute-start.2 = (bf16[8,16,1024]{2,1,0:T(8,128)(2,1)}, bf16[8,16,1024]{2,1,0:T(8,128)(2,1)S(1)}, u32[]{:S(2)}, u32[]{:S(2)}) collective-permute-start(bf16[8,16,1024]{2,1,0:T(8,128)(2,1)} %get-tuple-element.76), channel_id=1, source_target_pairs={{0,8},{1,9},{2,10},{3,11},{4,12},{5,13},{6,14},{7,15},{8,0},{9,1},... | collective-permute-start | bytes 786440 | tf_op jit(solution)/shard_map/ppermute | solution.py:403
  20.0 2.4 %shard_map.71 = bf16[16,16,1024]{2,1,0:T(8,128)(2,1)} custom-call(s32[1,128]{1,0:T(1,128)} %table_ref.2, s32[1,160]{1,0:T(1,128)} %rest_1_.2, bf16[160,1024]{1,0:T(8,128)(2,1)} %bitcast.70), custom_call_target="tpu_custom_call" | custom-call | tf_op jit(solution)/shard_map/pallas_call | solution.py:450
  23.5 4.9 %shard_map.70 = (bf16[8,16,1024]{2,1,0:T(8,128)(2,1)}, bf16[8,16,1024]{2,1,0:T(8,128)(2,1)}, bf16[8,16,1024]{2,1,0:T(8,128)(2,1)}, bf16[8,16,1024]{2,1,0:T(8,128...) custom-call(s32[1]{0:T(128)} %bitcast.own, ...), custom_call_target="tpu_custom_call" | custom-call | tf_op jit(solution)/shard_map/pallas_call | solution.py:459
  30.3 6.3 %all-to-all-start.1 = ((bf16[16,16,1024]{2,1,0:T(8,128)(2,1)}), bf16[16,16,1024]{2,1,0:T(8,128)(2,1)S(1)}, u32[]{:S(2)}, u32[]{:S(2)}) async-start(bf16[16,16,1024]{2,1,0:T(8,128)(2,1)} %shard_map.71), calls=%async_computation.1 | async-start | bytes 1048576 | tf_op jit(solution)/shard_map/all_to_all | solution.py:406
  36.7 1.9 %collective-permute-start.5 = (bf16[8,16,1024]{2,1,0:T(8,128)(2,1)}, bf16[8,16,1024]{2,1,0:T(8,128)(2,1)S(1)}, u32[]{:S(2)}, u32[]{:S(2)}) collective-permute-start(bf16[8,16,1024]{2,1,0:T(8,128)(2,1)} %get-tuple-element.79), channel_id=1, source_target_pairs={{0,5},{1,4},{2,7},{3,6},{4,1},{5,0},{6,3},{7,2},{8,13},{9,12},{10,... | collective-permute-start | bytes 786440 | tf_op jit(solution)/shard_map/ppermute | solution.py:403
  42.1 2.5 %collective-permute-start.7 = (bf16[8,16,1024]{2,1,0:T(8,128)(2,1)}, bf16[8,16,1024]{2,1,0:T(8,128)(2,1)S(1)}, u32[]{:S(2)}, u32[]{:S(2)}) collective-permute-start(bf16[8,16,1024]{2,1,0:T(8,128)(2,1)} %get-tuple-element.83), channel_id=1, source_target_pairs={{0,9},{1,8},{2,11},{3,10},{4,13},{5,12},{6,15},{7,14},{8,1},{9,0},... | collective-permute-start | bytes 786440 | tf_op jit(solution)/shard_map/ppermute | solution.py:403
  44.6 4.2 %collective-permute-done.3.rest_7_ = bf16[8,16,1024]{2,1,0:T(8,128)(2,1)S(1)} collective-permute-done((bf16[8,16,1024]{2,1,0:T(8,128)(2,1)}, bf16[8,16,1024]{2,1,0:T(8,128)(2,1)S(1)}, u32[]{:S(2)}, u32[]{:S(2)}) %collective-permute-start.3) | collective-permute-done | bytes 262176 | tf_op jit(solution)/shard_map/ppermute | solution.py:403
  48.8 3.3 %collective-permute-done.4.rest_8_ = bf16[8,16,1024]{2,1,0:T(8,128)(2,1)S(1)} collective-permute-done((bf16[8,16,1024]{2,1,0:T(8,128)(2,1)}, bf16[8,16,1024]{2,1,0:T(8,128)(2,1)S(1)}, u32[]{:S(2)}, u32[]{:S(2)}) %collective-permute-start.4) | collective-permute-done | bytes 262176 | tf_op jit(solution)/shard_map/ppermute | solution.py:403
  52.1 3.2 %collective-permute-start.9 = (bf16[8,16,1024]{2,1,0:T(8,128)(2,1)}, bf16[8,16,1024]{2,1,0:T(8,128)(2,1)}, u32[]{:S(2)}, u32[]{:S(2)}) collective-permute-start(bf16[8,16,1024]{2,1,0:T(8,128)(2,1)} %get-tuple-element.85), channel_id=1, source_target_pairs={{0,13},{1,12},{2,15},{3,14},{4,9},{5,8},{6,11},{7,10},{8,5},{9,4},... | collective-permute-start | bytes 786440 | tf_op jit(solution)/shard_map/ppermute | solution.py:403
  57.6 8.0 %shard_map.72 = bf16[128,16,1024]{2,1,0:T(8,128)(2,1)} custom-call(s32[16,2,128]{2,1,0:T(2,128)} %copy-done.1, s32[16,2,128]{2,1,0:T(2,128)} %copy-done.1, bf16[128,16,1024]{2,1,0:T(8,128)(2,1)} %store_hbm.3, bf16[16,16,1024]{2,1,0:T(8,128)(2,1)} %copy-done), custom_call_target="tpu_custom_call" | custom-call | bytes 8388608 | tf_op jit(solution)/shard_map/pallas_call | solution.py:480
  66.0 3.0 %collective-permute-start.11 = (bf16[8,16,1024]{2,1,0:T(8,128)(2,1)S(1)}, bf16[8,16,1024]{2,1,0:T(8,128)(2,1)}, u32[]{:S(2)}, u32[]{:S(2)}) collective-permute-start(bf16[8,16,1024]{2,1,0:T(8,128)(2,1)S(1)} %copy-done.17), channel_id=1, source_target_pairs={{0,10},{1,11},{2,8},{3,9},{4,14},{5,15},{6,12},{7,13},{8,2},{9,3},... | collective-permute-start | bytes 786440 | tf_op jit(solution)/shard_map/ppermute | solution.py:403
  69.9 2.1 %collective-permute-start.13 = (bf16[8,16,1024]{2,1,0:T(8,128)(2,1)S(1)}, bf16[8,16,1024]{2,1,0:T(8,128)(2,1)}, u32[]{:S(2)}, u32[]{:S(2)}) collective-permute-start(bf16[8,16,1024]{2,1,0:T(8,128)(2,1)S(1)} %copy-done.14), channel_id=1, source_target_pairs={{0,14},{1,15},{2,12},{3,13},{4,10},{5,11},{6,8},{7,9},{8,6},{9,7},... | collective-permute-start | bytes 786440 | tf_op jit(solution)/shard_map/ppermute | solution.py:403
  72.0 5.6 %collective-permute-done.9.rest_7_ = bf16[8,16,1024]{2,1,0:T(8,128)(2,1)} collective-permute-done((bf16[8,16,1024]{2,1,0:T(8,128)(2,1)}, bf16[8,16,1024]{2,1,0:T(8,128)(2,1)}, u32[]{:S(2)}, u32[]{:S(2)}) %collective-permute-start.9) | collective-permute-done | bytes 262176 | tf_op jit(solution)/shard_map/ppermute | solution.py:403
  79.4 20.4 %shard_map.73 = (f32[5,4,128,384]{3,2,1,0:T(8,128)}, f32[5,8,384]{2,1,0:T(8,128)}) custom-call(s32[48]{0:T(128)} %get-tuple-element.97.place, s32[48]{0:T(128)} %copy-done.10, s32[5]{0:T(128)} %fusion.7.tiles, s32[5,1,128]{2,1,0:T(1,128)} %tile.9.rest_0_, s32[1,160]{1,0:T(1,128)} %rest_1_.2, bf16[160,6144]{1,0:T(8,128)(2,1)} %bitcast.66, ...), custom_call_target="tpu_custom_call" | custom-call | flops 4831838208 | bytes 7995392 | tf_op jit(solution)/shard_map/pallas_call | solution.py:311
  100.2 4.7 %collective-permute-start.16 = (bf16[8,16,1024]{2,1,0:T(8,128)(2,1)S(1)}, bf16[8,16,1024]{2,1,0:T(8,128)(2,1)S(1)}, u32[]{:S(2)}, u32[]{:S(2)}) collective-permute-start(bf16[8,16,1024]{2,1,0:T(8,128)(2,1)S(1)} %copy-done.11), channel_id=1, source_target_pairs={{0,15},{1,14},{2,13},{3,12},{4,11},{5,10},{6,9},{7,8},{8,7},{9,6},... | collective-permute-start | bytes 786440 | tf_op jit(solution)/shard_map/ppermute | solution.py:403
  105.0 18.8 %shard_map.74 = (f32[5,4,128,384]{3,2,1,0:T(8,128)}, f32[5,8,384]{2,1,0:T(8,128)}) custom-call(s32[64]{0:T(128)} %get-tuple-element.99.place, s32[64]{0:T(128)} %copy-done.9, s32[5]{0:T(128)} %and_select_fusion.1.tiles, s32[5,1,128]{2,1,0:T(1,128)} %tile.9.rest_0_, s32[1,160]{1,0:T(1,128)} %rest_1_.2, bf16[160,6144]{1,0:T(8,128)(2,1)} %bitcast.67, ...), custom_call_target="tpu_custom_call" | custom-call | flops 4831838208 | bytes 7995392 | tf_op jit(solution)/shard_map/pallas_call | solution.py:311
  123.8 2.4 %collective-permute-done.16.rest_6_ = bf16[8,16,1024]{2,1,0:T(8,128)(2,1)S(1)} collective-permute-done((bf16[8,16,1024]{2,1,0:T(8,128)(2,1)S(1)}, bf16[8,16,1024]{2,1,0:T(8,128)(2,1)S(1)}, u32[]{:S(2)}, u32[]{:S(2)}) %collective-permute-start.16) | collective-permute-done | bytes 262176 | tf_op jit(solution)/shard_map/ppermute | solution.py:403
  126.9 10.7 %shard_map.75 = bf16[160,6144]{1,0:T(8,128)(2,1)} custom-call(s32[16]{0:T(128)} %get-tuple-element.101.place, s32[16]{0:T(128)} %copy-done.6, s32[5]{0:T(128)} %and_select_fusion.2.tiles, s32[5,1,128]{2,1,0:T(1,128)} %tile.9.rest_0_, s32[1,160]{1,0:T(1,128)} %rest_1_.2, bf16[160,6144]{1,0:T(8,128)(2,1)} %bitcast.68, ...), custom_call_target="tpu_custom_call" | custom-call | flops 1207959552 | bytes 6422528 | tf_op jit(solution)/shard_map/pallas_call | solution.py:311
  (94 shorter events, 13.4 us)
Async XLA Ops:
  2.3 3.5 %collective-permute-start = (s32[1,2,128]{2,1,0:T(2,128)}, s32[1,2,128]{2,1,0:T(2,128)S(1)}, u32[]{:S(2)}, u32[]{:S(2)}) collective-permute-start(s32[1,2,128]{2,1,0:T(2,128)} %get-tuple-element.49), channel_id=1, source_target_pairs={{0,8},{1,9},{2,10},{3,11},{4,12},{5,13},{6,14},{7,15},{8,0},{9,1},... | collective-permute-start | bytes 3080 | tf_op jit(solution)/shard_map/ppermute | solution.py:403
  4.6 2.6 %collective-permute-start.1 = (s32[1,2,128]{2,1,0:T(2,128)}, s32[1,2,128]{2,1,0:T(2,128)S(1)}, u32[]{:S(2)}, u32[]{:S(2)}) collective-permute-start(s32[1,2,128]{2,1,0:T(2,128)} %get-tuple-element.50), channel_id=1, source_target_pairs={{0,12},{1,13},{2,14},{3,15},{4,8},{5,9},{6,10},{7,11},{8,4},{9,5},... | collective-permute-start | bytes 3080 | tf_op jit(solution)/shard_map/ppermute | solution.py:403
  10.3 12.6 %all-to-all-start = ((s32[16,2,128]{2,1,0:T(2,128)}), s32[16,2,128]{2,1,0:T(2,128)S(1)}, u32[]{:S(2)}, u32[]{:S(2)}) async-start(s32[16,2,128]{2,1,0:T(2,128)} %get-tuple-element.54), calls=%async_computation | async-start | bytes 32768 | tf_op jit(solution)/shard_map/all_to_all | solution.py:406
  17.9 24.2 %collective-permute-start.2 = (bf16[8,16,1024]{2,1,0:T(8,128)(2,1)}, bf16[8,16,1024]{2,1,0:T(8,128)(2,1)S(1)}, u32[]{:S(2)}, u32[]{:S(2)}) collective-permute-start(bf16[8,16,1024]{2,1,0:T(8,128)(2,1)} %get-tuple-element.76), channel_id=1, source_target_pairs={{0,8},{1,9},{2,10},{3,11},{4,12},{5,13},{6,14},{7,15},{8,0},{9,1},... | collective-permute-start | bytes 786440 | tf_op jit(solution)/shard_map/ppermute | solution.py:403
  20.0 28.8 %collective-permute-start.3 = (bf16[8,16,1024]{2,1,0:T(8,128)(2,1)}, bf16[8,16,1024]{2,1,0:T(8,128)(2,1)S(1)}, u32[]{:S(2)}, u32[]{:S(2)}) collective-permute-start(bf16[8,16,1024]{2,1,0:T(8,128)(2,1)} %get-tuple-element.77), channel_id=1, source_target_pairs={{0,12},{1,13},{2,14},{3,15},{4,8},{5,9},{6,10},{7,11},{8,4},{9,5},... | collective-permute-start | bytes 786440 | tf_op jit(solution)/shard_map/ppermute | solution.py:403
  30.3 26.5 %all-to-all-start.1 = ((bf16[16,16,1024]{2,1,0:T(8,128)(2,1)}), bf16[16,16,1024]{2,1,0:T(8,128)(2,1)S(1)}, u32[]{:S(2)}, u32[]{:S(2)}) async-start(bf16[16,16,1024]{2,1,0:T(8,128)(2,1)} %shard_map.71), calls=%async_computation.1 | async-start | bytes 1048576 | tf_op jit(solution)/shard_map/all_to_all | solution.py:406
  36.6 15.5 %collective-permute-start.4 = (bf16[8,16,1024]{2,1,0:T(8,128)(2,1)}, bf16[8,16,1024]{2,1,0:T(8,128)(2,1)S(1)}, u32[]{:S(2)}, u32[]{:S(2)}) collective-permute-start(bf16[8,16,1024]{2,1,0:T(8,128)(2,1)} %get-tuple-element.78), channel_id=1, source_target_pairs={{0,4},{1,5},{2,6},{3,7},{4,0},{5,1},{6,2},{7,3},{8,12},{9,13},{10,... | collective-permute-start | bytes 786440 | tf_op jit(solution)/shard_map/ppermute | solution.py:403
  36.7 29.0 %collective-permute-start.5 = (bf16[8,16,1024]{2,1,0:T(8,128)(2,1)}, bf16[8,16,1024]{2,1,0:T(8,128)(2,1)S(1)}, u32[]{:S(2)}, u32[]{:S(2)}) collective-permute-start(bf16[8,16,1024]{2,1,0:T(8,128)(2,1)} %get-tuple-element.79), channel_id=1, source_target_pairs={{0,5},{1,4},{2,7},{3,6},{4,1},{5,0},{6,3},{7,2},{8,13},{9,12},{10,... | collective-permute-start | bytes 786440 | tf_op jit(solution)/shard_map/ppermute | solution.py:403
  38.6 27.4 %collective-permute-start.6 = (bf16[8,16,1024]{2,1,0:T(8,128)(2,1)}, bf16[8,16,1024]{2,1,0:T(8,128)(2,1)S(1)}, u32[]{:S(2)}, u32[]{:S(2)}) collective-permute-start(bf16[8,16,1024]{2,1,0:T(8,128)(2,1)} %get-tuple-element.80), channel_id=1, source_target_pairs={{0,1},{1,0},{2,3},{3,2},{4,5},{5,4},{6,7},{7,6},{8,9},{9,8},{10,11... | collective-permute-start | bytes 786440 | tf_op jit(solution)/shard_map/ppermute | solution.py:403
  39.4 26.3 %copy-start.10 = (s32[48]{0:T(128)}, s32[48]{0:T(128)S(1)}, u32[]{:S(2)}) copy-start(s32[48]{0:T(128)S(1)} %get-tuple-element.96.page_number) | copy-start | bytes 580
  42.1 37.3 %copy-start.16 = (bf16[8,16,1024]{2,1,0:T(8,128)(2,1)}, bf16[8,16,1024]{2,1,0:T(8,128)(2,1)S(1)}, u32[]{:S(2)}) copy-start(bf16[8,16,1024]{2,1,0:T(8,128)(2,1)S(1)} %collective-permute-done.2.rest_6_) | copy-start | bytes 786436
  42.1 26.9 %collective-permute-start.7 = (bf16[8,16,1024]{2,1,0:T(8,128)(2,1)}, bf16[8,16,1024]{2,1,0:T(8,128)(2,1)S(1)}, u32[]{:S(2)}, u32[]{:S(2)}) collective-permute-start(bf16[8,16,1024]{2,1,0:T(8,128)(2,1)} %get-tuple-element.83), channel_id=1, source_target_pairs={{0,9},{1,8},{2,11},{3,10},{4,13},{5,12},{6,15},{7,14},{8,1},{9,0},... | collective-permute-start | bytes 786440 | tf_op jit(solution)/shard_map/ppermute | solution.py:403
  48.8 30.6 %copy-start.18 = (bf16[8,16,1024]{2,1,0:T(8,128)(2,1)}, bf16[8,16,1024]{2,1,0:T(8,128)(2,1)S(1)}, u32[]{:S(2)}) copy-start(bf16[8,16,1024]{2,1,0:T(8,128)(2,1)S(1)} %collective-permute-done.3.rest_7_) | copy-start | bytes 786436
  48.8 21.1 %collective-permute-start.8 = (bf16[8,16,1024]{2,1,0:T(8,128)(2,1)}, bf16[8,16,1024]{2,1,0:T(8,128)(2,1)}, u32[]{:S(2)}, u32[]{:S(2)}) collective-permute-start(bf16[8,16,1024]{2,1,0:T(8,128)(2,1)} %get-tuple-element.84), channel_id=1, source_target_pairs={{0,6},{1,7},{2,4},{3,5},{4,2},{5,3},{6,0},{7,1},{8,14},{9,15},{10,... | collective-permute-start | bytes 786440 | tf_op jit(solution)/shard_map/ppermute | solution.py:403
  52.1 27.3 %copy-start.20 = (bf16[8,16,1024]{2,1,0:T(8,128)(2,1)}, bf16[8,16,1024]{2,1,0:T(8,128)(2,1)S(1)}, u32[]{:S(2)}) copy-start(bf16[8,16,1024]{2,1,0:T(8,128)(2,1)S(1)} %collective-permute-done.4.rest_8_) | copy-start | bytes 786436
  52.1 25.5 %collective-permute-start.9 = (bf16[8,16,1024]{2,1,0:T(8,128)(2,1)}, bf16[8,16,1024]{2,1,0:T(8,128)(2,1)}, u32[]{:S(2)}, u32[]{:S(2)}) collective-permute-start(bf16[8,16,1024]{2,1,0:T(8,128)(2,1)} %get-tuple-element.85), channel_id=1, source_target_pairs={{0,13},{1,12},{2,15},{3,14},{4,9},{5,8},{6,11},{7,10},{8,5},{9,4},... | collective-permute-start | bytes 786440 | tf_op jit(solution)/shard_map/ppermute | solution.py:403
  65.7 34.1 %collective-permute-start.10 = (bf16[8,16,1024]{2,1,0:T(8,128)(2,1)S(1)}, bf16[8,16,1024]{2,1,0:T(8,128)(2,1)}, u32[]{:S(2)}, u32[]{:S(2)}) collective-permute-start(bf16[8,16,1024]{2,1,0:T(8,128)(2,1)S(1)} %copy-done.19), channel_id=1, source_target_pairs={{0,7},{1,6},{2,5},{3,4},{4,3},{5,2},{6,1},{7,0},{8,15},{9,14},{10,... | collective-permute-start | bytes 786440 | tf_op jit(solution)/shard_map/ppermute | solution.py:403
  66.0 34.2 %collective-permute-start.11 = (bf16[8,16,1024]{2,1,0:T(8,128)(2,1)S(1)}, bf16[8,16,1024]{2,1,0:T(8,128)(2,1)}, u32[]{:S(2)}, u32[]{:S(2)}) collective-permute-start(bf16[8,16,1024]{2,1,0:T(8,128)(2,1)S(1)} %copy-done.17), channel_id=1, source_target_pairs={{0,10},{1,11},{2,8},{3,9},{4,14},{5,15},{6,12},{7,13},{8,2},{9,3},... | collective-permute-start | bytes 786440 | tf_op jit(solution)/shard_map/ppermute | solution.py:403
  69.0 30.8 %copy-start.22 = (bf16[8,16,1024]{2,1,0:T(8,128)(2,1)}, bf16[8,16,1024]{2,1,0:T(8,128)(2,1)S(1)}, u32[]{:S(2)}) copy-start(bf16[8,16,1024]{2,1,0:T(8,128)(2,1)S(1)} %collective-permute-done.7.rest_5_) | copy-start | bytes 786436
  69.0 35.9 %collective-permute-start.12 = (bf16[8,16,1024]{2,1,0:T(8,128)(2,1)S(1)}, bf16[8,16,1024]{2,1,0:T(8,128)(2,1)}, u32[]{:S(2)}, u32[]{:S(2)}) collective-permute-start(bf16[8,16,1024]{2,1,0:T(8,128)(2,1)S(1)} %copy-done.15), channel_id=1, source_target_pairs={{0,2},{1,3},{2,0},{3,1},{4,6},{5,7},{6,4},{7,5},{8,10},{9,11},{10,... | collective-permute-start | bytes 786440 | tf_op jit(solution)/shard_map/ppermute | solution.py:403
  69.9 35.1 %collective-permute-start.13 = (bf16[8,16,1024]{2,1,0:T(8,128)(2,1)S(1)}, bf16[8,16,1024]{2,1,0:T(8,128)(2,1)}, u32[]{:S(2)}, u32[]{:S(2)}) collective-permute-start(bf16[8,16,1024]{2,1,0:T(8,128)(2,1)S(1)} %copy-done.14), channel_id=1, source_target_pairs={{0,14},{1,15},{2,12},{3,13},{4,10},{5,11},{6,8},{7,9},{8,6},{9,7},... | collective-permute-start | bytes 786440 | tf_op jit(solution)/shard_map/ppermute | solution.py:403
  77.6 27.3 %collective-permute-start.14 = (bf16[8,16,1024]{2,1,0:T(8,128)(2,1)S(1)}, bf16[8,16,1024]{2,1,0:T(8,128)(2,1)}, u32[]{:S(2)}, u32[]{:S(2)}) collective-permute-start(bf16[8,16,1024]{2,1,0:T(8,128)(2,1)S(1)} %copy-done.13), channel_id=1, source_target_pairs={{0,3},{1,2},{2,1},{3,0},{4,7},{5,6},{6,5},{7,4},{8,11},{9,10},{10,... | collective-permute-start | bytes 786440 | tf_op jit(solution)/shard_map/ppermute | solution.py:403
  99.8 23.9 %collective-permute-start.15 = (bf16[8,16,1024]{2,1,0:T(8,128)(2,1)S(1)}, bf16[8,16,1024]{2,1,0:T(8,128)(2,1)S(1)}, u32[]{:S(2)}, u32[]{:S(2)}) collective-permute-start(bf16[8,16,1024]{2,1,0:T(8,128)(2,1)S(1)} %copy-done.12), channel_id=1, source_target_pairs={{0,11},{1,10},{2,9},{3,8},{4,15},{5,14},{6,13},{7,12},{8,3},{9,2},... | collective-permute-start | bytes 786440 | tf_op jit(solution)/shard_map/ppermute | solution.py:403
  100.2 26.0 %collective-permute-start.16 = (bf16[8,16,1024]{2,1,0:T(8,128)(2,1)S(1)}, bf16[8,16,1024]{2,1,0:T(8,128)(2,1)S(1)}, u32[]{:S(2)}, u32[]{:S(2)}) collective-permute-start(bf16[8,16,1024]{2,1,0:T(8,128)(2,1)S(1)} %copy-done.11), channel_id=1, source_target_pairs={{0,15},{1,14},{2,13},{3,12},{4,11},{5,10},{6,9},{7,8},{8,7},{9,6},... | collective-permute-start | bytes 786440 | tf_op jit(solution)/shard_map/ppermute | solution.py:403
  (19 other events, 238.2 us)

commit v6 on v5

--- a/solution.py
+++ b/solution.py
@@ -392,8 +392,8 @@
     wide = pltpu.VMEM((8, -(-picked // LANES) * LANES), jnp.int32)
     if holders == 16:
         first = (8, 12)
-        groups = [(0, 8, 12, 4, 5, 1), (9, 6, 13, 7, 10, 2, 14, 3), (11, 15)]
-        others = [d for group in groups for d in group if d not in first]
+        groups = [(0, 8, 12, 4, 5, 1), (9, 13, 6, 7, 10, 2, 14, 3), (11, 15)]
+        others = (0, 9, 13, 4, 5, 1, 6, 7, 10, 2, 14, 3, 11, 15)
     else:
         first = ()
         groups = [None]
@@ -445,14 +445,15 @@
         arrived = {d: swap(part, d) for d, part in zip(first, parts)}
     else:
         table, positions = page_table, sel_pos
-    index_in = exchange(index)
-
     packed = pl.pallas_call(
         functools.partial(rows_kernel, hold, page_len),
         out_shape=jax.ShapeDtypeStruct((holders, ROW_SLOTS, width), store.dtype),
         scratch_shapes=[wide],
         compiler_params=params,
     )(table, positions, fresh)
+    if first:
+        index, packed = lax.optimization_barrier((index, packed))
+    index_in = exchange(index)
 
     each = jax.ShapeDtypeStruct((capacity, page_len, width), store.dtype)
     whole = jax.ShapeDtypeStruct((holders, capacity, page_len, width), store.dtype)

time: 139 us -> 142 us (1.022)
  waiting for transfers between devices: 19.5 us -> 23.6 us
  starting transfers between devices: 37.7 us -> 35.8 us
    all_to_all x2, waiting for transfers between devices: 0.57 us -> 5.29 us  [exchange(): return lax.all_to_all(x, 'store', split_axis=0, concat_axis=0, tiled=True)]
  transfers between devices with their start and end apart: 19 -> 19, of which waited for: 8 -> 8; matrix products, arithmetic and copies ran while one was open for 5% -> 5% of each run, Pallas kernels for 40% -> 37%
where the time goes in v6:
time: 142 us; the launch traced here: 140 us
  Pallas kernels  69.3 us (49%)
  starting transfers between devices  35.8 us (25%)
  waiting for transfers between devices  23.6 us (17%)
  other arithmetic  5.27 us (4%)
  local copies, waits for them, and re-layouts  4.97 us (4%)
    pallas_call x3, Pallas kernels, attend(): pl.pallas_call(functools.partial(attend_kernel, first, last, len(contexts...  49.9 us
    ppermute x17, starting transfers between devices, swap(): return lax.ppermute(x, 'store', [(h, h ^ d) for h in range(holders)])  23.2 us
    ppermute x17, waiting for transfers between devices, swap(): return lax.ppermute(x, 'store', [(h, h ^ d) for h in range(holders)])  18.4 us
    all_to_all x2, starting transfers between devices, exchange(): return lax.all_to_all(x, 'store', split_axis=0, concat_axis=0, tiled=True)  12.6 us
    pallas_call x1, Pallas kernels, per_device(): pl.pallas_call(write_back_kernel, grid_spec=pltpu.PrefetchScalarGridSpec(...  8.02 us
    all_to_all x2, waiting for transfers between devices, exchange(): return lax.all_to_all(x, 'store', split_axis=0, concat_axis=0, tiled=True)  5.29 us
    pallas_call x1, Pallas kernels, per_device(): pl.pallas_call(functools.partial(gather_kernel, capacity, others), grid_s...  4.89 us
  transfers between devices with their start and end apart: 19, of which 8 were waited for; matrix products, arithmetic and copies ran while one was open for 5% of the time, Pallas kernels for 37%

profile of v6, /device:TPU:9, one launch (start us, length us, event | category | flops | bytes accessed | tf_op | source)
XLA Modules:
  0.0 140.0 jit_solution(4429660005390098801)
XLA Ops:
  0.6 1.7 %shard_map.68 = (s32[16,2,128]{2,1,0:T(2,128)}, s32[1,2,128]{2,1,0:T(2,128)}, s32[1,2,128]{2,1,0:T(2,128)}) custom-call(s32[1]{0:T(128)} %bitcast.own, s32[1,128]{1,0:T(1,128)} %table_ref.2, s32[1,160]{1,0:T(1,128)} %rest_1_.2), custom_call_target="tpu_custom_call" | custom-call | tf_op jit(solution)/shard_map/pallas_call | solution.py:408
  2.3 2.3 %collective-permute-start = (s32[1,2,128]{2,1,0:T(2,128)}, s32[1,2,128]{2,1,0:T(2,128)S(1)}, u32[]{:S(2)}, u32[]{:S(2)}) collective-permute-start(s32[1,2,128]{2,1,0:T(2,128)} %get-tuple-element.51), channel_id=1, source_target_pairs={{0,8},{1,9},{2,10},{3,11},{4,12},{5,13},{6,14},{7,15},{8,0},{9,1},... | collective-permute-start | bytes 3080 | tf_op jit(solution)/shard_map/ppermute | solution.py:403
  7.8 2.5 %shard_map.69 = (bf16[8,16,1024]{2,1,0:T(8,128)(2,1)}, bf16[8,16,1024]{2,1,0:T(8,128)(2,1)}) custom-call(s32[1,2,128]{2,1,0:T(2,128)} %copy-done.7, s32[1,2,128]{2,1,0:T(2,128)} %copy-done.8, bf16[128,16,1024]{2,1,0:T(8,128)(2,1)} %store_hbm.3), custom_call_target="tpu_custom_call" | custom-call | tf_op jit(solution)/shard_map/pallas_call | solution.py:426
  10.3 2.4 %shard_map.70 = bf16[16,16,1024]{2,1,0:T(8,128)(2,1)} custom-call(s32[1,128]{1,0:T(1,128)} %table_ref.2, s32[1,160]{1,0:T(1,128)} %rest_1_.2, bf16[160,1024]{1,0:T(8,128)(2,1)} %bitcast.70), custom_call_target="tpu_custom_call" | custom-call | tf_op jit(solution)/shard_map/pallas_call | solution.py:448
  12.7 7.5 %all-to-all-start = ((s32[16,2,128]{2,1,0:T(2,128)}), s32[16,2,128]{2,1,0:T(2,128)S(1)}, u32[]{:S(2)}, u32[]{:S(2)}) async-start(s32[16,2,128]{2,1,0:T(2,128)} %get-tuple-element.59), calls=%async_computation | async-start | bytes 32768 | tf_op jit(solution)/shard_map/all_to_all | solution.py:406
  20.2 2.1 %collective-permute-start.2 = (bf16[8,16,1024]{2,1,0:T(8,128)(2,1)}, bf16[8,16,1024]{2,1,0:T(8,128)(2,1)S(1)}, u32[]{:S(2)}, u32[]{:S(2)}) collective-permute-start(bf16[8,16,1024]{2,1,0:T(8,128)(2,1)} %get-tuple-element.80), channel_id=1, source_target_pairs={{0,8},{1,9},{2,10},{3,11},{4,12},{5,13},{6,14},{7,15},{8,0},{9,1},... | collective-permute-start | bytes 786440 | tf_op jit(solution)/shard_map/ppermute | solution.py:403
  22.3 2.9 %all-to-all-done.index.targets_ref = s32[16,2,128]{2,1,0:T(2,128)S(1)} async-done(((s32[16,2,128]{2,1,0:T(2,128)}), s32[16,2,128]{2,1,0:T(2,128)S(1)}, u32[]{:S(2)}, u32[]{:S(2)}) %all-to-all-start) | async-done | bytes 16416 | tf_op jit(solution)/shard_map/all_to_all | solution.py:406
  25.8 4.9 %shard_map.71 = (bf16[8,16,1024]{2,1,0:T(8,128)(2,1)}, bf16[8,16,1024]{2,1,0:T(8,128)(2,1)}, bf16[8,16,1024]{2,1,0:T(8,128)(2,1)}, bf16[8,16,1024]{2,1,0:T(8,128...) custom-call(s32[1]{0:T(128)} %bitcast.own, ...), custom_call_target="tpu_custom_call" | custom-call | tf_op jit(solution)/shard_map/pallas_call | solution.py:460
  32.7 5.1 %all-to-all-start.1 = ((bf16[16,16,1024]{2,1,0:T(8,128)(2,1)}), bf16[16,16,1024]{2,1,0:T(8,128)(2,1)S(1)}, u32[]{:S(2)}, u32[]{:S(2)}) async-start(bf16[16,16,1024]{2,1,0:T(8,128)(2,1)} %shard_map.70), calls=%async_computation.1 | async-start | bytes 1048576 | tf_op jit(solution)/shard_map/all_to_all | solution.py:406
  37.8 1.9 %collective-permute-start.5 = (bf16[8,16,1024]{2,1,0:T(8,128)(2,1)}, bf16[8,16,1024]{2,1,0:T(8,128)(2,1)S(1)}, u32[]{:S(2)}, u32[]{:S(2)}) collective-permute-start(bf16[8,16,1024]{2,1,0:T(8,128)(2,1)} %get-tuple-element.83), channel_id=1, source_target_pairs={{0,5},{1,4},{2,7},{3,6},{4,1},{5,0},{6,3},{7,2},{8,13},{9,12},{10,... | collective-permute-start | bytes 786440 | tf_op jit(solution)/shard_map/ppermute | solution.py:403
  43.3 2.9 %collective-permute-start.7 = (bf16[8,16,1024]{2,1,0:T(8,128)(2,1)}, bf16[8,16,1024]{2,1,0:T(8,128)(2,1)S(1)}, u32[]{:S(2)}, u32[]{:S(2)}) collective-permute-start(bf16[8,16,1024]{2,1,0:T(8,128)(2,1)} %get-tuple-element.87), channel_id=1, source_target_pairs={{0,9},{1,8},{2,11},{3,10},{4,13},{5,12},{6,15},{7,14},{8,1},{9,0},... | collective-permute-start | bytes 786440 | tf_op jit(solution)/shard_map/ppermute | solution.py:403
  46.2 5.0 %collective-permute-done.3.rest_7_ = bf16[8,16,1024]{2,1,0:T(8,128)(2,1)S(1)} collective-permute-done((bf16[8,16,1024]{2,1,0:T(8,128)(2,1)}, bf16[8,16,1024]{2,1,0:T(8,128)(2,1)S(1)}, u32[]{:S(2)}, u32[]{:S(2)}) %collective-permute-start.3) | collective-permute-done | bytes 262176 | tf_op jit(solution)/shard_map/ppermute | solution.py:403
  51.2 2.5 %collective-permute-start.8 = (bf16[8,16,1024]{2,1,0:T(8,128)(2,1)}, bf16[8,16,1024]{2,1,0:T(8,128)(2,1)}, u32[]{:S(2)}, u32[]{:S(2)}) collective-permute-start(bf16[8,16,1024]{2,1,0:T(8,128)(2,1)} %get-tuple-element.88), channel_id=1, source_target_pairs={{0,13},{1,12},{2,15},{3,14},{4,9},{5,8},{6,11},{7,10},{8,5},{9,4},... | collective-permute-start | bytes 786440 | tf_op jit(solution)/shard_map/ppermute | solution.py:403
  55.3 2.4 %all-to-all-done.1.rows_hbm = bf16[16,16,1024]{2,1,0:T(8,128)(2,1)S(1)} async-done(((bf16[16,16,1024]{2,1,0:T(8,128)(2,1)}), bf16[16,16,1024]{2,1,0:T(8,128)(2,1)S(1)}, u32[]{:S(2)}, u32[]{:S(2)}) %all-to-all-start.1) | async-done | bytes 524320 | tf_op jit(solution)/shard_map/all_to_all | solution.py:406
  58.4 8.0 %shard_map.72 = bf16[128,16,1024]{2,1,0:T(8,128)(2,1)} custom-call(s32[16,2,128]{2,1,0:T(2,128)} %copy-done.1, s32[16,2,128]{2,1,0:T(2,128)} %copy-done.1, bf16[128,16,1024]{2,1,0:T(8,128)(2,1)} %store_hbm.3, bf16[16,16,1024]{2,1,0:T(8,128)(2,1)} %copy-done), custom_call_target="tpu_custom_call" | custom-call | bytes 8388608 | tf_op jit(solution)/shard_map/pallas_call | solution.py:481
  67.1 4.3 %collective-permute-start.11 = (bf16[8,16,1024]{2,1,0:T(8,128)(2,1)S(1)}, bf16[8,16,1024]{2,1,0:T(8,128)(2,1)}, u32[]{:S(2)}, u32[]{:S(2)}) collective-permute-start(bf16[8,16,1024]{2,1,0:T(8,128)(2,1)S(1)} %copy-done.17), channel_id=1, source_target_pairs={{0,10},{1,11},{2,8},{3,9},{4,14},{5,15},{6,12},{7,13},{8,2},{9,3},... | collective-permute-start | bytes 786440 | tf_op jit(solution)/shard_map/ppermute | solution.py:403
  71.4 2.4 %collective-permute-done.7.rest_5_ = bf16[8,16,1024]{2,1,0:T(8,128)(2,1)S(1)} collective-permute-done((bf16[8,16,1024]{2,1,0:T(8,128)(2,1)}, bf16[8,16,1024]{2,1,0:T(8,128)(2,1)S(1)}, u32[]{:S(2)}, u32[]{:S(2)}) %collective-permute-start.7) | collective-permute-done | bytes 262176 | tf_op jit(solution)/shard_map/ppermute | solution.py:403
  75.0 5.0 %collective-permute-done.8.rest_6_ = bf16[8,16,1024]{2,1,0:T(8,128)(2,1)} collective-permute-done((bf16[8,16,1024]{2,1,0:T(8,128)(2,1)}, bf16[8,16,1024]{2,1,0:T(8,128)(2,1)}, u32[]{:S(2)}, u32[]{:S(2)}) %collective-permute-start.8) | collective-permute-done | bytes 262176 | tf_op jit(solution)/shard_map/ppermute | solution.py:403
  80.0 2.6 %collective-permute-start.13 = (bf16[8,16,1024]{2,1,0:T(8,128)(2,1)S(1)}, bf16[8,16,1024]{2,1,0:T(8,128)(2,1)}, u32[]{:S(2)}, u32[]{:S(2)}) collective-permute-start(bf16[8,16,1024]{2,1,0:T(8,128)(2,1)S(1)} %copy-done.14), channel_id=1, source_target_pairs={{0,14},{1,15},{2,12},{3,13},{4,10},{5,11},{6,8},{7,9},{8,6},{9,7},... | collective-permute-start | bytes 786440 | tf_op jit(solution)/shard_map/ppermute | solution.py:403
  84.1 20.4 %shard_map.73 = (f32[5,4,128,384]{3,2,1,0:T(8,128)}, f32[5,8,384]{2,1,0:T(8,128)}) custom-call(s32[48]{0:T(128)} %get-tuple-element.101.place, s32[48]{0:T(128)} %copy-done.10, s32[5]{0:T(128)} %fusion.7.tiles, s32[5,1,128]{2,1,0:T(1,128)} %tile.9.rest_0_, s32[1,160]{1,0:T(1,128)} %rest_1_.2, bf16[160,6144]{1,0:T(8,128)(2,1)} %bitcast.66, ...), custom_call_target="tpu_custom_call" | custom-call | flops 4831838208 | bytes 7995392 | tf_op jit(solution)/shard_map/pallas_call | solution.py:311
  104.6 1.8 %collective-permute-start.16 = (bf16[8,16,1024]{2,1,0:T(8,128)(2,1)S(1)}, bf16[8,16,1024]{2,1,0:T(8,128)(2,1)S(1)}, u32[]{:S(2)}, u32[]{:S(2)}) collective-permute-start(bf16[8,16,1024]{2,1,0:T(8,128)(2,1)S(1)} %copy-done.11), channel_id=1, source_target_pairs={{0,15},{1,14},{2,13},{3,12},{4,11},{5,10},{6,9},{7,8},{8,7},{9,6},... | collective-permute-start | bytes 786440 | tf_op jit(solution)/shard_map/ppermute | solution.py:403
  106.4 18.8 %shard_map.74 = (f32[5,4,128,384]{3,2,1,0:T(8,128)}, f32[5,8,384]{2,1,0:T(8,128)}) custom-call(s32[64]{0:T(128)} %get-tuple-element.103.place, s32[64]{0:T(128)} %copy-done.9, s32[5]{0:T(128)} %and_select_fusion.1.tiles, s32[5,1,128]{2,1,0:T(1,128)} %tile.9.rest_0_, s32[1,160]{1,0:T(1,128)} %rest_1_.2, bf16[160,6144]{1,0:T(8,128)(2,1)} %bitcast.67, ...), custom_call_target="tpu_custom_call" | custom-call | flops 4831838208 | bytes 7995392 | tf_op jit(solution)/shard_map/pallas_call | solution.py:311
  125.3 3.3 %collective-permute-done.16.rest_6_ = bf16[8,16,1024]{2,1,0:T(8,128)(2,1)S(1)} collective-permute-done((bf16[8,16,1024]{2,1,0:T(8,128)(2,1)S(1)}, bf16[8,16,1024]{2,1,0:T(8,128)(2,1)S(1)}, u32[]{:S(2)}, u32[]{:S(2)}) %collective-permute-start.16) | collective-permute-done | bytes 262176 | tf_op jit(solution)/shard_map/ppermute | solution.py:403
  129.2 10.7 %shard_map.75 = bf16[160,6144]{1,0:T(8,128)(2,1)} custom-call(s32[16]{0:T(128)} %get-tuple-element.105.place, s32[16]{0:T(128)} %copy-done.6, s32[5]{0:T(128)} %and_select_fusion.2.tiles, s32[5,1,128]{2,1,0:T(1,128)} %tile.9.rest_0_, s32[1,160]{1,0:T(1,128)} %rest_1_.2, bf16[160,6144]{1,0:T(8,128)(2,1)} %bitcast.68, ...), custom_call_target="tpu_custom_call" | custom-call | flops 1207959552 | bytes 6422528 | tf_op jit(solution)/shard_map/pallas_call | solution.py:311
  (94 shorter events, 15.6 us)
Async XLA Ops:
  2.3 3.5 %collective-permute-start = (s32[1,2,128]{2,1,0:T(2,128)}, s32[1,2,128]{2,1,0:T(2,128)S(1)}, u32[]{:S(2)}, u32[]{:S(2)}) collective-permute-start(s32[1,2,128]{2,1,0:T(2,128)} %get-tuple-element.51), channel_id=1, source_target_pairs={{0,8},{1,9},{2,10},{3,11},{4,12},{5,13},{6,14},{7,15},{8,0},{9,1},... | collective-permute-start | bytes 3080 | tf_op jit(solution)/shard_map/ppermute | solution.py:403
  4.6 2.6 %collective-permute-start.1 = (s32[1,2,128]{2,1,0:T(2,128)}, s32[1,2,128]{2,1,0:T(2,128)S(1)}, u32[]{:S(2)}, u32[]{:S(2)}) collective-permute-start(s32[1,2,128]{2,1,0:T(2,128)} %get-tuple-element.52), channel_id=1, source_target_pairs={{0,12},{1,13},{2,14},{3,15},{4,8},{5,9},{6,10},{7,11},{8,4},{9,5},... | collective-permute-start | bytes 3080 | tf_op jit(solution)/shard_map/ppermute | solution.py:403
  12.7 12.6 %all-to-all-start = ((s32[16,2,128]{2,1,0:T(2,128)}), s32[16,2,128]{2,1,0:T(2,128)S(1)}, u32[]{:S(2)}, u32[]{:S(2)}) async-start(s32[16,2,128]{2,1,0:T(2,128)} %get-tuple-element.59), calls=%async_computation | async-start | bytes 32768 | tf_op jit(solution)/shard_map/all_to_all | solution.py:406
  20.2 23.0 %collective-permute-start.2 = (bf16[8,16,1024]{2,1,0:T(8,128)(2,1)}, bf16[8,16,1024]{2,1,0:T(8,128)(2,1)S(1)}, u32[]{:S(2)}, u32[]{:S(2)}) collective-permute-start(bf16[8,16,1024]{2,1,0:T(8,128)(2,1)} %get-tuple-element.80), channel_id=1, source_target_pairs={{0,8},{1,9},{2,10},{3,11},{4,12},{5,13},{6,14},{7,15},{8,0},{9,1},... | collective-permute-start | bytes 786440 | tf_op jit(solution)/shard_map/ppermute | solution.py:403
  22.3 28.9 %collective-permute-start.3 = (bf16[8,16,1024]{2,1,0:T(8,128)(2,1)}, bf16[8,16,1024]{2,1,0:T(8,128)(2,1)S(1)}, u32[]{:S(2)}, u32[]{:S(2)}) collective-permute-start(bf16[8,16,1024]{2,1,0:T(8,128)(2,1)} %get-tuple-element.81), channel_id=1, source_target_pairs={{0,12},{1,13},{2,14},{3,15},{4,8},{5,9},{6,10},{7,11},{8,4},{9,5},... | collective-permute-start | bytes 786440 | tf_op jit(solution)/shard_map/ppermute | solution.py:403
  32.7 25.0 %all-to-all-start.1 = ((bf16[16,16,1024]{2,1,0:T(8,128)(2,1)}), bf16[16,16,1024]{2,1,0:T(8,128)(2,1)S(1)}, u32[]{:S(2)}, u32[]{:S(2)}) async-start(bf16[16,16,1024]{2,1,0:T(8,128)(2,1)} %shard_map.70), calls=%async_computation.1 | async-start | bytes 1048576 | tf_op jit(solution)/shard_map/all_to_all | solution.py:406
  37.8 15.9 %collective-permute-start.4 = (bf16[8,16,1024]{2,1,0:T(8,128)(2,1)}, bf16[8,16,1024]{2,1,0:T(8,128)(2,1)S(1)}, u32[]{:S(2)}, u32[]{:S(2)}) collective-permute-start(bf16[8,16,1024]{2,1,0:T(8,128)(2,1)} %get-tuple-element.82), channel_id=1, source_target_pairs={{0,4},{1,5},{2,6},{3,7},{4,0},{5,1},{6,2},{7,3},{8,12},{9,13},{10,... | collective-permute-start | bytes 786440 | tf_op jit(solution)/shard_map/ppermute | solution.py:403
  37.8 28.6 %collective-permute-start.5 = (bf16[8,16,1024]{2,1,0:T(8,128)(2,1)}, bf16[8,16,1024]{2,1,0:T(8,128)(2,1)S(1)}, u32[]{:S(2)}, u32[]{:S(2)}) collective-permute-start(bf16[8,16,1024]{2,1,0:T(8,128)(2,1)} %get-tuple-element.83), channel_id=1, source_target_pairs={{0,5},{1,4},{2,7},{3,6},{4,1},{5,0},{6,3},{7,2},{8,13},{9,12},{10,... | collective-permute-start | bytes 786440 | tf_op jit(solution)/shard_map/ppermute | solution.py:403
  39.8 27.3 %collective-permute-start.6 = (bf16[8,16,1024]{2,1,0:T(8,128)(2,1)}, bf16[8,16,1024]{2,1,0:T(8,128)(2,1)S(1)}, u32[]{:S(2)}, u32[]{:S(2)}) collective-permute-start(bf16[8,16,1024]{2,1,0:T(8,128)(2,1)} %get-tuple-element.84), channel_id=1, source_target_pairs={{0,1},{1,0},{2,3},{3,2},{4,5},{5,4},{6,7},{7,6},{8,9},{9,8},{10,11... | collective-permute-start | bytes 786440 | tf_op jit(solution)/shard_map/ppermute | solution.py:403
  43.2 40.8 %copy-start.16 = (bf16[8,16,1024]{2,1,0:T(8,128)(2,1)}, bf16[8,16,1024]{2,1,0:T(8,128)(2,1)S(1)}, u32[]{:S(2)}) copy-start(bf16[8,16,1024]{2,1,0:T(8,128)(2,1)S(1)} %collective-permute-done.2.rest_6_) | copy-start | bytes 786436
  43.3 30.6 %collective-permute-start.7 = (bf16[8,16,1024]{2,1,0:T(8,128)(2,1)}, bf16[8,16,1024]{2,1,0:T(8,128)(2,1)S(1)}, u32[]{:S(2)}, u32[]{:S(2)}) collective-permute-start(bf16[8,16,1024]{2,1,0:T(8,128)(2,1)} %get-tuple-element.87), channel_id=1, source_target_pairs={{0,9},{1,8},{2,11},{3,10},{4,13},{5,12},{6,15},{7,14},{8,1},{9,0},... | collective-permute-start | bytes 786440 | tf_op jit(solution)/shard_map/ppermute | solution.py:403
  51.2 32.9 %copy-start.18 = (bf16[8,16,1024]{2,1,0:T(8,128)(2,1)}, bf16[8,16,1024]{2,1,0:T(8,128)(2,1)S(1)}, u32[]{:S(2)}) copy-start(bf16[8,16,1024]{2,1,0:T(8,128)(2,1)S(1)} %collective-permute-done.3.rest_7_) | copy-start | bytes 786436
  51.2 28.8 %collective-permute-start.8 = (bf16[8,16,1024]{2,1,0:T(8,128)(2,1)}, bf16[8,16,1024]{2,1,0:T(8,128)(2,1)}, u32[]{:S(2)}, u32[]{:S(2)}) collective-permute-start(bf16[8,16,1024]{2,1,0:T(8,128)(2,1)} %get-tuple-element.88), channel_id=1, source_target_pairs={{0,13},{1,12},{2,15},{3,14},{4,9},{5,8},{6,11},{7,10},{8,5},{9,4},... | collective-permute-start | bytes 786440 | tf_op jit(solution)/shard_map/ppermute | solution.py:403
  53.7 30.4 %copy-start.20 = (bf16[8,16,1024]{2,1,0:T(8,128)(2,1)}, bf16[8,16,1024]{2,1,0:T(8,128)(2,1)S(1)}, u32[]{:S(2)}) copy-start(bf16[8,16,1024]{2,1,0:T(8,128)(2,1)S(1)} %collective-permute-done.4.rest_8_) | copy-start | bytes 786436
  53.7 28.9 %collective-permute-start.9 = (bf16[8,16,1024]{2,1,0:T(8,128)(2,1)}, bf16[8,16,1024]{2,1,0:T(8,128)(2,1)}, u32[]{:S(2)}, u32[]{:S(2)}) collective-permute-start(bf16[8,16,1024]{2,1,0:T(8,128)(2,1)} %get-tuple-element.89), channel_id=1, source_target_pairs={{0,6},{1,7},{2,4},{3,5},{4,2},{5,3},{6,0},{7,1},{8,14},{9,15},{10,... | collective-permute-start | bytes 786440 | tf_op jit(solution)/shard_map/ppermute | solution.py:403
  55.3 27.4 %copy-start.13 = (bf16[8,16,1024]{2,1,0:T(8,128)(2,1)S(1)}, bf16[8,16,1024]{2,1,0:T(8,128)(2,1)}, u32[]{:S(2)}) copy-start(bf16[8,16,1024]{2,1,0:T(8,128)(2,1)} %get-tuple-element.94) | copy-start | bytes 786436
  66.5 38.0 %collective-permute-start.10 = (bf16[8,16,1024]{2,1,0:T(8,128)(2,1)S(1)}, bf16[8,16,1024]{2,1,0:T(8,128)(2,1)}, u32[]{:S(2)}, u32[]{:S(2)}) collective-permute-start(bf16[8,16,1024]{2,1,0:T(8,128)(2,1)S(1)} %copy-done.19), channel_id=1, source_target_pairs={{0,7},{1,6},{2,5},{3,4},{4,3},{5,2},{6,1},{7,0},{8,15},{9,14},{10,... | collective-permute-start | bytes 786440 | tf_op jit(solution)/shard_map/ppermute | solution.py:403
  67.1 37.5 %collective-permute-start.11 = (bf16[8,16,1024]{2,1,0:T(8,128)(2,1)S(1)}, bf16[8,16,1024]{2,1,0:T(8,128)(2,1)}, u32[]{:S(2)}, u32[]{:S(2)}) collective-permute-start(bf16[8,16,1024]{2,1,0:T(8,128)(2,1)S(1)} %copy-done.17), channel_id=1, source_target_pairs={{0,10},{1,11},{2,8},{3,9},{4,14},{5,15},{6,12},{7,13},{8,2},{9,3},... | collective-permute-start | bytes 786440 | tf_op jit(solution)/shard_map/ppermute | solution.py:403
  73.8 30.7 %copy-start.22 = (bf16[8,16,1024]{2,1,0:T(8,128)(2,1)}, bf16[8,16,1024]{2,1,0:T(8,128)(2,1)S(1)}, u32[]{:S(2)}) copy-start(bf16[8,16,1024]{2,1,0:T(8,128)(2,1)S(1)} %collective-permute-done.7.rest_5_) | copy-start | bytes 786436
  73.8 32.6 %collective-permute-start.12 = (bf16[8,16,1024]{2,1,0:T(8,128)(2,1)S(1)}, bf16[8,16,1024]{2,1,0:T(8,128)(2,1)}, u32[]{:S(2)}, u32[]{:S(2)}) collective-permute-start(bf16[8,16,1024]{2,1,0:T(8,128)(2,1)S(1)} %copy-done.15), channel_id=1, source_target_pairs={{0,2},{1,3},{2,0},{3,1},{4,6},{5,7},{6,4},{7,5},{8,10},{9,11},{10,... | collective-permute-start | bytes 786440 | tf_op jit(solution)/shard_map/ppermute | solution.py:403
  80.0 26.4 %collective-permute-start.13 = (bf16[8,16,1024]{2,1,0:T(8,128)(2,1)S(1)}, bf16[8,16,1024]{2,1,0:T(8,128)(2,1)}, u32[]{:S(2)}, u32[]{:S(2)}) collective-permute-start(bf16[8,16,1024]{2,1,0:T(8,128)(2,1)S(1)} %copy-done.14), channel_id=1, source_target_pairs={{0,14},{1,15},{2,12},{3,13},{4,10},{5,11},{6,8},{7,9},{8,6},{9,7},... | collective-permute-start | bytes 786440 | tf_op jit(solution)/shard_map/ppermute | solution.py:403
  82.7 23.7 %collective-permute-start.14 = (bf16[8,16,1024]{2,1,0:T(8,128)(2,1)S(1)}, bf16[8,16,1024]{2,1,0:T(8,128)(2,1)}, u32[]{:S(2)}, u32[]{:S(2)}) collective-permute-start(bf16[8,16,1024]{2,1,0:T(8,128)(2,1)S(1)} %copy-done.13), channel_id=1, source_target_pairs={{0,3},{1,2},{2,1},{3,0},{4,7},{5,6},{6,5},{7,4},{8,11},{9,10},{10,... | collective-permute-start | bytes 786440 | tf_op jit(solution)/shard_map/ppermute | solution.py:403
  104.5 20.7 %collective-permute-start.15 = (bf16[8,16,1024]{2,1,0:T(8,128)(2,1)S(1)}, bf16[8,16,1024]{2,1,0:T(8,128)(2,1)S(1)}, u32[]{:S(2)}, u32[]{:S(2)}) collective-permute-start(bf16[8,16,1024]{2,1,0:T(8,128)(2,1)S(1)} %copy-done.12), channel_id=1, source_target_pairs={{0,11},{1,10},{2,9},{3,8},{4,15},{5,14},{6,13},{7,12},{8,3},{9,2},... | collective-permute-start | bytes 786440 | tf_op jit(solution)/shard_map/ppermute | solution.py:403
  104.6 23.9 %collective-permute-start.16 = (bf16[8,16,1024]{2,1,0:T(8,128)(2,1)S(1)}, bf16[8,16,1024]{2,1,0:T(8,128)(2,1)S(1)}, u32[]{:S(2)}, u32[]{:S(2)}) collective-permute-start(bf16[8,16,1024]{2,1,0:T(8,128)(2,1)S(1)} %copy-done.11), channel_id=1, source_target_pairs={{0,15},{1,14},{2,13},{3,12},{4,11},{5,10},{6,9},{7,8},{8,7},{9,6},... | collective-permute-start | bytes 786440 | tf_op jit(solution)/shard_map/ppermute | solution.py:403
  (19 other events, 278.3 us)

commit v7 on v6

--- a/solution.py
+++ b/solution.py
@@ -22,6 +22,14 @@
 
 def nt_dot(a, b):
     return lax.dot_general(a, b, (((1,), (1,)), ((), ())), preferred_element_type=jnp.float32)
+
+
+def distance(own, step):
+    mask, even, odd = step
+    bits = own & mask
+    bits = bits ^ (bits >> 2)
+    bits = (bits ^ (bits >> 1)) & 1
+    return even + bits * (odd - even)
 
 
 def one_hot(condition):
@@ -81,7 +89,7 @@
         out_ref[h, 0:1, :] = numbers[h : h + 1, :].astype(jnp.int32)
         out_ref[h, 1:2, :] = targets[h : h + 1, :].astype(jnp.int32)
     for d, ref in zip(first, first_refs):
-        ref[0] = out_ref[own[0] ^ d]
+        ref[0] = out_ref[own[0] ^ distance(own[0], d)]
 
 
 def rows_kernel(hold, page_len, table_ref, sel_ref, fresh_ref, packed, wide):
@@ -111,16 +119,20 @@
     pltpu.make_async_copy(held, held, send_sem).wait()
 
 
-def gather_kernel(capacity, distances, own, index, store_hbm, *rest):
-    sends, (store, load_sem, send_sem) = rest[:-3], rest[-3:]
+def gather_kernel(capacity, steps, own, index, *rest):
+    if steps:
+        numbers, *rest = rest
+    store_hbm, *sends = rest[:-3]
+    store, load_sem, send_sem = rest[-3:]
     load = pltpu.make_async_copy(store_hbm, store, load_sem)
     load.start()
     load.wait()
-    for i in range(len(distances) if distances else index.shape[0]):
-        r = own[0] ^ distances[i] if distances else i
-        send = sends[i] if distances else sends[0].at[i]
+    for i in range(len(steps) if steps else index.shape[0]):
+        r = own[0] ^ distance(own[0], steps[i]) if steps else i
+        send = sends[i] if steps else sends[0].at[i]
         for k in range(capacity):
-            pltpu.make_async_copy(store.at[index[r, 0, k]], send.at[k], send_sem).start()
+            number = numbers[0, 0, k] if steps and i == 0 else index[r, 0, k]
+            pltpu.make_async_copy(store.at[number], send.at[k], send_sem).start()
     for send in sends:
         pltpu.make_async_copy(send, send, send_sem).wait()
 
@@ -352,7 +364,6 @@
     before = number[None, :] < number[:, None]
     owners = slots // hold
     ranks = jnp.sum(((owners[None, :] == owners[:, None]) & before).astype(jnp.int32), axis=1)
-    distance = owners ^ own
     last_page = positions.reshape(-1, QUERY_BLOCK)[:, -1] // page_len
     orders = []
     for at, group in enumerate(groups):
@@ -361,8 +372,8 @@
             count = pages
         else:
             arrival = jnp.full((pages,), -1, jnp.int32)
-            for i, d in enumerate(group):
-                arrival = jnp.where(distance == d, i * capacity + ranks, arrival)
+            for i, step in enumerate(group):
+                arrival = jnp.where(owners ^ own == distance(own, step), i * capacity + ranks, arrival)
             count = len(group) * capacity
         member = arrival >= 0
         place = jnp.sum((member[None, :] & before).astype(jnp.int32), axis=1)
@@ -391,38 +402,42 @@
     fresh = fresh_kv[0]
     wide = pltpu.VMEM((8, -(-picked // LANES) * LANES), jnp.int32)
     if holders == 16:
-        first = (8, 12)
-        groups = [(0, 8, 12, 4, 5, 1), (9, 13, 6, 7, 10, 2, 14, 3), (11, 15)]
-        others = (0, 9, 13, 4, 5, 1, 6, 7, 10, 2, 14, 3, 11, 15)
+        local, near, first = (0, 0, 0), (0, 1, 1), [(0, 8, 8), (0, 12, 12)]
+        mixed = [(5, 13, 5), (9, 9, 4), (1, 10, 2), (1, 14, 6), (3, 11, 3), (3, 15, 7)]
+        mixed = [step for m, a, b in mixed for step in ((m, a, b), (m, b, a))]
+        groups = [[local, *first, near, *mixed[0:2]], mixed[2:6], mixed[6:10], mixed[10:12]]
+        others = [near, local, *mixed]
     else:
-        first = ()
+        first = []
         groups = [None]
         others = None
 
-    def swap(x, d):
-        return lax.ppermute(x, "store", [(h, h ^ d) for h in range(holders)])
+    def swap(x, step):
+        return lax.ppermute(x, "store", [(h, h ^ distance(h, step)) for h in range(holders)])
 
     def exchange(x):
         return lax.all_to_all(x, "store", split_axis=0, concat_axis=0, tiled=True)
 
+    ahead = [*first, near] if first else []
     index, *lists = pl.pallas_call(
-        functools.partial(index_kernel, hold, page_len, first),
+        functools.partial(index_kernel, hold, page_len, ahead),
         grid_spec=pltpu.PrefetchScalarGridSpec(
             num_scalar_prefetch=1,
             grid=(1,),
             in_specs=[vmem, vmem],
-            out_specs=[vmem] * (1 + len(first)),
+            out_specs=[vmem] * (1 + len(ahead)),
             scratch_shapes=[wide],
         ),
         out_shape=[
             jax.ShapeDtypeStruct((holders, 2, LANES), jnp.int32),
-            *[jax.ShapeDtypeStruct((1, 2, LANES), jnp.int32)] * len(first),
+            *[jax.ShapeDtypeStruct((1, 2, LANES), jnp.int32)] * len(ahead),
         ],
         compiler_params=params,
     )(own_word, page_table, sel_pos)
     arrived = {}
+    near_list = []
     if first:
-        lists = [swap(x, d) for x, d in zip(lists, first)]
+        early = [swap(x, step) for x, step in zip(lists, first)]
         parts = pl.pallas_call(
             functools.partial(first_gather_kernel, len(first)),
             grid_spec=pltpu.PrefetchScalarGridSpec(
@@ -438,11 +453,13 @@
             ),
             out_shape=[jax.ShapeDtypeStruct((capacity, page_len, width), store.dtype)] * len(first),
             compiler_params=params,
-        )(*lists, store)
-        parts, index, table, positions = lax.optimization_barrier(
-            (parts, index, page_table, sel_pos)
+        )(*early, store)
+        parts, near_list = lax.optimization_barrier((parts, lists[len(first)]))
+        arrived = {step: swap(part, step) for step, part in zip(first, parts)}
+        near_list, index, table, positions = lax.optimization_barrier(
+            (swap(near_list, near), index, page_table, sel_pos)
         )
-        arrived = {d: swap(part, d) for d, part in zip(first, parts)}
+        near_list = [near_list]
     else:
         table, positions = page_table, sel_pos
     packed = pl.pallas_call(
@@ -451,8 +468,6 @@
         scratch_shapes=[wide],
         compiler_params=params,
     )(table, positions, fresh)
-    if first:
-        index, packed = lax.optimization_barrier((index, packed))
     index_in = exchange(index)
 
     each = jax.ShapeDtypeStruct((capacity, page_len, width), store.dtype)
@@ -460,7 +475,7 @@
     parts = pl.pallas_call(
         functools.partial(gather_kernel, capacity, others),
         grid_spec=pltpu.PrefetchScalarGridSpec(
-            num_scalar_prefetch=2,
+            num_scalar_prefetch=2 + len(near_list),
             grid=(1,),
             in_specs=[hbm],
             out_specs=[hbm] * (len(others) if others else 1),
@@ -468,12 +483,12 @@
         ),
         out_shape=[each] * len(others) if others else [whole],
         compiler_params=params,
-    )(own_word, index_in, store)
+    )(own_word, index_in, *near_list, store)
     parts, packed, table, positions = lax.optimization_barrier((parts, packed, table, positions))
     if others:
-        for d, part in zip(others, parts):
-            arrived[d] = swap(part, d) if d else part
-        contexts = [[arrived[d] for d in group] for group in groups]
+        for step, part in zip(others, parts):
+            arrived[step] = part if step == local else swap(part, step)
+        contexts = [[arrived[step] for step in group] for group in groups]
     else:
         contexts = [[exchange(parts[0]).reshape(pages, page_len, width)]]
     rows_in = exchange(packed)

time: 142 us -> 169 us (1.19)
  the two profiles are of different devices: /device:TPU:9 before, /device:TPU:1 now
where the time goes in v7:
time: 169 us; the launch traced here: 168 us
  Pallas kernels  75.9 us (45%)
  starting transfers between devices  75.3 us (45%)
  other arithmetic  6.45 us (4%)
  local copies, waits for them, and re-layouts  4.94 us (3%)
  waiting for transfers between devices  4.55 us (3%)
    ppermute x18, starting transfers between devices, swap(): lax.ppermute(x, 'store', [(h, h ^ distance(h, step)) for h in range(holde...  66 us
    pallas_call x4, Pallas kernels, attend(): pl.pallas_call(functools.partial(attend_kernel, first, last, len(contexts...  56.4 us
    all_to_all x2, starting transfers between devices, exchange(): return lax.all_to_all(x, 'store', split_axis=0, concat_axis=0, tiled=True)  9.28 us
    pallas_call x1, Pallas kernels, per_device(): pl.pallas_call(write_back_kernel, grid_spec=pltpu.PrefetchScalarGridSpec(...  8.02 us
    pallas_call x1, Pallas kernels, per_device(): pl.pallas_call(functools.partial(gather_kernel, capacity, others), grid_s...  4.93 us
    ppermute x18, waiting for transfers between devices, swap(): lax.ppermute(x, 'store', [(h, h ^ distance(h, step)) for h in range(holde...  4.18 us
  transfers between devices with their start and end apart: 20, of which 5 were waited for; matrix products, arithmetic and copies ran while one was open for 5% of the time, Pallas kernels for 36%

profile of v7, /device:TPU:1, one launch (start us, length us, event | category | flops | bytes accessed | tf_op | source)
XLA Modules:
  0.0 168.1 jit_solution(18364037166938115423)
XLA Ops:
  0.6 1.7 shard_map.68
  2.3 3.1 %collective-permute-start = (s32[1,2,128]{2,1,0:T(2,128)}, s32[1,2,128]{2,1,0:T(2,128)S(1)}, u32[]{:S(2)}, u32[]{:S(2)}) collective-permute-start(s32[1,2,128]{2,1,0:T(2,128)} %get-tuple-element.54), channel_id=1, source_target_pairs={{0,8},{1,9},{2,10},{3,11},{4,12},{5,13},{6,14},{7,15},{8,0},{9,1},... | collective-permute-start | bytes 3080 | tf_op jit(solution)/shard_map/ppermute | solution.py:416
  6.6 3.3 %collective-permute-done.1.refs_1_ = s32[1,2,128]{2,1,0:T(2,128)S(1)} collective-permute-done((s32[1,2,128]{2,1,0:T(2,128)}, s32[1,2,128]{2,1,0:T(2,128)S(1)}, u32[]{:S(2)}, u32[]{:S(2)}) %collective-permute-start.1) | collective-permute-done | bytes 1056 | tf_op jit(solution)/shard_map/ppermute | solution.py:416
  10.4 2.5 %shard_map.69 = (bf16[8,16,1024]{2,1,0:T(8,128)(2,1)}, bf16[8,16,1024]{2,1,0:T(8,128)(2,1)}) custom-call(s32[1,2,128]{2,1,0:T(2,128)} %copy-done.10, s32[1,2,128]{2,1,0:T(2,128)} %copy-done.11, bf16[128,16,1024]{2,1,0:T(8,128)(2,1)} %store_hbm.1), custom_call_target="tpu_custom_call" | custom-call | tf_op jit(solution)/shard_map/pallas_call | solution.py:441
  12.9 2.2 %collective-permute-start.2 = (s32[1,2,128]{2,1,0:T(2,128)S(1)}, s32[1,2,128]{2,1,0:T(2,128)S(1)}, u32[]{:S(2)}, u32[]{:S(2)}) collective-permute-start(s32[1,2,128]{2,1,0:T(2,128)S(1)} %copy-done.26), channel_id=1, source_target_pairs={{0,1},{1,0},{2,3},{3,2},{4,5},{5,4},{6,7},{7,6},{8,9},{9,8},{10,11... | collective-permute-start | bytes 3080 | tf_op jit(solution)/shard_map/ppermute | solution.py:416
  15.9 3.9 %all-to-all-start = ((s32[16,2,128]{2,1,0:T(2,128)}), s32[16,2,128]{2,1,0:T(2,128)S(1)}, u32[]{:S(2)}, u32[]{:S(2)}) async-start(s32[16,2,128]{2,1,0:T(2,128)} %get-tuple-element.61), calls=%async_computation | async-start | bytes 32768 | tf_op jit(solution)/shard_map/all_to_all | solution.py:419
  19.8 2.3 %collective-permute-start.3 = (bf16[8,16,1024]{2,1,0:T(8,128)(2,1)}, bf16[8,16,1024]{2,1,0:T(8,128)(2,1)S(1)}, u32[]{:S(2)}, u32[]{:S(2)}) collective-permute-start(bf16[8,16,1024]{2,1,0:T(8,128)(2,1)} %get-tuple-element.84), channel_id=1, source_target_pairs={{0,8},{1,9},{2,10},{3,11},{4,12},{5,13},{6,14},{7,15},{8,0},{9,1},... | collective-permute-start | bytes 786440 | tf_op jit(solution)/shard_map/ppermute | solution.py:416
  23.3 2.4 %shard_map.71 = bf16[16,16,1024]{2,1,0:T(8,128)(2,1)} custom-call(s32[1,128]{1,0:T(1,128)} %table_ref.2, s32[1,160]{1,0:T(1,128)} %rest_1_.5, bf16[160,1024]{1,0:T(8,128)(2,1)} %bitcast.72), custom_call_target="tpu_custom_call" | custom-call | tf_op jit(solution)/shard_map/pallas_call | solution.py:465
  26.3 4.9 %shard_map.70 = (bf16[8,16,1024]{2,1,0:T(8,128)(2,1)}, bf16[8,16,1024]{2,1,0:T(8,128)(2,1)}, bf16[8,16,1024]{2,1,0:T(8,128)(2,1)}, bf16[8,16,1024]{2,1,0:T(8,128...) custom-call(s32[1]{0:T(128)} %bitcast.own, ...), custom_call_target="tpu_custom_call" | custom-call | tf_op jit(solution)/shard_map/pallas_call | solution.py:475
  33.1 5.4 %all-to-all-start.1 = ((bf16[16,16,1024]{2,1,0:T(8,128)(2,1)}), bf16[16,16,1024]{2,1,0:T(8,128)(2,1)S(1)}, u32[]{:S(2)}, u32[]{:S(2)}) async-start(bf16[16,16,1024]{2,1,0:T(8,128)(2,1)} %shard_map.71), calls=%async_computation.1 | async-start | bytes 1048576 | tf_op jit(solution)/shard_map/all_to_all | solution.py:419
  38.7 1.6 collective-permute-start.6
  40.3 2.3 %collective-permute-start.7 = (bf16[8,16,1024]{2,1,0:T(8,128)(2,1)}, bf16[8,16,1024]{2,1,0:T(8,128)(2,1)S(1)}, u32[]{:S(2)}, u32[]{:S(2)}) collective-permute-start(bf16[8,16,1024]{2,1,0:T(8,128)(2,1)} %get-tuple-element.88), channel_id=1, source_target_pairs={{0,5},{1,12},{2,7},{3,14},{4,9},{5,0},{6,11},{7,2},{8,13},{9,4},{1... | collective-permute-start | bytes 786440 | tf_op jit(solution)/shard_map/ppermute | solution.py:416
  48.2 9.6 %collective-permute-start.9 = (bf16[8,16,1024]{2,1,0:T(8,128)(2,1)}, bf16[8,16,1024]{2,1,0:T(8,128)(2,1)}, u32[]{:S(2)}, u32[]{:S(2)}) collective-permute-start(bf16[8,16,1024]{2,1,0:T(8,128)(2,1)} %get-tuple-element.92), channel_id=1, source_target_pairs={{0,4},{1,8},{2,6},{3,10},{4,0},{5,12},{6,2},{7,14},{8,1},{9,13},{1... | collective-permute-start | bytes 786440 | tf_op jit(solution)/shard_map/ppermute | solution.py:416
  57.8 1.3 collective-permute-start.10
  61.9 8.0 %shard_map.72 = bf16[128,16,1024]{2,1,0:T(8,128)(2,1)} custom-call(s32[16,2,128]{2,1,0:T(2,128)} %copy-done.1, s32[16,2,128]{2,1,0:T(2,128)} %copy-done.1, bf16[128,16,1024]{2,1,0:T(8,128)(2,1)} %store_hbm.1, bf16[16,16,1024]{2,1,0:T(8,128)(2,1)} %copy-done), custom_call_target="tpu_custom_call" | custom-call | bytes 8388608 | tf_op jit(solution)/shard_map/pallas_call | solution.py:496
  70.0 5.1 %collective-permute-start.11 = (bf16[8,16,1024]{2,1,0:T(8,128)(2,1)S(1)}, bf16[8,16,1024]{2,1,0:T(8,128)(2,1)}, u32[]{:S(2)}, u32[]{:S(2)}) collective-permute-start(bf16[8,16,1024]{2,1,0:T(8,128)(2,1)S(1)} %copy-done.21), channel_id=1, source_target_pairs={{0,2},{1,11},{2,0},{3,9},{4,6},{5,15},{6,4},{7,13},{8,10},{9,3},{1... | collective-permute-start | bytes 786440 | tf_op jit(solution)/shard_map/ppermute | solution.py:416
  75.1 4.3 %collective-permute-start.12 = (bf16[8,16,1024]{2,1,0:T(8,128)(2,1)S(1)}, bf16[8,16,1024]{2,1,0:T(8,128)(2,1)}, u32[]{:S(2)}, u32[]{:S(2)}) collective-permute-start(bf16[8,16,1024]{2,1,0:T(8,128)(2,1)S(1)} %copy-done.19), channel_id=1, source_target_pairs={{0,14},{1,7},{2,12},{3,5},{4,10},{5,3},{6,8},{7,1},{8,6},{9,15},{1... | collective-permute-start | bytes 786440 | tf_op jit(solution)/shard_map/ppermute | solution.py:416
  79.5 13.1 %collective-permute-start.13 = (bf16[8,16,1024]{2,1,0:T(8,128)(2,1)S(1)}, bf16[8,16,1024]{2,1,0:T(8,128)(2,1)}, u32[]{:S(2)}, u32[]{:S(2)}) collective-permute-start(bf16[8,16,1024]{2,1,0:T(8,128)(2,1)S(1)} %copy-done.17), channel_id=1, source_target_pairs={{0,6},{1,15},{2,4},{3,13},{4,2},{5,11},{6,0},{7,9},{8,14},{9,7},{1... | collective-permute-start | bytes 786440 | tf_op jit(solution)/shard_map/ppermute | solution.py:416
  92.6 11.4 %collective-permute-start.15 = (bf16[8,16,1024]{2,1,0:T(8,128)(2,1)S(1)}, bf16[8,16,1024]{2,1,0:T(8,128)(2,1)}, u32[]{:S(2)}, u32[]{:S(2)}) collective-permute-start(bf16[8,16,1024]{2,1,0:T(8,128)(2,1)S(1)} %copy-done.15), channel_id=1, source_target_pairs={{0,3},{1,10},{2,9},{3,0},{4,7},{5,14},{6,13},{7,4},{8,11},{9,2},{1... | collective-permute-start | bytes 786440 | tf_op jit(solution)/shard_map/ppermute | solution.py:416
  104.8 19.5 %shard_map.73 = (f32[5,4,128,384]{3,2,1,0:T(8,128)}, f32[5,8,384]{2,1,0:T(8,128)}) custom-call(s32[48]{0:T(128)} %get-tuple-element.107.place, s32[48]{0:T(128)} %copy-done.12, s32[5]{0:T(128)} %fusion.9.tiles, s32[5,1,128]{2,1,0:T(1,128)} %tile.9.rest_0_, s32[1,160]{1,0:T(1,128)} %rest_1_.5, bf16[160,6144]{1,0:T(8,128)(2,1)} %bitcast.67, ...), custom_call_target="tpu_custom_call" | custom-call | flops 4831838208 | bytes 7995392 | tf_op jit(solution)/shard_map/pallas_call | solution.py:323
  124.4 5.9 %collective-permute-start.17 = (bf16[8,16,1024]{2,1,0:T(8,128)(2,1)S(1)}, bf16[8,16,1024]{2,1,0:T(8,128)(2,1)S(1)}, u32[]{:S(2)}, u32[]{:S(2)}) collective-permute-start(bf16[8,16,1024]{2,1,0:T(8,128)(2,1)S(1)} %copy-done.13), channel_id=1, source_target_pairs={{0,7},{1,14},{2,13},{3,4},{4,3},{5,10},{6,9},{7,0},{8,15},{9,6},{1... | collective-permute-start | bytes 786440 | tf_op jit(solution)/shard_map/ppermute | solution.py:416
  130.3 13.1 %shard_map.74 = (f32[5,4,128,384]{3,2,1,0:T(8,128)}, f32[5,8,384]{2,1,0:T(8,128)}) custom-call(s32[32]{0:T(128)} %get-tuple-element.111.place, s32[32]{0:T(128)} %copy-done.8, s32[5]{0:T(128)} %and_select_fusion.1.tiles, s32[5,1,128]{2,1,0:T(1,128)} %tile.9.rest_0_, s32[1,160]{1,0:T(1,128)} %rest_1_.5, bf16[160,6144]{1,0:T(8,128)(2,1)} %bitcast.68, ...), custom_call_target="tpu_custom_call" | custom-call | flops 2415919104 | bytes 6946816 | tf_op jit(solution)/shard_map/pallas_call | solution.py:323
  143.5 13.1 %shard_map.75 = (f32[5,4,128,384]{3,2,1,0:T(8,128)}, f32[5,8,384]{2,1,0:T(8,128)}) custom-call(s32[32]{0:T(128)} %get-tuple-element.113.place, s32[32]{0:T(128)} %copy-done.7, s32[5]{0:T(128)} %and_select_fusion.2.tiles, s32[5,1,128]{2,1,0:T(1,128)} %tile.9.rest_0_, s32[1,160]{1,0:T(1,128)} %rest_1_.5, bf16[160,6144]{1,0:T(8,128)(2,1)} %bitcast.69, ...), custom_call_target="tpu_custom_call" | custom-call | flops 2415919104 | bytes 6946816 | tf_op jit(solution)/shard_map/pallas_call | solution.py:323
  157.4 10.7 %shard_map.76 = bf16[160,6144]{1,0:T(8,128)(2,1)} custom-call(s32[16]{0:T(128)} %get-tuple-element.115.place, s32[16]{0:T(128)} %copy-done.6, s32[5]{0:T(128)} %and_select_fusion.3.tiles, s32[5,1,128]{2,1,0:T(1,128)} %tile.9.rest_0_, s32[1,160]{1,0:T(1,128)} %rest_1_.5, bf16[160,6144]{1,0:T(8,128)(2,1)} %bitcast.70, ...), custom_call_target="tpu_custom_call" | custom-call | flops 1207959552 | bytes 6422528 | tf_op jit(solution)/shard_map/pallas_call | solution.py:323
  (107 shorter events, 16.4 us)
Async XLA Ops:
  2.3 4.3 %collective-permute-start = (s32[1,2,128]{2,1,0:T(2,128)}, s32[1,2,128]{2,1,0:T(2,128)S(1)}, u32[]{:S(2)}, u32[]{:S(2)}) collective-permute-start(s32[1,2,128]{2,1,0:T(2,128)} %get-tuple-element.54), channel_id=1, source_target_pairs={{0,8},{1,9},{2,10},{3,11},{4,12},{5,13},{6,14},{7,15},{8,0},{9,1},... | collective-permute-start | bytes 3080 | tf_op jit(solution)/shard_map/ppermute | solution.py:416
  5.4 4.4 %collective-permute-start.1 = (s32[1,2,128]{2,1,0:T(2,128)}, s32[1,2,128]{2,1,0:T(2,128)S(1)}, u32[]{:S(2)}, u32[]{:S(2)}) collective-permute-start(s32[1,2,128]{2,1,0:T(2,128)} %get-tuple-element.55), channel_id=1, source_target_pairs={{0,12},{1,13},{2,14},{3,15},{4,8},{5,9},{6,10},{7,11},{8,4},{9,5},... | collective-permute-start | bytes 3080 | tf_op jit(solution)/shard_map/ppermute | solution.py:416
  12.9 3.0 %collective-permute-start.2 = (s32[1,2,128]{2,1,0:T(2,128)S(1)}, s32[1,2,128]{2,1,0:T(2,128)S(1)}, u32[]{:S(2)}, u32[]{:S(2)}) collective-permute-start(s32[1,2,128]{2,1,0:T(2,128)S(1)} %copy-done.26), channel_id=1, source_target_pairs={{0,1},{1,0},{2,3},{3,2},{4,5},{5,4},{6,7},{7,6},{8,9},{9,8},{10,11... | collective-permute-start | bytes 3080 | tf_op jit(solution)/shard_map/ppermute | solution.py:416
  15.9 9.8 %all-to-all-start = ((s32[16,2,128]{2,1,0:T(2,128)}), s32[16,2,128]{2,1,0:T(2,128)S(1)}, u32[]{:S(2)}, u32[]{:S(2)}) async-start(s32[16,2,128]{2,1,0:T(2,128)} %get-tuple-element.61), calls=%async_computation | async-start | bytes 32768 | tf_op jit(solution)/shard_map/all_to_all | solution.py:419
  19.8 27.2 %collective-permute-start.3 = (bf16[8,16,1024]{2,1,0:T(8,128)(2,1)}, bf16[8,16,1024]{2,1,0:T(8,128)(2,1)S(1)}, u32[]{:S(2)}, u32[]{:S(2)}) collective-permute-start(bf16[8,16,1024]{2,1,0:T(8,128)(2,1)} %get-tuple-element.84), channel_id=1, source_target_pairs={{0,8},{1,9},{2,10},{3,11},{4,12},{5,13},{6,14},{7,15},{8,0},{9,1},... | collective-permute-start | bytes 786440 | tf_op jit(solution)/shard_map/ppermute | solution.py:416
  22.1 26.1 %collective-permute-start.4 = (bf16[8,16,1024]{2,1,0:T(8,128)(2,1)}, bf16[8,16,1024]{2,1,0:T(8,128)(2,1)S(1)}, u32[]{:S(2)}, u32[]{:S(2)}) collective-permute-start(bf16[8,16,1024]{2,1,0:T(8,128)(2,1)} %get-tuple-element.85), channel_id=1, source_target_pairs={{0,12},{1,13},{2,14},{3,15},{4,8},{5,9},{6,10},{7,11},{8,4},{9,5},... | collective-permute-start | bytes 786440 | tf_op jit(solution)/shard_map/ppermute | solution.py:416
  33.1 28.0 %all-to-all-start.1 = ((bf16[16,16,1024]{2,1,0:T(8,128)(2,1)}), bf16[16,16,1024]{2,1,0:T(8,128)(2,1)S(1)}, u32[]{:S(2)}, u32[]{:S(2)}) async-start(bf16[16,16,1024]{2,1,0:T(8,128)(2,1)} %shard_map.71), calls=%async_computation.1 | async-start | bytes 1048576 | tf_op jit(solution)/shard_map/all_to_all | solution.py:419
  38.5 19.3 %collective-permute-start.5 = (bf16[8,16,1024]{2,1,0:T(8,128)(2,1)}, bf16[8,16,1024]{2,1,0:T(8,128)(2,1)S(1)}, u32[]{:S(2)}, u32[]{:S(2)}) collective-permute-start(bf16[8,16,1024]{2,1,0:T(8,128)(2,1)} %get-tuple-element.86), channel_id=1, source_target_pairs={{0,1},{1,0},{2,3},{3,2},{4,5},{5,4},{6,7},{7,6},{8,9},{9,8},{10,11... | collective-permute-start | bytes 786440 | tf_op jit(solution)/shard_map/ppermute | solution.py:416
  38.7 31.3 %collective-permute-start.6 = (bf16[8,16,1024]{2,1,0:T(8,128)(2,1)}, bf16[8,16,1024]{2,1,0:T(8,128)(2,1)S(1)}, u32[]{:S(2)}, u32[]{:S(2)}) collective-permute-start(bf16[8,16,1024]{2,1,0:T(8,128)(2,1)} %get-tuple-element.87), channel_id=1, source_target_pairs={{0,13},{1,4},{2,15},{3,6},{4,1},{5,8},{6,3},{7,10},{8,5},{9,12},{1... | collective-permute-start | bytes 786440 | tf_op jit(solution)/shard_map/ppermute | solution.py:416
  40.3 34.8 %collective-permute-start.7 = (bf16[8,16,1024]{2,1,0:T(8,128)(2,1)}, bf16[8,16,1024]{2,1,0:T(8,128)(2,1)S(1)}, u32[]{:S(2)}, u32[]{:S(2)}) collective-permute-start(bf16[8,16,1024]{2,1,0:T(8,128)(2,1)} %get-tuple-element.88), channel_id=1, source_target_pairs={{0,5},{1,12},{2,7},{3,14},{4,9},{5,0},{6,11},{7,2},{8,13},{9,4},{1... | collective-permute-start | bytes 786440 | tf_op jit(solution)/shard_map/ppermute | solution.py:416
  47.0 57.7 %copy-start.18 = (bf16[8,16,1024]{2,1,0:T(8,128)(2,1)}, bf16[8,16,1024]{2,1,0:T(8,128)(2,1)S(1)}, u32[]{:S(2)}) copy-start(bf16[8,16,1024]{2,1,0:T(8,128)(2,1)S(1)} %collective-permute-done.3.rest_6_) | copy-start | bytes 786436
  47.0 32.5 %collective-permute-start.8 = (bf16[8,16,1024]{2,1,0:T(8,128)(2,1)}, bf16[8,16,1024]{2,1,0:T(8,128)(2,1)S(1)}, u32[]{:S(2)}, u32[]{:S(2)}) collective-permute-start(bf16[8,16,1024]{2,1,0:T(8,128)(2,1)} %get-tuple-element.91), channel_id=1, source_target_pairs={{0,9},{1,5},{2,11},{3,7},{4,13},{5,1},{6,15},{7,3},{8,12},{9,0},{1... | collective-permute-start | bytes 786440 | tf_op jit(solution)/shard_map/ppermute | solution.py:416
  48.2 56.5 %copy-start.20 = (bf16[8,16,1024]{2,1,0:T(8,128)(2,1)}, bf16[8,16,1024]{2,1,0:T(8,128)(2,1)S(1)}, u32[]{:S(2)}) copy-start(bf16[8,16,1024]{2,1,0:T(8,128)(2,1)S(1)} %collective-permute-done.4.rest_7_) | copy-start | bytes 786436
  48.2 44.3 %collective-permute-start.9 = (bf16[8,16,1024]{2,1,0:T(8,128)(2,1)}, bf16[8,16,1024]{2,1,0:T(8,128)(2,1)}, u32[]{:S(2)}, u32[]{:S(2)}) collective-permute-start(bf16[8,16,1024]{2,1,0:T(8,128)(2,1)} %get-tuple-element.92), channel_id=1, source_target_pairs={{0,4},{1,8},{2,6},{3,10},{4,0},{5,12},{6,2},{7,14},{8,1},{9,13},{1... | collective-permute-start | bytes 786440 | tf_op jit(solution)/shard_map/ppermute | solution.py:416
  57.8 46.9 %copy-start.22 = (bf16[8,16,1024]{2,1,0:T(8,128)(2,1)}, bf16[8,16,1024]{2,1,0:T(8,128)(2,1)S(1)}, u32[]{:S(2)}) copy-start(bf16[8,16,1024]{2,1,0:T(8,128)(2,1)S(1)} %collective-permute-done.5.rest_8_) | copy-start | bytes 786436
  57.8 34.8 %collective-permute-start.10 = (bf16[8,16,1024]{2,1,0:T(8,128)(2,1)}, bf16[8,16,1024]{2,1,0:T(8,128)(2,1)}, u32[]{:S(2)}, u32[]{:S(2)}) collective-permute-start(bf16[8,16,1024]{2,1,0:T(8,128)(2,1)} %get-tuple-element.93), channel_id=1, source_target_pairs={{0,10},{1,3},{2,8},{3,1},{4,14},{5,7},{6,12},{7,5},{8,2},{9,11},{1... | collective-permute-start | bytes 786440 | tf_op jit(solution)/shard_map/ppermute | solution.py:416
  70.0 54.3 %collective-permute-start.11 = (bf16[8,16,1024]{2,1,0:T(8,128)(2,1)S(1)}, bf16[8,16,1024]{2,1,0:T(8,128)(2,1)}, u32[]{:S(2)}, u32[]{:S(2)}) collective-permute-start(bf16[8,16,1024]{2,1,0:T(8,128)(2,1)S(1)} %copy-done.21), channel_id=1, source_target_pairs={{0,2},{1,11},{2,0},{3,9},{4,6},{5,15},{6,4},{7,13},{8,10},{9,3},{1... | collective-permute-start | bytes 786440 | tf_op jit(solution)/shard_map/ppermute | solution.py:416
  75.1 49.2 %collective-permute-start.12 = (bf16[8,16,1024]{2,1,0:T(8,128)(2,1)S(1)}, bf16[8,16,1024]{2,1,0:T(8,128)(2,1)}, u32[]{:S(2)}, u32[]{:S(2)}) collective-permute-start(bf16[8,16,1024]{2,1,0:T(8,128)(2,1)S(1)} %copy-done.19), channel_id=1, source_target_pairs={{0,14},{1,7},{2,12},{3,5},{4,10},{5,3},{6,8},{7,1},{8,6},{9,15},{1... | collective-permute-start | bytes 786440 | tf_op jit(solution)/shard_map/ppermute | solution.py:416
  79.5 44.8 %copy-start.25 = (bf16[8,16,1024]{2,1,0:T(8,128)(2,1)}, bf16[8,16,1024]{2,1,0:T(8,128)(2,1)S(1)}, u32[]{:S(2)}) copy-start(bf16[8,16,1024]{2,1,0:T(8,128)(2,1)S(1)} %collective-permute-done.8.rest_5_) | copy-start | bytes 786436
  79.5 63.9 %collective-permute-start.13 = (bf16[8,16,1024]{2,1,0:T(8,128)(2,1)S(1)}, bf16[8,16,1024]{2,1,0:T(8,128)(2,1)}, u32[]{:S(2)}, u32[]{:S(2)}) collective-permute-start(bf16[8,16,1024]{2,1,0:T(8,128)(2,1)S(1)} %copy-done.17), channel_id=1, source_target_pairs={{0,6},{1,15},{2,4},{3,13},{4,2},{5,11},{6,0},{7,9},{8,14},{9,7},{1... | collective-permute-start | bytes 786440 | tf_op jit(solution)/shard_map/ppermute | solution.py:416
  92.6 50.9 %collective-permute-start.14 = (bf16[8,16,1024]{2,1,0:T(8,128)(2,1)S(1)}, bf16[8,16,1024]{2,1,0:T(8,128)(2,1)}, u32[]{:S(2)}, u32[]{:S(2)}) collective-permute-start(bf16[8,16,1024]{2,1,0:T(8,128)(2,1)S(1)} %copy-done.16), channel_id=1, source_target_pairs={{0,11},{1,2},{2,1},{3,8},{4,15},{5,6},{6,5},{7,12},{8,3},{9,10},{1... | collective-permute-start | bytes 786440 | tf_op jit(solution)/shard_map/ppermute | solution.py:416
  92.6 50.9 %collective-permute-start.15 = (bf16[8,16,1024]{2,1,0:T(8,128)(2,1)S(1)}, bf16[8,16,1024]{2,1,0:T(8,128)(2,1)}, u32[]{:S(2)}, u32[]{:S(2)}) collective-permute-start(bf16[8,16,1024]{2,1,0:T(8,128)(2,1)S(1)} %copy-done.15), channel_id=1, source_target_pairs={{0,3},{1,10},{2,9},{3,0},{4,7},{5,14},{6,13},{7,4},{8,11},{9,2},{1... | collective-permute-start | bytes 786440 | tf_op jit(solution)/shard_map/ppermute | solution.py:416
  124.3 32.3 %collective-permute-start.16 = (bf16[8,16,1024]{2,1,0:T(8,128)(2,1)S(1)}, bf16[8,16,1024]{2,1,0:T(8,128)(2,1)S(1)}, u32[]{:S(2)}, u32[]{:S(2)}) collective-permute-start(bf16[8,16,1024]{2,1,0:T(8,128)(2,1)S(1)} %copy-done.14), channel_id=1, source_target_pairs={{0,15},{1,6},{2,5},{3,12},{4,11},{5,2},{6,1},{7,8},{8,7},{9,14},{1... | collective-permute-start | bytes 786440 | tf_op jit(solution)/shard_map/ppermute | solution.py:416
  124.4 32.2 %collective-permute-start.17 = (bf16[8,16,1024]{2,1,0:T(8,128)(2,1)S(1)}, bf16[8,16,1024]{2,1,0:T(8,128)(2,1)S(1)}, u32[]{:S(2)}, u32[]{:S(2)}) collective-permute-start(bf16[8,16,1024]{2,1,0:T(8,128)(2,1)S(1)} %copy-done.13), channel_id=1, source_target_pairs={{0,7},{1,14},{2,13},{3,4},{4,3},{5,10},{6,9},{7,0},{8,15},{9,6},{1... | collective-permute-start | bytes 786440 | tf_op jit(solution)/shard_map/ppermute | solution.py:416
  (23 other events, 391.3 us)

commit v8 on v5

--- a/solution.py
+++ b/solution.py
@@ -222,9 +222,11 @@
         lax.fori_loop(0, pages // TILE_PAGES, turn, 0)
 
     for g in range(KEY_VALUE_HEADS):
-        for i in range(QUERY_GROUP):
-            head = g * QUERY_GROUP + i
-            query[g, i * block : (i + 1) * block, :] = query_ref[:, head * LANES : (head + 1) * LANES]
+        heads = [
+            query_ref[:, (g * QUERY_GROUP + i) * LANES : (g * QUERY_GROUP + i + 1) * LANES]
+            for i in range(QUERY_GROUP)
+        ]
+        query[g] = nt_dot(eye, jnp.concatenate(heads, axis=0)).astype(bf16)
     if first:
         mixed[...] = jnp.zeros(mixed.shape, f32)
         stats[0:KEY_VALUE_HEADS, :] = jnp.full((KEY_VALUE_HEADS, lanes), HIDDEN, f32)
@@ -243,7 +245,7 @@
 
         def score(g):
             key = kv[here, :, g * LANES : (g + 1) * LANES].reshape(tile, LANES)
-            return nt_dot(key, query[g])
+            return jnp.dot(key, query[g], preferred_element_type=f32)
 
         upcoming = score(0)
         for g in range(KEY_VALUE_HEADS):
@@ -328,7 +330,7 @@
                     (pages // TILE_PAGES, KEY_VALUE_HEADS, LANES, TILE_PAGES * page_len), jnp.bfloat16
                 ),
                 pltpu.VMEM((pages * page_len, LANES), jnp.int32),
-                pltpu.VMEM((KEY_VALUE_HEADS, lanes, LANES), jnp.bfloat16),
+                pltpu.VMEM((KEY_VALUE_HEADS, LANES, lanes), jnp.bfloat16),
                 pltpu.VMEM((KEY_VALUE_HEADS, LANES, lanes), jnp.float32),
                 pltpu.VMEM((2 * KEY_VALUE_HEADS, lanes), jnp.float32),
                 pltpu.SemaphoreType.DMA,
@@ -392,8 +394,8 @@
     wide = pltpu.VMEM((8, -(-picked // LANES) * LANES), jnp.int32)
     if holders == 16:
         first = (8, 12)
-        groups = [(0, 8, 12, 4, 5, 1), (9, 6, 13, 7, 10, 2, 14, 3), (11, 15)]
-        others = [d for group in groups for d in group if d not in first]
+        groups = [(0, 8, 12, 4, 5, 1), (9, 13, 6, 10, 7, 2, 14, 3), (11, 15)]
+        others = (0, 9, 4, 13, 5, 1, 6, 10, 7, 2, 14, 3, 11, 15)
     else:
         first = ()
         groups = [None]
@@ -439,13 +441,14 @@
             out_shape=[jax.ShapeDtypeStruct((capacity, page_len, width), store.dtype)] * len(first),
             compiler_params=params,
         )(*lists, store)
-        parts, index, table, positions = lax.optimization_barrier(
-            (parts, index, page_table, sel_pos)
-        )
+        parts, table, positions = lax.optimization_barrier((parts, page_table, sel_pos))
         arrived = {d: swap(part, d) for d, part in zip(first, parts)}
+        lists = lax.all_gather(index, "store", axis=0)
+        index_in = lax.dynamic_index_in_dim(lists, own, axis=1, keepdims=False)
+        index_in, _ = lax.optimization_barrier((index_in, arrived[first[0]]))
     else:
         table, positions = page_table, sel_pos
-    index_in = exchange(index)
+        index_in = exchange(index)
 
     packed = pl.pallas_call(
         functools.partial(rows_kernel, hold, page_len),
@@ -453,6 +456,7 @@
         scratch_shapes=[wide],
         compiler_params=params,
     )(table, positions, fresh)
+    rows_in = exchange(packed)
 
     each = jax.ShapeDtypeStruct((capacity, page_len, width), store.dtype)
     whole = jax.ShapeDtypeStruct((holders, capacity, page_len, width), store.dtype)
@@ -468,14 +472,13 @@
         out_shape=[each] * len(others) if others else [whole],
         compiler_params=params,
     )(own_word, index_in, store)
-    parts, packed, table, positions = lax.optimization_barrier((parts, packed, table, positions))
+    parts, table, positions = lax.optimization_barrier((parts, table, positions))
     if others:
         for d, part in zip(others, parts):
             arrived[d] = swap(part, d) if d else part
         contexts = [[arrived[d] for d in group] for group in groups]
     else:
         contexts = [[exchange(parts[0]).reshape(pages, page_len, width)]]
-    rows_in = exchange(packed)
 
     store_out = pl.pallas_call(
         write_back_kernel,

time: 139 us -> 152 us (1.094)
  blocking collectives: 0 us -> 24.4 us
  starting transfers between devices: 37.7 us -> 29.9 us
  waiting for transfers between devices: 19.5 us -> 13.5 us
  Pallas kernels: 69.3 us -> 71.7 us
    all_gather x0 -> x1, blocking collectives: none -> 24.4 us  [per_device(): lists = lax.all_gather(index, 'store', axis=0)]
    all_to_all x2 -> x1, starting transfers between devices: 13.8 us -> 4.94 us  [exchange(): return lax.all_to_all(x, 'store', split_axis=0, concat_axis=0, tiled=True)]
    ppermute x17, waiting for transfers between devices: 18.9 us -> 13.4 us  [swap(): return lax.ppermute(x, 'store', [(h, h ^ d) for h in range(holders)])]
    pallas_call x3, Pallas kernels: 49.9 us -> 52.2 us  [attend(): pl.pallas_call(functools.partial(attend_kernel, first, last, len(contexts...]
  transfers between devices with their start and end apart: 19 -> 18, of which waited for: 8 -> 4; matrix products, arithmetic and copies ran while one was open for 5% -> 5% of each run, Pallas kernels for 40% -> 37%
where the time goes in v8:
time: 152 us; the launch traced here: 150 us
  Pallas kernels  71.7 us (47%)
  starting transfers between devices  29.9 us (20%)
  blocking collectives  24.4 us (16%)
  waiting for transfers between devices  13.5 us (9%)
  other arithmetic  5.17 us (3%)
  local copies, waits for them, and re-layouts  4.93 us (3%)
    pallas_call x3, Pallas kernels, attend(): pl.pallas_call(functools.partial(attend_kernel, first, last, len(contexts...  52.2 us
    ppermute x17, starting transfers between devices, swap(): return lax.ppermute(x, 'store', [(h, h ^ d) for h in range(holders)])  24.9 us
    all_gather x1, blocking collectives, per_device(): lists = lax.all_gather(index, 'store', axis=0)  24.4 us
    ppermute x17, waiting for transfers between devices, swap(): return lax.ppermute(x, 'store', [(h, h ^ d) for h in range(holders)])  13.4 us
    pallas_call x1, Pallas kernels, per_device(): pl.pallas_call(write_back_kernel, grid_spec=pltpu.PrefetchScalarGridSpec(...  8.02 us
    all_to_all x1, starting transfers between devices, exchange(): return lax.all_to_all(x, 'store', split_axis=0, concat_axis=0, tiled=True)  4.94 us
    pallas_call x1, Pallas kernels, per_device(): pl.pallas_call(functools.partial(gather_kernel, capacity, others), grid_s...  4.92 us
  transfers between devices with their start and end apart: 18, of which 4 were waited for; matrix products, arithmetic and copies ran while one was open for 5% of the time, Pallas kernels for 37%

profile of v8, /device:TPU:9, one launch (start us, length us, event | category | flops | bytes accessed | tf_op | source)
XLA Modules:
  0.0 150.4 jit_solution(16153097821794445325)
XLA Ops:
  0.6 1.7 %shard_map.68 = (s32[16,2,128]{2,1,0:T(2,128)}, s32[1,2,128]{2,1,0:T(2,128)}, s32[1,2,128]{2,1,0:T(2,128)}) custom-call(s32[1]{0:T(128)} %bitcast.own, s32[1,128]{1,0:T(1,128)} %table_ref.2, s32[1,160]{1,0:T(1,128)} %rest_1_.2), custom_call_target="tpu_custom_call" | custom-call | tf_op jit(solution)/shard_map/pallas_call | solution.py:410
  2.3 2.3 %collective-permute-start = (s32[1,2,128]{2,1,0:T(2,128)}, s32[1,2,128]{2,1,0:T(2,128)S(1)}, u32[]{:S(2)}, u32[]{:S(2)}) collective-permute-start(s32[1,2,128]{2,1,0:T(2,128)} %get-tuple-element.49), channel_id=1, source_target_pairs={{0,8},{1,9},{2,10},{3,11},{4,12},{5,13},{6,14},{7,15},{8,0},{9,1},... | collective-permute-start | bytes 3080 | tf_op jit(solution)/shard_map/ppermute | solution.py:405
  4.6 1.2 collective-permute-done.refs_0_
  5.8 1.4 collective-permute-done.1.refs_1_
  7.8 2.5 %shard_map.69 = (bf16[8,16,1024]{2,1,0:T(8,128)(2,1)}, bf16[8,16,1024]{2,1,0:T(8,128)(2,1)}) custom-call(s32[1,2,128]{2,1,0:T(2,128)} %copy-done.7, s32[1,2,128]{2,1,0:T(2,128)} %copy-done.8, bf16[128,16,1024]{2,1,0:T(8,128)(2,1)} %store_hbm.3), custom_call_target="tpu_custom_call" | custom-call | tf_op jit(solution)/shard_map/pallas_call | solution.py:428
  10.4 1.8 %collective-permute-start.2 = (bf16[8,16,1024]{2,1,0:T(8,128)(2,1)}, bf16[8,16,1024]{2,1,0:T(8,128)(2,1)S(1)}, u32[]{:S(2)}, u32[]{:S(2)}) collective-permute-start(bf16[8,16,1024]{2,1,0:T(8,128)(2,1)} %get-tuple-element.53), channel_id=1, source_target_pairs={{0,8},{1,9},{2,10},{3,11},{4,12},{5,13},{6,14},{7,15},{8,0},{9,1},... | collective-permute-start | bytes 786440 | tf_op jit(solution)/shard_map/ppermute | solution.py:405
  12.1 24.4 %all-gather = s32[256,2,128]{2,1,0:T(2,128)S(1)} all-gather(s32[16,2,128]{2,1,0:T(2,128)S(1)} %copy-done.4), channel_id=2, replica_groups=mesh['groups'=2,'store'=16] {'store'}, dimensions={0}, use_global_device_ids=true | all-gather | bytes 278528 | tf_op jit(solution)/shard_map/all_gather | solution.py:446
  38.3 2.4 %shard_map.71 = bf16[16,16,1024]{2,1,0:T(8,128)(2,1)} custom-call(s32[1,128]{1,0:T(1,128)} %table_ref.2, s32[1,160]{1,0:T(1,128)} %rest_1_.2, bf16[160,1024]{1,0:T(8,128)(2,1)} %bitcast.75), custom_call_target="tpu_custom_call" | custom-call | tf_op jit(solution)/shard_map/pallas_call | solution.py:453
  40.6 4.9 %all-to-all-start = ((bf16[16,16,1024]{2,1,0:T(8,128)(2,1)}), bf16[16,16,1024]{2,1,0:T(8,128)(2,1)S(1)}, u32[]{:S(2)}, u32[]{:S(2)}) async-start(bf16[16,16,1024]{2,1,0:T(8,128)(2,1)} %shard_map.71), calls=%async_computation | async-start | bytes 1048576 | tf_op jit(solution)/shard_map/all_to_all | solution.py:408
  45.6 4.9 %shard_map.70 = (bf16[8,16,1024]{2,1,0:T(8,128)(2,1)}, bf16[8,16,1024]{2,1,0:T(8,128)(2,1)}, bf16[8,16,1024]{2,1,0:T(8,128)(2,1)}, bf16[8,16,1024]{2,1,0:T(8,128...) custom-call(s32[1]{0:T(128)} %bitcast.own, ...), custom_call_target="tpu_custom_call" | custom-call | tf_op jit(solution)/shard_map/pallas_call | solution.py:463
  52.4 1.9 %collective-permute-start.5 = (bf16[8,16,1024]{2,1,0:T(8,128)(2,1)}, bf16[8,16,1024]{2,1,0:T(8,128)(2,1)S(1)}, u32[]{:S(2)}, u32[]{:S(2)}) collective-permute-start(bf16[8,16,1024]{2,1,0:T(8,128)(2,1)} %get-tuple-element.77), channel_id=1, source_target_pairs={{0,5},{1,4},{2,7},{3,6},{4,1},{5,0},{6,3},{7,2},{8,13},{9,12},{10,... | collective-permute-start | bytes 786440 | tf_op jit(solution)/shard_map/ppermute | solution.py:405
  54.3 2.5 %collective-permute-start.7 = (bf16[8,16,1024]{2,1,0:T(8,128)(2,1)}, bf16[8,16,1024]{2,1,0:T(8,128)(2,1)S(1)}, u32[]{:S(2)}, u32[]{:S(2)}) collective-permute-start(bf16[8,16,1024]{2,1,0:T(8,128)(2,1)} %get-tuple-element.81), channel_id=1, source_target_pairs={{0,9},{1,8},{2,11},{3,10},{4,13},{5,12},{6,15},{7,14},{8,1},{9,0},... | collective-permute-start | bytes 786440 | tf_op jit(solution)/shard_map/ppermute | solution.py:405
  60.4 7.3 %collective-permute-done.4.rest_8_ = bf16[8,16,1024]{2,1,0:T(8,128)(2,1)S(1)} collective-permute-done((bf16[8,16,1024]{2,1,0:T(8,128)(2,1)}, bf16[8,16,1024]{2,1,0:T(8,128)(2,1)S(1)}, u32[]{:S(2)}, u32[]{:S(2)}) %collective-permute-start.4) | collective-permute-done | bytes 262176 | tf_op jit(solution)/shard_map/ppermute | solution.py:405
  67.7 2.7 %collective-permute-start.9 = (bf16[8,16,1024]{2,1,0:T(8,128)(2,1)}, bf16[8,16,1024]{2,1,0:T(8,128)(2,1)}, u32[]{:S(2)}, u32[]{:S(2)}) collective-permute-start(bf16[8,16,1024]{2,1,0:T(8,128)(2,1)} %get-tuple-element.83), channel_id=1, source_target_pairs={{0,6},{1,7},{2,4},{3,5},{4,2},{5,3},{6,0},{7,1},{8,14},{9,15},{10,... | collective-permute-start | bytes 786440 | tf_op jit(solution)/shard_map/ppermute | solution.py:405
  72.7 8.0 %shard_map.72 = bf16[128,16,1024]{2,1,0:T(8,128)(2,1)} custom-call(s32[16,2,128]{2,1,0:T(2,128)} %dynamic-slice_bitcast_fusion.index.targets_ref, s32[16,2,128]{2,1,0:T(2,128)} %dynamic-slice_bitcast_fusion.index.targets_ref, bf16[128,16,1024]{2,1,0:T(8,128)(2,1)} %store_hbm.3, bf16[16,16,1024]{2,1,0:T(8,128)(2,1)} %copy-done), custom_call_target="tpu_custom_call" | custom-call | bytes 8388608 | tf_op jit(solution)/shard_map/pallas_call | solution.py:483
  80.8 3.7 %collective-permute-start.10 = (bf16[8,16,1024]{2,1,0:T(8,128)(2,1)S(1)}, bf16[8,16,1024]{2,1,0:T(8,128)(2,1)S(1)}, u32[]{:S(2)}, u32[]{:S(2)}) collective-permute-start(bf16[8,16,1024]{2,1,0:T(8,128)(2,1)S(1)} %copy-done.19), channel_id=1, source_target_pairs={{0,10},{1,11},{2,8},{3,9},{4,14},{5,15},{6,12},{7,13},{8,2},{9,3},... | collective-permute-start | bytes 786440 | tf_op jit(solution)/shard_map/ppermute | solution.py:405
  84.5 1.8 %collective-permute-start.11 = (bf16[8,16,1024]{2,1,0:T(8,128)(2,1)S(1)}, bf16[8,16,1024]{2,1,0:T(8,128)(2,1)}, u32[]{:S(2)}, u32[]{:S(2)}) collective-permute-start(bf16[8,16,1024]{2,1,0:T(8,128)(2,1)S(1)} %copy-done.18), channel_id=1, source_target_pairs={{0,7},{1,6},{2,5},{3,4},{4,3},{5,2},{6,1},{7,0},{8,15},{9,14},{10,... | collective-permute-start | bytes 786440 | tf_op jit(solution)/shard_map/ppermute | solution.py:405
  86.4 1.4 collective-permute-start.13
  89.4 21.1 %shard_map.73 = (f32[5,4,128,384]{3,2,1,0:T(8,128)}, f32[5,8,384]{2,1,0:T(8,128)}) custom-call(s32[48]{0:T(128)} %get-tuple-element.95.place, s32[48]{0:T(128)} %copy-done.10, s32[5]{0:T(128)} %fusion.7.tiles, s32[5,1,128]{2,1,0:T(1,128)} %tile.9.rest_0_, s32[1,160]{1,0:T(1,128)} %rest_1_.2, bf16[160,6144]{1,0:T(8,128)(2,1)} %bitcast.71, ...), custom_call_target="tpu_custom_call" | custom-call | flops 4831838208 | bytes 7995392 | tf_op jit(solution)/shard_map/pallas_call | solution.py:313
  110.6 2.4 %collective-permute-start.15 = (bf16[8,16,1024]{2,1,0:T(8,128)(2,1)S(1)}, bf16[8,16,1024]{2,1,0:T(8,128)(2,1)S(1)}, u32[]{:S(2)}, u32[]{:S(2)}) collective-permute-start(bf16[8,16,1024]{2,1,0:T(8,128)(2,1)S(1)} %copy-done.12), channel_id=1, source_target_pairs={{0,11},{1,10},{2,9},{3,8},{4,15},{5,14},{6,13},{7,12},{8,3},{9,2},... | collective-permute-start | bytes 786440 | tf_op jit(solution)/shard_map/ppermute | solution.py:405
  113.1 2.1 %collective-permute-start.16 = (bf16[8,16,1024]{2,1,0:T(8,128)(2,1)S(1)}, bf16[8,16,1024]{2,1,0:T(8,128)(2,1)S(1)}, u32[]{:S(2)}, u32[]{:S(2)}) collective-permute-start(bf16[8,16,1024]{2,1,0:T(8,128)(2,1)S(1)} %copy-done.11), channel_id=1, source_target_pairs={{0,15},{1,14},{2,13},{3,12},{4,11},{5,10},{6,9},{7,8},{8,7},{9,6},... | collective-permute-start | bytes 786440 | tf_op jit(solution)/shard_map/ppermute | solution.py:405
  115.2 19.6 %shard_map.74 = (f32[5,4,128,384]{3,2,1,0:T(8,128)}, f32[5,8,384]{2,1,0:T(8,128)}) custom-call(s32[64]{0:T(128)} %get-tuple-element.97.place, s32[64]{0:T(128)} %copy-done.9, s32[5]{0:T(128)} %and_select_fusion.1.tiles, s32[5,1,128]{2,1,0:T(1,128)} %tile.9.rest_0_, s32[1,160]{1,0:T(1,128)} %rest_1_.2, bf16[160,6144]{1,0:T(8,128)(2,1)} %bitcast.72, ...), custom_call_target="tpu_custom_call" | custom-call | flops 4831838208 | bytes 7995392 | tf_op jit(solution)/shard_map/pallas_call | solution.py:313
  134.8 3.4 %collective-permute-done.16.rest_6_ = bf16[8,16,1024]{2,1,0:T(8,128)(2,1)S(1)} collective-permute-done((bf16[8,16,1024]{2,1,0:T(8,128)(2,1)S(1)}, bf16[8,16,1024]{2,1,0:T(8,128)(2,1)S(1)}, u32[]{:S(2)}, u32[]{:S(2)}) %collective-permute-start.16) | collective-permute-done | bytes 262176 | tf_op jit(solution)/shard_map/ppermute | solution.py:405
  138.9 11.5 %shard_map.75 = bf16[160,6144]{1,0:T(8,128)(2,1)} custom-call(s32[16]{0:T(128)} %get-tuple-element.99.place, s32[16]{0:T(128)} %copy-done.6, s32[5]{0:T(128)} %and_select_fusion.2.tiles, s32[5,1,128]{2,1,0:T(1,128)} %tile.9.rest_0_, s32[1,160]{1,0:T(1,128)} %rest_1_.2, bf16[160,6144]{1,0:T(8,128)(2,1)} %bitcast.73, ...), custom_call_target="tpu_custom_call" | custom-call | flops 1207959552 | bytes 6422528 | tf_op jit(solution)/shard_map/pallas_call | solution.py:313
  (96 shorter events, 12.4 us)
Async XLA Ops:
  2.3 3.5 %collective-permute-start = (s32[1,2,128]{2,1,0:T(2,128)}, s32[1,2,128]{2,1,0:T(2,128)S(1)}, u32[]{:S(2)}, u32[]{:S(2)}) collective-permute-start(s32[1,2,128]{2,1,0:T(2,128)} %get-tuple-element.49), channel_id=1, source_target_pairs={{0,8},{1,9},{2,10},{3,11},{4,12},{5,13},{6,14},{7,15},{8,0},{9,1},... | collective-permute-start | bytes 3080 | tf_op jit(solution)/shard_map/ppermute | solution.py:405
  4.6 2.6 %collective-permute-start.1 = (s32[1,2,128]{2,1,0:T(2,128)}, s32[1,2,128]{2,1,0:T(2,128)S(1)}, u32[]{:S(2)}, u32[]{:S(2)}) collective-permute-start(s32[1,2,128]{2,1,0:T(2,128)} %get-tuple-element.50), channel_id=1, source_target_pairs={{0,12},{1,13},{2,14},{3,15},{4,8},{5,9},{6,10},{7,11},{8,4},{9,5},... | collective-permute-start | bytes 3080 | tf_op jit(solution)/shard_map/ppermute | solution.py:405
  10.3 40.2 %copy-start.5 = (s32[1,128]{1,0:T(1,128)S(1)}, s32[1,128]{1,0:T(1,128)}, u32[]{:S(2)}) copy-start(s32[1,128]{1,0:T(1,128)} %table_ref.2) | copy-start | bytes 1540
  10.3 41.0 %copy-start.3 = (s32[1,160]{1,0:T(1,128)S(1)}, s32[1,160]{1,0:T(1,128)}, u32[]{:S(2)}) copy-start(s32[1,160]{1,0:T(1,128)} %rest_1_.2) | copy-start | bytes 1924
  10.4 35.2 %collective-permute-start.2 = (bf16[8,16,1024]{2,1,0:T(8,128)(2,1)}, bf16[8,16,1024]{2,1,0:T(8,128)(2,1)S(1)}, u32[]{:S(2)}, u32[]{:S(2)}) collective-permute-start(bf16[8,16,1024]{2,1,0:T(8,128)(2,1)} %get-tuple-element.53), channel_id=1, source_target_pairs={{0,8},{1,9},{2,10},{3,11},{4,12},{5,13},{6,14},{7,15},{8,0},{9,1},... | collective-permute-start | bytes 786440 | tf_op jit(solution)/shard_map/ppermute | solution.py:405
  37.1 23.3 %collective-permute-start.3 = (bf16[8,16,1024]{2,1,0:T(8,128)(2,1)}, bf16[8,16,1024]{2,1,0:T(8,128)(2,1)S(1)}, u32[]{:S(2)}, u32[]{:S(2)}) collective-permute-start(bf16[8,16,1024]{2,1,0:T(8,128)(2,1)} %get-tuple-element.75), channel_id=1, source_target_pairs={{0,12},{1,13},{2,14},{3,15},{4,8},{5,9},{6,10},{7,11},{8,4},{9,5},... | collective-permute-start | bytes 786440 | tf_op jit(solution)/shard_map/ppermute | solution.py:405
  40.6 31.2 %all-to-all-start = ((bf16[16,16,1024]{2,1,0:T(8,128)(2,1)}), bf16[16,16,1024]{2,1,0:T(8,128)(2,1)S(1)}, u32[]{:S(2)}, u32[]{:S(2)}) async-start(bf16[16,16,1024]{2,1,0:T(8,128)(2,1)} %shard_map.71), calls=%async_computation | async-start | bytes 1048576 | tf_op jit(solution)/shard_map/all_to_all | solution.py:408
  45.6 35.1 %copy-start.13 = (bf16[8,16,1024]{2,1,0:T(8,128)(2,1)}, bf16[8,16,1024]{2,1,0:T(8,128)(2,1)S(1)}, u32[]{:S(2)}) copy-start(bf16[8,16,1024]{2,1,0:T(8,128)(2,1)S(1)} %collective-permute-done.2.rest_6_) | copy-start | bytes 786436
  52.2 15.5 %collective-permute-start.4 = (bf16[8,16,1024]{2,1,0:T(8,128)(2,1)}, bf16[8,16,1024]{2,1,0:T(8,128)(2,1)S(1)}, u32[]{:S(2)}, u32[]{:S(2)}) collective-permute-start(bf16[8,16,1024]{2,1,0:T(8,128)(2,1)} %get-tuple-element.76), channel_id=1, source_target_pairs={{0,4},{1,5},{2,6},{3,7},{4,0},{5,1},{6,2},{7,3},{8,12},{9,13},{10,... | collective-permute-start | bytes 786440 | tf_op jit(solution)/shard_map/ppermute | solution.py:405
  52.4 28.4 %collective-permute-start.5 = (bf16[8,16,1024]{2,1,0:T(8,128)(2,1)}, bf16[8,16,1024]{2,1,0:T(8,128)(2,1)S(1)}, u32[]{:S(2)}, u32[]{:S(2)}) collective-permute-start(bf16[8,16,1024]{2,1,0:T(8,128)(2,1)} %get-tuple-element.77), channel_id=1, source_target_pairs={{0,5},{1,4},{2,7},{3,6},{4,1},{5,0},{6,3},{7,2},{8,13},{9,12},{10,... | collective-permute-start | bytes 786440 | tf_op jit(solution)/shard_map/ppermute | solution.py:405
  54.3 30.2 %collective-permute-start.6 = (bf16[8,16,1024]{2,1,0:T(8,128)(2,1)}, bf16[8,16,1024]{2,1,0:T(8,128)(2,1)S(1)}, u32[]{:S(2)}, u32[]{:S(2)}) collective-permute-start(bf16[8,16,1024]{2,1,0:T(8,128)(2,1)} %get-tuple-element.78), channel_id=1, source_target_pairs={{0,1},{1,0},{2,3},{3,2},{4,5},{5,4},{6,7},{7,6},{8,9},{9,8},{10,11... | collective-permute-start | bytes 786440 | tf_op jit(solution)/shard_map/ppermute | solution.py:405
  54.3 32.0 %collective-permute-start.7 = (bf16[8,16,1024]{2,1,0:T(8,128)(2,1)}, bf16[8,16,1024]{2,1,0:T(8,128)(2,1)S(1)}, u32[]{:S(2)}, u32[]{:S(2)}) collective-permute-start(bf16[8,16,1024]{2,1,0:T(8,128)(2,1)} %get-tuple-element.81), channel_id=1, source_target_pairs={{0,9},{1,8},{2,11},{3,10},{4,13},{5,12},{6,15},{7,14},{8,1},{9,0},... | collective-permute-start | bytes 786440 | tf_op jit(solution)/shard_map/ppermute | solution.py:405
  60.4 29.1 %copy-start.17 = (bf16[8,16,1024]{2,1,0:T(8,128)(2,1)}, bf16[8,16,1024]{2,1,0:T(8,128)(2,1)S(1)}, u32[]{:S(2)}) copy-start(bf16[8,16,1024]{2,1,0:T(8,128)(2,1)S(1)} %collective-permute-done.3.rest_7_) | copy-start | bytes 786436
  60.4 26.0 %collective-permute-start.8 = (bf16[8,16,1024]{2,1,0:T(8,128)(2,1)}, bf16[8,16,1024]{2,1,0:T(8,128)(2,1)}, u32[]{:S(2)}, u32[]{:S(2)}) collective-permute-start(bf16[8,16,1024]{2,1,0:T(8,128)(2,1)} %get-tuple-element.82), channel_id=1, source_target_pairs={{0,13},{1,12},{2,15},{3,14},{4,9},{5,8},{6,11},{7,10},{8,5},{9,4},... | collective-permute-start | bytes 786440 | tf_op jit(solution)/shard_map/ppermute | solution.py:405
  67.7 20.0 %collective-permute-start.9 = (bf16[8,16,1024]{2,1,0:T(8,128)(2,1)}, bf16[8,16,1024]{2,1,0:T(8,128)(2,1)}, u32[]{:S(2)}, u32[]{:S(2)}) collective-permute-start(bf16[8,16,1024]{2,1,0:T(8,128)(2,1)} %get-tuple-element.83), channel_id=1, source_target_pairs={{0,6},{1,7},{2,4},{3,5},{4,2},{5,3},{6,0},{7,1},{8,14},{9,15},{10,... | collective-permute-start | bytes 786440 | tf_op jit(solution)/shard_map/ppermute | solution.py:405
  80.8 29.8 %collective-permute-start.10 = (bf16[8,16,1024]{2,1,0:T(8,128)(2,1)S(1)}, bf16[8,16,1024]{2,1,0:T(8,128)(2,1)S(1)}, u32[]{:S(2)}, u32[]{:S(2)}) collective-permute-start(bf16[8,16,1024]{2,1,0:T(8,128)(2,1)S(1)} %copy-done.19), channel_id=1, source_target_pairs={{0,10},{1,11},{2,8},{3,9},{4,14},{5,15},{6,12},{7,13},{8,2},{9,3},... | collective-permute-start | bytes 786440 | tf_op jit(solution)/shard_map/ppermute | solution.py:405
  84.5 28.6 %collective-permute-start.11 = (bf16[8,16,1024]{2,1,0:T(8,128)(2,1)S(1)}, bf16[8,16,1024]{2,1,0:T(8,128)(2,1)}, u32[]{:S(2)}, u32[]{:S(2)}) collective-permute-start(bf16[8,16,1024]{2,1,0:T(8,128)(2,1)S(1)} %copy-done.18), channel_id=1, source_target_pairs={{0,7},{1,6},{2,5},{3,4},{4,3},{5,2},{6,1},{7,0},{8,15},{9,14},{10,... | collective-permute-start | bytes 786440 | tf_op jit(solution)/shard_map/ppermute | solution.py:405
  86.3 24.3 %copy-start.20 = (bf16[8,16,1024]{2,1,0:T(8,128)(2,1)}, bf16[8,16,1024]{2,1,0:T(8,128)(2,1)S(1)}, u32[]{:S(2)}) copy-start(bf16[8,16,1024]{2,1,0:T(8,128)(2,1)S(1)} %collective-permute-done.7.rest_5_) | copy-start | bytes 786436
  86.3 28.9 %collective-permute-start.12 = (bf16[8,16,1024]{2,1,0:T(8,128)(2,1)S(1)}, bf16[8,16,1024]{2,1,0:T(8,128)(2,1)}, u32[]{:S(2)}, u32[]{:S(2)}) collective-permute-start(bf16[8,16,1024]{2,1,0:T(8,128)(2,1)S(1)} %copy-done.16), channel_id=1, source_target_pairs={{0,2},{1,3},{2,0},{3,1},{4,6},{5,7},{6,4},{7,5},{8,10},{9,11},{10,... | collective-permute-start | bytes 786440 | tf_op jit(solution)/shard_map/ppermute | solution.py:405
  86.4 28.8 %collective-permute-start.13 = (bf16[8,16,1024]{2,1,0:T(8,128)(2,1)S(1)}, bf16[8,16,1024]{2,1,0:T(8,128)(2,1)}, u32[]{:S(2)}, u32[]{:S(2)}) collective-permute-start(bf16[8,16,1024]{2,1,0:T(8,128)(2,1)S(1)} %copy-done.15), channel_id=1, source_target_pairs={{0,14},{1,15},{2,12},{3,13},{4,10},{5,11},{6,8},{7,9},{8,6},{9,7},... | collective-permute-start | bytes 786440 | tf_op jit(solution)/shard_map/ppermute | solution.py:405
  87.8 27.4 %collective-permute-start.14 = (bf16[8,16,1024]{2,1,0:T(8,128)(2,1)S(1)}, bf16[8,16,1024]{2,1,0:T(8,128)(2,1)}, u32[]{:S(2)}, u32[]{:S(2)}) collective-permute-start(bf16[8,16,1024]{2,1,0:T(8,128)(2,1)S(1)} %copy-done.14), channel_id=1, source_target_pairs={{0,3},{1,2},{2,1},{3,0},{4,7},{5,6},{6,5},{7,4},{8,11},{9,10},{10,... | collective-permute-start | bytes 786440 | tf_op jit(solution)/shard_map/ppermute | solution.py:405
  89.4 23.7 %copy-start.11 = (bf16[8,16,1024]{2,1,0:T(8,128)(2,1)S(1)}, bf16[8,16,1024]{2,1,0:T(8,128)(2,1)}, u32[]{:S(2)}) copy-start(bf16[8,16,1024]{2,1,0:T(8,128)(2,1)} %get-tuple-element.92) | copy-start | bytes 786436
  110.6 24.1 %collective-permute-start.15 = (bf16[8,16,1024]{2,1,0:T(8,128)(2,1)S(1)}, bf16[8,16,1024]{2,1,0:T(8,128)(2,1)S(1)}, u32[]{:S(2)}, u32[]{:S(2)}) collective-permute-start(bf16[8,16,1024]{2,1,0:T(8,128)(2,1)S(1)} %copy-done.12), channel_id=1, source_target_pairs={{0,11},{1,10},{2,9},{3,8},{4,15},{5,14},{6,13},{7,12},{8,3},{9,2},... | collective-permute-start | bytes 786440 | tf_op jit(solution)/shard_map/ppermute | solution.py:405
  113.1 25.1 %collective-permute-start.16 = (bf16[8,16,1024]{2,1,0:T(8,128)(2,1)S(1)}, bf16[8,16,1024]{2,1,0:T(8,128)(2,1)S(1)}, u32[]{:S(2)}, u32[]{:S(2)}) collective-permute-start(bf16[8,16,1024]{2,1,0:T(8,128)(2,1)S(1)} %copy-done.11), channel_id=1, source_target_pairs={{0,15},{1,14},{2,13},{3,12},{4,11},{5,10},{6,9},{7,8},{8,7},{9,6},... | collective-permute-start | bytes 786440 | tf_op jit(solution)/shard_map/ppermute | solution.py:405
  (19 other events, 211.3 us)

commit v9 on v5

--- a/solution.py
+++ b/solution.py
@@ -26,6 +26,11 @@
 
 def one_hot(condition):
     return jnp.where(condition, 1.0, 0.0)
+
+
+def over_rows(reduce, x):
+    blocks = reduce(x.reshape(x.shape[0] // 8, 8, x.shape[1]), axis=0)
+    return reduce(blocks, axis=0, keepdims=True)
 
 
 def pair_places(hold, page_len, table_ref, sel_ref, wide):
@@ -256,12 +261,10 @@
                 part = slice(n * LANES, (n + 1) * LANES)
                 s = scores[:, part] + bias
                 old = stats[g : g + 1, part]
-                new = jnp.maximum(old, jnp.max(s, axis=0, keepdims=True))
+                new = jnp.maximum(old, over_rows(jnp.max, s))
                 p = jnp.exp2((s - new) * scale)
                 shrink = jnp.exp2((old - new) * scale)
-                stats[at : at + 1, part] = stats[at : at + 1, part] * shrink + jnp.sum(
-                    p, axis=0, keepdims=True
-                )
+                stats[at : at + 1, part] = stats[at : at + 1, part] * shrink + over_rows(jnp.sum, p)
                 stats[g : g + 1, part] = new
                 raised.append(p.astype(bf16))
                 shrinks.append(shrink)
@@ -439,20 +442,23 @@
             out_shape=[jax.ShapeDtypeStruct((capacity, page_len, width), store.dtype)] * len(first),
             compiler_params=params,
         )(*lists, store)
-        parts, index, table, positions = lax.optimization_barrier(
-            (parts, index, page_table, sel_pos)
-        )
+        parts, table, positions = lax.optimization_barrier((parts, page_table, sel_pos))
         arrived = {d: swap(part, d) for d, part in zip(first, parts)}
     else:
         table, positions = page_table, sel_pos
-    index_in = exchange(index)
-
     packed = pl.pallas_call(
         functools.partial(rows_kernel, hold, page_len),
         out_shape=jax.ShapeDtypeStruct((holders, ROW_SLOTS, width), store.dtype),
         scratch_shapes=[wide],
         compiler_params=params,
     )(table, positions, fresh)
+    if first:
+        index, packed = lax.optimization_barrier((index, packed))
+        index_in = exchange(index)
+        index_in, _ = lax.optimization_barrier((index_in, [arrived[d] for d in first]))
+    else:
+        index_in = exchange(index)
+    rows_in = exchange(packed)
 
     each = jax.ShapeDtypeStruct((capacity, page_len, width), store.dtype)
     whole = jax.ShapeDtypeStruct((holders, capacity, page_len, width), store.dtype)
@@ -468,14 +474,13 @@
         out_shape=[each] * len(others) if others else [whole],
         compiler_params=params,
     )(own_word, index_in, store)
-    parts, packed, table, positions = lax.optimization_barrier((parts, packed, table, positions))
+    parts, table, positions = lax.optimization_barrier((parts, table, positions))
     if others:
         for d, part in zip(others, parts):
             arrived[d] = swap(part, d) if d else part
         contexts = [[arrived[d] for d in group] for group in groups]
     else:
         contexts = [[exchange(parts[0]).reshape(pages, page_len, width)]]
-    rows_in = exchange(packed)
 
     store_out = pl.pallas_call(
         write_back_kernel,

time: 139 us -> 151 us (1.086)
  blocking collectives: 0 us -> 22.1 us
  waiting for transfers between devices: 19.5 us -> 9.67 us
    all_to_all x0 -> x1, blocking collectives: none -> 22.1 us  [exchange(): return lax.all_to_all(x, 'store', split_axis=0, concat_axis=0, tiled=True)]
    ppermute x17, waiting for transfers between devices: 18.9 us -> 9.67 us  [swap(): return lax.ppermute(x, 'store', [(h, h ^ d) for h in range(holders)])]
    ppermute x17, starting transfers between devices: 23.8 us -> 32.9 us  [swap(): return lax.ppermute(x, 'store', [(h, h ^ d) for h in range(holders)])]
    all_to_all x2 -> x1, starting transfers between devices: 13.8 us -> 4.86 us  [exchange(): return lax.all_to_all(x, 'store', split_axis=0, concat_axis=0, tiled=True)]
  transfers between devices with their start and end apart: 19 -> 18, of which waited for: 8 -> 4; matrix products, arithmetic and copies ran while one was open for 5% -> 5% of each run, Pallas kernels for 40% -> 36%
where the time goes in v9:
time: 151 us; the launch traced here: 149 us
  Pallas kernels  69.3 us (46%)
  starting transfers between devices  37.7 us (25%)
  blocking collectives  22.1 us (15%)
  waiting for transfers between devices  9.67 us (6%)
  other arithmetic  5.31 us (4%)
  local copies, waits for them, and re-layouts  4.31 us (3%)
    pallas_call x3, Pallas kernels, attend(): pl.pallas_call(functools.partial(attend_kernel, first, last, len(contexts...  49.9 us
    ppermute x17, starting transfers between devices, swap(): return lax.ppermute(x, 'store', [(h, h ^ d) for h in range(holders)])  32.9 us
    all_to_all x1, blocking collectives, exchange(): return lax.all_to_all(x, 'store', split_axis=0, concat_axis=0, tiled=True)  22.1 us
    ppermute x17, waiting for transfers between devices, swap(): return lax.ppermute(x, 'store', [(h, h ^ d) for h in range(holders)])  9.67 us
    pallas_call x1, Pallas kernels, per_device(): pl.pallas_call(write_back_kernel, grid_spec=pltpu.PrefetchScalarGridSpec(...  8.02 us
    pallas_call x1, Pallas kernels, per_device(): pl.pallas_call(functools.partial(gather_kernel, capacity, others), grid_s...  4.9 us
    all_to_all x1, starting transfers between devices, exchange(): return lax.all_to_all(x, 'store', split_axis=0, concat_axis=0, tiled=True)  4.86 us
  transfers between devices with their start and end apart: 18, of which 4 were waited for; matrix products, arithmetic and copies ran while one was open for 5% of the time, Pallas kernels for 36%

profile of v9, /device:TPU:9, one launch (start us, length us, event | category | flops | bytes accessed | tf_op | source)
XLA Modules:
  0.0 149.5 jit_solution(17439940031623001922)
XLA Ops:
  0.6 1.6 %shard_map.68 = (s32[16,2,128]{2,1,0:T(2,128)}, s32[1,2,128]{2,1,0:T(2,128)}, s32[1,2,128]{2,1,0:T(2,128)}) custom-call(s32[1]{0:T(128)} %bitcast.own, s32[1,128]{1,0:T(1,128)} %table_ref.2, s32[1,160]{1,0:T(1,128)} %rest_1_.2), custom_call_target="tpu_custom_call" | custom-call | tf_op jit(solution)/shard_map/pallas_call | solution.py:411
  2.3 2.3 %collective-permute-start = (s32[1,2,128]{2,1,0:T(2,128)}, s32[1,2,128]{2,1,0:T(2,128)S(1)}, u32[]{:S(2)}, u32[]{:S(2)}) collective-permute-start(s32[1,2,128]{2,1,0:T(2,128)} %get-tuple-element.51), channel_id=1, source_target_pairs={{0,8},{1,9},{2,10},{3,11},{4,12},{5,13},{6,14},{7,15},{8,0},{9,1},... | collective-permute-start | bytes 3080 | tf_op jit(solution)/shard_map/ppermute | solution.py:406
  5.8 1.4 collective-permute-done.1.refs_1_
  7.8 2.5 %shard_map.69 = (bf16[8,16,1024]{2,1,0:T(8,128)(2,1)}, bf16[8,16,1024]{2,1,0:T(8,128)(2,1)}) custom-call(s32[1,2,128]{2,1,0:T(2,128)} %copy-done.7, s32[1,2,128]{2,1,0:T(2,128)} %copy-done.8, bf16[128,16,1024]{2,1,0:T(8,128)(2,1)} %store_hbm.3), custom_call_target="tpu_custom_call" | custom-call | tf_op jit(solution)/shard_map/pallas_call | solution.py:429
  10.3 1.9 %collective-permute-start.2 = (bf16[8,16,1024]{2,1,0:T(8,128)(2,1)}, bf16[8,16,1024]{2,1,0:T(8,128)(2,1)S(1)}, u32[]{:S(2)}, u32[]{:S(2)}) collective-permute-start(bf16[8,16,1024]{2,1,0:T(8,128)(2,1)} %get-tuple-element.58), channel_id=1, source_target_pairs={{0,8},{1,9},{2,10},{3,11},{4,12},{5,13},{6,14},{7,15},{8,0},{9,1},... | collective-permute-start | bytes 786440 | tf_op jit(solution)/shard_map/ppermute | solution.py:406
  12.2 1.3 collective-permute-start.3
  13.5 2.4 %shard_map.70 = bf16[16,16,1024]{2,1,0:T(8,128)(2,1)} custom-call(s32[1,128]{1,0:T(1,128)} %table_ref.2, s32[1,160]{1,0:T(1,128)} %rest_1_.2, bf16[160,1024]{1,0:T(8,128)(2,1)} %bitcast.70), custom_call_target="tpu_custom_call" | custom-call | tf_op jit(solution)/shard_map/pallas_call | solution.py:449
  15.9 22.1 %all_to_all.10.index.targets_ref = s32[16,2,128]{2,1,0:T(2,128)} all-to-all(s32[16,2,128]{2,1,0:T(2,128)S(1)} %copy-done.4), channel_id=1, replica_groups=mesh['groups'=2,'store'=16] {'store'}, dimensions={0} | all-to-all | bytes 32768 | tf_op jit(solution)/shard_map/all_to_all | solution.py:409
  38.0 4.9 %all-to-all-start.1 = ((bf16[16,16,1024]{2,1,0:T(8,128)(2,1)}), bf16[16,16,1024]{2,1,0:T(8,128)(2,1)S(1)}, u32[]{:S(2)}, u32[]{:S(2)}) async-start(bf16[16,16,1024]{2,1,0:T(8,128)(2,1)} %shard_map.70), calls=%async_computation.1 | async-start | bytes 1048576 | tf_op jit(solution)/shard_map/all_to_all | solution.py:409
  42.9 4.9 %shard_map.71 = (bf16[8,16,1024]{2,1,0:T(8,128)(2,1)}, bf16[8,16,1024]{2,1,0:T(8,128)(2,1)}, bf16[8,16,1024]{2,1,0:T(8,128)(2,1)}, bf16[8,16,1024]{2,1,0:T(8,128...) custom-call(s32[1]{0:T(128)} %bitcast.own, ...), custom_call_target="tpu_custom_call" | custom-call | tf_op jit(solution)/shard_map/pallas_call | solution.py:465
  49.8 1.9 %collective-permute-start.5 = (bf16[8,16,1024]{2,1,0:T(8,128)(2,1)}, bf16[8,16,1024]{2,1,0:T(8,128)(2,1)S(1)}, u32[]{:S(2)}, u32[]{:S(2)}) collective-permute-start(bf16[8,16,1024]{2,1,0:T(8,128)(2,1)} %get-tuple-element.81), channel_id=1, source_target_pairs={{0,5},{1,4},{2,7},{3,6},{4,1},{5,0},{6,3},{7,2},{8,13},{9,12},{10,... | collective-permute-start | bytes 786440 | tf_op jit(solution)/shard_map/ppermute | solution.py:406
  51.7 2.5 %collective-permute-start.7 = (bf16[8,16,1024]{2,1,0:T(8,128)(2,1)}, bf16[8,16,1024]{2,1,0:T(8,128)(2,1)S(1)}, u32[]{:S(2)}, u32[]{:S(2)}) collective-permute-start(bf16[8,16,1024]{2,1,0:T(8,128)(2,1)} %get-tuple-element.85), channel_id=1, source_target_pairs={{0,9},{1,8},{2,11},{3,10},{4,13},{5,12},{6,15},{7,14},{8,1},{9,0},... | collective-permute-start | bytes 786440 | tf_op jit(solution)/shard_map/ppermute | solution.py:406
  59.0 4.7 %collective-permute-done.4.rest_8_ = bf16[8,16,1024]{2,1,0:T(8,128)(2,1)S(1)} collective-permute-done((bf16[8,16,1024]{2,1,0:T(8,128)(2,1)}, bf16[8,16,1024]{2,1,0:T(8,128)(2,1)S(1)}, u32[]{:S(2)}, u32[]{:S(2)}) %collective-permute-start.4) | collective-permute-done | bytes 262176 | tf_op jit(solution)/shard_map/ppermute | solution.py:406
  63.7 3.0 %collective-permute-start.9 = (bf16[8,16,1024]{2,1,0:T(8,128)(2,1)}, bf16[8,16,1024]{2,1,0:T(8,128)(2,1)}, u32[]{:S(2)}, u32[]{:S(2)}) collective-permute-start(bf16[8,16,1024]{2,1,0:T(8,128)(2,1)} %get-tuple-element.87), channel_id=1, source_target_pairs={{0,13},{1,12},{2,15},{3,14},{4,9},{5,8},{6,11},{7,10},{8,5},{9,4},... | collective-permute-start | bytes 786440 | tf_op jit(solution)/shard_map/ppermute | solution.py:406
  68.9 8.0 %shard_map.72 = bf16[128,16,1024]{2,1,0:T(8,128)(2,1)} custom-call(s32[16,2,128]{2,1,0:T(2,128)} %all_to_all.10.index.targets_ref, s32[16,2,128]{2,1,0:T(2,128)} %all_to_all.10.index.targets_ref, bf16[128,16,1024]{2,1,0:T(8,128)(2,1)} %store_hbm.3, bf16[16,16,1024]{2,1,0:T(8,128)(2,1)} %copy-done), custom_call_target="tpu_custom_call" | custom-call | bytes 8388608 | tf_op jit(solution)/shard_map/pallas_call | solution.py:485
  77.0 2.5 %collective-permute-start.10 = (bf16[8,16,1024]{2,1,0:T(8,128)(2,1)S(1)}, bf16[8,16,1024]{2,1,0:T(8,128)(2,1)S(1)}, u32[]{:S(2)}, u32[]{:S(2)}) collective-permute-start(bf16[8,16,1024]{2,1,0:T(8,128)(2,1)S(1)} %copy-done.19), channel_id=1, source_target_pairs={{0,7},{1,6},{2,5},{3,4},{4,3},{5,2},{6,1},{7,0},{8,15},{9,14},{10,... | collective-permute-start | bytes 786440 | tf_op jit(solution)/shard_map/ppermute | solution.py:406
  80.9 2.6 %collective-permute-start.13 = (bf16[8,16,1024]{2,1,0:T(8,128)(2,1)S(1)}, bf16[8,16,1024]{2,1,0:T(8,128)(2,1)}, u32[]{:S(2)}, u32[]{:S(2)}) collective-permute-start(bf16[8,16,1024]{2,1,0:T(8,128)(2,1)S(1)} %copy-done.16), channel_id=1, source_target_pairs={{0,14},{1,15},{2,12},{3,13},{4,10},{5,11},{6,8},{7,9},{8,6},{9,7},... | collective-permute-start | bytes 786440 | tf_op jit(solution)/shard_map/ppermute | solution.py:406
  83.5 6.0 %collective-permute-start.14 = (bf16[8,16,1024]{2,1,0:T(8,128)(2,1)S(1)}, bf16[8,16,1024]{2,1,0:T(8,128)(2,1)}, u32[]{:S(2)}, u32[]{:S(2)}) collective-permute-start(bf16[8,16,1024]{2,1,0:T(8,128)(2,1)S(1)} %copy-done.14), channel_id=1, source_target_pairs={{0,3},{1,2},{2,1},{3,0},{4,7},{5,6},{6,5},{7,4},{8,11},{9,10},{10,... | collective-permute-start | bytes 786440 | tf_op jit(solution)/shard_map/ppermute | solution.py:406
  90.3 20.4 %shard_map.73 = (f32[5,4,128,384]{3,2,1,0:T(8,128)}, f32[5,8,384]{2,1,0:T(8,128)}) custom-call(s32[48]{0:T(128)} %get-tuple-element.99.place, s32[48]{0:T(128)} %copy-done.10, s32[5]{0:T(128)} %fusion.7.tiles, s32[5,1,128]{2,1,0:T(1,128)} %tile.9.rest_0_, s32[1,160]{1,0:T(1,128)} %rest_1_.2, bf16[160,6144]{1,0:T(8,128)(2,1)} %bitcast.66, ...), custom_call_target="tpu_custom_call" | custom-call | flops 4831838208 | bytes 7995392 | tf_op jit(solution)/shard_map/pallas_call | solution.py:314
  110.7 1.6 %collective-permute-start.15 = (bf16[8,16,1024]{2,1,0:T(8,128)(2,1)S(1)}, bf16[8,16,1024]{2,1,0:T(8,128)(2,1)S(1)}, u32[]{:S(2)}, u32[]{:S(2)}) collective-permute-start(bf16[8,16,1024]{2,1,0:T(8,128)(2,1)S(1)} %copy-done.12), channel_id=1, source_target_pairs={{0,11},{1,10},{2,9},{3,8},{4,15},{5,14},{6,13},{7,12},{8,3},{9,2},... | collective-permute-start | bytes 786440 | tf_op jit(solution)/shard_map/ppermute | solution.py:406
  112.4 4.5 %collective-permute-start.16 = (bf16[8,16,1024]{2,1,0:T(8,128)(2,1)S(1)}, bf16[8,16,1024]{2,1,0:T(8,128)(2,1)S(1)}, u32[]{:S(2)}, u32[]{:S(2)}) collective-permute-start(bf16[8,16,1024]{2,1,0:T(8,128)(2,1)S(1)} %copy-done.11), channel_id=1, source_target_pairs={{0,15},{1,14},{2,13},{3,12},{4,11},{5,10},{6,9},{7,8},{8,7},{9,6},... | collective-permute-start | bytes 786440 | tf_op jit(solution)/shard_map/ppermute | solution.py:406
  116.9 18.8 %shard_map.74 = (f32[5,4,128,384]{3,2,1,0:T(8,128)}, f32[5,8,384]{2,1,0:T(8,128)}) custom-call(s32[64]{0:T(128)} %get-tuple-element.101.place, s32[64]{0:T(128)} %copy-done.9, s32[5]{0:T(128)} %and_select_fusion.1.tiles, s32[5,1,128]{2,1,0:T(1,128)} %tile.9.rest_0_, s32[1,160]{1,0:T(1,128)} %rest_1_.2, bf16[160,6144]{1,0:T(8,128)(2,1)} %bitcast.67, ...), custom_call_target="tpu_custom_call" | custom-call | flops 4831838208 | bytes 7995392 | tf_op jit(solution)/shard_map/pallas_call | solution.py:314
  135.7 2.3 %collective-permute-done.16.rest_6_ = bf16[8,16,1024]{2,1,0:T(8,128)(2,1)S(1)} collective-permute-done((bf16[8,16,1024]{2,1,0:T(8,128)(2,1)S(1)}, bf16[8,16,1024]{2,1,0:T(8,128)(2,1)S(1)}, u32[]{:S(2)}, u32[]{:S(2)}) %collective-permute-start.16) | collective-permute-done | bytes 262176 | tf_op jit(solution)/shard_map/ppermute | solution.py:406
  138.7 10.7 %shard_map.75 = bf16[160,6144]{1,0:T(8,128)(2,1)} custom-call(s32[16]{0:T(128)} %get-tuple-element.103.place, s32[16]{0:T(128)} %copy-done.6, s32[5]{0:T(128)} %and_select_fusion.2.tiles, s32[5,1,128]{2,1,0:T(1,128)} %tile.9.rest_0_, s32[1,160]{1,0:T(1,128)} %rest_1_.2, bf16[160,6144]{1,0:T(8,128)(2,1)} %bitcast.68, ...), custom_call_target="tpu_custom_call" | custom-call | flops 1207959552 | bytes 6422528 | tf_op jit(solution)/shard_map/pallas_call | solution.py:314
  (97 shorter events, 13.5 us)
Async XLA Ops:
  2.3 3.5 %collective-permute-start = (s32[1,2,128]{2,1,0:T(2,128)}, s32[1,2,128]{2,1,0:T(2,128)S(1)}, u32[]{:S(2)}, u32[]{:S(2)}) collective-permute-start(s32[1,2,128]{2,1,0:T(2,128)} %get-tuple-element.51), channel_id=1, source_target_pairs={{0,8},{1,9},{2,10},{3,11},{4,12},{5,13},{6,14},{7,15},{8,0},{9,1},... | collective-permute-start | bytes 3080 | tf_op jit(solution)/shard_map/ppermute | solution.py:406
  4.6 2.6 %collective-permute-start.1 = (s32[1,2,128]{2,1,0:T(2,128)}, s32[1,2,128]{2,1,0:T(2,128)S(1)}, u32[]{:S(2)}, u32[]{:S(2)}) collective-permute-start(s32[1,2,128]{2,1,0:T(2,128)} %get-tuple-element.52), channel_id=1, source_target_pairs={{0,12},{1,13},{2,14},{3,15},{4,8},{5,9},{6,10},{7,11},{8,4},{9,5},... | collective-permute-start | bytes 3080 | tf_op jit(solution)/shard_map/ppermute | solution.py:406
  10.3 37.5 %copy-start.5 = (s32[1,128]{1,0:T(1,128)S(1)}, s32[1,128]{1,0:T(1,128)}, u32[]{:S(2)}) copy-start(s32[1,128]{1,0:T(1,128)} %table_ref.2) | copy-start | bytes 1540
  10.3 38.4 %copy-start.3 = (s32[1,160]{1,0:T(1,128)S(1)}, s32[1,160]{1,0:T(1,128)}, u32[]{:S(2)}) copy-start(s32[1,160]{1,0:T(1,128)} %rest_1_.2) | copy-start | bytes 1924
  10.3 32.6 %collective-permute-start.2 = (bf16[8,16,1024]{2,1,0:T(8,128)(2,1)}, bf16[8,16,1024]{2,1,0:T(8,128)(2,1)S(1)}, u32[]{:S(2)}, u32[]{:S(2)}) collective-permute-start(bf16[8,16,1024]{2,1,0:T(8,128)(2,1)} %get-tuple-element.58), channel_id=1, source_target_pairs={{0,8},{1,9},{2,10},{3,11},{4,12},{5,13},{6,14},{7,15},{8,0},{9,1},... | collective-permute-start | bytes 786440 | tf_op jit(solution)/shard_map/ppermute | solution.py:406
  12.2 30.7 %collective-permute-start.3 = (bf16[8,16,1024]{2,1,0:T(8,128)(2,1)}, bf16[8,16,1024]{2,1,0:T(8,128)(2,1)S(1)}, u32[]{:S(2)}, u32[]{:S(2)}) collective-permute-start(bf16[8,16,1024]{2,1,0:T(8,128)(2,1)} %get-tuple-element.59), channel_id=1, source_target_pairs={{0,12},{1,13},{2,14},{3,15},{4,8},{5,9},{6,10},{7,11},{8,4},{9,5},... | collective-permute-start | bytes 786440 | tf_op jit(solution)/shard_map/ppermute | solution.py:406
  38.0 30.1 %all-to-all-start.1 = ((bf16[16,16,1024]{2,1,0:T(8,128)(2,1)}), bf16[16,16,1024]{2,1,0:T(8,128)(2,1)S(1)}, u32[]{:S(2)}, u32[]{:S(2)}) async-start(bf16[16,16,1024]{2,1,0:T(8,128)(2,1)} %shard_map.70), calls=%async_computation.1 | async-start | bytes 1048576 | tf_op jit(solution)/shard_map/all_to_all | solution.py:409
  42.9 34.1 %copy-start.13 = (bf16[8,16,1024]{2,1,0:T(8,128)(2,1)}, bf16[8,16,1024]{2,1,0:T(8,128)(2,1)S(1)}, u32[]{:S(2)}) copy-start(bf16[8,16,1024]{2,1,0:T(8,128)(2,1)S(1)} %collective-permute-done.2.rest_6_) | copy-start | bytes 786436
  42.9 34.1 %copy-start.15 = (bf16[8,16,1024]{2,1,0:T(8,128)(2,1)}, bf16[8,16,1024]{2,1,0:T(8,128)(2,1)S(1)}, u32[]{:S(2)}) copy-start(bf16[8,16,1024]{2,1,0:T(8,128)(2,1)S(1)} %collective-permute-done.3.rest_7_) | copy-start | bytes 786436
  49.6 14.0 %collective-permute-start.4 = (bf16[8,16,1024]{2,1,0:T(8,128)(2,1)}, bf16[8,16,1024]{2,1,0:T(8,128)(2,1)S(1)}, u32[]{:S(2)}, u32[]{:S(2)}) collective-permute-start(bf16[8,16,1024]{2,1,0:T(8,128)(2,1)} %get-tuple-element.80), channel_id=1, source_target_pairs={{0,4},{1,5},{2,6},{3,7},{4,0},{5,1},{6,2},{7,3},{8,12},{9,13},{10,... | collective-permute-start | bytes 786440 | tf_op jit(solution)/shard_map/ppermute | solution.py:406
  49.8 27.2 %collective-permute-start.5 = (bf16[8,16,1024]{2,1,0:T(8,128)(2,1)}, bf16[8,16,1024]{2,1,0:T(8,128)(2,1)S(1)}, u32[]{:S(2)}, u32[]{:S(2)}) collective-permute-start(bf16[8,16,1024]{2,1,0:T(8,128)(2,1)} %get-tuple-element.81), channel_id=1, source_target_pairs={{0,5},{1,4},{2,7},{3,6},{4,1},{5,0},{6,3},{7,2},{8,13},{9,12},{10,... | collective-permute-start | bytes 786440 | tf_op jit(solution)/shard_map/ppermute | solution.py:406
  51.7 27.8 %collective-permute-start.6 = (bf16[8,16,1024]{2,1,0:T(8,128)(2,1)}, bf16[8,16,1024]{2,1,0:T(8,128)(2,1)}, u32[]{:S(2)}, u32[]{:S(2)}) collective-permute-start(bf16[8,16,1024]{2,1,0:T(8,128)(2,1)} %get-tuple-element.82), channel_id=1, source_target_pairs={{0,1},{1,0},{2,3},{3,2},{4,5},{5,4},{6,7},{7,6},{8,9},{9,8},{10,11... | collective-permute-start | bytes 786440 | tf_op jit(solution)/shard_map/ppermute | solution.py:406
  51.7 29.0 %collective-permute-start.7 = (bf16[8,16,1024]{2,1,0:T(8,128)(2,1)}, bf16[8,16,1024]{2,1,0:T(8,128)(2,1)S(1)}, u32[]{:S(2)}, u32[]{:S(2)}) collective-permute-start(bf16[8,16,1024]{2,1,0:T(8,128)(2,1)} %get-tuple-element.85), channel_id=1, source_target_pairs={{0,9},{1,8},{2,11},{3,10},{4,13},{5,12},{6,15},{7,14},{8,1},{9,0},... | collective-permute-start | bytes 786440 | tf_op jit(solution)/shard_map/ppermute | solution.py:406
  54.2 26.6 %collective-permute-start.8 = (bf16[8,16,1024]{2,1,0:T(8,128)(2,1)}, bf16[8,16,1024]{2,1,0:T(8,128)(2,1)S(1)}, u32[]{:S(2)}, u32[]{:S(2)}) collective-permute-start(bf16[8,16,1024]{2,1,0:T(8,128)(2,1)} %get-tuple-element.86), channel_id=1, source_target_pairs={{0,6},{1,7},{2,4},{3,5},{4,2},{5,3},{6,0},{7,1},{8,14},{9,15},{10,... | collective-permute-start | bytes 786440 | tf_op jit(solution)/shard_map/ppermute | solution.py:406
  63.7 19.8 %collective-permute-start.9 = (bf16[8,16,1024]{2,1,0:T(8,128)(2,1)}, bf16[8,16,1024]{2,1,0:T(8,128)(2,1)}, u32[]{:S(2)}, u32[]{:S(2)}) collective-permute-start(bf16[8,16,1024]{2,1,0:T(8,128)(2,1)} %get-tuple-element.87), channel_id=1, source_target_pairs={{0,13},{1,12},{2,15},{3,14},{4,9},{5,8},{6,11},{7,10},{8,5},{9,4},... | collective-permute-start | bytes 786440 | tf_op jit(solution)/shard_map/ppermute | solution.py:406
  77.0 33.7 %collective-permute-start.10 = (bf16[8,16,1024]{2,1,0:T(8,128)(2,1)S(1)}, bf16[8,16,1024]{2,1,0:T(8,128)(2,1)S(1)}, u32[]{:S(2)}, u32[]{:S(2)}) collective-permute-start(bf16[8,16,1024]{2,1,0:T(8,128)(2,1)S(1)} %copy-done.19), channel_id=1, source_target_pairs={{0,7},{1,6},{2,5},{3,4},{4,3},{5,2},{6,1},{7,0},{8,15},{9,14},{10,... | collective-permute-start | bytes 786440 | tf_op jit(solution)/shard_map/ppermute | solution.py:406
  79.5 32.8 %collective-permute-start.11 = (bf16[8,16,1024]{2,1,0:T(8,128)(2,1)S(1)}, bf16[8,16,1024]{2,1,0:T(8,128)(2,1)S(1)}, u32[]{:S(2)}, u32[]{:S(2)}) collective-permute-start(bf16[8,16,1024]{2,1,0:T(8,128)(2,1)S(1)} %copy-done.18), channel_id=1, source_target_pairs={{0,10},{1,11},{2,8},{3,9},{4,14},{5,15},{6,12},{7,13},{8,2},{9,3},... | collective-permute-start | bytes 786440 | tf_op jit(solution)/shard_map/ppermute | solution.py:406
  80.7 30.0 %copy-start.20 = (bf16[8,16,1024]{2,1,0:T(8,128)(2,1)}, bf16[8,16,1024]{2,1,0:T(8,128)(2,1)S(1)}, u32[]{:S(2)}) copy-start(bf16[8,16,1024]{2,1,0:T(8,128)(2,1)S(1)} %collective-permute-done.7.rest_5_) | copy-start | bytes 786436
  80.7 36.1 %collective-permute-start.12 = (bf16[8,16,1024]{2,1,0:T(8,128)(2,1)S(1)}, bf16[8,16,1024]{2,1,0:T(8,128)(2,1)}, u32[]{:S(2)}, u32[]{:S(2)}) collective-permute-start(bf16[8,16,1024]{2,1,0:T(8,128)(2,1)S(1)} %copy-done.17), channel_id=1, source_target_pairs={{0,2},{1,3},{2,0},{3,1},{4,6},{5,7},{6,4},{7,5},{8,10},{9,11},{10,... | collective-permute-start | bytes 786440 | tf_op jit(solution)/shard_map/ppermute | solution.py:406
  80.9 29.8 %copy-start.21 = (bf16[8,16,1024]{2,1,0:T(8,128)(2,1)}, bf16[8,16,1024]{2,1,0:T(8,128)(2,1)S(1)}, u32[]{:S(2)}) copy-start(bf16[8,16,1024]{2,1,0:T(8,128)(2,1)S(1)} %collective-permute-done.8.rest_6_) | copy-start | bytes 786436
  80.9 36.0 %collective-permute-start.13 = (bf16[8,16,1024]{2,1,0:T(8,128)(2,1)S(1)}, bf16[8,16,1024]{2,1,0:T(8,128)(2,1)}, u32[]{:S(2)}, u32[]{:S(2)}) collective-permute-start(bf16[8,16,1024]{2,1,0:T(8,128)(2,1)S(1)} %copy-done.16), channel_id=1, source_target_pairs={{0,14},{1,15},{2,12},{3,13},{4,10},{5,11},{6,8},{7,9},{8,6},{9,7},... | collective-permute-start | bytes 786440 | tf_op jit(solution)/shard_map/ppermute | solution.py:406
  83.5 33.4 %collective-permute-start.14 = (bf16[8,16,1024]{2,1,0:T(8,128)(2,1)S(1)}, bf16[8,16,1024]{2,1,0:T(8,128)(2,1)}, u32[]{:S(2)}, u32[]{:S(2)}) collective-permute-start(bf16[8,16,1024]{2,1,0:T(8,128)(2,1)S(1)} %copy-done.14), channel_id=1, source_target_pairs={{0,3},{1,2},{2,1},{3,0},{4,7},{5,6},{6,5},{7,4},{8,11},{9,10},{10,... | collective-permute-start | bytes 786440 | tf_op jit(solution)/shard_map/ppermute | solution.py:406
  110.7 25.0 %collective-permute-start.15 = (bf16[8,16,1024]{2,1,0:T(8,128)(2,1)S(1)}, bf16[8,16,1024]{2,1,0:T(8,128)(2,1)S(1)}, u32[]{:S(2)}, u32[]{:S(2)}) collective-permute-start(bf16[8,16,1024]{2,1,0:T(8,128)(2,1)S(1)} %copy-done.12), channel_id=1, source_target_pairs={{0,11},{1,10},{2,9},{3,8},{4,15},{5,14},{6,13},{7,12},{8,3},{9,2},... | collective-permute-start | bytes 786440 | tf_op jit(solution)/shard_map/ppermute | solution.py:406
  112.4 25.7 %collective-permute-start.16 = (bf16[8,16,1024]{2,1,0:T(8,128)(2,1)S(1)}, bf16[8,16,1024]{2,1,0:T(8,128)(2,1)S(1)}, u32[]{:S(2)}, u32[]{:S(2)}) collective-permute-start(bf16[8,16,1024]{2,1,0:T(8,128)(2,1)S(1)} %copy-done.11), channel_id=1, source_target_pairs={{0,15},{1,14},{2,13},{3,12},{4,11},{5,10},{6,9},{7,8},{8,7},{9,6},... | collective-permute-start | bytes 786440 | tf_op jit(solution)/shard_map/ppermute | solution.py:406
  (20 other events, 233.7 us)

commit v10 on v5

--- a/solution.py
+++ b/solution.py
@@ -241,34 +241,30 @@
             position[pl.ds(pl.multiple_of(t * tile, tile), tile), :] <= sel, 0.0, HIDDEN
         ).astype(f32)
 
-        def score(g):
+        parts = [slice(n * LANES, (n + 1) * LANES) for n in range(lanes // LANES)]
+        chains = [(g, part) for g in range(KEY_VALUE_HEADS) for part in parts]
+
+        def score(chain):
+            g, part = chain
             key = kv[here, :, g * LANES : (g + 1) * LANES].reshape(tile, LANES)
-            return nt_dot(key, query[g])
-
-        upcoming = score(0)
-        for g in range(KEY_VALUE_HEADS):
-            scores = upcoming
-            if g + 1 < KEY_VALUE_HEADS:
-                upcoming = score(g + 1)
-            raised, shrinks = [], []
+            return nt_dot(key, query[g, part, :])
+
+        upcoming = score(chains[0])
+        for following, (g, part) in zip([*chains[1:], None], chains):
+            s = upcoming + bias
+            if following:
+                upcoming = score(following)
             at = KEY_VALUE_HEADS + g
-            for n in range(lanes // LANES):
-                part = slice(n * LANES, (n + 1) * LANES)
-                s = scores[:, part] + bias
-                old = stats[g : g + 1, part]
-                new = jnp.maximum(old, jnp.max(s, axis=0, keepdims=True))
-                p = jnp.exp2((s - new) * scale)
-                shrink = jnp.exp2((old - new) * scale)
-                stats[at : at + 1, part] = stats[at : at + 1, part] * shrink + jnp.sum(
-                    p, axis=0, keepdims=True
-                )
-                stats[g : g + 1, part] = new
-                raised.append(p.astype(bf16))
-                shrinks.append(shrink)
-            raised = jnp.concatenate(raised, axis=1)
-            shrink = jnp.concatenate(shrinks, axis=1)
-            mixed[g] = mixed[g] * shrink + jnp.dot(
-                values[t, g], raised, preferred_element_type=f32
+            old = stats[g : g + 1, part]
+            new = jnp.maximum(old, jnp.max(s, axis=0, keepdims=True))
+            p = jnp.exp2((s - new) * scale)
+            shrink = jnp.exp2((old - new) * scale)
+            stats[at : at + 1, part] = stats[at : at + 1, part] * shrink + jnp.sum(
+                p, axis=0, keepdims=True
+            )
+            stats[g : g + 1, part] = new
+            mixed[g, :, part] = mixed[g, :, part] * shrink + jnp.dot(
+                values[t, g], p.astype(bf16), preferred_element_type=f32
             )
         return carry
 

time: 139 us -> 142 us (1.022)
  Pallas kernels: 69.3 us -> 73.4 us
    pallas_call x3, Pallas kernels: 49.9 us -> 54 us  [attend(): pl.pallas_call(functools.partial(attend_kernel, first, last, len(contexts...]
  transfers between devices with their start and end apart: 19 -> 19, of which waited for: 8 -> 8; matrix products, arithmetic and copies ran while one was open for 5% -> 5% of each run, Pallas kernels for 40% -> 41%
where the time goes in v10:
time: 142 us; the launch traced here: 141 us
  Pallas kernels  73.4 us (52%)
  starting transfers between devices  37.7 us (27%)
  waiting for transfers between devices  18.8 us (13%)
  other arithmetic  5.27 us (4%)
  local copies, waits for them, and re-layouts  4.97 us (4%)
    pallas_call x3, Pallas kernels, attend(): pl.pallas_call(functools.partial(attend_kernel, first, last, len(contexts...  54 us
    ppermute x17, starting transfers between devices, swap(): return lax.ppermute(x, 'store', [(h, h ^ d) for h in range(holders)])  23.8 us
    ppermute x17, waiting for transfers between devices, swap(): return lax.ppermute(x, 'store', [(h, h ^ d) for h in range(holders)])  18.2 us
    all_to_all x2, starting transfers between devices, exchange(): return lax.all_to_all(x, 'store', split_axis=0, concat_axis=0, tiled=True)  13.8 us
    pallas_call x1, Pallas kernels, per_device(): pl.pallas_call(write_back_kernel, grid_spec=pltpu.PrefetchScalarGridSpec(...  8.02 us
    pallas_call x1, Pallas kernels, per_device(): pl.pallas_call(functools.partial(gather_kernel, capacity, others), grid_s...  4.89 us
  transfers between devices with their start and end apart: 19, of which 8 were waited for; matrix products, arithmetic and copies ran while one was open for 5% of the time, Pallas kernels for 41%

profile of v10, /device:TPU:9, one launch (start us, length us, event | category | flops | bytes accessed | tf_op | source)
XLA Modules:
  0.0 141.0 jit_solution(5648907505272606883)
XLA Ops:
  0.6 1.7 %shard_map.68 = (s32[16,2,128]{2,1,0:T(2,128)}, s32[1,2,128]{2,1,0:T(2,128)}, s32[1,2,128]{2,1,0:T(2,128)}) custom-call(s32[1]{0:T(128)} %bitcast.own, s32[1,128]{1,0:T(1,128)} %table_ref.2, s32[1,160]{1,0:T(1,128)} %rest_1_.2), custom_call_target="tpu_custom_call" | custom-call | tf_op jit(solution)/shard_map/pallas_call | solution.py:404
  2.3 2.3 %collective-permute-start = (s32[1,2,128]{2,1,0:T(2,128)}, s32[1,2,128]{2,1,0:T(2,128)S(1)}, u32[]{:S(2)}, u32[]{:S(2)}) collective-permute-start(s32[1,2,128]{2,1,0:T(2,128)} %get-tuple-element.49), channel_id=1, source_target_pairs={{0,8},{1,9},{2,10},{3,11},{4,12},{5,13},{6,14},{7,15},{8,0},{9,1},... | collective-permute-start | bytes 3080 | tf_op jit(solution)/shard_map/ppermute | solution.py:399
  4.6 1.2 collective-permute-done.refs_0_
  5.8 1.4 %collective-permute-done.1.refs_1_ = s32[1,2,128]{2,1,0:T(2,128)S(1)} collective-permute-done((s32[1,2,128]{2,1,0:T(2,128)}, s32[1,2,128]{2,1,0:T(2,128)S(1)}, u32[]{:S(2)}, u32[]{:S(2)}) %collective-permute-start.1) | collective-permute-done | bytes 1056 | tf_op jit(solution)/shard_map/ppermute | solution.py:399
  7.8 2.5 %shard_map.69 = (bf16[8,16,1024]{2,1,0:T(8,128)(2,1)}, bf16[8,16,1024]{2,1,0:T(8,128)(2,1)}) custom-call(s32[1,2,128]{2,1,0:T(2,128)} %copy-done.7, s32[1,2,128]{2,1,0:T(2,128)} %copy-done.8, bf16[128,16,1024]{2,1,0:T(8,128)(2,1)} %store_hbm.3), custom_call_target="tpu_custom_call" | custom-call | tf_op jit(solution)/shard_map/pallas_call | solution.py:422
  10.3 7.6 %all-to-all-start = ((s32[16,2,128]{2,1,0:T(2,128)}), s32[16,2,128]{2,1,0:T(2,128)S(1)}, u32[]{:S(2)}, u32[]{:S(2)}) async-start(s32[16,2,128]{2,1,0:T(2,128)} %get-tuple-element.54), calls=%async_computation | async-start | bytes 32768 | tf_op jit(solution)/shard_map/all_to_all | solution.py:402
  17.9 2.1 %collective-permute-start.2 = (bf16[8,16,1024]{2,1,0:T(8,128)(2,1)}, bf16[8,16,1024]{2,1,0:T(8,128)(2,1)S(1)}, u32[]{:S(2)}, u32[]{:S(2)}) collective-permute-start(bf16[8,16,1024]{2,1,0:T(8,128)(2,1)} %get-tuple-element.76), channel_id=1, source_target_pairs={{0,8},{1,9},{2,10},{3,11},{4,12},{5,13},{6,14},{7,15},{8,0},{9,1},... | collective-permute-start | bytes 786440 | tf_op jit(solution)/shard_map/ppermute | solution.py:399
  20.0 2.4 %shard_map.71 = bf16[16,16,1024]{2,1,0:T(8,128)(2,1)} custom-call(s32[1,128]{1,0:T(1,128)} %table_ref.2, s32[1,160]{1,0:T(1,128)} %rest_1_.2, bf16[160,1024]{1,0:T(8,128)(2,1)} %bitcast.70), custom_call_target="tpu_custom_call" | custom-call | tf_op jit(solution)/shard_map/pallas_call | solution.py:446
  23.5 4.9 %shard_map.70 = (bf16[8,16,1024]{2,1,0:T(8,128)(2,1)}, bf16[8,16,1024]{2,1,0:T(8,128)(2,1)}, bf16[8,16,1024]{2,1,0:T(8,128)(2,1)}, bf16[8,16,1024]{2,1,0:T(8,128...) custom-call(s32[1]{0:T(128)} %bitcast.own, ...), custom_call_target="tpu_custom_call" | custom-call | tf_op jit(solution)/shard_map/pallas_call | solution.py:455
  30.3 6.3 %all-to-all-start.1 = ((bf16[16,16,1024]{2,1,0:T(8,128)(2,1)}), bf16[16,16,1024]{2,1,0:T(8,128)(2,1)S(1)}, u32[]{:S(2)}, u32[]{:S(2)}) async-start(bf16[16,16,1024]{2,1,0:T(8,128)(2,1)} %shard_map.71), calls=%async_computation.1 | async-start | bytes 1048576 | tf_op jit(solution)/shard_map/all_to_all | solution.py:402
  36.7 1.9 %collective-permute-start.5 = (bf16[8,16,1024]{2,1,0:T(8,128)(2,1)}, bf16[8,16,1024]{2,1,0:T(8,128)(2,1)S(1)}, u32[]{:S(2)}, u32[]{:S(2)}) collective-permute-start(bf16[8,16,1024]{2,1,0:T(8,128)(2,1)} %get-tuple-element.79), channel_id=1, source_target_pairs={{0,5},{1,4},{2,7},{3,6},{4,1},{5,0},{6,3},{7,2},{8,13},{9,12},{10,... | collective-permute-start | bytes 786440 | tf_op jit(solution)/shard_map/ppermute | solution.py:399
  42.1 2.5 %collective-permute-start.7 = (bf16[8,16,1024]{2,1,0:T(8,128)(2,1)}, bf16[8,16,1024]{2,1,0:T(8,128)(2,1)S(1)}, u32[]{:S(2)}, u32[]{:S(2)}) collective-permute-start(bf16[8,16,1024]{2,1,0:T(8,128)(2,1)} %get-tuple-element.83), channel_id=1, source_target_pairs={{0,9},{1,8},{2,11},{3,10},{4,13},{5,12},{6,15},{7,14},{8,1},{9,0},... | collective-permute-start | bytes 786440 | tf_op jit(solution)/shard_map/ppermute | solution.py:399
  44.6 4.2 %collective-permute-done.3.rest_7_ = bf16[8,16,1024]{2,1,0:T(8,128)(2,1)S(1)} collective-permute-done((bf16[8,16,1024]{2,1,0:T(8,128)(2,1)}, bf16[8,16,1024]{2,1,0:T(8,128)(2,1)S(1)}, u32[]{:S(2)}, u32[]{:S(2)}) %collective-permute-start.3) | collective-permute-done | bytes 262176 | tf_op jit(solution)/shard_map/ppermute | solution.py:399
  48.8 3.3 %collective-permute-done.4.rest_8_ = bf16[8,16,1024]{2,1,0:T(8,128)(2,1)S(1)} collective-permute-done((bf16[8,16,1024]{2,1,0:T(8,128)(2,1)}, bf16[8,16,1024]{2,1,0:T(8,128)(2,1)S(1)}, u32[]{:S(2)}, u32[]{:S(2)}) %collective-permute-start.4) | collective-permute-done | bytes 262176 | tf_op jit(solution)/shard_map/ppermute | solution.py:399
  52.1 3.2 %collective-permute-start.9 = (bf16[8,16,1024]{2,1,0:T(8,128)(2,1)}, bf16[8,16,1024]{2,1,0:T(8,128)(2,1)}, u32[]{:S(2)}, u32[]{:S(2)}) collective-permute-start(bf16[8,16,1024]{2,1,0:T(8,128)(2,1)} %get-tuple-element.85), channel_id=1, source_target_pairs={{0,13},{1,12},{2,15},{3,14},{4,9},{5,8},{6,11},{7,10},{8,5},{9,4},... | collective-permute-start | bytes 786440 | tf_op jit(solution)/shard_map/ppermute | solution.py:399
  57.6 8.0 %shard_map.72 = bf16[128,16,1024]{2,1,0:T(8,128)(2,1)} custom-call(s32[16,2,128]{2,1,0:T(2,128)} %copy-done.1, s32[16,2,128]{2,1,0:T(2,128)} %copy-done.1, bf16[128,16,1024]{2,1,0:T(8,128)(2,1)} %store_hbm.3, bf16[16,16,1024]{2,1,0:T(8,128)(2,1)} %copy-done), custom_call_target="tpu_custom_call" | custom-call | bytes 8388608 | tf_op jit(solution)/shard_map/pallas_call | solution.py:476
  66.0 3.0 %collective-permute-start.11 = (bf16[8,16,1024]{2,1,0:T(8,128)(2,1)S(1)}, bf16[8,16,1024]{2,1,0:T(8,128)(2,1)}, u32[]{:S(2)}, u32[]{:S(2)}) collective-permute-start(bf16[8,16,1024]{2,1,0:T(8,128)(2,1)S(1)} %copy-done.17), channel_id=1, source_target_pairs={{0,10},{1,11},{2,8},{3,9},{4,14},{5,15},{6,12},{7,13},{8,2},{9,3},... | collective-permute-start | bytes 786440 | tf_op jit(solution)/shard_map/ppermute | solution.py:399
  69.9 2.1 %collective-permute-start.13 = (bf16[8,16,1024]{2,1,0:T(8,128)(2,1)S(1)}, bf16[8,16,1024]{2,1,0:T(8,128)(2,1)}, u32[]{:S(2)}, u32[]{:S(2)}) collective-permute-start(bf16[8,16,1024]{2,1,0:T(8,128)(2,1)S(1)} %copy-done.14), channel_id=1, source_target_pairs={{0,14},{1,15},{2,12},{3,13},{4,10},{5,11},{6,8},{7,9},{8,6},{9,7},... | collective-permute-start | bytes 786440 | tf_op jit(solution)/shard_map/ppermute | solution.py:399
  72.0 5.6 %collective-permute-done.9.rest_7_ = bf16[8,16,1024]{2,1,0:T(8,128)(2,1)} collective-permute-done((bf16[8,16,1024]{2,1,0:T(8,128)(2,1)}, bf16[8,16,1024]{2,1,0:T(8,128)(2,1)}, u32[]{:S(2)}, u32[]{:S(2)}) %collective-permute-start.9) | collective-permute-done | bytes 262176 | tf_op jit(solution)/shard_map/ppermute | solution.py:399
  79.4 22.2 %shard_map.73 = (f32[5,4,128,384]{3,2,1,0:T(8,128)}, f32[5,8,384]{2,1,0:T(8,128)}) custom-call(s32[48]{0:T(128)} %get-tuple-element.97.place, s32[48]{0:T(128)} %copy-done.10, s32[5]{0:T(128)} %fusion.7.tiles, s32[5,1,128]{2,1,0:T(1,128)} %tile.9.rest_0_, s32[1,160]{1,0:T(1,128)} %rest_1_.2, bf16[160,6144]{1,0:T(8,128)(2,1)} %bitcast.66, ...), custom_call_target="tpu_custom_call" | custom-call | flops 4831838208 | bytes 7995392 | tf_op jit(solution)/shard_map/pallas_call | solution.py:307
  102.1 4.7 %collective-permute-start.16 = (bf16[8,16,1024]{2,1,0:T(8,128)(2,1)S(1)}, bf16[8,16,1024]{2,1,0:T(8,128)(2,1)S(1)}, u32[]{:S(2)}, u32[]{:S(2)}) collective-permute-start(bf16[8,16,1024]{2,1,0:T(8,128)(2,1)S(1)} %copy-done.11), channel_id=1, source_target_pairs={{0,15},{1,14},{2,13},{3,12},{4,11},{5,10},{6,9},{7,8},{8,7},{9,6},... | collective-permute-start | bytes 786440 | tf_op jit(solution)/shard_map/ppermute | solution.py:399
  106.8 20.5 %shard_map.74 = (f32[5,4,128,384]{3,2,1,0:T(8,128)}, f32[5,8,384]{2,1,0:T(8,128)}) custom-call(s32[64]{0:T(128)} %get-tuple-element.99.place, s32[64]{0:T(128)} %copy-done.9, s32[5]{0:T(128)} %and_select_fusion.1.tiles, s32[5,1,128]{2,1,0:T(1,128)} %tile.9.rest_0_, s32[1,160]{1,0:T(1,128)} %rest_1_.2, bf16[160,6144]{1,0:T(8,128)(2,1)} %bitcast.67, ...), custom_call_target="tpu_custom_call" | custom-call | flops 4831838208 | bytes 7995392 | tf_op jit(solution)/shard_map/pallas_call | solution.py:307
  127.3 1.7 %collective-permute-done.16.rest_6_ = bf16[8,16,1024]{2,1,0:T(8,128)(2,1)S(1)} collective-permute-done((bf16[8,16,1024]{2,1,0:T(8,128)(2,1)S(1)}, bf16[8,16,1024]{2,1,0:T(8,128)(2,1)S(1)}, u32[]{:S(2)}, u32[]{:S(2)}) %collective-permute-start.16) | collective-permute-done | bytes 262176 | tf_op jit(solution)/shard_map/ppermute | solution.py:399
  129.7 11.2 %shard_map.75 = bf16[160,6144]{1,0:T(8,128)(2,1)} custom-call(s32[16]{0:T(128)} %get-tuple-element.101.place, s32[16]{0:T(128)} %copy-done.6, s32[5]{0:T(128)} %and_select_fusion.2.tiles, s32[5,1,128]{2,1,0:T(1,128)} %tile.9.rest_0_, s32[1,160]{1,0:T(1,128)} %rest_1_.2, bf16[160,6144]{1,0:T(8,128)(2,1)} %bitcast.68, ...), custom_call_target="tpu_custom_call" | custom-call | flops 1207959552 | bytes 6422528 | tf_op jit(solution)/shard_map/pallas_call | solution.py:307
  (94 shorter events, 13.4 us)
Async XLA Ops:
  2.3 3.5 %collective-permute-start = (s32[1,2,128]{2,1,0:T(2,128)}, s32[1,2,128]{2,1,0:T(2,128)S(1)}, u32[]{:S(2)}, u32[]{:S(2)}) collective-permute-start(s32[1,2,128]{2,1,0:T(2,128)} %get-tuple-element.49), channel_id=1, source_target_pairs={{0,8},{1,9},{2,10},{3,11},{4,12},{5,13},{6,14},{7,15},{8,0},{9,1},... | collective-permute-start | bytes 3080 | tf_op jit(solution)/shard_map/ppermute | solution.py:399
  4.6 2.6 %collective-permute-start.1 = (s32[1,2,128]{2,1,0:T(2,128)}, s32[1,2,128]{2,1,0:T(2,128)S(1)}, u32[]{:S(2)}, u32[]{:S(2)}) collective-permute-start(s32[1,2,128]{2,1,0:T(2,128)} %get-tuple-element.50), channel_id=1, source_target_pairs={{0,12},{1,13},{2,14},{3,15},{4,8},{5,9},{6,10},{7,11},{8,4},{9,5},... | collective-permute-start | bytes 3080 | tf_op jit(solution)/shard_map/ppermute | solution.py:399
  10.3 12.6 %all-to-all-start = ((s32[16,2,128]{2,1,0:T(2,128)}), s32[16,2,128]{2,1,0:T(2,128)S(1)}, u32[]{:S(2)}, u32[]{:S(2)}) async-start(s32[16,2,128]{2,1,0:T(2,128)} %get-tuple-element.54), calls=%async_computation | async-start | bytes 32768 | tf_op jit(solution)/shard_map/all_to_all | solution.py:402
  17.9 24.2 %collective-permute-start.2 = (bf16[8,16,1024]{2,1,0:T(8,128)(2,1)}, bf16[8,16,1024]{2,1,0:T(8,128)(2,1)S(1)}, u32[]{:S(2)}, u32[]{:S(2)}) collective-permute-start(bf16[8,16,1024]{2,1,0:T(8,128)(2,1)} %get-tuple-element.76), channel_id=1, source_target_pairs={{0,8},{1,9},{2,10},{3,11},{4,12},{5,13},{6,14},{7,15},{8,0},{9,1},... | collective-permute-start | bytes 786440 | tf_op jit(solution)/shard_map/ppermute | solution.py:399
  20.0 28.8 %collective-permute-start.3 = (bf16[8,16,1024]{2,1,0:T(8,128)(2,1)}, bf16[8,16,1024]{2,1,0:T(8,128)(2,1)S(1)}, u32[]{:S(2)}, u32[]{:S(2)}) collective-permute-start(bf16[8,16,1024]{2,1,0:T(8,128)(2,1)} %get-tuple-element.77), channel_id=1, source_target_pairs={{0,12},{1,13},{2,14},{3,15},{4,8},{5,9},{6,10},{7,11},{8,4},{9,5},... | collective-permute-start | bytes 786440 | tf_op jit(solution)/shard_map/ppermute | solution.py:399
  30.3 26.5 %all-to-all-start.1 = ((bf16[16,16,1024]{2,1,0:T(8,128)(2,1)}), bf16[16,16,1024]{2,1,0:T(8,128)(2,1)S(1)}, u32[]{:S(2)}, u32[]{:S(2)}) async-start(bf16[16,16,1024]{2,1,0:T(8,128)(2,1)} %shard_map.71), calls=%async_computation.1 | async-start | bytes 1048576 | tf_op jit(solution)/shard_map/all_to_all | solution.py:402
  36.6 15.5 %collective-permute-start.4 = (bf16[8,16,1024]{2,1,0:T(8,128)(2,1)}, bf16[8,16,1024]{2,1,0:T(8,128)(2,1)S(1)}, u32[]{:S(2)}, u32[]{:S(2)}) collective-permute-start(bf16[8,16,1024]{2,1,0:T(8,128)(2,1)} %get-tuple-element.78), channel_id=1, source_target_pairs={{0,4},{1,5},{2,6},{3,7},{4,0},{5,1},{6,2},{7,3},{8,12},{9,13},{10,... | collective-permute-start | bytes 786440 | tf_op jit(solution)/shard_map/ppermute | solution.py:399
  36.7 29.0 %collective-permute-start.5 = (bf16[8,16,1024]{2,1,0:T(8,128)(2,1)}, bf16[8,16,1024]{2,1,0:T(8,128)(2,1)S(1)}, u32[]{:S(2)}, u32[]{:S(2)}) collective-permute-start(bf16[8,16,1024]{2,1,0:T(8,128)(2,1)} %get-tuple-element.79), channel_id=1, source_target_pairs={{0,5},{1,4},{2,7},{3,6},{4,1},{5,0},{6,3},{7,2},{8,13},{9,12},{10,... | collective-permute-start | bytes 786440 | tf_op jit(solution)/shard_map/ppermute | solution.py:399
  38.6 27.4 %collective-permute-start.6 = (bf16[8,16,1024]{2,1,0:T(8,128)(2,1)}, bf16[8,16,1024]{2,1,0:T(8,128)(2,1)S(1)}, u32[]{:S(2)}, u32[]{:S(2)}) collective-permute-start(bf16[8,16,1024]{2,1,0:T(8,128)(2,1)} %get-tuple-element.80), channel_id=1, source_target_pairs={{0,1},{1,0},{2,3},{3,2},{4,5},{5,4},{6,7},{7,6},{8,9},{9,8},{10,11... | collective-permute-start | bytes 786440 | tf_op jit(solution)/shard_map/ppermute | solution.py:399
  39.4 26.3 %copy-start.10 = (s32[48]{0:T(128)}, s32[48]{0:T(128)S(1)}, u32[]{:S(2)}) copy-start(s32[48]{0:T(128)S(1)} %get-tuple-element.96.page_number) | copy-start | bytes 580
  42.1 37.3 %copy-start.16 = (bf16[8,16,1024]{2,1,0:T(8,128)(2,1)}, bf16[8,16,1024]{2,1,0:T(8,128)(2,1)S(1)}, u32[]{:S(2)}) copy-start(bf16[8,16,1024]{2,1,0:T(8,128)(2,1)S(1)} %collective-permute-done.2.rest_6_) | copy-start | bytes 786436
  42.1 26.9 %collective-permute-start.7 = (bf16[8,16,1024]{2,1,0:T(8,128)(2,1)}, bf16[8,16,1024]{2,1,0:T(8,128)(2,1)S(1)}, u32[]{:S(2)}, u32[]{:S(2)}) collective-permute-start(bf16[8,16,1024]{2,1,0:T(8,128)(2,1)} %get-tuple-element.83), channel_id=1, source_target_pairs={{0,9},{1,8},{2,11},{3,10},{4,13},{5,12},{6,15},{7,14},{8,1},{9,0},... | collective-permute-start | bytes 786440 | tf_op jit(solution)/shard_map/ppermute | solution.py:399
  48.8 30.6 %copy-start.18 = (bf16[8,16,1024]{2,1,0:T(8,128)(2,1)}, bf16[8,16,1024]{2,1,0:T(8,128)(2,1)S(1)}, u32[]{:S(2)}) copy-start(bf16[8,16,1024]{2,1,0:T(8,128)(2,1)S(1)} %collective-permute-done.3.rest_7_) | copy-start | bytes 786436
  48.8 21.1 %collective-permute-start.8 = (bf16[8,16,1024]{2,1,0:T(8,128)(2,1)}, bf16[8,16,1024]{2,1,0:T(8,128)(2,1)}, u32[]{:S(2)}, u32[]{:S(2)}) collective-permute-start(bf16[8,16,1024]{2,1,0:T(8,128)(2,1)} %get-tuple-element.84), channel_id=1, source_target_pairs={{0,6},{1,7},{2,4},{3,5},{4,2},{5,3},{6,0},{7,1},{8,14},{9,15},{10,... | collective-permute-start | bytes 786440 | tf_op jit(solution)/shard_map/ppermute | solution.py:399
  52.1 27.3 %copy-start.20 = (bf16[8,16,1024]{2,1,0:T(8,128)(2,1)}, bf16[8,16,1024]{2,1,0:T(8,128)(2,1)S(1)}, u32[]{:S(2)}) copy-start(bf16[8,16,1024]{2,1,0:T(8,128)(2,1)S(1)} %collective-permute-done.4.rest_8_) | copy-start | bytes 786436
  52.1 25.5 %collective-permute-start.9 = (bf16[8,16,1024]{2,1,0:T(8,128)(2,1)}, bf16[8,16,1024]{2,1,0:T(8,128)(2,1)}, u32[]{:S(2)}, u32[]{:S(2)}) collective-permute-start(bf16[8,16,1024]{2,1,0:T(8,128)(2,1)} %get-tuple-element.85), channel_id=1, source_target_pairs={{0,13},{1,12},{2,15},{3,14},{4,9},{5,8},{6,11},{7,10},{8,5},{9,4},... | collective-permute-start | bytes 786440 | tf_op jit(solution)/shard_map/ppermute | solution.py:399
  65.7 36.0 %collective-permute-start.10 = (bf16[8,16,1024]{2,1,0:T(8,128)(2,1)S(1)}, bf16[8,16,1024]{2,1,0:T(8,128)(2,1)}, u32[]{:S(2)}, u32[]{:S(2)}) collective-permute-start(bf16[8,16,1024]{2,1,0:T(8,128)(2,1)S(1)} %copy-done.19), channel_id=1, source_target_pairs={{0,7},{1,6},{2,5},{3,4},{4,3},{5,2},{6,1},{7,0},{8,15},{9,14},{10,... | collective-permute-start | bytes 786440 | tf_op jit(solution)/shard_map/ppermute | solution.py:399
  66.0 36.1 %collective-permute-start.11 = (bf16[8,16,1024]{2,1,0:T(8,128)(2,1)S(1)}, bf16[8,16,1024]{2,1,0:T(8,128)(2,1)}, u32[]{:S(2)}, u32[]{:S(2)}) collective-permute-start(bf16[8,16,1024]{2,1,0:T(8,128)(2,1)S(1)} %copy-done.17), channel_id=1, source_target_pairs={{0,10},{1,11},{2,8},{3,9},{4,14},{5,15},{6,12},{7,13},{8,2},{9,3},... | collective-permute-start | bytes 786440 | tf_op jit(solution)/shard_map/ppermute | solution.py:399
  69.0 32.6 %copy-start.22 = (bf16[8,16,1024]{2,1,0:T(8,128)(2,1)}, bf16[8,16,1024]{2,1,0:T(8,128)(2,1)S(1)}, u32[]{:S(2)}) copy-start(bf16[8,16,1024]{2,1,0:T(8,128)(2,1)S(1)} %collective-permute-done.7.rest_5_) | copy-start | bytes 786436
  69.0 37.8 %collective-permute-start.12 = (bf16[8,16,1024]{2,1,0:T(8,128)(2,1)S(1)}, bf16[8,16,1024]{2,1,0:T(8,128)(2,1)}, u32[]{:S(2)}, u32[]{:S(2)}) collective-permute-start(bf16[8,16,1024]{2,1,0:T(8,128)(2,1)S(1)} %copy-done.15), channel_id=1, source_target_pairs={{0,2},{1,3},{2,0},{3,1},{4,6},{5,7},{6,4},{7,5},{8,10},{9,11},{10,... | collective-permute-start | bytes 786440 | tf_op jit(solution)/shard_map/ppermute | solution.py:399
  69.9 37.0 %collective-permute-start.13 = (bf16[8,16,1024]{2,1,0:T(8,128)(2,1)S(1)}, bf16[8,16,1024]{2,1,0:T(8,128)(2,1)}, u32[]{:S(2)}, u32[]{:S(2)}) collective-permute-start(bf16[8,16,1024]{2,1,0:T(8,128)(2,1)S(1)} %copy-done.14), channel_id=1, source_target_pairs={{0,14},{1,15},{2,12},{3,13},{4,10},{5,11},{6,8},{7,9},{8,6},{9,7},... | collective-permute-start | bytes 786440 | tf_op jit(solution)/shard_map/ppermute | solution.py:399
  77.6 29.2 %collective-permute-start.14 = (bf16[8,16,1024]{2,1,0:T(8,128)(2,1)S(1)}, bf16[8,16,1024]{2,1,0:T(8,128)(2,1)}, u32[]{:S(2)}, u32[]{:S(2)}) collective-permute-start(bf16[8,16,1024]{2,1,0:T(8,128)(2,1)S(1)} %copy-done.13), channel_id=1, source_target_pairs={{0,3},{1,2},{2,1},{3,0},{4,7},{5,6},{6,5},{7,4},{8,11},{9,10},{10,... | collective-permute-start | bytes 786440 | tf_op jit(solution)/shard_map/ppermute | solution.py:399
  101.7 25.6 %collective-permute-start.15 = (bf16[8,16,1024]{2,1,0:T(8,128)(2,1)S(1)}, bf16[8,16,1024]{2,1,0:T(8,128)(2,1)S(1)}, u32[]{:S(2)}, u32[]{:S(2)}) collective-permute-start(bf16[8,16,1024]{2,1,0:T(8,128)(2,1)S(1)} %copy-done.12), channel_id=1, source_target_pairs={{0,11},{1,10},{2,9},{3,8},{4,15},{5,14},{6,13},{7,12},{8,3},{9,2},... | collective-permute-start | bytes 786440 | tf_op jit(solution)/shard_map/ppermute | solution.py:399
  102.1 27.0 %collective-permute-start.16 = (bf16[8,16,1024]{2,1,0:T(8,128)(2,1)S(1)}, bf16[8,16,1024]{2,1,0:T(8,128)(2,1)S(1)}, u32[]{:S(2)}, u32[]{:S(2)}) collective-permute-start(bf16[8,16,1024]{2,1,0:T(8,128)(2,1)S(1)} %copy-done.11), channel_id=1, source_target_pairs={{0,15},{1,14},{2,13},{3,12},{4,11},{5,10},{6,9},{7,8},{8,7},{9,6},... | collective-permute-start | bytes 786440 | tf_op jit(solution)/shard_map/ppermute | solution.py:399
  (19 other events, 241.2 us)

commit v11 on v5

--- a/solution.py
+++ b/solution.py
@@ -172,7 +172,7 @@
     block = query_ref.shape[0]
     tile = TILE_PAGES * page_len
     lanes = QUERY_GROUP * block
-    scale = 1.4426950408889634 / HEAD_WIDTH**0.5
+    scale = 1.0 / HEAD_WIDTH**0.5
     f32 = jnp.float32
     bf16 = jnp.bfloat16
     step = pl.program_id(0)
@@ -257,8 +257,8 @@
                 s = scores[:, part] + bias
                 old = stats[g : g + 1, part]
                 new = jnp.maximum(old, jnp.max(s, axis=0, keepdims=True))
-                p = jnp.exp2((s - new) * scale)
-                shrink = jnp.exp2((old - new) * scale)
+                p = jnp.exp((s - new) * scale)
+                shrink = jnp.exp((old - new) * scale)
                 stats[at : at + 1, part] = stats[at : at + 1, part] * shrink + jnp.sum(
                     p, axis=0, keepdims=True
                 )
@@ -392,7 +392,7 @@
     wide = pltpu.VMEM((8, -(-picked // LANES) * LANES), jnp.int32)
     if holders == 16:
         first = (8, 12)
-        groups = [(0, 8, 12, 4, 5, 1), (9, 6, 13, 7, 10, 2, 14, 3), (11, 15)]
+        groups = [(0, 8, 12, 4, 5, 1), (9, 6, 7, 13, 2, 10, 3, 14), (11, 15)]
         others = [d for group in groups for d in group if d not in first]
     else:
         first = ()

time: 139 us -> 149 us (1.072)
  waiting for transfers between devices: 19.5 us -> 23.4 us
  Pallas kernels: 69.3 us -> 72.4 us
  starting transfers between devices: 37.7 us -> 40.5 us
    ppermute x17, waiting for transfers between devices: 18.9 us -> 22.8 us  [swap(): return lax.ppermute(x, 'store', [(h, h ^ d) for h in range(holders)])]
    pallas_call x3, Pallas kernels: 49.9 us -> 53 us  [attend(): pl.pallas_call(functools.partial(attend_kernel, first, last, len(contexts...]
    ppermute x17, starting transfers between devices: 23.8 us -> 26.7 us  [swap(): return lax.ppermute(x, 'store', [(h, h ^ d) for h in range(holders)])]
  transfers between devices with their start and end apart: 19 -> 19, of which waited for: 8 -> 7; matrix products, arithmetic and copies ran while one was open for 5% -> 5% of each run, Pallas kernels for 40% -> 39%
where the time goes in v11:
time: 149 us; the launch traced here: 147 us
  Pallas kernels  72.4 us (49%)
  starting transfers between devices  40.5 us (27%)
  waiting for transfers between devices  23.4 us (16%)
  other arithmetic  5.27 us (4%)
  local copies, waits for them, and re-layouts  4.97 us (3%)
    pallas_call x3, Pallas kernels, attend(): pl.pallas_call(functools.partial(attend_kernel, first, last, len(contexts...  53 us
    ppermute x17, starting transfers between devices, swap(): return lax.ppermute(x, 'store', [(h, h ^ d) for h in range(holders)])  26.7 us
    ppermute x17, waiting for transfers between devices, swap(): return lax.ppermute(x, 'store', [(h, h ^ d) for h in range(holders)])  22.8 us
    all_to_all x2, starting transfers between devices, exchange(): return lax.all_to_all(x, 'store', split_axis=0, concat_axis=0, tiled=True)  13.8 us
    pallas_call x1, Pallas kernels, per_device(): pl.pallas_call(write_back_kernel, grid_spec=pltpu.PrefetchScalarGridSpec(...  8.02 us
    pallas_call x1, Pallas kernels, per_device(): pl.pallas_call(functools.partial(gather_kernel, capacity, others), grid_s...  4.89 us
  transfers between devices with their start and end apart: 19, of which 7 were waited for; matrix products, arithmetic and copies ran while one was open for 5% of the time, Pallas kernels for 39%

profile of v11, /device:TPU:9, one launch (start us, length us, event | category | flops | bytes accessed | tf_op | source)
XLA Modules:
  0.0 147.5 jit_solution(13754215683311407546)
XLA Ops:
  0.6 1.7 %shard_map.68 = (s32[16,2,128]{2,1,0:T(2,128)}, s32[1,2,128]{2,1,0:T(2,128)}, s32[1,2,128]{2,1,0:T(2,128)}) custom-call(s32[1]{0:T(128)} %bitcast.own, s32[1,128]{1,0:T(1,128)} %table_ref.2, s32[1,160]{1,0:T(1,128)} %rest_1_.2), custom_call_target="tpu_custom_call" | custom-call | tf_op jit(solution)/shard_map/pallas_call | solution.py:408
  2.3 2.3 %collective-permute-start = (s32[1,2,128]{2,1,0:T(2,128)}, s32[1,2,128]{2,1,0:T(2,128)S(1)}, u32[]{:S(2)}, u32[]{:S(2)}) collective-permute-start(s32[1,2,128]{2,1,0:T(2,128)} %get-tuple-element.49), channel_id=1, source_target_pairs={{0,8},{1,9},{2,10},{3,11},{4,12},{5,13},{6,14},{7,15},{8,0},{9,1},... | collective-permute-start | bytes 3080 | tf_op jit(solution)/shard_map/ppermute | solution.py:403
  4.6 1.2 collective-permute-done.refs_0_
  5.8 1.4 collective-permute-done.1.refs_1_
  7.8 2.5 %shard_map.69 = (bf16[8,16,1024]{2,1,0:T(8,128)(2,1)}, bf16[8,16,1024]{2,1,0:T(8,128)(2,1)}) custom-call(s32[1,2,128]{2,1,0:T(2,128)} %copy-done.7, s32[1,2,128]{2,1,0:T(2,128)} %copy-done.8, bf16[128,16,1024]{2,1,0:T(8,128)(2,1)} %store_hbm.3), custom_call_target="tpu_custom_call" | custom-call | tf_op jit(solution)/shard_map/pallas_call | solution.py:426
  10.3 7.6 %all-to-all-start = ((s32[16,2,128]{2,1,0:T(2,128)}), s32[16,2,128]{2,1,0:T(2,128)S(1)}, u32[]{:S(2)}, u32[]{:S(2)}) async-start(s32[16,2,128]{2,1,0:T(2,128)} %get-tuple-element.54), calls=%async_computation | async-start | bytes 32768 | tf_op jit(solution)/shard_map/all_to_all | solution.py:406
  17.9 2.1 %collective-permute-start.2 = (bf16[8,16,1024]{2,1,0:T(8,128)(2,1)}, bf16[8,16,1024]{2,1,0:T(8,128)(2,1)S(1)}, u32[]{:S(2)}, u32[]{:S(2)}) collective-permute-start(bf16[8,16,1024]{2,1,0:T(8,128)(2,1)} %get-tuple-element.76), channel_id=1, source_target_pairs={{0,8},{1,9},{2,10},{3,11},{4,12},{5,13},{6,14},{7,15},{8,0},{9,1},... | collective-permute-start | bytes 786440 | tf_op jit(solution)/shard_map/ppermute | solution.py:403
  20.0 2.4 %shard_map.71 = bf16[16,16,1024]{2,1,0:T(8,128)(2,1)} custom-call(s32[1,128]{1,0:T(1,128)} %table_ref.2, s32[1,160]{1,0:T(1,128)} %rest_1_.2, bf16[160,1024]{1,0:T(8,128)(2,1)} %bitcast.70), custom_call_target="tpu_custom_call" | custom-call | tf_op jit(solution)/shard_map/pallas_call | solution.py:450
  23.5 4.9 %shard_map.70 = (bf16[8,16,1024]{2,1,0:T(8,128)(2,1)}, bf16[8,16,1024]{2,1,0:T(8,128)(2,1)}, bf16[8,16,1024]{2,1,0:T(8,128)(2,1)}, bf16[8,16,1024]{2,1,0:T(8,128...) custom-call(s32[1]{0:T(128)} %bitcast.own, ...), custom_call_target="tpu_custom_call" | custom-call | tf_op jit(solution)/shard_map/pallas_call | solution.py:459
  30.3 6.3 %all-to-all-start.1 = ((bf16[16,16,1024]{2,1,0:T(8,128)(2,1)}), bf16[16,16,1024]{2,1,0:T(8,128)(2,1)S(1)}, u32[]{:S(2)}, u32[]{:S(2)}) async-start(bf16[16,16,1024]{2,1,0:T(8,128)(2,1)} %shard_map.71), calls=%async_computation.1 | async-start | bytes 1048576 | tf_op jit(solution)/shard_map/all_to_all | solution.py:406
  36.7 1.9 %collective-permute-start.5 = (bf16[8,16,1024]{2,1,0:T(8,128)(2,1)}, bf16[8,16,1024]{2,1,0:T(8,128)(2,1)S(1)}, u32[]{:S(2)}, u32[]{:S(2)}) collective-permute-start(bf16[8,16,1024]{2,1,0:T(8,128)(2,1)} %get-tuple-element.79), channel_id=1, source_target_pairs={{0,5},{1,4},{2,7},{3,6},{4,1},{5,0},{6,3},{7,2},{8,13},{9,12},{10,... | collective-permute-start | bytes 786440 | tf_op jit(solution)/shard_map/ppermute | solution.py:403
  42.1 2.5 %collective-permute-start.7 = (bf16[8,16,1024]{2,1,0:T(8,128)(2,1)}, bf16[8,16,1024]{2,1,0:T(8,128)(2,1)S(1)}, u32[]{:S(2)}, u32[]{:S(2)}) collective-permute-start(bf16[8,16,1024]{2,1,0:T(8,128)(2,1)} %get-tuple-element.83), channel_id=1, source_target_pairs={{0,9},{1,8},{2,11},{3,10},{4,13},{5,12},{6,15},{7,14},{8,1},{9,0},... | collective-permute-start | bytes 786440 | tf_op jit(solution)/shard_map/ppermute | solution.py:403
  44.6 4.2 %collective-permute-done.3.rest_7_ = bf16[8,16,1024]{2,1,0:T(8,128)(2,1)S(1)} collective-permute-done((bf16[8,16,1024]{2,1,0:T(8,128)(2,1)}, bf16[8,16,1024]{2,1,0:T(8,128)(2,1)S(1)}, u32[]{:S(2)}, u32[]{:S(2)}) %collective-permute-start.3) | collective-permute-done | bytes 262176 | tf_op jit(solution)/shard_map/ppermute | solution.py:403
  48.8 3.3 %collective-permute-done.4.rest_8_ = bf16[8,16,1024]{2,1,0:T(8,128)(2,1)S(1)} collective-permute-done((bf16[8,16,1024]{2,1,0:T(8,128)(2,1)}, bf16[8,16,1024]{2,1,0:T(8,128)(2,1)S(1)}, u32[]{:S(2)}, u32[]{:S(2)}) %collective-permute-start.4) | collective-permute-done | bytes 262176 | tf_op jit(solution)/shard_map/ppermute | solution.py:403
  52.1 1.8 %collective-permute-start.9 = (bf16[8,16,1024]{2,1,0:T(8,128)(2,1)}, bf16[8,16,1024]{2,1,0:T(8,128)(2,1)}, u32[]{:S(2)}, u32[]{:S(2)}) collective-permute-start(bf16[8,16,1024]{2,1,0:T(8,128)(2,1)} %get-tuple-element.85), channel_id=1, source_target_pairs={{0,7},{1,6},{2,5},{3,4},{4,3},{5,2},{6,1},{7,0},{8,15},{9,14},{10,... | collective-permute-start | bytes 786440 | tf_op jit(solution)/shard_map/ppermute | solution.py:403
  56.2 8.0 %shard_map.72 = bf16[128,16,1024]{2,1,0:T(8,128)(2,1)} custom-call(s32[16,2,128]{2,1,0:T(2,128)} %copy-done.1, s32[16,2,128]{2,1,0:T(2,128)} %copy-done.1, bf16[128,16,1024]{2,1,0:T(8,128)(2,1)} %store_hbm.3, bf16[16,16,1024]{2,1,0:T(8,128)(2,1)} %copy-done), custom_call_target="tpu_custom_call" | custom-call | bytes 8388608 | tf_op jit(solution)/shard_map/pallas_call | solution.py:480
  64.3 2.6 %collective-permute-start.10 = (bf16[8,16,1024]{2,1,0:T(8,128)(2,1)S(1)}, bf16[8,16,1024]{2,1,0:T(8,128)(2,1)}, u32[]{:S(2)}, u32[]{:S(2)}) collective-permute-start(bf16[8,16,1024]{2,1,0:T(8,128)(2,1)S(1)} %copy-done.19), channel_id=1, source_target_pairs={{0,13},{1,12},{2,15},{3,14},{4,9},{5,8},{6,11},{7,10},{8,5},{9,4},... | collective-permute-start | bytes 786440 | tf_op jit(solution)/shard_map/ppermute | solution.py:403
  67.0 2.9 %collective-permute-start.12 = (bf16[8,16,1024]{2,1,0:T(8,128)(2,1)S(1)}, bf16[8,16,1024]{2,1,0:T(8,128)(2,1)}, u32[]{:S(2)}, u32[]{:S(2)}) collective-permute-start(bf16[8,16,1024]{2,1,0:T(8,128)(2,1)S(1)} %copy-done.15), channel_id=1, source_target_pairs={{0,10},{1,11},{2,8},{3,9},{4,14},{5,15},{6,12},{7,13},{8,2},{9,3},... | collective-permute-start | bytes 786440 | tf_op jit(solution)/shard_map/ppermute | solution.py:403
  69.9 1.1 collective-permute-start.13
  71.0 11.5 %collective-permute-done.9.rest_7_ = bf16[8,16,1024]{2,1,0:T(8,128)(2,1)} collective-permute-done((bf16[8,16,1024]{2,1,0:T(8,128)(2,1)}, bf16[8,16,1024]{2,1,0:T(8,128)(2,1)}, u32[]{:S(2)}, u32[]{:S(2)}) %collective-permute-start.9) | collective-permute-done | bytes 262176 | tf_op jit(solution)/shard_map/ppermute | solution.py:403
  84.4 21.7 %shard_map.73 = (f32[5,4,128,384]{3,2,1,0:T(8,128)}, f32[5,8,384]{2,1,0:T(8,128)}) custom-call(s32[48]{0:T(128)} %get-tuple-element.97.place, s32[48]{0:T(128)} %copy-done.10, s32[5]{0:T(128)} %fusion.7.tiles, s32[5,1,128]{2,1,0:T(1,128)} %tile.9.rest_0_, s32[1,160]{1,0:T(1,128)} %rest_1_.2, bf16[160,6144]{1,0:T(8,128)(2,1)} %bitcast.66, ...), custom_call_target="tpu_custom_call" | custom-call | flops 4831838208 | bytes 7995392 | tf_op jit(solution)/shard_map/pallas_call | solution.py:311
  106.2 8.2 %collective-permute-start.15 = (bf16[8,16,1024]{2,1,0:T(8,128)(2,1)S(1)}, bf16[8,16,1024]{2,1,0:T(8,128)(2,1)S(1)}, u32[]{:S(2)}, u32[]{:S(2)}) collective-permute-start(bf16[8,16,1024]{2,1,0:T(8,128)(2,1)S(1)} %copy-done.12), channel_id=1, source_target_pairs={{0,11},{1,10},{2,9},{3,8},{4,15},{5,14},{6,13},{7,12},{8,3},{9,2},... | collective-permute-start | bytes 786440 | tf_op jit(solution)/shard_map/ppermute | solution.py:403
  114.4 20.1 %shard_map.74 = (f32[5,4,128,384]{3,2,1,0:T(8,128)}, f32[5,8,384]{2,1,0:T(8,128)}) custom-call(s32[64]{0:T(128)} %get-tuple-element.99.place, s32[64]{0:T(128)} %copy-done.9, s32[5]{0:T(128)} %and_select_fusion.1.tiles, s32[5,1,128]{2,1,0:T(1,128)} %tile.9.rest_0_, s32[1,160]{1,0:T(1,128)} %rest_1_.2, bf16[160,6144]{1,0:T(8,128)(2,1)} %bitcast.67, ...), custom_call_target="tpu_custom_call" | custom-call | flops 4831838208 | bytes 7995392 | tf_op jit(solution)/shard_map/pallas_call | solution.py:311
  136.3 11.1 %shard_map.75 = bf16[160,6144]{1,0:T(8,128)(2,1)} custom-call(s32[16]{0:T(128)} %get-tuple-element.101.place, s32[16]{0:T(128)} %copy-done.6, s32[5]{0:T(128)} %and_select_fusion.2.tiles, s32[5,1,128]{2,1,0:T(1,128)} %tile.9.rest_0_, s32[1,160]{1,0:T(1,128)} %rest_1_.2, bf16[160,6144]{1,0:T(8,128)(2,1)} %bitcast.68, ...), custom_call_target="tpu_custom_call" | custom-call | flops 1207959552 | bytes 6422528 | tf_op jit(solution)/shard_map/pallas_call | solution.py:311
  (94 shorter events, 13.2 us)
Async XLA Ops:
  2.3 3.5 %collective-permute-start = (s32[1,2,128]{2,1,0:T(2,128)}, s32[1,2,128]{2,1,0:T(2,128)S(1)}, u32[]{:S(2)}, u32[]{:S(2)}) collective-permute-start(s32[1,2,128]{2,1,0:T(2,128)} %get-tuple-element.49), channel_id=1, source_target_pairs={{0,8},{1,9},{2,10},{3,11},{4,12},{5,13},{6,14},{7,15},{8,0},{9,1},... | collective-permute-start | bytes 3080 | tf_op jit(solution)/shard_map/ppermute | solution.py:403
  4.6 2.6 %collective-permute-start.1 = (s32[1,2,128]{2,1,0:T(2,128)}, s32[1,2,128]{2,1,0:T(2,128)S(1)}, u32[]{:S(2)}, u32[]{:S(2)}) collective-permute-start(s32[1,2,128]{2,1,0:T(2,128)} %get-tuple-element.50), channel_id=1, source_target_pairs={{0,12},{1,13},{2,14},{3,15},{4,8},{5,9},{6,10},{7,11},{8,4},{9,5},... | collective-permute-start | bytes 3080 | tf_op jit(solution)/shard_map/ppermute | solution.py:403
  10.3 12.6 %all-to-all-start = ((s32[16,2,128]{2,1,0:T(2,128)}), s32[16,2,128]{2,1,0:T(2,128)S(1)}, u32[]{:S(2)}, u32[]{:S(2)}) async-start(s32[16,2,128]{2,1,0:T(2,128)} %get-tuple-element.54), calls=%async_computation | async-start | bytes 32768 | tf_op jit(solution)/shard_map/all_to_all | solution.py:406
  17.9 24.2 %collective-permute-start.2 = (bf16[8,16,1024]{2,1,0:T(8,128)(2,1)}, bf16[8,16,1024]{2,1,0:T(8,128)(2,1)S(1)}, u32[]{:S(2)}, u32[]{:S(2)}) collective-permute-start(bf16[8,16,1024]{2,1,0:T(8,128)(2,1)} %get-tuple-element.76), channel_id=1, source_target_pairs={{0,8},{1,9},{2,10},{3,11},{4,12},{5,13},{6,14},{7,15},{8,0},{9,1},... | collective-permute-start | bytes 786440 | tf_op jit(solution)/shard_map/ppermute | solution.py:403
  20.0 28.8 %collective-permute-start.3 = (bf16[8,16,1024]{2,1,0:T(8,128)(2,1)}, bf16[8,16,1024]{2,1,0:T(8,128)(2,1)S(1)}, u32[]{:S(2)}, u32[]{:S(2)}) collective-permute-start(bf16[8,16,1024]{2,1,0:T(8,128)(2,1)} %get-tuple-element.77), channel_id=1, source_target_pairs={{0,12},{1,13},{2,14},{3,15},{4,8},{5,9},{6,10},{7,11},{8,4},{9,5},... | collective-permute-start | bytes 786440 | tf_op jit(solution)/shard_map/ppermute | solution.py:403
  30.3 25.1 %all-to-all-start.1 = ((bf16[16,16,1024]{2,1,0:T(8,128)(2,1)}), bf16[16,16,1024]{2,1,0:T(8,128)(2,1)S(1)}, u32[]{:S(2)}, u32[]{:S(2)}) async-start(bf16[16,16,1024]{2,1,0:T(8,128)(2,1)} %shard_map.71), calls=%async_computation.1 | async-start | bytes 1048576 | tf_op jit(solution)/shard_map/all_to_all | solution.py:406
  36.6 15.5 %collective-permute-start.4 = (bf16[8,16,1024]{2,1,0:T(8,128)(2,1)}, bf16[8,16,1024]{2,1,0:T(8,128)(2,1)S(1)}, u32[]{:S(2)}, u32[]{:S(2)}) collective-permute-start(bf16[8,16,1024]{2,1,0:T(8,128)(2,1)} %get-tuple-element.78), channel_id=1, source_target_pairs={{0,4},{1,5},{2,6},{3,7},{4,0},{5,1},{6,2},{7,3},{8,12},{9,13},{10,... | collective-permute-start | bytes 786440 | tf_op jit(solution)/shard_map/ppermute | solution.py:403
  36.7 27.6 %collective-permute-start.5 = (bf16[8,16,1024]{2,1,0:T(8,128)(2,1)}, bf16[8,16,1024]{2,1,0:T(8,128)(2,1)S(1)}, u32[]{:S(2)}, u32[]{:S(2)}) collective-permute-start(bf16[8,16,1024]{2,1,0:T(8,128)(2,1)} %get-tuple-element.79), channel_id=1, source_target_pairs={{0,5},{1,4},{2,7},{3,6},{4,1},{5,0},{6,3},{7,2},{8,13},{9,12},{10,... | collective-permute-start | bytes 786440 | tf_op jit(solution)/shard_map/ppermute | solution.py:403
  38.6 28.3 %collective-permute-start.6 = (bf16[8,16,1024]{2,1,0:T(8,128)(2,1)}, bf16[8,16,1024]{2,1,0:T(8,128)(2,1)S(1)}, u32[]{:S(2)}, u32[]{:S(2)}) collective-permute-start(bf16[8,16,1024]{2,1,0:T(8,128)(2,1)} %get-tuple-element.80), channel_id=1, source_target_pairs={{0,1},{1,0},{2,3},{3,2},{4,5},{5,4},{6,7},{7,6},{8,9},{9,8},{10,11... | collective-permute-start | bytes 786440 | tf_op jit(solution)/shard_map/ppermute | solution.py:403
  42.1 42.3 %copy-start.16 = (bf16[8,16,1024]{2,1,0:T(8,128)(2,1)}, bf16[8,16,1024]{2,1,0:T(8,128)(2,1)S(1)}, u32[]{:S(2)}) copy-start(bf16[8,16,1024]{2,1,0:T(8,128)(2,1)S(1)} %collective-permute-done.2.rest_6_) | copy-start | bytes 786436
  42.1 24.9 %collective-permute-start.7 = (bf16[8,16,1024]{2,1,0:T(8,128)(2,1)}, bf16[8,16,1024]{2,1,0:T(8,128)(2,1)S(1)}, u32[]{:S(2)}, u32[]{:S(2)}) collective-permute-start(bf16[8,16,1024]{2,1,0:T(8,128)(2,1)} %get-tuple-element.83), channel_id=1, source_target_pairs={{0,9},{1,8},{2,11},{3,10},{4,13},{5,12},{6,15},{7,14},{8,1},{9,0},... | collective-permute-start | bytes 786440 | tf_op jit(solution)/shard_map/ppermute | solution.py:403
  48.8 35.6 %copy-start.18 = (bf16[8,16,1024]{2,1,0:T(8,128)(2,1)}, bf16[8,16,1024]{2,1,0:T(8,128)(2,1)S(1)}, u32[]{:S(2)}) copy-start(bf16[8,16,1024]{2,1,0:T(8,128)(2,1)S(1)} %collective-permute-done.3.rest_7_) | copy-start | bytes 786436
  48.8 21.1 %collective-permute-start.8 = (bf16[8,16,1024]{2,1,0:T(8,128)(2,1)}, bf16[8,16,1024]{2,1,0:T(8,128)(2,1)}, u32[]{:S(2)}, u32[]{:S(2)}) collective-permute-start(bf16[8,16,1024]{2,1,0:T(8,128)(2,1)} %get-tuple-element.84), channel_id=1, source_target_pairs={{0,6},{1,7},{2,4},{3,5},{4,2},{5,3},{6,0},{7,1},{8,14},{9,15},{10,... | collective-permute-start | bytes 786440 | tf_op jit(solution)/shard_map/ppermute | solution.py:403
  52.1 32.3 %copy-start.20 = (bf16[8,16,1024]{2,1,0:T(8,128)(2,1)}, bf16[8,16,1024]{2,1,0:T(8,128)(2,1)S(1)}, u32[]{:S(2)}) copy-start(bf16[8,16,1024]{2,1,0:T(8,128)(2,1)S(1)} %collective-permute-done.4.rest_8_) | copy-start | bytes 786436
  52.1 30.5 %collective-permute-start.9 = (bf16[8,16,1024]{2,1,0:T(8,128)(2,1)}, bf16[8,16,1024]{2,1,0:T(8,128)(2,1)}, u32[]{:S(2)}, u32[]{:S(2)}) collective-permute-start(bf16[8,16,1024]{2,1,0:T(8,128)(2,1)} %get-tuple-element.85), channel_id=1, source_target_pairs={{0,7},{1,6},{2,5},{3,4},{4,3},{5,2},{6,1},{7,0},{8,15},{9,14},{10,... | collective-permute-start | bytes 786440 | tf_op jit(solution)/shard_map/ppermute | solution.py:403
  64.3 41.9 %collective-permute-start.10 = (bf16[8,16,1024]{2,1,0:T(8,128)(2,1)S(1)}, bf16[8,16,1024]{2,1,0:T(8,128)(2,1)}, u32[]{:S(2)}, u32[]{:S(2)}) collective-permute-start(bf16[8,16,1024]{2,1,0:T(8,128)(2,1)S(1)} %copy-done.19), channel_id=1, source_target_pairs={{0,13},{1,12},{2,15},{3,14},{4,9},{5,8},{6,11},{7,10},{8,5},{9,4},... | collective-permute-start | bytes 786440 | tf_op jit(solution)/shard_map/ppermute | solution.py:403
  66.9 47.5 %collective-permute-start.11 = (bf16[8,16,1024]{2,1,0:T(8,128)(2,1)S(1)}, bf16[8,16,1024]{2,1,0:T(8,128)(2,1)}, u32[]{:S(2)}, u32[]{:S(2)}) collective-permute-start(bf16[8,16,1024]{2,1,0:T(8,128)(2,1)S(1)} %copy-done.17), channel_id=1, source_target_pairs={{0,2},{1,3},{2,0},{3,1},{4,6},{5,7},{6,4},{7,5},{8,10},{9,11},{10,... | collective-permute-start | bytes 786440 | tf_op jit(solution)/shard_map/ppermute | solution.py:403
  67.0 39.1 %copy-start.22 = (bf16[8,16,1024]{2,1,0:T(8,128)(2,1)}, bf16[8,16,1024]{2,1,0:T(8,128)(2,1)S(1)}, u32[]{:S(2)}) copy-start(bf16[8,16,1024]{2,1,0:T(8,128)(2,1)S(1)} %collective-permute-done.7.rest_5_) | copy-start | bytes 786436
  67.0 47.3 %collective-permute-start.12 = (bf16[8,16,1024]{2,1,0:T(8,128)(2,1)S(1)}, bf16[8,16,1024]{2,1,0:T(8,128)(2,1)}, u32[]{:S(2)}, u32[]{:S(2)}) collective-permute-start(bf16[8,16,1024]{2,1,0:T(8,128)(2,1)S(1)} %copy-done.15), channel_id=1, source_target_pairs={{0,10},{1,11},{2,8},{3,9},{4,14},{5,15},{6,12},{7,13},{8,2},{9,3},... | collective-permute-start | bytes 786440 | tf_op jit(solution)/shard_map/ppermute | solution.py:403
  69.9 44.5 %collective-permute-start.13 = (bf16[8,16,1024]{2,1,0:T(8,128)(2,1)S(1)}, bf16[8,16,1024]{2,1,0:T(8,128)(2,1)}, u32[]{:S(2)}, u32[]{:S(2)}) collective-permute-start(bf16[8,16,1024]{2,1,0:T(8,128)(2,1)S(1)} %copy-done.14), channel_id=1, source_target_pairs={{0,3},{1,2},{2,1},{3,0},{4,7},{5,6},{6,5},{7,4},{8,11},{9,10},{10,... | collective-permute-start | bytes 786440 | tf_op jit(solution)/shard_map/ppermute | solution.py:403
  82.6 31.8 %collective-permute-start.14 = (bf16[8,16,1024]{2,1,0:T(8,128)(2,1)S(1)}, bf16[8,16,1024]{2,1,0:T(8,128)(2,1)}, u32[]{:S(2)}, u32[]{:S(2)}) collective-permute-start(bf16[8,16,1024]{2,1,0:T(8,128)(2,1)S(1)} %copy-done.13), channel_id=1, source_target_pairs={{0,14},{1,15},{2,12},{3,13},{4,10},{5,11},{6,8},{7,9},{8,6},{9,7},... | collective-permute-start | bytes 786440 | tf_op jit(solution)/shard_map/ppermute | solution.py:403
  84.4 30.0 %copy-start.11 = (bf16[8,16,1024]{2,1,0:T(8,128)(2,1)S(1)}, bf16[8,16,1024]{2,1,0:T(8,128)(2,1)}, u32[]{:S(2)}) copy-start(bf16[8,16,1024]{2,1,0:T(8,128)(2,1)} %get-tuple-element.94) | copy-start | bytes 786436
  106.2 28.4 %collective-permute-start.15 = (bf16[8,16,1024]{2,1,0:T(8,128)(2,1)S(1)}, bf16[8,16,1024]{2,1,0:T(8,128)(2,1)S(1)}, u32[]{:S(2)}, u32[]{:S(2)}) collective-permute-start(bf16[8,16,1024]{2,1,0:T(8,128)(2,1)S(1)} %copy-done.12), channel_id=1, source_target_pairs={{0,11},{1,10},{2,9},{3,8},{4,15},{5,14},{6,13},{7,12},{8,3},{9,2},... | collective-permute-start | bytes 786440 | tf_op jit(solution)/shard_map/ppermute | solution.py:403
  114.4 21.3 %collective-permute-start.16 = (bf16[8,16,1024]{2,1,0:T(8,128)(2,1)S(1)}, bf16[8,16,1024]{2,1,0:T(8,128)(2,1)S(1)}, u32[]{:S(2)}, u32[]{:S(2)}) collective-permute-start(bf16[8,16,1024]{2,1,0:T(8,128)(2,1)S(1)} %copy-done.11), channel_id=1, source_target_pairs={{0,15},{1,14},{2,13},{3,12},{4,11},{5,10},{6,9},{7,8},{8,7},{9,6},... | collective-permute-start | bytes 786440 | tf_op jit(solution)/shard_map/ppermute | solution.py:403
  (19 other events, 259.4 us)

commit v12 on v5

--- a/solution.py
+++ b/solution.py
@@ -392,7 +392,7 @@
     wide = pltpu.VMEM((8, -(-picked // LANES) * LANES), jnp.int32)
     if holders == 16:
         first = (8, 12)
-        groups = [(0, 8, 12, 4, 5, 1), (9, 6, 13, 7, 10, 2, 14, 3), (11, 15)]
+        groups = [(0, 8, 12, 4), (5, 1, 9, 6), (13, 7, 10, 2, 14, 3), (11, 15)]
         others = [d for group in groups for d in group if d not in first]
     else:
         first = ()
@@ -446,6 +446,8 @@
     else:
         table, positions = page_table, sel_pos
     index_in = exchange(index)
+    if first:
+        index_in, _ = lax.optimization_barrier((index_in, arrived[first[0]]))
 
     packed = pl.pallas_call(
         functools.partial(rows_kernel, hold, page_len),
@@ -501,9 +503,10 @@
     orders = page_order(table[0], positions[0], own, hold, capacity, groups, page_len)
     sel_lanes = jnp.tile(positions.reshape(-1, 1, QUERY_BLOCK), (1, 1, LANES // QUERY_BLOCK))
     sel_rows = jnp.broadcast_to(positions.reshape(picked, 1), (picked, LANES))
-    store_out, sel_lanes = lax.optimization_barrier((store_out, sel_lanes))
     state = ()
     for at, (arrays, order) in enumerate(zip(contexts, orders)):
+        if at == 1:
+            store_out, sel_lanes = lax.optimization_barrier((store_out, sel_lanes))
         state = attend(
             at == 0,
             at == len(groups) - 1,

time: 139 us -> 172 us (1.24)
  starting transfers between devices: 37.7 us -> 51.7 us
  waiting for transfers between devices: 19.5 us -> 28.1 us
  Pallas kernels: 69.3 us -> 76.3 us
    ppermute x17, starting transfers between devices: 23.8 us -> 39.6 us  [swap(): return lax.ppermute(x, 'store', [(h, h ^ d) for h in range(holders)])]
    all_to_all x2, waiting for transfers between devices: 0.57 us -> 9.3 us  [exchange(): return lax.all_to_all(x, 'store', split_axis=0, concat_axis=0, tiled=True)]
    pallas_call x3 -> x4, Pallas kernels: 49.9 us -> 56.9 us  [attend(): pl.pallas_call(functools.partial(attend_kernel, first, last, len(contexts...]
    all_to_all x2, starting transfers between devices: 13.8 us -> 12.1 us  [exchange(): return lax.all_to_all(x, 'store', split_axis=0, concat_axis=0, tiled=True)]
    unnamed x49 -> x51, local copies, waits for them, and re-layouts: 2.83 us -> 3.52 us
  transfers between devices with their start and end apart: 19 -> 19, of which waited for: 8 -> 7; matrix products, arithmetic and copies ran while one was open for 5% -> 5% of each run, Pallas kernels for 40% -> 36%
where the time goes in v12:
time: 172 us; the launch traced here: 169 us
  Pallas kernels  76.3 us (44%)
  starting transfers between devices  51.7 us (30%)
  waiting for transfers between devices  28.1 us (16%)
  other arithmetic  6.54 us (4%)
  local copies, waits for them, and re-layouts  5.59 us (3%)
    pallas_call x4, Pallas kernels, attend(): pl.pallas_call(functools.partial(attend_kernel, first, last, len(contexts...  56.9 us
    ppermute x17, starting transfers between devices, swap(): return lax.ppermute(x, 'store', [(h, h ^ d) for h in range(holders)])  39.6 us
    ppermute x17, waiting for transfers between devices, swap(): return lax.ppermute(x, 'store', [(h, h ^ d) for h in range(holders)])  18.8 us
    all_to_all x2, starting transfers between devices, exchange(): return lax.all_to_all(x, 'store', split_axis=0, concat_axis=0, tiled=True)  12.1 us
    all_to_all x2, waiting for transfers between devices, exchange(): return lax.all_to_all(x, 'store', split_axis=0, concat_axis=0, tiled=True)  9.3 us
    pallas_call x1, Pallas kernels, per_device(): pl.pallas_call(write_back_kernel, grid_spec=pltpu.PrefetchScalarGridSpec(...  8.02 us
    pallas_call x1, Pallas kernels, per_device(): pl.pallas_call(functools.partial(gather_kernel, capacity, others), grid_s...  4.9 us
    unnamed x51, local copies, waits for them, and re-layouts  3.52 us
  transfers between devices with their start and end apart: 19, of which 7 were waited for; matrix products, arithmetic and copies ran while one was open for 5% of the time, Pallas kernels for 36%

profile of v12, /device:TPU:9, one launch (start us, length us, event | category | flops | bytes accessed | tf_op | source)
XLA Modules:
  0.0 169.2 jit_solution(4650783110974569654)
XLA Ops:
  0.6 1.6 shard_map.68
  2.3 2.3 %collective-permute-start = (s32[1,2,128]{2,1,0:T(2,128)}, s32[1,2,128]{2,1,0:T(2,128)S(1)}, u32[]{:S(2)}, u32[]{:S(2)}) collective-permute-start(s32[1,2,128]{2,1,0:T(2,128)} %get-tuple-element.52), channel_id=1, source_target_pairs={{0,8},{1,9},{2,10},{3,11},{4,12},{5,13},{6,14},{7,15},{8,0},{9,1},... | collective-permute-start | bytes 3080 | tf_op jit(solution)/shard_map/ppermute | solution.py:403
  7.8 2.5 %shard_map.69 = (bf16[8,16,1024]{2,1,0:T(8,128)(2,1)}, bf16[8,16,1024]{2,1,0:T(8,128)(2,1)}) custom-call(s32[1,2,128]{2,1,0:T(2,128)} %copy-done.9, s32[1,2,128]{2,1,0:T(2,128)} %copy-done.10, bf16[128,16,1024]{2,1,0:T(8,128)(2,1)} %store_hbm.3), custom_call_target="tpu_custom_call" | custom-call | tf_op jit(solution)/shard_map/pallas_call | solution.py:426
  10.3 1.9 %collective-permute-start.2 = (bf16[8,16,1024]{2,1,0:T(8,128)(2,1)}, bf16[8,16,1024]{2,1,0:T(8,128)(2,1)S(1)}, u32[]{:S(2)}, u32[]{:S(2)}) collective-permute-start(bf16[8,16,1024]{2,1,0:T(8,128)(2,1)} %get-tuple-element.58), channel_id=1, source_target_pairs={{0,8},{1,9},{2,10},{3,11},{4,12},{5,13},{6,14},{7,15},{8,0},{9,1},... | collective-permute-start | bytes 786440 | tf_op jit(solution)/shard_map/ppermute | solution.py:403
  12.2 7.3 %all-to-all-start = ((s32[16,2,128]{2,1,0:T(2,128)}), s32[16,2,128]{2,1,0:T(2,128)S(1)}, u32[]{:S(2)}, u32[]{:S(2)}) async-start(s32[16,2,128]{2,1,0:T(2,128)} %get-tuple-element.57), calls=%async_computation | async-start | bytes 32768 | tf_op jit(solution)/shard_map/all_to_all | solution.py:406
  20.7 2.4 %shard_map.71 = bf16[16,16,1024]{2,1,0:T(8,128)(2,1)} custom-call(s32[1,128]{1,0:T(1,128)} %table_ref.2, s32[1,160]{1,0:T(1,128)} %rest_1_.3, bf16[160,1024]{1,0:T(8,128)(2,1)} %bitcast.72), custom_call_target="tpu_custom_call" | custom-call | tf_op jit(solution)/shard_map/pallas_call | solution.py:452
  23.0 9.3 %all-to-all-done.index.targets_ref = s32[16,2,128]{2,1,0:T(2,128)S(1)} async-done(((s32[16,2,128]{2,1,0:T(2,128)}), s32[16,2,128]{2,1,0:T(2,128)S(1)}, u32[]{:S(2)}, u32[]{:S(2)}) %all-to-all-start) | async-done | bytes 16416 | tf_op jit(solution)/shard_map/all_to_all | solution.py:406
  32.9 4.9 %shard_map.70 = (bf16[8,16,1024]{2,1,0:T(8,128)(2,1)}, bf16[8,16,1024]{2,1,0:T(8,128)(2,1)}, bf16[8,16,1024]{2,1,0:T(8,128)(2,1)}, bf16[8,16,1024]{2,1,0:T(8,128...) custom-call(s32[1]{0:T(128)} %bitcast.own, ...), custom_call_target="tpu_custom_call" | custom-call | tf_op jit(solution)/shard_map/pallas_call | solution.py:461
  41.2 4.8 %all-to-all-start.1 = ((bf16[16,16,1024]{2,1,0:T(8,128)(2,1)}), bf16[16,16,1024]{2,1,0:T(8,128)(2,1)S(1)}, u32[]{:S(2)}, u32[]{:S(2)}) async-start(bf16[16,16,1024]{2,1,0:T(8,128)(2,1)} %shard_map.71), calls=%async_computation.1 | async-start | bytes 1048576 | tf_op jit(solution)/shard_map/all_to_all | solution.py:406
  46.1 1.9 %collective-permute-start.5 = (bf16[8,16,1024]{2,1,0:T(8,128)(2,1)}, bf16[8,16,1024]{2,1,0:T(8,128)(2,1)S(1)}, u32[]{:S(2)}, u32[]{:S(2)}) collective-permute-start(bf16[8,16,1024]{2,1,0:T(8,128)(2,1)} %get-tuple-element.85), channel_id=1, source_target_pairs={{0,5},{1,4},{2,7},{3,6},{4,1},{5,0},{6,3},{7,2},{8,13},{9,12},{10,... | collective-permute-start | bytes 786440 | tf_op jit(solution)/shard_map/ppermute | solution.py:403
  48.0 2.5 %collective-permute-start.7 = (bf16[8,16,1024]{2,1,0:T(8,128)(2,1)}, bf16[8,16,1024]{2,1,0:T(8,128)(2,1)S(1)}, u32[]{:S(2)}, u32[]{:S(2)}) collective-permute-start(bf16[8,16,1024]{2,1,0:T(8,128)(2,1)} %get-tuple-element.87), channel_id=1, source_target_pairs={{0,9},{1,8},{2,11},{3,10},{4,13},{5,12},{6,15},{7,14},{8,1},{9,0},... | collective-permute-start | bytes 786440 | tf_op jit(solution)/shard_map/ppermute | solution.py:403
  54.7 11.4 %collective-permute-done.4.rest_8_ = bf16[8,16,1024]{2,1,0:T(8,128)(2,1)S(1)} collective-permute-done((bf16[8,16,1024]{2,1,0:T(8,128)(2,1)}, bf16[8,16,1024]{2,1,0:T(8,128)(2,1)S(1)}, u32[]{:S(2)}, u32[]{:S(2)}) %collective-permute-start.4) | collective-permute-done | bytes 262176 | tf_op jit(solution)/shard_map/ppermute | solution.py:403
  66.1 2.4 %collective-permute-start.9 = (bf16[8,16,1024]{2,1,0:T(8,128)(2,1)}, bf16[8,16,1024]{2,1,0:T(8,128)(2,1)S(1)}, u32[]{:S(2)}, u32[]{:S(2)}) collective-permute-start(bf16[8,16,1024]{2,1,0:T(8,128)(2,1)} %get-tuple-element.91), channel_id=1, source_target_pairs={{0,13},{1,12},{2,15},{3,14},{4,9},{5,8},{6,11},{7,10},{8,5},{9,4},... | collective-permute-start | bytes 786440 | tf_op jit(solution)/shard_map/ppermute | solution.py:403
  71.7 3.3 %collective-permute-start.10 = (bf16[8,16,1024]{2,1,0:T(8,128)(2,1)}, bf16[8,16,1024]{2,1,0:T(8,128)(2,1)S(1)}, u32[]{:S(2)}, u32[]{:S(2)}) collective-permute-start(bf16[8,16,1024]{2,1,0:T(8,128)(2,1)} %get-tuple-element.92), channel_id=1, source_target_pairs={{0,7},{1,6},{2,5},{3,4},{4,3},{5,2},{6,1},{7,0},{8,15},{9,14},{10,... | collective-permute-start | bytes 786440 | tf_op jit(solution)/shard_map/ppermute | solution.py:403
  77.3 1.9 %collective-permute-done.8.rest_8_ = bf16[8,16,1024]{2,1,0:T(8,128)(2,1)S(1)} collective-permute-done((bf16[8,16,1024]{2,1,0:T(8,128)(2,1)}, bf16[8,16,1024]{2,1,0:T(8,128)(2,1)S(1)}, u32[]{:S(2)}, u32[]{:S(2)}) %collective-permute-start.8) | collective-permute-done | bytes 262176 | tf_op jit(solution)/shard_map/ppermute | solution.py:403
  79.2 2.2 %collective-permute-start.13 = (bf16[8,16,1024]{2,1,0:T(8,128)(2,1)}, bf16[8,16,1024]{2,1,0:T(8,128)(2,1)}, u32[]{:S(2)}, u32[]{:S(2)}) collective-permute-start(bf16[8,16,1024]{2,1,0:T(8,128)(2,1)} %get-tuple-element.95), channel_id=1, source_target_pairs={{0,14},{1,15},{2,12},{3,13},{4,10},{5,11},{6,8},{7,9},{8,6},{9,7},... | collective-permute-start | bytes 786440 | tf_op jit(solution)/shard_map/ppermute | solution.py:403
  81.4 10.9 %collective-permute-start.14 = (bf16[8,16,1024]{2,1,0:T(8,128)(2,1)}, bf16[8,16,1024]{2,1,0:T(8,128)(2,1)}, u32[]{:S(2)}, u32[]{:S(2)}) collective-permute-start(bf16[8,16,1024]{2,1,0:T(8,128)(2,1)} %get-tuple-element.96), channel_id=1, source_target_pairs={{0,3},{1,2},{2,1},{3,0},{4,7},{5,6},{6,5},{7,4},{8,11},{9,10},{10,... | collective-permute-start | bytes 786440 | tf_op jit(solution)/shard_map/ppermute | solution.py:403
  93.0 16.3 %shard_map.73 = (f32[5,4,128,384]{3,2,1,0:T(8,128)}, f32[5,8,384]{2,1,0:T(8,128)}) custom-call(s32[32]{0:T(128)} %get-tuple-element.105.place, s32[32]{0:T(128)} %copy-done.8, s32[5]{0:T(128)} %fusion.9.tiles, s32[5,1,128]{2,1,0:T(1,128)} %tile.9.rest_0_, s32[1,160]{1,0:T(1,128)} %rest_1_.3, bf16[160,6144]{1,0:T(8,128)(2,1)} %bitcast.67, ...), custom_call_target="tpu_custom_call" | custom-call | flops 3623878656 | bytes 7471104 | tf_op jit(solution)/shard_map/pallas_call | solution.py:311
  110.2 8.0 %shard_map.72 = bf16[128,16,1024]{2,1,0:T(8,128)(2,1)} custom-call(s32[16,2,128]{2,1,0:T(2,128)} %copy-done.1, s32[16,2,128]{2,1,0:T(2,128)} %copy-done.1, bf16[128,16,1024]{2,1,0:T(8,128)(2,1)} %store_hbm.3, bf16[16,16,1024]{2,1,0:T(8,128)(2,1)} %copy-done), custom_call_target="tpu_custom_call" | custom-call | bytes 8388608 | tf_op jit(solution)/shard_map/pallas_call | solution.py:482
  118.3 13.2 %shard_map.74 = (f32[5,4,128,384]{3,2,1,0:T(8,128)}, f32[5,8,384]{2,1,0:T(8,128)}) custom-call(s32[32]{0:T(128)} %get-tuple-element.107.place, s32[32]{0:T(128)} %copy-done.7, s32[5]{0:T(128)} %and_select_fusion.1.tiles, s32[5,1,128]{2,1,0:T(1,128)} %tile.9.rest_0_, s32[1,160]{1,0:T(1,128)} %rest_1_.3, bf16[160,6144]{1,0:T(8,128)(2,1)} %bitcast.68, ...), custom_call_target="tpu_custom_call" | custom-call | flops 2415919104 | bytes 6946816 | tf_op jit(solution)/shard_map/pallas_call | solution.py:311
  131.5 2.4 %collective-permute-start.15 = (bf16[8,16,1024]{2,1,0:T(8,128)(2,1)S(1)}, bf16[8,16,1024]{2,1,0:T(8,128)(2,1)S(1)}, u32[]{:S(2)}, u32[]{:S(2)}) collective-permute-start(bf16[8,16,1024]{2,1,0:T(8,128)(2,1)S(1)} %copy-done.13), channel_id=1, source_target_pairs={{0,11},{1,10},{2,9},{3,8},{4,15},{5,14},{6,13},{7,12},{8,3},{9,2},... | collective-permute-start | bytes 786440 | tf_op jit(solution)/shard_map/ppermute | solution.py:403
  134.0 4.9 %collective-permute-start.16 = (bf16[8,16,1024]{2,1,0:T(8,128)(2,1)S(1)}, bf16[8,16,1024]{2,1,0:T(8,128)(2,1)S(1)}, u32[]{:S(2)}, u32[]{:S(2)}) collective-permute-start(bf16[8,16,1024]{2,1,0:T(8,128)(2,1)S(1)} %copy-done.12), channel_id=1, source_target_pairs={{0,15},{1,14},{2,13},{3,12},{4,11},{5,10},{6,9},{7,8},{8,7},{9,6},... | collective-permute-start | bytes 786440 | tf_op jit(solution)/shard_map/ppermute | solution.py:403
  139.6 16.6 %shard_map.75 = (f32[5,4,128,384]{3,2,1,0:T(8,128)}, f32[5,8,384]{2,1,0:T(8,128)}) custom-call(s32[48]{0:T(128)} %get-tuple-element.109.place, s32[48]{0:T(128)} %copy-done.11, s32[5]{0:T(128)} %and_select_fusion.2.tiles, s32[5,1,128]{2,1,0:T(1,128)} %tile.9.rest_0_, s32[1,160]{1,0:T(1,128)} %rest_1_.3, bf16[160,6144]{1,0:T(8,128)(2,1)} %bitcast.69, ...), custom_call_target="tpu_custom_call" | custom-call | flops 3623878656 | bytes 7471104 | tf_op jit(solution)/shard_map/pallas_call | solution.py:311
  158.5 10.7 %shard_map.76 = bf16[160,6144]{1,0:T(8,128)(2,1)} custom-call(s32[16]{0:T(128)} %get-tuple-element.111.place, s32[16]{0:T(128)} %copy-done.6, s32[5]{0:T(128)} %and_select_fusion.3.tiles, s32[5,1,128]{2,1,0:T(1,128)} %tile.9.rest_0_, s32[1,160]{1,0:T(1,128)} %rest_1_.3, bf16[160,6144]{1,0:T(8,128)(2,1)} %bitcast.70, ...), custom_call_target="tpu_custom_call" | custom-call | flops 1207959552 | bytes 6422528 | tf_op jit(solution)/shard_map/pallas_call | solution.py:311
  (101 shorter events, 22.5 us)
Async XLA Ops:
  2.3 3.5 %collective-permute-start = (s32[1,2,128]{2,1,0:T(2,128)}, s32[1,2,128]{2,1,0:T(2,128)S(1)}, u32[]{:S(2)}, u32[]{:S(2)}) collective-permute-start(s32[1,2,128]{2,1,0:T(2,128)} %get-tuple-element.52), channel_id=1, source_target_pairs={{0,8},{1,9},{2,10},{3,11},{4,12},{5,13},{6,14},{7,15},{8,0},{9,1},... | collective-permute-start | bytes 3080 | tf_op jit(solution)/shard_map/ppermute | solution.py:403
  4.6 2.6 %collective-permute-start.1 = (s32[1,2,128]{2,1,0:T(2,128)}, s32[1,2,128]{2,1,0:T(2,128)S(1)}, u32[]{:S(2)}, u32[]{:S(2)}) collective-permute-start(s32[1,2,128]{2,1,0:T(2,128)} %get-tuple-element.53), channel_id=1, source_target_pairs={{0,12},{1,13},{2,14},{3,15},{4,8},{5,9},{6,10},{7,11},{8,4},{9,5},... | collective-permute-start | bytes 3080 | tf_op jit(solution)/shard_map/ppermute | solution.py:403
  10.3 22.0 %collective-permute-start.2 = (bf16[8,16,1024]{2,1,0:T(8,128)(2,1)}, bf16[8,16,1024]{2,1,0:T(8,128)(2,1)S(1)}, u32[]{:S(2)}, u32[]{:S(2)}) collective-permute-start(bf16[8,16,1024]{2,1,0:T(8,128)(2,1)} %get-tuple-element.58), channel_id=1, source_target_pairs={{0,8},{1,9},{2,10},{3,11},{4,12},{5,13},{6,14},{7,15},{8,0},{9,1},... | collective-permute-start | bytes 786440 | tf_op jit(solution)/shard_map/ppermute | solution.py:403
  12.2 20.1 %all-to-all-start = ((s32[16,2,128]{2,1,0:T(2,128)}), s32[16,2,128]{2,1,0:T(2,128)S(1)}, u32[]{:S(2)}, u32[]{:S(2)}) async-start(s32[16,2,128]{2,1,0:T(2,128)} %get-tuple-element.57), calls=%async_computation | async-start | bytes 32768 | tf_op jit(solution)/shard_map/all_to_all | solution.py:406
  19.5 34.0 %collective-permute-start.3 = (bf16[8,16,1024]{2,1,0:T(8,128)(2,1)}, bf16[8,16,1024]{2,1,0:T(8,128)(2,1)S(1)}, u32[]{:S(2)}, u32[]{:S(2)}) collective-permute-start(bf16[8,16,1024]{2,1,0:T(8,128)(2,1)} %get-tuple-element.81), channel_id=1, source_target_pairs={{0,12},{1,13},{2,14},{3,15},{4,8},{5,9},{6,10},{7,11},{8,4},{9,5},... | collective-permute-start | bytes 786440 | tf_op jit(solution)/shard_map/ppermute | solution.py:403
  32.9 60.1 %copy-start.14 = (bf16[8,16,1024]{2,1,0:T(8,128)(2,1)}, bf16[8,16,1024]{2,1,0:T(8,128)(2,1)S(1)}, u32[]{:S(2)}) copy-start(bf16[8,16,1024]{2,1,0:T(8,128)(2,1)S(1)} %collective-permute-done.2.rest_6_) | copy-start | bytes 786436
  40.5 68.8 %copy-start.11 = (s32[48]{0:T(128)}, s32[48]{0:T(128)S(1)}, u32[]{:S(2)}) copy-start(s32[48]{0:T(128)S(1)} %get-tuple-element.108.page_number) | copy-start | bytes 580
  41.2 68.2 %all-to-all-start.1 = ((bf16[16,16,1024]{2,1,0:T(8,128)(2,1)}), bf16[16,16,1024]{2,1,0:T(8,128)(2,1)S(1)}, u32[]{:S(2)}, u32[]{:S(2)}) async-start(bf16[16,16,1024]{2,1,0:T(8,128)(2,1)} %shard_map.71), calls=%async_computation.1 | async-start | bytes 1048576 | tf_op jit(solution)/shard_map/all_to_all | solution.py:406
  46.1 20.0 %collective-permute-start.4 = (bf16[8,16,1024]{2,1,0:T(8,128)(2,1)}, bf16[8,16,1024]{2,1,0:T(8,128)(2,1)S(1)}, u32[]{:S(2)}, u32[]{:S(2)}) collective-permute-start(bf16[8,16,1024]{2,1,0:T(8,128)(2,1)} %get-tuple-element.82), channel_id=1, source_target_pairs={{0,4},{1,5},{2,6},{3,7},{4,0},{5,1},{6,2},{7,3},{8,12},{9,13},{10,... | collective-permute-start | bytes 786440 | tf_op jit(solution)/shard_map/ppermute | solution.py:403
  46.1 25.6 %collective-permute-start.5 = (bf16[8,16,1024]{2,1,0:T(8,128)(2,1)}, bf16[8,16,1024]{2,1,0:T(8,128)(2,1)S(1)}, u32[]{:S(2)}, u32[]{:S(2)}) collective-permute-start(bf16[8,16,1024]{2,1,0:T(8,128)(2,1)} %get-tuple-element.85), channel_id=1, source_target_pairs={{0,5},{1,4},{2,7},{3,6},{4,1},{5,0},{6,3},{7,2},{8,13},{9,12},{10,... | collective-permute-start | bytes 786440 | tf_op jit(solution)/shard_map/ppermute | solution.py:403
  48.0 26.9 %collective-permute-start.6 = (bf16[8,16,1024]{2,1,0:T(8,128)(2,1)}, bf16[8,16,1024]{2,1,0:T(8,128)(2,1)S(1)}, u32[]{:S(2)}, u32[]{:S(2)}) collective-permute-start(bf16[8,16,1024]{2,1,0:T(8,128)(2,1)} %get-tuple-element.86), channel_id=1, source_target_pairs={{0,1},{1,0},{2,3},{3,2},{4,5},{5,4},{6,7},{7,6},{8,9},{9,8},{10,11... | collective-permute-start | bytes 786440 | tf_op jit(solution)/shard_map/ppermute | solution.py:403
  48.0 28.2 %collective-permute-start.7 = (bf16[8,16,1024]{2,1,0:T(8,128)(2,1)}, bf16[8,16,1024]{2,1,0:T(8,128)(2,1)S(1)}, u32[]{:S(2)}, u32[]{:S(2)}) collective-permute-start(bf16[8,16,1024]{2,1,0:T(8,128)(2,1)} %get-tuple-element.87), channel_id=1, source_target_pairs={{0,9},{1,8},{2,11},{3,10},{4,13},{5,12},{6,15},{7,14},{8,1},{9,0},... | collective-permute-start | bytes 786440 | tf_op jit(solution)/shard_map/ppermute | solution.py:403
  51.3 41.8 %copy-start.8 = (s32[32]{0:T(128)}, s32[32]{0:T(128)S(1)}, u32[]{:S(2)}) copy-start(s32[32]{0:T(128)S(1)} %get-tuple-element.104.page_number) | copy-start | bytes 388
  51.9 57.4 %copy-start.6 = (s32[16]{0:T(128)}, s32[16]{0:T(128)S(1)}, u32[]{:S(2)}) copy-start(s32[16]{0:T(128)S(1)} %get-tuple-element.110.page_number) | copy-start | bytes 196
  52.6 56.7 %copy-start.7 = (s32[32]{0:T(128)}, s32[32]{0:T(128)S(1)}, u32[]{:S(2)}) copy-start(s32[32]{0:T(128)S(1)} %get-tuple-element.106.page_number) | copy-start | bytes 388
  53.5 25.7 %collective-permute-start.8 = (bf16[8,16,1024]{2,1,0:T(8,128)(2,1)}, bf16[8,16,1024]{2,1,0:T(8,128)(2,1)S(1)}, u32[]{:S(2)}, u32[]{:S(2)}) collective-permute-start(bf16[8,16,1024]{2,1,0:T(8,128)(2,1)} %get-tuple-element.88), channel_id=1, source_target_pairs={{0,6},{1,7},{2,4},{3,5},{4,2},{5,3},{6,0},{7,1},{8,14},{9,15},{10,... | collective-permute-start | bytes 786440 | tf_op jit(solution)/shard_map/ppermute | solution.py:403
  66.1 15.3 %collective-permute-start.9 = (bf16[8,16,1024]{2,1,0:T(8,128)(2,1)}, bf16[8,16,1024]{2,1,0:T(8,128)(2,1)S(1)}, u32[]{:S(2)}, u32[]{:S(2)}) collective-permute-start(bf16[8,16,1024]{2,1,0:T(8,128)(2,1)} %get-tuple-element.91), channel_id=1, source_target_pairs={{0,13},{1,12},{2,15},{3,14},{4,9},{5,8},{6,11},{7,10},{8,5},{9,4},... | collective-permute-start | bytes 786440 | tf_op jit(solution)/shard_map/ppermute | solution.py:403
  71.7 59.8 %collective-permute-start.10 = (bf16[8,16,1024]{2,1,0:T(8,128)(2,1)}, bf16[8,16,1024]{2,1,0:T(8,128)(2,1)S(1)}, u32[]{:S(2)}, u32[]{:S(2)}) collective-permute-start(bf16[8,16,1024]{2,1,0:T(8,128)(2,1)} %get-tuple-element.92), channel_id=1, source_target_pairs={{0,7},{1,6},{2,5},{3,4},{4,3},{5,2},{6,1},{7,0},{8,15},{9,14},{10,... | collective-permute-start | bytes 786440 | tf_op jit(solution)/shard_map/ppermute | solution.py:403
  75.0 59.0 %collective-permute-start.11 = (bf16[8,16,1024]{2,1,0:T(8,128)(2,1)}, bf16[8,16,1024]{2,1,0:T(8,128)(2,1)S(1)}, u32[]{:S(2)}, u32[]{:S(2)}) collective-permute-start(bf16[8,16,1024]{2,1,0:T(8,128)(2,1)} %get-tuple-element.93), channel_id=1, source_target_pairs={{0,10},{1,11},{2,8},{3,9},{4,14},{5,15},{6,12},{7,13},{8,2},{9,3},... | collective-permute-start | bytes 786440 | tf_op jit(solution)/shard_map/ppermute | solution.py:403
  76.3 62.6 %collective-permute-start.12 = (bf16[8,16,1024]{2,1,0:T(8,128)(2,1)}, bf16[8,16,1024]{2,1,0:T(8,128)(2,1)S(1)}, u32[]{:S(2)}, u32[]{:S(2)}) collective-permute-start(bf16[8,16,1024]{2,1,0:T(8,128)(2,1)} %get-tuple-element.94), channel_id=1, source_target_pairs={{0,2},{1,3},{2,0},{3,1},{4,6},{5,7},{6,4},{7,5},{8,10},{9,11},{10,... | collective-permute-start | bytes 786440 | tf_op jit(solution)/shard_map/ppermute | solution.py:403
  79.2 59.7 %collective-permute-start.13 = (bf16[8,16,1024]{2,1,0:T(8,128)(2,1)}, bf16[8,16,1024]{2,1,0:T(8,128)(2,1)}, u32[]{:S(2)}, u32[]{:S(2)}) collective-permute-start(bf16[8,16,1024]{2,1,0:T(8,128)(2,1)} %get-tuple-element.95), channel_id=1, source_target_pairs={{0,14},{1,15},{2,12},{3,13},{4,10},{5,11},{6,8},{7,9},{8,6},{9,7},... | collective-permute-start | bytes 786440 | tf_op jit(solution)/shard_map/ppermute | solution.py:403
  81.4 57.5 %collective-permute-start.14 = (bf16[8,16,1024]{2,1,0:T(8,128)(2,1)}, bf16[8,16,1024]{2,1,0:T(8,128)(2,1)}, u32[]{:S(2)}, u32[]{:S(2)}) collective-permute-start(bf16[8,16,1024]{2,1,0:T(8,128)(2,1)} %get-tuple-element.96), channel_id=1, source_target_pairs={{0,3},{1,2},{2,1},{3,0},{4,7},{5,6},{6,5},{7,4},{8,11},{9,10},{10,... | collective-permute-start | bytes 786440 | tf_op jit(solution)/shard_map/ppermute | solution.py:403
  131.5 24.7 %collective-permute-start.15 = (bf16[8,16,1024]{2,1,0:T(8,128)(2,1)S(1)}, bf16[8,16,1024]{2,1,0:T(8,128)(2,1)S(1)}, u32[]{:S(2)}, u32[]{:S(2)}) collective-permute-start(bf16[8,16,1024]{2,1,0:T(8,128)(2,1)S(1)} %copy-done.13), channel_id=1, source_target_pairs={{0,11},{1,10},{2,9},{3,8},{4,15},{5,14},{6,13},{7,12},{8,3},{9,2},... | collective-permute-start | bytes 786440 | tf_op jit(solution)/shard_map/ppermute | solution.py:403
  134.0 23.8 %collective-permute-start.16 = (bf16[8,16,1024]{2,1,0:T(8,128)(2,1)S(1)}, bf16[8,16,1024]{2,1,0:T(8,128)(2,1)S(1)}, u32[]{:S(2)}, u32[]{:S(2)}) collective-permute-start(bf16[8,16,1024]{2,1,0:T(8,128)(2,1)S(1)} %copy-done.12), channel_id=1, source_target_pairs={{0,15},{1,14},{2,13},{3,12},{4,11},{5,10},{6,9},{7,8},{8,7},{9,6},... | collective-permute-start | bytes 786440 | tf_op jit(solution)/shard_map/ppermute | solution.py:403
  (20 other events, 345.1 us)

commit v13 on v10

--- a/solution.py
+++ b/solution.py
@@ -15,7 +15,9 @@
 ROW_SLOTS = 16
 VMEM_LIMIT = 60 * 1024 * 1024
 QUERY_BLOCK = 32
-TILE_PAGES = 16
+TILE_PAGES = 32
+LATE_TILE_PAGES = 16
+FRESH_PAGES = 16
 HIDDEN = -1e30
 FAR_POSITION = 1 << 24
 
@@ -157,7 +159,7 @@
     pltpu.make_async_copy(store_out, store_out, out_sem).wait()
 
 
-def attend_kernel(first, last, sources, place, page_number, tiles, *rest):
+def attend_kernel(first, last, tile_pages, sources, place, page_number, tiles, *rest):
     sel_ref, positions_ref, query_ref, *rest = rest
     if first:
         fresh_ref, fresh_positions, *rest = rest
@@ -165,12 +167,12 @@
     rest = rest if first else rest[2:]
     contexts, rest = rest[:sources], rest[sources:]
     outs, rest = (rest[:1], rest[1:]) if last else (rest[:2], rest[2:])
-    kv, values, position, query, mixed, stats, sem = rest
+    kv, values, position, query, scores, raised, mixed, stats, sem = rest
     pages, page_len, width = kv.shape
     each = contexts[0].shape[0]
-    ahead = TILE_PAGES if first else 0
+    ahead = FRESH_PAGES if first else 0
     block = query_ref.shape[0]
-    tile = TILE_PAGES * page_len
+    tile = tile_pages * page_len
     lanes = QUERY_GROUP * block
     scale = 1.4426950408889634 / HEAD_WIDTH**0.5
     f32 = jnp.float32
@@ -192,34 +194,36 @@
             kv[0:count] = fresh_ref[...].reshape(count, page_len, width)
             kv[count:ahead] = jnp.zeros((ahead - count, page_len, width), bf16)
             position[0:picked, :] = fresh_positions[...]
-            position[picked:tile, :] = jnp.full((tile - picked, LANES), FAR_POSITION, jnp.int32)
+            start = ahead * page_len
+            position[picked:start, :] = jnp.full((start - picked, LANES), FAR_POSITION, jnp.int32)
         positions = positions_ref[...]
         row = lax.broadcasted_iota(jnp.int32, (page_len, positions.shape[1]), 0)
         ones = jnp.ones((positions.shape[1], LANES), bf16)
         row_lanes = lax.broadcasted_iota(jnp.int32, (page_len, LANES), 0)
 
         def place_rows(t, carry):
-            starts = [page_number[t * TILE_PAGES + k] * page_len for k in range(TILE_PAGES)]
+            starts = [page_number[t * FRESH_PAGES + k] * page_len for k in range(FRESH_PAGES)]
             hit = jnp.concatenate([one_hot(row + start == positions) for start in starts], axis=0)
             hidden = jnp.dot(hit.astype(bf16), ones, preferred_element_type=f32)
             plain = jnp.concatenate([row_lanes + start for start in starts], axis=0)
-            here = pl.ds(pl.multiple_of(ahead * page_len + t * tile, tile), tile)
+            some = FRESH_PAGES * page_len
+            here = pl.ds(pl.multiple_of(ahead * page_len + t * some, some), some)
             position[here, :] = jnp.where(hidden > 0.0, FAR_POSITION, plain)
             return carry
 
-        lax.fori_loop(0, (pages - ahead) // TILE_PAGES, place_rows, 0)
+        lax.fori_loop(0, (pages - ahead) // FRESH_PAGES, place_rows, 0)
         used = kv.at[ahead:]
         pltpu.make_async_copy(used, used, sem).wait()
 
         def turn(t, carry):
-            here = pl.ds(t * TILE_PAGES, TILE_PAGES)
+            here = pl.ds(t * tile_pages, tile_pages)
             for g in range(KEY_VALUE_HEADS):
                 at = (KEY_VALUE_HEADS + g) * LANES
                 value = kv[here, :, at : at + LANES].reshape(tile, LANES)
                 values[t, g] = nt_dot(eye, value).astype(bf16)
             return carry
 
-        lax.fori_loop(0, pages // TILE_PAGES, turn, 0)
+        lax.fori_loop(0, pages // tile_pages, turn, 0)
 
     for g in range(KEY_VALUE_HEADS):
         for i in range(QUERY_GROUP):
@@ -236,35 +240,36 @@
     sel = sel_ref[0]
 
     def one_tile(t, carry):
-        here = pl.ds(t * TILE_PAGES, TILE_PAGES)
+        here = pl.ds(t * tile_pages, tile_pages)
         bias = jnp.where(
             position[pl.ds(pl.multiple_of(t * tile, tile), tile), :] <= sel, 0.0, HIDDEN
         ).astype(f32)
 
         parts = [slice(n * LANES, (n + 1) * LANES) for n in range(lanes // LANES)]
         chains = [(g, part) for g in range(KEY_VALUE_HEADS) for part in parts]
-
-        def score(chain):
-            g, part = chain
+        for g in range(KEY_VALUE_HEADS):
             key = kv[here, :, g * LANES : (g + 1) * LANES].reshape(tile, LANES)
-            return nt_dot(key, query[g, part, :])
-
-        upcoming = score(chains[0])
-        for following, (g, part) in zip([*chains[1:], None], chains):
-            s = upcoming + bias
-            if following:
-                upcoming = score(following)
+            product = nt_dot(key, query[g])
+            for part in parts:
+                scores[g, :, part] = product[:, part] + bias
+        peaks, shrinks = [], []
+        for g, part in chains:
+            old = stats[g : g + 1, part]
+            new = jnp.maximum(old, jnp.max(scores[g, :, part], axis=0, keepdims=True))
+            stats[g : g + 1, part] = new
+            peaks.append(new)
+            shrinks.append(jnp.exp2((old - new) * scale))
+        for (g, part), new, shrink in zip(chains, peaks, shrinks):
             at = KEY_VALUE_HEADS + g
-            old = stats[g : g + 1, part]
-            new = jnp.maximum(old, jnp.max(s, axis=0, keepdims=True))
-            p = jnp.exp2((s - new) * scale)
-            shrink = jnp.exp2((old - new) * scale)
+            p = jnp.exp2((scores[g, :, part] - new) * scale)
             stats[at : at + 1, part] = stats[at : at + 1, part] * shrink + jnp.sum(
                 p, axis=0, keepdims=True
             )
-            stats[g : g + 1, part] = new
-            mixed[g, :, part] = mixed[g, :, part] * shrink + jnp.dot(
-                values[t, g], p.astype(bf16), preferred_element_type=f32
+            raised[g, :, part] = p.astype(bf16)
+        for g in range(KEY_VALUE_HEADS):
+            shrink = jnp.concatenate(shrinks[g * len(parts) : (g + 1) * len(parts)], axis=1)
+            mixed[g] = mixed[g] * shrink + jnp.dot(
+                values[t, g], raised[g], preferred_element_type=f32
             )
         return carry
 
@@ -288,10 +293,10 @@
         outs[1][0] = stats[...]
 
 
-def attend(first, last, order, sel_lanes, positions, queries, fresh, state, contexts):
+def attend(first, last, tile_pages, order, sel_lanes, positions, queries, fresh, state, contexts):
     picked, features = queries.shape
     each, page_len, width = contexts[0].shape
-    pages = each * len(contexts) + (TILE_PAGES if first else 0)
+    pages = each * len(contexts) + (FRESH_PAGES if first else 0)
     steps = picked // QUERY_BLOCK
     lanes = QUERY_GROUP * QUERY_BLOCK
     wide = pl.BlockSpec((QUERY_BLOCK, features), lambda b, *_: (b, 0))
@@ -305,7 +310,7 @@
     ]
     share = 0.6
     return pl.pallas_call(
-        functools.partial(attend_kernel, first, last, len(contexts)),
+        functools.partial(attend_kernel, first, last, tile_pages, len(contexts)),
         grid_spec=pltpu.PrefetchScalarGridSpec(
             num_scalar_prefetch=3,
             grid=(steps,),
@@ -321,10 +326,12 @@
             scratch_shapes=[
                 pltpu.VMEM((pages, page_len, width), jnp.bfloat16),
                 pltpu.VMEM(
-                    (pages // TILE_PAGES, KEY_VALUE_HEADS, LANES, TILE_PAGES * page_len), jnp.bfloat16
+                    (pages // tile_pages, KEY_VALUE_HEADS, LANES, tile_pages * page_len), jnp.bfloat16
                 ),
                 pltpu.VMEM((pages * page_len, LANES), jnp.int32),
                 pltpu.VMEM((KEY_VALUE_HEADS, lanes, LANES), jnp.bfloat16),
+                pltpu.VMEM((KEY_VALUE_HEADS, tile_pages * page_len, lanes), jnp.float32),
+                pltpu.VMEM((KEY_VALUE_HEADS, tile_pages * page_len, lanes), jnp.bfloat16),
                 pltpu.VMEM((KEY_VALUE_HEADS, LANES, lanes), jnp.float32),
                 pltpu.VMEM((2 * KEY_VALUE_HEADS, lanes), jnp.float32),
                 pltpu.SemaphoreType.DMA,
@@ -342,7 +349,7 @@
     )(*order, sel_lanes, positions, queries, *[x for x in fresh if first], *state, *contexts)
 
 
-def page_order(slots, positions, own, hold, capacity, groups, page_len):
+def page_order(slots, positions, own, hold, capacity, groups, tiles, page_len):
     pages = slots.shape[0]
     number = jnp.arange(pages)
     before = number[None, :] < number[:, None]
@@ -351,7 +358,7 @@
     distance = owners ^ own
     last_page = positions.reshape(-1, QUERY_BLOCK)[:, -1] // page_len
     orders = []
-    for at, group in enumerate(groups):
+    for at, (group, tile_pages) in enumerate(zip(groups, tiles)):
         if group is None:
             arrival = owners * capacity + ranks
             count = pages
@@ -368,7 +375,8 @@
             jnp.where(member[None, :] & (place[None, :] == index), number[None, :], 0), axis=1
         )
         seen = jnp.sum((page[None, :] <= last_page[:, None]).astype(jnp.int32), axis=1)
-        orders.append((places, page, (seen + TILE_PAGES - 1) // TILE_PAGES + (at == 0)))
+        seen = seen + (FRESH_PAGES if at == 0 else 0)
+        orders.append((places, page, (seen + tile_pages - 1) // tile_pages))
     return orders
 
 
@@ -494,7 +502,8 @@
         cost_estimate=pl.CostEstimate(flops=0, bytes_accessed=4 * store.size, transcendentals=0),
     )(index_in, index_in, store, rows_in)
 
-    orders = page_order(table[0], positions[0], own, hold, capacity, groups, page_len)
+    tiles = [LATE_TILE_PAGES if at == len(groups) - 1 else TILE_PAGES for at in range(len(groups))]
+    orders = page_order(table[0], positions[0], own, hold, capacity, groups, tiles, page_len)
     sel_lanes = jnp.tile(positions.reshape(-1, 1, QUERY_BLOCK), (1, 1, LANES // QUERY_BLOCK))
     sel_rows = jnp.broadcast_to(positions.reshape(picked, 1), (picked, LANES))
     store_out, sel_lanes = lax.optimization_barrier((store_out, sel_lanes))
@@ -503,6 +512,7 @@
         state = attend(
             at == 0,
             at == len(groups) - 1,
+            tiles[at],
             order,
             sel_lanes,
             positions,

time: 142 us -> 139 us (0.979); the launches traced: 141 us -> 137 us
  Pallas kernels: 73.4 us -> 66.6 us
  starting transfers between devices: 37.7 us -> 39.2 us
    pallas_call x3, Pallas kernels: 54 us -> 47.1 us  [attend(): pl.pallas_call(functools.partial(attend_kernel, first, last, tile_pages,...]
    ppermute x17, starting transfers between devices: 23.8 us -> 25.4 us  [swap(): return lax.ppermute(x, 'store', [(h, h ^ d) for h in range(holders)])]
  transfers between devices with their start and end apart: 19 -> 19, of which waited for: 8 -> 8; matrix products, arithmetic and copies ran while one was open for 5% -> 5% of each run, Pallas kernels for 41% -> 38%
where the time goes in v13:
time: 139 us; the launch traced here: 137 us
  Pallas kernels  66.6 us (48%)
  starting transfers between devices  39.2 us (28%)
  waiting for transfers between devices  19.6 us (14%)
  other arithmetic  5.27 us (4%)
  local copies, waits for them, and re-layouts  4.97 us (4%)
    pallas_call x3, Pallas kernels, attend(): pl.pallas_call(functools.partial(attend_kernel, first, last, tile_pages,...  47.1 us
    ppermute x17, starting transfers between devices, swap(): return lax.ppermute(x, 'store', [(h, h ^ d) for h in range(holders)])  25.4 us
    ppermute x17, waiting for transfers between devices, swap(): return lax.ppermute(x, 'store', [(h, h ^ d) for h in range(holders)])  19 us
    all_to_all x2, starting transfers between devices, exchange(): return lax.all_to_all(x, 'store', split_axis=0, concat_axis=0, tiled=True)  13.8 us
    pallas_call x1, Pallas kernels, per_device(): pl.pallas_call(write_back_kernel, grid_spec=pltpu.PrefetchScalarGridSpec(...  8.02 us
    pallas_call x1, Pallas kernels, per_device(): pl.pallas_call(functools.partial(gather_kernel, capacity, others), grid_s...  4.89 us
    unnamed x49, local copies, waits for them, and re-layouts  2.83 us
  transfers between devices with their start and end apart: 19, of which 8 were waited for; matrix products, arithmetic and copies ran while one was open for 5% of the time, Pallas kernels for 38%

profile of v13, /device:TPU:9, one launch (start us, length us, event | category | flops | bytes accessed | tf_op | source)
XLA Modules:
  0.0 136.5 jit_solution(12710119888297442013)
XLA Ops:
  0.6 1.7 %shard_map.68 = (s32[16,2,128]{2,1,0:T(2,128)}, s32[1,2,128]{2,1,0:T(2,128)}, s32[1,2,128]{2,1,0:T(2,128)}) custom-call(s32[1]{0:T(128)} %bitcast.own, s32[1,128]{1,0:T(1,128)} %table_ref.2, s32[1,160]{1,0:T(1,128)} %rest_1_.2), custom_call_target="tpu_custom_call" | custom-call | tf_op jit(solution)/shard_map/pallas_call | solution.py:412
  2.3 2.3 %collective-permute-start = (s32[1,2,128]{2,1,0:T(2,128)}, s32[1,2,128]{2,1,0:T(2,128)S(1)}, u32[]{:S(2)}, u32[]{:S(2)}) collective-permute-start(s32[1,2,128]{2,1,0:T(2,128)} %get-tuple-element.49), channel_id=1, source_target_pairs={{0,8},{1,9},{2,10},{3,11},{4,12},{5,13},{6,14},{7,15},{8,0},{9,1},... | collective-permute-start | bytes 3080 | tf_op jit(solution)/shard_map/ppermute | solution.py:407
  5.8 1.4 %collective-permute-done.1.refs_1_ = s32[1,2,128]{2,1,0:T(2,128)S(1)} collective-permute-done((s32[1,2,128]{2,1,0:T(2,128)}, s32[1,2,128]{2,1,0:T(2,128)S(1)}, u32[]{:S(2)}, u32[]{:S(2)}) %collective-permute-start.1) | collective-permute-done | bytes 1056 | tf_op jit(solution)/shard_map/ppermute | solution.py:407
  7.8 2.5 %shard_map.69 = (bf16[8,16,1024]{2,1,0:T(8,128)(2,1)}, bf16[8,16,1024]{2,1,0:T(8,128)(2,1)}) custom-call(s32[1,2,128]{2,1,0:T(2,128)} %copy-done.7, s32[1,2,128]{2,1,0:T(2,128)} %copy-done.8, bf16[128,16,1024]{2,1,0:T(8,128)(2,1)} %store_hbm.3), custom_call_target="tpu_custom_call" | custom-call | tf_op jit(solution)/shard_map/pallas_call | solution.py:430
  10.3 7.6 %all-to-all-start = ((s32[16,2,128]{2,1,0:T(2,128)}), s32[16,2,128]{2,1,0:T(2,128)S(1)}, u32[]{:S(2)}, u32[]{:S(2)}) async-start(s32[16,2,128]{2,1,0:T(2,128)} %get-tuple-element.54), calls=%async_computation | async-start | bytes 32768 | tf_op jit(solution)/shard_map/all_to_all | solution.py:410
  17.9 2.1 %collective-permute-start.2 = (bf16[8,16,1024]{2,1,0:T(8,128)(2,1)}, bf16[8,16,1024]{2,1,0:T(8,128)(2,1)S(1)}, u32[]{:S(2)}, u32[]{:S(2)}) collective-permute-start(bf16[8,16,1024]{2,1,0:T(8,128)(2,1)} %get-tuple-element.76), channel_id=1, source_target_pairs={{0,8},{1,9},{2,10},{3,11},{4,12},{5,13},{6,14},{7,15},{8,0},{9,1},... | collective-permute-start | bytes 786440 | tf_op jit(solution)/shard_map/ppermute | solution.py:407
  20.0 2.4 %shard_map.71 = bf16[16,16,1024]{2,1,0:T(8,128)(2,1)} custom-call(s32[1,128]{1,0:T(1,128)} %table_ref.2, s32[1,160]{1,0:T(1,128)} %rest_1_.2, bf16[160,1024]{1,0:T(8,128)(2,1)} %bitcast.70), custom_call_target="tpu_custom_call" | custom-call | tf_op jit(solution)/shard_map/pallas_call | solution.py:454
  23.5 4.9 %shard_map.70 = (bf16[8,16,1024]{2,1,0:T(8,128)(2,1)}, bf16[8,16,1024]{2,1,0:T(8,128)(2,1)}, bf16[8,16,1024]{2,1,0:T(8,128)(2,1)}, bf16[8,16,1024]{2,1,0:T(8,128...) custom-call(s32[1]{0:T(128)} %bitcast.own, ...), custom_call_target="tpu_custom_call" | custom-call | tf_op jit(solution)/shard_map/pallas_call | solution.py:463
  30.3 6.3 %all-to-all-start.1 = ((bf16[16,16,1024]{2,1,0:T(8,128)(2,1)}), bf16[16,16,1024]{2,1,0:T(8,128)(2,1)S(1)}, u32[]{:S(2)}, u32[]{:S(2)}) async-start(bf16[16,16,1024]{2,1,0:T(8,128)(2,1)} %shard_map.71), calls=%async_computation.1 | async-start | bytes 1048576 | tf_op jit(solution)/shard_map/all_to_all | solution.py:410
  36.7 1.9 %collective-permute-start.5 = (bf16[8,16,1024]{2,1,0:T(8,128)(2,1)}, bf16[8,16,1024]{2,1,0:T(8,128)(2,1)S(1)}, u32[]{:S(2)}, u32[]{:S(2)}) collective-permute-start(bf16[8,16,1024]{2,1,0:T(8,128)(2,1)} %get-tuple-element.79), channel_id=1, source_target_pairs={{0,5},{1,4},{2,7},{3,6},{4,1},{5,0},{6,3},{7,2},{8,13},{9,12},{10,... | collective-permute-start | bytes 786440 | tf_op jit(solution)/shard_map/ppermute | solution.py:407
  42.1 2.5 %collective-permute-start.7 = (bf16[8,16,1024]{2,1,0:T(8,128)(2,1)}, bf16[8,16,1024]{2,1,0:T(8,128)(2,1)S(1)}, u32[]{:S(2)}, u32[]{:S(2)}) collective-permute-start(bf16[8,16,1024]{2,1,0:T(8,128)(2,1)} %get-tuple-element.83), channel_id=1, source_target_pairs={{0,9},{1,8},{2,11},{3,10},{4,13},{5,12},{6,15},{7,14},{8,1},{9,0},... | collective-permute-start | bytes 786440 | tf_op jit(solution)/shard_map/ppermute | solution.py:407
  44.6 4.2 %collective-permute-done.3.rest_7_ = bf16[8,16,1024]{2,1,0:T(8,128)(2,1)S(1)} collective-permute-done((bf16[8,16,1024]{2,1,0:T(8,128)(2,1)}, bf16[8,16,1024]{2,1,0:T(8,128)(2,1)S(1)}, u32[]{:S(2)}, u32[]{:S(2)}) %collective-permute-start.3) | collective-permute-done | bytes 262176 | tf_op jit(solution)/shard_map/ppermute | solution.py:407
  48.8 3.3 %collective-permute-done.4.rest_8_ = bf16[8,16,1024]{2,1,0:T(8,128)(2,1)S(1)} collective-permute-done((bf16[8,16,1024]{2,1,0:T(8,128)(2,1)}, bf16[8,16,1024]{2,1,0:T(8,128)(2,1)S(1)}, u32[]{:S(2)}, u32[]{:S(2)}) %collective-permute-start.4) | collective-permute-done | bytes 262176 | tf_op jit(solution)/shard_map/ppermute | solution.py:407
  52.1 3.2 %collective-permute-start.9 = (bf16[8,16,1024]{2,1,0:T(8,128)(2,1)}, bf16[8,16,1024]{2,1,0:T(8,128)(2,1)}, u32[]{:S(2)}, u32[]{:S(2)}) collective-permute-start(bf16[8,16,1024]{2,1,0:T(8,128)(2,1)} %get-tuple-element.85), channel_id=1, source_target_pairs={{0,13},{1,12},{2,15},{3,14},{4,9},{5,8},{6,11},{7,10},{8,5},{9,4},... | collective-permute-start | bytes 786440 | tf_op jit(solution)/shard_map/ppermute | solution.py:407
  57.6 8.0 %shard_map.72 = bf16[128,16,1024]{2,1,0:T(8,128)(2,1)} custom-call(s32[16,2,128]{2,1,0:T(2,128)} %copy-done.1, s32[16,2,128]{2,1,0:T(2,128)} %copy-done.1, bf16[128,16,1024]{2,1,0:T(8,128)(2,1)} %store_hbm.3, bf16[16,16,1024]{2,1,0:T(8,128)(2,1)} %copy-done), custom_call_target="tpu_custom_call" | custom-call | bytes 8388608 | tf_op jit(solution)/shard_map/pallas_call | solution.py:484
  66.0 3.0 %collective-permute-start.11 = (bf16[8,16,1024]{2,1,0:T(8,128)(2,1)S(1)}, bf16[8,16,1024]{2,1,0:T(8,128)(2,1)}, u32[]{:S(2)}, u32[]{:S(2)}) collective-permute-start(bf16[8,16,1024]{2,1,0:T(8,128)(2,1)S(1)} %copy-done.17), channel_id=1, source_target_pairs={{0,10},{1,11},{2,8},{3,9},{4,14},{5,15},{6,12},{7,13},{8,2},{9,3},... | collective-permute-start | bytes 786440 | tf_op jit(solution)/shard_map/ppermute | solution.py:407
  69.9 2.1 %collective-permute-start.13 = (bf16[8,16,1024]{2,1,0:T(8,128)(2,1)S(1)}, bf16[8,16,1024]{2,1,0:T(8,128)(2,1)}, u32[]{:S(2)}, u32[]{:S(2)}) collective-permute-start(bf16[8,16,1024]{2,1,0:T(8,128)(2,1)S(1)} %copy-done.14), channel_id=1, source_target_pairs={{0,14},{1,15},{2,12},{3,13},{4,10},{5,11},{6,8},{7,9},{8,6},{9,7},... | collective-permute-start | bytes 786440 | tf_op jit(solution)/shard_map/ppermute | solution.py:407
  72.0 5.6 %collective-permute-done.9.rest_7_ = bf16[8,16,1024]{2,1,0:T(8,128)(2,1)} collective-permute-done((bf16[8,16,1024]{2,1,0:T(8,128)(2,1)}, bf16[8,16,1024]{2,1,0:T(8,128)(2,1)}, u32[]{:S(2)}, u32[]{:S(2)}) %collective-permute-start.9) | collective-permute-done | bytes 262176 | tf_op jit(solution)/shard_map/ppermute | solution.py:407
  79.4 18.2 %shard_map.73 = (f32[5,4,128,384]{3,2,1,0:T(8,128)}, f32[5,8,384]{2,1,0:T(8,128)}) custom-call(s32[48]{0:T(128)} %get-tuple-element.97.place, s32[48]{0:T(128)} %copy-done.10, s32[5]{0:T(128)} %and_select_fusion.tiles, s32[5,1,128]{2,1,0:T(1,128)} %tile.9.rest_0_, s32[1,160]{1,0:T(1,128)} %rest_1_.2, bf16[160,6144]{1,0:T(8,128)(2,1)} %bitcast.66, ...), custom_call_target="tpu_custom_call" | custom-call | flops 4831838208 | bytes 7995392 | tf_op jit(solution)/shard_map/pallas_call | solution.py:312
  97.7 1.9 %collective-permute-start.15 = (bf16[8,16,1024]{2,1,0:T(8,128)(2,1)S(1)}, bf16[8,16,1024]{2,1,0:T(8,128)(2,1)S(1)}, u32[]{:S(2)}, u32[]{:S(2)}) collective-permute-start(bf16[8,16,1024]{2,1,0:T(8,128)(2,1)S(1)} %copy-done.12), channel_id=1, source_target_pairs={{0,11},{1,10},{2,9},{3,8},{4,15},{5,14},{6,13},{7,12},{8,3},{9,2},... | collective-permute-start | bytes 786440 | tf_op jit(solution)/shard_map/ppermute | solution.py:407
  99.6 4.7 %collective-permute-start.16 = (bf16[8,16,1024]{2,1,0:T(8,128)(2,1)S(1)}, bf16[8,16,1024]{2,1,0:T(8,128)(2,1)S(1)}, u32[]{:S(2)}, u32[]{:S(2)}) collective-permute-start(bf16[8,16,1024]{2,1,0:T(8,128)(2,1)S(1)} %copy-done.11), channel_id=1, source_target_pairs={{0,15},{1,14},{2,13},{3,12},{4,11},{5,10},{6,9},{7,8},{8,7},{9,6},... | collective-permute-start | bytes 786440 | tf_op jit(solution)/shard_map/ppermute | solution.py:407
  104.4 18.3 %shard_map.74 = (f32[5,4,128,384]{3,2,1,0:T(8,128)}, f32[5,8,384]{2,1,0:T(8,128)}) custom-call(s32[64]{0:T(128)} %get-tuple-element.99.place, s32[64]{0:T(128)} %copy-done.9, s32[5]{0:T(128)} %and_select_fusion.1.tiles, s32[5,1,128]{2,1,0:T(1,128)} %tile.9.rest_0_, s32[1,160]{1,0:T(1,128)} %rest_1_.2, bf16[160,6144]{1,0:T(8,128)(2,1)} %bitcast.67, ...), custom_call_target="tpu_custom_call" | custom-call | flops 4831838208 | bytes 7995392 | tf_op jit(solution)/shard_map/pallas_call | solution.py:312
  122.7 2.5 %collective-permute-done.16.rest_6_ = bf16[8,16,1024]{2,1,0:T(8,128)(2,1)S(1)} collective-permute-done((bf16[8,16,1024]{2,1,0:T(8,128)(2,1)S(1)}, bf16[8,16,1024]{2,1,0:T(8,128)(2,1)S(1)}, u32[]{:S(2)}, u32[]{:S(2)}) %collective-permute-start.16) | collective-permute-done | bytes 262176 | tf_op jit(solution)/shard_map/ppermute | solution.py:407
  125.9 10.6 %shard_map.75 = bf16[160,6144]{1,0:T(8,128)(2,1)} custom-call(s32[16]{0:T(128)} %get-tuple-element.101.place, s32[16]{0:T(128)} %copy-done.6, s32[5]{0:T(128)} %and_select_fusion.2.tiles, s32[5,1,128]{2,1,0:T(1,128)} %tile.9.rest_0_, s32[1,160]{1,0:T(1,128)} %rest_1_.2, bf16[160,6144]{1,0:T(8,128)(2,1)} %bitcast.68, ...), custom_call_target="tpu_custom_call" | custom-call | flops 1207959552 | bytes 6422528 | tf_op jit(solution)/shard_map/pallas_call | solution.py:312
  (94 shorter events, 14.3 us)
Async XLA Ops:
  2.3 3.5 %collective-permute-start = (s32[1,2,128]{2,1,0:T(2,128)}, s32[1,2,128]{2,1,0:T(2,128)S(1)}, u32[]{:S(2)}, u32[]{:S(2)}) collective-permute-start(s32[1,2,128]{2,1,0:T(2,128)} %get-tuple-element.49), channel_id=1, source_target_pairs={{0,8},{1,9},{2,10},{3,11},{4,12},{5,13},{6,14},{7,15},{8,0},{9,1},... | collective-permute-start | bytes 3080 | tf_op jit(solution)/shard_map/ppermute | solution.py:407
  4.6 2.6 %collective-permute-start.1 = (s32[1,2,128]{2,1,0:T(2,128)}, s32[1,2,128]{2,1,0:T(2,128)S(1)}, u32[]{:S(2)}, u32[]{:S(2)}) collective-permute-start(s32[1,2,128]{2,1,0:T(2,128)} %get-tuple-element.50), channel_id=1, source_target_pairs={{0,12},{1,13},{2,14},{3,15},{4,8},{5,9},{6,10},{7,11},{8,4},{9,5},... | collective-permute-start | bytes 3080 | tf_op jit(solution)/shard_map/ppermute | solution.py:407
  10.3 12.6 %all-to-all-start = ((s32[16,2,128]{2,1,0:T(2,128)}), s32[16,2,128]{2,1,0:T(2,128)S(1)}, u32[]{:S(2)}, u32[]{:S(2)}) async-start(s32[16,2,128]{2,1,0:T(2,128)} %get-tuple-element.54), calls=%async_computation | async-start | bytes 32768 | tf_op jit(solution)/shard_map/all_to_all | solution.py:410
  17.9 24.2 %collective-permute-start.2 = (bf16[8,16,1024]{2,1,0:T(8,128)(2,1)}, bf16[8,16,1024]{2,1,0:T(8,128)(2,1)S(1)}, u32[]{:S(2)}, u32[]{:S(2)}) collective-permute-start(bf16[8,16,1024]{2,1,0:T(8,128)(2,1)} %get-tuple-element.76), channel_id=1, source_target_pairs={{0,8},{1,9},{2,10},{3,11},{4,12},{5,13},{6,14},{7,15},{8,0},{9,1},... | collective-permute-start | bytes 786440 | tf_op jit(solution)/shard_map/ppermute | solution.py:407
  20.0 28.8 %collective-permute-start.3 = (bf16[8,16,1024]{2,1,0:T(8,128)(2,1)}, bf16[8,16,1024]{2,1,0:T(8,128)(2,1)S(1)}, u32[]{:S(2)}, u32[]{:S(2)}) collective-permute-start(bf16[8,16,1024]{2,1,0:T(8,128)(2,1)} %get-tuple-element.77), channel_id=1, source_target_pairs={{0,12},{1,13},{2,14},{3,15},{4,8},{5,9},{6,10},{7,11},{8,4},{9,5},... | collective-permute-start | bytes 786440 | tf_op jit(solution)/shard_map/ppermute | solution.py:407
  30.3 26.5 %all-to-all-start.1 = ((bf16[16,16,1024]{2,1,0:T(8,128)(2,1)}), bf16[16,16,1024]{2,1,0:T(8,128)(2,1)S(1)}, u32[]{:S(2)}, u32[]{:S(2)}) async-start(bf16[16,16,1024]{2,1,0:T(8,128)(2,1)} %shard_map.71), calls=%async_computation.1 | async-start | bytes 1048576 | tf_op jit(solution)/shard_map/all_to_all | solution.py:410
  36.6 15.5 %collective-permute-start.4 = (bf16[8,16,1024]{2,1,0:T(8,128)(2,1)}, bf16[8,16,1024]{2,1,0:T(8,128)(2,1)S(1)}, u32[]{:S(2)}, u32[]{:S(2)}) collective-permute-start(bf16[8,16,1024]{2,1,0:T(8,128)(2,1)} %get-tuple-element.78), channel_id=1, source_target_pairs={{0,4},{1,5},{2,6},{3,7},{4,0},{5,1},{6,2},{7,3},{8,12},{9,13},{10,... | collective-permute-start | bytes 786440 | tf_op jit(solution)/shard_map/ppermute | solution.py:407
  36.7 29.0 %collective-permute-start.5 = (bf16[8,16,1024]{2,1,0:T(8,128)(2,1)}, bf16[8,16,1024]{2,1,0:T(8,128)(2,1)S(1)}, u32[]{:S(2)}, u32[]{:S(2)}) collective-permute-start(bf16[8,16,1024]{2,1,0:T(8,128)(2,1)} %get-tuple-element.79), channel_id=1, source_target_pairs={{0,5},{1,4},{2,7},{3,6},{4,1},{5,0},{6,3},{7,2},{8,13},{9,12},{10,... | collective-permute-start | bytes 786440 | tf_op jit(solution)/shard_map/ppermute | solution.py:407
  38.6 27.4 %collective-permute-start.6 = (bf16[8,16,1024]{2,1,0:T(8,128)(2,1)}, bf16[8,16,1024]{2,1,0:T(8,128)(2,1)S(1)}, u32[]{:S(2)}, u32[]{:S(2)}) collective-permute-start(bf16[8,16,1024]{2,1,0:T(8,128)(2,1)} %get-tuple-element.80), channel_id=1, source_target_pairs={{0,1},{1,0},{2,3},{3,2},{4,5},{5,4},{6,7},{7,6},{8,9},{9,8},{10,11... | collective-permute-start | bytes 786440 | tf_op jit(solution)/shard_map/ppermute | solution.py:407
  39.4 26.3 %copy-start.10 = (s32[48]{0:T(128)}, s32[48]{0:T(128)S(1)}, u32[]{:S(2)}) copy-start(s32[48]{0:T(128)S(1)} %get-tuple-element.96.page_number) | copy-start | bytes 580
  42.1 37.3 %copy-start.16 = (bf16[8,16,1024]{2,1,0:T(8,128)(2,1)}, bf16[8,16,1024]{2,1,0:T(8,128)(2,1)S(1)}, u32[]{:S(2)}) copy-start(bf16[8,16,1024]{2,1,0:T(8,128)(2,1)S(1)} %collective-permute-done.2.rest_6_) | copy-start | bytes 786436
  42.1 27.0 %collective-permute-start.7 = (bf16[8,16,1024]{2,1,0:T(8,128)(2,1)}, bf16[8,16,1024]{2,1,0:T(8,128)(2,1)S(1)}, u32[]{:S(2)}, u32[]{:S(2)}) collective-permute-start(bf16[8,16,1024]{2,1,0:T(8,128)(2,1)} %get-tuple-element.83), channel_id=1, source_target_pairs={{0,9},{1,8},{2,11},{3,10},{4,13},{5,12},{6,15},{7,14},{8,1},{9,0},... | collective-permute-start | bytes 786440 | tf_op jit(solution)/shard_map/ppermute | solution.py:407
  48.8 30.6 %copy-start.18 = (bf16[8,16,1024]{2,1,0:T(8,128)(2,1)}, bf16[8,16,1024]{2,1,0:T(8,128)(2,1)S(1)}, u32[]{:S(2)}) copy-start(bf16[8,16,1024]{2,1,0:T(8,128)(2,1)S(1)} %collective-permute-done.3.rest_7_) | copy-start | bytes 786436
  48.8 21.1 %collective-permute-start.8 = (bf16[8,16,1024]{2,1,0:T(8,128)(2,1)}, bf16[8,16,1024]{2,1,0:T(8,128)(2,1)}, u32[]{:S(2)}, u32[]{:S(2)}) collective-permute-start(bf16[8,16,1024]{2,1,0:T(8,128)(2,1)} %get-tuple-element.84), channel_id=1, source_target_pairs={{0,6},{1,7},{2,4},{3,5},{4,2},{5,3},{6,0},{7,1},{8,14},{9,15},{10,... | collective-permute-start | bytes 786440 | tf_op jit(solution)/shard_map/ppermute | solution.py:407
  52.1 27.3 %copy-start.20 = (bf16[8,16,1024]{2,1,0:T(8,128)(2,1)}, bf16[8,16,1024]{2,1,0:T(8,128)(2,1)S(1)}, u32[]{:S(2)}) copy-start(bf16[8,16,1024]{2,1,0:T(8,128)(2,1)S(1)} %collective-permute-done.4.rest_8_) | copy-start | bytes 786436
  52.1 25.5 %collective-permute-start.9 = (bf16[8,16,1024]{2,1,0:T(8,128)(2,1)}, bf16[8,16,1024]{2,1,0:T(8,128)(2,1)}, u32[]{:S(2)}, u32[]{:S(2)}) collective-permute-start(bf16[8,16,1024]{2,1,0:T(8,128)(2,1)} %get-tuple-element.85), channel_id=1, source_target_pairs={{0,13},{1,12},{2,15},{3,14},{4,9},{5,8},{6,11},{7,10},{8,5},{9,4},... | collective-permute-start | bytes 786440 | tf_op jit(solution)/shard_map/ppermute | solution.py:407
  65.7 32.0 %collective-permute-start.10 = (bf16[8,16,1024]{2,1,0:T(8,128)(2,1)S(1)}, bf16[8,16,1024]{2,1,0:T(8,128)(2,1)}, u32[]{:S(2)}, u32[]{:S(2)}) collective-permute-start(bf16[8,16,1024]{2,1,0:T(8,128)(2,1)S(1)} %copy-done.19), channel_id=1, source_target_pairs={{0,7},{1,6},{2,5},{3,4},{4,3},{5,2},{6,1},{7,0},{8,15},{9,14},{10,... | collective-permute-start | bytes 786440 | tf_op jit(solution)/shard_map/ppermute | solution.py:407
  66.0 33.6 %collective-permute-start.11 = (bf16[8,16,1024]{2,1,0:T(8,128)(2,1)S(1)}, bf16[8,16,1024]{2,1,0:T(8,128)(2,1)}, u32[]{:S(2)}, u32[]{:S(2)}) collective-permute-start(bf16[8,16,1024]{2,1,0:T(8,128)(2,1)S(1)} %copy-done.17), channel_id=1, source_target_pairs={{0,10},{1,11},{2,8},{3,9},{4,14},{5,15},{6,12},{7,13},{8,2},{9,3},... | collective-permute-start | bytes 786440 | tf_op jit(solution)/shard_map/ppermute | solution.py:407
  69.0 28.6 %copy-start.22 = (bf16[8,16,1024]{2,1,0:T(8,128)(2,1)}, bf16[8,16,1024]{2,1,0:T(8,128)(2,1)S(1)}, u32[]{:S(2)}) copy-start(bf16[8,16,1024]{2,1,0:T(8,128)(2,1)S(1)} %collective-permute-done.7.rest_5_) | copy-start | bytes 786436
  69.0 35.3 %collective-permute-start.12 = (bf16[8,16,1024]{2,1,0:T(8,128)(2,1)S(1)}, bf16[8,16,1024]{2,1,0:T(8,128)(2,1)}, u32[]{:S(2)}, u32[]{:S(2)}) collective-permute-start(bf16[8,16,1024]{2,1,0:T(8,128)(2,1)S(1)} %copy-done.15), channel_id=1, source_target_pairs={{0,2},{1,3},{2,0},{3,1},{4,6},{5,7},{6,4},{7,5},{8,10},{9,11},{10,... | collective-permute-start | bytes 786440 | tf_op jit(solution)/shard_map/ppermute | solution.py:407
  69.9 34.5 %collective-permute-start.13 = (bf16[8,16,1024]{2,1,0:T(8,128)(2,1)S(1)}, bf16[8,16,1024]{2,1,0:T(8,128)(2,1)}, u32[]{:S(2)}, u32[]{:S(2)}) collective-permute-start(bf16[8,16,1024]{2,1,0:T(8,128)(2,1)S(1)} %copy-done.14), channel_id=1, source_target_pairs={{0,14},{1,15},{2,12},{3,13},{4,10},{5,11},{6,8},{7,9},{8,6},{9,7},... | collective-permute-start | bytes 786440 | tf_op jit(solution)/shard_map/ppermute | solution.py:407
  77.6 26.7 %collective-permute-start.14 = (bf16[8,16,1024]{2,1,0:T(8,128)(2,1)S(1)}, bf16[8,16,1024]{2,1,0:T(8,128)(2,1)}, u32[]{:S(2)}, u32[]{:S(2)}) collective-permute-start(bf16[8,16,1024]{2,1,0:T(8,128)(2,1)S(1)} %copy-done.13), channel_id=1, source_target_pairs={{0,3},{1,2},{2,1},{3,0},{4,7},{5,6},{6,5},{7,4},{8,11},{9,10},{10,... | collective-permute-start | bytes 786440 | tf_op jit(solution)/shard_map/ppermute | solution.py:407
  97.7 25.0 %collective-permute-start.15 = (bf16[8,16,1024]{2,1,0:T(8,128)(2,1)S(1)}, bf16[8,16,1024]{2,1,0:T(8,128)(2,1)S(1)}, u32[]{:S(2)}, u32[]{:S(2)}) collective-permute-start(bf16[8,16,1024]{2,1,0:T(8,128)(2,1)S(1)} %copy-done.12), channel_id=1, source_target_pairs={{0,11},{1,10},{2,9},{3,8},{4,15},{5,14},{6,13},{7,12},{8,3},{9,2},... | collective-permute-start | bytes 786440 | tf_op jit(solution)/shard_map/ppermute | solution.py:407
  99.6 25.6 %collective-permute-start.16 = (bf16[8,16,1024]{2,1,0:T(8,128)(2,1)S(1)}, bf16[8,16,1024]{2,1,0:T(8,128)(2,1)S(1)}, u32[]{:S(2)}, u32[]{:S(2)}) collective-permute-start(bf16[8,16,1024]{2,1,0:T(8,128)(2,1)S(1)} %copy-done.11), channel_id=1, source_target_pairs={{0,15},{1,14},{2,13},{3,12},{4,11},{5,10},{6,9},{7,8},{8,7},{9,6},... | collective-permute-start | bytes 786440 | tf_op jit(solution)/shard_map/ppermute | solution.py:407
  (19 other events, 235.5 us)

commit v14 on v13

--- a/solution.py
+++ b/solution.py
@@ -159,18 +159,19 @@
     pltpu.make_async_copy(store_out, store_out, out_sem).wait()
 
 
-def attend_kernel(first, last, tile_pages, sources, place, page_number, tiles, *rest):
-    sel_ref, positions_ref, query_ref, *rest = rest
+def attend_kernel(first, last, tile_pages, sources, place, tiles, *rest):
+    sel_ref, position, query_ref, *rest = rest
     if first:
-        fresh_ref, fresh_positions, *rest = rest
+        fresh_ref, *rest = rest
     state_in = () if first else rest[:2]
     rest = rest if first else rest[2:]
     contexts, rest = rest[:sources], rest[sources:]
     outs, rest = (rest[:1], rest[1:]) if last else (rest[:2], rest[2:])
-    kv, values, position, query, scores, raised, mixed, stats, sem = rest
+    kv, values, query, scores, raised, mixed, stats, sem = rest
     pages, page_len, width = kv.shape
     each = contexts[0].shape[0]
     ahead = FRESH_PAGES if first else 0
+    direct = last and not first
     block = query_ref.shape[0]
     tile = tile_pages * page_len
     lanes = QUERY_GROUP * block
@@ -186,34 +187,19 @@
     @pl.when(step == 0)
     def _():
         for i, context in enumerate(contexts):
-            for k in range(each):
-                pltpu.make_async_copy(context.at[k], kv.at[ahead + place[i * each + k]], sem).start()
+            if direct:
+                kv[i * each : (i + 1) * each] = context[...]
+            else:
+                for k in range(each):
+                    to = kv.at[ahead + place[i * each + k]]
+                    pltpu.make_async_copy(context.at[k], to, sem).start()
         if first:
-            picked = fresh_ref.shape[0]
-            count = picked // page_len
+            count = fresh_ref.shape[0] // page_len
             kv[0:count] = fresh_ref[...].reshape(count, page_len, width)
             kv[count:ahead] = jnp.zeros((ahead - count, page_len, width), bf16)
-            position[0:picked, :] = fresh_positions[...]
-            start = ahead * page_len
-            position[picked:start, :] = jnp.full((start - picked, LANES), FAR_POSITION, jnp.int32)
-        positions = positions_ref[...]
-        row = lax.broadcasted_iota(jnp.int32, (page_len, positions.shape[1]), 0)
-        ones = jnp.ones((positions.shape[1], LANES), bf16)
-        row_lanes = lax.broadcasted_iota(jnp.int32, (page_len, LANES), 0)
-
-        def place_rows(t, carry):
-            starts = [page_number[t * FRESH_PAGES + k] * page_len for k in range(FRESH_PAGES)]
-            hit = jnp.concatenate([one_hot(row + start == positions) for start in starts], axis=0)
-            hidden = jnp.dot(hit.astype(bf16), ones, preferred_element_type=f32)
-            plain = jnp.concatenate([row_lanes + start for start in starts], axis=0)
-            some = FRESH_PAGES * page_len
-            here = pl.ds(pl.multiple_of(ahead * page_len + t * some, some), some)
-            position[here, :] = jnp.where(hidden > 0.0, FAR_POSITION, plain)
-            return carry
-
-        lax.fori_loop(0, (pages - ahead) // FRESH_PAGES, place_rows, 0)
-        used = kv.at[ahead:]
-        pltpu.make_async_copy(used, used, sem).wait()
+        if not direct:
+            used = kv.at[ahead:]
+            pltpu.make_async_copy(used, used, sem).wait()
 
         def turn(t, carry):
             here = pl.ds(t * tile_pages, tile_pages)
@@ -293,7 +279,8 @@
         outs[1][0] = stats[...]
 
 
-def attend(first, last, tile_pages, order, sel_lanes, positions, queries, fresh, state, contexts):
+def attend(first, last, tile_pages, order, sel_lanes, queries, fresh, state, contexts):
+    place, tiles, position = order
     picked, features = queries.shape
     each, page_len, width = contexts[0].shape
     pages = each * len(contexts) + (FRESH_PAGES if first else 0)
@@ -312,15 +299,19 @@
     return pl.pallas_call(
         functools.partial(attend_kernel, first, last, tile_pages, len(contexts)),
         grid_spec=pltpu.PrefetchScalarGridSpec(
-            num_scalar_prefetch=3,
+            num_scalar_prefetch=2,
             grid=(steps,),
             in_specs=[
                 pl.BlockSpec((1, 1, LANES), lambda b, *_: (b, 0, 0)),
-                pl.BlockSpec(positions.shape, lambda b, *_: (0, 0)),
+                pl.BlockSpec(position.shape, lambda b, *_: (0, 0)),
                 wide,
-                *[pl.BlockSpec(x.shape, lambda b, *_: (0, 0)) for x in fresh if first],
-                *([] if first else state_specs),
-                *[pl.BlockSpec(memory_space=pltpu.HBM)] * len(contexts),
+                *([pl.BlockSpec(fresh.shape, lambda b, *_: (0, 0))] if first else state_specs),
+                *[
+                    pl.BlockSpec(x.shape, lambda b, *_: (0, 0, 0))
+                    if last and not first
+                    else pl.BlockSpec(memory_space=pltpu.HBM)
+                    for x in contexts
+                ],
             ],
             out_specs=[wide] if last else state_specs,
             scratch_shapes=[
@@ -328,7 +319,6 @@
                 pltpu.VMEM(
                     (pages // tile_pages, KEY_VALUE_HEADS, LANES, tile_pages * page_len), jnp.bfloat16
                 ),
-                pltpu.VMEM((pages * page_len, LANES), jnp.int32),
                 pltpu.VMEM((KEY_VALUE_HEADS, lanes, LANES), jnp.bfloat16),
                 pltpu.VMEM((KEY_VALUE_HEADS, tile_pages * page_len, lanes), jnp.float32),
                 pltpu.VMEM((KEY_VALUE_HEADS, tile_pages * page_len, lanes), jnp.bfloat16),
@@ -346,7 +336,7 @@
             bytes_accessed=2 * pages * page_len * width + 6 * picked * features,
             transcendentals=int(share * picked * features // LANES * pages * page_len),
         ),
-    )(*order, sel_lanes, positions, queries, *[x for x in fresh if first], *state, *contexts)
+    )(place, tiles, sel_lanes, position, queries, *([fresh] if first else state), *contexts)
 
 
 def page_order(slots, positions, own, hold, capacity, groups, tiles, page_len):
@@ -369,6 +359,8 @@
             count = len(group) * capacity
         member = arrival >= 0
         place = jnp.sum((member[None, :] & before).astype(jnp.int32), axis=1)
+        if at == len(groups) - 1 and at > 0:
+            place = arrival
         index = jnp.arange(count)[:, None]
         places = jnp.sum(jnp.where(arrival[None, :] == index, place[None, :], 0), axis=1)
         page = jnp.sum(
@@ -376,7 +368,15 @@
         )
         seen = jnp.sum((page[None, :] <= last_page[:, None]).astype(jnp.int32), axis=1)
         seen = seen + (FRESH_PAGES if at == 0 else 0)
-        orders.append((places, page, (seen + tile_pages - 1) // tile_pages))
+        rows = (page[:, None] * page_len + jnp.arange(page_len)[None, :]).reshape(-1, 1)
+        replaced = jnp.any(rows == positions[None, :], axis=1, keepdims=True)
+        rows = jnp.where(replaced, FAR_POSITION, rows)
+        if at == 0:
+            room = FRESH_PAGES * page_len - positions.shape[0]
+            room = jnp.full((room, 1), FAR_POSITION, jnp.int32)
+            rows = jnp.concatenate([positions[:, None], room, rows])
+        rows = jnp.broadcast_to(rows, (rows.shape[0], LANES))
+        orders.append((places, (seen + tile_pages - 1) // tile_pages, rows))
     return orders
 
 
@@ -474,11 +474,12 @@
     )(own_word, index_in, store)
     parts, packed, table, positions = lax.optimization_barrier((parts, packed, table, positions))
     if others:
-        for d, part in zip(others, parts):
-            arrived[d] = swap(part, d) if d else part
-        contexts = [[arrived[d] for d in group] for group in groups]
+        parts = dict(zip(others, parts))
+        held = others[-4:]
+        for d in others[:-4]:
+            arrived[d] = swap(parts[d], d) if d else parts[d]
     else:
-        contexts = [[exchange(parts[0]).reshape(pages, page_len, width)]]
+        arrived[None] = exchange(parts[0]).reshape(pages, page_len, width)
     rows_in = exchange(packed)
 
     store_out = pl.pallas_call(
@@ -505,22 +506,24 @@
     tiles = [LATE_TILE_PAGES if at == len(groups) - 1 else TILE_PAGES for at in range(len(groups))]
     orders = page_order(table[0], positions[0], own, hold, capacity, groups, tiles, page_len)
     sel_lanes = jnp.tile(positions.reshape(-1, 1, QUERY_BLOCK), (1, 1, LANES // QUERY_BLOCK))
-    sel_rows = jnp.broadcast_to(positions.reshape(picked, 1), (picked, LANES))
     store_out, sel_lanes = lax.optimization_barrier((store_out, sel_lanes))
     state = ()
-    for at, (arrays, order) in enumerate(zip(contexts, orders)):
+    for at, (group, order) in enumerate(zip(groups, orders)):
         state = attend(
             at == 0,
             at == len(groups) - 1,
             tiles[at],
             order,
             sel_lanes,
-            positions,
             queries[0],
-            (fresh, sel_rows),
+            fresh,
             state,
-            arrays,
+            [arrived[d] for d in group or [None]],
         )
+        if at == 0 and others:
+            state, late = lax.optimization_barrier((state, [parts[d] for d in held]))
+            for d, part in zip(held, late):
+                arrived[d] = swap(part, d)
     return (state[0][None], store_out)
 
 

time: 139 us -> 162 us (1.17)
  waiting for transfers between devices: 19.6 us -> 42.6 us
  starting transfers between devices: 39.2 us -> 35.9 us
  local copies, waits for them, and re-layouts: 4.97 us -> 6.71 us
    ppermute x17, waiting for transfers between devices: 19 us -> 31.4 us  [swap(): return lax.ppermute(x, 'store', [(h, h ^ d) for h in range(holders)])]
    all_to_all x2, waiting for transfers between devices: 0.57 us -> 11.2 us  [exchange(): return lax.all_to_all(x, 'store', split_axis=0, concat_axis=0, tiled=True)]
    ppermute x17, starting transfers between devices: 25.4 us -> 22 us  [swap(): return lax.ppermute(x, 'store', [(h, h ^ d) for h in range(holders)])]
    broadcast_in_dim x1 -> x4, local copies, waits for them, and re-layouts: 0.71 us -> 2.8 us  [the longest x3 2.8 us: page_order(): rows = jnp.broadcast_to(rows, (rows.shape[0], LANES))]
  transfers between devices with their start and end apart: 19 -> 19, of which waited for: 8 -> 6; matrix products, arithmetic and copies ran while one was open for 5% -> 6% of each run, Pallas kernels for 38% -> 34%
where the time goes in v14:
time: 162 us; the launch traced here: 160 us
  Pallas kernels  68.1 us (42%)
  waiting for transfers between devices  42.6 us (26%)
  starting transfers between devices  35.9 us (22%)
  local copies, waits for them, and re-layouts  6.71 us (4%)
  other arithmetic  5.85 us (4%)
    pallas_call x3, Pallas kernels, attend(): pl.pallas_call(functools.partial(attend_kernel, first, last, tile_pages,...  48.6 us
    ppermute x17, waiting for transfers between devices, swap(): return lax.ppermute(x, 'store', [(h, h ^ d) for h in range(holders)])  31.4 us
    ppermute x17, starting transfers between devices, swap(): return lax.ppermute(x, 'store', [(h, h ^ d) for h in range(holders)])  22 us
    all_to_all x2, starting transfers between devices, exchange(): return lax.all_to_all(x, 'store', split_axis=0, concat_axis=0, tiled=True)  13.9 us
    all_to_all x2, waiting for transfers between devices, exchange(): return lax.all_to_all(x, 'store', split_axis=0, concat_axis=0, tiled=True)  11.2 us
    pallas_call x1, Pallas kernels, per_device(): pl.pallas_call(write_back_kernel, grid_spec=pltpu.PrefetchScalarGridSpec(...  8.02 us
    pallas_call x1, Pallas kernels, per_device(): pl.pallas_call(functools.partial(gather_kernel, capacity, others), grid_s...  4.92 us
  transfers between devices with their start and end apart: 19, of which 6 were waited for; matrix products, arithmetic and copies ran while one was open for 6% of the time, Pallas kernels for 34%

profile of v14, /device:TPU:9, one launch (start us, length us, event | category | flops | bytes accessed | tf_op | source)
XLA Modules:
  0.0 160.2 jit_solution(1679015284202681805)
XLA Ops:
  0.6 1.7 %shard_map.68 = (s32[16,2,128]{2,1,0:T(2,128)}, s32[1,2,128]{2,1,0:T(2,128)}, s32[1,2,128]{2,1,0:T(2,128)}) custom-call(s32[1]{0:T(128)} %bitcast.own, s32[1,128]{1,0:T(1,128)} %table_ref.2, s32[1,160]{1,0:T(1,128)} %sel_ref.2), custom_call_target="tpu_custom_call" | custom-call | tf_op jit(solution)/shard_map/pallas_call | solution.py:412
  2.3 2.3 %collective-permute-start = (s32[1,2,128]{2,1,0:T(2,128)}, s32[1,2,128]{2,1,0:T(2,128)S(1)}, u32[]{:S(2)}, u32[]{:S(2)}) collective-permute-start(s32[1,2,128]{2,1,0:T(2,128)} %get-tuple-element.55), channel_id=1, source_target_pairs={{0,8},{1,9},{2,10},{3,11},{4,12},{5,13},{6,14},{7,15},{8,0},{9,1},... | collective-permute-start | bytes 3080 | tf_op jit(solution)/shard_map/ppermute | solution.py:407
  4.6 1.2 collective-permute-done.refs_0_
  5.8 1.4 collective-permute-done.1.refs_1_
  7.8 2.5 %shard_map.69 = (bf16[8,16,1024]{2,1,0:T(8,128)(2,1)}, bf16[8,16,1024]{2,1,0:T(8,128)(2,1)}) custom-call(s32[1,2,128]{2,1,0:T(2,128)} %copy-done.6, s32[1,2,128]{2,1,0:T(2,128)} %copy-done.7, bf16[128,16,1024]{2,1,0:T(8,128)(2,1)} %store_hbm.3), custom_call_target="tpu_custom_call" | custom-call | tf_op jit(solution)/shard_map/pallas_call | solution.py:430
  10.3 7.6 %all-to-all-start = ((s32[16,2,128]{2,1,0:T(2,128)}), s32[16,2,128]{2,1,0:T(2,128)S(1)}, u32[]{:S(2)}, u32[]{:S(2)}) async-start(s32[16,2,128]{2,1,0:T(2,128)} %get-tuple-element.60), calls=%async_computation | async-start | bytes 32768 | tf_op jit(solution)/shard_map/all_to_all | solution.py:410
  18.0 2.1 %collective-permute-start.2 = (bf16[8,16,1024]{2,1,0:T(8,128)(2,1)}, bf16[8,16,1024]{2,1,0:T(8,128)(2,1)S(1)}, u32[]{:S(2)}, u32[]{:S(2)}) collective-permute-start(bf16[8,16,1024]{2,1,0:T(8,128)(2,1)} %get-tuple-element.82), channel_id=1, source_target_pairs={{0,8},{1,9},{2,10},{3,11},{4,12},{5,13},{6,14},{7,15},{8,0},{9,1},... | collective-permute-start | bytes 786440 | tf_op jit(solution)/shard_map/ppermute | solution.py:407
  20.1 2.4 %shard_map.71 = bf16[16,16,1024]{2,1,0:T(8,128)(2,1)} custom-call(s32[1,128]{1,0:T(1,128)} %table_ref.2, s32[1,160]{1,0:T(1,128)} %sel_ref.2, bf16[160,1024]{1,0:T(8,128)(2,1)} %bitcast.73), custom_call_target="tpu_custom_call" | custom-call | tf_op jit(solution)/shard_map/pallas_call | solution.py:454
  23.5 4.9 %shard_map.70 = (bf16[8,16,1024]{2,1,0:T(8,128)(2,1)}, bf16[8,16,1024]{2,1,0:T(8,128)(2,1)}, bf16[8,16,1024]{2,1,0:T(8,128)(2,1)}, bf16[8,16,1024]{2,1,0:T(8,128...) custom-call(s32[1]{0:T(128)} %bitcast.own, ...), custom_call_target="tpu_custom_call" | custom-call | tf_op jit(solution)/shard_map/pallas_call | solution.py:463
  32.8 6.4 %all-to-all-start.1 = ((bf16[16,16,1024]{2,1,0:T(8,128)(2,1)}), bf16[16,16,1024]{2,1,0:T(8,128)(2,1)S(1)}, u32[]{:S(2)}, u32[]{:S(2)}) async-start(bf16[16,16,1024]{2,1,0:T(8,128)(2,1)} %shard_map.71), calls=%async_computation.1 | async-start | bytes 1048576 | tf_op jit(solution)/shard_map/all_to_all | solution.py:410
  39.2 1.9 %collective-permute-start.5 = (bf16[8,16,1024]{2,1,0:T(8,128)(2,1)}, bf16[8,16,1024]{2,1,0:T(8,128)(2,1)S(1)}, u32[]{:S(2)}, u32[]{:S(2)}) collective-permute-start(bf16[8,16,1024]{2,1,0:T(8,128)(2,1)} %get-tuple-element.85), channel_id=1, source_target_pairs={{0,5},{1,4},{2,7},{3,6},{4,1},{5,0},{6,3},{7,2},{8,13},{9,12},{10,... | collective-permute-start | bytes 786440 | tf_op jit(solution)/shard_map/ppermute | solution.py:407
  44.4 10.7 %all-to-all-done.1.rows_hbm = bf16[16,16,1024]{2,1,0:T(8,128)(2,1)S(1)} async-done(((bf16[16,16,1024]{2,1,0:T(8,128)(2,1)}), bf16[16,16,1024]{2,1,0:T(8,128)(2,1)S(1)}, u32[]{:S(2)}, u32[]{:S(2)}) %all-to-all-start.1) | async-done | bytes 524320 | tf_op jit(solution)/shard_map/all_to_all | solution.py:410
  55.9 8.0 %shard_map.72 = bf16[128,16,1024]{2,1,0:T(8,128)(2,1)} custom-call(s32[16,2,128]{2,1,0:T(2,128)} %copy-done.1, s32[16,2,128]{2,1,0:T(2,128)} %copy-done.1, bf16[128,16,1024]{2,1,0:T(8,128)(2,1)} %store_hbm.3, bf16[16,16,1024]{2,1,0:T(8,128)(2,1)} %copy-done), custom_call_target="tpu_custom_call" | custom-call | bytes 8388608 | tf_op jit(solution)/shard_map/pallas_call | solution.py:485
  64.3 4.7 %collective-permute-start.11 = (bf16[8,16,1024]{2,1,0:T(8,128)(2,1)S(1)}, bf16[8,16,1024]{2,1,0:T(8,128)(2,1)S(1)}, u32[]{:S(2)}, u32[]{:S(2)}) collective-permute-start(bf16[8,16,1024]{2,1,0:T(8,128)(2,1)S(1)} %copy-done.16), channel_id=1, source_target_pairs={{0,10},{1,11},{2,8},{3,9},{4,14},{5,15},{6,12},{7,13},{8,2},{9,3},... | collective-permute-start | bytes 786440 | tf_op jit(solution)/shard_map/ppermute | solution.py:407
  69.7 1.3 collective-permute-start.8
  72.1 20.0 %shard_map.73 = (f32[5,4,128,384]{3,2,1,0:T(8,128)}, f32[5,8,384]{2,1,0:T(8,128)}) custom-call(s32[48]{0:T(128)} %get-tuple-element.109.place, s32[5]{0:T(128)} %and_select_fusion.tiles, s32[5,1,128]{2,1,0:T(1,128)} %tile.9.rest_0_, s32[1024,128]{1,0:T(8,128)} %broadcast_in_dim.141.rest_1_, bf16[160,6144]{1,0:T(8,128)(2,1)} %bitcast.69, ...), custom_call_target="tpu_custom_call" | custom-call | flops 4831838208 | bytes 7995392 | tf_op jit(solution)/shard_map/pallas_call | solution.py:299
  92.1 2.6 %collective-permute-start.9 = (bf16[8,16,1024]{2,1,0:T(8,128)(2,1)S(1)}, bf16[8,16,1024]{2,1,0:T(8,128)(2,1)S(1)}, u32[]{:S(2)}, u32[]{:S(2)}) collective-permute-start(bf16[8,16,1024]{2,1,0:T(8,128)(2,1)S(1)} %copy-done.12), channel_id=1, source_target_pairs={{0,13},{1,12},{2,15},{3,14},{4,9},{5,8},{6,11},{7,10},{8,5},{9,4},... | collective-permute-start | bytes 786440 | tf_op jit(solution)/shard_map/ppermute | solution.py:407
  95.1 1.3 collective-permute-start.14
  96.6 4.2 %collective-permute-start.15 = (bf16[8,16,1024]{2,1,0:T(8,128)(2,1)S(1)}, bf16[8,16,1024]{2,1,0:T(8,128)(2,1)S(1)}, u32[]{:S(2)}, u32[]{:S(2)}) collective-permute-start(bf16[8,16,1024]{2,1,0:T(8,128)(2,1)S(1)} %copy-done.9), channel_id=1, source_target_pairs={{0,11},{1,10},{2,9},{3,8},{4,15},{5,14},{6,13},{7,12},{8,3},{9,2},... | collective-permute-start | bytes 786440 | tf_op jit(solution)/shard_map/ppermute | solution.py:407
  100.9 23.3 %collective-permute-done.9.rest_7_ = bf16[8,16,1024]{2,1,0:T(8,128)(2,1)S(1)} collective-permute-done((bf16[8,16,1024]{2,1,0:T(8,128)(2,1)S(1)}, bf16[8,16,1024]{2,1,0:T(8,128)(2,1)S(1)}, u32[]{:S(2)}, u32[]{:S(2)}) %collective-permute-start.9) | collective-permute-done | bytes 262176 | tf_op jit(solution)/shard_map/ppermute | solution.py:407
  124.2 5.4 %collective-permute-done.13.rest_11_ = bf16[8,16,1024]{2,1,0:T(8,128)(2,1)S(1)} collective-permute-done((bf16[8,16,1024]{2,1,0:T(8,128)(2,1)S(1)}, bf16[8,16,1024]{2,1,0:T(8,128)(2,1)S(1)}, u32[]{:S(2)}, u32[]{:S(2)}) %collective-permute-start.13) | collective-permute-done | bytes 262176 | tf_op jit(solution)/shard_map/ppermute | solution.py:407
  129.7 1.0 broadcast_in_dim.134.rest_1_
  130.7 18.8 %shard_map.74 = (f32[5,4,128,384]{3,2,1,0:T(8,128)}, f32[5,8,384]{2,1,0:T(8,128)}) custom-call(s32[64]{0:T(128)} %get-tuple-element.111.place, s32[5]{0:T(128)} %and_select_fusion.1.tiles, s32[5,1,128]{2,1,0:T(1,128)} %tile.9.rest_0_, s32[1024,128]{1,0:T(8,128)} %broadcast_in_dim.134.rest_1_, bf16[160,6144]{1,0:T(8,128)(2,1)} %bitcast.70, ...), custom_call_target="tpu_custom_call" | custom-call | flops 4831838208 | bytes 7995392 | tf_op jit(solution)/shard_map/pallas_call | solution.py:299
  150.3 9.9 %shard_map.75 = bf16[160,6144]{1,0:T(8,128)(2,1)} custom-call(s32[16]{0:T(128)} %get-tuple-element.113.place, s32[5]{0:T(128)} %and_select_fusion.2.tiles, s32[5,1,128]{2,1,0:T(1,128)} %tile.9.rest_0_, s32[256,128]{1,0:T(8,128)} %broadcast_in_dim.79.rest_1_, bf16[160,6144]{1,0:T(8,128)(2,1)} %bitcast.71, f32[5,4,128,384]{3,2,1,0:T(8,128)} %get-tuple-element.103.rest_3_, ...), custom_call_target="tpu_custom_call" | custom-call | flops 1207959552 | bytes 6422528 | tf_op jit(solution)/shard_map/pallas_call | solution.py:299
  (122 shorter events, 13.6 us)
Async XLA Ops:
  2.3 3.5 %collective-permute-start = (s32[1,2,128]{2,1,0:T(2,128)}, s32[1,2,128]{2,1,0:T(2,128)S(1)}, u32[]{:S(2)}, u32[]{:S(2)}) collective-permute-start(s32[1,2,128]{2,1,0:T(2,128)} %get-tuple-element.55), channel_id=1, source_target_pairs={{0,8},{1,9},{2,10},{3,11},{4,12},{5,13},{6,14},{7,15},{8,0},{9,1},... | collective-permute-start | bytes 3080 | tf_op jit(solution)/shard_map/ppermute | solution.py:407
  4.6 25.7 %copy-start.4 = (s32[1,160]{1,0:T(1,128)S(1)}, s32[1,160]{1,0:T(1,128)}, u32[]{:S(2)}) copy-start(s32[1,160]{1,0:T(1,128)} %sel_ref.2) | copy-start | bytes 1924
  4.6 2.6 %collective-permute-start.1 = (s32[1,2,128]{2,1,0:T(2,128)}, s32[1,2,128]{2,1,0:T(2,128)S(1)}, u32[]{:S(2)}, u32[]{:S(2)}) collective-permute-start(s32[1,2,128]{2,1,0:T(2,128)} %get-tuple-element.56), channel_id=1, source_target_pairs={{0,12},{1,13},{2,14},{3,15},{4,8},{5,9},{6,10},{7,11},{8,4},{9,5},... | collective-permute-start | bytes 3080 | tf_op jit(solution)/shard_map/ppermute | solution.py:407
  10.3 12.6 %all-to-all-start = ((s32[16,2,128]{2,1,0:T(2,128)}), s32[16,2,128]{2,1,0:T(2,128)S(1)}, u32[]{:S(2)}, u32[]{:S(2)}) async-start(s32[16,2,128]{2,1,0:T(2,128)} %get-tuple-element.60), calls=%async_computation | async-start | bytes 32768 | tf_op jit(solution)/shard_map/all_to_all | solution.py:410
  18.0 46.0 %collective-permute-start.2 = (bf16[8,16,1024]{2,1,0:T(8,128)(2,1)}, bf16[8,16,1024]{2,1,0:T(8,128)(2,1)S(1)}, u32[]{:S(2)}, u32[]{:S(2)}) collective-permute-start(bf16[8,16,1024]{2,1,0:T(8,128)(2,1)} %get-tuple-element.82), channel_id=1, source_target_pairs={{0,8},{1,9},{2,10},{3,11},{4,12},{5,13},{6,14},{7,15},{8,0},{9,1},... | collective-permute-start | bytes 786440 | tf_op jit(solution)/shard_map/ppermute | solution.py:407
  20.1 44.2 %collective-permute-start.3 = (bf16[8,16,1024]{2,1,0:T(8,128)(2,1)}, bf16[8,16,1024]{2,1,0:T(8,128)(2,1)S(1)}, u32[]{:S(2)}, u32[]{:S(2)}) collective-permute-start(bf16[8,16,1024]{2,1,0:T(8,128)(2,1)} %get-tuple-element.83), channel_id=1, source_target_pairs={{0,12},{1,13},{2,14},{3,15},{4,8},{5,9},{6,10},{7,11},{8,4},{9,5},... | collective-permute-start | bytes 786440 | tf_op jit(solution)/shard_map/ppermute | solution.py:407
  32.8 22.4 %all-to-all-start.1 = ((bf16[16,16,1024]{2,1,0:T(8,128)(2,1)}), bf16[16,16,1024]{2,1,0:T(8,128)(2,1)S(1)}, u32[]{:S(2)}, u32[]{:S(2)}) async-start(bf16[16,16,1024]{2,1,0:T(8,128)(2,1)} %shard_map.71), calls=%async_computation.1 | async-start | bytes 1048576 | tf_op jit(solution)/shard_map/all_to_all | solution.py:410
  39.1 29.9 %collective-permute-start.4 = (bf16[8,16,1024]{2,1,0:T(8,128)(2,1)}, bf16[8,16,1024]{2,1,0:T(8,128)(2,1)S(1)}, u32[]{:S(2)}, u32[]{:S(2)}) collective-permute-start(bf16[8,16,1024]{2,1,0:T(8,128)(2,1)} %get-tuple-element.84), channel_id=1, source_target_pairs={{0,4},{1,5},{2,6},{3,7},{4,0},{5,1},{6,2},{7,3},{8,12},{9,13},{10,... | collective-permute-start | bytes 786440 | tf_op jit(solution)/shard_map/ppermute | solution.py:407
  39.2 29.9 %collective-permute-start.5 = (bf16[8,16,1024]{2,1,0:T(8,128)(2,1)}, bf16[8,16,1024]{2,1,0:T(8,128)(2,1)S(1)}, u32[]{:S(2)}, u32[]{:S(2)}) collective-permute-start(bf16[8,16,1024]{2,1,0:T(8,128)(2,1)} %get-tuple-element.85), channel_id=1, source_target_pairs={{0,5},{1,4},{2,7},{3,6},{4,1},{5,0},{6,3},{7,2},{8,13},{9,12},{10,... | collective-permute-start | bytes 786440 | tf_op jit(solution)/shard_map/ppermute | solution.py:407
  41.1 28.6 %collective-permute-start.6 = (bf16[8,16,1024]{2,1,0:T(8,128)(2,1)}, bf16[8,16,1024]{2,1,0:T(8,128)(2,1)}, u32[]{:S(2)}, u32[]{:S(2)}) collective-permute-start(bf16[8,16,1024]{2,1,0:T(8,128)(2,1)} %get-tuple-element.86), channel_id=1, source_target_pairs={{0,1},{1,0},{2,3},{3,2},{4,5},{5,4},{6,7},{7,6},{8,9},{9,8},{10,11... | collective-permute-start | bytes 786440 | tf_op jit(solution)/shard_map/ppermute | solution.py:407
  44.4 24.8 %copy-start.14 = (bf16[8,16,1024]{2,1,0:T(8,128)(2,1)S(1)}, bf16[8,16,1024]{2,1,0:T(8,128)(2,1)}, u32[]{:S(2)}) copy-start(bf16[8,16,1024]{2,1,0:T(8,128)(2,1)} %get-tuple-element.95) | copy-start | bytes 786436
  44.4 25.3 %copy-start.13 = (bf16[8,16,1024]{2,1,0:T(8,128)(2,1)S(1)}, bf16[8,16,1024]{2,1,0:T(8,128)(2,1)}, u32[]{:S(2)}) copy-start(bf16[8,16,1024]{2,1,0:T(8,128)(2,1)} %get-tuple-element.96) | copy-start | bytes 786436
  64.0 28.1 %collective-permute-start.10 = (bf16[8,16,1024]{2,1,0:T(8,128)(2,1)S(1)}, bf16[8,16,1024]{2,1,0:T(8,128)(2,1)S(1)}, u32[]{:S(2)}, u32[]{:S(2)}) collective-permute-start(bf16[8,16,1024]{2,1,0:T(8,128)(2,1)S(1)} %copy-done.19), channel_id=1, source_target_pairs={{0,7},{1,6},{2,5},{3,4},{4,3},{5,2},{6,1},{7,0},{8,15},{9,14},{10,... | collective-permute-start | bytes 786440 | tf_op jit(solution)/shard_map/ppermute | solution.py:407
  64.3 30.4 %collective-permute-start.11 = (bf16[8,16,1024]{2,1,0:T(8,128)(2,1)S(1)}, bf16[8,16,1024]{2,1,0:T(8,128)(2,1)S(1)}, u32[]{:S(2)}, u32[]{:S(2)}) collective-permute-start(bf16[8,16,1024]{2,1,0:T(8,128)(2,1)S(1)} %copy-done.16), channel_id=1, source_target_pairs={{0,10},{1,11},{2,8},{3,9},{4,14},{5,15},{6,12},{7,13},{8,2},{9,3},... | collective-permute-start | bytes 786440 | tf_op jit(solution)/shard_map/ppermute | solution.py:407
  69.0 26.0 %collective-permute-start.12 = (bf16[8,16,1024]{2,1,0:T(8,128)(2,1)S(1)}, bf16[8,16,1024]{2,1,0:T(8,128)(2,1)S(1)}, u32[]{:S(2)}, u32[]{:S(2)}) collective-permute-start(bf16[8,16,1024]{2,1,0:T(8,128)(2,1)S(1)} %copy-done.15), channel_id=1, source_target_pairs={{0,2},{1,3},{2,0},{3,1},{4,6},{5,7},{6,4},{7,5},{8,10},{9,11},{10,... | collective-permute-start | bytes 786440 | tf_op jit(solution)/shard_map/ppermute | solution.py:407
  69.1 27.4 %collective-permute-start.7 = (bf16[8,16,1024]{2,1,0:T(8,128)(2,1)S(1)}, bf16[8,16,1024]{2,1,0:T(8,128)(2,1)}, u32[]{:S(2)}, u32[]{:S(2)}) collective-permute-start(bf16[8,16,1024]{2,1,0:T(8,128)(2,1)S(1)} %copy-done.14), channel_id=1, source_target_pairs={{0,9},{1,8},{2,11},{3,10},{4,13},{5,12},{6,15},{7,14},{8,1},{9,0},... | collective-permute-start | bytes 786440 | tf_op jit(solution)/shard_map/ppermute | solution.py:407
  69.7 31.0 %collective-permute-start.8 = (bf16[8,16,1024]{2,1,0:T(8,128)(2,1)S(1)}, bf16[8,16,1024]{2,1,0:T(8,128)(2,1)}, u32[]{:S(2)}, u32[]{:S(2)}) collective-permute-start(bf16[8,16,1024]{2,1,0:T(8,128)(2,1)S(1)} %copy-done.13), channel_id=1, source_target_pairs={{0,6},{1,7},{2,4},{3,5},{4,2},{5,3},{6,0},{7,1},{8,14},{9,15},{10,... | collective-permute-start | bytes 786440 | tf_op jit(solution)/shard_map/ppermute | solution.py:407
  72.0 28.7 %copy-start.8 = (bf16[8,16,1024]{2,1,0:T(8,128)(2,1)S(1)}, bf16[8,16,1024]{2,1,0:T(8,128)(2,1)}, u32[]{:S(2)}) copy-start(bf16[8,16,1024]{2,1,0:T(8,128)(2,1)} %get-tuple-element.106) | copy-start | bytes 786436
  92.1 38.6 %copy-start.20 = (bf16[8,16,1024]{2,1,0:T(8,128)(2,1)}, bf16[8,16,1024]{2,1,0:T(8,128)(2,1)S(1)}, u32[]{:S(2)}) copy-start(bf16[8,16,1024]{2,1,0:T(8,128)(2,1)S(1)} %collective-permute-done.10.rest_8_) | copy-start | bytes 786436
  92.1 32.2 %collective-permute-start.9 = (bf16[8,16,1024]{2,1,0:T(8,128)(2,1)S(1)}, bf16[8,16,1024]{2,1,0:T(8,128)(2,1)S(1)}, u32[]{:S(2)}, u32[]{:S(2)}) collective-permute-start(bf16[8,16,1024]{2,1,0:T(8,128)(2,1)S(1)} %copy-done.12), channel_id=1, source_target_pairs={{0,13},{1,12},{2,15},{3,14},{4,9},{5,8},{6,11},{7,10},{8,5},{9,4},... | collective-permute-start | bytes 786440 | tf_op jit(solution)/shard_map/ppermute | solution.py:407
  94.7 34.9 %collective-permute-start.13 = (bf16[8,16,1024]{2,1,0:T(8,128)(2,1)S(1)}, bf16[8,16,1024]{2,1,0:T(8,128)(2,1)S(1)}, u32[]{:S(2)}, u32[]{:S(2)}) collective-permute-start(bf16[8,16,1024]{2,1,0:T(8,128)(2,1)S(1)} %copy-done.11), channel_id=1, source_target_pairs={{0,14},{1,15},{2,12},{3,13},{4,10},{5,11},{6,8},{7,9},{8,6},{9,7},... | collective-permute-start | bytes 786440 | tf_op jit(solution)/shard_map/ppermute | solution.py:407
  95.1 34.6 %collective-permute-start.14 = (bf16[8,16,1024]{2,1,0:T(8,128)(2,1)S(1)}, bf16[8,16,1024]{2,1,0:T(8,128)(2,1)S(1)}, u32[]{:S(2)}, u32[]{:S(2)}) collective-permute-start(bf16[8,16,1024]{2,1,0:T(8,128)(2,1)S(1)} %copy-done.10), channel_id=1, source_target_pairs={{0,3},{1,2},{2,1},{3,0},{4,7},{5,6},{6,5},{7,4},{8,11},{9,10},{10,... | collective-permute-start | bytes 786440 | tf_op jit(solution)/shard_map/ppermute | solution.py:407
  96.6 52.9 %collective-permute-start.15 = (bf16[8,16,1024]{2,1,0:T(8,128)(2,1)S(1)}, bf16[8,16,1024]{2,1,0:T(8,128)(2,1)S(1)}, u32[]{:S(2)}, u32[]{:S(2)}) collective-permute-start(bf16[8,16,1024]{2,1,0:T(8,128)(2,1)S(1)} %copy-done.9), channel_id=1, source_target_pairs={{0,11},{1,10},{2,9},{3,8},{4,15},{5,14},{6,13},{7,12},{8,3},{9,2},... | collective-permute-start | bytes 786440 | tf_op jit(solution)/shard_map/ppermute | solution.py:407
  100.7 48.7 %collective-permute-start.16 = (bf16[8,16,1024]{2,1,0:T(8,128)(2,1)S(1)}, bf16[8,16,1024]{2,1,0:T(8,128)(2,1)S(1)}, u32[]{:S(2)}, u32[]{:S(2)}) collective-permute-start(bf16[8,16,1024]{2,1,0:T(8,128)(2,1)S(1)} %copy-done.8), channel_id=1, source_target_pairs={{0,15},{1,14},{2,13},{3,12},{4,11},{5,10},{6,9},{7,8},{8,7},{9,6},... | collective-permute-start | bytes 786440 | tf_op jit(solution)/shard_map/ppermute | solution.py:407
  (23 other events, 221.0 us)

commit v15 on v14

--- a/solution.py
+++ b/solution.py
@@ -15,9 +15,7 @@
 ROW_SLOTS = 16
 VMEM_LIMIT = 60 * 1024 * 1024
 QUERY_BLOCK = 32
-TILE_PAGES = 32
-LATE_TILE_PAGES = 16
-FRESH_PAGES = 16
+TILE_PAGES = 16
 HIDDEN = -1e30
 FAR_POSITION = 1 << 24
 
@@ -159,7 +157,7 @@
     pltpu.make_async_copy(store_out, store_out, out_sem).wait()
 
 
-def attend_kernel(first, last, tile_pages, sources, place, tiles, *rest):
+def attend_kernel(first, last, sources, place, tiles, *rest):
     sel_ref, position, query_ref, *rest = rest
     if first:
         fresh_ref, *rest = rest
@@ -170,10 +168,9 @@
     kv, values, query, scores, raised, mixed, stats, sem = rest
     pages, page_len, width = kv.shape
     each = contexts[0].shape[0]
-    ahead = FRESH_PAGES if first else 0
     direct = last and not first
     block = query_ref.shape[0]
-    tile = tile_pages * page_len
+    tile = TILE_PAGES * page_len
     lanes = QUERY_GROUP * block
     scale = 1.4426950408889634 / HEAD_WIDTH**0.5
     f32 = jnp.float32
@@ -191,25 +188,29 @@
                 kv[i * each : (i + 1) * each] = context[...]
             else:
                 for k in range(each):
-                    to = kv.at[ahead + place[i * each + k]]
+                    to = kv.at[place[i * each + k]]
                     pltpu.make_async_copy(context.at[k], to, sem).start()
         if first:
             count = fresh_ref.shape[0] // page_len
-            kv[0:count] = fresh_ref[...].reshape(count, page_len, width)
-            kv[count:ahead] = jnp.zeros((ahead - count, page_len, width), bf16)
+            for p in range(count):
+                page = fresh_ref[p * page_len : (p + 1) * page_len, :]
+                kv[place[sources * each + p]] = page
+            used = sources * each + count
+            if pages > used:
+                kv[used:] = jnp.zeros((pages - used, page_len, width), bf16)
         if not direct:
-            used = kv.at[ahead:]
-            pltpu.make_async_copy(used, used, sem).wait()
+            arrived = kv.at[0 : sources * each]
+            pltpu.make_async_copy(arrived, arrived, sem).wait()
 
         def turn(t, carry):
-            here = pl.ds(t * tile_pages, tile_pages)
+            here = pl.ds(t * TILE_PAGES, TILE_PAGES)
             for g in range(KEY_VALUE_HEADS):
                 at = (KEY_VALUE_HEADS + g) * LANES
                 value = kv[here, :, at : at + LANES].reshape(tile, LANES)
                 values[t, g] = nt_dot(eye, value).astype(bf16)
             return carry
 
-        lax.fori_loop(0, pages // tile_pages, turn, 0)
+        lax.fori_loop(0, pages // TILE_PAGES, turn, 0)
 
     for g in range(KEY_VALUE_HEADS):
         for i in range(QUERY_GROUP):
@@ -226,7 +227,7 @@
     sel = sel_ref[0]
 
     def one_tile(t, carry):
-        here = pl.ds(t * tile_pages, tile_pages)
+        here = pl.ds(t * TILE_PAGES, TILE_PAGES)
         bias = jnp.where(
             position[pl.ds(pl.multiple_of(t * tile, tile), tile), :] <= sel, 0.0, HIDDEN
         ).astype(f32)
@@ -279,11 +280,11 @@
         outs[1][0] = stats[...]
 
 
-def attend(first, last, tile_pages, order, sel_lanes, queries, fresh, state, contexts):
+def attend(first, last, order, sel_lanes, queries, fresh, state, contexts):
     place, tiles, position = order
     picked, features = queries.shape
     each, page_len, width = contexts[0].shape
-    pages = each * len(contexts) + (FRESH_PAGES if first else 0)
+    pages = position.shape[0] // page_len
     steps = picked // QUERY_BLOCK
     lanes = QUERY_GROUP * QUERY_BLOCK
     wide = pl.BlockSpec((QUERY_BLOCK, features), lambda b, *_: (b, 0))
@@ -297,7 +298,7 @@
     ]
     share = 0.6
     return pl.pallas_call(
-        functools.partial(attend_kernel, first, last, tile_pages, len(contexts)),
+        functools.partial(attend_kernel, first, last, len(contexts)),
         grid_spec=pltpu.PrefetchScalarGridSpec(
             num_scalar_prefetch=2,
             grid=(steps,),
@@ -317,11 +318,11 @@
             scratch_shapes=[
                 pltpu.VMEM((pages, page_len, width), jnp.bfloat16),
                 pltpu.VMEM(
-                    (pages // tile_pages, KEY_VALUE_HEADS, LANES, tile_pages * page_len), jnp.bfloat16
+                    (pages // TILE_PAGES, KEY_VALUE_HEADS, LANES, TILE_PAGES * page_len), jnp.bfloat16
                 ),
                 pltpu.VMEM((KEY_VALUE_HEADS, lanes, LANES), jnp.bfloat16),
-                pltpu.VMEM((KEY_VALUE_HEADS, tile_pages * page_len, lanes), jnp.float32),
-                pltpu.VMEM((KEY_VALUE_HEADS, tile_pages * page_len, lanes), jnp.bfloat16),
+                pltpu.VMEM((KEY_VALUE_HEADS, TILE_PAGES * page_len, lanes), jnp.float32),
+                pltpu.VMEM((KEY_VALUE_HEADS, TILE_PAGES * page_len, lanes), jnp.bfloat16),
                 pltpu.VMEM((KEY_VALUE_HEADS, LANES, lanes), jnp.float32),
                 pltpu.VMEM((2 * KEY_VALUE_HEADS, lanes), jnp.float32),
                 pltpu.SemaphoreType.DMA,
@@ -339,16 +340,21 @@
     )(place, tiles, sel_lanes, position, queries, *([fresh] if first else state), *contexts)
 
 
-def page_order(slots, positions, own, hold, capacity, groups, tiles, page_len):
+def page_order(slots, positions, own, hold, capacity, groups, page_len):
     pages = slots.shape[0]
     number = jnp.arange(pages)
     before = number[None, :] < number[:, None]
     owners = slots // hold
     ranks = jnp.sum(((owners[None, :] == owners[:, None]) & before).astype(jnp.int32), axis=1)
     distance = owners ^ own
-    last_page = positions.reshape(-1, QUERY_BLOCK)[:, -1] // page_len
+    last_position = positions.reshape(-1, QUERY_BLOCK)[:, -1:]
+    starts = number * page_len
+    replaced = jnp.any(
+        (starts[:, None] + jnp.arange(page_len)[None, :])[:, :, None] == positions, axis=2
+    )
+    fresh = positions.reshape(-1, page_len)
     orders = []
-    for at, (group, tile_pages) in enumerate(zip(groups, tiles)):
+    for at, group in enumerate(groups):
         if group is None:
             arrival = owners * capacity + ranks
             count = pages
@@ -359,24 +365,33 @@
             count = len(group) * capacity
         member = arrival >= 0
         place = jnp.sum((member[None, :] & before).astype(jnp.int32), axis=1)
-        if at == len(groups) - 1 and at > 0:
+        seen = jnp.sum((member & (starts <= last_position)).astype(jnp.int32), axis=1)
+        total = count
+        if at == 0:
+            place = place + jnp.sum((fresh[None, :, 0] < starts[:, None]).astype(jnp.int32), axis=1)
+            ahead = jnp.sum((member & (starts <= fresh[:, 0:1])).astype(jnp.int32), axis=1)
+            fresh_place = jnp.arange(fresh.shape[0]) + ahead
+            seen = seen + jnp.sum((fresh[None, :, 0] <= last_position).astype(jnp.int32), axis=1)
+            total = count + fresh.shape[0]
+        elif at == len(groups) - 1:
             place = arrival
-        index = jnp.arange(count)[:, None]
-        places = jnp.sum(jnp.where(arrival[None, :] == index, place[None, :], 0), axis=1)
-        page = jnp.sum(
-            jnp.where(member[None, :] & (place[None, :] == index), number[None, :], 0), axis=1
-        )
-        seen = jnp.sum((page[None, :] <= last_page[:, None]).astype(jnp.int32), axis=1)
-        seen = seen + (FRESH_PAGES if at == 0 else 0)
-        rows = (page[:, None] * page_len + jnp.arange(page_len)[None, :]).reshape(-1, 1)
-        replaced = jnp.any(rows == positions[None, :], axis=1, keepdims=True)
+        places = jnp.where(arrival == jnp.arange(count)[:, None], place, 0)
+        places = jnp.sum(places, axis=1)
+        index = jnp.arange(-(-total // TILE_PAGES) * TILE_PAGES)[:, None]
+        here = member & (place == index)
+        inside = jnp.arange(page_len)
+        rows = starts[:, None] + inside
         rows = jnp.where(replaced, FAR_POSITION, rows)
+        rows = jnp.sum(jnp.where(here[:, :, None], rows, 0), axis=1)
+        filled = jnp.any(here, axis=1, keepdims=True)
         if at == 0:
-            room = FRESH_PAGES * page_len - positions.shape[0]
-            room = jnp.full((room, 1), FAR_POSITION, jnp.int32)
-            rows = jnp.concatenate([positions[:, None], room, rows])
+            there = fresh_place == index
+            rows = rows + jnp.sum(jnp.where(there[:, :, None], fresh, 0), axis=1)
+            filled = filled | jnp.any(there, axis=1, keepdims=True)
+            places = jnp.concatenate([places, fresh_place])
+        rows = jnp.where(filled, rows, FAR_POSITION).reshape(-1, 1)
         rows = jnp.broadcast_to(rows, (rows.shape[0], LANES))
-        orders.append((places, (seen + tile_pages - 1) // tile_pages, rows))
+        orders.append((places, (seen + TILE_PAGES - 1) // TILE_PAGES, rows))
     return orders
 
 
@@ -396,7 +411,7 @@
     wide = pltpu.VMEM((8, -(-picked // LANES) * LANES), jnp.int32)
     if holders == 16:
         first = (8, 12)
-        groups = [(0, 8, 12, 4, 5, 1), (9, 6, 13, 7, 10, 2, 14, 3), (11, 15)]
+        groups = [(0, 8, 12, 4), (5, 1, 9, 6, 13, 7, 10, 2, 14, 3), (11, 15)]
         others = [d for group in groups for d in group if d not in first]
     else:
         first = ()
@@ -475,8 +490,7 @@
     parts, packed, table, positions = lax.optimization_barrier((parts, packed, table, positions))
     if others:
         parts = dict(zip(others, parts))
-        held = others[-4:]
-        for d in others[:-4]:
+        for d in others:
             arrived[d] = swap(parts[d], d) if d else parts[d]
     else:
         arrived[None] = exchange(parts[0]).reshape(pages, page_len, width)
@@ -503,8 +517,7 @@
         cost_estimate=pl.CostEstimate(flops=0, bytes_accessed=4 * store.size, transcendentals=0),
     )(index_in, index_in, store, rows_in)
 
-    tiles = [LATE_TILE_PAGES if at == len(groups) - 1 else TILE_PAGES for at in range(len(groups))]
-    orders = page_order(table[0], positions[0], own, hold, capacity, groups, tiles, page_len)
+    orders = page_order(table[0], positions[0], own, hold, capacity, groups, page_len)
     sel_lanes = jnp.tile(positions.reshape(-1, 1, QUERY_BLOCK), (1, 1, LANES // QUERY_BLOCK))
     store_out, sel_lanes = lax.optimization_barrier((store_out, sel_lanes))
     state = ()
@@ -512,7 +525,6 @@
         state = attend(
             at == 0,
             at == len(groups) - 1,
-            tiles[at],
             order,
             sel_lanes,
             queries[0],
@@ -520,10 +532,6 @@
             state,
             [arrived[d] for d in group or [None]],
         )
-        if at == 0 and others:
-            state, late = lax.optimization_barrier((state, [parts[d] for d in held]))
-            for d, part in zip(held, late):
-                arrived[d] = swap(part, d)
     return (state[0][None], store_out)
 
 

time: 162 us -> 144 us (0.89)
  waiting for transfers between devices: 42.6 us -> 14.4 us
  starting transfers between devices: 35.9 us -> 45 us
  other arithmetic: 5.85 us -> 9.32 us
  Pallas kernels: 68.1 us -> 66.2 us
    ppermute x17, waiting for transfers between devices: 31.4 us -> 13.9 us  [swap(): return lax.ppermute(x, 'store', [(h, h ^ d) for h in range(holders)])]
    all_to_all x2, waiting for transfers between devices: 11.2 us -> 0.49 us  [exchange(): return lax.all_to_all(x, 'store', split_axis=0, concat_axis=0, tiled=True)]
    ppermute x17, starting transfers between devices: 22 us -> 31.1 us  [swap(): return lax.ppermute(x, 'store', [(h, h ^ d) for h in range(holders)])]
    reduce_sum x6 -> x11, other arithmetic: 2.54 us -> 4.89 us  [the longest x3 2.67 us: page_order(): rows = jnp.sum(jnp.where(here[:, :, None], rows, 0), axis=1)]
    pallas_call x3, Pallas kernels: 48.6 us -> 46.8 us  [attend(): pl.pallas_call(functools.partial(attend_kernel, first, last, len(contexts...]
  transfers between devices with their start and end apart: 19 -> 19, of which waited for: 6 -> 6; matrix products, arithmetic and copies ran while one was open for 6% -> 9% of each run, Pallas kernels for 34% -> 37%
where the time goes in v15:
time: 144 us; the launch traced here: 143 us
  Pallas kernels  66.2 us (46%)
  starting transfers between devices  45 us (31%)
  waiting for transfers between devices  14.4 us (10%)
  other arithmetic  9.32 us (6%)
  local copies, waits for them, and re-layouts  6.85 us (5%)
    pallas_call x3, Pallas kernels, attend(): pl.pallas_call(functools.partial(attend_kernel, first, last, len(contexts...  46.8 us
    ppermute x17, starting transfers between devices, swap(): return lax.ppermute(x, 'store', [(h, h ^ d) for h in range(holders)])  31.1 us
    all_to_all x2, starting transfers between devices, exchange(): return lax.all_to_all(x, 'store', split_axis=0, concat_axis=0, tiled=True)  13.9 us
    ppermute x17, waiting for transfers between devices, swap(): return lax.ppermute(x, 'store', [(h, h ^ d) for h in range(holders)])  13.9 us
    pallas_call x1, Pallas kernels, per_device(): pl.pallas_call(write_back_kernel, grid_spec=pltpu.PrefetchScalarGridSpec(...  8.02 us
    pallas_call x1, Pallas kernels, per_device(): pl.pallas_call(functools.partial(gather_kernel, capacity, others), grid_s...  4.9 us
  transfers between devices with their start and end apart: 19, of which 6 were waited for; matrix products, arithmetic and copies ran while one was open for 9% of the time, Pallas kernels for 37%

profile of v15, /device:TPU:9, one launch (start us, length us, event | category | flops | bytes accessed | tf_op | source)
XLA Modules:
  0.0 142.7 jit_solution(6966891885248788386)
XLA Ops:
  0.6 1.7 %shard_map.68 = (s32[16,2,128]{2,1,0:T(2,128)}, s32[1,2,128]{2,1,0:T(2,128)}, s32[1,2,128]{2,1,0:T(2,128)}) custom-call(s32[1]{0:T(128)} %bitcast.own, s32[1,128]{1,0:T(1,128)} %table_ref.2, s32[1,160]{1,0:T(1,128)} %sel_ref.2), custom_call_target="tpu_custom_call" | custom-call | tf_op jit(solution)/shard_map/pallas_call | solution.py:427
  2.3 2.3 %collective-permute-start = (s32[1,2,128]{2,1,0:T(2,128)}, s32[1,2,128]{2,1,0:T(2,128)S(1)}, u32[]{:S(2)}, u32[]{:S(2)}) collective-permute-start(s32[1,2,128]{2,1,0:T(2,128)} %get-tuple-element.49), channel_id=1, source_target_pairs={{0,8},{1,9},{2,10},{3,11},{4,12},{5,13},{6,14},{7,15},{8,0},{9,1},... | collective-permute-start | bytes 3080 | tf_op jit(solution)/shard_map/ppermute | solution.py:422
  5.8 1.4 collective-permute-done.1.refs_1_
  7.8 2.5 %shard_map.69 = (bf16[8,16,1024]{2,1,0:T(8,128)(2,1)}, bf16[8,16,1024]{2,1,0:T(8,128)(2,1)}) custom-call(s32[1,2,128]{2,1,0:T(2,128)} %copy-done.6, s32[1,2,128]{2,1,0:T(2,128)} %copy-done.7, bf16[128,16,1024]{2,1,0:T(8,128)(2,1)} %store_hbm.3), custom_call_target="tpu_custom_call" | custom-call | tf_op jit(solution)/shard_map/pallas_call | solution.py:445
  10.4 7.5 %all-to-all-start = ((s32[16,2,128]{2,1,0:T(2,128)}), s32[16,2,128]{2,1,0:T(2,128)S(1)}, u32[]{:S(2)}, u32[]{:S(2)}) async-start(s32[16,2,128]{2,1,0:T(2,128)} %get-tuple-element.54), calls=%async_computation | async-start | bytes 32768 | tf_op jit(solution)/shard_map/all_to_all | solution.py:425
  17.9 2.2 %collective-permute-start.2 = (bf16[8,16,1024]{2,1,0:T(8,128)(2,1)}, bf16[8,16,1024]{2,1,0:T(8,128)(2,1)S(1)}, u32[]{:S(2)}, u32[]{:S(2)}) collective-permute-start(bf16[8,16,1024]{2,1,0:T(8,128)(2,1)} %get-tuple-element.76), channel_id=1, source_target_pairs={{0,8},{1,9},{2,10},{3,11},{4,12},{5,13},{6,14},{7,15},{8,0},{9,1},... | collective-permute-start | bytes 786440 | tf_op jit(solution)/shard_map/ppermute | solution.py:422
  20.1 2.4 %shard_map.71 = bf16[16,16,1024]{2,1,0:T(8,128)(2,1)} custom-call(s32[1,128]{1,0:T(1,128)} %table_ref.2, s32[1,160]{1,0:T(1,128)} %sel_ref.2, bf16[160,1024]{1,0:T(8,128)(2,1)} %bitcast.76), custom_call_target="tpu_custom_call" | custom-call | tf_op jit(solution)/shard_map/pallas_call | solution.py:469
  23.5 4.9 %shard_map.70 = (bf16[8,16,1024]{2,1,0:T(8,128)(2,1)}, bf16[8,16,1024]{2,1,0:T(8,128)(2,1)}, bf16[8,16,1024]{2,1,0:T(8,128)(2,1)}, bf16[8,16,1024]{2,1,0:T(8,128...) custom-call(s32[1]{0:T(128)} %bitcast.own, ...), custom_call_target="tpu_custom_call" | custom-call | tf_op jit(solution)/shard_map/pallas_call | solution.py:478
  32.0 6.4 %all-to-all-start.1 = ((bf16[16,16,1024]{2,1,0:T(8,128)(2,1)}), bf16[16,16,1024]{2,1,0:T(8,128)(2,1)S(1)}, u32[]{:S(2)}, u32[]{:S(2)}) async-start(bf16[16,16,1024]{2,1,0:T(8,128)(2,1)} %shard_map.71), calls=%async_computation.1 | async-start | bytes 1048576 | tf_op jit(solution)/shard_map/all_to_all | solution.py:425
  41.6 2.8 %collective-permute-start.10 = (bf16[8,16,1024]{2,1,0:T(8,128)(2,1)}, bf16[8,16,1024]{2,1,0:T(8,128)(2,1)S(1)}, u32[]{:S(2)}, u32[]{:S(2)}) collective-permute-start(bf16[8,16,1024]{2,1,0:T(8,128)(2,1)} %get-tuple-element.86), channel_id=1, source_target_pairs={{0,7},{1,6},{2,5},{3,4},{4,3},{5,2},{6,1},{7,0},{8,15},{9,14},{10,... | collective-permute-start | bytes 786440 | tf_op jit(solution)/shard_map/ppermute | solution.py:422
  44.4 2.1 %collective-permute-start.11 = (bf16[8,16,1024]{2,1,0:T(8,128)(2,1)}, bf16[8,16,1024]{2,1,0:T(8,128)(2,1)S(1)}, u32[]{:S(2)}, u32[]{:S(2)}) collective-permute-start(bf16[8,16,1024]{2,1,0:T(8,128)(2,1)} %get-tuple-element.87), channel_id=1, source_target_pairs={{0,10},{1,11},{2,8},{3,9},{4,14},{5,15},{6,12},{7,13},{8,2},{9,3},... | collective-permute-start | bytes 786440 | tf_op jit(solution)/shard_map/ppermute | solution.py:422
  50.4 1.5 %collective-permute-start.13 = (bf16[8,16,1024]{2,1,0:T(8,128)(2,1)}, bf16[8,16,1024]{2,1,0:T(8,128)(2,1)}, u32[]{:S(2)}, u32[]{:S(2)}) collective-permute-start(bf16[8,16,1024]{2,1,0:T(8,128)(2,1)} %get-tuple-element.89), channel_id=1, source_target_pairs={{0,14},{1,15},{2,12},{3,13},{4,10},{5,11},{6,8},{7,9},{8,6},{9,7},... | collective-permute-start | bytes 786440 | tf_op jit(solution)/shard_map/ppermute | solution.py:422
  51.9 2.0 %collective-permute-done.4.rest_7_ = bf16[8,16,1024]{2,1,0:T(8,128)(2,1)S(1)} collective-permute-done((bf16[8,16,1024]{2,1,0:T(8,128)(2,1)}, bf16[8,16,1024]{2,1,0:T(8,128)(2,1)S(1)}, u32[]{:S(2)}, u32[]{:S(2)}) %collective-permute-start.4) | collective-permute-done | bytes 262176 | tf_op jit(solution)/shard_map/ppermute | solution.py:422
  53.9 2.3 %collective-permute-start.14 = (bf16[8,16,1024]{2,1,0:T(8,128)(2,1)}, bf16[8,16,1024]{2,1,0:T(8,128)(2,1)}, u32[]{:S(2)}, u32[]{:S(2)}) collective-permute-start(bf16[8,16,1024]{2,1,0:T(8,128)(2,1)} %get-tuple-element.90), channel_id=1, source_target_pairs={{0,3},{1,2},{2,1},{3,0},{4,7},{5,6},{6,5},{7,4},{8,11},{9,10},{10,... | collective-permute-start | bytes 786440 | tf_op jit(solution)/shard_map/ppermute | solution.py:422
  59.1 8.0 %shard_map.72 = bf16[128,16,1024]{2,1,0:T(8,128)(2,1)} custom-call(s32[16,2,128]{2,1,0:T(2,128)} %copy-done.1, s32[16,2,128]{2,1,0:T(2,128)} %copy-done.1, bf16[128,16,1024]{2,1,0:T(8,128)(2,1)} %store_hbm.3, bf16[16,16,1024]{2,1,0:T(8,128)(2,1)} %copy-done), custom_call_target="tpu_custom_call" | custom-call | bytes 8388608 | tf_op jit(solution)/shard_map/pallas_call | solution.py:499
  67.6 3.9 %collective-permute-done.11.rest_11_ = bf16[8,16,1024]{2,1,0:T(8,128)(2,1)S(1)} collective-permute-done((bf16[8,16,1024]{2,1,0:T(8,128)(2,1)}, bf16[8,16,1024]{2,1,0:T(8,128)(2,1)S(1)}, u32[]{:S(2)}, u32[]{:S(2)}) %collective-permute-start.11) | collective-permute-done | bytes 262176 | tf_op jit(solution)/shard_map/ppermute | solution.py:422
  72.1 5.0 %collective-permute-start.7 = (bf16[8,16,1024]{2,1,0:T(8,128)(2,1)S(1)}, bf16[8,16,1024]{2,1,0:T(8,128)(2,1)}, u32[]{:S(2)}, u32[]{:S(2)}) collective-permute-start(bf16[8,16,1024]{2,1,0:T(8,128)(2,1)S(1)} %copy-done.12), channel_id=1, source_target_pairs={{0,9},{1,8},{2,11},{3,10},{4,13},{5,12},{6,15},{7,14},{8,1},{9,0},... | collective-permute-start | bytes 786440 | tf_op jit(solution)/shard_map/ppermute | solution.py:422
  77.1 5.4 %collective-permute-done.13.rest_13_ = bf16[8,16,1024]{2,1,0:T(8,128)(2,1)} collective-permute-done((bf16[8,16,1024]{2,1,0:T(8,128)(2,1)}, bf16[8,16,1024]{2,1,0:T(8,128)(2,1)}, u32[]{:S(2)}, u32[]{:S(2)}) %collective-permute-start.13) | collective-permute-done | bytes 262176 | tf_op jit(solution)/shard_map/ppermute | solution.py:422
  82.5 4.1 %collective-permute-start.9 = (bf16[8,16,1024]{2,1,0:T(8,128)(2,1)S(1)}, bf16[8,16,1024]{2,1,0:T(8,128)(2,1)}, u32[]{:S(2)}, u32[]{:S(2)}) collective-permute-start(bf16[8,16,1024]{2,1,0:T(8,128)(2,1)S(1)} %copy-done.10), channel_id=1, source_target_pairs={{0,13},{1,12},{2,15},{3,14},{4,9},{5,8},{6,11},{7,10},{8,5},{9,4},... | collective-permute-start | bytes 786440 | tf_op jit(solution)/shard_map/ppermute | solution.py:422
  87.5 13.7 %shard_map.73 = (f32[5,4,128,384]{3,2,1,0:T(8,128)}, f32[5,8,384]{2,1,0:T(8,128)}) custom-call(s32[42]{0:T(128)} %pad_add_fusion.place, s32[5]{0:T(128)} %and_select_fusion.tiles, s32[5,1,128]{2,1,0:T(1,128)} %tile.9.rest_0_, s32[768,128]{1,0:T(8,128)} %broadcast_in_dim.223.rest_1_, bf16[160,6144]{1,0:T(8,128)(2,1)} %bitcast.72, bf16[160,1024]{1,0:T(8,128)(2,1)} %bitcast.77, ...), custom_call_target="tpu_custom_call" | custom-call | flops 3623878656 | bytes 7471104 | tf_op jit(solution)/shard_map/pallas_call | solution.py:300
  101.2 3.9 %collective-permute-start.15 = (bf16[8,16,1024]{2,1,0:T(8,128)(2,1)S(1)}, bf16[8,16,1024]{2,1,0:T(8,128)(2,1)S(1)}, u32[]{:S(2)}, u32[]{:S(2)}) collective-permute-start(bf16[8,16,1024]{2,1,0:T(8,128)(2,1)S(1)} %copy-done.9), channel_id=1, source_target_pairs={{0,11},{1,10},{2,9},{3,8},{4,15},{5,14},{6,13},{7,12},{8,3},{9,2},... | collective-permute-start | bytes 786440 | tf_op jit(solution)/shard_map/ppermute | solution.py:422
  105.1 2.6 %collective-permute-start.16 = (bf16[8,16,1024]{2,1,0:T(8,128)(2,1)S(1)}, bf16[8,16,1024]{2,1,0:T(8,128)(2,1)S(1)}, u32[]{:S(2)}, u32[]{:S(2)}) collective-permute-start(bf16[8,16,1024]{2,1,0:T(8,128)(2,1)S(1)} %copy-done.8), channel_id=1, source_target_pairs={{0,15},{1,14},{2,13},{3,12},{4,11},{5,10},{6,9},{7,8},{8,7},{9,6},... | collective-permute-start | bytes 786440 | tf_op jit(solution)/shard_map/ppermute | solution.py:422
  108.8 23.2 %shard_map.74 = (f32[5,4,128,384]{3,2,1,0:T(8,128)}, f32[5,8,384]{2,1,0:T(8,128)}) custom-call(s32[80]{0:T(128)} %select_reduce_fusion.4.place, s32[5]{0:T(128)} %and_select_fusion.1.tiles, s32[5,1,128]{2,1,0:T(1,128)} %tile.9.rest_0_, s32[1280,128]{1,0:T(8,128)} %broadcast_in_dim.212.rest_1_, bf16[160,6144]{1,0:T(8,128)(2,1)} %bitcast.73, ...), custom_call_target="tpu_custom_call" | custom-call | flops 6039797760 | bytes 8519680 | tf_op jit(solution)/shard_map/pallas_call | solution.py:300
  132.9 9.9 %shard_map.75 = bf16[160,6144]{1,0:T(8,128)(2,1)} custom-call(s32[16]{0:T(128)} %select_reduce_fusion.6.place, s32[5]{0:T(128)} %and_select_fusion.2.tiles, s32[5,1,128]{2,1,0:T(1,128)} %tile.9.rest_0_, s32[256,128]{1,0:T(8,128)} %broadcast_in_dim.204.rest_1_, bf16[160,6144]{1,0:T(8,128)(2,1)} %bitcast.74, f32[5,4,128,384]{3,2,1,0:T(8,128)} %get-tuple-element.91.rest_3_, ...), custom_call_target="tpu_custom_call" | custom-call | flops 1207959552 | bytes 6422528 | tf_op jit(solution)/shard_map/pallas_call | solution.py:300
  (116 shorter events, 20.3 us)
Async XLA Ops:
  2.3 3.5 %collective-permute-start = (s32[1,2,128]{2,1,0:T(2,128)}, s32[1,2,128]{2,1,0:T(2,128)S(1)}, u32[]{:S(2)}, u32[]{:S(2)}) collective-permute-start(s32[1,2,128]{2,1,0:T(2,128)} %get-tuple-element.49), channel_id=1, source_target_pairs={{0,8},{1,9},{2,10},{3,11},{4,12},{5,13},{6,14},{7,15},{8,0},{9,1},... | collective-permute-start | bytes 3080 | tf_op jit(solution)/shard_map/ppermute | solution.py:422
  4.6 2.6 %collective-permute-start.1 = (s32[1,2,128]{2,1,0:T(2,128)}, s32[1,2,128]{2,1,0:T(2,128)S(1)}, u32[]{:S(2)}, u32[]{:S(2)}) collective-permute-start(s32[1,2,128]{2,1,0:T(2,128)} %get-tuple-element.50), channel_id=1, source_target_pairs={{0,12},{1,13},{2,14},{3,15},{4,8},{5,9},{6,10},{7,11},{8,4},{9,5},... | collective-permute-start | bytes 3080 | tf_op jit(solution)/shard_map/ppermute | solution.py:422
  10.4 12.6 %all-to-all-start = ((s32[16,2,128]{2,1,0:T(2,128)}), s32[16,2,128]{2,1,0:T(2,128)S(1)}, u32[]{:S(2)}, u32[]{:S(2)}) async-start(s32[16,2,128]{2,1,0:T(2,128)} %get-tuple-element.54), calls=%async_computation | async-start | bytes 32768 | tf_op jit(solution)/shard_map/all_to_all | solution.py:425
  17.9 31.2 %collective-permute-start.2 = (bf16[8,16,1024]{2,1,0:T(8,128)(2,1)}, bf16[8,16,1024]{2,1,0:T(8,128)(2,1)S(1)}, u32[]{:S(2)}, u32[]{:S(2)}) collective-permute-start(bf16[8,16,1024]{2,1,0:T(8,128)(2,1)} %get-tuple-element.76), channel_id=1, source_target_pairs={{0,8},{1,9},{2,10},{3,11},{4,12},{5,13},{6,14},{7,15},{8,0},{9,1},... | collective-permute-start | bytes 786440 | tf_op jit(solution)/shard_map/ppermute | solution.py:422
  20.1 30.3 %collective-permute-start.3 = (bf16[8,16,1024]{2,1,0:T(8,128)(2,1)}, bf16[8,16,1024]{2,1,0:T(8,128)(2,1)S(1)}, u32[]{:S(2)}, u32[]{:S(2)}) collective-permute-start(bf16[8,16,1024]{2,1,0:T(8,128)(2,1)} %get-tuple-element.77), channel_id=1, source_target_pairs={{0,12},{1,13},{2,14},{3,15},{4,8},{5,9},{6,10},{7,11},{8,4},{9,5},... | collective-permute-start | bytes 786440 | tf_op jit(solution)/shard_map/ppermute | solution.py:422
  32.0 26.3 %all-to-all-start.1 = ((bf16[16,16,1024]{2,1,0:T(8,128)(2,1)}), bf16[16,16,1024]{2,1,0:T(8,128)(2,1)S(1)}, u32[]{:S(2)}, u32[]{:S(2)}) async-start(bf16[16,16,1024]{2,1,0:T(8,128)(2,1)} %shard_map.71), calls=%async_computation.1 | async-start | bytes 1048576 | tf_op jit(solution)/shard_map/all_to_all | solution.py:425
  38.4 15.5 %collective-permute-start.4 = (bf16[8,16,1024]{2,1,0:T(8,128)(2,1)}, bf16[8,16,1024]{2,1,0:T(8,128)(2,1)S(1)}, u32[]{:S(2)}, u32[]{:S(2)}) collective-permute-start(bf16[8,16,1024]{2,1,0:T(8,128)(2,1)} %get-tuple-element.78), channel_id=1, source_target_pairs={{0,4},{1,5},{2,6},{3,7},{4,0},{5,1},{6,2},{7,3},{8,12},{9,13},{10,... | collective-permute-start | bytes 786440 | tf_op jit(solution)/shard_map/ppermute | solution.py:422
  41.6 25.5 %collective-permute-start.10 = (bf16[8,16,1024]{2,1,0:T(8,128)(2,1)}, bf16[8,16,1024]{2,1,0:T(8,128)(2,1)S(1)}, u32[]{:S(2)}, u32[]{:S(2)}) collective-permute-start(bf16[8,16,1024]{2,1,0:T(8,128)(2,1)} %get-tuple-element.86), channel_id=1, source_target_pairs={{0,7},{1,6},{2,5},{3,4},{4,3},{5,2},{6,1},{7,0},{8,15},{9,14},{10,... | collective-permute-start | bytes 786440 | tf_op jit(solution)/shard_map/ppermute | solution.py:422
  44.4 27.0 %collective-permute-start.11 = (bf16[8,16,1024]{2,1,0:T(8,128)(2,1)}, bf16[8,16,1024]{2,1,0:T(8,128)(2,1)S(1)}, u32[]{:S(2)}, u32[]{:S(2)}) collective-permute-start(bf16[8,16,1024]{2,1,0:T(8,128)(2,1)} %get-tuple-element.87), channel_id=1, source_target_pairs={{0,10},{1,11},{2,8},{3,9},{4,14},{5,15},{6,12},{7,13},{8,2},{9,3},... | collective-permute-start | bytes 786440 | tf_op jit(solution)/shard_map/ppermute | solution.py:422
  49.1 38.4 %copy-start.13 = (bf16[8,16,1024]{2,1,0:T(8,128)(2,1)}, bf16[8,16,1024]{2,1,0:T(8,128)(2,1)S(1)}, u32[]{:S(2)}) copy-start(bf16[8,16,1024]{2,1,0:T(8,128)(2,1)S(1)} %collective-permute-done.2.rest_5_) | copy-start | bytes 786436
  49.1 23.0 %collective-permute-start.12 = (bf16[8,16,1024]{2,1,0:T(8,128)(2,1)}, bf16[8,16,1024]{2,1,0:T(8,128)(2,1)S(1)}, u32[]{:S(2)}, u32[]{:S(2)}) collective-permute-start(bf16[8,16,1024]{2,1,0:T(8,128)(2,1)} %get-tuple-element.88), channel_id=1, source_target_pairs={{0,2},{1,3},{2,0},{3,1},{4,6},{5,7},{6,4},{7,5},{8,10},{9,11},{10,... | collective-permute-start | bytes 786440 | tf_op jit(solution)/shard_map/ppermute | solution.py:422
  50.4 37.1 %copy-start.14 = (bf16[8,16,1024]{2,1,0:T(8,128)(2,1)}, bf16[8,16,1024]{2,1,0:T(8,128)(2,1)S(1)}, u32[]{:S(2)}) copy-start(bf16[8,16,1024]{2,1,0:T(8,128)(2,1)S(1)} %collective-permute-done.3.rest_6_) | copy-start | bytes 786436
  50.4 32.1 %collective-permute-start.13 = (bf16[8,16,1024]{2,1,0:T(8,128)(2,1)}, bf16[8,16,1024]{2,1,0:T(8,128)(2,1)}, u32[]{:S(2)}, u32[]{:S(2)}) collective-permute-start(bf16[8,16,1024]{2,1,0:T(8,128)(2,1)} %get-tuple-element.89), channel_id=1, source_target_pairs={{0,14},{1,15},{2,12},{3,13},{4,10},{5,11},{6,8},{7,9},{8,6},{9,7},... | collective-permute-start | bytes 786440 | tf_op jit(solution)/shard_map/ppermute | solution.py:422
  53.9 33.6 %copy-start.19 = (bf16[8,16,1024]{2,1,0:T(8,128)(2,1)}, bf16[8,16,1024]{2,1,0:T(8,128)(2,1)S(1)}, u32[]{:S(2)}) copy-start(bf16[8,16,1024]{2,1,0:T(8,128)(2,1)S(1)} %collective-permute-done.4.rest_7_) | copy-start | bytes 786436
  53.9 28.6 %collective-permute-start.14 = (bf16[8,16,1024]{2,1,0:T(8,128)(2,1)}, bf16[8,16,1024]{2,1,0:T(8,128)(2,1)}, u32[]{:S(2)}, u32[]{:S(2)}) collective-permute-start(bf16[8,16,1024]{2,1,0:T(8,128)(2,1)} %get-tuple-element.90), channel_id=1, source_target_pairs={{0,3},{1,2},{2,1},{3,0},{4,7},{5,6},{6,5},{7,4},{8,11},{9,10},{10,... | collective-permute-start | bytes 786440 | tf_op jit(solution)/shard_map/ppermute | solution.py:422
  67.2 34.0 %copy-start.17 = (bf16[8,16,1024]{2,1,0:T(8,128)(2,1)}, bf16[8,16,1024]{2,1,0:T(8,128)(2,1)S(1)}, u32[]{:S(2)}) copy-start(bf16[8,16,1024]{2,1,0:T(8,128)(2,1)S(1)} %collective-permute-done.10.rest_10_) | copy-start | bytes 786436
  67.2 34.1 %collective-permute-start.5 = (bf16[8,16,1024]{2,1,0:T(8,128)(2,1)S(1)}, bf16[8,16,1024]{2,1,0:T(8,128)(2,1)}, u32[]{:S(2)}, u32[]{:S(2)}) collective-permute-start(bf16[8,16,1024]{2,1,0:T(8,128)(2,1)S(1)} %copy-done.16), channel_id=1, source_target_pairs={{0,5},{1,4},{2,7},{3,6},{4,1},{5,0},{6,3},{7,2},{8,13},{9,12},{10,... | collective-permute-start | bytes 786440 | tf_op jit(solution)/shard_map/ppermute | solution.py:422
  71.4 29.8 %copy-start.18 = (bf16[8,16,1024]{2,1,0:T(8,128)(2,1)}, bf16[8,16,1024]{2,1,0:T(8,128)(2,1)S(1)}, u32[]{:S(2)}) copy-start(bf16[8,16,1024]{2,1,0:T(8,128)(2,1)S(1)} %collective-permute-done.11.rest_11_) | copy-start | bytes 786436
  71.4 33.7 %collective-permute-start.6 = (bf16[8,16,1024]{2,1,0:T(8,128)(2,1)S(1)}, bf16[8,16,1024]{2,1,0:T(8,128)(2,1)}, u32[]{:S(2)}, u32[]{:S(2)}) collective-permute-start(bf16[8,16,1024]{2,1,0:T(8,128)(2,1)S(1)} %copy-done.15), channel_id=1, source_target_pairs={{0,1},{1,0},{2,3},{3,2},{4,5},{5,4},{6,7},{7,6},{8,9},{9,8},{10,11... | collective-permute-start | bytes 786440 | tf_op jit(solution)/shard_map/ppermute | solution.py:422
  72.1 35.6 %collective-permute-start.7 = (bf16[8,16,1024]{2,1,0:T(8,128)(2,1)S(1)}, bf16[8,16,1024]{2,1,0:T(8,128)(2,1)}, u32[]{:S(2)}, u32[]{:S(2)}) collective-permute-start(bf16[8,16,1024]{2,1,0:T(8,128)(2,1)S(1)} %copy-done.12), channel_id=1, source_target_pairs={{0,9},{1,8},{2,11},{3,10},{4,13},{5,12},{6,15},{7,14},{8,1},{9,0},... | collective-permute-start | bytes 786440 | tf_op jit(solution)/shard_map/ppermute | solution.py:422
  82.5 25.3 %collective-permute-start.8 = (bf16[8,16,1024]{2,1,0:T(8,128)(2,1)S(1)}, bf16[8,16,1024]{2,1,0:T(8,128)(2,1)}, u32[]{:S(2)}, u32[]{:S(2)}) collective-permute-start(bf16[8,16,1024]{2,1,0:T(8,128)(2,1)S(1)} %copy-done.11), channel_id=1, source_target_pairs={{0,6},{1,7},{2,4},{3,5},{4,2},{5,3},{6,0},{7,1},{8,14},{9,15},{10,... | collective-permute-start | bytes 786440 | tf_op jit(solution)/shard_map/ppermute | solution.py:422
  82.5 25.3 %collective-permute-start.9 = (bf16[8,16,1024]{2,1,0:T(8,128)(2,1)S(1)}, bf16[8,16,1024]{2,1,0:T(8,128)(2,1)}, u32[]{:S(2)}, u32[]{:S(2)}) collective-permute-start(bf16[8,16,1024]{2,1,0:T(8,128)(2,1)S(1)} %copy-done.10), channel_id=1, source_target_pairs={{0,13},{1,12},{2,15},{3,14},{4,9},{5,8},{6,11},{7,10},{8,5},{9,4},... | collective-permute-start | bytes 786440 | tf_op jit(solution)/shard_map/ppermute | solution.py:422
  101.2 30.8 %collective-permute-start.15 = (bf16[8,16,1024]{2,1,0:T(8,128)(2,1)S(1)}, bf16[8,16,1024]{2,1,0:T(8,128)(2,1)S(1)}, u32[]{:S(2)}, u32[]{:S(2)}) collective-permute-start(bf16[8,16,1024]{2,1,0:T(8,128)(2,1)S(1)} %copy-done.9), channel_id=1, source_target_pairs={{0,11},{1,10},{2,9},{3,8},{4,15},{5,14},{6,13},{7,12},{8,3},{9,2},... | collective-permute-start | bytes 786440 | tf_op jit(solution)/shard_map/ppermute | solution.py:422
  105.1 26.9 %collective-permute-start.16 = (bf16[8,16,1024]{2,1,0:T(8,128)(2,1)S(1)}, bf16[8,16,1024]{2,1,0:T(8,128)(2,1)S(1)}, u32[]{:S(2)}, u32[]{:S(2)}) collective-permute-start(bf16[8,16,1024]{2,1,0:T(8,128)(2,1)S(1)} %copy-done.8), channel_id=1, source_target_pairs={{0,15},{1,14},{2,13},{3,12},{4,11},{5,10},{6,9},{7,8},{8,7},{9,6},... | collective-permute-start | bytes 786440 | tf_op jit(solution)/shard_map/ppermute | solution.py:422
  (16 other events, 197.5 us)

commit v16 on v15

--- a/solution.py
+++ b/solution.py
@@ -411,7 +411,7 @@
     wide = pltpu.VMEM((8, -(-picked // LANES) * LANES), jnp.int32)
     if holders == 16:
         first = (8, 12)
-        groups = [(0, 8, 12, 4), (5, 1, 9, 6, 13, 7, 10, 2, 14, 3), (11, 15)]
+        groups = [(0, 8, 12, 4), (7, 10, 2, 14, 3, 5, 1, 9, 6, 13), (11, 15)]
         others = [d for group in groups for d in group if d not in first]
     else:
         first = ()

time: 144 us -> 148 us (1.028)
  waiting for transfers between devices: 14.4 us -> 22.2 us
  starting transfers between devices: 45 us -> 41 us
    ppermute x17, waiting for transfers between devices: 13.9 us -> 21.7 us  [swap(): return lax.ppermute(x, 'store', [(h, h ^ d) for h in range(holders)])]
    ppermute x17, starting transfers between devices: 31.1 us -> 27.1 us  [swap(): return lax.ppermute(x, 'store', [(h, h ^ d) for h in range(holders)])]
  transfers between devices with their start and end apart: 19 -> 19, of which waited for: 6 -> 7; matrix products, arithmetic and copies ran while one was open for 9% -> 9% of each run, Pallas kernels for 37% -> 35%
where the time goes in v16:
time: 148 us; the launch traced here: 146 us
  Pallas kernels  65.4 us (44%)
  starting transfers between devices  41 us (28%)
  waiting for transfers between devices  22.2 us (15%)
  other arithmetic  9.32 us (6%)
  local copies, waits for them, and re-layouts  6.85 us (5%)
    pallas_call x3, Pallas kernels, attend(): pl.pallas_call(functools.partial(attend_kernel, first, last, len(contexts...  45.9 us
    ppermute x17, starting transfers between devices, swap(): return lax.ppermute(x, 'store', [(h, h ^ d) for h in range(holders)])  27.1 us
    ppermute x17, waiting for transfers between devices, swap(): return lax.ppermute(x, 'store', [(h, h ^ d) for h in range(holders)])  21.7 us
    all_to_all x2, starting transfers between devices, exchange(): return lax.all_to_all(x, 'store', split_axis=0, concat_axis=0, tiled=True)  13.9 us
    pallas_call x1, Pallas kernels, per_device(): pl.pallas_call(write_back_kernel, grid_spec=pltpu.PrefetchScalarGridSpec(...  8.02 us
    pallas_call x1, Pallas kernels, per_device(): pl.pallas_call(functools.partial(gather_kernel, capacity, others), grid_s...  4.9 us
  transfers between devices with their start and end apart: 19, of which 7 were waited for; matrix products, arithmetic and copies ran while one was open for 9% of the time, Pallas kernels for 35%

profile of v16, /device:TPU:9, one launch (start us, length us, event | category | flops | bytes accessed | tf_op | source)
XLA Modules:
  0.0 145.8 jit_solution(4650643990459472102)
XLA Ops:
  0.6 1.7 %shard_map.68 = (s32[16,2,128]{2,1,0:T(2,128)}, s32[1,2,128]{2,1,0:T(2,128)}, s32[1,2,128]{2,1,0:T(2,128)}) custom-call(s32[1]{0:T(128)} %bitcast.own, s32[1,128]{1,0:T(1,128)} %table_ref.2, s32[1,160]{1,0:T(1,128)} %sel_ref.2), custom_call_target="tpu_custom_call" | custom-call | tf_op jit(solution)/shard_map/pallas_call | solution.py:427
  2.3 2.3 %collective-permute-start = (s32[1,2,128]{2,1,0:T(2,128)}, s32[1,2,128]{2,1,0:T(2,128)S(1)}, u32[]{:S(2)}, u32[]{:S(2)}) collective-permute-start(s32[1,2,128]{2,1,0:T(2,128)} %get-tuple-element.49), channel_id=1, source_target_pairs={{0,8},{1,9},{2,10},{3,11},{4,12},{5,13},{6,14},{7,15},{8,0},{9,1},... | collective-permute-start | bytes 3080 | tf_op jit(solution)/shard_map/ppermute | solution.py:422
  5.8 1.4 collective-permute-done.1.refs_1_
  7.8 2.5 %shard_map.69 = (bf16[8,16,1024]{2,1,0:T(8,128)(2,1)}, bf16[8,16,1024]{2,1,0:T(8,128)(2,1)}) custom-call(s32[1,2,128]{2,1,0:T(2,128)} %copy-done.6, s32[1,2,128]{2,1,0:T(2,128)} %copy-done.7, bf16[128,16,1024]{2,1,0:T(8,128)(2,1)} %store_hbm.3), custom_call_target="tpu_custom_call" | custom-call | tf_op jit(solution)/shard_map/pallas_call | solution.py:445
  10.4 7.5 %all-to-all-start = ((s32[16,2,128]{2,1,0:T(2,128)}), s32[16,2,128]{2,1,0:T(2,128)S(1)}, u32[]{:S(2)}, u32[]{:S(2)}) async-start(s32[16,2,128]{2,1,0:T(2,128)} %get-tuple-element.54), calls=%async_computation | async-start | bytes 32768 | tf_op jit(solution)/shard_map/all_to_all | solution.py:425
  17.9 2.2 %collective-permute-start.2 = (bf16[8,16,1024]{2,1,0:T(8,128)(2,1)}, bf16[8,16,1024]{2,1,0:T(8,128)(2,1)S(1)}, u32[]{:S(2)}, u32[]{:S(2)}) collective-permute-start(bf16[8,16,1024]{2,1,0:T(8,128)(2,1)} %get-tuple-element.76), channel_id=1, source_target_pairs={{0,8},{1,9},{2,10},{3,11},{4,12},{5,13},{6,14},{7,15},{8,0},{9,1},... | collective-permute-start | bytes 786440 | tf_op jit(solution)/shard_map/ppermute | solution.py:422
  20.1 2.4 %shard_map.71 = bf16[16,16,1024]{2,1,0:T(8,128)(2,1)} custom-call(s32[1,128]{1,0:T(1,128)} %table_ref.2, s32[1,160]{1,0:T(1,128)} %sel_ref.2, bf16[160,1024]{1,0:T(8,128)(2,1)} %bitcast.76), custom_call_target="tpu_custom_call" | custom-call | tf_op jit(solution)/shard_map/pallas_call | solution.py:469
  23.5 4.9 %shard_map.70 = (bf16[8,16,1024]{2,1,0:T(8,128)(2,1)}, bf16[8,16,1024]{2,1,0:T(8,128)(2,1)}, bf16[8,16,1024]{2,1,0:T(8,128)(2,1)}, bf16[8,16,1024]{2,1,0:T(8,128...) custom-call(s32[1]{0:T(128)} %bitcast.own, ...), custom_call_target="tpu_custom_call" | custom-call | tf_op jit(solution)/shard_map/pallas_call | solution.py:478
  32.0 6.4 %all-to-all-start.1 = ((bf16[16,16,1024]{2,1,0:T(8,128)(2,1)}), bf16[16,16,1024]{2,1,0:T(8,128)(2,1)S(1)}, u32[]{:S(2)}, u32[]{:S(2)}) async-start(bf16[16,16,1024]{2,1,0:T(8,128)(2,1)} %shard_map.71), calls=%async_computation.1 | async-start | bytes 1048576 | tf_op jit(solution)/shard_map/all_to_all | solution.py:425
  41.6 1.9 %collective-permute-start.10 = (bf16[8,16,1024]{2,1,0:T(8,128)(2,1)}, bf16[8,16,1024]{2,1,0:T(8,128)(2,1)S(1)}, u32[]{:S(2)}, u32[]{:S(2)}) collective-permute-start(bf16[8,16,1024]{2,1,0:T(8,128)(2,1)} %get-tuple-element.86), channel_id=1, source_target_pairs={{0,5},{1,4},{2,7},{3,6},{4,1},{5,0},{6,3},{7,2},{8,13},{9,12},{10,... | collective-permute-start | bytes 786440 | tf_op jit(solution)/shard_map/ppermute | solution.py:422
  46.1 2.5 %collective-permute-start.12 = (bf16[8,16,1024]{2,1,0:T(8,128)(2,1)}, bf16[8,16,1024]{2,1,0:T(8,128)(2,1)S(1)}, u32[]{:S(2)}, u32[]{:S(2)}) collective-permute-start(bf16[8,16,1024]{2,1,0:T(8,128)(2,1)} %get-tuple-element.88), channel_id=1, source_target_pairs={{0,9},{1,8},{2,11},{3,10},{4,13},{5,12},{6,15},{7,14},{8,1},{9,0},... | collective-permute-start | bytes 786440 | tf_op jit(solution)/shard_map/ppermute | solution.py:422
  49.9 4.0 %collective-permute-done.4.rest_7_ = bf16[8,16,1024]{2,1,0:T(8,128)(2,1)S(1)} collective-permute-done((bf16[8,16,1024]{2,1,0:T(8,128)(2,1)}, bf16[8,16,1024]{2,1,0:T(8,128)(2,1)S(1)}, u32[]{:S(2)}, u32[]{:S(2)}) %collective-permute-start.4) | collective-permute-done | bytes 262176 | tf_op jit(solution)/shard_map/ppermute | solution.py:422
  53.9 3.2 %collective-permute-start.14 = (bf16[8,16,1024]{2,1,0:T(8,128)(2,1)}, bf16[8,16,1024]{2,1,0:T(8,128)(2,1)}, u32[]{:S(2)}, u32[]{:S(2)}) collective-permute-start(bf16[8,16,1024]{2,1,0:T(8,128)(2,1)} %get-tuple-element.90), channel_id=1, source_target_pairs={{0,13},{1,12},{2,15},{3,14},{4,9},{5,8},{6,11},{7,10},{8,5},{9,4},... | collective-permute-start | bytes 786440 | tf_op jit(solution)/shard_map/ppermute | solution.py:422
  60.1 8.0 %shard_map.72 = bf16[128,16,1024]{2,1,0:T(8,128)(2,1)} custom-call(s32[16,2,128]{2,1,0:T(2,128)} %copy-done.1, s32[16,2,128]{2,1,0:T(2,128)} %copy-done.1, bf16[128,16,1024]{2,1,0:T(8,128)(2,1)} %store_hbm.3, bf16[16,16,1024]{2,1,0:T(8,128)(2,1)} %copy-done), custom_call_target="tpu_custom_call" | custom-call | bytes 8388608 | tf_op jit(solution)/shard_map/pallas_call | solution.py:499
  68.5 2.2 %collective-permute-start.6 = (bf16[8,16,1024]{2,1,0:T(8,128)(2,1)S(1)}, bf16[8,16,1024]{2,1,0:T(8,128)(2,1)}, u32[]{:S(2)}, u32[]{:S(2)}) collective-permute-start(bf16[8,16,1024]{2,1,0:T(8,128)(2,1)S(1)} %copy-done.15), channel_id=1, source_target_pairs={{0,10},{1,11},{2,8},{3,9},{4,14},{5,15},{6,12},{7,13},{8,2},{9,3},... | collective-permute-start | bytes 786440 | tf_op jit(solution)/shard_map/ppermute | solution.py:422
  71.6 2.1 %collective-permute-start.8 = (bf16[8,16,1024]{2,1,0:T(8,128)(2,1)S(1)}, bf16[8,16,1024]{2,1,0:T(8,128)(2,1)}, u32[]{:S(2)}, u32[]{:S(2)}) collective-permute-start(bf16[8,16,1024]{2,1,0:T(8,128)(2,1)S(1)} %copy-done.11), channel_id=1, source_target_pairs={{0,14},{1,15},{2,12},{3,13},{4,10},{5,11},{6,8},{7,9},{8,6},{9,7},... | collective-permute-start | bytes 786440 | tf_op jit(solution)/shard_map/ppermute | solution.py:422
  73.8 3.3 %collective-permute-done.14.rest_14_ = bf16[8,16,1024]{2,1,0:T(8,128)(2,1)} collective-permute-done((bf16[8,16,1024]{2,1,0:T(8,128)(2,1)}, bf16[8,16,1024]{2,1,0:T(8,128)(2,1)}, u32[]{:S(2)}, u32[]{:S(2)}) %collective-permute-start.14) | collective-permute-done | bytes 262176 | tf_op jit(solution)/shard_map/ppermute | solution.py:422
  77.1 1.8 %collective-permute-start.9 = (bf16[8,16,1024]{2,1,0:T(8,128)(2,1)S(1)}, bf16[8,16,1024]{2,1,0:T(8,128)(2,1)}, u32[]{:S(2)}, u32[]{:S(2)}) collective-permute-start(bf16[8,16,1024]{2,1,0:T(8,128)(2,1)S(1)} %copy-done.10), channel_id=1, source_target_pairs={{0,3},{1,2},{2,1},{3,0},{4,7},{5,6},{6,5},{7,4},{8,11},{9,10},{10,... | collective-permute-start | bytes 786440 | tf_op jit(solution)/shard_map/ppermute | solution.py:422
  79.9 13.7 %shard_map.73 = (f32[5,4,128,384]{3,2,1,0:T(8,128)}, f32[5,8,384]{2,1,0:T(8,128)}) custom-call(s32[42]{0:T(128)} %pad_add_fusion.place, s32[5]{0:T(128)} %and_select_fusion.tiles, s32[5,1,128]{2,1,0:T(1,128)} %tile.9.rest_0_, s32[768,128]{1,0:T(8,128)} %broadcast_in_dim.223.rest_1_, bf16[160,6144]{1,0:T(8,128)(2,1)} %bitcast.72, bf16[160,1024]{1,0:T(8,128)(2,1)} %bitcast.77, ...), custom_call_target="tpu_custom_call" | custom-call | flops 3623878656 | bytes 7471104 | tf_op jit(solution)/shard_map/pallas_call | solution.py:300
  93.6 3.3 %collective-permute-start.15 = (bf16[8,16,1024]{2,1,0:T(8,128)(2,1)S(1)}, bf16[8,16,1024]{2,1,0:T(8,128)(2,1)S(1)}, u32[]{:S(2)}, u32[]{:S(2)}) collective-permute-start(bf16[8,16,1024]{2,1,0:T(8,128)(2,1)S(1)} %copy-done.9), channel_id=1, source_target_pairs={{0,11},{1,10},{2,9},{3,8},{4,15},{5,14},{6,13},{7,12},{8,3},{9,2},... | collective-permute-start | bytes 786440 | tf_op jit(solution)/shard_map/ppermute | solution.py:422
  97.0 3.2 %collective-permute-start.16 = (bf16[8,16,1024]{2,1,0:T(8,128)(2,1)S(1)}, bf16[8,16,1024]{2,1,0:T(8,128)(2,1)S(1)}, u32[]{:S(2)}, u32[]{:S(2)}) collective-permute-start(bf16[8,16,1024]{2,1,0:T(8,128)(2,1)S(1)} %copy-done.8), channel_id=1, source_target_pairs={{0,15},{1,14},{2,13},{3,12},{4,11},{5,10},{6,9},{7,8},{8,7},{9,6},... | collective-permute-start | bytes 786440 | tf_op jit(solution)/shard_map/ppermute | solution.py:422
  100.1 11.5 %collective-permute-done.8.rest_8_ = bf16[8,16,1024]{2,1,0:T(8,128)(2,1)} collective-permute-done((bf16[8,16,1024]{2,1,0:T(8,128)(2,1)S(1)}, bf16[8,16,1024]{2,1,0:T(8,128)(2,1)}, u32[]{:S(2)}, u32[]{:S(2)}) %collective-permute-start.8) | collective-permute-done | bytes 262176 | tf_op jit(solution)/shard_map/ppermute | solution.py:422
  112.7 22.3 %shard_map.74 = (f32[5,4,128,384]{3,2,1,0:T(8,128)}, f32[5,8,384]{2,1,0:T(8,128)}) custom-call(s32[80]{0:T(128)} %select_reduce_fusion.4.place, s32[5]{0:T(128)} %and_select_fusion.1.tiles, s32[5,1,128]{2,1,0:T(1,128)} %tile.9.rest_0_, s32[1280,128]{1,0:T(8,128)} %broadcast_in_dim.212.rest_1_, bf16[160,6144]{1,0:T(8,128)(2,1)} %bitcast.73, ...), custom_call_target="tpu_custom_call" | custom-call | flops 6039797760 | bytes 8519680 | tf_op jit(solution)/shard_map/pallas_call | solution.py:300
  135.9 9.9 %shard_map.75 = bf16[160,6144]{1,0:T(8,128)(2,1)} custom-call(s32[16]{0:T(128)} %select_reduce_fusion.6.place, s32[5]{0:T(128)} %and_select_fusion.2.tiles, s32[5,1,128]{2,1,0:T(1,128)} %tile.9.rest_0_, s32[256,128]{1,0:T(8,128)} %broadcast_in_dim.204.rest_1_, bf16[160,6144]{1,0:T(8,128)(2,1)} %bitcast.74, f32[5,4,128,384]{3,2,1,0:T(8,128)} %get-tuple-element.91.rest_3_, ...), custom_call_target="tpu_custom_call" | custom-call | flops 1207959552 | bytes 6422528 | tf_op jit(solution)/shard_map/pallas_call | solution.py:300
  (116 shorter events, 20.5 us)
Async XLA Ops:
  2.3 3.5 %collective-permute-start = (s32[1,2,128]{2,1,0:T(2,128)}, s32[1,2,128]{2,1,0:T(2,128)S(1)}, u32[]{:S(2)}, u32[]{:S(2)}) collective-permute-start(s32[1,2,128]{2,1,0:T(2,128)} %get-tuple-element.49), channel_id=1, source_target_pairs={{0,8},{1,9},{2,10},{3,11},{4,12},{5,13},{6,14},{7,15},{8,0},{9,1},... | collective-permute-start | bytes 3080 | tf_op jit(solution)/shard_map/ppermute | solution.py:422
  4.6 2.6 %collective-permute-start.1 = (s32[1,2,128]{2,1,0:T(2,128)}, s32[1,2,128]{2,1,0:T(2,128)S(1)}, u32[]{:S(2)}, u32[]{:S(2)}) collective-permute-start(s32[1,2,128]{2,1,0:T(2,128)} %get-tuple-element.50), channel_id=1, source_target_pairs={{0,12},{1,13},{2,14},{3,15},{4,8},{5,9},{6,10},{7,11},{8,4},{9,5},... | collective-permute-start | bytes 3080 | tf_op jit(solution)/shard_map/ppermute | solution.py:422
  10.4 12.6 %all-to-all-start = ((s32[16,2,128]{2,1,0:T(2,128)}), s32[16,2,128]{2,1,0:T(2,128)S(1)}, u32[]{:S(2)}, u32[]{:S(2)}) async-start(s32[16,2,128]{2,1,0:T(2,128)} %get-tuple-element.54), calls=%async_computation | async-start | bytes 32768 | tf_op jit(solution)/shard_map/all_to_all | solution.py:425
  17.9 28.2 %collective-permute-start.2 = (bf16[8,16,1024]{2,1,0:T(8,128)(2,1)}, bf16[8,16,1024]{2,1,0:T(8,128)(2,1)S(1)}, u32[]{:S(2)}, u32[]{:S(2)}) collective-permute-start(bf16[8,16,1024]{2,1,0:T(8,128)(2,1)} %get-tuple-element.76), channel_id=1, source_target_pairs={{0,8},{1,9},{2,10},{3,11},{4,12},{5,13},{6,14},{7,15},{8,0},{9,1},... | collective-permute-start | bytes 786440 | tf_op jit(solution)/shard_map/ppermute | solution.py:422
  20.1 28.8 %collective-permute-start.3 = (bf16[8,16,1024]{2,1,0:T(8,128)(2,1)}, bf16[8,16,1024]{2,1,0:T(8,128)(2,1)S(1)}, u32[]{:S(2)}, u32[]{:S(2)}) collective-permute-start(bf16[8,16,1024]{2,1,0:T(8,128)(2,1)} %get-tuple-element.77), channel_id=1, source_target_pairs={{0,12},{1,13},{2,14},{3,15},{4,8},{5,9},{6,10},{7,11},{8,4},{9,5},... | collective-permute-start | bytes 786440 | tf_op jit(solution)/shard_map/ppermute | solution.py:422
  32.0 27.2 %all-to-all-start.1 = ((bf16[16,16,1024]{2,1,0:T(8,128)(2,1)}), bf16[16,16,1024]{2,1,0:T(8,128)(2,1)S(1)}, u32[]{:S(2)}, u32[]{:S(2)}) async-start(bf16[16,16,1024]{2,1,0:T(8,128)(2,1)} %shard_map.71), calls=%async_computation.1 | async-start | bytes 1048576 | tf_op jit(solution)/shard_map/all_to_all | solution.py:425
  38.4 15.5 %collective-permute-start.4 = (bf16[8,16,1024]{2,1,0:T(8,128)(2,1)}, bf16[8,16,1024]{2,1,0:T(8,128)(2,1)S(1)}, u32[]{:S(2)}, u32[]{:S(2)}) collective-permute-start(bf16[8,16,1024]{2,1,0:T(8,128)(2,1)} %get-tuple-element.78), channel_id=1, source_target_pairs={{0,4},{1,5},{2,6},{3,7},{4,0},{5,1},{6,2},{7,3},{8,12},{9,13},{10,... | collective-permute-start | bytes 786440 | tf_op jit(solution)/shard_map/ppermute | solution.py:422
  41.6 26.5 %collective-permute-start.10 = (bf16[8,16,1024]{2,1,0:T(8,128)(2,1)}, bf16[8,16,1024]{2,1,0:T(8,128)(2,1)S(1)}, u32[]{:S(2)}, u32[]{:S(2)}) collective-permute-start(bf16[8,16,1024]{2,1,0:T(8,128)(2,1)} %get-tuple-element.86), channel_id=1, source_target_pairs={{0,5},{1,4},{2,7},{3,6},{4,1},{5,0},{6,3},{7,2},{8,13},{9,12},{10,... | collective-permute-start | bytes 786440 | tf_op jit(solution)/shard_map/ppermute | solution.py:422
  43.5 25.0 %collective-permute-start.11 = (bf16[8,16,1024]{2,1,0:T(8,128)(2,1)}, bf16[8,16,1024]{2,1,0:T(8,128)(2,1)S(1)}, u32[]{:S(2)}, u32[]{:S(2)}) collective-permute-start(bf16[8,16,1024]{2,1,0:T(8,128)(2,1)} %get-tuple-element.87), channel_id=1, source_target_pairs={{0,1},{1,0},{2,3},{3,2},{4,5},{5,4},{6,7},{7,6},{8,9},{9,8},{10,11... | collective-permute-start | bytes 786440 | tf_op jit(solution)/shard_map/ppermute | solution.py:422
  46.1 33.7 %copy-start.13 = (bf16[8,16,1024]{2,1,0:T(8,128)(2,1)}, bf16[8,16,1024]{2,1,0:T(8,128)(2,1)S(1)}, u32[]{:S(2)}) copy-start(bf16[8,16,1024]{2,1,0:T(8,128)(2,1)S(1)} %collective-permute-done.2.rest_5_) | copy-start | bytes 786436
  46.1 24.5 %collective-permute-start.12 = (bf16[8,16,1024]{2,1,0:T(8,128)(2,1)}, bf16[8,16,1024]{2,1,0:T(8,128)(2,1)S(1)}, u32[]{:S(2)}, u32[]{:S(2)}) collective-permute-start(bf16[8,16,1024]{2,1,0:T(8,128)(2,1)} %get-tuple-element.88), channel_id=1, source_target_pairs={{0,9},{1,8},{2,11},{3,10},{4,13},{5,12},{6,15},{7,14},{8,1},{9,0},... | collective-permute-start | bytes 786440 | tf_op jit(solution)/shard_map/ppermute | solution.py:422
  48.9 31.0 %copy-start.14 = (bf16[8,16,1024]{2,1,0:T(8,128)(2,1)}, bf16[8,16,1024]{2,1,0:T(8,128)(2,1)S(1)}, u32[]{:S(2)}) copy-start(bf16[8,16,1024]{2,1,0:T(8,128)(2,1)S(1)} %collective-permute-done.3.rest_6_) | copy-start | bytes 786436
  48.9 22.7 %collective-permute-start.13 = (bf16[8,16,1024]{2,1,0:T(8,128)(2,1)}, bf16[8,16,1024]{2,1,0:T(8,128)(2,1)}, u32[]{:S(2)}, u32[]{:S(2)}) collective-permute-start(bf16[8,16,1024]{2,1,0:T(8,128)(2,1)} %get-tuple-element.89), channel_id=1, source_target_pairs={{0,6},{1,7},{2,4},{3,5},{4,2},{5,3},{6,0},{7,1},{8,14},{9,15},{10,... | collective-permute-start | bytes 786440 | tf_op jit(solution)/shard_map/ppermute | solution.py:422
  53.9 26.0 %copy-start.19 = (bf16[8,16,1024]{2,1,0:T(8,128)(2,1)}, bf16[8,16,1024]{2,1,0:T(8,128)(2,1)S(1)}, u32[]{:S(2)}) copy-start(bf16[8,16,1024]{2,1,0:T(8,128)(2,1)S(1)} %collective-permute-done.4.rest_7_) | copy-start | bytes 786436
  53.9 23.3 %collective-permute-start.14 = (bf16[8,16,1024]{2,1,0:T(8,128)(2,1)}, bf16[8,16,1024]{2,1,0:T(8,128)(2,1)}, u32[]{:S(2)}, u32[]{:S(2)}) collective-permute-start(bf16[8,16,1024]{2,1,0:T(8,128)(2,1)} %get-tuple-element.90), channel_id=1, source_target_pairs={{0,13},{1,12},{2,15},{3,14},{4,9},{5,8},{6,11},{7,10},{8,5},{9,4},... | collective-permute-start | bytes 786440 | tf_op jit(solution)/shard_map/ppermute | solution.py:422
  68.1 25.5 %copy-start.17 = (bf16[8,16,1024]{2,1,0:T(8,128)(2,1)}, bf16[8,16,1024]{2,1,0:T(8,128)(2,1)S(1)}, u32[]{:S(2)}) copy-start(bf16[8,16,1024]{2,1,0:T(8,128)(2,1)S(1)} %collective-permute-done.10.rest_10_) | copy-start | bytes 786436
  68.1 25.5 %collective-permute-start.5 = (bf16[8,16,1024]{2,1,0:T(8,128)(2,1)S(1)}, bf16[8,16,1024]{2,1,0:T(8,128)(2,1)}, u32[]{:S(2)}, u32[]{:S(2)}) collective-permute-start(bf16[8,16,1024]{2,1,0:T(8,128)(2,1)S(1)} %copy-done.16), channel_id=1, source_target_pairs={{0,7},{1,6},{2,5},{3,4},{4,3},{5,2},{6,1},{7,0},{8,15},{9,14},{10,... | collective-permute-start | bytes 786440 | tf_op jit(solution)/shard_map/ppermute | solution.py:422
  68.5 25.1 %copy-start.18 = (bf16[8,16,1024]{2,1,0:T(8,128)(2,1)}, bf16[8,16,1024]{2,1,0:T(8,128)(2,1)S(1)}, u32[]{:S(2)}) copy-start(bf16[8,16,1024]{2,1,0:T(8,128)(2,1)S(1)} %collective-permute-done.11.rest_11_) | copy-start | bytes 786436
  68.5 28.5 %collective-permute-start.6 = (bf16[8,16,1024]{2,1,0:T(8,128)(2,1)S(1)}, bf16[8,16,1024]{2,1,0:T(8,128)(2,1)}, u32[]{:S(2)}, u32[]{:S(2)}) collective-permute-start(bf16[8,16,1024]{2,1,0:T(8,128)(2,1)S(1)} %copy-done.15), channel_id=1, source_target_pairs={{0,10},{1,11},{2,8},{3,9},{4,14},{5,15},{6,12},{7,13},{8,2},{9,3},... | collective-permute-start | bytes 786440 | tf_op jit(solution)/shard_map/ppermute | solution.py:422
  70.7 29.5 %collective-permute-start.7 = (bf16[8,16,1024]{2,1,0:T(8,128)(2,1)S(1)}, bf16[8,16,1024]{2,1,0:T(8,128)(2,1)}, u32[]{:S(2)}, u32[]{:S(2)}) collective-permute-start(bf16[8,16,1024]{2,1,0:T(8,128)(2,1)S(1)} %copy-done.12), channel_id=1, source_target_pairs={{0,2},{1,3},{2,0},{3,1},{4,6},{5,7},{6,4},{7,5},{8,10},{9,11},{10,... | collective-permute-start | bytes 786440 | tf_op jit(solution)/shard_map/ppermute | solution.py:422
  71.6 40.0 %collective-permute-start.8 = (bf16[8,16,1024]{2,1,0:T(8,128)(2,1)S(1)}, bf16[8,16,1024]{2,1,0:T(8,128)(2,1)}, u32[]{:S(2)}, u32[]{:S(2)}) collective-permute-start(bf16[8,16,1024]{2,1,0:T(8,128)(2,1)S(1)} %copy-done.11), channel_id=1, source_target_pairs={{0,14},{1,15},{2,12},{3,13},{4,10},{5,11},{6,8},{7,9},{8,6},{9,7},... | collective-permute-start | bytes 786440 | tf_op jit(solution)/shard_map/ppermute | solution.py:422
  77.1 34.5 %collective-permute-start.9 = (bf16[8,16,1024]{2,1,0:T(8,128)(2,1)S(1)}, bf16[8,16,1024]{2,1,0:T(8,128)(2,1)}, u32[]{:S(2)}, u32[]{:S(2)}) collective-permute-start(bf16[8,16,1024]{2,1,0:T(8,128)(2,1)S(1)} %copy-done.10), channel_id=1, source_target_pairs={{0,3},{1,2},{2,1},{3,0},{4,7},{5,6},{6,5},{7,4},{8,11},{9,10},{10,... | collective-permute-start | bytes 786440 | tf_op jit(solution)/shard_map/ppermute | solution.py:422
  93.6 41.4 %collective-permute-start.15 = (bf16[8,16,1024]{2,1,0:T(8,128)(2,1)S(1)}, bf16[8,16,1024]{2,1,0:T(8,128)(2,1)S(1)}, u32[]{:S(2)}, u32[]{:S(2)}) collective-permute-start(bf16[8,16,1024]{2,1,0:T(8,128)(2,1)S(1)} %copy-done.9), channel_id=1, source_target_pairs={{0,11},{1,10},{2,9},{3,8},{4,15},{5,14},{6,13},{7,12},{8,3},{9,2},... | collective-permute-start | bytes 786440 | tf_op jit(solution)/shard_map/ppermute | solution.py:422
  97.0 38.1 %collective-permute-start.16 = (bf16[8,16,1024]{2,1,0:T(8,128)(2,1)S(1)}, bf16[8,16,1024]{2,1,0:T(8,128)(2,1)S(1)}, u32[]{:S(2)}, u32[]{:S(2)}) collective-permute-start(bf16[8,16,1024]{2,1,0:T(8,128)(2,1)S(1)} %copy-done.8), channel_id=1, source_target_pairs={{0,15},{1,14},{2,13},{3,12},{4,11},{5,10},{6,9},{7,8},{8,7},{9,6},... | collective-permute-start | bytes 786440 | tf_op jit(solution)/shard_map/ppermute | solution.py:422
  (16 other events, 166.5 us)

commit v17 on v16

--- a/solution.py
+++ b/solution.py
@@ -411,7 +411,7 @@
     wide = pltpu.VMEM((8, -(-picked // LANES) * LANES), jnp.int32)
     if holders == 16:
         first = (8, 12)
-        groups = [(0, 8, 12, 4), (7, 10, 2, 14, 3, 5, 1, 9, 6, 13), (11, 15)]
+        groups = [(0, 8, 12, 4, 5, 1), (9, 6, 13, 7, 10, 2, 14, 3), (11, 15)]
         others = [d for group in groups for d in group if d not in first]
     else:
         first = ()
@@ -519,7 +519,7 @@
 
     orders = page_order(table[0], positions[0], own, hold, capacity, groups, page_len)
     sel_lanes = jnp.tile(positions.reshape(-1, 1, QUERY_BLOCK), (1, 1, LANES // QUERY_BLOCK))
-    store_out, sel_lanes = lax.optimization_barrier((store_out, sel_lanes))
+    store_out, sel_lanes, orders = lax.optimization_barrier((store_out, sel_lanes, orders))
     state = ()
     for at, (group, order) in enumerate(zip(groups, orders)):
         state = attend(

time: 148 us -> 144 us (0.973); the launches traced: 146 us -> 143 us
  starting transfers between devices: 41 us -> 38.4 us
    ppermute x17, starting transfers between devices: 27.1 us -> 24.5 us  [swap(): return lax.ppermute(x, 'store', [(h, h ^ d) for h in range(holders)])]
  transfers between devices with their start and end apart: 19 -> 19, of which waited for: 7 -> 7; matrix products, arithmetic and copies ran while one was open for 9% -> 9% of each run, Pallas kernels for 35% -> 36%
where the time goes in v17:
time: 144 us; the launch traced here: 143 us
  Pallas kernels  65.2 us (45%)
  starting transfers between devices  38.4 us (27%)
  waiting for transfers between devices  22.7 us (16%)
  other arithmetic  8.51 us (6%)
  local copies, waits for them, and re-layouts  7.52 us (5%)
    pallas_call x3, Pallas kernels, attend(): pl.pallas_call(functools.partial(attend_kernel, first, last, len(contexts...  45.8 us
    ppermute x17, starting transfers between devices, swap(): return lax.ppermute(x, 'store', [(h, h ^ d) for h in range(holders)])  24.5 us
    ppermute x17, waiting for transfers between devices, swap(): return lax.ppermute(x, 'store', [(h, h ^ d) for h in range(holders)])  22.2 us
    all_to_all x2, starting transfers between devices, exchange(): return lax.all_to_all(x, 'store', split_axis=0, concat_axis=0, tiled=True)  13.9 us
    pallas_call x1, Pallas kernels, per_device(): pl.pallas_call(write_back_kernel, grid_spec=pltpu.PrefetchScalarGridSpec(...  8.02 us
    pallas_call x1, Pallas kernels, per_device(): pl.pallas_call(functools.partial(gather_kernel, capacity, others), grid_s...  4.9 us
    unnamed x44, local copies, waits for them, and re-layouts  2.99 us
  transfers between devices with their start and end apart: 19, of which 7 were waited for; matrix products, arithmetic and copies ran while one was open for 9% of the time, Pallas kernels for 36%

profile of v17, /device:TPU:9, one launch (start us, length us, event | category | flops | bytes accessed | tf_op | source)
XLA Modules:
  0.0 143.3 jit_solution(1832892150006927940)
XLA Ops:
  0.6 1.7 %shard_map.68 = (s32[16,2,128]{2,1,0:T(2,128)}, s32[1,2,128]{2,1,0:T(2,128)}, s32[1,2,128]{2,1,0:T(2,128)}) custom-call(s32[1]{0:T(128)} %bitcast.own, s32[1,128]{1,0:T(1,128)} %table_ref.2, s32[1,160]{1,0:T(1,128)} %sel_ref.2), custom_call_target="tpu_custom_call" | custom-call | tf_op jit(solution)/shard_map/pallas_call | solution.py:427
  2.3 2.3 %collective-permute-start = (s32[1,2,128]{2,1,0:T(2,128)}, s32[1,2,128]{2,1,0:T(2,128)S(1)}, u32[]{:S(2)}, u32[]{:S(2)}) collective-permute-start(s32[1,2,128]{2,1,0:T(2,128)} %get-tuple-element.58), channel_id=1, source_target_pairs={{0,8},{1,9},{2,10},{3,11},{4,12},{5,13},{6,14},{7,15},{8,0},{9,1},... | collective-permute-start | bytes 3080 | tf_op jit(solution)/shard_map/ppermute | solution.py:422
  5.8 1.4 collective-permute-done.1.refs_1_
  7.8 2.5 %shard_map.69 = (bf16[8,16,1024]{2,1,0:T(8,128)(2,1)}, bf16[8,16,1024]{2,1,0:T(8,128)(2,1)}) custom-call(s32[1,2,128]{2,1,0:T(2,128)} %copy-done.6, s32[1,2,128]{2,1,0:T(2,128)} %copy-done.7, bf16[128,16,1024]{2,1,0:T(8,128)(2,1)} %store_hbm.3), custom_call_target="tpu_custom_call" | custom-call | tf_op jit(solution)/shard_map/pallas_call | solution.py:445
  10.4 7.5 %all-to-all-start = ((s32[16,2,128]{2,1,0:T(2,128)}), s32[16,2,128]{2,1,0:T(2,128)S(1)}, u32[]{:S(2)}, u32[]{:S(2)}) async-start(s32[16,2,128]{2,1,0:T(2,128)} %get-tuple-element.63), calls=%async_computation | async-start | bytes 32768 | tf_op jit(solution)/shard_map/all_to_all | solution.py:425
  17.9 2.2 %collective-permute-start.2 = (bf16[8,16,1024]{2,1,0:T(8,128)(2,1)}, bf16[8,16,1024]{2,1,0:T(8,128)(2,1)S(1)}, u32[]{:S(2)}, u32[]{:S(2)}) collective-permute-start(bf16[8,16,1024]{2,1,0:T(8,128)(2,1)} %get-tuple-element.94), channel_id=1, source_target_pairs={{0,8},{1,9},{2,10},{3,11},{4,12},{5,13},{6,14},{7,15},{8,0},{9,1},... | collective-permute-start | bytes 786440 | tf_op jit(solution)/shard_map/ppermute | solution.py:422
  20.1 2.4 %shard_map.71 = bf16[16,16,1024]{2,1,0:T(8,128)(2,1)} custom-call(s32[1,128]{1,0:T(1,128)} %table_ref.2, s32[1,160]{1,0:T(1,128)} %sel_ref.2, bf16[160,1024]{1,0:T(8,128)(2,1)} %bitcast.74), custom_call_target="tpu_custom_call" | custom-call | tf_op jit(solution)/shard_map/pallas_call | solution.py:469
  23.5 4.9 %shard_map.70 = (bf16[8,16,1024]{2,1,0:T(8,128)(2,1)}, bf16[8,16,1024]{2,1,0:T(8,128)(2,1)}, bf16[8,16,1024]{2,1,0:T(8,128)(2,1)}, bf16[8,16,1024]{2,1,0:T(8,128...) custom-call(s32[1]{0:T(128)} %bitcast.own, ...), custom_call_target="tpu_custom_call" | custom-call | tf_op jit(solution)/shard_map/pallas_call | solution.py:478
  31.9 6.4 %all-to-all-start.1 = ((bf16[16,16,1024]{2,1,0:T(8,128)(2,1)}), bf16[16,16,1024]{2,1,0:T(8,128)(2,1)S(1)}, u32[]{:S(2)}, u32[]{:S(2)}) async-start(bf16[16,16,1024]{2,1,0:T(8,128)(2,1)} %shard_map.71), calls=%async_computation.1 | async-start | bytes 1048576 | tf_op jit(solution)/shard_map/all_to_all | solution.py:425
  39.3 1.9 %collective-permute-start.5 = (bf16[8,16,1024]{2,1,0:T(8,128)(2,1)}, bf16[8,16,1024]{2,1,0:T(8,128)(2,1)S(1)}, u32[]{:S(2)}, u32[]{:S(2)}) collective-permute-start(bf16[8,16,1024]{2,1,0:T(8,128)(2,1)} %get-tuple-element.97), channel_id=1, source_target_pairs={{0,5},{1,4},{2,7},{3,6},{4,1},{5,0},{6,3},{7,2},{8,13},{9,12},{10,... | collective-permute-start | bytes 786440 | tf_op jit(solution)/shard_map/ppermute | solution.py:422
  42.2 2.2 %select_reduce_fusion = (s32[64,16]{1,0:T(8,128)S(1)}, s32[64,16]{1,0:T(8,128)S(1)}) fusion(s32[128,16]{0,1:T(8,128)S(1)} %broadcast_select_fusion.2, pred[64,128]{1,0:T(8,128)(4,1)S(1)} %get-tuple-element.128, pred[64,128]{1,0:T(8,128)(4,1)S(1)} %get-tuple-element.137), kind=kLoop, calls=%fused_computation.1 | loop fusion | flops 522240 | bytes 32768 | tf_op jit(solution)/shard_map/reduce_sum | solution.py:385
  45.4 2.5 %collective-permute-start.7 = (bf16[8,16,1024]{2,1,0:T(8,128)(2,1)}, bf16[8,16,1024]{2,1,0:T(8,128)(2,1)S(1)}, u32[]{:S(2)}, u32[]{:S(2)}) collective-permute-start(bf16[8,16,1024]{2,1,0:T(8,128)(2,1)} %get-tuple-element.101), channel_id=1, source_target_pairs={{0,9},{1,8},{2,11},{3,10},{4,13},{5,12},{6,15},{7,14},{8,1},{9,0},... | collective-permute-start | bytes 786440 | tf_op jit(solution)/shard_map/ppermute | solution.py:422
  49.2 4.6 %collective-permute-done.4.rest_7_ = bf16[8,16,1024]{2,1,0:T(8,128)(2,1)S(1)} collective-permute-done((bf16[8,16,1024]{2,1,0:T(8,128)(2,1)}, bf16[8,16,1024]{2,1,0:T(8,128)(2,1)S(1)}, u32[]{:S(2)}, u32[]{:S(2)}) %collective-permute-start.4) | collective-permute-done | bytes 262176 | tf_op jit(solution)/shard_map/ppermute | solution.py:422
  53.8 3.2 %collective-permute-start.9 = (bf16[8,16,1024]{2,1,0:T(8,128)(2,1)}, bf16[8,16,1024]{2,1,0:T(8,128)(2,1)}, u32[]{:S(2)}, u32[]{:S(2)}) collective-permute-start(bf16[8,16,1024]{2,1,0:T(8,128)(2,1)} %get-tuple-element.103), channel_id=1, source_target_pairs={{0,13},{1,12},{2,15},{3,14},{4,9},{5,8},{6,11},{7,10},{8,5},{9,4},... | collective-permute-start | bytes 786440 | tf_op jit(solution)/shard_map/ppermute | solution.py:422
  59.9 8.0 %shard_map.72 = bf16[128,16,1024]{2,1,0:T(8,128)(2,1)} custom-call(s32[16,2,128]{2,1,0:T(2,128)} %copy-done.1, s32[16,2,128]{2,1,0:T(2,128)} %copy-done.1, bf16[128,16,1024]{2,1,0:T(8,128)(2,1)} %store_hbm.3, bf16[16,16,1024]{2,1,0:T(8,128)(2,1)} %copy-done), custom_call_target="tpu_custom_call" | custom-call | bytes 8388608 | tf_op jit(solution)/shard_map/pallas_call | solution.py:499
  71.0 2.1 %collective-permute-start.11 = (bf16[8,16,1024]{2,1,0:T(8,128)(2,1)S(1)}, bf16[8,16,1024]{2,1,0:T(8,128)(2,1)}, u32[]{:S(2)}, u32[]{:S(2)}) collective-permute-start(bf16[8,16,1024]{2,1,0:T(8,128)(2,1)S(1)} %copy-done.15), channel_id=1, source_target_pairs={{0,10},{1,11},{2,8},{3,9},{4,14},{5,15},{6,12},{7,13},{8,2},{9,3},... | collective-permute-start | bytes 786440 | tf_op jit(solution)/shard_map/ppermute | solution.py:422
  74.7 2.5 %collective-permute-done.9.rest_7_ = bf16[8,16,1024]{2,1,0:T(8,128)(2,1)} collective-permute-done((bf16[8,16,1024]{2,1,0:T(8,128)(2,1)}, bf16[8,16,1024]{2,1,0:T(8,128)(2,1)}, u32[]{:S(2)}, u32[]{:S(2)}) %collective-permute-start.9) | collective-permute-done | bytes 262176 | tf_op jit(solution)/shard_map/ppermute | solution.py:422
  77.2 1.6 %collective-permute-start.14 = (bf16[8,16,1024]{2,1,0:T(8,128)(2,1)S(1)}, bf16[8,16,1024]{2,1,0:T(8,128)(2,1)}, u32[]{:S(2)}, u32[]{:S(2)}) collective-permute-start(bf16[8,16,1024]{2,1,0:T(8,128)(2,1)S(1)} %copy-done.10), channel_id=1, source_target_pairs={{0,3},{1,2},{2,1},{3,0},{4,7},{5,6},{6,5},{7,4},{8,11},{9,10},{10,... | collective-permute-start | bytes 786440 | tf_op jit(solution)/shard_map/ppermute | solution.py:422
  78.8 16.5 %shard_map.73 = (f32[5,4,128,384]{3,2,1,0:T(8,128)}, f32[5,8,384]{2,1,0:T(8,128)}) custom-call(s32[58]{0:T(128)} %pad_add_fusion.place, s32[5]{0:T(128)} %and_select_fusion.2.tiles, s32[5,1,128]{2,1,0:T(1,128)} %tile.12.rest_0_, s32[1024,128]{1,0:T(8,128)} %broadcast_in_dim.192.rest_1_, bf16[160,6144]{1,0:T(8,128)(2,1)} %bitcast.70, ...), custom_call_target="tpu_custom_call" | custom-call | flops 4831838208 | bytes 7995392 | tf_op jit(solution)/shard_map/pallas_call | solution.py:300
  95.4 3.1 %collective-permute-start.15 = (bf16[8,16,1024]{2,1,0:T(8,128)(2,1)S(1)}, bf16[8,16,1024]{2,1,0:T(8,128)(2,1)S(1)}, u32[]{:S(2)}, u32[]{:S(2)}) collective-permute-start(bf16[8,16,1024]{2,1,0:T(8,128)(2,1)S(1)} %copy-done.9), channel_id=1, source_target_pairs={{0,11},{1,10},{2,9},{3,8},{4,15},{5,14},{6,13},{7,12},{8,3},{9,2},... | collective-permute-start | bytes 786440 | tf_op jit(solution)/shard_map/ppermute | solution.py:422
  98.5 3.2 %collective-permute-start.16 = (bf16[8,16,1024]{2,1,0:T(8,128)(2,1)S(1)}, bf16[8,16,1024]{2,1,0:T(8,128)(2,1)S(1)}, u32[]{:S(2)}, u32[]{:S(2)}) collective-permute-start(bf16[8,16,1024]{2,1,0:T(8,128)(2,1)S(1)} %copy-done.8), channel_id=1, source_target_pairs={{0,15},{1,14},{2,13},{3,12},{4,11},{5,10},{6,9},{7,8},{8,7},{9,6},... | collective-permute-start | bytes 786440 | tf_op jit(solution)/shard_map/ppermute | solution.py:422
  101.7 11.5 %collective-permute-done.13.rest_11_ = bf16[8,16,1024]{2,1,0:T(8,128)(2,1)} collective-permute-done((bf16[8,16,1024]{2,1,0:T(8,128)(2,1)S(1)}, bf16[8,16,1024]{2,1,0:T(8,128)(2,1)}, u32[]{:S(2)}, u32[]{:S(2)}) %collective-permute-start.13) | collective-permute-done | bytes 262176 | tf_op jit(solution)/shard_map/ppermute | solution.py:422
  113.3 19.4 %shard_map.74 = (f32[5,4,128,384]{3,2,1,0:T(8,128)}, f32[5,8,384]{2,1,0:T(8,128)}) custom-call(s32[64]{0:T(128)} %select_reduce_fusion.4.place, s32[5]{0:T(128)} %get-tuple-element.88.tiles, s32[5,1,128]{2,1,0:T(1,128)} %tile.12.rest_0_, s32[1024,128]{1,0:T(8,128)} %broadcast_in_dim.197.rest_1_, bf16[160,6144]{1,0:T(8,128)(2,1)} %bitcast.71, ...), custom_call_target="tpu_custom_call" | custom-call | flops 4831838208 | bytes 7995392 | tf_op jit(solution)/shard_map/pallas_call | solution.py:300
  133.4 9.9 %shard_map.75 = bf16[160,6144]{1,0:T(8,128)(2,1)} custom-call(s32[16]{0:T(128)} %select_reduce_fusion.6.place, s32[5]{0:T(128)} %get-tuple-element.84.tiles, s32[5,1,128]{2,1,0:T(1,128)} %tile.12.rest_0_, s32[256,128]{1,0:T(8,128)} %broadcast_in_dim.205.rest_1_, bf16[160,6144]{1,0:T(8,128)(2,1)} %bitcast.72, f32[5,4,128,384]{3,2,1,0:T(8,128)} %get-tuple-element.109.rest_3_, ...), custom_call_target="tpu_custom_call" | custom-call | flops 1207959552 | bytes 6422528 | tf_op jit(solution)/shard_map/pallas_call | solution.py:300
  (113 shorter events, 18.7 us)
Async XLA Ops:
  2.3 3.5 %collective-permute-start = (s32[1,2,128]{2,1,0:T(2,128)}, s32[1,2,128]{2,1,0:T(2,128)S(1)}, u32[]{:S(2)}, u32[]{:S(2)}) collective-permute-start(s32[1,2,128]{2,1,0:T(2,128)} %get-tuple-element.58), channel_id=1, source_target_pairs={{0,8},{1,9},{2,10},{3,11},{4,12},{5,13},{6,14},{7,15},{8,0},{9,1},... | collective-permute-start | bytes 3080 | tf_op jit(solution)/shard_map/ppermute | solution.py:422
  4.6 2.6 %collective-permute-start.1 = (s32[1,2,128]{2,1,0:T(2,128)}, s32[1,2,128]{2,1,0:T(2,128)S(1)}, u32[]{:S(2)}, u32[]{:S(2)}) collective-permute-start(s32[1,2,128]{2,1,0:T(2,128)} %get-tuple-element.59), channel_id=1, source_target_pairs={{0,12},{1,13},{2,14},{3,15},{4,8},{5,9},{6,10},{7,11},{8,4},{9,5},... | collective-permute-start | bytes 3080 | tf_op jit(solution)/shard_map/ppermute | solution.py:422
  4.6 23.9 %copy-start.5 = (s32[1,128]{1,0:T(1,128)S(1)}, s32[1,128]{1,0:T(1,128)}, u32[]{:S(2)}) copy-start(s32[1,128]{1,0:T(1,128)} %table_ref.2) | copy-start | bytes 1540
  4.6 24.2 %copy-start.4 = (s32[1,160]{1,0:T(1,128)S(1)}, s32[1,160]{1,0:T(1,128)}, u32[]{:S(2)}) copy-start(s32[1,160]{1,0:T(1,128)} %sel_ref.2) | copy-start | bytes 1924
  10.4 12.6 %all-to-all-start = ((s32[16,2,128]{2,1,0:T(2,128)}), s32[16,2,128]{2,1,0:T(2,128)S(1)}, u32[]{:S(2)}, u32[]{:S(2)}) async-start(s32[16,2,128]{2,1,0:T(2,128)} %get-tuple-element.63), calls=%async_computation | async-start | bytes 32768 | tf_op jit(solution)/shard_map/all_to_all | solution.py:425
  17.9 27.5 %collective-permute-start.2 = (bf16[8,16,1024]{2,1,0:T(8,128)(2,1)}, bf16[8,16,1024]{2,1,0:T(8,128)(2,1)S(1)}, u32[]{:S(2)}, u32[]{:S(2)}) collective-permute-start(bf16[8,16,1024]{2,1,0:T(8,128)(2,1)} %get-tuple-element.94), channel_id=1, source_target_pairs={{0,8},{1,9},{2,10},{3,11},{4,12},{5,13},{6,14},{7,15},{8,0},{9,1},... | collective-permute-start | bytes 786440 | tf_op jit(solution)/shard_map/ppermute | solution.py:422
  20.1 28.8 %collective-permute-start.3 = (bf16[8,16,1024]{2,1,0:T(8,128)(2,1)}, bf16[8,16,1024]{2,1,0:T(8,128)(2,1)S(1)}, u32[]{:S(2)}, u32[]{:S(2)}) collective-permute-start(bf16[8,16,1024]{2,1,0:T(8,128)(2,1)} %get-tuple-element.95), channel_id=1, source_target_pairs={{0,12},{1,13},{2,14},{3,15},{4,8},{5,9},{6,10},{7,11},{8,4},{9,5},... | collective-permute-start | bytes 786440 | tf_op jit(solution)/shard_map/ppermute | solution.py:422
  31.9 27.2 %all-to-all-start.1 = ((bf16[16,16,1024]{2,1,0:T(8,128)(2,1)}), bf16[16,16,1024]{2,1,0:T(8,128)(2,1)S(1)}, u32[]{:S(2)}, u32[]{:S(2)}) async-start(bf16[16,16,1024]{2,1,0:T(8,128)(2,1)} %shard_map.71), calls=%async_computation.1 | async-start | bytes 1048576 | tf_op jit(solution)/shard_map/all_to_all | solution.py:425
  39.1 14.7 %collective-permute-start.4 = (bf16[8,16,1024]{2,1,0:T(8,128)(2,1)}, bf16[8,16,1024]{2,1,0:T(8,128)(2,1)S(1)}, u32[]{:S(2)}, u32[]{:S(2)}) collective-permute-start(bf16[8,16,1024]{2,1,0:T(8,128)(2,1)} %get-tuple-element.96), channel_id=1, source_target_pairs={{0,4},{1,5},{2,6},{3,7},{4,0},{5,1},{6,2},{7,3},{8,12},{9,13},{10,... | collective-permute-start | bytes 786440 | tf_op jit(solution)/shard_map/ppermute | solution.py:422
  39.3 31.4 %collective-permute-start.5 = (bf16[8,16,1024]{2,1,0:T(8,128)(2,1)}, bf16[8,16,1024]{2,1,0:T(8,128)(2,1)S(1)}, u32[]{:S(2)}, u32[]{:S(2)}) collective-permute-start(bf16[8,16,1024]{2,1,0:T(8,128)(2,1)} %get-tuple-element.97), channel_id=1, source_target_pairs={{0,5},{1,4},{2,7},{3,6},{4,1},{5,0},{6,3},{7,2},{8,13},{9,12},{10,... | collective-permute-start | bytes 786440 | tf_op jit(solution)/shard_map/ppermute | solution.py:422
  41.1 29.9 %collective-permute-start.6 = (bf16[8,16,1024]{2,1,0:T(8,128)(2,1)}, bf16[8,16,1024]{2,1,0:T(8,128)(2,1)S(1)}, u32[]{:S(2)}, u32[]{:S(2)}) collective-permute-start(bf16[8,16,1024]{2,1,0:T(8,128)(2,1)} %get-tuple-element.98), channel_id=1, source_target_pairs={{0,1},{1,0},{2,3},{3,2},{4,5},{5,4},{6,7},{7,6},{8,9},{9,8},{10,11... | collective-permute-start | bytes 786440 | tf_op jit(solution)/shard_map/ppermute | solution.py:422
  45.4 33.3 %copy-start.13 = (bf16[8,16,1024]{2,1,0:T(8,128)(2,1)}, bf16[8,16,1024]{2,1,0:T(8,128)(2,1)S(1)}, u32[]{:S(2)}) copy-start(bf16[8,16,1024]{2,1,0:T(8,128)(2,1)S(1)} %collective-permute-done.2.rest_5_) | copy-start | bytes 786436
  45.4 27.7 %collective-permute-start.7 = (bf16[8,16,1024]{2,1,0:T(8,128)(2,1)}, bf16[8,16,1024]{2,1,0:T(8,128)(2,1)S(1)}, u32[]{:S(2)}, u32[]{:S(2)}) collective-permute-start(bf16[8,16,1024]{2,1,0:T(8,128)(2,1)} %get-tuple-element.101), channel_id=1, source_target_pairs={{0,9},{1,8},{2,11},{3,10},{4,13},{5,12},{6,15},{7,14},{8,1},{9,0},... | collective-permute-start | bytes 786440 | tf_op jit(solution)/shard_map/ppermute | solution.py:422
  48.9 29.8 %copy-start.14 = (bf16[8,16,1024]{2,1,0:T(8,128)(2,1)}, bf16[8,16,1024]{2,1,0:T(8,128)(2,1)S(1)}, u32[]{:S(2)}) copy-start(bf16[8,16,1024]{2,1,0:T(8,128)(2,1)S(1)} %collective-permute-done.3.rest_6_) | copy-start | bytes 786436
  48.9 25.3 %collective-permute-start.8 = (bf16[8,16,1024]{2,1,0:T(8,128)(2,1)}, bf16[8,16,1024]{2,1,0:T(8,128)(2,1)}, u32[]{:S(2)}, u32[]{:S(2)}) collective-permute-start(bf16[8,16,1024]{2,1,0:T(8,128)(2,1)} %get-tuple-element.102), channel_id=1, source_target_pairs={{0,6},{1,7},{2,4},{3,5},{4,2},{5,3},{6,0},{7,1},{8,14},{9,15},{10,... | collective-permute-start | bytes 786440 | tf_op jit(solution)/shard_map/ppermute | solution.py:422
  53.8 25.0 %copy-start.17 = (bf16[8,16,1024]{2,1,0:T(8,128)(2,1)}, bf16[8,16,1024]{2,1,0:T(8,128)(2,1)S(1)}, u32[]{:S(2)}) copy-start(bf16[8,16,1024]{2,1,0:T(8,128)(2,1)S(1)} %collective-permute-done.4.rest_7_) | copy-start | bytes 786436
  53.8 23.4 %collective-permute-start.9 = (bf16[8,16,1024]{2,1,0:T(8,128)(2,1)}, bf16[8,16,1024]{2,1,0:T(8,128)(2,1)}, u32[]{:S(2)}, u32[]{:S(2)}) collective-permute-start(bf16[8,16,1024]{2,1,0:T(8,128)(2,1)} %get-tuple-element.103), channel_id=1, source_target_pairs={{0,13},{1,12},{2,15},{3,14},{4,9},{5,8},{6,11},{7,10},{8,5},{9,4},... | collective-permute-start | bytes 786440 | tf_op jit(solution)/shard_map/ppermute | solution.py:422
  70.7 24.6 %collective-permute-start.10 = (bf16[8,16,1024]{2,1,0:T(8,128)(2,1)S(1)}, bf16[8,16,1024]{2,1,0:T(8,128)(2,1)}, u32[]{:S(2)}, u32[]{:S(2)}) collective-permute-start(bf16[8,16,1024]{2,1,0:T(8,128)(2,1)S(1)} %copy-done.16), channel_id=1, source_target_pairs={{0,7},{1,6},{2,5},{3,4},{4,3},{5,2},{6,1},{7,0},{8,15},{9,14},{10,... | collective-permute-start | bytes 786440 | tf_op jit(solution)/shard_map/ppermute | solution.py:422
  71.0 27.4 %collective-permute-start.11 = (bf16[8,16,1024]{2,1,0:T(8,128)(2,1)S(1)}, bf16[8,16,1024]{2,1,0:T(8,128)(2,1)}, u32[]{:S(2)}, u32[]{:S(2)}) collective-permute-start(bf16[8,16,1024]{2,1,0:T(8,128)(2,1)S(1)} %copy-done.15), channel_id=1, source_target_pairs={{0,10},{1,11},{2,8},{3,9},{4,14},{5,15},{6,12},{7,13},{8,2},{9,3},... | collective-permute-start | bytes 786440 | tf_op jit(solution)/shard_map/ppermute | solution.py:422
  73.1 28.6 %collective-permute-start.12 = (bf16[8,16,1024]{2,1,0:T(8,128)(2,1)S(1)}, bf16[8,16,1024]{2,1,0:T(8,128)(2,1)}, u32[]{:S(2)}, u32[]{:S(2)}) collective-permute-start(bf16[8,16,1024]{2,1,0:T(8,128)(2,1)S(1)} %copy-done.12), channel_id=1, source_target_pairs={{0,2},{1,3},{2,0},{3,1},{4,6},{5,7},{6,4},{7,5},{8,10},{9,11},{10,... | collective-permute-start | bytes 786440 | tf_op jit(solution)/shard_map/ppermute | solution.py:422
  74.2 39.0 %collective-permute-start.13 = (bf16[8,16,1024]{2,1,0:T(8,128)(2,1)S(1)}, bf16[8,16,1024]{2,1,0:T(8,128)(2,1)}, u32[]{:S(2)}, u32[]{:S(2)}) collective-permute-start(bf16[8,16,1024]{2,1,0:T(8,128)(2,1)S(1)} %copy-done.11), channel_id=1, source_target_pairs={{0,14},{1,15},{2,12},{3,13},{4,10},{5,11},{6,8},{7,9},{8,6},{9,7},... | collective-permute-start | bytes 786440 | tf_op jit(solution)/shard_map/ppermute | solution.py:422
  77.2 36.1 %collective-permute-start.14 = (bf16[8,16,1024]{2,1,0:T(8,128)(2,1)S(1)}, bf16[8,16,1024]{2,1,0:T(8,128)(2,1)}, u32[]{:S(2)}, u32[]{:S(2)}) collective-permute-start(bf16[8,16,1024]{2,1,0:T(8,128)(2,1)S(1)} %copy-done.10), channel_id=1, source_target_pairs={{0,3},{1,2},{2,1},{3,0},{4,7},{5,6},{6,5},{7,4},{8,11},{9,10},{10,... | collective-permute-start | bytes 786440 | tf_op jit(solution)/shard_map/ppermute | solution.py:422
  95.4 37.3 %collective-permute-start.15 = (bf16[8,16,1024]{2,1,0:T(8,128)(2,1)S(1)}, bf16[8,16,1024]{2,1,0:T(8,128)(2,1)S(1)}, u32[]{:S(2)}, u32[]{:S(2)}) collective-permute-start(bf16[8,16,1024]{2,1,0:T(8,128)(2,1)S(1)} %copy-done.9), channel_id=1, source_target_pairs={{0,11},{1,10},{2,9},{3,8},{4,15},{5,14},{6,13},{7,12},{8,3},{9,2},... | collective-permute-start | bytes 786440 | tf_op jit(solution)/shard_map/ppermute | solution.py:422
  98.5 34.2 %collective-permute-start.16 = (bf16[8,16,1024]{2,1,0:T(8,128)(2,1)S(1)}, bf16[8,16,1024]{2,1,0:T(8,128)(2,1)S(1)}, u32[]{:S(2)}, u32[]{:S(2)}) collective-permute-start(bf16[8,16,1024]{2,1,0:T(8,128)(2,1)S(1)} %copy-done.8), channel_id=1, source_target_pairs={{0,15},{1,14},{2,13},{3,12},{4,11},{5,10},{6,9},{7,8},{8,7},{9,6},... | collective-permute-start | bytes 786440 | tf_op jit(solution)/shard_map/ppermute | solution.py:422
  (16 other events, 149.9 us)

commit v18 on v17

--- a/solution.py
+++ b/solution.py
@@ -158,14 +158,14 @@
 
 
 def attend_kernel(first, last, sources, place, tiles, *rest):
-    sel_ref, position, query_ref, *rest = rest
+    sel_ref, position_ref, query_ref, *rest = rest
     if first:
         fresh_ref, *rest = rest
     state_in = () if first else rest[:2]
     rest = rest if first else rest[2:]
     contexts, rest = rest[:sources], rest[sources:]
     outs, rest = (rest[:1], rest[1:]) if last else (rest[:2], rest[2:])
-    kv, values, query, scores, raised, mixed, stats, sem = rest
+    kv, values, position, query, scores, raised, mixed, stats, sem = rest
     pages, page_len, width = kv.shape
     each = contexts[0].shape[0]
     direct = last and not first
@@ -198,6 +198,10 @@
             used = sources * each + count
             if pages > used:
                 kv[used:] = jnp.zeros((pages - used, page_len, width), bf16)
+        for c in range(position_ref.shape[1] // LANES):
+            part = slice(c * LANES, (c + 1) * LANES)
+            row = jnp.broadcast_to(position_ref[:, part], (LANES, LANES)).astype(f32)
+            position[part, :] = row.T.astype(jnp.int32)
         if not direct:
             arrived = kv.at[0 : sources * each]
             pltpu.make_async_copy(arrived, arrived, sem).wait()
@@ -284,7 +288,7 @@
     place, tiles, position = order
     picked, features = queries.shape
     each, page_len, width = contexts[0].shape
-    pages = position.shape[0] // page_len
+    pages = position.shape[1] // page_len
     steps = picked // QUERY_BLOCK
     lanes = QUERY_GROUP * QUERY_BLOCK
     wide = pl.BlockSpec((QUERY_BLOCK, features), lambda b, *_: (b, 0))
@@ -320,6 +324,7 @@
                 pltpu.VMEM(
                     (pages // TILE_PAGES, KEY_VALUE_HEADS, LANES, TILE_PAGES * page_len), jnp.bfloat16
                 ),
+                pltpu.VMEM((pages * page_len, LANES), jnp.int32),
                 pltpu.VMEM((KEY_VALUE_HEADS, lanes, LANES), jnp.bfloat16),
                 pltpu.VMEM((KEY_VALUE_HEADS, TILE_PAGES * page_len, lanes), jnp.float32),
                 pltpu.VMEM((KEY_VALUE_HEADS, TILE_PAGES * page_len, lanes), jnp.bfloat16),
@@ -389,8 +394,7 @@
             rows = rows + jnp.sum(jnp.where(there[:, :, None], fresh, 0), axis=1)
             filled = filled | jnp.any(there, axis=1, keepdims=True)
             places = jnp.concatenate([places, fresh_place])
-        rows = jnp.where(filled, rows, FAR_POSITION).reshape(-1, 1)
-        rows = jnp.broadcast_to(rows, (rows.shape[0], LANES))
+        rows = jnp.where(filled, rows, FAR_POSITION).reshape(1, -1)
         orders.append((places, (seen + TILE_PAGES - 1) // TILE_PAGES, rows))
     return orders
 
@@ -491,7 +495,8 @@
     if others:
         parts = dict(zip(others, parts))
         for d in others:
-            arrived[d] = swap(parts[d], d) if d else parts[d]
+            if d not in groups[2]:
+                arrived[d] = swap(parts[d], d) if d else parts[d]
     else:
         arrived[None] = exchange(parts[0]).reshape(pages, page_len, width)
     rows_in = exchange(packed)
@@ -519,7 +524,7 @@
 
     orders = page_order(table[0], positions[0], own, hold, capacity, groups, page_len)
     sel_lanes = jnp.tile(positions.reshape(-1, 1, QUERY_BLOCK), (1, 1, LANES // QUERY_BLOCK))
-    store_out, sel_lanes, orders = lax.optimization_barrier((store_out, sel_lanes, orders))
+    store_out, sel_lanes = lax.optimization_barrier((store_out, sel_lanes))
     state = ()
     for at, (group, order) in enumerate(zip(groups, orders)):
         state = attend(
@@ -532,6 +537,11 @@
             state,
             [arrived[d] for d in group or [None]],
         )
+        if at == 0 and others:
+            middle = [arrived[d] for d in groups[1]]
+            late, state, _ = lax.optimization_barrier(([parts[d] for d in groups[2]], state, middle))
+            for d, part in zip(groups[2], late):
+                arrived[d] = swap(part, d)
     return (state[0][None], store_out)
 
 

time: 144 us -> 144 us (level)
  starting transfers between devices: 38.4 us -> 41 us
  waiting for transfers between devices: 22.7 us -> 20.3 us
    broadcast_in_dim x3 -> x0, local copies, waits for them, and re-layouts: 2.73 us -> none  [page_order(): rows = jnp.broadcast_to(rows, (rows.shape[0], LANES))]
    ppermute x17, starting transfers between devices: 24.5 us -> 27.1 us  [swap(): return lax.ppermute(x, 'store', [(h, h ^ d) for h in range(holders)])]
    ppermute x17, waiting for transfers between devices: 22.2 us -> 19.8 us  [swap(): return lax.ppermute(x, 'store', [(h, h ^ d) for h in range(holders)])]
    select_n x3, local copies, waits for them, and re-layouts: 0.23 us -> 2.03 us  [page_order(): rows = jnp.where(filled, rows, FAR_POSITION).reshape(1, -1)]
    unnamed x44 -> x48, local copies, waits for them, and re-layouts: 2.99 us -> 2.93 us
where the time goes in v18:
time: 144 us; the launch traced here: 142 us
  Pallas kernels  64.7 us (45%)
  starting transfers between devices  41 us (28%)
  waiting for transfers between devices  20.3 us (14%)
  other arithmetic  9.06 us (6%)
  local copies, waits for them, and re-layouts  6.48 us (4%)
    pallas_call x3, Pallas kernels, attend(): pl.pallas_call(functools.partial(attend_kernel, first, last, len(contexts...  45.2 us
    ppermute x17, starting transfers between devices, swap(): return lax.ppermute(x, 'store', [(h, h ^ d) for h in range(holders)])  27.1 us
    ppermute x17, waiting for transfers between devices, swap(): return lax.ppermute(x, 'store', [(h, h ^ d) for h in range(holders)])  19.8 us
    all_to_all x2, starting transfers between devices, exchange(): return lax.all_to_all(x, 'store', split_axis=0, concat_axis=0, tiled=True)  13.9 us
    pallas_call x1, Pallas kernels, per_device(): pl.pallas_call(write_back_kernel, grid_spec=pltpu.PrefetchScalarGridSpec(...  8.02 us
    pallas_call x1, Pallas kernels, per_device(): pl.pallas_call(functools.partial(gather_kernel, capacity, others), grid_s...  4.9 us
    unnamed x48, local copies, waits for them, and re-layouts  2.93 us
  transfers between devices with their start and end apart: 19, of which 7 were waited for; matrix products, arithmetic and copies ran while one was open for 9% of the time, Pallas kernels for 36%

profile of v18, /device:TPU:9, one launch (start us, length us, event | category | flops | bytes accessed | tf_op | source)
XLA Modules:
  0.0 142.5 jit_solution(2636553142981253150)
XLA Ops:
  0.6 1.7 %shard_map.68 = (s32[16,2,128]{2,1,0:T(2,128)}, s32[1,2,128]{2,1,0:T(2,128)}, s32[1,2,128]{2,1,0:T(2,128)}) custom-call(s32[1]{0:T(128)} %bitcast.own, s32[1,128]{1,0:T(1,128)} %table_ref.2, s32[1,160]{1,0:T(1,128)} %sel_ref.2), custom_call_target="tpu_custom_call" | custom-call | tf_op jit(solution)/shard_map/pallas_call | solution.py:431
  2.3 2.3 %collective-permute-start = (s32[1,2,128]{2,1,0:T(2,128)}, s32[1,2,128]{2,1,0:T(2,128)S(1)}, u32[]{:S(2)}, u32[]{:S(2)}) collective-permute-start(s32[1,2,128]{2,1,0:T(2,128)} %get-tuple-element.53), channel_id=1, source_target_pairs={{0,8},{1,9},{2,10},{3,11},{4,12},{5,13},{6,14},{7,15},{8,0},{9,1},... | collective-permute-start | bytes 3080 | tf_op jit(solution)/shard_map/ppermute | solution.py:426
  7.8 2.5 %shard_map.69 = (bf16[8,16,1024]{2,1,0:T(8,128)(2,1)}, bf16[8,16,1024]{2,1,0:T(8,128)(2,1)}) custom-call(s32[1,2,128]{2,1,0:T(2,128)} %copy-done.6, s32[1,2,128]{2,1,0:T(2,128)} %copy-done.7, bf16[128,16,1024]{2,1,0:T(8,128)(2,1)} %store_hbm.3), custom_call_target="tpu_custom_call" | custom-call | tf_op jit(solution)/shard_map/pallas_call | solution.py:449
  10.4 7.5 %all-to-all-start = ((s32[16,2,128]{2,1,0:T(2,128)}), s32[16,2,128]{2,1,0:T(2,128)S(1)}, u32[]{:S(2)}, u32[]{:S(2)}) async-start(s32[16,2,128]{2,1,0:T(2,128)} %get-tuple-element.58), calls=%async_computation | async-start | bytes 32768 | tf_op jit(solution)/shard_map/all_to_all | solution.py:429
  17.9 2.2 %collective-permute-start.2 = (bf16[8,16,1024]{2,1,0:T(8,128)(2,1)}, bf16[8,16,1024]{2,1,0:T(8,128)(2,1)S(1)}, u32[]{:S(2)}, u32[]{:S(2)}) collective-permute-start(bf16[8,16,1024]{2,1,0:T(8,128)(2,1)} %get-tuple-element.82), channel_id=1, source_target_pairs={{0,8},{1,9},{2,10},{3,11},{4,12},{5,13},{6,14},{7,15},{8,0},{9,1},... | collective-permute-start | bytes 786440 | tf_op jit(solution)/shard_map/ppermute | solution.py:426
  20.1 2.4 %shard_map.71 = bf16[16,16,1024]{2,1,0:T(8,128)(2,1)} custom-call(s32[1,128]{1,0:T(1,128)} %table_ref.2, s32[1,160]{1,0:T(1,128)} %sel_ref.2, bf16[160,1024]{1,0:T(8,128)(2,1)} %bitcast.74), custom_call_target="tpu_custom_call" | custom-call | tf_op jit(solution)/shard_map/pallas_call | solution.py:473
  23.5 4.9 %shard_map.70 = (bf16[8,16,1024]{2,1,0:T(8,128)(2,1)}, bf16[8,16,1024]{2,1,0:T(8,128)(2,1)}, bf16[8,16,1024]{2,1,0:T(8,128)(2,1)}, bf16[8,16,1024]{2,1,0:T(8,128...) custom-call(s32[1]{0:T(128)} %bitcast.own, ...), custom_call_target="tpu_custom_call" | custom-call | tf_op jit(solution)/shard_map/pallas_call | solution.py:482
  33.0 6.4 %all-to-all-start.1 = ((bf16[16,16,1024]{2,1,0:T(8,128)(2,1)}), bf16[16,16,1024]{2,1,0:T(8,128)(2,1)S(1)}, u32[]{:S(2)}, u32[]{:S(2)}) async-start(bf16[16,16,1024]{2,1,0:T(8,128)(2,1)} %shard_map.71), calls=%async_computation.1 | async-start | bytes 1048576 | tf_op jit(solution)/shard_map/all_to_all | solution.py:429
  40.8 2.2 %select_reduce_fusion = (s32[64,16]{1,0:T(8,128)S(1)}, s32[64,16]{1,0:T(8,128)S(1)}) fusion(s32[128,16]{0,1:T(8,128)S(1)} %broadcast_select_fusion.2, pred[64,128]{1,0:T(8,128)(4,1)S(1)} %get-tuple-element.116, pred[64,128]{1,0:T(8,128)(4,1)S(1)} %get-tuple-element.127), kind=kLoop, calls=%fused_computation.1 | loop fusion | flops 522240 | bytes 32768 | tf_op jit(solution)/shard_map/reduce_sum | solution.py:390
  43.9 1.9 %collective-permute-start.5 = (bf16[8,16,1024]{2,1,0:T(8,128)(2,1)}, bf16[8,16,1024]{2,1,0:T(8,128)(2,1)}, u32[]{:S(2)}, u32[]{:S(2)}) collective-permute-start(bf16[8,16,1024]{2,1,0:T(8,128)(2,1)} %get-tuple-element.85), channel_id=1, source_target_pairs={{0,5},{1,4},{2,7},{3,6},{4,1},{5,0},{6,3},{7,2},{8,13},{9,12},{10,... | collective-permute-start | bytes 786440 | tf_op jit(solution)/shard_map/ppermute | solution.py:426
  45.9 2.5 %collective-permute-start.7 = (bf16[8,16,1024]{2,1,0:T(8,128)(2,1)}, bf16[8,16,1024]{2,1,0:T(8,128)(2,1)S(1)}, u32[]{:S(2)}, u32[]{:S(2)}) collective-permute-start(bf16[8,16,1024]{2,1,0:T(8,128)(2,1)} %get-tuple-element.89), channel_id=1, source_target_pairs={{0,9},{1,8},{2,11},{3,10},{4,13},{5,12},{6,15},{7,14},{8,1},{9,0},... | collective-permute-start | bytes 786440 | tf_op jit(solution)/shard_map/ppermute | solution.py:426
  49.7 5.2 %collective-permute-done.4.rest_7_ = bf16[8,16,1024]{2,1,0:T(8,128)(2,1)S(1)} collective-permute-done((bf16[8,16,1024]{2,1,0:T(8,128)(2,1)}, bf16[8,16,1024]{2,1,0:T(8,128)(2,1)S(1)}, u32[]{:S(2)}, u32[]{:S(2)}) %collective-permute-start.4) | collective-permute-done | bytes 262176 | tf_op jit(solution)/shard_map/ppermute | solution.py:426
  54.8 3.3 %collective-permute-start.9 = (bf16[8,16,1024]{2,1,0:T(8,128)(2,1)}, bf16[8,16,1024]{2,1,0:T(8,128)(2,1)S(1)}, u32[]{:S(2)}, u32[]{:S(2)}) collective-permute-start(bf16[8,16,1024]{2,1,0:T(8,128)(2,1)} %get-tuple-element.91), channel_id=1, source_target_pairs={{0,13},{1,12},{2,15},{3,14},{4,9},{5,8},{6,11},{7,10},{8,5},{9,4},... | collective-permute-start | bytes 786440 | tf_op jit(solution)/shard_map/ppermute | solution.py:426
  62.8 8.0 %shard_map.72 = bf16[128,16,1024]{2,1,0:T(8,128)(2,1)} custom-call(s32[16,2,128]{2,1,0:T(2,128)} %copy-done.1, s32[16,2,128]{2,1,0:T(2,128)} %copy-done.1, bf16[128,16,1024]{2,1,0:T(8,128)(2,1)} %store_hbm.3, bf16[16,16,1024]{2,1,0:T(8,128)(2,1)} %copy-done), custom_call_target="tpu_custom_call" | custom-call | bytes 8388608 | tf_op jit(solution)/shard_map/pallas_call | solution.py:504
  70.8 5.6 %collective-permute-start.10 = (bf16[8,16,1024]{2,1,0:T(8,128)(2,1)S(1)}, bf16[8,16,1024]{2,1,0:T(8,128)(2,1)S(1)}, u32[]{:S(2)}, u32[]{:S(2)}) collective-permute-start(bf16[8,16,1024]{2,1,0:T(8,128)(2,1)S(1)} %copy-done.16), channel_id=1, source_target_pairs={{0,7},{1,6},{2,5},{3,4},{4,3},{5,2},{6,1},{7,0},{8,15},{9,14},{10,... | collective-permute-start | bytes 786440 | tf_op jit(solution)/shard_map/ppermute | solution.py:426
  76.4 2.1 %collective-permute-start.11 = (bf16[8,16,1024]{2,1,0:T(8,128)(2,1)S(1)}, bf16[8,16,1024]{2,1,0:T(8,128)(2,1)S(1)}, u32[]{:S(2)}, u32[]{:S(2)}) collective-permute-start(bf16[8,16,1024]{2,1,0:T(8,128)(2,1)S(1)} %copy-done.15), channel_id=1, source_target_pairs={{0,10},{1,11},{2,8},{3,9},{4,14},{5,15},{6,12},{7,13},{8,2},{9,3},... | collective-permute-start | bytes 786440 | tf_op jit(solution)/shard_map/ppermute | solution.py:426
  79.0 2.3 %collective-permute-start.14 = (bf16[8,16,1024]{2,1,0:T(8,128)(2,1)S(1)}, bf16[8,16,1024]{2,1,0:T(8,128)(2,1)}, u32[]{:S(2)}, u32[]{:S(2)}) collective-permute-start(bf16[8,16,1024]{2,1,0:T(8,128)(2,1)S(1)} %copy-done.10), channel_id=1, source_target_pairs={{0,3},{1,2},{2,1},{3,0},{4,7},{5,6},{6,5},{7,4},{8,11},{9,10},{10,... | collective-permute-start | bytes 786440 | tf_op jit(solution)/shard_map/ppermute | solution.py:426
  81.3 17.2 %shard_map.73 = (f32[5,4,128,384]{3,2,1,0:T(8,128)}, f32[5,8,384]{2,1,0:T(8,128)}) custom-call(s32[58]{0:T(128)} %pad_add_fusion.place, s32[5]{0:T(128)} %and_select_fusion.tiles, s32[5,1,128]{2,1,0:T(1,128)} %tile.9.rest_0_, s32[1,1024]{1,0:T(1,128)} %select_n.223.rest_1_, bf16[160,6144]{1,0:T(8,128)(2,1)} %bitcast.70, bf16[160,1024]{1,0:T(8,128)(2,1)} %bitcast.75, ...), custom_call_target="tpu_custom_call" | custom-call | flops 4831838208 | bytes 7995392 | tf_op jit(solution)/shard_map/pallas_call | solution.py:304
  98.6 4.3 %collective-permute-done.13.rest_11_ = bf16[8,16,1024]{2,1,0:T(8,128)(2,1)} collective-permute-done((bf16[8,16,1024]{2,1,0:T(8,128)(2,1)S(1)}, bf16[8,16,1024]{2,1,0:T(8,128)(2,1)}, u32[]{:S(2)}, u32[]{:S(2)}) %collective-permute-start.13) | collective-permute-done | bytes 262176 | tf_op jit(solution)/shard_map/ppermute | solution.py:426
  102.9 3.9 %collective-permute-done.14.rest_12_ = bf16[8,16,1024]{2,1,0:T(8,128)(2,1)} collective-permute-done((bf16[8,16,1024]{2,1,0:T(8,128)(2,1)S(1)}, bf16[8,16,1024]{2,1,0:T(8,128)(2,1)}, u32[]{:S(2)}, u32[]{:S(2)}) %collective-permute-start.14) | collective-permute-done | bytes 262176 | tf_op jit(solution)/shard_map/ppermute | solution.py:426
  106.8 2.2 %collective-permute-start.15 = (bf16[8,16,1024]{2,1,0:T(8,128)(2,1)S(1)}, bf16[8,16,1024]{2,1,0:T(8,128)(2,1)S(1)}, u32[]{:S(2)}, u32[]{:S(2)}) collective-permute-start(bf16[8,16,1024]{2,1,0:T(8,128)(2,1)S(1)} %copy-done.9), channel_id=1, source_target_pairs={{0,11},{1,10},{2,9},{3,8},{4,15},{5,14},{6,13},{7,12},{8,3},{9,2},... | collective-permute-start | bytes 786440 | tf_op jit(solution)/shard_map/ppermute | solution.py:426
  109.9 18.2 %shard_map.74 = (f32[5,4,128,384]{3,2,1,0:T(8,128)}, f32[5,8,384]{2,1,0:T(8,128)}) custom-call(s32[64]{0:T(128)} %select_reduce_fusion.4.place, s32[5]{0:T(128)} %and_select_fusion.1.tiles, s32[5,1,128]{2,1,0:T(1,128)} %tile.9.rest_0_, s32[1,1024]{1,0:T(1,128)} %select_n.211.rest_1_, bf16[160,6144]{1,0:T(8,128)(2,1)} %bitcast.71, ...), custom_call_target="tpu_custom_call" | custom-call | flops 4831838208 | bytes 7995392 | tf_op jit(solution)/shard_map/pallas_call | solution.py:304
  128.1 3.8 %collective-permute-done.16.rest_6_ = bf16[8,16,1024]{2,1,0:T(8,128)(2,1)S(1)} collective-permute-done((bf16[8,16,1024]{2,1,0:T(8,128)(2,1)S(1)}, bf16[8,16,1024]{2,1,0:T(8,128)(2,1)S(1)}, u32[]{:S(2)}, u32[]{:S(2)}) %collective-permute-start.16) | collective-permute-done | bytes 262176 | tf_op jit(solution)/shard_map/ppermute | solution.py:426
  132.7 9.8 %shard_map.75 = bf16[160,6144]{1,0:T(8,128)(2,1)} custom-call(s32[16]{0:T(128)} %select_reduce_fusion.6.place, s32[5]{0:T(128)} %and_select_fusion.2.tiles, s32[5,1,128]{2,1,0:T(1,128)} %tile.9.rest_0_, s32[1,256]{1,0:T(1,128)} %select_n.198.rest_1_, bf16[160,6144]{1,0:T(8,128)(2,1)} %bitcast.72, f32[5,4,128,384]{3,2,1,0:T(8,128)} %get-tuple-element.99.rest_3_, ...), custom_call_target="tpu_custom_call" | custom-call | flops 1207959552 | bytes 6422528 | tf_op jit(solution)/shard_map/pallas_call | solution.py:304
  (115 shorter events, 19.1 us)
Async XLA Ops:
  2.3 3.5 %collective-permute-start = (s32[1,2,128]{2,1,0:T(2,128)}, s32[1,2,128]{2,1,0:T(2,128)S(1)}, u32[]{:S(2)}, u32[]{:S(2)}) collective-permute-start(s32[1,2,128]{2,1,0:T(2,128)} %get-tuple-element.53), channel_id=1, source_target_pairs={{0,8},{1,9},{2,10},{3,11},{4,12},{5,13},{6,14},{7,15},{8,0},{9,1},... | collective-permute-start | bytes 3080 | tf_op jit(solution)/shard_map/ppermute | solution.py:426
  4.6 2.6 %collective-permute-start.1 = (s32[1,2,128]{2,1,0:T(2,128)}, s32[1,2,128]{2,1,0:T(2,128)S(1)}, u32[]{:S(2)}, u32[]{:S(2)}) collective-permute-start(s32[1,2,128]{2,1,0:T(2,128)} %get-tuple-element.54), channel_id=1, source_target_pairs={{0,12},{1,13},{2,14},{3,15},{4,8},{5,9},{6,10},{7,11},{8,4},{9,5},... | collective-permute-start | bytes 3080 | tf_op jit(solution)/shard_map/ppermute | solution.py:426
  10.4 12.6 %all-to-all-start = ((s32[16,2,128]{2,1,0:T(2,128)}), s32[16,2,128]{2,1,0:T(2,128)S(1)}, u32[]{:S(2)}, u32[]{:S(2)}) async-start(s32[16,2,128]{2,1,0:T(2,128)} %get-tuple-element.58), calls=%async_computation | async-start | bytes 32768 | tf_op jit(solution)/shard_map/all_to_all | solution.py:429
  17.9 28.0 %collective-permute-start.2 = (bf16[8,16,1024]{2,1,0:T(8,128)(2,1)}, bf16[8,16,1024]{2,1,0:T(8,128)(2,1)S(1)}, u32[]{:S(2)}, u32[]{:S(2)}) collective-permute-start(bf16[8,16,1024]{2,1,0:T(8,128)(2,1)} %get-tuple-element.82), channel_id=1, source_target_pairs={{0,8},{1,9},{2,10},{3,11},{4,12},{5,13},{6,14},{7,15},{8,0},{9,1},... | collective-permute-start | bytes 786440 | tf_op jit(solution)/shard_map/ppermute | solution.py:426
  20.1 28.4 %collective-permute-start.3 = (bf16[8,16,1024]{2,1,0:T(8,128)(2,1)}, bf16[8,16,1024]{2,1,0:T(8,128)(2,1)S(1)}, u32[]{:S(2)}, u32[]{:S(2)}) collective-permute-start(bf16[8,16,1024]{2,1,0:T(8,128)(2,1)} %get-tuple-element.83), channel_id=1, source_target_pairs={{0,12},{1,13},{2,14},{3,15},{4,8},{5,9},{6,10},{7,11},{8,4},{9,5},... | collective-permute-start | bytes 786440 | tf_op jit(solution)/shard_map/ppermute | solution.py:426
  33.0 29.0 %all-to-all-start.1 = ((bf16[16,16,1024]{2,1,0:T(8,128)(2,1)}), bf16[16,16,1024]{2,1,0:T(8,128)(2,1)S(1)}, u32[]{:S(2)}, u32[]{:S(2)}) async-start(bf16[16,16,1024]{2,1,0:T(8,128)(2,1)} %shard_map.71), calls=%async_computation.1 | async-start | bytes 1048576 | tf_op jit(solution)/shard_map/all_to_all | solution.py:429
  40.2 14.7 %collective-permute-start.4 = (bf16[8,16,1024]{2,1,0:T(8,128)(2,1)}, bf16[8,16,1024]{2,1,0:T(8,128)(2,1)S(1)}, u32[]{:S(2)}, u32[]{:S(2)}) collective-permute-start(bf16[8,16,1024]{2,1,0:T(8,128)(2,1)} %get-tuple-element.84), channel_id=1, source_target_pairs={{0,4},{1,5},{2,6},{3,7},{4,0},{5,1},{6,2},{7,3},{8,12},{9,13},{10,... | collective-permute-start | bytes 786440 | tf_op jit(solution)/shard_map/ppermute | solution.py:426
  43.9 26.9 %collective-permute-start.5 = (bf16[8,16,1024]{2,1,0:T(8,128)(2,1)}, bf16[8,16,1024]{2,1,0:T(8,128)(2,1)}, u32[]{:S(2)}, u32[]{:S(2)}) collective-permute-start(bf16[8,16,1024]{2,1,0:T(8,128)(2,1)} %get-tuple-element.85), channel_id=1, source_target_pairs={{0,5},{1,4},{2,7},{3,6},{4,1},{5,0},{6,3},{7,2},{8,13},{9,12},{10,... | collective-permute-start | bytes 786440 | tf_op jit(solution)/shard_map/ppermute | solution.py:426
  45.8 30.6 %collective-permute-start.6 = (bf16[8,16,1024]{2,1,0:T(8,128)(2,1)}, bf16[8,16,1024]{2,1,0:T(8,128)(2,1)}, u32[]{:S(2)}, u32[]{:S(2)}) collective-permute-start(bf16[8,16,1024]{2,1,0:T(8,128)(2,1)} %get-tuple-element.86), channel_id=1, source_target_pairs={{0,1},{1,0},{2,3},{3,2},{4,5},{5,4},{6,7},{7,6},{8,9},{9,8},{10,11... | collective-permute-start | bytes 786440 | tf_op jit(solution)/shard_map/ppermute | solution.py:426
  45.9 35.4 %copy-start.11 = (bf16[8,16,1024]{2,1,0:T(8,128)(2,1)}, bf16[8,16,1024]{2,1,0:T(8,128)(2,1)S(1)}, u32[]{:S(2)}) copy-start(bf16[8,16,1024]{2,1,0:T(8,128)(2,1)S(1)} %collective-permute-done.2.rest_5_) | copy-start | bytes 786436
  45.9 32.6 %collective-permute-start.7 = (bf16[8,16,1024]{2,1,0:T(8,128)(2,1)}, bf16[8,16,1024]{2,1,0:T(8,128)(2,1)S(1)}, u32[]{:S(2)}, u32[]{:S(2)}) collective-permute-start(bf16[8,16,1024]{2,1,0:T(8,128)(2,1)} %get-tuple-element.89), channel_id=1, source_target_pairs={{0,9},{1,8},{2,11},{3,10},{4,13},{5,12},{6,15},{7,14},{8,1},{9,0},... | collective-permute-start | bytes 786440 | tf_op jit(solution)/shard_map/ppermute | solution.py:426
  48.5 32.8 %copy-start.13 = (bf16[8,16,1024]{2,1,0:T(8,128)(2,1)}, bf16[8,16,1024]{2,1,0:T(8,128)(2,1)S(1)}, u32[]{:S(2)}) copy-start(bf16[8,16,1024]{2,1,0:T(8,128)(2,1)S(1)} %collective-permute-done.3.rest_6_) | copy-start | bytes 786436
  48.5 30.4 %collective-permute-start.8 = (bf16[8,16,1024]{2,1,0:T(8,128)(2,1)}, bf16[8,16,1024]{2,1,0:T(8,128)(2,1)S(1)}, u32[]{:S(2)}, u32[]{:S(2)}) collective-permute-start(bf16[8,16,1024]{2,1,0:T(8,128)(2,1)} %get-tuple-element.90), channel_id=1, source_target_pairs={{0,6},{1,7},{2,4},{3,5},{4,2},{5,3},{6,0},{7,1},{8,14},{9,15},{10,... | collective-permute-start | bytes 786440 | tf_op jit(solution)/shard_map/ppermute | solution.py:426
  54.8 26.5 %copy-start.17 = (bf16[8,16,1024]{2,1,0:T(8,128)(2,1)}, bf16[8,16,1024]{2,1,0:T(8,128)(2,1)S(1)}, u32[]{:S(2)}) copy-start(bf16[8,16,1024]{2,1,0:T(8,128)(2,1)S(1)} %collective-permute-done.4.rest_7_) | copy-start | bytes 786436
  54.8 24.2 %collective-permute-start.9 = (bf16[8,16,1024]{2,1,0:T(8,128)(2,1)}, bf16[8,16,1024]{2,1,0:T(8,128)(2,1)S(1)}, u32[]{:S(2)}, u32[]{:S(2)}) collective-permute-start(bf16[8,16,1024]{2,1,0:T(8,128)(2,1)} %get-tuple-element.91), channel_id=1, source_target_pairs={{0,13},{1,12},{2,15},{3,14},{4,9},{5,8},{6,11},{7,10},{8,5},{9,4},... | collective-permute-start | bytes 786440 | tf_op jit(solution)/shard_map/ppermute | solution.py:426
  70.8 27.7 %collective-permute-start.10 = (bf16[8,16,1024]{2,1,0:T(8,128)(2,1)S(1)}, bf16[8,16,1024]{2,1,0:T(8,128)(2,1)S(1)}, u32[]{:S(2)}, u32[]{:S(2)}) collective-permute-start(bf16[8,16,1024]{2,1,0:T(8,128)(2,1)S(1)} %copy-done.16), channel_id=1, source_target_pairs={{0,7},{1,6},{2,5},{3,4},{4,3},{5,2},{6,1},{7,0},{8,15},{9,14},{10,... | collective-permute-start | bytes 786440 | tf_op jit(solution)/shard_map/ppermute | solution.py:426
  76.4 22.1 %collective-permute-start.11 = (bf16[8,16,1024]{2,1,0:T(8,128)(2,1)S(1)}, bf16[8,16,1024]{2,1,0:T(8,128)(2,1)S(1)}, u32[]{:S(2)}, u32[]{:S(2)}) collective-permute-start(bf16[8,16,1024]{2,1,0:T(8,128)(2,1)S(1)} %copy-done.15), channel_id=1, source_target_pairs={{0,10},{1,11},{2,8},{3,9},{4,14},{5,15},{6,12},{7,13},{8,2},{9,3},... | collective-permute-start | bytes 786440 | tf_op jit(solution)/shard_map/ppermute | solution.py:426
  78.6 20.0 %collective-permute-start.12 = (bf16[8,16,1024]{2,1,0:T(8,128)(2,1)S(1)}, bf16[8,16,1024]{2,1,0:T(8,128)(2,1)}, u32[]{:S(2)}, u32[]{:S(2)}) collective-permute-start(bf16[8,16,1024]{2,1,0:T(8,128)(2,1)S(1)} %copy-done.14), channel_id=1, source_target_pairs={{0,2},{1,3},{2,0},{3,1},{4,6},{5,7},{6,4},{7,5},{8,10},{9,11},{10,... | collective-permute-start | bytes 786440 | tf_op jit(solution)/shard_map/ppermute | solution.py:426
  78.9 24.0 %collective-permute-start.13 = (bf16[8,16,1024]{2,1,0:T(8,128)(2,1)S(1)}, bf16[8,16,1024]{2,1,0:T(8,128)(2,1)}, u32[]{:S(2)}, u32[]{:S(2)}) collective-permute-start(bf16[8,16,1024]{2,1,0:T(8,128)(2,1)S(1)} %copy-done.12), channel_id=1, source_target_pairs={{0,14},{1,15},{2,12},{3,13},{4,10},{5,11},{6,8},{7,9},{8,6},{9,7},... | collective-permute-start | bytes 786440 | tf_op jit(solution)/shard_map/ppermute | solution.py:426
  79.0 27.7 %collective-permute-start.14 = (bf16[8,16,1024]{2,1,0:T(8,128)(2,1)S(1)}, bf16[8,16,1024]{2,1,0:T(8,128)(2,1)}, u32[]{:S(2)}, u32[]{:S(2)}) collective-permute-start(bf16[8,16,1024]{2,1,0:T(8,128)(2,1)S(1)} %copy-done.10), channel_id=1, source_target_pairs={{0,3},{1,2},{2,1},{3,0},{4,7},{5,6},{6,5},{7,4},{8,11},{9,10},{10,... | collective-permute-start | bytes 786440 | tf_op jit(solution)/shard_map/ppermute | solution.py:426
  81.3 25.5 %copy-start.9 = (bf16[8,16,1024]{2,1,0:T(8,128)(2,1)S(1)}, bf16[8,16,1024]{2,1,0:T(8,128)(2,1)}, u32[]{:S(2)}) copy-start(bf16[8,16,1024]{2,1,0:T(8,128)(2,1)} %get-tuple-element.101) | copy-start | bytes 786436
  81.3 27.7 %copy-start.8 = (bf16[8,16,1024]{2,1,0:T(8,128)(2,1)S(1)}, bf16[8,16,1024]{2,1,0:T(8,128)(2,1)}, u32[]{:S(2)}) copy-start(bf16[8,16,1024]{2,1,0:T(8,128)(2,1)} %get-tuple-element.102) | copy-start | bytes 786436
  106.8 21.3 %collective-permute-start.15 = (bf16[8,16,1024]{2,1,0:T(8,128)(2,1)S(1)}, bf16[8,16,1024]{2,1,0:T(8,128)(2,1)S(1)}, u32[]{:S(2)}, u32[]{:S(2)}) collective-permute-start(bf16[8,16,1024]{2,1,0:T(8,128)(2,1)S(1)} %copy-done.9), channel_id=1, source_target_pairs={{0,11},{1,10},{2,9},{3,8},{4,15},{5,14},{6,13},{7,12},{8,3},{9,2},... | collective-permute-start | bytes 786440 | tf_op jit(solution)/shard_map/ppermute | solution.py:426
  109.0 23.0 %collective-permute-start.16 = (bf16[8,16,1024]{2,1,0:T(8,128)(2,1)S(1)}, bf16[8,16,1024]{2,1,0:T(8,128)(2,1)S(1)}, u32[]{:S(2)}, u32[]{:S(2)}) collective-permute-start(bf16[8,16,1024]{2,1,0:T(8,128)(2,1)S(1)} %copy-done.8), channel_id=1, source_target_pairs={{0,15},{1,14},{2,13},{3,12},{4,11},{5,10},{6,9},{7,8},{8,7},{9,6},... | collective-permute-start | bytes 786440 | tf_op jit(solution)/shard_map/ppermute | solution.py:426
  (18 other events, 205.4 us)

commit v19 on v18

--- a/solution.py
+++ b/solution.py
@@ -501,7 +501,11 @@
         arrived[None] = exchange(parts[0]).reshape(pages, page_len, width)
     rows_in = exchange(packed)
 
-    store_out = pl.pallas_call(
+    if others:
+        table, positions, _ = lax.optimization_barrier((table, positions, arrived[8]))
+    orders = page_order(table[0], positions[0], own, hold, capacity, groups, page_len)
+    sel_lanes = jnp.tile(positions.reshape(-1, 1, QUERY_BLOCK), (1, 1, LANES // QUERY_BLOCK))
+    write_back = pl.pallas_call(
         write_back_kernel,
         grid_spec=pltpu.PrefetchScalarGridSpec(
             num_scalar_prefetch=1,
@@ -520,11 +524,7 @@
         out_shape=jax.ShapeDtypeStruct(store.shape, store.dtype),
         compiler_params=params,
         cost_estimate=pl.CostEstimate(flops=0, bytes_accessed=4 * store.size, transcendentals=0),
-    )(index_in, index_in, store, rows_in)
-
-    orders = page_order(table[0], positions[0], own, hold, capacity, groups, page_len)
-    sel_lanes = jnp.tile(positions.reshape(-1, 1, QUERY_BLOCK), (1, 1, LANES // QUERY_BLOCK))
-    store_out, sel_lanes = lax.optimization_barrier((store_out, sel_lanes))
+    )
     state = ()
     for at, (group, order) in enumerate(zip(groups, orders)):
         state = attend(
@@ -537,11 +537,15 @@
             state,
             [arrived[d] for d in group or [None]],
         )
-        if at == 0 and others:
-            middle = [arrived[d] for d in groups[1]]
-            late, state, _ = lax.optimization_barrier(([parts[d] for d in groups[2]], state, middle))
-            for d, part in zip(groups[2], late):
-                arrived[d] = swap(part, d)
+        if at == 0:
+            rows_in, state = lax.optimization_barrier((rows_in, state))
+            store_out = write_back(index_in, index_in, store, rows_in)
+            if others:
+                middle = [arrived[d] for d in groups[1]]
+                late = [parts[d] for d in groups[2]]
+                late, state, store_out, _ = lax.optimization_barrier((late, state, store_out, middle))
+                for d, part in zip(groups[2], late):
+                    arrived[d] = swap(part, d)
     return (state[0][None], store_out)
 
 

time: 144 us -> 154 us (1.069)
  starting transfers between devices: 41 us -> 50.2 us
    ppermute x17, starting transfers between devices: 27.1 us -> 38 us  [swap(): return lax.ppermute(x, 'store', [(h, h ^ d) for h in range(holders)])]
    all_to_all x2, waiting for transfers between devices: 0.49 us -> 9.23 us  [exchange(): return lax.all_to_all(x, 'store', split_axis=0, concat_axis=0, tiled=True)]
    ppermute x17, waiting for transfers between devices: 19.8 us -> 12.4 us  [swap(): return lax.ppermute(x, 'store', [(h, h ^ d) for h in range(holders)])]
    all_to_all x2, starting transfers between devices: 13.9 us -> 12.1 us  [exchange(): return lax.all_to_all(x, 'store', split_axis=0, concat_axis=0, tiled=True)]
  transfers between devices with their start and end apart: 19 -> 19, of which waited for: 7 -> 6; matrix products, arithmetic and copies ran while one was open for 9% -> 8% of each run, Pallas kernels for 36% -> 33%
where the time goes in v19:
time: 154 us; the launch traced here: 152 us
  Pallas kernels  63.8 us (41%)
  starting transfers between devices  50.2 us (33%)
  waiting for transfers between devices  21.6 us (14%)
  other arithmetic  9.02 us (6%)
  local copies, waits for them, and re-layouts  6.46 us (4%)
    pallas_call x3, Pallas kernels, attend(): pl.pallas_call(functools.partial(attend_kernel, first, last, len(contexts...  44.2 us
    ppermute x17, starting transfers between devices, swap(): return lax.ppermute(x, 'store', [(h, h ^ d) for h in range(holders)])  38 us
    ppermute x17, waiting for transfers between devices, swap(): return lax.ppermute(x, 'store', [(h, h ^ d) for h in range(holders)])  12.4 us
    all_to_all x2, starting transfers between devices, exchange(): return lax.all_to_all(x, 'store', split_axis=0, concat_axis=0, tiled=True)  12.1 us
    all_to_all x2, waiting for transfers between devices, exchange(): return lax.all_to_all(x, 'store', split_axis=0, concat_axis=0, tiled=True)  9.23 us
    pallas_call x1, Pallas kernels, per_device(): store_out = write_back(index_in, index_in, store, rows_in)  8.15 us
    pallas_call x1, Pallas kernels, per_device(): pl.pallas_call(functools.partial(gather_kernel, capacity, others), grid_s...  4.89 us
  transfers between devices with their start and end apart: 19, of which 6 were waited for; matrix products, arithmetic and copies ran while one was open for 8% of the time, Pallas kernels for 33%

profile of v19, /device:TPU:9, one launch (start us, length us, event | category | flops | bytes accessed | tf_op | source)
XLA Modules:
  0.0 152.0 jit_solution(2734406355544634520)
XLA Ops:
  0.6 1.7 %shard_map.68 = (s32[16,2,128]{2,1,0:T(2,128)}, s32[1,2,128]{2,1,0:T(2,128)}, s32[1,2,128]{2,1,0:T(2,128)}) custom-call(s32[1]{0:T(128)} %bitcast.own, s32[1,128]{1,0:T(1,128)} %table_ref.2, s32[1,160]{1,0:T(1,128)} %sel_ref.2), custom_call_target="tpu_custom_call" | custom-call | tf_op jit(solution)/shard_map/pallas_call | solution.py:431
  2.3 2.3 %collective-permute-start = (s32[1,2,128]{2,1,0:T(2,128)}, s32[1,2,128]{2,1,0:T(2,128)S(1)}, u32[]{:S(2)}, u32[]{:S(2)}) collective-permute-start(s32[1,2,128]{2,1,0:T(2,128)} %get-tuple-element.57), channel_id=1, source_target_pairs={{0,8},{1,9},{2,10},{3,11},{4,12},{5,13},{6,14},{7,15},{8,0},{9,1},... | collective-permute-start | bytes 3080 | tf_op jit(solution)/shard_map/ppermute | solution.py:426
  7.8 2.6 %shard_map.69 = (bf16[8,16,1024]{2,1,0:T(8,128)(2,1)}, bf16[8,16,1024]{2,1,0:T(8,128)(2,1)}) custom-call(s32[1,2,128]{2,1,0:T(2,128)} %copy-done.6, s32[1,2,128]{2,1,0:T(2,128)} %copy-done.7, bf16[128,16,1024]{2,1,0:T(8,128)(2,1)} %store_hbm.3), custom_call_target="tpu_custom_call" | custom-call | tf_op jit(solution)/shard_map/pallas_call | solution.py:449
  10.4 1.9 %collective-permute-start.2 = (bf16[8,16,1024]{2,1,0:T(8,128)(2,1)}, bf16[8,16,1024]{2,1,0:T(8,128)(2,1)S(1)}, u32[]{:S(2)}, u32[]{:S(2)}) collective-permute-start(bf16[8,16,1024]{2,1,0:T(8,128)(2,1)} %get-tuple-element.81), channel_id=1, source_target_pairs={{0,8},{1,9},{2,10},{3,11},{4,12},{5,13},{6,14},{7,15},{8,0},{9,1},... | collective-permute-start | bytes 786440 | tf_op jit(solution)/shard_map/ppermute | solution.py:426
  12.3 7.3 %all-to-all-start = ((s32[16,2,128]{2,1,0:T(2,128)}), s32[16,2,128]{2,1,0:T(2,128)S(1)}, u32[]{:S(2)}, u32[]{:S(2)}) async-start(s32[16,2,128]{2,1,0:T(2,128)} %get-tuple-element.62), calls=%async_computation | async-start | bytes 32768 | tf_op jit(solution)/shard_map/all_to_all | solution.py:429
  20.8 2.4 %shard_map.71 = bf16[16,16,1024]{2,1,0:T(8,128)(2,1)} custom-call(s32[1,128]{1,0:T(1,128)} %table_ref.2, s32[1,160]{1,0:T(1,128)} %sel_ref.2, bf16[160,1024]{1,0:T(8,128)(2,1)} %bitcast.74), custom_call_target="tpu_custom_call" | custom-call | tf_op jit(solution)/shard_map/pallas_call | solution.py:473
  23.2 9.2 %all-to-all-done.index.targets_ref = s32[16,2,128]{2,1,0:T(2,128)S(1)} async-done(((s32[16,2,128]{2,1,0:T(2,128)}), s32[16,2,128]{2,1,0:T(2,128)S(1)}, u32[]{:S(2)}, u32[]{:S(2)}) %all-to-all-start) | async-done | bytes 16416 | tf_op jit(solution)/shard_map/all_to_all | solution.py:429
  33.0 4.9 %shard_map.70 = (bf16[8,16,1024]{2,1,0:T(8,128)(2,1)}, bf16[8,16,1024]{2,1,0:T(8,128)(2,1)}, bf16[8,16,1024]{2,1,0:T(8,128)(2,1)}, bf16[8,16,1024]{2,1,0:T(8,128...) custom-call(s32[1]{0:T(128)} %bitcast.own, ...), custom_call_target="tpu_custom_call" | custom-call | tf_op jit(solution)/shard_map/pallas_call | solution.py:482
  37.9 4.8 %all-to-all-start.1 = ((bf16[16,16,1024]{2,1,0:T(8,128)(2,1)}), bf16[16,16,1024]{2,1,0:T(8,128)(2,1)S(1)}, u32[]{:S(2)}, u32[]{:S(2)}) async-start(bf16[16,16,1024]{2,1,0:T(8,128)(2,1)} %shard_map.71), calls=%async_computation.1 | async-start | bytes 1048576 | tf_op jit(solution)/shard_map/all_to_all | solution.py:429
  42.8 1.9 %collective-permute-start.5 = (bf16[8,16,1024]{2,1,0:T(8,128)(2,1)}, bf16[8,16,1024]{2,1,0:T(8,128)(2,1)S(1)}, u32[]{:S(2)}, u32[]{:S(2)}) collective-permute-start(bf16[8,16,1024]{2,1,0:T(8,128)(2,1)} %get-tuple-element.90), channel_id=1, source_target_pairs={{0,5},{1,4},{2,7},{3,6},{4,1},{5,0},{6,3},{7,2},{8,13},{9,12},{10,... | collective-permute-start | bytes 786440 | tf_op jit(solution)/shard_map/ppermute | solution.py:426
  44.8 2.5 %collective-permute-start.7 = (bf16[8,16,1024]{2,1,0:T(8,128)(2,1)}, bf16[8,16,1024]{2,1,0:T(8,128)(2,1)S(1)}, u32[]{:S(2)}, u32[]{:S(2)}) collective-permute-start(bf16[8,16,1024]{2,1,0:T(8,128)(2,1)} %get-tuple-element.97), channel_id=1, source_target_pairs={{0,9},{1,8},{2,11},{3,10},{4,13},{5,12},{6,15},{7,14},{8,1},{9,0},... | collective-permute-start | bytes 786440 | tf_op jit(solution)/shard_map/ppermute | solution.py:426
  52.7 2.2 %select_reduce_fusion = (s32[64,16]{1,0:T(8,128)S(1)}, s32[64,16]{1,0:T(8,128)S(1)}) fusion(s32[128,16]{0,1:T(8,128)S(1)} %broadcast_select_fusion.2, pred[64,128]{1,0:T(8,128)(4,1)S(1)} %get-tuple-element.124, pred[64,128]{1,0:T(8,128)(4,1)S(1)} %get-tuple-element.135), kind=kLoop, calls=%fused_computation.1 | loop fusion | flops 522240 | bytes 32768 | tf_op jit(solution)/shard_map/reduce_sum | solution.py:390
  57.5 5.3 %collective-permute-done.4.rest_7_ = bf16[8,16,1024]{2,1,0:T(8,128)(2,1)S(1)} collective-permute-done((bf16[8,16,1024]{2,1,0:T(8,128)(2,1)}, bf16[8,16,1024]{2,1,0:T(8,128)(2,1)S(1)}, u32[]{:S(2)}, u32[]{:S(2)}) %collective-permute-start.4) | collective-permute-done | bytes 262176 | tf_op jit(solution)/shard_map/ppermute | solution.py:426
  62.8 2.4 %collective-permute-start.9 = (bf16[8,16,1024]{2,1,0:T(8,128)(2,1)}, bf16[8,16,1024]{2,1,0:T(8,128)(2,1)S(1)}, u32[]{:S(2)}, u32[]{:S(2)}) collective-permute-start(bf16[8,16,1024]{2,1,0:T(8,128)(2,1)} %get-tuple-element.99), channel_id=1, source_target_pairs={{0,13},{1,12},{2,15},{3,14},{4,9},{5,8},{6,11},{7,10},{8,5},{9,4},... | collective-permute-start | bytes 786440 | tf_op jit(solution)/shard_map/ppermute | solution.py:426
  69.1 3.0 %collective-permute-start.10 = (bf16[8,16,1024]{2,1,0:T(8,128)(2,1)}, bf16[8,16,1024]{2,1,0:T(8,128)(2,1)S(1)}, u32[]{:S(2)}, u32[]{:S(2)}) collective-permute-start(bf16[8,16,1024]{2,1,0:T(8,128)(2,1)} %get-tuple-element.100), channel_id=1, source_target_pairs={{0,7},{1,6},{2,5},{3,4},{4,3},{5,2},{6,1},{7,0},{8,15},{9,14},{10,... | collective-permute-start | bytes 786440 | tf_op jit(solution)/shard_map/ppermute | solution.py:426
  74.0 1.9 %collective-permute-done.8.rest_6_ = bf16[8,16,1024]{2,1,0:T(8,128)(2,1)S(1)} collective-permute-done((bf16[8,16,1024]{2,1,0:T(8,128)(2,1)}, bf16[8,16,1024]{2,1,0:T(8,128)(2,1)S(1)}, u32[]{:S(2)}, u32[]{:S(2)}) %collective-permute-start.8) | collective-permute-done | bytes 262176 | tf_op jit(solution)/shard_map/ppermute | solution.py:426
  75.9 2.2 %collective-permute-start.13 = (bf16[8,16,1024]{2,1,0:T(8,128)(2,1)}, bf16[8,16,1024]{2,1,0:T(8,128)(2,1)}, u32[]{:S(2)}, u32[]{:S(2)}) collective-permute-start(bf16[8,16,1024]{2,1,0:T(8,128)(2,1)} %get-tuple-element.103), channel_id=1, source_target_pairs={{0,14},{1,15},{2,12},{3,13},{4,10},{5,11},{6,8},{7,9},{8,6},{9,7},... | collective-permute-start | bytes 786440 | tf_op jit(solution)/shard_map/ppermute | solution.py:426
  78.1 10.9 %collective-permute-start.14 = (bf16[8,16,1024]{2,1,0:T(8,128)(2,1)}, bf16[8,16,1024]{2,1,0:T(8,128)(2,1)}, u32[]{:S(2)}, u32[]{:S(2)}) collective-permute-start(bf16[8,16,1024]{2,1,0:T(8,128)(2,1)} %get-tuple-element.104), channel_id=1, source_target_pairs={{0,3},{1,2},{2,1},{3,0},{4,7},{5,6},{6,5},{7,4},{8,11},{9,10},{10,... | collective-permute-start | bytes 786440 | tf_op jit(solution)/shard_map/ppermute | solution.py:426
  89.1 17.1 %shard_map.72 = (f32[5,4,128,384]{3,2,1,0:T(8,128)}, f32[5,8,384]{2,1,0:T(8,128)}) custom-call(s32[58]{0:T(128)} %pad_add_fusion.place, s32[5]{0:T(128)} %and_select_fusion.tiles, s32[5,1,128]{2,1,0:T(1,128)} %tile.9.rest_0_, s32[1,1024]{1,0:T(1,128)} %select_n.223.rest_1_, bf16[160,6144]{1,0:T(8,128)(2,1)} %bitcast.70, bf16[160,1024]{1,0:T(8,128)(2,1)} %bitcast.75, ...), custom_call_target="tpu_custom_call" | custom-call | flops 4831838208 | bytes 7995392 | tf_op jit(solution)/shard_map/pallas_call | solution.py:304
  107.0 8.1 %shard_map.73 = bf16[128,16,1024]{2,1,0:T(8,128)(2,1)} custom-call(s32[16,2,128]{2,1,0:T(2,128)} %copy-done.1, s32[16,2,128]{2,1,0:T(2,128)} %copy-done.1, bf16[128,16,1024]{2,1,0:T(8,128)(2,1)} %store_hbm.3, bf16[16,16,1024]{2,1,0:T(8,128)(2,1)} %copy-done), custom_call_target="tpu_custom_call" | custom-call | bytes 8388608 | tf_op jit(solution)/shard_map/pallas_call | solution.py:542
  116.9 4.7 %collective-permute-start.16 = (bf16[8,16,1024]{2,1,0:T(8,128)(2,1)S(1)}, bf16[8,16,1024]{2,1,0:T(8,128)(2,1)S(1)}, u32[]{:S(2)}, u32[]{:S(2)}) collective-permute-start(bf16[8,16,1024]{2,1,0:T(8,128)(2,1)S(1)} %copy-done.8), channel_id=1, source_target_pairs={{0,15},{1,14},{2,13},{3,12},{4,11},{5,10},{6,9},{7,8},{8,7},{9,6},... | collective-permute-start | bytes 786440 | tf_op jit(solution)/shard_map/ppermute | solution.py:426
  121.6 17.3 %shard_map.74 = (f32[5,4,128,384]{3,2,1,0:T(8,128)}, f32[5,8,384]{2,1,0:T(8,128)}) custom-call(s32[64]{0:T(128)} %select_reduce_fusion.4.place, s32[5]{0:T(128)} %and_select_fusion.1.tiles, s32[5,1,128]{2,1,0:T(1,128)} %tile.9.rest_0_, s32[1,1024]{1,0:T(1,128)} %select_n.211.rest_1_, bf16[160,6144]{1,0:T(8,128)(2,1)} %bitcast.71, ...), custom_call_target="tpu_custom_call" | custom-call | flops 4831838208 | bytes 7995392 | tf_op jit(solution)/shard_map/pallas_call | solution.py:304
  138.9 2.5 %collective-permute-done.16.rest_6_ = bf16[8,16,1024]{2,1,0:T(8,128)(2,1)S(1)} collective-permute-done((bf16[8,16,1024]{2,1,0:T(8,128)(2,1)S(1)}, bf16[8,16,1024]{2,1,0:T(8,128)(2,1)S(1)}, u32[]{:S(2)}, u32[]{:S(2)}) %collective-permute-start.16) | collective-permute-done | bytes 262176 | tf_op jit(solution)/shard_map/ppermute | solution.py:426
  142.2 9.8 %shard_map.75 = bf16[160,6144]{1,0:T(8,128)(2,1)} custom-call(s32[16]{0:T(128)} %select_reduce_fusion.6.place, s32[5]{0:T(128)} %and_select_fusion.2.tiles, s32[5,1,128]{2,1,0:T(1,128)} %tile.9.rest_0_, s32[1,256]{1,0:T(1,128)} %select_n.198.rest_1_, bf16[160,6144]{1,0:T(8,128)(2,1)} %bitcast.72, f32[5,4,128,384]{3,2,1,0:T(8,128)} %get-tuple-element.107.rest_3_, ...), custom_call_target="tpu_custom_call" | custom-call | flops 1207959552 | bytes 6422528 | tf_op jit(solution)/shard_map/pallas_call | solution.py:304
  (109 shorter events, 22.0 us)
Async XLA Ops:
  2.3 3.5 %collective-permute-start = (s32[1,2,128]{2,1,0:T(2,128)}, s32[1,2,128]{2,1,0:T(2,128)S(1)}, u32[]{:S(2)}, u32[]{:S(2)}) collective-permute-start(s32[1,2,128]{2,1,0:T(2,128)} %get-tuple-element.57), channel_id=1, source_target_pairs={{0,8},{1,9},{2,10},{3,11},{4,12},{5,13},{6,14},{7,15},{8,0},{9,1},... | collective-permute-start | bytes 3080 | tf_op jit(solution)/shard_map/ppermute | solution.py:426
  4.6 2.6 %collective-permute-start.1 = (s32[1,2,128]{2,1,0:T(2,128)}, s32[1,2,128]{2,1,0:T(2,128)S(1)}, u32[]{:S(2)}, u32[]{:S(2)}) collective-permute-start(s32[1,2,128]{2,1,0:T(2,128)} %get-tuple-element.58), channel_id=1, source_target_pairs={{0,12},{1,13},{2,14},{3,15},{4,8},{5,9},{6,10},{7,11},{8,4},{9,5},... | collective-permute-start | bytes 3080 | tf_op jit(solution)/shard_map/ppermute | solution.py:426
  10.4 36.9 %copy-start.5 = (s32[1,128]{1,0:T(1,128)S(1)}, s32[1,128]{1,0:T(1,128)}, u32[]{:S(2)}) copy-start(s32[1,128]{1,0:T(1,128)} %table_ref.2) | copy-start | bytes 1540
  10.4 37.3 %copy-start.4 = (s32[1,160]{1,0:T(1,128)S(1)}, s32[1,160]{1,0:T(1,128)}, u32[]{:S(2)}) copy-start(s32[1,160]{1,0:T(1,128)} %sel_ref.2) | copy-start | bytes 1924
  10.4 34.4 %collective-permute-start.2 = (bf16[8,16,1024]{2,1,0:T(8,128)(2,1)}, bf16[8,16,1024]{2,1,0:T(8,128)(2,1)S(1)}, u32[]{:S(2)}, u32[]{:S(2)}) collective-permute-start(bf16[8,16,1024]{2,1,0:T(8,128)(2,1)} %get-tuple-element.81), channel_id=1, source_target_pairs={{0,8},{1,9},{2,10},{3,11},{4,12},{5,13},{6,14},{7,15},{8,0},{9,1},... | collective-permute-start | bytes 786440 | tf_op jit(solution)/shard_map/ppermute | solution.py:426
  12.3 20.1 %all-to-all-start = ((s32[16,2,128]{2,1,0:T(2,128)}), s32[16,2,128]{2,1,0:T(2,128)S(1)}, u32[]{:S(2)}, u32[]{:S(2)}) async-start(s32[16,2,128]{2,1,0:T(2,128)} %get-tuple-element.62), calls=%async_computation | async-start | bytes 32768 | tf_op jit(solution)/shard_map/all_to_all | solution.py:429
  19.6 36.7 %collective-permute-start.3 = (bf16[8,16,1024]{2,1,0:T(8,128)(2,1)}, bf16[8,16,1024]{2,1,0:T(8,128)(2,1)S(1)}, u32[]{:S(2)}, u32[]{:S(2)}) collective-permute-start(bf16[8,16,1024]{2,1,0:T(8,128)(2,1)} %get-tuple-element.88), channel_id=1, source_target_pairs={{0,12},{1,13},{2,14},{3,15},{4,8},{5,9},{6,10},{7,11},{8,4},{9,5},... | collective-permute-start | bytes 786440 | tf_op jit(solution)/shard_map/ppermute | solution.py:426
  37.9 68.2 %all-to-all-start.1 = ((bf16[16,16,1024]{2,1,0:T(8,128)(2,1)}), bf16[16,16,1024]{2,1,0:T(8,128)(2,1)S(1)}, u32[]{:S(2)}, u32[]{:S(2)}) async-start(bf16[16,16,1024]{2,1,0:T(8,128)(2,1)} %shard_map.71), calls=%async_computation.1 | async-start | bytes 1048576 | tf_op jit(solution)/shard_map/all_to_all | solution.py:429
  42.8 20.0 %collective-permute-start.4 = (bf16[8,16,1024]{2,1,0:T(8,128)(2,1)}, bf16[8,16,1024]{2,1,0:T(8,128)(2,1)S(1)}, u32[]{:S(2)}, u32[]{:S(2)}) collective-permute-start(bf16[8,16,1024]{2,1,0:T(8,128)(2,1)} %get-tuple-element.89), channel_id=1, source_target_pairs={{0,4},{1,5},{2,6},{3,7},{4,0},{5,1},{6,2},{7,3},{8,12},{9,13},{10,... | collective-permute-start | bytes 786440 | tf_op jit(solution)/shard_map/ppermute | solution.py:426
  42.8 26.2 %collective-permute-start.5 = (bf16[8,16,1024]{2,1,0:T(8,128)(2,1)}, bf16[8,16,1024]{2,1,0:T(8,128)(2,1)S(1)}, u32[]{:S(2)}, u32[]{:S(2)}) collective-permute-start(bf16[8,16,1024]{2,1,0:T(8,128)(2,1)} %get-tuple-element.90), channel_id=1, source_target_pairs={{0,5},{1,4},{2,7},{3,6},{4,1},{5,0},{6,3},{7,2},{8,13},{9,12},{10,... | collective-permute-start | bytes 786440 | tf_op jit(solution)/shard_map/ppermute | solution.py:426
  44.8 27.4 %collective-permute-start.6 = (bf16[8,16,1024]{2,1,0:T(8,128)(2,1)}, bf16[8,16,1024]{2,1,0:T(8,128)(2,1)S(1)}, u32[]{:S(2)}, u32[]{:S(2)}) collective-permute-start(bf16[8,16,1024]{2,1,0:T(8,128)(2,1)} %get-tuple-element.91), channel_id=1, source_target_pairs={{0,1},{1,0},{2,3},{3,2},{4,5},{5,4},{6,7},{7,6},{8,9},{9,8},{10,11... | collective-permute-start | bytes 786440 | tf_op jit(solution)/shard_map/ppermute | solution.py:426
  44.8 44.3 %copy-start.10 = (bf16[8,16,1024]{2,1,0:T(8,128)(2,1)}, bf16[8,16,1024]{2,1,0:T(8,128)(2,1)S(1)}, u32[]{:S(2)}) copy-start(bf16[8,16,1024]{2,1,0:T(8,128)(2,1)S(1)} %collective-permute-done.2.rest_5_) | copy-start | bytes 786436
  44.8 28.3 %collective-permute-start.7 = (bf16[8,16,1024]{2,1,0:T(8,128)(2,1)}, bf16[8,16,1024]{2,1,0:T(8,128)(2,1)S(1)}, u32[]{:S(2)}, u32[]{:S(2)}) collective-permute-start(bf16[8,16,1024]{2,1,0:T(8,128)(2,1)} %get-tuple-element.97), channel_id=1, source_target_pairs={{0,9},{1,8},{2,11},{3,10},{4,13},{5,12},{6,15},{7,14},{8,1},{9,0},... | collective-permute-start | bytes 786440 | tf_op jit(solution)/shard_map/ppermute | solution.py:426
  56.3 32.8 %copy-start.12 = (bf16[8,16,1024]{2,1,0:T(8,128)(2,1)}, bf16[8,16,1024]{2,1,0:T(8,128)(2,1)S(1)}, u32[]{:S(2)}) copy-start(bf16[8,16,1024]{2,1,0:T(8,128)(2,1)S(1)} %collective-permute-done.3.rest_6_) | copy-start | bytes 786436
  56.3 19.6 %collective-permute-start.8 = (bf16[8,16,1024]{2,1,0:T(8,128)(2,1)}, bf16[8,16,1024]{2,1,0:T(8,128)(2,1)S(1)}, u32[]{:S(2)}, u32[]{:S(2)}) collective-permute-start(bf16[8,16,1024]{2,1,0:T(8,128)(2,1)} %get-tuple-element.98), channel_id=1, source_target_pairs={{0,6},{1,7},{2,4},{3,5},{4,2},{5,3},{6,0},{7,1},{8,14},{9,15},{10,... | collective-permute-start | bytes 786440 | tf_op jit(solution)/shard_map/ppermute | solution.py:426
  62.8 15.3 %collective-permute-start.9 = (bf16[8,16,1024]{2,1,0:T(8,128)(2,1)}, bf16[8,16,1024]{2,1,0:T(8,128)(2,1)S(1)}, u32[]{:S(2)}, u32[]{:S(2)}) collective-permute-start(bf16[8,16,1024]{2,1,0:T(8,128)(2,1)} %get-tuple-element.99), channel_id=1, source_target_pairs={{0,13},{1,12},{2,15},{3,14},{4,9},{5,8},{6,11},{7,10},{8,5},{9,4},... | collective-permute-start | bytes 786440 | tf_op jit(solution)/shard_map/ppermute | solution.py:426
  69.1 46.1 %collective-permute-start.10 = (bf16[8,16,1024]{2,1,0:T(8,128)(2,1)}, bf16[8,16,1024]{2,1,0:T(8,128)(2,1)S(1)}, u32[]{:S(2)}, u32[]{:S(2)}) collective-permute-start(bf16[8,16,1024]{2,1,0:T(8,128)(2,1)} %get-tuple-element.100), channel_id=1, source_target_pairs={{0,7},{1,6},{2,5},{3,4},{4,3},{5,2},{6,1},{7,0},{8,15},{9,14},{10,... | collective-permute-start | bytes 786440 | tf_op jit(solution)/shard_map/ppermute | solution.py:426
  72.1 43.0 %collective-permute-start.11 = (bf16[8,16,1024]{2,1,0:T(8,128)(2,1)}, bf16[8,16,1024]{2,1,0:T(8,128)(2,1)S(1)}, u32[]{:S(2)}, u32[]{:S(2)}) collective-permute-start(bf16[8,16,1024]{2,1,0:T(8,128)(2,1)} %get-tuple-element.101), channel_id=1, source_target_pairs={{0,10},{1,11},{2,8},{3,9},{4,14},{5,15},{6,12},{7,13},{8,2},{9,3},... | collective-permute-start | bytes 786440 | tf_op jit(solution)/shard_map/ppermute | solution.py:426
  73.1 33.1 %copy-start.11 = (bf16[8,16,1024]{2,1,0:T(8,128)(2,1)}, bf16[8,16,1024]{2,1,0:T(8,128)(2,1)S(1)}, u32[]{:S(2)}) copy-start(bf16[8,16,1024]{2,1,0:T(8,128)(2,1)S(1)} %collective-permute-done.7.rest_5_) | copy-start | bytes 786436
  73.1 42.1 %collective-permute-start.12 = (bf16[8,16,1024]{2,1,0:T(8,128)(2,1)}, bf16[8,16,1024]{2,1,0:T(8,128)(2,1)}, u32[]{:S(2)}, u32[]{:S(2)}) collective-permute-start(bf16[8,16,1024]{2,1,0:T(8,128)(2,1)} %get-tuple-element.102), channel_id=1, source_target_pairs={{0,2},{1,3},{2,0},{3,1},{4,6},{5,7},{6,4},{7,5},{8,10},{9,11},{10,... | collective-permute-start | bytes 786440 | tf_op jit(solution)/shard_map/ppermute | solution.py:426
  75.9 39.3 %collective-permute-start.13 = (bf16[8,16,1024]{2,1,0:T(8,128)(2,1)}, bf16[8,16,1024]{2,1,0:T(8,128)(2,1)}, u32[]{:S(2)}, u32[]{:S(2)}) collective-permute-start(bf16[8,16,1024]{2,1,0:T(8,128)(2,1)} %get-tuple-element.103), channel_id=1, source_target_pairs={{0,14},{1,15},{2,12},{3,13},{4,10},{5,11},{6,8},{7,9},{8,6},{9,7},... | collective-permute-start | bytes 786440 | tf_op jit(solution)/shard_map/ppermute | solution.py:426
  78.1 37.1 %collective-permute-start.14 = (bf16[8,16,1024]{2,1,0:T(8,128)(2,1)}, bf16[8,16,1024]{2,1,0:T(8,128)(2,1)}, u32[]{:S(2)}, u32[]{:S(2)}) collective-permute-start(bf16[8,16,1024]{2,1,0:T(8,128)(2,1)} %get-tuple-element.104), channel_id=1, source_target_pairs={{0,3},{1,2},{2,1},{3,0},{4,7},{5,6},{6,5},{7,4},{8,11},{9,10},{10,... | collective-permute-start | bytes 786440 | tf_op jit(solution)/shard_map/ppermute | solution.py:426
  115.2 23.7 %collective-permute-start.15 = (bf16[8,16,1024]{2,1,0:T(8,128)(2,1)S(1)}, bf16[8,16,1024]{2,1,0:T(8,128)(2,1)S(1)}, u32[]{:S(2)}, u32[]{:S(2)}) collective-permute-start(bf16[8,16,1024]{2,1,0:T(8,128)(2,1)S(1)} %copy-done.9), channel_id=1, source_target_pairs={{0,11},{1,10},{2,9},{3,8},{4,15},{5,14},{6,13},{7,12},{8,3},{9,2},... | collective-permute-start | bytes 786440 | tf_op jit(solution)/shard_map/ppermute | solution.py:426
  116.9 24.6 %collective-permute-start.16 = (bf16[8,16,1024]{2,1,0:T(8,128)(2,1)S(1)}, bf16[8,16,1024]{2,1,0:T(8,128)(2,1)S(1)}, u32[]{:S(2)}, u32[]{:S(2)}) collective-permute-start(bf16[8,16,1024]{2,1,0:T(8,128)(2,1)S(1)} %copy-done.8), channel_id=1, source_target_pairs={{0,15},{1,14},{2,13},{3,12},{4,11},{5,10},{6,9},{7,8},{8,7},{9,6},... | collective-permute-start | bytes 786440 | tf_op jit(solution)/shard_map/ppermute | solution.py:426
  (15 other events, 159.1 us)

commit v20 on v13

--- a/solution.py
+++ b/solution.py
@@ -171,6 +171,7 @@
     pages, page_len, width = kv.shape
     each = contexts[0].shape[0]
     ahead = FRESH_PAGES if first else 0
+    direct = last and not first
     block = query_ref.shape[0]
     tile = tile_pages * page_len
     lanes = QUERY_GROUP * block
@@ -186,8 +187,12 @@
     @pl.when(step == 0)
     def _():
         for i, context in enumerate(contexts):
-            for k in range(each):
-                pltpu.make_async_copy(context.at[k], kv.at[ahead + place[i * each + k]], sem).start()
+            if direct:
+                kv[i * each : (i + 1) * each] = context[...]
+            else:
+                for k in range(each):
+                    to = kv.at[ahead + place[i * each + k]]
+                    pltpu.make_async_copy(context.at[k], to, sem).start()
         if first:
             picked = fresh_ref.shape[0]
             count = picked // page_len
@@ -212,8 +217,9 @@
             return carry
 
         lax.fori_loop(0, (pages - ahead) // FRESH_PAGES, place_rows, 0)
-        used = kv.at[ahead:]
-        pltpu.make_async_copy(used, used, sem).wait()
+        if not direct:
+            used = kv.at[ahead:]
+            pltpu.make_async_copy(used, used, sem).wait()
 
         def turn(t, carry):
             here = pl.ds(t * tile_pages, tile_pages)
@@ -320,7 +326,12 @@
                 wide,
                 *[pl.BlockSpec(x.shape, lambda b, *_: (0, 0)) for x in fresh if first],
                 *([] if first else state_specs),
-                *[pl.BlockSpec(memory_space=pltpu.HBM)] * len(contexts),
+                *[
+                    pl.BlockSpec(x.shape, lambda b, *_: (0, 0, 0))
+                    if last and not first
+                    else pl.BlockSpec(memory_space=pltpu.HBM)
+                    for x in contexts
+                ],
             ],
             out_specs=[wide] if last else state_specs,
             scratch_shapes=[
@@ -369,6 +380,8 @@
             count = len(group) * capacity
         member = arrival >= 0
         place = jnp.sum((member[None, :] & before).astype(jnp.int32), axis=1)
+        if at == len(groups) - 1 and at > 0:
+            place = arrival
         index = jnp.arange(count)[:, None]
         places = jnp.sum(jnp.where(arrival[None, :] == index, place[None, :], 0), axis=1)
         page = jnp.sum(
@@ -474,14 +487,19 @@
     )(own_word, index_in, store)
     parts, packed, table, positions = lax.optimization_barrier((parts, packed, table, positions))
     if others:
-        for d, part in zip(others, parts):
-            arrived[d] = swap(part, d) if d else part
-        contexts = [[arrived[d] for d in group] for group in groups]
+        parts = dict(zip(others, parts))
+        for d in others:
+            if d not in groups[2]:
+                arrived[d] = swap(parts[d], d) if d else parts[d]
     else:
-        contexts = [[exchange(parts[0]).reshape(pages, page_len, width)]]
+        arrived[None] = [exchange(parts[0]).reshape(pages, page_len, width)]
     rows_in = exchange(packed)
 
-    store_out = pl.pallas_call(
+    tiles = [LATE_TILE_PAGES if at == len(groups) - 1 else TILE_PAGES for at in range(len(groups))]
+    orders = page_order(table[0], positions[0], own, hold, capacity, groups, tiles, page_len)
+    sel_lanes = jnp.tile(positions.reshape(-1, 1, QUERY_BLOCK), (1, 1, LANES // QUERY_BLOCK))
+    sel_rows = jnp.broadcast_to(positions.reshape(picked, 1), (picked, LANES))
+    write_back = pl.pallas_call(
         write_back_kernel,
         grid_spec=pltpu.PrefetchScalarGridSpec(
             num_scalar_prefetch=1,
@@ -500,15 +518,9 @@
         out_shape=jax.ShapeDtypeStruct(store.shape, store.dtype),
         compiler_params=params,
         cost_estimate=pl.CostEstimate(flops=0, bytes_accessed=4 * store.size, transcendentals=0),
-    )(index_in, index_in, store, rows_in)
-
-    tiles = [LATE_TILE_PAGES if at == len(groups) - 1 else TILE_PAGES for at in range(len(groups))]
-    orders = page_order(table[0], positions[0], own, hold, capacity, groups, tiles, page_len)
-    sel_lanes = jnp.tile(positions.reshape(-1, 1, QUERY_BLOCK), (1, 1, LANES // QUERY_BLOCK))
-    sel_rows = jnp.broadcast_to(positions.reshape(picked, 1), (picked, LANES))
-    store_out, sel_lanes = lax.optimization_barrier((store_out, sel_lanes))
+    )
     state = ()
-    for at, (arrays, order) in enumerate(zip(contexts, orders)):
+    for at, (group, order) in enumerate(zip(groups, orders)):
         state = attend(
             at == 0,
             at == len(groups) - 1,
@@ -519,8 +531,17 @@
             queries[0],
             (fresh, sel_rows),
             state,
-            arrays,
+            [arrived[d] for d in group] if group else arrived[None],
         )
+        if at == 0:
+            rows_in, state = lax.optimization_barrier((rows_in, state))
+            store_out = write_back(index_in, index_in, store, rows_in)
+            if others:
+                middle = [arrived[d] for d in groups[1]]
+                late = [parts[d] for d in groups[2]]
+                late, state, store_out, _ = lax.optimization_barrier((late, state, store_out, middle))
+                for d, part in zip(groups[2], late):
+                    arrived[d] = swap(part, d)
     return (state[0][None], store_out)
 
 

time: 139 us -> 147 us (1.058)
  waiting for transfers between devices: 19.6 us -> 25.2 us
    ppermute x17, waiting for transfers between devices: 19 us -> 24.6 us  [swap(): return lax.ppermute(x, 'store', [(h, h ^ d) for h in range(holders)])]
  transfers between devices with their start and end apart: 19 -> 19, of which waited for: 8 -> 10; matrix products, arithmetic and copies ran while one was open for 5% -> 5% of each run, Pallas kernels for 38% -> 37%
where the time goes in v20:
time: 147 us; the launch traced here: 144 us
  Pallas kernels  67.4 us (46%)
  starting transfers between devices  40.4 us (27%)
  waiting for transfers between devices  25.2 us (17%)
  other arithmetic  5.27 us (4%)
  local copies, waits for them, and re-layouts  4.91 us (3%)
    pallas_call x3, Pallas kernels, attend(): pl.pallas_call(functools.partial(attend_kernel, first, last, tile_pages,...  47.8 us
    ppermute x17, starting transfers between devices, swap(): return lax.ppermute(x, 'store', [(h, h ^ d) for h in range(holders)])  26.5 us
    ppermute x17, waiting for transfers between devices, swap(): return lax.ppermute(x, 'store', [(h, h ^ d) for h in range(holders)])  24.6 us
    all_to_all x2, starting transfers between devices, exchange(): return lax.all_to_all(x, 'store', split_axis=0, concat_axis=0, tiled=True)  13.8 us
    pallas_call x1, Pallas kernels, per_device(): store_out = write_back(index_in, index_in, store, rows_in)  8.15 us
    pallas_call x1, Pallas kernels, per_device(): pl.pallas_call(functools.partial(gather_kernel, capacity, others), grid_s...  4.9 us
  transfers between devices with their start and end apart: 19, of which 10 were waited for; matrix products, arithmetic and copies ran while one was open for 5% of the time, Pallas kernels for 37%

profile of v20, /device:TPU:9, one launch (start us, length us, event | category | flops | bytes accessed | tf_op | source)
XLA Modules:
  0.0 144.1 jit_solution(4246410145964098075)
XLA Ops:
  0.6 1.7 %shard_map.68 = (s32[16,2,128]{2,1,0:T(2,128)}, s32[1,2,128]{2,1,0:T(2,128)}, s32[1,2,128]{2,1,0:T(2,128)}) custom-call(s32[1]{0:T(128)} %bitcast.own, s32[1,128]{1,0:T(1,128)} %table_ref.2, s32[1,160]{1,0:T(1,128)} %rest_1_.2), custom_call_target="tpu_custom_call" | custom-call | tf_op jit(solution)/shard_map/pallas_call | solution.py:425
  2.3 2.3 %collective-permute-start = (s32[1,2,128]{2,1,0:T(2,128)}, s32[1,2,128]{2,1,0:T(2,128)S(1)}, u32[]{:S(2)}, u32[]{:S(2)}) collective-permute-start(s32[1,2,128]{2,1,0:T(2,128)} %get-tuple-element.55), channel_id=1, source_target_pairs={{0,8},{1,9},{2,10},{3,11},{4,12},{5,13},{6,14},{7,15},{8,0},{9,1},... | collective-permute-start | bytes 3080 | tf_op jit(solution)/shard_map/ppermute | solution.py:420
  7.8 2.5 %shard_map.69 = (bf16[8,16,1024]{2,1,0:T(8,128)(2,1)}, bf16[8,16,1024]{2,1,0:T(8,128)(2,1)}) custom-call(s32[1,2,128]{2,1,0:T(2,128)} %copy-done.7, s32[1,2,128]{2,1,0:T(2,128)} %copy-done.8, bf16[128,16,1024]{2,1,0:T(8,128)(2,1)} %store_hbm.3), custom_call_target="tpu_custom_call" | custom-call | tf_op jit(solution)/shard_map/pallas_call | solution.py:443
  10.4 7.6 %all-to-all-start = ((s32[16,2,128]{2,1,0:T(2,128)}), s32[16,2,128]{2,1,0:T(2,128)S(1)}, u32[]{:S(2)}, u32[]{:S(2)}) async-start(s32[16,2,128]{2,1,0:T(2,128)} %get-tuple-element.60), calls=%async_computation | async-start | bytes 32768 | tf_op jit(solution)/shard_map/all_to_all | solution.py:423
  17.9 2.1 %collective-permute-start.2 = (bf16[8,16,1024]{2,1,0:T(8,128)(2,1)}, bf16[8,16,1024]{2,1,0:T(8,128)(2,1)S(1)}, u32[]{:S(2)}, u32[]{:S(2)}) collective-permute-start(bf16[8,16,1024]{2,1,0:T(8,128)(2,1)} %get-tuple-element.83), channel_id=1, source_target_pairs={{0,8},{1,9},{2,10},{3,11},{4,12},{5,13},{6,14},{7,15},{8,0},{9,1},... | collective-permute-start | bytes 786440 | tf_op jit(solution)/shard_map/ppermute | solution.py:420
  20.0 2.4 %shard_map.71 = bf16[16,16,1024]{2,1,0:T(8,128)(2,1)} custom-call(s32[1,128]{1,0:T(1,128)} %table_ref.2, s32[1,160]{1,0:T(1,128)} %rest_1_.2, bf16[160,1024]{1,0:T(8,128)(2,1)} %bitcast.70), custom_call_target="tpu_custom_call" | custom-call | tf_op jit(solution)/shard_map/pallas_call | solution.py:467
  23.6 4.9 %shard_map.70 = (bf16[8,16,1024]{2,1,0:T(8,128)(2,1)}, bf16[8,16,1024]{2,1,0:T(8,128)(2,1)}, bf16[8,16,1024]{2,1,0:T(8,128)(2,1)}, bf16[8,16,1024]{2,1,0:T(8,128...) custom-call(s32[1]{0:T(128)} %bitcast.own, ...), custom_call_target="tpu_custom_call" | custom-call | tf_op jit(solution)/shard_map/pallas_call | solution.py:476
  31.7 6.3 %all-to-all-start.1 = ((bf16[16,16,1024]{2,1,0:T(8,128)(2,1)}), bf16[16,16,1024]{2,1,0:T(8,128)(2,1)S(1)}, u32[]{:S(2)}, u32[]{:S(2)}) async-start(bf16[16,16,1024]{2,1,0:T(8,128)(2,1)} %shard_map.71), calls=%async_computation.1 | async-start | bytes 1048576 | tf_op jit(solution)/shard_map/all_to_all | solution.py:423
  38.1 1.9 %collective-permute-start.5 = (bf16[8,16,1024]{2,1,0:T(8,128)(2,1)}, bf16[8,16,1024]{2,1,0:T(8,128)(2,1)S(1)}, u32[]{:S(2)}, u32[]{:S(2)}) collective-permute-start(bf16[8,16,1024]{2,1,0:T(8,128)(2,1)} %get-tuple-element.86), channel_id=1, source_target_pairs={{0,5},{1,4},{2,7},{3,6},{4,1},{5,0},{6,3},{7,2},{8,13},{9,12},{10,... | collective-permute-start | bytes 786440 | tf_op jit(solution)/shard_map/ppermute | solution.py:420
  42.1 2.5 %collective-permute-start.7 = (bf16[8,16,1024]{2,1,0:T(8,128)(2,1)}, bf16[8,16,1024]{2,1,0:T(8,128)(2,1)S(1)}, u32[]{:S(2)}, u32[]{:S(2)}) collective-permute-start(bf16[8,16,1024]{2,1,0:T(8,128)(2,1)} %get-tuple-element.93), channel_id=1, source_target_pairs={{0,9},{1,8},{2,11},{3,10},{4,13},{5,12},{6,15},{7,14},{8,1},{9,0},... | collective-permute-start | bytes 786440 | tf_op jit(solution)/shard_map/ppermute | solution.py:420
  44.5 4.3 %collective-permute-done.3.rest_7_ = bf16[8,16,1024]{2,1,0:T(8,128)(2,1)S(1)} collective-permute-done((bf16[8,16,1024]{2,1,0:T(8,128)(2,1)}, bf16[8,16,1024]{2,1,0:T(8,128)(2,1)S(1)}, u32[]{:S(2)}, u32[]{:S(2)}) %collective-permute-start.3) | collective-permute-done | bytes 262176 | tf_op jit(solution)/shard_map/ppermute | solution.py:420
  48.9 4.6 %collective-permute-done.4.rest_8_ = bf16[8,16,1024]{2,1,0:T(8,128)(2,1)S(1)} collective-permute-done((bf16[8,16,1024]{2,1,0:T(8,128)(2,1)}, bf16[8,16,1024]{2,1,0:T(8,128)(2,1)S(1)}, u32[]{:S(2)}, u32[]{:S(2)}) %collective-permute-start.4) | collective-permute-done | bytes 262176 | tf_op jit(solution)/shard_map/ppermute | solution.py:420
  53.5 3.2 %collective-permute-start.9 = (bf16[8,16,1024]{2,1,0:T(8,128)(2,1)}, bf16[8,16,1024]{2,1,0:T(8,128)(2,1)S(1)}, u32[]{:S(2)}, u32[]{:S(2)}) collective-permute-start(bf16[8,16,1024]{2,1,0:T(8,128)(2,1)} %get-tuple-element.95), channel_id=1, source_target_pairs={{0,13},{1,12},{2,15},{3,14},{4,9},{5,8},{6,11},{7,10},{8,5},{9,4},... | collective-permute-start | bytes 786440 | tf_op jit(solution)/shard_map/ppermute | solution.py:420
  58.2 5.5 %collective-permute-done.5.rest_9_ = bf16[8,16,1024]{2,1,0:T(8,128)(2,1)S(1)} collective-permute-done((bf16[8,16,1024]{2,1,0:T(8,128)(2,1)}, bf16[8,16,1024]{2,1,0:T(8,128)(2,1)S(1)}, u32[]{:S(2)}, u32[]{:S(2)}) %collective-permute-start.5) | collective-permute-done | bytes 262176 | tf_op jit(solution)/shard_map/ppermute | solution.py:420
  63.6 3.3 %collective-permute-start.10 = (bf16[8,16,1024]{2,1,0:T(8,128)(2,1)}, bf16[8,16,1024]{2,1,0:T(8,128)(2,1)S(1)}, u32[]{:S(2)}, u32[]{:S(2)}) collective-permute-start(bf16[8,16,1024]{2,1,0:T(8,128)(2,1)} %get-tuple-element.96), channel_id=1, source_target_pairs={{0,7},{1,6},{2,5},{3,4},{4,3},{5,2},{6,1},{7,0},{8,15},{9,14},{10,... | collective-permute-start | bytes 786440 | tf_op jit(solution)/shard_map/ppermute | solution.py:420
  68.6 2.5 %collective-permute-done.8.rest_6_ = bf16[8,16,1024]{2,1,0:T(8,128)(2,1)S(1)} collective-permute-done((bf16[8,16,1024]{2,1,0:T(8,128)(2,1)}, bf16[8,16,1024]{2,1,0:T(8,128)(2,1)S(1)}, u32[]{:S(2)}, u32[]{:S(2)}) %collective-permute-start.8) | collective-permute-done | bytes 262176 | tf_op jit(solution)/shard_map/ppermute | solution.py:420
  71.1 2.1 %collective-permute-start.13 = (bf16[8,16,1024]{2,1,0:T(8,128)(2,1)}, bf16[8,16,1024]{2,1,0:T(8,128)(2,1)}, u32[]{:S(2)}, u32[]{:S(2)}) collective-permute-start(bf16[8,16,1024]{2,1,0:T(8,128)(2,1)} %get-tuple-element.99), channel_id=1, source_target_pairs={{0,14},{1,15},{2,12},{3,13},{4,10},{5,11},{6,8},{7,9},{8,6},{9,7},... | collective-permute-start | bytes 786440 | tf_op jit(solution)/shard_map/ppermute | solution.py:420
  73.3 3.8 %collective-permute-done.9.rest_7_ = bf16[8,16,1024]{2,1,0:T(8,128)(2,1)S(1)} collective-permute-done((bf16[8,16,1024]{2,1,0:T(8,128)(2,1)}, bf16[8,16,1024]{2,1,0:T(8,128)(2,1)S(1)}, u32[]{:S(2)}, u32[]{:S(2)}) %collective-permute-start.9) | collective-permute-done | bytes 262176 | tf_op jit(solution)/shard_map/ppermute | solution.py:420
  77.1 1.7 %collective-permute-start.14 = (bf16[8,16,1024]{2,1,0:T(8,128)(2,1)}, bf16[8,16,1024]{2,1,0:T(8,128)(2,1)}, u32[]{:S(2)}, u32[]{:S(2)}) collective-permute-start(bf16[8,16,1024]{2,1,0:T(8,128)(2,1)} %get-tuple-element.100), channel_id=1, source_target_pairs={{0,3},{1,2},{2,1},{3,0},{4,7},{5,6},{6,5},{7,4},{8,11},{9,10},{10,... | collective-permute-start | bytes 786440 | tf_op jit(solution)/shard_map/ppermute | solution.py:420
  79.5 19.6 %shard_map.72 = (f32[5,4,128,384]{3,2,1,0:T(8,128)}, f32[5,8,384]{2,1,0:T(8,128)}) custom-call(s32[48]{0:T(128)} %get-tuple-element.109.place, s32[48]{0:T(128)} %copy-done.10, s32[5]{0:T(128)} %and_select_fusion.tiles, s32[5,1,128]{2,1,0:T(1,128)} %tile.9.rest_0_, s32[1,160]{1,0:T(1,128)} %rest_1_.2, bf16[160,6144]{1,0:T(8,128)(2,1)} %bitcast.66, ...), custom_call_target="tpu_custom_call" | custom-call | flops 4831838208 | bytes 7995392 | tf_op jit(solution)/shard_map/pallas_call | solution.py:318
  100.0 8.2 %shard_map.73 = bf16[128,16,1024]{2,1,0:T(8,128)(2,1)} custom-call(s32[16,2,128]{2,1,0:T(2,128)} %copy-done.1, s32[16,2,128]{2,1,0:T(2,128)} %copy-done.1, bf16[128,16,1024]{2,1,0:T(8,128)(2,1)} %store_hbm.3, bf16[16,16,1024]{2,1,0:T(8,128)(2,1)} %copy-done), custom_call_target="tpu_custom_call" | custom-call | bytes 8388608 | tf_op jit(solution)/shard_map/pallas_call | solution.py:538
  109.7 4.7 %collective-permute-start.16 = (bf16[8,16,1024]{2,1,0:T(8,128)(2,1)S(1)}, bf16[8,16,1024]{2,1,0:T(8,128)(2,1)S(1)}, u32[]{:S(2)}, u32[]{:S(2)}) collective-permute-start(bf16[8,16,1024]{2,1,0:T(8,128)(2,1)S(1)} %copy-done.11), channel_id=1, source_target_pairs={{0,15},{1,14},{2,13},{3,12},{4,11},{5,10},{6,9},{7,8},{8,7},{9,6},... | collective-permute-start | bytes 786440 | tf_op jit(solution)/shard_map/ppermute | solution.py:420
  114.4 18.3 %shard_map.74 = (f32[5,4,128,384]{3,2,1,0:T(8,128)}, f32[5,8,384]{2,1,0:T(8,128)}) custom-call(s32[64]{0:T(128)} %get-tuple-element.111.place, s32[64]{0:T(128)} %copy-done.9, s32[5]{0:T(128)} %and_select_fusion.1.tiles, s32[5,1,128]{2,1,0:T(1,128)} %tile.9.rest_0_, s32[1,160]{1,0:T(1,128)} %rest_1_.2, bf16[160,6144]{1,0:T(8,128)(2,1)} %bitcast.67, ...), custom_call_target="tpu_custom_call" | custom-call | flops 4831838208 | bytes 7995392 | tf_op jit(solution)/shard_map/pallas_call | solution.py:318
  134.2 9.9 %shard_map.75 = bf16[160,6144]{1,0:T(8,128)(2,1)} custom-call(s32[16]{0:T(128)} %get-tuple-element.113.place, s32[16]{0:T(128)} %copy-done.6, s32[5]{0:T(128)} %and_select_fusion.2.tiles, s32[5,1,128]{2,1,0:T(1,128)} %tile.9.rest_0_, s32[1,160]{1,0:T(1,128)} %rest_1_.2, bf16[160,6144]{1,0:T(8,128)(2,1)} %bitcast.68, ...), custom_call_target="tpu_custom_call" | custom-call | flops 1207959552 | bytes 6422528 | tf_op jit(solution)/shard_map/pallas_call | solution.py:318
  (93 shorter events, 17.4 us)
Async XLA Ops:
  2.3 3.5 %collective-permute-start = (s32[1,2,128]{2,1,0:T(2,128)}, s32[1,2,128]{2,1,0:T(2,128)S(1)}, u32[]{:S(2)}, u32[]{:S(2)}) collective-permute-start(s32[1,2,128]{2,1,0:T(2,128)} %get-tuple-element.55), channel_id=1, source_target_pairs={{0,8},{1,9},{2,10},{3,11},{4,12},{5,13},{6,14},{7,15},{8,0},{9,1},... | collective-permute-start | bytes 3080 | tf_op jit(solution)/shard_map/ppermute | solution.py:420
  4.6 2.6 %collective-permute-start.1 = (s32[1,2,128]{2,1,0:T(2,128)}, s32[1,2,128]{2,1,0:T(2,128)S(1)}, u32[]{:S(2)}, u32[]{:S(2)}) collective-permute-start(s32[1,2,128]{2,1,0:T(2,128)} %get-tuple-element.56), channel_id=1, source_target_pairs={{0,12},{1,13},{2,14},{3,15},{4,8},{5,9},{6,10},{7,11},{8,4},{9,5},... | collective-permute-start | bytes 3080 | tf_op jit(solution)/shard_map/ppermute | solution.py:420
  10.4 12.6 %all-to-all-start = ((s32[16,2,128]{2,1,0:T(2,128)}), s32[16,2,128]{2,1,0:T(2,128)S(1)}, u32[]{:S(2)}, u32[]{:S(2)}) async-start(s32[16,2,128]{2,1,0:T(2,128)} %get-tuple-element.60), calls=%async_computation | async-start | bytes 32768 | tf_op jit(solution)/shard_map/all_to_all | solution.py:423
  17.9 24.1 %collective-permute-start.2 = (bf16[8,16,1024]{2,1,0:T(8,128)(2,1)}, bf16[8,16,1024]{2,1,0:T(8,128)(2,1)S(1)}, u32[]{:S(2)}, u32[]{:S(2)}) collective-permute-start(bf16[8,16,1024]{2,1,0:T(8,128)(2,1)} %get-tuple-element.83), channel_id=1, source_target_pairs={{0,8},{1,9},{2,10},{3,11},{4,12},{5,13},{6,14},{7,15},{8,0},{9,1},... | collective-permute-start | bytes 786440 | tf_op jit(solution)/shard_map/ppermute | solution.py:420
  20.0 28.8 %collective-permute-start.3 = (bf16[8,16,1024]{2,1,0:T(8,128)(2,1)}, bf16[8,16,1024]{2,1,0:T(8,128)(2,1)S(1)}, u32[]{:S(2)}, u32[]{:S(2)}) collective-permute-start(bf16[8,16,1024]{2,1,0:T(8,128)(2,1)} %get-tuple-element.84), channel_id=1, source_target_pairs={{0,12},{1,13},{2,14},{3,15},{4,8},{5,9},{6,10},{7,11},{8,4},{9,5},... | collective-permute-start | bytes 786440 | tf_op jit(solution)/shard_map/ppermute | solution.py:420
  31.0 48.5 %copy-start.10 = (s32[48]{0:T(128)}, s32[48]{0:T(128)S(1)}, u32[]{:S(2)}) copy-start(s32[48]{0:T(128)S(1)} %get-tuple-element.108.page_number) | copy-start | bytes 580
  31.7 67.5 %all-to-all-start.1 = ((bf16[16,16,1024]{2,1,0:T(8,128)(2,1)}), bf16[16,16,1024]{2,1,0:T(8,128)(2,1)S(1)}, u32[]{:S(2)}, u32[]{:S(2)}) async-start(bf16[16,16,1024]{2,1,0:T(8,128)(2,1)} %shard_map.71), calls=%async_computation.1 | async-start | bytes 1048576 | tf_op jit(solution)/shard_map/all_to_all | solution.py:423
  38.0 15.5 %collective-permute-start.4 = (bf16[8,16,1024]{2,1,0:T(8,128)(2,1)}, bf16[8,16,1024]{2,1,0:T(8,128)(2,1)S(1)}, u32[]{:S(2)}, u32[]{:S(2)}) collective-permute-start(bf16[8,16,1024]{2,1,0:T(8,128)(2,1)} %get-tuple-element.85), channel_id=1, source_target_pairs={{0,4},{1,5},{2,6},{3,7},{4,0},{5,1},{6,2},{7,3},{8,12},{9,13},{10,... | collective-permute-start | bytes 786440 | tf_op jit(solution)/shard_map/ppermute | solution.py:420
  38.1 25.5 %collective-permute-start.5 = (bf16[8,16,1024]{2,1,0:T(8,128)(2,1)}, bf16[8,16,1024]{2,1,0:T(8,128)(2,1)S(1)}, u32[]{:S(2)}, u32[]{:S(2)}) collective-permute-start(bf16[8,16,1024]{2,1,0:T(8,128)(2,1)} %get-tuple-element.86), channel_id=1, source_target_pairs={{0,5},{1,4},{2,7},{3,6},{4,1},{5,0},{6,3},{7,2},{8,13},{9,12},{10,... | collective-permute-start | bytes 786440 | tf_op jit(solution)/shard_map/ppermute | solution.py:420
  40.0 26.9 %collective-permute-start.6 = (bf16[8,16,1024]{2,1,0:T(8,128)(2,1)}, bf16[8,16,1024]{2,1,0:T(8,128)(2,1)S(1)}, u32[]{:S(2)}, u32[]{:S(2)}) collective-permute-start(bf16[8,16,1024]{2,1,0:T(8,128)(2,1)} %get-tuple-element.87), channel_id=1, source_target_pairs={{0,1},{1,0},{2,3},{3,2},{4,5},{5,4},{6,7},{7,6},{8,9},{9,8},{10,11... | collective-permute-start | bytes 786440 | tf_op jit(solution)/shard_map/ppermute | solution.py:420
  40.6 58.5 %copy-start.6 = (s32[16]{0:T(128)}, s32[16]{0:T(128)S(1)}, u32[]{:S(2)}) copy-start(s32[16]{0:T(128)S(1)} %get-tuple-element.112.page_number) | copy-start | bytes 196
  41.3 57.8 %copy-start.9 = (s32[64]{0:T(128)}, s32[64]{0:T(128)S(1)}, u32[]{:S(2)}) copy-start(s32[64]{0:T(128)S(1)} %get-tuple-element.110.page_number) | copy-start | bytes 772
  42.1 37.4 %copy-start.13 = (bf16[8,16,1024]{2,1,0:T(8,128)(2,1)}, bf16[8,16,1024]{2,1,0:T(8,128)(2,1)S(1)}, u32[]{:S(2)}) copy-start(bf16[8,16,1024]{2,1,0:T(8,128)(2,1)S(1)} %collective-permute-done.2.rest_6_) | copy-start | bytes 786436
  42.1 25.3 %collective-permute-start.7 = (bf16[8,16,1024]{2,1,0:T(8,128)(2,1)}, bf16[8,16,1024]{2,1,0:T(8,128)(2,1)S(1)}, u32[]{:S(2)}, u32[]{:S(2)}) collective-permute-start(bf16[8,16,1024]{2,1,0:T(8,128)(2,1)} %get-tuple-element.93), channel_id=1, source_target_pairs={{0,9},{1,8},{2,11},{3,10},{4,13},{5,12},{6,15},{7,14},{8,1},{9,0},... | collective-permute-start | bytes 786440 | tf_op jit(solution)/shard_map/ppermute | solution.py:420
  48.9 22.3 %collective-permute-start.8 = (bf16[8,16,1024]{2,1,0:T(8,128)(2,1)}, bf16[8,16,1024]{2,1,0:T(8,128)(2,1)S(1)}, u32[]{:S(2)}, u32[]{:S(2)}) collective-permute-start(bf16[8,16,1024]{2,1,0:T(8,128)(2,1)} %get-tuple-element.94), channel_id=1, source_target_pairs={{0,6},{1,7},{2,4},{3,5},{4,2},{5,3},{6,0},{7,1},{8,14},{9,15},{10,... | collective-permute-start | bytes 786440 | tf_op jit(solution)/shard_map/ppermute | solution.py:420
  53.5 23.6 %collective-permute-start.9 = (bf16[8,16,1024]{2,1,0:T(8,128)(2,1)}, bf16[8,16,1024]{2,1,0:T(8,128)(2,1)S(1)}, u32[]{:S(2)}, u32[]{:S(2)}) collective-permute-start(bf16[8,16,1024]{2,1,0:T(8,128)(2,1)} %get-tuple-element.95), channel_id=1, source_target_pairs={{0,13},{1,12},{2,15},{3,14},{4,9},{5,8},{6,11},{7,10},{8,5},{9,4},... | collective-permute-start | bytes 786440 | tf_op jit(solution)/shard_map/ppermute | solution.py:420
  63.6 44.5 %collective-permute-start.10 = (bf16[8,16,1024]{2,1,0:T(8,128)(2,1)}, bf16[8,16,1024]{2,1,0:T(8,128)(2,1)S(1)}, u32[]{:S(2)}, u32[]{:S(2)}) collective-permute-start(bf16[8,16,1024]{2,1,0:T(8,128)(2,1)} %get-tuple-element.96), channel_id=1, source_target_pairs={{0,7},{1,6},{2,5},{3,4},{4,3},{5,2},{6,1},{7,0},{8,15},{9,14},{10,... | collective-permute-start | bytes 786440 | tf_op jit(solution)/shard_map/ppermute | solution.py:420
  66.9 41.3 %collective-permute-start.11 = (bf16[8,16,1024]{2,1,0:T(8,128)(2,1)}, bf16[8,16,1024]{2,1,0:T(8,128)(2,1)S(1)}, u32[]{:S(2)}, u32[]{:S(2)}) collective-permute-start(bf16[8,16,1024]{2,1,0:T(8,128)(2,1)} %get-tuple-element.97), channel_id=1, source_target_pairs={{0,10},{1,11},{2,8},{3,9},{4,14},{5,15},{6,12},{7,13},{8,2},{9,3},... | collective-permute-start | bytes 786440 | tf_op jit(solution)/shard_map/ppermute | solution.py:420
  67.4 31.7 %copy-start.15 = (bf16[8,16,1024]{2,1,0:T(8,128)(2,1)}, bf16[8,16,1024]{2,1,0:T(8,128)(2,1)S(1)}, u32[]{:S(2)}) copy-start(bf16[8,16,1024]{2,1,0:T(8,128)(2,1)S(1)} %collective-permute-done.7.rest_5_) | copy-start | bytes 786436
  67.4 40.8 %collective-permute-start.12 = (bf16[8,16,1024]{2,1,0:T(8,128)(2,1)}, bf16[8,16,1024]{2,1,0:T(8,128)(2,1)S(1)}, u32[]{:S(2)}, u32[]{:S(2)}) collective-permute-start(bf16[8,16,1024]{2,1,0:T(8,128)(2,1)} %get-tuple-element.98), channel_id=1, source_target_pairs={{0,2},{1,3},{2,0},{3,1},{4,6},{5,7},{6,4},{7,5},{8,10},{9,11},{10,... | collective-permute-start | bytes 786440 | tf_op jit(solution)/shard_map/ppermute | solution.py:420
  71.1 37.1 %collective-permute-start.13 = (bf16[8,16,1024]{2,1,0:T(8,128)(2,1)}, bf16[8,16,1024]{2,1,0:T(8,128)(2,1)}, u32[]{:S(2)}, u32[]{:S(2)}) collective-permute-start(bf16[8,16,1024]{2,1,0:T(8,128)(2,1)} %get-tuple-element.99), channel_id=1, source_target_pairs={{0,14},{1,15},{2,12},{3,13},{4,10},{5,11},{6,8},{7,9},{8,6},{9,7},... | collective-permute-start | bytes 786440 | tf_op jit(solution)/shard_map/ppermute | solution.py:420
  77.1 31.1 %collective-permute-start.14 = (bf16[8,16,1024]{2,1,0:T(8,128)(2,1)}, bf16[8,16,1024]{2,1,0:T(8,128)(2,1)}, u32[]{:S(2)}, u32[]{:S(2)}) collective-permute-start(bf16[8,16,1024]{2,1,0:T(8,128)(2,1)} %get-tuple-element.100), channel_id=1, source_target_pairs={{0,3},{1,2},{2,1},{3,0},{4,7},{5,6},{6,5},{7,4},{8,11},{9,10},{10,... | collective-permute-start | bytes 786440 | tf_op jit(solution)/shard_map/ppermute | solution.py:420
  108.2 24.5 %collective-permute-start.15 = (bf16[8,16,1024]{2,1,0:T(8,128)(2,1)S(1)}, bf16[8,16,1024]{2,1,0:T(8,128)(2,1)S(1)}, u32[]{:S(2)}, u32[]{:S(2)}) collective-permute-start(bf16[8,16,1024]{2,1,0:T(8,128)(2,1)S(1)} %copy-done.12), channel_id=1, source_target_pairs={{0,11},{1,10},{2,9},{3,8},{4,15},{5,14},{6,13},{7,12},{8,3},{9,2},... | collective-permute-start | bytes 786440 | tf_op jit(solution)/shard_map/ppermute | solution.py:420
  109.7 23.8 %collective-permute-start.16 = (bf16[8,16,1024]{2,1,0:T(8,128)(2,1)S(1)}, bf16[8,16,1024]{2,1,0:T(8,128)(2,1)S(1)}, u32[]{:S(2)}, u32[]{:S(2)}) collective-permute-start(bf16[8,16,1024]{2,1,0:T(8,128)(2,1)S(1)} %copy-done.11), channel_id=1, source_target_pairs={{0,15},{1,14},{2,13},{3,12},{4,11},{5,10},{6,9},{7,8},{8,7},{9,6},... | collective-permute-start | bytes 786440 | tf_op jit(solution)/shard_map/ppermute | solution.py:420
  (19 other events, 225.2 us)

commit v21 on v13

--- a/solution.py
+++ b/solution.py
@@ -171,6 +171,7 @@
     pages, page_len, width = kv.shape
     each = contexts[0].shape[0]
     ahead = FRESH_PAGES if first else 0
+    direct = last and not first
     block = query_ref.shape[0]
     tile = tile_pages * page_len
     lanes = QUERY_GROUP * block
@@ -186,8 +187,12 @@
     @pl.when(step == 0)
     def _():
         for i, context in enumerate(contexts):
-            for k in range(each):
-                pltpu.make_async_copy(context.at[k], kv.at[ahead + place[i * each + k]], sem).start()
+            if direct:
+                kv[i * each : (i + 1) * each] = context[...]
+            else:
+                for k in range(each):
+                    to = kv.at[ahead + place[i * each + k]]
+                    pltpu.make_async_copy(context.at[k], to, sem).start()
         if first:
             picked = fresh_ref.shape[0]
             count = picked // page_len
@@ -212,8 +217,9 @@
             return carry
 
         lax.fori_loop(0, (pages - ahead) // FRESH_PAGES, place_rows, 0)
-        used = kv.at[ahead:]
-        pltpu.make_async_copy(used, used, sem).wait()
+        if not direct:
+            used = kv.at[ahead:]
+            pltpu.make_async_copy(used, used, sem).wait()
 
         def turn(t, carry):
             here = pl.ds(t * tile_pages, tile_pages)
@@ -320,7 +326,12 @@
                 wide,
                 *[pl.BlockSpec(x.shape, lambda b, *_: (0, 0)) for x in fresh if first],
                 *([] if first else state_specs),
-                *[pl.BlockSpec(memory_space=pltpu.HBM)] * len(contexts),
+                *[
+                    pl.BlockSpec(x.shape, lambda b, *_: (0, 0, 0))
+                    if last and not first
+                    else pl.BlockSpec(memory_space=pltpu.HBM)
+                    for x in contexts
+                ],
             ],
             out_specs=[wide] if last else state_specs,
             scratch_shapes=[
@@ -369,6 +380,8 @@
             count = len(group) * capacity
         member = arrival >= 0
         place = jnp.sum((member[None, :] & before).astype(jnp.int32), axis=1)
+        if at == len(groups) - 1 and at > 0:
+            place = arrival
         index = jnp.arange(count)[:, None]
         places = jnp.sum(jnp.where(arrival[None, :] == index, place[None, :], 0), axis=1)
         page = jnp.sum(

time: 139 us -> 138 us (level); the launches traced: 137 us -> 137 us
  starting transfers between devices: 39.2 us -> 37.7 us
  waiting for transfers between devices: 19.6 us -> 21.1 us
    ppermute x17, starting transfers between devices: 25.4 us -> 23.9 us  [swap(): return lax.ppermute(x, 'store', [(h, h ^ d) for h in range(holders)])]
    ppermute x17, waiting for transfers between devices: 19 us -> 20.5 us  [swap(): return lax.ppermute(x, 'store', [(h, h ^ d) for h in range(holders)])]
  transfers between devices with their start and end apart: 19 -> 19, of which waited for: 8 -> 8; matrix products, arithmetic and copies ran while one was open for 5% -> 5% of each run, Pallas kernels for 38% -> 39%
where the time goes in v21:
time: 138 us; the launch traced here: 137 us
  Pallas kernels  67.4 us (49%)
  starting transfers between devices  37.7 us (27%)
  waiting for transfers between devices  21.1 us (15%)
  other arithmetic  5.03 us (4%)
  local copies, waits for them, and re-layouts  4.95 us (4%)
    pallas_call x3, Pallas kernels, attend(): pl.pallas_call(functools.partial(attend_kernel, first, last, tile_pages,...  47.9 us
    ppermute x17, starting transfers between devices, swap(): return lax.ppermute(x, 'store', [(h, h ^ d) for h in range(holders)])  23.9 us
    ppermute x17, waiting for transfers between devices, swap(): return lax.ppermute(x, 'store', [(h, h ^ d) for h in range(holders)])  20.5 us
    all_to_all x2, starting transfers between devices, exchange(): return lax.all_to_all(x, 'store', split_axis=0, concat_axis=0, tiled=True)  13.9 us
    pallas_call x1, Pallas kernels, per_device(): pl.pallas_call(write_back_kernel, grid_spec=pltpu.PrefetchScalarGridSpec(...  8.02 us
    pallas_call x1, Pallas kernels, per_device(): pl.pallas_call(functools.partial(gather_kernel, capacity, others), grid_s...  4.9 us
    unnamed x49, local copies, waits for them, and re-layouts  2.83 us
  transfers between devices with their start and end apart: 19, of which 8 were waited for; matrix products, arithmetic and copies ran while one was open for 5% of the time, Pallas kernels for 39%

profile of v21, /device:TPU:9, one launch (start us, length us, event | category | flops | bytes accessed | tf_op | source)
XLA Modules:
  0.0 137.1 jit_solution(6667715028494035369)
XLA Ops:
  0.6 1.7 %shard_map.68 = (s32[16,2,128]{2,1,0:T(2,128)}, s32[1,2,128]{2,1,0:T(2,128)}, s32[1,2,128]{2,1,0:T(2,128)}) custom-call(s32[1]{0:T(128)} %bitcast.own, s32[1,128]{1,0:T(1,128)} %table_ref.2, s32[1,160]{1,0:T(1,128)} %rest_1_.2), custom_call_target="tpu_custom_call" | custom-call | tf_op jit(solution)/shard_map/pallas_call | solution.py:425
  2.3 2.3 %collective-permute-start = (s32[1,2,128]{2,1,0:T(2,128)}, s32[1,2,128]{2,1,0:T(2,128)S(1)}, u32[]{:S(2)}, u32[]{:S(2)}) collective-permute-start(s32[1,2,128]{2,1,0:T(2,128)} %get-tuple-element.49), channel_id=1, source_target_pairs={{0,8},{1,9},{2,10},{3,11},{4,12},{5,13},{6,14},{7,15},{8,0},{9,1},... | collective-permute-start | bytes 3080 | tf_op jit(solution)/shard_map/ppermute | solution.py:420
  4.6 1.2 collective-permute-done.refs_0_
  5.8 1.4 %collective-permute-done.1.refs_1_ = s32[1,2,128]{2,1,0:T(2,128)S(1)} collective-permute-done((s32[1,2,128]{2,1,0:T(2,128)}, s32[1,2,128]{2,1,0:T(2,128)S(1)}, u32[]{:S(2)}, u32[]{:S(2)}) %collective-permute-start.1) | collective-permute-done | bytes 1056 | tf_op jit(solution)/shard_map/ppermute | solution.py:420
  7.8 2.5 %shard_map.69 = (bf16[8,16,1024]{2,1,0:T(8,128)(2,1)}, bf16[8,16,1024]{2,1,0:T(8,128)(2,1)}) custom-call(s32[1,2,128]{2,1,0:T(2,128)} %copy-done.7, s32[1,2,128]{2,1,0:T(2,128)} %copy-done.8, bf16[128,16,1024]{2,1,0:T(8,128)(2,1)} %store_hbm.3), custom_call_target="tpu_custom_call" | custom-call | tf_op jit(solution)/shard_map/pallas_call | solution.py:443
  10.3 7.6 %all-to-all-start = ((s32[16,2,128]{2,1,0:T(2,128)}), s32[16,2,128]{2,1,0:T(2,128)S(1)}, u32[]{:S(2)}, u32[]{:S(2)}) async-start(s32[16,2,128]{2,1,0:T(2,128)} %get-tuple-element.54), calls=%async_computation | async-start | bytes 32768 | tf_op jit(solution)/shard_map/all_to_all | solution.py:423
  17.9 2.1 %collective-permute-start.2 = (bf16[8,16,1024]{2,1,0:T(8,128)(2,1)}, bf16[8,16,1024]{2,1,0:T(8,128)(2,1)S(1)}, u32[]{:S(2)}, u32[]{:S(2)}) collective-permute-start(bf16[8,16,1024]{2,1,0:T(8,128)(2,1)} %get-tuple-element.76), channel_id=1, source_target_pairs={{0,8},{1,9},{2,10},{3,11},{4,12},{5,13},{6,14},{7,15},{8,0},{9,1},... | collective-permute-start | bytes 786440 | tf_op jit(solution)/shard_map/ppermute | solution.py:420
  20.0 2.4 %shard_map.71 = bf16[16,16,1024]{2,1,0:T(8,128)(2,1)} custom-call(s32[1,128]{1,0:T(1,128)} %table_ref.2, s32[1,160]{1,0:T(1,128)} %rest_1_.2, bf16[160,1024]{1,0:T(8,128)(2,1)} %bitcast.70), custom_call_target="tpu_custom_call" | custom-call | tf_op jit(solution)/shard_map/pallas_call | solution.py:467
  23.5 4.9 %shard_map.70 = (bf16[8,16,1024]{2,1,0:T(8,128)(2,1)}, bf16[8,16,1024]{2,1,0:T(8,128)(2,1)}, bf16[8,16,1024]{2,1,0:T(8,128)(2,1)}, bf16[8,16,1024]{2,1,0:T(8,128...) custom-call(s32[1]{0:T(128)} %bitcast.own, ...), custom_call_target="tpu_custom_call" | custom-call | tf_op jit(solution)/shard_map/pallas_call | solution.py:476
  30.1 6.3 %all-to-all-start.1 = ((bf16[16,16,1024]{2,1,0:T(8,128)(2,1)}), bf16[16,16,1024]{2,1,0:T(8,128)(2,1)S(1)}, u32[]{:S(2)}, u32[]{:S(2)}) async-start(bf16[16,16,1024]{2,1,0:T(8,128)(2,1)} %shard_map.71), calls=%async_computation.1 | async-start | bytes 1048576 | tf_op jit(solution)/shard_map/all_to_all | solution.py:423
  36.5 1.9 %collective-permute-start.5 = (bf16[8,16,1024]{2,1,0:T(8,128)(2,1)}, bf16[8,16,1024]{2,1,0:T(8,128)(2,1)S(1)}, u32[]{:S(2)}, u32[]{:S(2)}) collective-permute-start(bf16[8,16,1024]{2,1,0:T(8,128)(2,1)} %get-tuple-element.79), channel_id=1, source_target_pairs={{0,5},{1,4},{2,7},{3,6},{4,1},{5,0},{6,3},{7,2},{8,13},{9,12},{10,... | collective-permute-start | bytes 786440 | tf_op jit(solution)/shard_map/ppermute | solution.py:420
  41.9 2.5 %collective-permute-start.7 = (bf16[8,16,1024]{2,1,0:T(8,128)(2,1)}, bf16[8,16,1024]{2,1,0:T(8,128)(2,1)S(1)}, u32[]{:S(2)}, u32[]{:S(2)}) collective-permute-start(bf16[8,16,1024]{2,1,0:T(8,128)(2,1)} %get-tuple-element.83), channel_id=1, source_target_pairs={{0,9},{1,8},{2,11},{3,10},{4,13},{5,12},{6,15},{7,14},{8,1},{9,0},... | collective-permute-start | bytes 786440 | tf_op jit(solution)/shard_map/ppermute | solution.py:420
  44.4 4.4 %collective-permute-done.3.rest_7_ = bf16[8,16,1024]{2,1,0:T(8,128)(2,1)S(1)} collective-permute-done((bf16[8,16,1024]{2,1,0:T(8,128)(2,1)}, bf16[8,16,1024]{2,1,0:T(8,128)(2,1)S(1)}, u32[]{:S(2)}, u32[]{:S(2)}) %collective-permute-start.3) | collective-permute-done | bytes 262176 | tf_op jit(solution)/shard_map/ppermute | solution.py:420
  48.8 3.1 %collective-permute-done.4.rest_8_ = bf16[8,16,1024]{2,1,0:T(8,128)(2,1)S(1)} collective-permute-done((bf16[8,16,1024]{2,1,0:T(8,128)(2,1)}, bf16[8,16,1024]{2,1,0:T(8,128)(2,1)S(1)}, u32[]{:S(2)}, u32[]{:S(2)}) %collective-permute-start.4) | collective-permute-done | bytes 262176 | tf_op jit(solution)/shard_map/ppermute | solution.py:420
  51.9 3.2 %collective-permute-start.9 = (bf16[8,16,1024]{2,1,0:T(8,128)(2,1)}, bf16[8,16,1024]{2,1,0:T(8,128)(2,1)}, u32[]{:S(2)}, u32[]{:S(2)}) collective-permute-start(bf16[8,16,1024]{2,1,0:T(8,128)(2,1)} %get-tuple-element.85), channel_id=1, source_target_pairs={{0,13},{1,12},{2,15},{3,14},{4,9},{5,8},{6,11},{7,10},{8,5},{9,4},... | collective-permute-start | bytes 786440 | tf_op jit(solution)/shard_map/ppermute | solution.py:420
  57.4 8.0 %shard_map.72 = bf16[128,16,1024]{2,1,0:T(8,128)(2,1)} custom-call(s32[16,2,128]{2,1,0:T(2,128)} %copy-done.1, s32[16,2,128]{2,1,0:T(2,128)} %copy-done.1, bf16[128,16,1024]{2,1,0:T(8,128)(2,1)} %store_hbm.3, bf16[16,16,1024]{2,1,0:T(8,128)(2,1)} %copy-done), custom_call_target="tpu_custom_call" | custom-call | bytes 8388608 | tf_op jit(solution)/shard_map/pallas_call | solution.py:497
  65.7 3.3 %collective-permute-start.11 = (bf16[8,16,1024]{2,1,0:T(8,128)(2,1)S(1)}, bf16[8,16,1024]{2,1,0:T(8,128)(2,1)}, u32[]{:S(2)}, u32[]{:S(2)}) collective-permute-start(bf16[8,16,1024]{2,1,0:T(8,128)(2,1)S(1)} %copy-done.17), channel_id=1, source_target_pairs={{0,10},{1,11},{2,8},{3,9},{4,14},{5,15},{6,12},{7,13},{8,2},{9,3},... | collective-permute-start | bytes 786440 | tf_op jit(solution)/shard_map/ppermute | solution.py:420
  69.7 2.1 %collective-permute-start.13 = (bf16[8,16,1024]{2,1,0:T(8,128)(2,1)S(1)}, bf16[8,16,1024]{2,1,0:T(8,128)(2,1)}, u32[]{:S(2)}, u32[]{:S(2)}) collective-permute-start(bf16[8,16,1024]{2,1,0:T(8,128)(2,1)S(1)} %copy-done.14), channel_id=1, source_target_pairs={{0,14},{1,15},{2,12},{3,13},{4,10},{5,11},{6,8},{7,9},{8,6},{9,7},... | collective-permute-start | bytes 786440 | tf_op jit(solution)/shard_map/ppermute | solution.py:420
  71.8 5.8 %collective-permute-done.9.rest_7_ = bf16[8,16,1024]{2,1,0:T(8,128)(2,1)} collective-permute-done((bf16[8,16,1024]{2,1,0:T(8,128)(2,1)}, bf16[8,16,1024]{2,1,0:T(8,128)(2,1)}, u32[]{:S(2)}, u32[]{:S(2)}) %collective-permute-start.9) | collective-permute-done | bytes 262176 | tf_op jit(solution)/shard_map/ppermute | solution.py:420
  79.4 19.8 %shard_map.73 = (f32[5,4,128,384]{3,2,1,0:T(8,128)}, f32[5,8,384]{2,1,0:T(8,128)}) custom-call(s32[48]{0:T(128)} %get-tuple-element.97.place, s32[48]{0:T(128)} %copy-done.10, s32[5]{0:T(128)} %and_select_fusion.tiles, s32[5,1,128]{2,1,0:T(1,128)} %tile.9.rest_0_, s32[1,160]{1,0:T(1,128)} %rest_1_.2, bf16[160,6144]{1,0:T(8,128)(2,1)} %bitcast.66, ...), custom_call_target="tpu_custom_call" | custom-call | flops 4831838208 | bytes 7995392 | tf_op jit(solution)/shard_map/pallas_call | solution.py:318
  99.8 4.4 %collective-permute-start.16 = (bf16[8,16,1024]{2,1,0:T(8,128)(2,1)S(1)}, bf16[8,16,1024]{2,1,0:T(8,128)(2,1)S(1)}, u32[]{:S(2)}, u32[]{:S(2)}) collective-permute-start(bf16[8,16,1024]{2,1,0:T(8,128)(2,1)S(1)} %copy-done.11), channel_id=1, source_target_pairs={{0,15},{1,14},{2,13},{3,12},{4,11},{5,10},{6,9},{7,8},{8,7},{9,6},... | collective-permute-start | bytes 786440 | tf_op jit(solution)/shard_map/ppermute | solution.py:420
  104.2 18.3 %shard_map.74 = (f32[5,4,128,384]{3,2,1,0:T(8,128)}, f32[5,8,384]{2,1,0:T(8,128)}) custom-call(s32[64]{0:T(128)} %get-tuple-element.99.place, s32[64]{0:T(128)} %copy-done.9, s32[5]{0:T(128)} %and_select_fusion.1.tiles, s32[5,1,128]{2,1,0:T(1,128)} %tile.9.rest_0_, s32[1,160]{1,0:T(1,128)} %rest_1_.2, bf16[160,6144]{1,0:T(8,128)(2,1)} %bitcast.67, ...), custom_call_target="tpu_custom_call" | custom-call | flops 4831838208 | bytes 7995392 | tf_op jit(solution)/shard_map/pallas_call | solution.py:318
  122.5 3.9 %collective-permute-done.16.rest_6_ = bf16[8,16,1024]{2,1,0:T(8,128)(2,1)S(1)} collective-permute-done((bf16[8,16,1024]{2,1,0:T(8,128)(2,1)S(1)}, bf16[8,16,1024]{2,1,0:T(8,128)(2,1)S(1)}, u32[]{:S(2)}, u32[]{:S(2)}) %collective-permute-start.16) | collective-permute-done | bytes 262176 | tf_op jit(solution)/shard_map/ppermute | solution.py:420
  127.2 9.9 %shard_map.75 = bf16[160,6144]{1,0:T(8,128)(2,1)} custom-call(s32[16]{0:T(128)} %get-tuple-element.101.place, s32[16]{0:T(128)} %copy-done.6, s32[5]{0:T(128)} %and_select_fusion.2.tiles, s32[5,1,128]{2,1,0:T(1,128)} %tile.9.rest_0_, s32[1,160]{1,0:T(1,128)} %rest_1_.2, bf16[160,6144]{1,0:T(8,128)(2,1)} %bitcast.68, ...), custom_call_target="tpu_custom_call" | custom-call | flops 1207959552 | bytes 6422528 | tf_op jit(solution)/shard_map/pallas_call | solution.py:318
  (93 shorter events, 13.2 us)
Async XLA Ops:
  2.3 3.5 %collective-permute-start = (s32[1,2,128]{2,1,0:T(2,128)}, s32[1,2,128]{2,1,0:T(2,128)S(1)}, u32[]{:S(2)}, u32[]{:S(2)}) collective-permute-start(s32[1,2,128]{2,1,0:T(2,128)} %get-tuple-element.49), channel_id=1, source_target_pairs={{0,8},{1,9},{2,10},{3,11},{4,12},{5,13},{6,14},{7,15},{8,0},{9,1},... | collective-permute-start | bytes 3080 | tf_op jit(solution)/shard_map/ppermute | solution.py:420
  4.6 2.6 %collective-permute-start.1 = (s32[1,2,128]{2,1,0:T(2,128)}, s32[1,2,128]{2,1,0:T(2,128)S(1)}, u32[]{:S(2)}, u32[]{:S(2)}) collective-permute-start(s32[1,2,128]{2,1,0:T(2,128)} %get-tuple-element.50), channel_id=1, source_target_pairs={{0,12},{1,13},{2,14},{3,15},{4,8},{5,9},{6,10},{7,11},{8,4},{9,5},... | collective-permute-start | bytes 3080 | tf_op jit(solution)/shard_map/ppermute | solution.py:420
  10.3 12.6 %all-to-all-start = ((s32[16,2,128]{2,1,0:T(2,128)}), s32[16,2,128]{2,1,0:T(2,128)S(1)}, u32[]{:S(2)}, u32[]{:S(2)}) async-start(s32[16,2,128]{2,1,0:T(2,128)} %get-tuple-element.54), calls=%async_computation | async-start | bytes 32768 | tf_op jit(solution)/shard_map/all_to_all | solution.py:423
  17.9 24.0 %collective-permute-start.2 = (bf16[8,16,1024]{2,1,0:T(8,128)(2,1)}, bf16[8,16,1024]{2,1,0:T(8,128)(2,1)S(1)}, u32[]{:S(2)}, u32[]{:S(2)}) collective-permute-start(bf16[8,16,1024]{2,1,0:T(8,128)(2,1)} %get-tuple-element.76), channel_id=1, source_target_pairs={{0,8},{1,9},{2,10},{3,11},{4,12},{5,13},{6,14},{7,15},{8,0},{9,1},... | collective-permute-start | bytes 786440 | tf_op jit(solution)/shard_map/ppermute | solution.py:420
  20.0 28.8 %collective-permute-start.3 = (bf16[8,16,1024]{2,1,0:T(8,128)(2,1)}, bf16[8,16,1024]{2,1,0:T(8,128)(2,1)S(1)}, u32[]{:S(2)}, u32[]{:S(2)}) collective-permute-start(bf16[8,16,1024]{2,1,0:T(8,128)(2,1)} %get-tuple-element.77), channel_id=1, source_target_pairs={{0,12},{1,13},{2,14},{3,15},{4,8},{5,9},{6,10},{7,11},{8,4},{9,5},... | collective-permute-start | bytes 786440 | tf_op jit(solution)/shard_map/ppermute | solution.py:420
  30.1 26.4 %all-to-all-start.1 = ((bf16[16,16,1024]{2,1,0:T(8,128)(2,1)}), bf16[16,16,1024]{2,1,0:T(8,128)(2,1)S(1)}, u32[]{:S(2)}, u32[]{:S(2)}) async-start(bf16[16,16,1024]{2,1,0:T(8,128)(2,1)} %shard_map.71), calls=%async_computation.1 | async-start | bytes 1048576 | tf_op jit(solution)/shard_map/all_to_all | solution.py:423
  36.4 15.5 %collective-permute-start.4 = (bf16[8,16,1024]{2,1,0:T(8,128)(2,1)}, bf16[8,16,1024]{2,1,0:T(8,128)(2,1)S(1)}, u32[]{:S(2)}, u32[]{:S(2)}) collective-permute-start(bf16[8,16,1024]{2,1,0:T(8,128)(2,1)} %get-tuple-element.78), channel_id=1, source_target_pairs={{0,4},{1,5},{2,6},{3,7},{4,0},{5,1},{6,2},{7,3},{8,12},{9,13},{10,... | collective-permute-start | bytes 786440 | tf_op jit(solution)/shard_map/ppermute | solution.py:420
  36.5 28.9 %collective-permute-start.5 = (bf16[8,16,1024]{2,1,0:T(8,128)(2,1)}, bf16[8,16,1024]{2,1,0:T(8,128)(2,1)S(1)}, u32[]{:S(2)}, u32[]{:S(2)}) collective-permute-start(bf16[8,16,1024]{2,1,0:T(8,128)(2,1)} %get-tuple-element.79), channel_id=1, source_target_pairs={{0,5},{1,4},{2,7},{3,6},{4,1},{5,0},{6,3},{7,2},{8,13},{9,12},{10,... | collective-permute-start | bytes 786440 | tf_op jit(solution)/shard_map/ppermute | solution.py:420
  38.4 27.3 %collective-permute-start.6 = (bf16[8,16,1024]{2,1,0:T(8,128)(2,1)}, bf16[8,16,1024]{2,1,0:T(8,128)(2,1)S(1)}, u32[]{:S(2)}, u32[]{:S(2)}) collective-permute-start(bf16[8,16,1024]{2,1,0:T(8,128)(2,1)} %get-tuple-element.80), channel_id=1, source_target_pairs={{0,1},{1,0},{2,3},{3,2},{4,5},{5,4},{6,7},{7,6},{8,9},{9,8},{10,11... | collective-permute-start | bytes 786440 | tf_op jit(solution)/shard_map/ppermute | solution.py:420
  39.1 26.3 %copy-start.10 = (s32[48]{0:T(128)}, s32[48]{0:T(128)S(1)}, u32[]{:S(2)}) copy-start(s32[48]{0:T(128)S(1)} %get-tuple-element.96.page_number) | copy-start | bytes 580
  41.9 37.5 %copy-start.16 = (bf16[8,16,1024]{2,1,0:T(8,128)(2,1)}, bf16[8,16,1024]{2,1,0:T(8,128)(2,1)S(1)}, u32[]{:S(2)}) copy-start(bf16[8,16,1024]{2,1,0:T(8,128)(2,1)S(1)} %collective-permute-done.2.rest_6_) | copy-start | bytes 786436
  41.9 27.1 %collective-permute-start.7 = (bf16[8,16,1024]{2,1,0:T(8,128)(2,1)}, bf16[8,16,1024]{2,1,0:T(8,128)(2,1)S(1)}, u32[]{:S(2)}, u32[]{:S(2)}) collective-permute-start(bf16[8,16,1024]{2,1,0:T(8,128)(2,1)} %get-tuple-element.83), channel_id=1, source_target_pairs={{0,9},{1,8},{2,11},{3,10},{4,13},{5,12},{6,15},{7,14},{8,1},{9,0},... | collective-permute-start | bytes 786440 | tf_op jit(solution)/shard_map/ppermute | solution.py:420
  48.8 30.6 %copy-start.18 = (bf16[8,16,1024]{2,1,0:T(8,128)(2,1)}, bf16[8,16,1024]{2,1,0:T(8,128)(2,1)S(1)}, u32[]{:S(2)}) copy-start(bf16[8,16,1024]{2,1,0:T(8,128)(2,1)S(1)} %collective-permute-done.3.rest_7_) | copy-start | bytes 786436
  48.8 20.9 %collective-permute-start.8 = (bf16[8,16,1024]{2,1,0:T(8,128)(2,1)}, bf16[8,16,1024]{2,1,0:T(8,128)(2,1)}, u32[]{:S(2)}, u32[]{:S(2)}) collective-permute-start(bf16[8,16,1024]{2,1,0:T(8,128)(2,1)} %get-tuple-element.84), channel_id=1, source_target_pairs={{0,6},{1,7},{2,4},{3,5},{4,2},{5,3},{6,0},{7,1},{8,14},{9,15},{10,... | collective-permute-start | bytes 786440 | tf_op jit(solution)/shard_map/ppermute | solution.py:420
  51.9 27.5 %copy-start.20 = (bf16[8,16,1024]{2,1,0:T(8,128)(2,1)}, bf16[8,16,1024]{2,1,0:T(8,128)(2,1)S(1)}, u32[]{:S(2)}) copy-start(bf16[8,16,1024]{2,1,0:T(8,128)(2,1)S(1)} %collective-permute-done.4.rest_8_) | copy-start | bytes 786436
  51.9 25.7 %collective-permute-start.9 = (bf16[8,16,1024]{2,1,0:T(8,128)(2,1)}, bf16[8,16,1024]{2,1,0:T(8,128)(2,1)}, u32[]{:S(2)}, u32[]{:S(2)}) collective-permute-start(bf16[8,16,1024]{2,1,0:T(8,128)(2,1)} %get-tuple-element.85), channel_id=1, source_target_pairs={{0,13},{1,12},{2,15},{3,14},{4,9},{5,8},{6,11},{7,10},{8,5},{9,4},... | collective-permute-start | bytes 786440 | tf_op jit(solution)/shard_map/ppermute | solution.py:420
  65.5 33.8 %collective-permute-start.10 = (bf16[8,16,1024]{2,1,0:T(8,128)(2,1)S(1)}, bf16[8,16,1024]{2,1,0:T(8,128)(2,1)}, u32[]{:S(2)}, u32[]{:S(2)}) collective-permute-start(bf16[8,16,1024]{2,1,0:T(8,128)(2,1)S(1)} %copy-done.19), channel_id=1, source_target_pairs={{0,7},{1,6},{2,5},{3,4},{4,3},{5,2},{6,1},{7,0},{8,15},{9,14},{10,... | collective-permute-start | bytes 786440 | tf_op jit(solution)/shard_map/ppermute | solution.py:420
  65.7 34.1 %collective-permute-start.11 = (bf16[8,16,1024]{2,1,0:T(8,128)(2,1)S(1)}, bf16[8,16,1024]{2,1,0:T(8,128)(2,1)}, u32[]{:S(2)}, u32[]{:S(2)}) collective-permute-start(bf16[8,16,1024]{2,1,0:T(8,128)(2,1)S(1)} %copy-done.17), channel_id=1, source_target_pairs={{0,10},{1,11},{2,8},{3,9},{4,14},{5,15},{6,12},{7,13},{8,2},{9,3},... | collective-permute-start | bytes 786440 | tf_op jit(solution)/shard_map/ppermute | solution.py:420
  69.0 30.2 %copy-start.21 = (bf16[8,16,1024]{2,1,0:T(8,128)(2,1)}, bf16[8,16,1024]{2,1,0:T(8,128)(2,1)S(1)}, u32[]{:S(2)}) copy-start(bf16[8,16,1024]{2,1,0:T(8,128)(2,1)S(1)} %collective-permute-done.7.rest_5_) | copy-start | bytes 786436
  69.0 35.2 %collective-permute-start.12 = (bf16[8,16,1024]{2,1,0:T(8,128)(2,1)S(1)}, bf16[8,16,1024]{2,1,0:T(8,128)(2,1)}, u32[]{:S(2)}, u32[]{:S(2)}) collective-permute-start(bf16[8,16,1024]{2,1,0:T(8,128)(2,1)S(1)} %copy-done.15), channel_id=1, source_target_pairs={{0,2},{1,3},{2,0},{3,1},{4,6},{5,7},{6,4},{7,5},{8,10},{9,11},{10,... | collective-permute-start | bytes 786440 | tf_op jit(solution)/shard_map/ppermute | solution.py:420
  69.7 34.5 %collective-permute-start.13 = (bf16[8,16,1024]{2,1,0:T(8,128)(2,1)S(1)}, bf16[8,16,1024]{2,1,0:T(8,128)(2,1)}, u32[]{:S(2)}, u32[]{:S(2)}) collective-permute-start(bf16[8,16,1024]{2,1,0:T(8,128)(2,1)S(1)} %copy-done.14), channel_id=1, source_target_pairs={{0,14},{1,15},{2,12},{3,13},{4,10},{5,11},{6,8},{7,9},{8,6},{9,7},... | collective-permute-start | bytes 786440 | tf_op jit(solution)/shard_map/ppermute | solution.py:420
  77.6 26.6 %collective-permute-start.14 = (bf16[8,16,1024]{2,1,0:T(8,128)(2,1)S(1)}, bf16[8,16,1024]{2,1,0:T(8,128)(2,1)}, u32[]{:S(2)}, u32[]{:S(2)}) collective-permute-start(bf16[8,16,1024]{2,1,0:T(8,128)(2,1)S(1)} %copy-done.13), channel_id=1, source_target_pairs={{0,3},{1,2},{2,1},{3,0},{4,7},{5,6},{6,5},{7,4},{8,11},{9,10},{10,... | collective-permute-start | bytes 786440 | tf_op jit(solution)/shard_map/ppermute | solution.py:420
  99.2 23.3 %collective-permute-start.15 = (bf16[8,16,1024]{2,1,0:T(8,128)(2,1)S(1)}, bf16[8,16,1024]{2,1,0:T(8,128)(2,1)S(1)}, u32[]{:S(2)}, u32[]{:S(2)}) collective-permute-start(bf16[8,16,1024]{2,1,0:T(8,128)(2,1)S(1)} %copy-done.12), channel_id=1, source_target_pairs={{0,11},{1,10},{2,9},{3,8},{4,15},{5,14},{6,13},{7,12},{8,3},{9,2},... | collective-permute-start | bytes 786440 | tf_op jit(solution)/shard_map/ppermute | solution.py:420
  99.8 26.7 %collective-permute-start.16 = (bf16[8,16,1024]{2,1,0:T(8,128)(2,1)S(1)}, bf16[8,16,1024]{2,1,0:T(8,128)(2,1)S(1)}, u32[]{:S(2)}, u32[]{:S(2)}) collective-permute-start(bf16[8,16,1024]{2,1,0:T(8,128)(2,1)S(1)} %copy-done.11), channel_id=1, source_target_pairs={{0,15},{1,14},{2,13},{3,12},{4,11},{5,10},{6,9},{7,8},{8,7},{9,6},... | collective-permute-start | bytes 786440 | tf_op jit(solution)/shard_map/ppermute | solution.py:420
  (19 other events, 239.6 us)

commit v22 on v21

--- a/solution.py
+++ b/solution.py
@@ -409,7 +409,7 @@
     wide = pltpu.VMEM((8, -(-picked // LANES) * LANES), jnp.int32)
     if holders == 16:
         first = (8, 12)
-        groups = [(0, 8, 12, 4, 5, 1), (9, 6, 13, 7, 10, 2, 14, 3), (11, 15)]
+        groups = [(0, 8, 12, 4, 2, 1), (9, 5, 13, 6, 10, 7, 14, 3), (11, 15)]
         others = [d for group in groups for d in group if d not in first]
     else:
         first = ()

time: 138 us -> 137 us (level)
  starting transfers between devices: 37.7 us -> 35.8 us
    all_to_all x2, waiting for transfers between devices: 0.57 us -> 4.92 us  [exchange(): return lax.all_to_all(x, 'store', split_axis=0, concat_axis=0, tiled=True)]
    ppermute x17, waiting for transfers between devices: 20.5 us -> 16.2 us  [swap(): return lax.ppermute(x, 'store', [(h, h ^ d) for h in range(holders)])]
    ppermute x17, starting transfers between devices: 23.9 us -> 21.9 us  [swap(): return lax.ppermute(x, 'store', [(h, h ^ d) for h in range(holders)])]
  transfers between devices with their start and end apart: 19 -> 19, of which waited for: 8 -> 9; matrix products, arithmetic and copies ran while one was open for 5% -> 5% of each run, Pallas kernels for 39% -> 39%
where the time goes in v22:
time: 137 us; the launch traced here: 135 us
  Pallas kernels  67.3 us (49%)
  starting transfers between devices  35.8 us (26%)
  waiting for transfers between devices  21.1 us (15%)
  other arithmetic  5.03 us (4%)
  local copies, waits for them, and re-layouts  4.96 us (4%)
    pallas_call x3, Pallas kernels, attend(): pl.pallas_call(functools.partial(attend_kernel, first, last, tile_pages,...  47.9 us
    ppermute x17, starting transfers between devices, swap(): return lax.ppermute(x, 'store', [(h, h ^ d) for h in range(holders)])  21.9 us
    ppermute x17, waiting for transfers between devices, swap(): return lax.ppermute(x, 'store', [(h, h ^ d) for h in range(holders)])  16.2 us
    all_to_all x2, starting transfers between devices, exchange(): return lax.all_to_all(x, 'store', split_axis=0, concat_axis=0, tiled=True)  13.9 us
    pallas_call x1, Pallas kernels, per_device(): pl.pallas_call(write_back_kernel, grid_spec=pltpu.PrefetchScalarGridSpec(...  8.02 us
    all_to_all x2, waiting for transfers between devices, exchange(): return lax.all_to_all(x, 'store', split_axis=0, concat_axis=0, tiled=True)  4.92 us
    pallas_call x1, Pallas kernels, per_device(): pl.pallas_call(functools.partial(gather_kernel, capacity, others), grid_s...  4.9 us
    unnamed x49, local copies, waits for them, and re-layouts  2.83 us
  transfers between devices with their start and end apart: 19, of which 9 were waited for; matrix products, arithmetic and copies ran while one was open for 5% of the time, Pallas kernels for 39%

profile of v22, /device:TPU:9, one launch (start us, length us, event | category | flops | bytes accessed | tf_op | source)
XLA Modules:
  0.0 135.2 jit_solution(4135963365830255290)
XLA Ops:
  0.6 1.7 %shard_map.68 = (s32[16,2,128]{2,1,0:T(2,128)}, s32[1,2,128]{2,1,0:T(2,128)}, s32[1,2,128]{2,1,0:T(2,128)}) custom-call(s32[1]{0:T(128)} %bitcast.own, s32[1,128]{1,0:T(1,128)} %table_ref.2, s32[1,160]{1,0:T(1,128)} %rest_1_.2), custom_call_target="tpu_custom_call" | custom-call | tf_op jit(solution)/shard_map/pallas_call | solution.py:425
  2.3 2.3 %collective-permute-start = (s32[1,2,128]{2,1,0:T(2,128)}, s32[1,2,128]{2,1,0:T(2,128)S(1)}, u32[]{:S(2)}, u32[]{:S(2)}) collective-permute-start(s32[1,2,128]{2,1,0:T(2,128)} %get-tuple-element.49), channel_id=1, source_target_pairs={{0,8},{1,9},{2,10},{3,11},{4,12},{5,13},{6,14},{7,15},{8,0},{9,1},... | collective-permute-start | bytes 3080 | tf_op jit(solution)/shard_map/ppermute | solution.py:420
  5.8 1.4 %collective-permute-done.1.refs_1_ = s32[1,2,128]{2,1,0:T(2,128)S(1)} collective-permute-done((s32[1,2,128]{2,1,0:T(2,128)}, s32[1,2,128]{2,1,0:T(2,128)S(1)}, u32[]{:S(2)}, u32[]{:S(2)}) %collective-permute-start.1) | collective-permute-done | bytes 1056 | tf_op jit(solution)/shard_map/ppermute | solution.py:420
  7.8 2.5 %shard_map.69 = (bf16[8,16,1024]{2,1,0:T(8,128)(2,1)}, bf16[8,16,1024]{2,1,0:T(8,128)(2,1)}) custom-call(s32[1,2,128]{2,1,0:T(2,128)} %copy-done.7, s32[1,2,128]{2,1,0:T(2,128)} %copy-done.8, bf16[128,16,1024]{2,1,0:T(8,128)(2,1)} %store_hbm.3), custom_call_target="tpu_custom_call" | custom-call | tf_op jit(solution)/shard_map/pallas_call | solution.py:443
  10.3 7.6 %all-to-all-start = ((s32[16,2,128]{2,1,0:T(2,128)}), s32[16,2,128]{2,1,0:T(2,128)S(1)}, u32[]{:S(2)}, u32[]{:S(2)}) async-start(s32[16,2,128]{2,1,0:T(2,128)} %get-tuple-element.54), calls=%async_computation | async-start | bytes 32768 | tf_op jit(solution)/shard_map/all_to_all | solution.py:423
  17.9 2.1 %collective-permute-start.2 = (bf16[8,16,1024]{2,1,0:T(8,128)(2,1)}, bf16[8,16,1024]{2,1,0:T(8,128)(2,1)S(1)}, u32[]{:S(2)}, u32[]{:S(2)}) collective-permute-start(bf16[8,16,1024]{2,1,0:T(8,128)(2,1)} %get-tuple-element.76), channel_id=1, source_target_pairs={{0,8},{1,9},{2,10},{3,11},{4,12},{5,13},{6,14},{7,15},{8,0},{9,1},... | collective-permute-start | bytes 786440 | tf_op jit(solution)/shard_map/ppermute | solution.py:420
  20.0 2.4 %shard_map.71 = bf16[16,16,1024]{2,1,0:T(8,128)(2,1)} custom-call(s32[1,128]{1,0:T(1,128)} %table_ref.2, s32[1,160]{1,0:T(1,128)} %rest_1_.2, bf16[160,1024]{1,0:T(8,128)(2,1)} %bitcast.70), custom_call_target="tpu_custom_call" | custom-call | tf_op jit(solution)/shard_map/pallas_call | solution.py:467
  23.5 4.9 %shard_map.70 = (bf16[8,16,1024]{2,1,0:T(8,128)(2,1)}, bf16[8,16,1024]{2,1,0:T(8,128)(2,1)}, bf16[8,16,1024]{2,1,0:T(8,128)(2,1)}, bf16[8,16,1024]{2,1,0:T(8,128...) custom-call(s32[1]{0:T(128)} %bitcast.own, ...), custom_call_target="tpu_custom_call" | custom-call | tf_op jit(solution)/shard_map/pallas_call | solution.py:476
  30.1 6.3 %all-to-all-start.1 = ((bf16[16,16,1024]{2,1,0:T(8,128)(2,1)}), bf16[16,16,1024]{2,1,0:T(8,128)(2,1)S(1)}, u32[]{:S(2)}, u32[]{:S(2)}) async-start(bf16[16,16,1024]{2,1,0:T(8,128)(2,1)} %shard_map.71), calls=%async_computation.1 | async-start | bytes 1048576 | tf_op jit(solution)/shard_map/all_to_all | solution.py:423
  36.5 1.4 %collective-permute-start.5 = (bf16[8,16,1024]{2,1,0:T(8,128)(2,1)}, bf16[8,16,1024]{2,1,0:T(8,128)(2,1)S(1)}, u32[]{:S(2)}, u32[]{:S(2)}) collective-permute-start(bf16[8,16,1024]{2,1,0:T(8,128)(2,1)} %get-tuple-element.79), channel_id=1, source_target_pairs={{0,2},{1,3},{2,0},{3,1},{4,6},{5,7},{6,4},{7,5},{8,10},{9,11},{10,... | collective-permute-start | bytes 786440 | tf_op jit(solution)/shard_map/ppermute | solution.py:420
  42.3 2.0 %collective-permute-start.7 = (bf16[8,16,1024]{2,1,0:T(8,128)(2,1)}, bf16[8,16,1024]{2,1,0:T(8,128)(2,1)S(1)}, u32[]{:S(2)}, u32[]{:S(2)}) collective-permute-start(bf16[8,16,1024]{2,1,0:T(8,128)(2,1)} %get-tuple-element.83), channel_id=1, source_target_pairs={{0,9},{1,8},{2,11},{3,10},{4,13},{5,12},{6,15},{7,14},{8,1},{9,0},... | collective-permute-start | bytes 786440 | tf_op jit(solution)/shard_map/ppermute | solution.py:420
  44.3 4.5 %collective-permute-done.3.rest_7_ = bf16[8,16,1024]{2,1,0:T(8,128)(2,1)S(1)} collective-permute-done((bf16[8,16,1024]{2,1,0:T(8,128)(2,1)}, bf16[8,16,1024]{2,1,0:T(8,128)(2,1)S(1)}, u32[]{:S(2)}, u32[]{:S(2)}) %collective-permute-start.3) | collective-permute-done | bytes 262176 | tf_op jit(solution)/shard_map/ppermute | solution.py:420
  48.8 3.1 %collective-permute-done.4.rest_8_ = bf16[8,16,1024]{2,1,0:T(8,128)(2,1)S(1)} collective-permute-done((bf16[8,16,1024]{2,1,0:T(8,128)(2,1)}, bf16[8,16,1024]{2,1,0:T(8,128)(2,1)S(1)}, u32[]{:S(2)}, u32[]{:S(2)}) %collective-permute-start.4) | collective-permute-done | bytes 262176 | tf_op jit(solution)/shard_map/ppermute | solution.py:420
  51.9 3.2 %collective-permute-start.9 = (bf16[8,16,1024]{2,1,0:T(8,128)(2,1)}, bf16[8,16,1024]{2,1,0:T(8,128)(2,1)}, u32[]{:S(2)}, u32[]{:S(2)}) collective-permute-start(bf16[8,16,1024]{2,1,0:T(8,128)(2,1)} %get-tuple-element.85), channel_id=1, source_target_pairs={{0,13},{1,12},{2,15},{3,14},{4,9},{5,8},{6,11},{7,10},{8,5},{9,4},... | collective-permute-start | bytes 786440 | tf_op jit(solution)/shard_map/ppermute | solution.py:420
  56.6 4.4 %all-to-all-done.1.rows_hbm = bf16[16,16,1024]{2,1,0:T(8,128)(2,1)S(1)} async-done(((bf16[16,16,1024]{2,1,0:T(8,128)(2,1)}), bf16[16,16,1024]{2,1,0:T(8,128)(2,1)S(1)}, u32[]{:S(2)}, u32[]{:S(2)}) %all-to-all-start.1) | async-done | bytes 524320 | tf_op jit(solution)/shard_map/all_to_all | solution.py:423
  61.7 8.0 %shard_map.72 = bf16[128,16,1024]{2,1,0:T(8,128)(2,1)} custom-call(s32[16,2,128]{2,1,0:T(2,128)} %copy-done.1, s32[16,2,128]{2,1,0:T(2,128)} %copy-done.1, bf16[128,16,1024]{2,1,0:T(8,128)(2,1)} %store_hbm.3, bf16[16,16,1024]{2,1,0:T(8,128)(2,1)} %copy-done), custom_call_target="tpu_custom_call" | custom-call | bytes 8388608 | tf_op jit(solution)/shard_map/pallas_call | solution.py:497
  69.9 4.2 %collective-permute-start.11 = (bf16[8,16,1024]{2,1,0:T(8,128)(2,1)S(1)}, bf16[8,16,1024]{2,1,0:T(8,128)(2,1)}, u32[]{:S(2)}, u32[]{:S(2)}) collective-permute-start(bf16[8,16,1024]{2,1,0:T(8,128)(2,1)S(1)} %copy-done.17), channel_id=1, source_target_pairs={{0,10},{1,11},{2,8},{3,9},{4,14},{5,15},{6,12},{7,13},{8,2},{9,3},... | collective-permute-start | bytes 786440 | tf_op jit(solution)/shard_map/ppermute | solution.py:420
  74.1 2.1 %collective-permute-start.12 = (bf16[8,16,1024]{2,1,0:T(8,128)(2,1)S(1)}, bf16[8,16,1024]{2,1,0:T(8,128)(2,1)}, u32[]{:S(2)}, u32[]{:S(2)}) collective-permute-start(bf16[8,16,1024]{2,1,0:T(8,128)(2,1)S(1)} %copy-done.15), channel_id=1, source_target_pairs={{0,7},{1,6},{2,5},{3,4},{4,3},{5,2},{6,1},{7,0},{8,15},{9,14},{10,... | collective-permute-start | bytes 786440 | tf_op jit(solution)/shard_map/ppermute | solution.py:420
  76.2 1.4 %collective-permute-done.9.rest_7_ = bf16[8,16,1024]{2,1,0:T(8,128)(2,1)} collective-permute-done((bf16[8,16,1024]{2,1,0:T(8,128)(2,1)}, bf16[8,16,1024]{2,1,0:T(8,128)(2,1)}, u32[]{:S(2)}, u32[]{:S(2)}) %collective-permute-start.9) | collective-permute-done | bytes 262176 | tf_op jit(solution)/shard_map/ppermute | solution.py:420
  79.3 19.8 %shard_map.73 = (f32[5,4,128,384]{3,2,1,0:T(8,128)}, f32[5,8,384]{2,1,0:T(8,128)}) custom-call(s32[48]{0:T(128)} %get-tuple-element.97.place, s32[48]{0:T(128)} %copy-done.10, s32[5]{0:T(128)} %and_select_fusion.tiles, s32[5,1,128]{2,1,0:T(1,128)} %tile.9.rest_0_, s32[1,160]{1,0:T(1,128)} %rest_1_.2, bf16[160,6144]{1,0:T(8,128)(2,1)} %bitcast.66, ...), custom_call_target="tpu_custom_call" | custom-call | flops 4831838208 | bytes 7995392 | tf_op jit(solution)/shard_map/pallas_call | solution.py:318
  99.1 2.7 %collective-permute-start.15 = (bf16[8,16,1024]{2,1,0:T(8,128)(2,1)S(1)}, bf16[8,16,1024]{2,1,0:T(8,128)(2,1)S(1)}, u32[]{:S(2)}, u32[]{:S(2)}) collective-permute-start(bf16[8,16,1024]{2,1,0:T(8,128)(2,1)S(1)} %copy-done.12), channel_id=1, source_target_pairs={{0,11},{1,10},{2,9},{3,8},{4,15},{5,14},{6,13},{7,12},{8,3},{9,2},... | collective-permute-start | bytes 786440 | tf_op jit(solution)/shard_map/ppermute | solution.py:420
  102.5 18.3 %shard_map.74 = (f32[5,4,128,384]{3,2,1,0:T(8,128)}, f32[5,8,384]{2,1,0:T(8,128)}) custom-call(s32[64]{0:T(128)} %get-tuple-element.99.place, s32[64]{0:T(128)} %copy-done.9, s32[5]{0:T(128)} %and_select_fusion.1.tiles, s32[5,1,128]{2,1,0:T(1,128)} %tile.9.rest_0_, s32[1,160]{1,0:T(1,128)} %rest_1_.2, bf16[160,6144]{1,0:T(8,128)(2,1)} %bitcast.67, ...), custom_call_target="tpu_custom_call" | custom-call | flops 4831838208 | bytes 7995392 | tf_op jit(solution)/shard_map/pallas_call | solution.py:318
  120.8 3.8 %collective-permute-done.16.rest_6_ = bf16[8,16,1024]{2,1,0:T(8,128)(2,1)S(1)} collective-permute-done((bf16[8,16,1024]{2,1,0:T(8,128)(2,1)S(1)}, bf16[8,16,1024]{2,1,0:T(8,128)(2,1)S(1)}, u32[]{:S(2)}, u32[]{:S(2)}) %collective-permute-start.16) | collective-permute-done | bytes 262176 | tf_op jit(solution)/shard_map/ppermute | solution.py:420
  125.3 9.9 %shard_map.75 = bf16[160,6144]{1,0:T(8,128)(2,1)} custom-call(s32[16]{0:T(128)} %get-tuple-element.101.place, s32[16]{0:T(128)} %copy-done.6, s32[5]{0:T(128)} %and_select_fusion.2.tiles, s32[5,1,128]{2,1,0:T(1,128)} %tile.9.rest_0_, s32[1,160]{1,0:T(1,128)} %rest_1_.2, bf16[160,6144]{1,0:T(8,128)(2,1)} %bitcast.68, ...), custom_call_target="tpu_custom_call" | custom-call | flops 1207959552 | bytes 6422528 | tf_op jit(solution)/shard_map/pallas_call | solution.py:318
  (93 shorter events, 14.4 us)
Async XLA Ops:
  2.3 3.5 %collective-permute-start = (s32[1,2,128]{2,1,0:T(2,128)}, s32[1,2,128]{2,1,0:T(2,128)S(1)}, u32[]{:S(2)}, u32[]{:S(2)}) collective-permute-start(s32[1,2,128]{2,1,0:T(2,128)} %get-tuple-element.49), channel_id=1, source_target_pairs={{0,8},{1,9},{2,10},{3,11},{4,12},{5,13},{6,14},{7,15},{8,0},{9,1},... | collective-permute-start | bytes 3080 | tf_op jit(solution)/shard_map/ppermute | solution.py:420
  4.6 2.6 %collective-permute-start.1 = (s32[1,2,128]{2,1,0:T(2,128)}, s32[1,2,128]{2,1,0:T(2,128)S(1)}, u32[]{:S(2)}, u32[]{:S(2)}) collective-permute-start(s32[1,2,128]{2,1,0:T(2,128)} %get-tuple-element.50), channel_id=1, source_target_pairs={{0,12},{1,13},{2,14},{3,15},{4,8},{5,9},{6,10},{7,11},{8,4},{9,5},... | collective-permute-start | bytes 3080 | tf_op jit(solution)/shard_map/ppermute | solution.py:420
  10.3 12.6 %all-to-all-start = ((s32[16,2,128]{2,1,0:T(2,128)}), s32[16,2,128]{2,1,0:T(2,128)S(1)}, u32[]{:S(2)}, u32[]{:S(2)}) async-start(s32[16,2,128]{2,1,0:T(2,128)} %get-tuple-element.54), calls=%async_computation | async-start | bytes 32768 | tf_op jit(solution)/shard_map/all_to_all | solution.py:423
  17.9 24.4 %collective-permute-start.2 = (bf16[8,16,1024]{2,1,0:T(8,128)(2,1)}, bf16[8,16,1024]{2,1,0:T(8,128)(2,1)S(1)}, u32[]{:S(2)}, u32[]{:S(2)}) collective-permute-start(bf16[8,16,1024]{2,1,0:T(8,128)(2,1)} %get-tuple-element.76), channel_id=1, source_target_pairs={{0,8},{1,9},{2,10},{3,11},{4,12},{5,13},{6,14},{7,15},{8,0},{9,1},... | collective-permute-start | bytes 786440 | tf_op jit(solution)/shard_map/ppermute | solution.py:420
  20.0 28.8 %collective-permute-start.3 = (bf16[8,16,1024]{2,1,0:T(8,128)(2,1)}, bf16[8,16,1024]{2,1,0:T(8,128)(2,1)S(1)}, u32[]{:S(2)}, u32[]{:S(2)}) collective-permute-start(bf16[8,16,1024]{2,1,0:T(8,128)(2,1)} %get-tuple-element.77), channel_id=1, source_target_pairs={{0,12},{1,13},{2,14},{3,15},{4,8},{5,9},{6,10},{7,11},{8,4},{9,5},... | collective-permute-start | bytes 786440 | tf_op jit(solution)/shard_map/ppermute | solution.py:420
  30.1 30.8 %all-to-all-start.1 = ((bf16[16,16,1024]{2,1,0:T(8,128)(2,1)}), bf16[16,16,1024]{2,1,0:T(8,128)(2,1)S(1)}, u32[]{:S(2)}, u32[]{:S(2)}) async-start(bf16[16,16,1024]{2,1,0:T(8,128)(2,1)} %shard_map.71), calls=%async_computation.1 | async-start | bytes 1048576 | tf_op jit(solution)/shard_map/all_to_all | solution.py:423
  36.4 15.5 %collective-permute-start.4 = (bf16[8,16,1024]{2,1,0:T(8,128)(2,1)}, bf16[8,16,1024]{2,1,0:T(8,128)(2,1)S(1)}, u32[]{:S(2)}, u32[]{:S(2)}) collective-permute-start(bf16[8,16,1024]{2,1,0:T(8,128)(2,1)} %get-tuple-element.78), channel_id=1, source_target_pairs={{0,4},{1,5},{2,6},{3,7},{4,0},{5,1},{6,2},{7,3},{8,12},{9,13},{10,... | collective-permute-start | bytes 786440 | tf_op jit(solution)/shard_map/ppermute | solution.py:420
  36.5 33.3 %collective-permute-start.5 = (bf16[8,16,1024]{2,1,0:T(8,128)(2,1)}, bf16[8,16,1024]{2,1,0:T(8,128)(2,1)S(1)}, u32[]{:S(2)}, u32[]{:S(2)}) collective-permute-start(bf16[8,16,1024]{2,1,0:T(8,128)(2,1)} %get-tuple-element.79), channel_id=1, source_target_pairs={{0,2},{1,3},{2,0},{3,1},{4,6},{5,7},{6,4},{7,5},{8,10},{9,11},{10,... | collective-permute-start | bytes 786440 | tf_op jit(solution)/shard_map/ppermute | solution.py:420
  37.9 32.0 %collective-permute-start.6 = (bf16[8,16,1024]{2,1,0:T(8,128)(2,1)}, bf16[8,16,1024]{2,1,0:T(8,128)(2,1)S(1)}, u32[]{:S(2)}, u32[]{:S(2)}) collective-permute-start(bf16[8,16,1024]{2,1,0:T(8,128)(2,1)} %get-tuple-element.80), channel_id=1, source_target_pairs={{0,1},{1,0},{2,3},{3,2},{4,5},{5,4},{6,7},{7,6},{8,9},{9,8},{10,11... | collective-permute-start | bytes 786440 | tf_op jit(solution)/shard_map/ppermute | solution.py:420
  39.5 30.2 %copy-start.10 = (s32[48]{0:T(128)}, s32[48]{0:T(128)S(1)}, u32[]{:S(2)}) copy-start(s32[48]{0:T(128)S(1)} %get-tuple-element.96.page_number) | copy-start | bytes 580
  40.2 29.6 %copy-start.9 = (s32[64]{0:T(128)}, s32[64]{0:T(128)S(1)}, u32[]{:S(2)}) copy-start(s32[64]{0:T(128)S(1)} %get-tuple-element.98.page_number) | copy-start | bytes 772
  41.0 28.8 %copy-start.6 = (s32[16]{0:T(128)}, s32[16]{0:T(128)S(1)}, u32[]{:S(2)}) copy-start(s32[16]{0:T(128)S(1)} %get-tuple-element.100.page_number) | copy-start | bytes 196
  42.3 36.9 %copy-start.16 = (bf16[8,16,1024]{2,1,0:T(8,128)(2,1)}, bf16[8,16,1024]{2,1,0:T(8,128)(2,1)S(1)}, u32[]{:S(2)}) copy-start(bf16[8,16,1024]{2,1,0:T(8,128)(2,1)S(1)} %collective-permute-done.2.rest_6_) | copy-start | bytes 786436
  42.3 31.9 %collective-permute-start.7 = (bf16[8,16,1024]{2,1,0:T(8,128)(2,1)}, bf16[8,16,1024]{2,1,0:T(8,128)(2,1)S(1)}, u32[]{:S(2)}, u32[]{:S(2)}) collective-permute-start(bf16[8,16,1024]{2,1,0:T(8,128)(2,1)} %get-tuple-element.83), channel_id=1, source_target_pairs={{0,9},{1,8},{2,11},{3,10},{4,13},{5,12},{6,15},{7,14},{8,1},{9,0},... | collective-permute-start | bytes 786440 | tf_op jit(solution)/shard_map/ppermute | solution.py:420
  48.8 30.4 %copy-start.18 = (bf16[8,16,1024]{2,1,0:T(8,128)(2,1)}, bf16[8,16,1024]{2,1,0:T(8,128)(2,1)S(1)}, u32[]{:S(2)}) copy-start(bf16[8,16,1024]{2,1,0:T(8,128)(2,1)S(1)} %collective-permute-done.3.rest_7_) | copy-start | bytes 786436
  48.8 27.4 %collective-permute-start.8 = (bf16[8,16,1024]{2,1,0:T(8,128)(2,1)}, bf16[8,16,1024]{2,1,0:T(8,128)(2,1)}, u32[]{:S(2)}, u32[]{:S(2)}) collective-permute-start(bf16[8,16,1024]{2,1,0:T(8,128)(2,1)} %get-tuple-element.84), channel_id=1, source_target_pairs={{0,5},{1,4},{2,7},{3,6},{4,1},{5,0},{6,3},{7,2},{8,13},{9,12},{10,... | collective-permute-start | bytes 786440 | tf_op jit(solution)/shard_map/ppermute | solution.py:420
  51.9 25.7 %collective-permute-start.9 = (bf16[8,16,1024]{2,1,0:T(8,128)(2,1)}, bf16[8,16,1024]{2,1,0:T(8,128)(2,1)}, u32[]{:S(2)}, u32[]{:S(2)}) collective-permute-start(bf16[8,16,1024]{2,1,0:T(8,128)(2,1)} %get-tuple-element.85), channel_id=1, source_target_pairs={{0,13},{1,12},{2,15},{3,14},{4,9},{5,8},{6,11},{7,10},{8,5},{9,4},... | collective-permute-start | bytes 786440 | tf_op jit(solution)/shard_map/ppermute | solution.py:420
  69.8 29.3 %collective-permute-start.10 = (bf16[8,16,1024]{2,1,0:T(8,128)(2,1)S(1)}, bf16[8,16,1024]{2,1,0:T(8,128)(2,1)}, u32[]{:S(2)}, u32[]{:S(2)}) collective-permute-start(bf16[8,16,1024]{2,1,0:T(8,128)(2,1)S(1)} %copy-done.19), channel_id=1, source_target_pairs={{0,6},{1,7},{2,4},{3,5},{4,2},{5,3},{6,0},{7,1},{8,14},{9,15},{10,... | collective-permute-start | bytes 786440 | tf_op jit(solution)/shard_map/ppermute | solution.py:420
  69.9 31.8 %collective-permute-start.11 = (bf16[8,16,1024]{2,1,0:T(8,128)(2,1)S(1)}, bf16[8,16,1024]{2,1,0:T(8,128)(2,1)}, u32[]{:S(2)}, u32[]{:S(2)}) collective-permute-start(bf16[8,16,1024]{2,1,0:T(8,128)(2,1)S(1)} %copy-done.17), channel_id=1, source_target_pairs={{0,10},{1,11},{2,8},{3,9},{4,14},{5,15},{6,12},{7,13},{8,2},{9,3},... | collective-permute-start | bytes 786440 | tf_op jit(solution)/shard_map/ppermute | solution.py:420
  74.1 27.6 %collective-permute-start.12 = (bf16[8,16,1024]{2,1,0:T(8,128)(2,1)S(1)}, bf16[8,16,1024]{2,1,0:T(8,128)(2,1)}, u32[]{:S(2)}, u32[]{:S(2)}) collective-permute-start(bf16[8,16,1024]{2,1,0:T(8,128)(2,1)S(1)} %copy-done.15), channel_id=1, source_target_pairs={{0,7},{1,6},{2,5},{3,4},{4,3},{5,2},{6,1},{7,0},{8,15},{9,14},{10,... | collective-permute-start | bytes 786440 | tf_op jit(solution)/shard_map/ppermute | solution.py:420
  76.2 25.5 %collective-permute-start.13 = (bf16[8,16,1024]{2,1,0:T(8,128)(2,1)S(1)}, bf16[8,16,1024]{2,1,0:T(8,128)(2,1)}, u32[]{:S(2)}, u32[]{:S(2)}) collective-permute-start(bf16[8,16,1024]{2,1,0:T(8,128)(2,1)S(1)} %copy-done.14), channel_id=1, source_target_pairs={{0,14},{1,15},{2,12},{3,13},{4,10},{5,11},{6,8},{7,9},{8,6},{9,7},... | collective-permute-start | bytes 786440 | tf_op jit(solution)/shard_map/ppermute | solution.py:420
  77.6 24.8 %collective-permute-start.14 = (bf16[8,16,1024]{2,1,0:T(8,128)(2,1)S(1)}, bf16[8,16,1024]{2,1,0:T(8,128)(2,1)}, u32[]{:S(2)}, u32[]{:S(2)}) collective-permute-start(bf16[8,16,1024]{2,1,0:T(8,128)(2,1)S(1)} %copy-done.13), channel_id=1, source_target_pairs={{0,3},{1,2},{2,1},{3,0},{4,7},{5,6},{6,5},{7,4},{8,11},{9,10},{10,... | collective-permute-start | bytes 786440 | tf_op jit(solution)/shard_map/ppermute | solution.py:420
  99.1 21.7 %collective-permute-start.15 = (bf16[8,16,1024]{2,1,0:T(8,128)(2,1)S(1)}, bf16[8,16,1024]{2,1,0:T(8,128)(2,1)S(1)}, u32[]{:S(2)}, u32[]{:S(2)}) collective-permute-start(bf16[8,16,1024]{2,1,0:T(8,128)(2,1)S(1)} %copy-done.12), channel_id=1, source_target_pairs={{0,11},{1,10},{2,9},{3,8},{4,15},{5,14},{6,13},{7,12},{8,3},{9,2},... | collective-permute-start | bytes 786440 | tf_op jit(solution)/shard_map/ppermute | solution.py:420
  101.7 22.9 %collective-permute-start.16 = (bf16[8,16,1024]{2,1,0:T(8,128)(2,1)S(1)}, bf16[8,16,1024]{2,1,0:T(8,128)(2,1)S(1)}, u32[]{:S(2)}, u32[]{:S(2)}) collective-permute-start(bf16[8,16,1024]{2,1,0:T(8,128)(2,1)S(1)} %copy-done.11), channel_id=1, source_target_pairs={{0,15},{1,14},{2,13},{3,12},{4,11},{5,10},{6,9},{7,8},{8,7},{9,6},... | collective-permute-start | bytes 786440 | tf_op jit(solution)/shard_map/ppermute | solution.py:420
  (19 other events, 254.7 us)

commit v23 on v22

--- a/solution.py
+++ b/solution.py
@@ -409,7 +409,7 @@
     wide = pltpu.VMEM((8, -(-picked // LANES) * LANES), jnp.int32)
     if holders == 16:
         first = (8, 12)
-        groups = [(0, 8, 12, 4, 2, 1), (9, 5, 13, 6, 10, 7, 14, 3), (11, 15)]
+        groups = [(0, 8, 12, 4, 2, 1), (9, 3, 13, 5, 10, 6, 14, 7), (11, 15)]
         others = [d for group in groups for d in group if d not in first]
     else:
         first = ()

time: 137 us -> 146 us (1.066)
  the two profiles are of different devices: /device:TPU:9 before, /device:TPU:19 now
where the time goes in v23:
time: 146 us; the launch traced here: 145 us
  Pallas kernels  67.3 us (46%)
  starting transfers between devices  35.8 us (25%)
  waiting for transfers between devices  30.8 us (21%)
  local copies, waits for them, and re-layouts  5.46 us (4%)
  other arithmetic  5.03 us (3%)
    pallas_call x3, Pallas kernels, attend(): pl.pallas_call(functools.partial(attend_kernel, first, last, tile_pages,...  47.9 us
    ppermute x17, starting transfers between devices, swap(): return lax.ppermute(x, 'store', [(h, h ^ d) for h in range(holders)])  20.9 us
    ppermute x17, waiting for transfers between devices, swap(): return lax.ppermute(x, 'store', [(h, h ^ d) for h in range(holders)])  20.3 us
    all_to_all x2, starting transfers between devices, exchange(): return lax.all_to_all(x, 'store', split_axis=0, concat_axis=0, tiled=True)  14.9 us
    all_to_all x2, waiting for transfers between devices, exchange(): return lax.all_to_all(x, 'store', split_axis=0, concat_axis=0, tiled=True)  10.5 us
    pallas_call x1, Pallas kernels, per_device(): pl.pallas_call(write_back_kernel, grid_spec=pltpu.PrefetchScalarGridSpec(...  8.02 us
    pallas_call x1, Pallas kernels, per_device(): pl.pallas_call(functools.partial(gather_kernel, capacity, others), grid_s...  4.9 us
    unnamed x49, local copies, waits for them, and re-layouts  3.34 us
  transfers between devices with their start and end apart: 19, of which 6 were waited for; matrix products, arithmetic and copies ran while one was open for 5% of the time, Pallas kernels for 37%

profile of v23, /device:TPU:19, one launch (start us, length us, event | category | flops | bytes accessed | tf_op | source)
XLA Modules:
  0.0 145.3 jit_solution(4546200611100312953)
XLA Ops:
  0.6 1.7 %shard_map.68 = (s32[16,2,128]{2,1,0:T(2,128)}, s32[1,2,128]{2,1,0:T(2,128)}, s32[1,2,128]{2,1,0:T(2,128)}) custom-call(s32[1]{0:T(128)} %bitcast.own, s32[1,128]{1,0:T(1,128)} %table_ref.2, s32[1,160]{1,0:T(1,128)} %rest_1_.2), custom_call_target="tpu_custom_call" | custom-call | tf_op jit(solution)/shard_map/pallas_call | solution.py:425
  2.3 2.4 %collective-permute-start.1 = (s32[1,2,128]{2,1,0:T(2,128)}, s32[1,2,128]{2,1,0:T(2,128)S(1)}, u32[]{:S(2)}, u32[]{:S(2)}) collective-permute-start(s32[1,2,128]{2,1,0:T(2,128)} %get-tuple-element.50), channel_id=1, source_target_pairs={{0,12},{1,13},{2,14},{3,15},{4,8},{5,9},{6,10},{7,11},{8,4},{9,5},... | collective-permute-start | bytes 3080 | tf_op jit(solution)/shard_map/ppermute | solution.py:420
  4.8 1.0 collective-permute-done.refs_0_
  7.0 2.5 %shard_map.69 = (bf16[8,16,1024]{2,1,0:T(8,128)(2,1)}, bf16[8,16,1024]{2,1,0:T(8,128)(2,1)}) custom-call(s32[1,2,128]{2,1,0:T(2,128)} %copy-done.7, s32[1,2,128]{2,1,0:T(2,128)} %copy-done.8, bf16[128,16,1024]{2,1,0:T(8,128)(2,1)} %store_hbm.3), custom_call_target="tpu_custom_call" | custom-call | tf_op jit(solution)/shard_map/pallas_call | solution.py:443
  9.5 8.3 %all-to-all-start = ((s32[16,2,128]{2,1,0:T(2,128)}), s32[16,2,128]{2,1,0:T(2,128)S(1)}, u32[]{:S(2)}, u32[]{:S(2)}) async-start(s32[16,2,128]{2,1,0:T(2,128)} %get-tuple-element.54), calls=%async_computation | async-start | bytes 32768 | tf_op jit(solution)/shard_map/all_to_all | solution.py:423
  18.0 2.1 %collective-permute-start.3 = (bf16[8,16,1024]{2,1,0:T(8,128)(2,1)}, bf16[8,16,1024]{2,1,0:T(8,128)(2,1)S(1)}, u32[]{:S(2)}, u32[]{:S(2)}) collective-permute-start(bf16[8,16,1024]{2,1,0:T(8,128)(2,1)} %get-tuple-element.77), channel_id=1, source_target_pairs={{0,12},{1,13},{2,14},{3,15},{4,8},{5,9},{6,10},{7,11},{8,4},{9,5},... | collective-permute-start | bytes 786440 | tf_op jit(solution)/shard_map/ppermute | solution.py:420
  20.1 2.4 %shard_map.71 = bf16[16,16,1024]{2,1,0:T(8,128)(2,1)} custom-call(s32[1,128]{1,0:T(1,128)} %table_ref.2, s32[1,160]{1,0:T(1,128)} %rest_1_.2, bf16[160,1024]{1,0:T(8,128)(2,1)} %bitcast.70), custom_call_target="tpu_custom_call" | custom-call | tf_op jit(solution)/shard_map/pallas_call | solution.py:467
  23.1 4.9 %shard_map.70 = (bf16[8,16,1024]{2,1,0:T(8,128)(2,1)}, bf16[8,16,1024]{2,1,0:T(8,128)(2,1)}, bf16[8,16,1024]{2,1,0:T(8,128)(2,1)}, bf16[8,16,1024]{2,1,0:T(8,128...) custom-call(s32[1]{0:T(128)} %bitcast.own, ...), custom_call_target="tpu_custom_call" | custom-call | tf_op jit(solution)/shard_map/pallas_call | solution.py:476
  29.7 6.6 %all-to-all-start.1 = ((bf16[16,16,1024]{2,1,0:T(8,128)(2,1)}), bf16[16,16,1024]{2,1,0:T(8,128)(2,1)S(1)}, u32[]{:S(2)}, u32[]{:S(2)}) async-start(bf16[16,16,1024]{2,1,0:T(8,128)(2,1)} %shard_map.71), calls=%async_computation.1 | async-start | bytes 1048576 | tf_op jit(solution)/shard_map/all_to_all | solution.py:423
  36.3 1.2 collective-permute-start.4
  37.8 0.9 collective-permute-start.6
  42.3 7.3 %collective-permute-done.3.rest_7_ = bf16[8,16,1024]{2,1,0:T(8,128)(2,1)S(1)} collective-permute-done((bf16[8,16,1024]{2,1,0:T(8,128)(2,1)}, bf16[8,16,1024]{2,1,0:T(8,128)(2,1)S(1)}, u32[]{:S(2)}, u32[]{:S(2)}) %collective-permute-start.3) | collective-permute-done | bytes 262176 | tf_op jit(solution)/shard_map/ppermute | solution.py:420
  50.3 2.3 %collective-permute-done.4.rest_8_ = bf16[8,16,1024]{2,1,0:T(8,128)(2,1)S(1)} collective-permute-done((bf16[8,16,1024]{2,1,0:T(8,128)(2,1)}, bf16[8,16,1024]{2,1,0:T(8,128)(2,1)S(1)}, u32[]{:S(2)}, u32[]{:S(2)}) %collective-permute-start.4) | collective-permute-done | bytes 262176 | tf_op jit(solution)/shard_map/ppermute | solution.py:420
  54.6 10.5 %all-to-all-done.1.rows_hbm = bf16[16,16,1024]{2,1,0:T(8,128)(2,1)S(1)} async-done(((bf16[16,16,1024]{2,1,0:T(8,128)(2,1)}), bf16[16,16,1024]{2,1,0:T(8,128)(2,1)S(1)}, u32[]{:S(2)}, u32[]{:S(2)}) %all-to-all-start.1) | async-done | bytes 524320 | tf_op jit(solution)/shard_map/all_to_all | solution.py:423
  65.8 8.0 %shard_map.72 = bf16[128,16,1024]{2,1,0:T(8,128)(2,1)} custom-call(s32[16,2,128]{2,1,0:T(2,128)} %copy-done.1, s32[16,2,128]{2,1,0:T(2,128)} %copy-done.1, bf16[128,16,1024]{2,1,0:T(8,128)(2,1)} %store_hbm.3, bf16[16,16,1024]{2,1,0:T(8,128)(2,1)} %copy-done), custom_call_target="tpu_custom_call" | custom-call | bytes 8388608 | tf_op jit(solution)/shard_map/pallas_call | solution.py:497
  73.9 2.9 %collective-permute-start.10 = (bf16[8,16,1024]{2,1,0:T(8,128)(2,1)S(1)}, bf16[8,16,1024]{2,1,0:T(8,128)(2,1)}, u32[]{:S(2)}, u32[]{:S(2)}) collective-permute-start(bf16[8,16,1024]{2,1,0:T(8,128)(2,1)S(1)} %copy-done.19), channel_id=1, source_target_pairs={{0,5},{1,4},{2,7},{3,6},{4,1},{5,0},{6,3},{7,2},{8,13},{9,12},{10,... | collective-permute-start | bytes 786440 | tf_op jit(solution)/shard_map/ppermute | solution.py:420
  77.0 1.4 collective-permute-start.12
  78.4 1.7 %collective-permute-start.13 = (bf16[8,16,1024]{2,1,0:T(8,128)(2,1)S(1)}, bf16[8,16,1024]{2,1,0:T(8,128)(2,1)}, u32[]{:S(2)}, u32[]{:S(2)}) collective-permute-start(bf16[8,16,1024]{2,1,0:T(8,128)(2,1)S(1)} %copy-done.14), channel_id=1, source_target_pairs={{0,14},{1,15},{2,12},{3,13},{4,10},{5,11},{6,8},{7,9},{8,6},{9,7},... | collective-permute-start | bytes 786440 | tf_op jit(solution)/shard_map/ppermute | solution.py:420
  80.0 3.2 %collective-permute-start.14 = (bf16[8,16,1024]{2,1,0:T(8,128)(2,1)S(1)}, bf16[8,16,1024]{2,1,0:T(8,128)(2,1)}, u32[]{:S(2)}, u32[]{:S(2)}) collective-permute-start(bf16[8,16,1024]{2,1,0:T(8,128)(2,1)S(1)} %copy-done.13), channel_id=1, source_target_pairs={{0,7},{1,6},{2,5},{3,4},{4,3},{5,2},{6,1},{7,0},{8,15},{9,14},{10,... | collective-permute-start | bytes 786440 | tf_op jit(solution)/shard_map/ppermute | solution.py:420
  84.0 19.8 %shard_map.73 = (f32[5,4,128,384]{3,2,1,0:T(8,128)}, f32[5,8,384]{2,1,0:T(8,128)}) custom-call(s32[48]{0:T(128)} %get-tuple-element.97.place, s32[48]{0:T(128)} %copy-done.10, s32[5]{0:T(128)} %and_select_fusion.tiles, s32[5,1,128]{2,1,0:T(1,128)} %tile.9.rest_0_, s32[1,160]{1,0:T(1,128)} %rest_1_.2, bf16[160,6144]{1,0:T(8,128)(2,1)} %bitcast.66, ...), custom_call_target="tpu_custom_call" | custom-call | flops 4831838208 | bytes 7995392 | tf_op jit(solution)/shard_map/pallas_call | solution.py:318
  103.9 2.9 %collective-permute-start.16 = (bf16[8,16,1024]{2,1,0:T(8,128)(2,1)S(1)}, bf16[8,16,1024]{2,1,0:T(8,128)(2,1)S(1)}, u32[]{:S(2)}, u32[]{:S(2)}) collective-permute-start(bf16[8,16,1024]{2,1,0:T(8,128)(2,1)S(1)} %copy-done.11), channel_id=1, source_target_pairs={{0,15},{1,14},{2,13},{3,12},{4,11},{5,10},{6,9},{7,8},{8,7},{9,6},... | collective-permute-start | bytes 786440 | tf_op jit(solution)/shard_map/ppermute | solution.py:420
  106.8 9.6 %collective-permute-done.14.rest_12_ = bf16[8,16,1024]{2,1,0:T(8,128)(2,1)} collective-permute-done((bf16[8,16,1024]{2,1,0:T(8,128)(2,1)S(1)}, bf16[8,16,1024]{2,1,0:T(8,128)(2,1)}, u32[]{:S(2)}, u32[]{:S(2)}) %collective-permute-start.14) | collective-permute-done | bytes 262176 | tf_op jit(solution)/shard_map/ppermute | solution.py:420
  116.4 18.3 %shard_map.74 = (f32[5,4,128,384]{3,2,1,0:T(8,128)}, f32[5,8,384]{2,1,0:T(8,128)}) custom-call(s32[64]{0:T(128)} %get-tuple-element.99.place, s32[64]{0:T(128)} %copy-done.9, s32[5]{0:T(128)} %and_select_fusion.1.tiles, s32[5,1,128]{2,1,0:T(1,128)} %tile.9.rest_0_, s32[1,160]{1,0:T(1,128)} %rest_1_.2, bf16[160,6144]{1,0:T(8,128)(2,1)} %bitcast.67, ...), custom_call_target="tpu_custom_call" | custom-call | flops 4831838208 | bytes 7995392 | tf_op jit(solution)/shard_map/pallas_call | solution.py:318
  135.5 9.9 %shard_map.75 = bf16[160,6144]{1,0:T(8,128)(2,1)} custom-call(s32[16]{0:T(128)} %get-tuple-element.101.place, s32[16]{0:T(128)} %copy-done.6, s32[5]{0:T(128)} %and_select_fusion.2.tiles, s32[5,1,128]{2,1,0:T(1,128)} %tile.9.rest_0_, s32[1,160]{1,0:T(1,128)} %rest_1_.2, bf16[160,6144]{1,0:T(8,128)(2,1)} %bitcast.68, ...), custom_call_target="tpu_custom_call" | custom-call | flops 1207959552 | bytes 6422528 | tf_op jit(solution)/shard_map/pallas_call | solution.py:318
  (93 shorter events, 12.8 us)
Async XLA Ops:
  2.3 3.5 %collective-permute-start = (s32[1,2,128]{2,1,0:T(2,128)}, s32[1,2,128]{2,1,0:T(2,128)S(1)}, u32[]{:S(2)}, u32[]{:S(2)}) collective-permute-start(s32[1,2,128]{2,1,0:T(2,128)} %get-tuple-element.49), channel_id=1, source_target_pairs={{0,8},{1,9},{2,10},{3,11},{4,12},{5,13},{6,14},{7,15},{8,0},{9,1},... | collective-permute-start | bytes 3080 | tf_op jit(solution)/shard_map/ppermute | solution.py:420
  2.3 3.6 %collective-permute-start.1 = (s32[1,2,128]{2,1,0:T(2,128)}, s32[1,2,128]{2,1,0:T(2,128)S(1)}, u32[]{:S(2)}, u32[]{:S(2)}) collective-permute-start(s32[1,2,128]{2,1,0:T(2,128)} %get-tuple-element.50), channel_id=1, source_target_pairs={{0,12},{1,13},{2,14},{3,15},{4,8},{5,9},{6,10},{7,11},{8,4},{9,5},... | collective-permute-start | bytes 3080 | tf_op jit(solution)/shard_map/ppermute | solution.py:420
  9.5 13.0 %all-to-all-start = ((s32[16,2,128]{2,1,0:T(2,128)}), s32[16,2,128]{2,1,0:T(2,128)S(1)}, u32[]{:S(2)}, u32[]{:S(2)}) async-start(s32[16,2,128]{2,1,0:T(2,128)} %get-tuple-element.54), calls=%async_computation | async-start | bytes 32768 | tf_op jit(solution)/shard_map/all_to_all | solution.py:423
  17.7 24.4 %collective-permute-start.2 = (bf16[8,16,1024]{2,1,0:T(8,128)(2,1)}, bf16[8,16,1024]{2,1,0:T(8,128)(2,1)S(1)}, u32[]{:S(2)}, u32[]{:S(2)}) collective-permute-start(bf16[8,16,1024]{2,1,0:T(8,128)(2,1)} %get-tuple-element.76), channel_id=1, source_target_pairs={{0,8},{1,9},{2,10},{3,11},{4,12},{5,13},{6,14},{7,15},{8,0},{9,1},... | collective-permute-start | bytes 786440 | tf_op jit(solution)/shard_map/ppermute | solution.py:420
  18.0 31.6 %collective-permute-start.3 = (bf16[8,16,1024]{2,1,0:T(8,128)(2,1)}, bf16[8,16,1024]{2,1,0:T(8,128)(2,1)S(1)}, u32[]{:S(2)}, u32[]{:S(2)}) collective-permute-start(bf16[8,16,1024]{2,1,0:T(8,128)(2,1)} %get-tuple-element.77), channel_id=1, source_target_pairs={{0,12},{1,13},{2,14},{3,15},{4,8},{5,9},{6,10},{7,11},{8,4},{9,5},... | collective-permute-start | bytes 786440 | tf_op jit(solution)/shard_map/ppermute | solution.py:420
  29.7 35.3 %all-to-all-start.1 = ((bf16[16,16,1024]{2,1,0:T(8,128)(2,1)}), bf16[16,16,1024]{2,1,0:T(8,128)(2,1)S(1)}, u32[]{:S(2)}, u32[]{:S(2)}) async-start(bf16[16,16,1024]{2,1,0:T(8,128)(2,1)} %shard_map.71), calls=%async_computation.1 | async-start | bytes 1048576 | tf_op jit(solution)/shard_map/all_to_all | solution.py:423
  36.3 16.3 %collective-permute-start.4 = (bf16[8,16,1024]{2,1,0:T(8,128)(2,1)}, bf16[8,16,1024]{2,1,0:T(8,128)(2,1)S(1)}, u32[]{:S(2)}, u32[]{:S(2)}) collective-permute-start(bf16[8,16,1024]{2,1,0:T(8,128)(2,1)} %get-tuple-element.78), channel_id=1, source_target_pairs={{0,4},{1,5},{2,6},{3,7},{4,0},{5,1},{6,2},{7,3},{8,12},{9,13},{10,... | collective-permute-start | bytes 786440 | tf_op jit(solution)/shard_map/ppermute | solution.py:420
  37.5 36.4 %collective-permute-start.5 = (bf16[8,16,1024]{2,1,0:T(8,128)(2,1)}, bf16[8,16,1024]{2,1,0:T(8,128)(2,1)S(1)}, u32[]{:S(2)}, u32[]{:S(2)}) collective-permute-start(bf16[8,16,1024]{2,1,0:T(8,128)(2,1)} %get-tuple-element.79), channel_id=1, source_target_pairs={{0,2},{1,3},{2,0},{3,1},{4,6},{5,7},{6,4},{7,5},{8,10},{9,11},{10,... | collective-permute-start | bytes 786440 | tf_op jit(solution)/shard_map/ppermute | solution.py:420
  37.8 39.1 %collective-permute-start.6 = (bf16[8,16,1024]{2,1,0:T(8,128)(2,1)}, bf16[8,16,1024]{2,1,0:T(8,128)(2,1)S(1)}, u32[]{:S(2)}, u32[]{:S(2)}) collective-permute-start(bf16[8,16,1024]{2,1,0:T(8,128)(2,1)} %get-tuple-element.80), channel_id=1, source_target_pairs={{0,1},{1,0},{2,3},{3,2},{4,5},{5,4},{6,7},{7,6},{8,9},{9,8},{10,11... | collective-permute-start | bytes 786440 | tf_op jit(solution)/shard_map/ppermute | solution.py:420
  39.4 34.5 %copy-start.10 = (s32[48]{0:T(128)}, s32[48]{0:T(128)S(1)}, u32[]{:S(2)}) copy-start(s32[48]{0:T(128)S(1)} %get-tuple-element.96.page_number) | copy-start | bytes 580
  40.0 33.8 %copy-start.9 = (s32[64]{0:T(128)}, s32[64]{0:T(128)S(1)}, u32[]{:S(2)}) copy-start(s32[64]{0:T(128)S(1)} %get-tuple-element.98.page_number) | copy-start | bytes 772
  40.8 33.0 %copy-start.6 = (s32[16]{0:T(128)}, s32[16]{0:T(128)S(1)}, u32[]{:S(2)}) copy-start(s32[16]{0:T(128)S(1)} %get-tuple-element.100.page_number) | copy-start | bytes 196
  42.1 41.8 %copy-start.16 = (bf16[8,16,1024]{2,1,0:T(8,128)(2,1)}, bf16[8,16,1024]{2,1,0:T(8,128)(2,1)S(1)}, u32[]{:S(2)}) copy-start(bf16[8,16,1024]{2,1,0:T(8,128)(2,1)S(1)} %collective-permute-done.2.rest_6_) | copy-start | bytes 786436
  42.1 34.8 %collective-permute-start.7 = (bf16[8,16,1024]{2,1,0:T(8,128)(2,1)}, bf16[8,16,1024]{2,1,0:T(8,128)(2,1)S(1)}, u32[]{:S(2)}, u32[]{:S(2)}) collective-permute-start(bf16[8,16,1024]{2,1,0:T(8,128)(2,1)} %get-tuple-element.83), channel_id=1, source_target_pairs={{0,9},{1,8},{2,11},{3,10},{4,13},{5,12},{6,15},{7,14},{8,1},{9,0},... | collective-permute-start | bytes 786440 | tf_op jit(solution)/shard_map/ppermute | solution.py:420
  49.6 34.4 %copy-start.18 = (bf16[8,16,1024]{2,1,0:T(8,128)(2,1)}, bf16[8,16,1024]{2,1,0:T(8,128)(2,1)S(1)}, u32[]{:S(2)}) copy-start(bf16[8,16,1024]{2,1,0:T(8,128)(2,1)S(1)} %collective-permute-done.3.rest_7_) | copy-start | bytes 786436
  49.6 28.8 %collective-permute-start.8 = (bf16[8,16,1024]{2,1,0:T(8,128)(2,1)}, bf16[8,16,1024]{2,1,0:T(8,128)(2,1)}, u32[]{:S(2)}, u32[]{:S(2)}) collective-permute-start(bf16[8,16,1024]{2,1,0:T(8,128)(2,1)} %get-tuple-element.84), channel_id=1, source_target_pairs={{0,3},{1,2},{2,1},{3,0},{4,7},{5,6},{6,5},{7,4},{8,11},{9,10},{10,... | collective-permute-start | bytes 786440 | tf_op jit(solution)/shard_map/ppermute | solution.py:420
  52.6 27.5 %collective-permute-start.9 = (bf16[8,16,1024]{2,1,0:T(8,128)(2,1)}, bf16[8,16,1024]{2,1,0:T(8,128)(2,1)}, u32[]{:S(2)}, u32[]{:S(2)}) collective-permute-start(bf16[8,16,1024]{2,1,0:T(8,128)(2,1)} %get-tuple-element.85), channel_id=1, source_target_pairs={{0,13},{1,12},{2,15},{3,14},{4,9},{5,8},{6,11},{7,10},{8,5},{9,4},... | collective-permute-start | bytes 786440 | tf_op jit(solution)/shard_map/ppermute | solution.py:420
  73.9 29.9 %collective-permute-start.10 = (bf16[8,16,1024]{2,1,0:T(8,128)(2,1)S(1)}, bf16[8,16,1024]{2,1,0:T(8,128)(2,1)}, u32[]{:S(2)}, u32[]{:S(2)}) collective-permute-start(bf16[8,16,1024]{2,1,0:T(8,128)(2,1)S(1)} %copy-done.19), channel_id=1, source_target_pairs={{0,5},{1,4},{2,7},{3,6},{4,1},{5,0},{6,3},{7,2},{8,13},{9,12},{10,... | collective-permute-start | bytes 786440 | tf_op jit(solution)/shard_map/ppermute | solution.py:420
  76.8 27.0 %collective-permute-start.11 = (bf16[8,16,1024]{2,1,0:T(8,128)(2,1)S(1)}, bf16[8,16,1024]{2,1,0:T(8,128)(2,1)}, u32[]{:S(2)}, u32[]{:S(2)}) collective-permute-start(bf16[8,16,1024]{2,1,0:T(8,128)(2,1)S(1)} %copy-done.17), channel_id=1, source_target_pairs={{0,10},{1,11},{2,8},{3,9},{4,14},{5,15},{6,12},{7,13},{8,2},{9,3},... | collective-permute-start | bytes 786440 | tf_op jit(solution)/shard_map/ppermute | solution.py:420
  77.0 29.8 %collective-permute-start.12 = (bf16[8,16,1024]{2,1,0:T(8,128)(2,1)S(1)}, bf16[8,16,1024]{2,1,0:T(8,128)(2,1)}, u32[]{:S(2)}, u32[]{:S(2)}) collective-permute-start(bf16[8,16,1024]{2,1,0:T(8,128)(2,1)S(1)} %copy-done.15), channel_id=1, source_target_pairs={{0,6},{1,7},{2,4},{3,5},{4,2},{5,3},{6,0},{7,1},{8,14},{9,15},{10,... | collective-permute-start | bytes 786440 | tf_op jit(solution)/shard_map/ppermute | solution.py:420
  78.4 28.4 %collective-permute-start.13 = (bf16[8,16,1024]{2,1,0:T(8,128)(2,1)S(1)}, bf16[8,16,1024]{2,1,0:T(8,128)(2,1)}, u32[]{:S(2)}, u32[]{:S(2)}) collective-permute-start(bf16[8,16,1024]{2,1,0:T(8,128)(2,1)S(1)} %copy-done.14), channel_id=1, source_target_pairs={{0,14},{1,15},{2,12},{3,13},{4,10},{5,11},{6,8},{7,9},{8,6},{9,7},... | collective-permute-start | bytes 786440 | tf_op jit(solution)/shard_map/ppermute | solution.py:420
  80.0 36.3 %collective-permute-start.14 = (bf16[8,16,1024]{2,1,0:T(8,128)(2,1)S(1)}, bf16[8,16,1024]{2,1,0:T(8,128)(2,1)}, u32[]{:S(2)}, u32[]{:S(2)}) collective-permute-start(bf16[8,16,1024]{2,1,0:T(8,128)(2,1)S(1)} %copy-done.13), channel_id=1, source_target_pairs={{0,7},{1,6},{2,5},{3,4},{4,3},{5,2},{6,1},{7,0},{8,15},{9,14},{10,... | collective-permute-start | bytes 786440 | tf_op jit(solution)/shard_map/ppermute | solution.py:420
  103.8 30.9 %collective-permute-start.15 = (bf16[8,16,1024]{2,1,0:T(8,128)(2,1)S(1)}, bf16[8,16,1024]{2,1,0:T(8,128)(2,1)S(1)}, u32[]{:S(2)}, u32[]{:S(2)}) collective-permute-start(bf16[8,16,1024]{2,1,0:T(8,128)(2,1)S(1)} %copy-done.12), channel_id=1, source_target_pairs={{0,11},{1,10},{2,9},{3,8},{4,15},{5,14},{6,13},{7,12},{8,3},{9,2},... | collective-permute-start | bytes 786440 | tf_op jit(solution)/shard_map/ppermute | solution.py:420
  103.9 30.8 %collective-permute-start.16 = (bf16[8,16,1024]{2,1,0:T(8,128)(2,1)S(1)}, bf16[8,16,1024]{2,1,0:T(8,128)(2,1)S(1)}, u32[]{:S(2)}, u32[]{:S(2)}) collective-permute-start(bf16[8,16,1024]{2,1,0:T(8,128)(2,1)S(1)} %copy-done.11), channel_id=1, source_target_pairs={{0,15},{1,14},{2,13},{3,12},{4,11},{5,10},{6,9},{7,8},{8,7},{9,6},... | collective-permute-start | bytes 786440 | tf_op jit(solution)/shard_map/ppermute | solution.py:420
  (19 other events, 284.5 us)
